TPU v7x, 32 devices: a whole 2x2x4 slice. The times are simulated.
32 devices in a mesh: en: 2 (over x), ph: 4 (over y, core), blk: 4 (over z).
Axes of the slice: x: 2, y: 2, z: 4, core: 2. Of those that a mesh axis runs over, the one named last changes fastest.
Arguments:
- lesser_in: bfloat16 [6, 8, 512, 512], P('en', 'blk', 'ph'), may hold values from -6 to 6
- greater_in: bfloat16 [6, 8, 512, 512], P('en', 'blk', 'ph'), may hold values from -6 to 6
- inverse: bfloat16 [6, 8, 512, 512], P('en', 'blk', 'ph'), may hold values from -0.25 to 0.25
- offsets: int32 [6, 8], P('en', 'ph'), may hold values from -9 to 9, as said below
- couplings: float32 [6, 8], P('en', 'ph'), may hold values from 0.2 to 1
Outputs:
- lesser_out: bfloat16 [6, 8, 512, 512], P('en', 'blk', 'ph')
- greater_out: bfloat16 [6, 8, 512, 512], P('en', 'blk', 'ph')
Inputs may be any that keep to these rules, and one draw needn't show every extreme that they name: `offsets`: both extremes occur in every draw.
All inputs are finite; a program needn't handle non-finite values.
Results may differ from a plain program's by a relative error of at most 0.0057.
Values may be sent and summed in bfloat16 or wider, within the bound.
No kernel may reach another device: no remote copies, remote signals or barrier semaphores. Data moves between devices by JAX's collectives and lax.ppermute only.
A program may use at most 64 MiB of HBM per device.

v0:
```python
import jax
import jax.numpy as jnp
from jax import lax
from jax.sharding import PartitionSpec as P


def shortened(x):
    return jax.tree.map(lambda a: a.astype(jnp.bfloat16) if a.dtype == jnp.float32 else a, x)


def on_device(lesser_in, greater_in, inverse, offsets, couplings):
    shifts = lax.all_gather(offsets, "ph", axis=1, tiled=True)
    weights_all = lax.all_gather(couplings, "ph", axis=1, tiled=True)
    shift_every = lax.all_gather(shifts, "en", axis=0, tiled=True)
    weight_every = lax.all_gather(weights_all, "en", axis=0, tiled=True)
    energy_count = shift_every.shape[0]
    target_every = jnp.arange(energy_count, dtype=jnp.int32)[:, None] + shift_every
    energy_cols = jnp.arange(energy_count, dtype=jnp.int32)
    full_mixing = jnp.sum(
        jnp.where(
            energy_cols[None, None, :] == target_every[:, :, None],
            weight_every[:, :, None],
            jnp.float32(0.0),
        ),
        axis=1,
    )
    moved = (
        lax.all_to_all(lesser_in, "en", split_axis=3, concat_axis=0, tiled=True),
        lax.all_to_all(greater_in, "en", split_axis=3, concat_axis=0, tiled=True),
    )
    mixed = tuple(
        (
            jnp.dot(
                full_mixing,
                incoming.reshape(energy_count, -1),
                precision=lax.Precision.HIGHEST,
                preferred_element_type=jnp.float32,
            )
            .reshape(incoming.shape)
            .astype(jnp.bfloat16)
            for incoming in moved
        )
    )
    returned = jax.tree.map(
        lambda part, own: part.astype(own.dtype),
        lax.all_to_all(shortened(mixed), "en", split_axis=0, concat_axis=3, tiled=True),
        mixed,
    )
    self_energy = jnp.stack(returned)
    sigma_full, inverse_full = (
        lax.all_gather(self_energy, "ph", axis=3, tiled=True),
        lax.all_gather(inverse, "ph", axis=2, tiled=True),
    )
    left_product = jnp.einsum(
        "ebrk,sebkc->sebrc", inverse, sigma_full, preferred_element_type=jnp.float32
    ).astype(jnp.bfloat16)
    result = jnp.einsum(
        "sebrk,ebck->sebrc", left_product, inverse_full, preferred_element_type=jnp.float32
    ).astype(jnp.bfloat16)
    return (result[0], result[1])


def solution(mesh):
    placed = (
        P("en", "blk", "ph", None),
        P("en", "blk", "ph", None),
        P("en", "blk", "ph", None),
        P("en", "ph"),
        P("en", "ph"),
    )
    return jax.shard_map(
        on_device,
        mesh=mesh,
        in_specs=placed,
        out_specs=(P("en", "blk", "ph", None), P("en", "blk", "ph", None)),
        check_vma=False,
    )
```

profile of v0, /device:TPU:0, one launch (start us, length us, event | category | flops | bytes accessed | tf_op | source)
XLA Modules:
  0.0 143.7 jit_solution(1933757303607697813)
XLA Ops:
  7.2 0.0 copy-start.2
  7.2 0.0 copy-start.3
  7.2 0.0 copy-start
  7.2 0.0 all-gather.9.cloned.1.call-start
  7.2 0.7 all-gather.9.cloned.1.call-update
  7.9 2.4 %copy.45 = bf16[3,2,128,512]{2,0,1,3:T(4,128)(2,1)} copy(bf16[3,2,128,512]{3,2,1,0:T(8,128)(2,1)} %param.5) | data formatting | bytes 1572864 | tf_op args[0]
  10.4 4.2 %all-to-all-start = ((bf16[3,2,128,512]{2,0,1,3:T(4,128)(2,1)}), bf16[3,2,128,512]{2,0,1,3:T(4,128)(2,1)S(1)}, u32[]{:S(2)}, u32[]{:S(2)}) async-start(bf16[3,2,128,512]{2,0,1,3:T(4,128)(2,1)} %copy.45), calls=%async_computation | async-start | bytes 2097152 | tf_op jit(solution)/shard_map/all_to_all | solution.py:28
  14.6 0.0 copy-done.2
  14.6 5.4 %all-gather = s32[4,2,3]{2,1,0:T(2,128)S(1)} all-gather(s32[1,2,3]{2,1,0:T(2,128)S(1)} %bitcast.89), channel_id=1, replica_groups=mesh['en'=2,'ph'=4,'blk'=4] {'ph'}, dimensions={0}, use_global_device_ids=true | all-gather | bytes 120 | tf_op jit(solution)/shard_map/all_gather | solution.py:12
  20.0 0.0 copy-done.3
  20.0 5.3 %all-gather.2 = f32[4,2,3]{2,1,0:T(2,128)S(1)} all-gather(f32[1,2,3]{2,1,0:T(2,128)S(1)} %bitcast.90), channel_id=1, replica_groups=mesh['en'=2,'ph'=4,'blk'=4] {'ph'}, dimensions={0}, use_global_device_ids=true | all-gather | bytes 120 | tf_op jit(solution)/shard_map/all_gather | solution.py:13
  25.3 0.1 copy.43
  25.4 4.3 %all-gather.1 = s32[2,3,8]{2,1,0:T(4,128)S(1)} all-gather(s32[1,3,8]{2,1,0:T(4,128)S(1)} %bitcast.87), channel_id=1, replica_groups=mesh['en'=2,'ph'=4,'blk'=4] {'en'}, dimensions={0}, use_global_device_ids=true | all-gather | bytes 288 | tf_op jit(solution)/shard_map/all_gather | solution.py:14
  29.7 0.0 copy-done
  29.7 1.5 %copy.49 = bf16[3,2,128,512]{2,0,1,3:T(4,128)(2,1)} copy(bf16[3,2,128,512]{3,2,1,0:T(8,128)(2,1)S(1)} %copy-done) | data formatting | bytes 1572864 | tf_op args[1]
  31.2 0.0 all-to-all-done
  31.2 3.6 %all-to-all-start.2 = ((bf16[3,2,128,512]{2,0,1,3:T(4,128)(2,1)}), bf16[3,2,128,512]{2,0,1,3:T(4,128)(2,1)S(1)}, u32[]{:S(2)}, u32[]{:S(2)}) async-start(bf16[3,2,128,512]{2,0,1,3:T(4,128)(2,1)} %copy.49), calls=%async_computation.2 | async-start | bytes 2097152 | tf_op jit(solution)/shard_map/all_to_all | solution.py:29
  34.8 0.1 copy.44
  34.9 13.8 %all-gather.3 = f32[2,3,8]{2,1,0:T(4,128)S(1)} all-gather(f32[1,3,8]{2,1,0:T(4,128)S(1)} %bitcast.88), channel_id=1, replica_groups=mesh['en'=2,'ph'=4,'blk'=4] {'en'}, dimensions={0}, use_global_device_ids=true | all-gather | bytes 288 | tf_op jit(solution)/shard_map/all_gather | solution.py:15
  48.7 0.1 select_reduce_fusion
  48.8 0.6 copy.46
  49.4 0.8 reshape.20
  50.2 1.0 convolution_convert_fusion.2
  51.2 1.0 copy.47
  52.3 0.0 all-to-all-done.2
  52.3 4.3 %all-to-all-start.1 = ((bf16[6,2,128,256]{3,2,1,0:T(8,128)(2,1)}), bf16[6,2,128,256]{3,2,1,0:T(8,128)(2,1)}, u32[]{:S(2)}, u32[]{:S(2)}) async-start(bf16[6,2,128,256]{3,2,1,0:T(8,128)(2,1)} %copy.47), calls=%async_computation.1 | async-start | bytes 1572864 | tf_op jit(solution)/shard_map/all_to_all | solution.py:46
  56.6 0.6 copy.50
  57.2 0.8 reshape.21
  58.0 1.0 convolution_convert_fusion.1
  59.0 1.0 copy.51
  60.1 6.8 %all-to-all-done.1 = bf16[6,2,128,256]{3,2,1,0:T(8,128)(2,1)} async-done(((bf16[6,2,128,256]{3,2,1,0:T(8,128)(2,1)}), bf16[6,2,128,256]{3,2,1,0:T(8,128)(2,1)}, u32[]{:S(2)}, u32[]{:S(2)}) %all-to-all-start.1) | async-done | bytes 786464 | tf_op jit(solution)/shard_map/all_to_all | solution.py:46
  66.9 3.5 %all-to-all-start.3 = ((bf16[6,2,128,256]{3,2,1,0:T(8,128)(2,1)}), bf16[6,2,128,256]{3,2,1,0:T(8,128)(2,1)S(1)}, u32[]{:S(2)}, u32[]{:S(2)}) async-start(bf16[6,2,128,256]{3,2,1,0:T(8,128)(2,1)} %copy.51), calls=%async_computation.3 | async-start | bytes 1572864 | tf_op jit(solution)/shard_map/all_to_all | solution.py:46
  70.4 0.0 all-gather.7.cloned.1.call-start
  70.5 1.5 %copy.48 = bf16[3,2,128,2,256]{2,4,3,1,0:T(8,128)(2,1)S(1)} copy(bf16[3,2,128,2,256]{4,2,1,0,3:T(8,128)(2,1)} %bitcast.17) | data formatting | bytes 1572864 | tf_op jit(solution)/shard_map/all_to_all | solution.py:46
  72.0 7.7 %all-to-all-done.3 = bf16[6,2,128,256]{3,2,1,0:T(8,128)(2,1)S(1)} async-done(((bf16[6,2,128,256]{3,2,1,0:T(8,128)(2,1)}), bf16[6,2,128,256]{3,2,1,0:T(8,128)(2,1)S(1)}, u32[]{:S(2)}, u32[]{:S(2)}) %all-to-all-start.3) | async-done | bytes 786464 | tf_op jit(solution)/shard_map/all_to_all | solution.py:46
  79.7 0.0 copy-start.1
  79.7 0.4 copy.52
  80.1 1.3 pad_maximum_fusion
  81.4 0.0 all-gather.7.cloned.1.call-update
  81.4 0.0 all-gather.9.cloned.1.call-done
  81.4 47.8 %all-gather.7.cloned.1.call-done = bf16[2,3,2,512,512]{3,4,0,2,1:T(8,128)(2,1)} async-done(((bf16[2,3,2,128,512]{3,4,0,2,1:T(8,128)(2,1)}), bf16[2,3,2,512,512]{3,4,0,2,1:T(8,128)(2,1)}) %all-gather.7.cloned.1.call-update) | async-done | bytes 6291472 | tf_op jit(solution)/shard_map/all_gather | solution.py:51
  129.2 0.0 copy-done.1
  129.2 6.3 %fusion.6 = bf16[2,3,2,128,512]{4,3,0,2,1:T(8,128)(2,1)S(1)} fusion(bf16[3,2,512,512]{3,2,1,0:T(8,128)(2,1)} %all-gather.9.cloned.1.call-done, bf16[2,3,2,512,512]{3,4,0,2,1:T(8,128)(2,1)} %all-gather.7.cloned.1.call-done, bf16[3,2,128,512]{3,2,1,0:T(8,128)(2,1)S(1)} %copy-done.1), kind=kOutput, calls=%fused_computation.6 | convolution fusion | flops 1612185600 | bytes 11796480 | tf_op jit(solution)/shard_map/sebrk,ebck->sebrc/dot_general | solution.py:57
  135.6 1.3 slice_bitcast_fusion
  (3 shorter events, 0.0 us)
Async XLA Ops:
  7.2 7.4 %copy-start.2 = (s32[3,2]{0,1:T(2,128)S(1)}, s32[3,2]{0,1:T(2,128)}, u32[]{:S(2)}) copy-start(s32[3,2]{0,1:T(2,128)} %param.8) | copy-start | bytes 76
  7.2 12.8 %copy-start.3 = (f32[3,2]{0,1:T(2,128)S(1)}, f32[3,2]{0,1:T(2,128)}, u32[]{:S(2)}) copy-start(f32[3,2]{0,1:T(2,128)} %param.9) | copy-start | bytes 76
  7.2 22.5 %copy-start = (bf16[3,2,128,512]{3,2,1,0:T(8,128)(2,1)S(1)}, bf16[3,2,128,512]{3,2,1,0:T(8,128)(2,1)}, u32[]{:S(2)}) copy-start(bf16[3,2,128,512]{3,2,1,0:T(8,128)(2,1)} %param.6) | copy-start | bytes 2359300
  7.2 74.2 %all-gather.9.cloned.1.call-start = ((), (), s32[]{:S(2)}) async-start(), calls=%async_computation.5 | async-start | bytes 3932160 | tf_op jit(solution)/shard_map/all_gather | solution.py:52
  10.4 20.8 %all-to-all-start = ((bf16[3,2,128,512]{2,0,1,3:T(4,128)(2,1)}), bf16[3,2,128,512]{2,0,1,3:T(4,128)(2,1)S(1)}, u32[]{:S(2)}, u32[]{:S(2)}) async-start(bf16[3,2,128,512]{2,0,1,3:T(4,128)(2,1)} %copy.45), calls=%async_computation | async-start | bytes 2097152 | tf_op jit(solution)/shard_map/all_to_all | solution.py:28
  31.2 21.1 %all-to-all-start.2 = ((bf16[3,2,128,512]{2,0,1,3:T(4,128)(2,1)}), bf16[3,2,128,512]{2,0,1,3:T(4,128)(2,1)S(1)}, u32[]{:S(2)}, u32[]{:S(2)}) async-start(bf16[3,2,128,512]{2,0,1,3:T(4,128)(2,1)} %copy.49), calls=%async_computation.2 | async-start | bytes 2097152 | tf_op jit(solution)/shard_map/all_to_all | solution.py:29
  52.3 14.6 %all-to-all-start.1 = ((bf16[6,2,128,256]{3,2,1,0:T(8,128)(2,1)}), bf16[6,2,128,256]{3,2,1,0:T(8,128)(2,1)}, u32[]{:S(2)}, u32[]{:S(2)}) async-start(bf16[6,2,128,256]{3,2,1,0:T(8,128)(2,1)} %copy.47), calls=%async_computation.1 | async-start | bytes 1572864 | tf_op jit(solution)/shard_map/all_to_all | solution.py:46
  66.9 12.8 %all-to-all-start.3 = ((bf16[6,2,128,256]{3,2,1,0:T(8,128)(2,1)}), bf16[6,2,128,256]{3,2,1,0:T(8,128)(2,1)S(1)}, u32[]{:S(2)}, u32[]{:S(2)}) async-start(bf16[6,2,128,256]{3,2,1,0:T(8,128)(2,1)} %copy.51), calls=%async_computation.3 | async-start | bytes 1572864 | tf_op jit(solution)/shard_map/all_to_all | solution.py:46
  70.4 58.8 %all-gather.7.cloned.1.call-start = ((), (), s32[]{:S(2)}) async-start(), calls=%async_computation.4 | async-start | bytes 7864320 | tf_op jit(solution)/shard_map/all_gather | solution.py:51
  79.7 49.5 %copy-start.1 = (bf16[3,2,128,512]{3,2,1,0:T(8,128)(2,1)S(1)}, bf16[3,2,128,512]{3,2,1,0:T(8,128)(2,1)}, u32[]{:S(2)}) copy-start(bf16[3,2,128,512]{3,2,1,0:T(8,128)(2,1)} %param.7) | copy-start | bytes 2359300
Sparse Core Ops, SparseCore 0:
  9.6 31.2 all-gather.8
  81.5 47.6 all-gather.6
where the time goes:
time: 144 us
  waiting for transfers between devices  63.1 us (44%)
  blocking collectives  28.9 us (20%)
  starting transfers between devices  15.7 us (11%)
  between operations  14.2 us (10%)
  local copies, waits for them, and re-layouts  12.2 us (8%)
  matrix products  8.25 us (6%)
    all_gather x1, waiting for transfers between devices, on_device(): lax.all_gather(self_energy, 'ph', axis=3, tiled=True)  47.8 us
    all_to_all x2, waiting for transfers between devices, on_device(): lax.all_to_all(shortened(mixed), 'en', split_axis=0, concat_axis=3, tiled...  14.6 us
    all_gather x1, blocking collectives, on_device(): weight_every = lax.all_gather(weights_all, 'en', axis=0, tiled=True)  13.8 us
    all_to_all x2, starting transfers between devices, on_device(): lax.all_to_all(shortened(mixed), 'en', split_axis=0, concat_axis=3, tiled...  7.86 us
    dot_general x1, matrix products, on_device(): jnp.einsum('sebrk,ebck->sebrc', left_product, inverse_full, preferred_ele...  6.32 us
    all_gather x1, blocking collectives, on_device(): shifts = lax.all_gather(offsets, 'ph', axis=1, tiled=True)  5.4 us
    all_gather x1, blocking collectives, on_device(): weights_all = lax.all_gather(couplings, 'ph', axis=1, tiled=True)  5.35 us
    all_gather x1, blocking collectives, on_device(): shift_every = lax.all_gather(shifts, 'en', axis=0, tiled=True)  4.33 us
  transfers between devices with their start and end apart: 6, of which 3 were waited for; matrix products, arithmetic and copies ran while one was open for 10% of the time, Pallas kernels for 0%

commit v1 on v0

v1 whole, which is shorter than its diff:
```python
import functools
import math

import jax
import jax.numpy as jnp
from jax import lax
from jax.experimental import pallas as pl
from jax.experimental.pallas import tpu as pltpu
from jax.sharding import PartitionSpec as P

MAXOFF = 9
BF16 = jnp.bfloat16


def mix_kernel(sources, index_ref, weight_ref, *refs):
    ins, out_ref = refs[:sources], refs[sources]
    e, blocks, rows, _ = out_ref.shape
    step = 16
    weights = [
        [weight_ref[n, m] for m in range(sources * e)] for n in range(e)
    ]
    for b in range(blocks):

        @pl.loop(0, rows // step)
        def _(i):
            at = pl.ds(pl.multiple_of(i * step, step), step)
            totals = [None] * e
            for t in range(sources):
                for m in range(e):
                    g = ins[t][m, b, at, :].astype(jnp.float32)
                    for n in range(e):
                        term = weights[n][t * e + m] * g
                        totals[n] = term if totals[n] is None else totals[n] + term
            for n in range(e):
                out_ref[n, b, at, :] = totals[n].astype(out_ref.dtype)


def mix(ins, index, weights, owned):
    e, _, rows, o = ins[0].shape
    chunk = math.gcd(rows, 32)
    spec = pl.BlockSpec((e, owned, chunk, o), lambda i, at: (0, at[0], i, 0))
    return pl.pallas_call(
        functools.partial(mix_kernel, len(ins)),
        grid_spec=pltpu.PrefetchScalarGridSpec(
            num_scalar_prefetch=1,
            grid=(rows // chunk,),
            in_specs=[pl.BlockSpec(memory_space=pltpu.SMEM)] + [spec] * len(ins),
            out_specs=pl.BlockSpec((e, owned, chunk, o), lambda i, at: (0, 0, i, 0)),
        ),
        out_shape=jax.ShapeDtypeStruct((e, owned, rows, o), BF16),
        cost_estimate=pl.CostEstimate(
            flops=2 * len(ins) * e * e * owned * rows * o,
            bytes_accessed=2 * (len(ins) + 1) * e * owned * rows * o,
            transcendentals=0,
        ),
        name="mix",
    )(index.reshape(1), weights, *ins)


def product_kernel(pieces, lefts, place_ref, *refs):
    a_in, s_in = refs[:pieces], refs[pieces : 2 * pieces]
    outs = refs[2 * pieces : 2 * pieces + lefts]
    a_full, s_full, sems = refs[2 * pieces + lefts :]
    e, blocks, rows, _ = outs[0].shape
    copies = []
    for n in range(e):
        batch = []
        for k, (ins, full) in enumerate(((a_in, a_full), (s_in, s_full))):
            for i in range(pieces):
                at = pl.ds(pl.multiple_of(place_ref[i] * rows, rows), rows)
                batch.append(
                    pltpu.make_async_copy(
                        ins[i].at[n], full.at[n, :, at, :], sems.at[n, k, i]
                    )
                )
        for copy in batch:
            copy.start()
        copies.append(batch)
    for n in range(e):
        for copy in copies[n]:
            copy.wait()
        for b in range(blocks):
            left = jnp.concatenate(
                [
                    a_full[n, b, pl.ds(pl.multiple_of(place_ref[i] * rows, rows), rows), :]
                    for i in range(lefts)
                ],
                axis=0,
            )
            first = jnp.dot(
                left, s_full[n, b], preferred_element_type=jnp.float32
            ).astype(BF16)
            both = lax.dot_general(
                first,
                a_full[n, b],
                (((1,), (1,)), ((), ())),
                preferred_element_type=jnp.float32,
            ).astype(BF16)
            for i in range(lefts):
                outs[i][n, b] = both[i * rows : (i + 1) * rows]


def product(a_pieces, s_pieces, places, lefts):
    pieces = len(a_pieces)
    e, blocks, rows, o = a_pieces[0].shape
    anywhere = pl.BlockSpec(memory_space=pl.ANY)
    full = pltpu.VMEM((e, blocks, pieces * rows, o), BF16)
    return pl.pallas_call(
        functools.partial(product_kernel, pieces, lefts),
        in_specs=[pl.BlockSpec(memory_space=pltpu.SMEM)] + [anywhere] * (2 * pieces),
        out_specs=[pl.BlockSpec(memory_space=pltpu.VMEM)] * lefts,
        out_shape=[jax.ShapeDtypeStruct((e, blocks, rows, o), BF16)] * lefts,
        scratch_shapes=[full, full, pltpu.SemaphoreType.DMA((e, 2, pieces))],
        compiler_params=pltpu.CompilerParams(vmem_limit_bytes=32 * 1024 * 1024),
        cost_estimate=pl.CostEstimate(
            flops=4 * e * blocks * lefts * rows * o * o,
            bytes_accessed=2 * e * blocks * rows * o * (2 * pieces + lefts),
            transcendentals=0,
        ),
        name="product",
    )(places, *a_pieces, *s_pieces)


def solution(mesh):
    en, ph = mesh.shape["en"], mesh.shape["ph"]

    def on_device(lesser_in, greater_in, inverse, offsets, couplings):
        e, nb, r, o = lesser_in.shape
        owners = math.gcd(nb, ph)
        lanes = ph // owners
        owned = nb // owners
        en_at, ph_at = lax.axis_index("en"), lax.axis_index("ph")
        owner, lane = ph_at // lanes, ph_at % lanes

        def to_owner(x, d):
            pairs = [
                (p, (p // lanes + d) % owners * lanes + p % lanes) for p in range(ph)
            ]
            return lax.ppermute(x, "ph", pairs)

        def to_lane(x, d):
            pairs = [
                (p, p // lanes * lanes + (p % lanes + d) % lanes) for p in range(ph)
            ]
            return lax.ppermute(x, "ph", pairs)

        def to_energy(x, t):
            return lax.ppermute(x, "en", [((i + t) % en, i) for i in range(en)])

        def blocks_of(x, at):
            return lax.dynamic_slice_in_dim(x, at * owned, owned, axis=1)

        reach = (MAXOFF + e - 1) // e
        shifts = [t for t in range(1, en) if t <= reach or en - t <= reach]
        sources = len(shifts) + 1

        lesser_from = [lesser_in] + [to_energy(lesser_in, t) for t in shifts]
        greater_own = blocks_of(greater_in, owner)
        greater_rows = [greater_own] + [
            to_owner(blocks_of(greater_in, (owner + d) % owners), d) for d in range(1, owners)
        ]
        inverse_rows = [blocks_of(inverse, owner)] + [
            to_owner(blocks_of(inverse, (owner + d) % owners), d) for d in range(1, owners)
        ]

        small = lax.all_gather(
            jnp.stack([offsets.astype(jnp.float32), couplings]), "ph", axis=2, tiled=True
        )
        away = jnp.stack(
            [((en_at + t) % en - en_at) * e for t in [0] + shifts]
        )
        apart = (away[:, None] + jnp.arange(e)[None, :]).reshape(1, -1) - jnp.arange(e)[:, None]
        weights = jnp.sum(
            jnp.where(
                small[0][:, None, :] == apart[:, :, None].astype(jnp.float32),
                small[1][:, None, :],
                jnp.float32(0.0),
            ),
            axis=2,
        )

        zero = jnp.zeros((), jnp.int32)
        lesser_rows = [None] * owners
        for d in range(1, owners):
            lesser_rows[d] = to_owner(mix(lesser_from, (owner + d) % owners, weights, owned), d)
        lesser_rows[0] = mix(lesser_from, owner, weights, owned)
        greater_mixed = [
            mix([rows] + [to_energy(rows, t) for t in shifts], zero, weights, owned)
            for rows in greater_rows
        ]

        places = jnp.stack(
            [
                (owner - d) % owners * lanes + (lane - q) % lanes
                for q in range(lanes)
                for d in range(owners)
            ]
        )

        def all_lanes(pieces):
            return pieces + [to_lane(x, q) for q in range(1, lanes) for x in pieces]

        inverse_full = all_lanes(inverse_rows)

        def finish(sigma_rows):
            outs = product(inverse_full, all_lanes(sigma_rows), places, owners)
            result = jnp.zeros((e, nb, r, o), BF16)
            for d in range(owners):
                back = outs[d] if d == 0 else to_owner(outs[d], owners - d)
                result = lax.dynamic_update_slice_in_dim(
                    result, back, (owner + d) % owners * owned, axis=1
                )
            return result

        return finish(lesser_rows), finish(greater_mixed)

    block, coupled = P("en", "blk", "ph", None), P("en", "ph")
    return jax.shard_map(
        on_device,
        mesh=mesh,
        in_specs=(block, block, block, coupled, coupled),
        out_specs=(block, block),
        check_vma=False,
    )
```

time: 144 us -> 80.6 us (0.56)
  waiting for transfers between devices: 63.1 us -> 20.3 us
  Pallas kernels: 0 us -> 26.4 us
  blocking collectives: 28.9 us -> 13.9 us
  between operations: 14.2 us -> 0.84 us
  matrix products: 8.25 us -> 0 us
  starting transfers between devices: 15.7 us -> 10.2 us
  local copies, waits for them, and re-layouts: 12.2 us -> 7.46 us
    all_gather x2 -> x0, waiting for transfers between devices: 47.8 us -> none  [the longest x1 47.8 us: on_device(): lax.all_gather(self_energy, 'ph', axis=3, tiled=True)]
    pallas_call x0 -> x6, Pallas kernels: none -> 26.4 us  [the longest x4 13.8 us: mix(): pl.pallas_call(functools.partial(mix_kernel, len(ins)), grid_spec=pltpu.P...]
    ppermute x0 -> x14, waiting for transfers between devices: none -> 20.3 us  [the longest x5 12.5 us: to_owner(): return lax.ppermute(x, 'ph', pairs)]
    all_to_all x4 -> x0, starting transfers between devices: 15.6 us -> none  [the longest x2 7.86 us: on_device(): lax.all_to_all(shortened(mixed), 'en', split_axis=0, concat_axis=3, tiled...]
    all_gather x4 -> x1, blocking collectives: 28.9 us -> 13.9 us  [on_device(): lax.all_gather(jnp.stack([offsets.astype(jnp.float32), couplings]), 'ph',...]
    all_to_all x4 -> x0, waiting for transfers between devices: 14.6 us -> none  [the longest x2 14.6 us: on_device(): lax.all_to_all(shortened(mixed), 'en', split_axis=0, concat_axis=3, tiled...]
    ppermute x0 -> x14, starting transfers between devices: none -> 10.2 us  [the longest x5 5.75 us: to_owner(): return lax.ppermute(x, 'ph', pairs)]
    dot_general x3 -> x0, matrix products: 8.25 us -> none  [the longest x1 6.32 us: on_device(): jnp.einsum('sebrk,ebck->sebrc', left_product, inverse_full, preferred_ele...]
  transfers between devices with their start and end apart: 6 -> 14, of which waited for: 3 -> 3; matrix products, arithmetic and copies ran while one was open for 10% -> 3% of each run, Pallas kernels for 0% -> 33%
where the time goes in v1:
time: 80.6 us; the launch traced here: 80 us
  Pallas kernels  26.4 us (33%)
  waiting for transfers between devices  20.3 us (25%)
  blocking collectives  13.9 us (17%)
  starting transfers between devices  10.2 us (13%)
  local copies, waits for them, and re-layouts  7.46 us (9%)
  other arithmetic  0.98 us (1%)
  between operations  0.84 us (1%)
    all_gather x1, blocking collectives, on_device(): lax.all_gather(jnp.stack([offsets.astype(jnp.float32), couplings]), 'ph',...  13.9 us
    pallas_call x4, Pallas kernels, mix(): pl.pallas_call(functools.partial(mix_kernel, len(ins)), grid_spec=pltpu.P...  13.8 us
    pallas_call x2, Pallas kernels, product(): pl.pallas_call(functools.partial(product_kernel, pieces, lefts), in_specs...  12.6 us
    ppermute x5, waiting for transfers between devices, to_owner(): return lax.ppermute(x, 'ph', pairs)  12.5 us
    ppermute x3, waiting for transfers between devices, to_energy(): return lax.ppermute(x, 'en', [((i + t) % en, i) for i in range(en)])  7.71 us
    ppermute x5, starting transfers between devices, to_owner(): return lax.ppermute(x, 'ph', pairs)  5.75 us
    unnamed x26, local copies, waits for them, and re-layouts  4.88 us
    ppermute x3, starting transfers between devices, to_energy(): return lax.ppermute(x, 'en', [((i + t) % en, i) for i in range(en)])  3.39 us
  transfers between devices with their start and end apart: 14, of which 3 were waited for; matrix products, arithmetic and copies ran while one was open for 3% of the time, Pallas kernels for 33%

profile of v1, /device:TPU:0, one launch (start us, length us, event | category | flops | bytes accessed | tf_op | source)
XLA Modules:
  0.0 80.0 jit_solution(6406437427913961984)
XLA Ops:
  0.7 0.0 copy-start.10
  0.7 1.2 %constant_dynamic-slice_fusion = (bf16[3,1,128,512]{3,2,1,0:T(8,128)(2,1)S(1)}, bf16[3,1,128,512]{3,2,1,0:T(8,128)(2,1)S(1)}) fusion(bf16[3,2,128,512]{3,2,1,0:T(8,128)(2,1)} %param.6, s32[]{:T(128)S(6)} %select_n.85, s32[]{:T(128)S(6)} %select_n.83), kind=kLoop, calls=%fused_computation.5 | loop fusion | bytes 1572872 | tf_op jit(solution)/shard_map/dynamic_slice | solution.py:151
  1.9 0.0 copy-start.7
  1.9 3.0 %collective-permute-start.9 = (bf16[3,1,128,512]{3,2,1,0:T(8,128)(2,1)S(1)}, bf16[3,1,128,512]{3,2,1,0:T(8,128)(2,1)}, u32[]{:S(2)}, u32[]{:S(2)}) collective-permute-start(bf16[3,1,128,512]{3,2,1,0:T(8,128)(2,1)S(1)} %get-tuple-element.10), channel_id=1, source_target_pairs={{0,8},{4,12},{8,0},{12,4},{1,9},{5,13},{9,1},{13,5},{2,10},{6,14},... | collective-permute-start | bytes 1179656 | tf_op jit(solution)/shard_map/ppermute | solution.py:139
  5.0 1.5 %collective-permute-start.8 = (bf16[3,1,128,512]{3,2,1,0:T(8,128)(2,1)S(1)}, bf16[3,1,128,512]{3,2,1,0:T(8,128)(2,1)}, u32[]{:S(2)}, u32[]{:S(2)}) collective-permute-start(bf16[3,1,128,512]{3,2,1,0:T(8,128)(2,1)S(1)} %get-tuple-element.11.refs_0_), channel_id=1, source_target_pairs={{16,0},{0,16},{17,1},{1,17},{18,2},{2,18},{19,3},{3,19},{20,4},{4,... | collective-permute-start | bytes 1179656 | tf_op jit(solution)/shard_map/ppermute | solution.py:148
  6.5 0.0 copy-done.10
  6.5 0.8 %constant_dynamic-slice_fusion.2 = (bf16[3,1,128,512]{3,2,1,0:T(8,128)(2,1)}, bf16[3,1,128,512]{3,2,1,0:T(8,128)(2,1)S(1)}) fusion(bf16[3,2,128,512]{3,2,1,0:T(8,128)(2,1)S(1)} %copy-done.10, s32[]{:T(128)S(6)} %select_n.85, s32[]{:T(128)S(6)} %select_n.83), kind=kLoop, calls=%fused_computation.9 | loop fusion | bytes 1572872 | tf_op jit(solution)/shard_map/dynamic_slice | solution.py:151
  7.3 0.0 copy-done.7
  7.3 0.5 collective-permute-start
  7.8 0.0 collective-permute-start.1
  7.8 0.0 copy-done.5
  7.8 0.1 collective-permute-start.3
  7.9 0.7 copy-done.11
  8.6 0.1 pad_add_fusion.1
  8.7 0.1 iota_add_fusion
  8.8 0.1 add.113
  8.9 0.7 copy-done.12
  9.5 13.9 %all_gather.3 = f32[2,3,8]{1,0,2:T(2,128)S(1)} all-gather(f32[2,3,2]{1,0,2:T(2,128)S(1)} %copy.12), channel_id=1, replica_groups=mesh['en'=2,'ph'=4,'blk'=4] {'ph'}, dimensions={2}, use_global_device_ids=true | all-gather | bytes 240 | tf_op jit(solution)/shard_map/all_gather | solution.py:166
  23.5 0.0 collective-permute-done.9.refs_0_
  23.5 1.8 %collective-permute-start.10 = (bf16[3,1,128,512]{3,2,1,0:T(8,128)(2,1)}, bf16[3,1,128,512]{3,2,1,0:T(8,128)(2,1)}, u32[]{:S(2)}, u32[]{:S(2)}) collective-permute-start(bf16[3,1,128,512]{3,2,1,0:T(8,128)(2,1)} %collective-permute-done.9.refs_0_), channel_id=1, source_target_pairs={{16,0},{0,16},{17,1},{1,17},{18,2},{2,18},{19,3},{3,19},{20,4},{4,... | collective-permute-start | bytes 1179656 | tf_op jit(solution)/shard_map/ppermute | solution.py:148
  25.3 0.1 copy.14
  25.3 0.1 copy.13
  25.4 0.7 select_reduce_fusion.weight_ref
  26.2 7.7 %collective-permute-done.3.refs_1_ = bf16[3,2,128,512]{3,2,1,0:T(8,128)(2,1)S(1)} collective-permute-done((bf16[3,2,128,512]{3,2,1,0:T(8,128)(2,1)S(1)}, bf16[3,2,128,512]{3,2,1,0:T(8,128)(2,1)S(1)}, u32[]{:S(2)}, u32[]{:S(2)}) %collective-permute-start.3) | collective-permute-done | bytes 786464 | tf_op jit(solution)/shard_map/ppermute | solution.py:148
  33.9 0.9 %copy-done.6 = bf16[3,2,128,512]{3,2,1,0:T(8,128)(2,1)} copy-done((bf16[3,2,128,512]{3,2,1,0:T(8,128)(2,1)}, bf16[3,2,128,512]{3,2,1,0:T(8,128)(2,1)S(1)}, u32[]{:S(2)}) %copy-start.6) | copy-done | bytes 786456
  34.8 3.4 %mix.5 = bf16[3,1,128,512]{3,2,1,0:T(8,128)(2,1)} custom-call(s32[1]{0:T(128)} %bitcast.11.index_ref, f32[3,6]{1,0:T(4,128)} %select_reduce_fusion.weight_ref, bf16[3,2,128,512]{3,2,1,0:T(8,128)(2,1)} %refs_0_.3, bf16[3,2,128,512]{3,2,1,0:T(8,128)(2,1)} %copy-done.6), custom_call_target="tpu_custom_call" | custom-call | flops 2359296 | bytes 1179648 | tf_op jit(solution)/shard_map/mix/pallas_call | solution.py:42
  38.2 0.1 collective-permute-start.4
  38.2 0.0 collective-permute-done.8.refs_1_
  38.2 3.4 %mix.6.refs_4_ = bf16[3,1,128,512]{3,2,1,0:T(8,128)(2,1)} custom-call(s32[1]{0:T(128)} %constant.94.clone.1.index_ref, f32[3,6]{1,0:T(4,128)} %select_reduce_fusion.weight_ref, bf16[3,1,128,512]{3,2,1,0:T(8,128)(2,1)} %copy-done.7, bf16[3,1,128,512]{3,2,1,0:T(8,128)(2,1)} %collective-permute-done.8.refs_1_), custom_call_target="tpu_custom_call" | custom-call | flops 2359296 | bytes 1179648 | tf_op jit(solution)/shard_map/mix/pallas_call | solution.py:42
  41.7 0.0 collective-permute-start.11
  41.7 0.0 collective-permute-done.refs_1_
  41.7 0.5 collective-permute-start.2
  42.2 0.0 collective-permute-done.10.refs_1_
  42.2 3.4 %mix.7.refs_5_ = bf16[3,1,128,512]{3,2,1,0:T(8,128)(2,1)} custom-call(s32[1]{0:T(128)} %constant.94.clone.1.index_ref, f32[3,6]{1,0:T(4,128)} %select_reduce_fusion.weight_ref, bf16[3,1,128,512]{3,2,1,0:T(8,128)(2,1)} %collective-permute-done.9.refs_0_, bf16[3,1,128,512]{3,2,1,0:T(8,128)(2,1)} %collective-permute-done.10.refs_1_), custom_call_target="tpu_custom_call" | custom-call | flops 2359296 | bytes 1179648 | tf_op jit(solution)/shard_map/mix/pallas_call | solution.py:42
  45.6 0.1 collective-permute-start.12
  45.7 3.5 %mix.4.refs_4_ = bf16[3,1,128,512]{3,2,1,0:T(8,128)(2,1)} custom-call(s32[1]{0:T(128)} %bitcast.4.index_ref, f32[3,6]{1,0:T(4,128)} %select_reduce_fusion.weight_ref, bf16[3,2,128,512]{3,2,1,0:T(8,128)(2,1)} %refs_0_.3, bf16[3,2,128,512]{3,2,1,0:T(8,128)(2,1)} %copy-done.6), custom_call_target="tpu_custom_call" | custom-call | flops 2359296 | bytes 1179648 | tf_op jit(solution)/shard_map/mix/pallas_call | solution.py:42
  49.2 0.0 collective-permute-done.1.refs_2_
  49.2 0.4 collective-permute-start.5
  49.6 0.0 collective-permute-done.4.refs_5_
  49.6 0.1 collective-permute-start.6
  49.7 0.1 pad_add_fusion.place_ref
  49.8 0.0 collective-permute-done.11.refs_6_
  49.8 0.0 collective-permute-done.2.refs_3_
  49.8 0.0 collective-permute-done.12.refs_7_
  49.8 0.0 copy-start.3
  49.8 0.7 copy-done.3
  50.6 0.0 copy-done.1
  50.6 0.0 copy-done.2
  50.6 1.0 %copy-done.4 = bf16[3,1,128,512]{3,2,1,0:T(8,128)(2,1)S(1)} copy-done((bf16[3,1,128,512]{3,2,1,0:T(8,128)(2,1)S(1)}, bf16[3,1,128,512]{3,2,1,0:T(8,128)(2,1)}, u32[]{:S(2)}) %copy-start.4) | copy-done | bytes 393240
  51.6 7.2 %product.3 = (bf16[3,1,128,512]{3,2,1,0:T(8,128)(2,1)S(1)}, bf16[3,1,128,512]{3,2,1,0:T(8,128)(2,1)}) custom-call(s32[4]{0:T(128)S(1)} %pad_add_fusion.place_ref, bf16[3,1,128,512]{3,2,1,0:T(8,128)(2,1)S(1)} %get-tuple-element.13.refs_0_, bf16[3,1,128,512]{3,2,1,0:T(8,128)(2,1)S(1)} %collective-permute-done.refs_1_, ...), custom_call_target="tpu_custom_call" | custom-call | flops 805306368 | bytes 3932160 | tf_op jit(solution)/shard_map/product/pallas_call | solution.py:108
  58.7 2.0 %collective-permute-start.13 = (bf16[3,1,128,512]{3,2,1,0:T(8,128)(2,1)}, bf16[3,1,128,512]{3,2,1,0:T(8,128)(2,1)S(1)}, u32[]{:S(2)}, u32[]{:S(2)}) collective-permute-start(bf16[3,1,128,512]{3,2,1,0:T(8,128)(2,1)} %get-tuple-element.9), channel_id=1, source_target_pairs={{0,8},{4,12},{8,0},{12,4},{1,9},{5,13},{9,1},{13,5},{2,10},{6,14},... | collective-permute-start | bytes 1179656 | tf_op jit(solution)/shard_map/ppermute | solution.py:139
  60.8 0.0 collective-permute-done.5.refs_6_
  60.8 0.0 collective-permute-done.6.refs_7_
  60.8 0.0 copy-done
  60.8 5.4 %product.2 = (bf16[3,1,128,512]{3,2,1,0:T(8,128)(2,1)S(1)}, bf16[3,1,128,512]{3,2,1,0:T(8,128)(2,1)S(1)}) custom-call(s32[4]{0:T(128)S(1)} %pad_add_fusion.place_ref, bf16[3,1,128,512]{3,2,1,0:T(8,128)(2,1)S(1)} %get-tuple-element.13.refs_0_, bf16[3,1,128,512]{3,2,1,0:T(8,128)(2,1)S(1)} %collective-permute-done.refs_1_, ...), custom_call_target="tpu_custom_call" | custom-call | flops 805306368 | bytes 3932160 | tf_op jit(solution)/shard_map/product/pallas_call | solution.py:108
  66.2 0.1 collective-permute-start.7
  66.3 0.1 broadcast.27.clone.1
  66.4 0.1 broadcast.27.clone
  66.5 4.5 %collective-permute-done.13 = bf16[3,1,128,512]{3,2,1,0:T(8,128)(2,1)S(1)} collective-permute-done((bf16[3,1,128,512]{3,2,1,0:T(8,128)(2,1)}, bf16[3,1,128,512]{3,2,1,0:T(8,128)(2,1)S(1)}, u32[]{:S(2)}, u32[]{:S(2)}) %collective-permute-start.13) | collective-permute-done | bytes 393248 | tf_op jit(solution)/shard_map/ppermute | solution.py:139
  71.0 0.0 copy-start.9
  71.0 8.1 %collective-permute-done.7 = bf16[3,1,128,512]{3,2,1,0:T(8,128)(2,1)S(1)} collective-permute-done((bf16[3,1,128,512]{3,2,1,0:T(8,128)(2,1)S(1)}, bf16[3,1,128,512]{3,2,1,0:T(8,128)(2,1)S(1)}, u32[]{:S(2)}, u32[]{:S(2)}) %collective-permute-start.7) | collective-permute-done | bytes 393248 | tf_op jit(solution)/shard_map/ppermute | solution.py:139
  79.2 0.0 copy-done.9
  79.2 0.0 copy-start.8
  79.2 0.9 %copy-done.8 = bf16[3,2,128,512]{3,2,1,0:T(8,128)(2,1)} copy-done((bf16[3,2,128,512]{3,2,1,0:T(8,128)(2,1)}, bf16[3,2,128,512]{3,2,1,0:T(8,128)(2,1)S(1)}, u32[]{:S(2)}) %copy-start.8) | copy-done | bytes 786456
  (17 shorter events, 0.2 us)
Async XLA Ops:
  0.7 5.8 %copy-start.10 = (bf16[3,2,128,512]{3,2,1,0:T(8,128)(2,1)S(1)}, bf16[3,2,128,512]{3,2,1,0:T(8,128)(2,1)}, u32[]{:S(2)}) copy-start(bf16[3,2,128,512]{3,2,1,0:T(8,128)(2,1)} %param.7) | copy-start | bytes 2359300
  1.9 5.4 %copy-start.7 = (bf16[3,1,128,512]{3,2,1,0:T(8,128)(2,1)}, bf16[3,1,128,512]{3,2,1,0:T(8,128)(2,1)S(1)}, u32[]{:S(2)}) copy-start(bf16[3,1,128,512]{3,2,1,0:T(8,128)(2,1)S(1)} %get-tuple-element.11.refs_0_) | copy-start | bytes 1179652
  1.9 21.5 %collective-permute-start.9 = (bf16[3,1,128,512]{3,2,1,0:T(8,128)(2,1)S(1)}, bf16[3,1,128,512]{3,2,1,0:T(8,128)(2,1)}, u32[]{:S(2)}, u32[]{:S(2)}) collective-permute-start(bf16[3,1,128,512]{3,2,1,0:T(8,128)(2,1)S(1)} %get-tuple-element.10), channel_id=1, source_target_pairs={{0,8},{4,12},{8,0},{12,4},{1,9},{5,13},{9,1},{13,5},{2,10},{6,14},... | collective-permute-start | bytes 1179656 | tf_op jit(solution)/shard_map/ppermute | solution.py:139
  5.0 2.8 %copy-start.5 = (bf16[3,2,128,512]{3,2,1,0:T(8,128)(2,1)S(1)}, bf16[3,2,128,512]{3,2,1,0:T(8,128)(2,1)}, u32[]{:S(2)}) copy-start(bf16[3,2,128,512]{3,2,1,0:T(8,128)(2,1)} %refs_0_.3) | copy-start | bytes 2359300
  5.0 33.3 %collective-permute-start.8 = (bf16[3,1,128,512]{3,2,1,0:T(8,128)(2,1)S(1)}, bf16[3,1,128,512]{3,2,1,0:T(8,128)(2,1)}, u32[]{:S(2)}, u32[]{:S(2)}) collective-permute-start(bf16[3,1,128,512]{3,2,1,0:T(8,128)(2,1)S(1)} %get-tuple-element.11.refs_0_), channel_id=1, source_target_pairs={{16,0},{0,16},{17,1},{1,17},{18,2},{2,18},{19,3},{3,19},{20,4},{4,... | collective-permute-start | bytes 1179656 | tf_op jit(solution)/shard_map/ppermute | solution.py:148
  7.3 34.4 %collective-permute-start = (bf16[3,1,128,512]{3,2,1,0:T(8,128)(2,1)}, bf16[3,1,128,512]{3,2,1,0:T(8,128)(2,1)S(1)}, u32[]{:S(2)}, u32[]{:S(2)}) collective-permute-start(bf16[3,1,128,512]{3,2,1,0:T(8,128)(2,1)} %get-tuple-element.12), channel_id=1, source_target_pairs={{0,8},{4,12},{8,0},{12,4},{1,9},{5,13},{9,1},{13,5},{2,10},{6,14},... | collective-permute-start | bytes 1179656 | tf_op jit(solution)/shard_map/ppermute | solution.py:139
  7.8 41.4 %collective-permute-start.1 = (bf16[3,1,128,512]{3,2,1,0:T(8,128)(2,1)S(1)}, bf16[3,1,128,512]{3,2,1,0:T(8,128)(2,1)S(1)}, u32[]{:S(2)}, u32[]{:S(2)}) collective-permute-start(bf16[3,1,128,512]{3,2,1,0:T(8,128)(2,1)S(1)} %get-tuple-element.13.refs_0_), channel_id=1, source_target_pairs={{0,4},{4,0},{8,12},{12,8},{1,5},{5,1},{9,13},{13,9},{2,6},{6,2},{1... | collective-permute-start | bytes 1179656 | tf_op jit(solution)/shard_map/ppermute | solution.py:145
  7.8 26.1 %collective-permute-start.3 = (bf16[3,2,128,512]{3,2,1,0:T(8,128)(2,1)S(1)}, bf16[3,2,128,512]{3,2,1,0:T(8,128)(2,1)S(1)}, u32[]{:S(2)}, u32[]{:S(2)}) collective-permute-start(bf16[3,2,128,512]{3,2,1,0:T(8,128)(2,1)S(1)} %copy-done.5), channel_id=1, source_target_pairs={{16,0},{0,16},{17,1},{1,17},{18,2},{2,18},{19,3},{3,19},{20,4},{4,... | collective-permute-start | bytes 2359304 | tf_op jit(solution)/shard_map/ppermute | solution.py:148
  7.9 0.7 copy-start.11
  8.9 0.7 copy-start.12
  23.5 18.7 %collective-permute-start.10 = (bf16[3,1,128,512]{3,2,1,0:T(8,128)(2,1)}, bf16[3,1,128,512]{3,2,1,0:T(8,128)(2,1)}, u32[]{:S(2)}, u32[]{:S(2)}) collective-permute-start(bf16[3,1,128,512]{3,2,1,0:T(8,128)(2,1)} %collective-permute-done.9.refs_0_), channel_id=1, source_target_pairs={{16,0},{0,16},{17,1},{1,17},{18,2},{2,18},{19,3},{3,19},{20,4},{4,... | collective-permute-start | bytes 1179656 | tf_op jit(solution)/shard_map/ppermute | solution.py:148
  33.9 0.9 %copy-start.6 = (bf16[3,2,128,512]{3,2,1,0:T(8,128)(2,1)}, bf16[3,2,128,512]{3,2,1,0:T(8,128)(2,1)S(1)}, u32[]{:S(2)}) copy-start(bf16[3,2,128,512]{3,2,1,0:T(8,128)(2,1)S(1)} %collective-permute-done.3.refs_1_) | copy-start | bytes 2359300
  38.2 11.5 %collective-permute-start.4 = (bf16[3,1,128,512]{3,2,1,0:T(8,128)(2,1)}, bf16[3,1,128,512]{3,2,1,0:T(8,128)(2,1)S(1)}, u32[]{:S(2)}, u32[]{:S(2)}) collective-permute-start(bf16[3,1,128,512]{3,2,1,0:T(8,128)(2,1)} %mix.5), channel_id=1, source_target_pairs={{0,8},{4,12},{8,0},{12,4},{1,9},{5,13},{9,1},{13,5},{2,10},{6,14},... | collective-permute-start | bytes 1179656 | tf_op jit(solution)/shard_map/ppermute | solution.py:139
  41.7 8.1 %collective-permute-start.11 = (bf16[3,1,128,512]{3,2,1,0:T(8,128)(2,1)}, bf16[3,1,128,512]{3,2,1,0:T(8,128)(2,1)S(1)}, u32[]{:S(2)}, u32[]{:S(2)}) collective-permute-start(bf16[3,1,128,512]{3,2,1,0:T(8,128)(2,1)} %mix.6.refs_4_), channel_id=1, source_target_pairs={{0,4},{4,0},{8,12},{12,8},{1,5},{5,1},{9,13},{13,9},{2,6},{6,2},{1... | collective-permute-start | bytes 1179656 | tf_op jit(solution)/shard_map/ppermute | solution.py:145
  41.7 8.1 %collective-permute-start.2 = (bf16[3,1,128,512]{3,2,1,0:T(8,128)(2,1)S(1)}, bf16[3,1,128,512]{3,2,1,0:T(8,128)(2,1)S(1)}, u32[]{:S(2)}, u32[]{:S(2)}) collective-permute-start(bf16[3,1,128,512]{3,2,1,0:T(8,128)(2,1)S(1)} %collective-permute-done.refs_1_), channel_id=1, source_target_pairs={{0,4},{4,0},{8,12},{12,8},{1,5},{5,1},{9,13},{13,9},{2,6},{6,2},{1... | collective-permute-start | bytes 1179656 | tf_op jit(solution)/shard_map/ppermute | solution.py:145
  45.6 4.2 %collective-permute-start.12 = (bf16[3,1,128,512]{3,2,1,0:T(8,128)(2,1)}, bf16[3,1,128,512]{3,2,1,0:T(8,128)(2,1)S(1)}, u32[]{:S(2)}, u32[]{:S(2)}) collective-permute-start(bf16[3,1,128,512]{3,2,1,0:T(8,128)(2,1)} %mix.7.refs_5_), channel_id=1, source_target_pairs={{0,4},{4,0},{8,12},{12,8},{1,5},{5,1},{9,13},{13,9},{2,6},{6,2},{1... | collective-permute-start | bytes 1179656 | tf_op jit(solution)/shard_map/ppermute | solution.py:145
  45.7 4.9 %copy-start.1 = (bf16[3,1,128,512]{3,2,1,0:T(8,128)(2,1)S(1)}, bf16[3,1,128,512]{3,2,1,0:T(8,128)(2,1)}, u32[]{:S(2)}) copy-start(bf16[3,1,128,512]{3,2,1,0:T(8,128)(2,1)} %mix.6.refs_4_) | copy-start | bytes 1179652
  45.7 4.9 %copy-start.2 = (bf16[3,1,128,512]{3,2,1,0:T(8,128)(2,1)S(1)}, bf16[3,1,128,512]{3,2,1,0:T(8,128)(2,1)}, u32[]{:S(2)}) copy-start(bf16[3,1,128,512]{3,2,1,0:T(8,128)(2,1)} %mix.7.refs_5_) | copy-start | bytes 1179652
  49.2 11.6 %collective-permute-start.5 = (bf16[3,1,128,512]{3,2,1,0:T(8,128)(2,1)}, bf16[3,1,128,512]{3,2,1,0:T(8,128)(2,1)}, u32[]{:S(2)}, u32[]{:S(2)}) collective-permute-start(bf16[3,1,128,512]{3,2,1,0:T(8,128)(2,1)} %mix.4.refs_4_), channel_id=1, source_target_pairs={{0,4},{4,0},{8,12},{12,8},{1,5},{5,1},{9,13},{13,9},{2,6},{6,2},{1... | collective-permute-start | bytes 1179656 | tf_op jit(solution)/shard_map/ppermute | solution.py:145
  49.6 11.1 %collective-permute-start.6 = (bf16[3,1,128,512]{3,2,1,0:T(8,128)(2,1)S(1)}, bf16[3,1,128,512]{3,2,1,0:T(8,128)(2,1)}, u32[]{:S(2)}, u32[]{:S(2)}) collective-permute-start(bf16[3,1,128,512]{3,2,1,0:T(8,128)(2,1)S(1)} %collective-permute-done.4.refs_5_), channel_id=1, source_target_pairs={{0,4},{4,0},{8,12},{12,8},{1,5},{5,1},{9,13},{13,9},{2,6},{6,2},{1... | collective-permute-start | bytes 1179656 | tf_op jit(solution)/shard_map/ppermute | solution.py:145
  49.8 11.0 %copy-start = (bf16[3,1,128,512]{3,2,1,0:T(8,128)(2,1)S(1)}, bf16[3,1,128,512]{3,2,1,0:T(8,128)(2,1)}, u32[]{:S(2)}) copy-start(bf16[3,1,128,512]{3,2,1,0:T(8,128)(2,1)} %mix.4.refs_4_) | copy-start | bytes 1179652
  49.8 0.7 copy-start.3
  50.6 1.0 %copy-start.4 = (bf16[3,1,128,512]{3,2,1,0:T(8,128)(2,1)S(1)}, bf16[3,1,128,512]{3,2,1,0:T(8,128)(2,1)}, u32[]{:S(2)}) copy-start(bf16[3,1,128,512]{3,2,1,0:T(8,128)(2,1)} %copy-done.3) | copy-start | bytes 1179652
  58.7 12.3 %collective-permute-start.13 = (bf16[3,1,128,512]{3,2,1,0:T(8,128)(2,1)}, bf16[3,1,128,512]{3,2,1,0:T(8,128)(2,1)S(1)}, u32[]{:S(2)}, u32[]{:S(2)}) collective-permute-start(bf16[3,1,128,512]{3,2,1,0:T(8,128)(2,1)} %get-tuple-element.9), channel_id=1, source_target_pairs={{0,8},{4,12},{8,0},{12,4},{1,9},{5,13},{9,1},{13,5},{2,10},{6,14},... | collective-permute-start | bytes 1179656 | tf_op jit(solution)/shard_map/ppermute | solution.py:139
  66.2 12.9 %collective-permute-start.7 = (bf16[3,1,128,512]{3,2,1,0:T(8,128)(2,1)S(1)}, bf16[3,1,128,512]{3,2,1,0:T(8,128)(2,1)S(1)}, u32[]{:S(2)}, u32[]{:S(2)}) collective-permute-start(bf16[3,1,128,512]{3,2,1,0:T(8,128)(2,1)S(1)} %get-tuple-element.7), channel_id=1, source_target_pairs={{0,8},{4,12},{8,0},{12,4},{1,9},{5,13},{9,1},{13,5},{2,10},{6,14},... | collective-permute-start | bytes 1179656 | tf_op jit(solution)/shard_map/ppermute | solution.py:139
  71.0 8.1 %copy-start.9 = (bf16[3,2,128,512]{3,2,1,0:T(8,128)(2,1)}, bf16[3,2,128,512]{3,2,1,0:T(8,128)(2,1)S(1)}, u32[]{:S(2)}) copy-start(bf16[3,2,128,512]{3,2,1,0:T(8,128)(2,1)S(1)} %constant_dynamic-update-slice_fusion) | copy-start | bytes 2359300
  79.2 0.9 %copy-start.8 = (bf16[3,2,128,512]{3,2,1,0:T(8,128)(2,1)}, bf16[3,2,128,512]{3,2,1,0:T(8,128)(2,1)S(1)}, u32[]{:S(2)}) copy-start(bf16[3,2,128,512]{3,2,1,0:T(8,128)(2,1)S(1)} %constant_dynamic-update-slice_fusion.2) | copy-start | bytes 2359300

commit v2 on v1

--- a/solution.py
+++ b/solution.py
@@ -16,10 +16,9 @@
     ins, out_ref = refs[:sources], refs[sources]
     e, blocks, rows, _ = out_ref.shape
     step = 16
-    weights = [
-        [weight_ref[n, m] for m in range(sources * e)] for n in range(e)
-    ]
+    weights = [[weight_ref[n, m] for m in range(sources * e)] for n in range(e)]
     for b in range(blocks):
+        block = index_ref[0] * blocks + b
 
         @pl.loop(0, rows // step)
         def _(i):
@@ -27,7 +26,7 @@
             totals = [None] * e
             for t in range(sources):
                 for m in range(e):
-                    g = ins[t][m, b, at, :].astype(jnp.float32)
+                    g = ins[t][m, block, at, :].astype(jnp.float32)
                     for n in range(e):
                         term = weights[n][t * e + m] * g
                         totals[n] = term if totals[n] is None else totals[n] + term
@@ -37,17 +36,13 @@
 
 def mix(ins, index, weights, owned):
     e, _, rows, o = ins[0].shape
-    chunk = math.gcd(rows, 32)
-    spec = pl.BlockSpec((e, owned, chunk, o), lambda i, at: (0, at[0], i, 0))
+    scalars, whole = pl.BlockSpec(memory_space=pltpu.SMEM), pl.BlockSpec(memory_space=pltpu.VMEM)
     return pl.pallas_call(
         functools.partial(mix_kernel, len(ins)),
-        grid_spec=pltpu.PrefetchScalarGridSpec(
-            num_scalar_prefetch=1,
-            grid=(rows // chunk,),
-            in_specs=[pl.BlockSpec(memory_space=pltpu.SMEM)] + [spec] * len(ins),
-            out_specs=pl.BlockSpec((e, owned, chunk, o), lambda i, at: (0, 0, i, 0)),
-        ),
+        in_specs=[scalars, scalars] + [whole] * len(ins),
+        out_specs=whole,
         out_shape=jax.ShapeDtypeStruct((e, owned, rows, o), BF16),
+        compiler_params=pltpu.CompilerParams(vmem_limit_bytes=32 * 1024 * 1024),
         cost_estimate=pl.CostEstimate(
             flops=2 * len(ins) * e * e * owned * rows * o,
             bytes_accessed=2 * (len(ins) + 1) * e * owned * rows * o,
@@ -59,58 +54,43 @@
 
 def product_kernel(pieces, lefts, place_ref, *refs):
     a_in, s_in = refs[:pieces], refs[pieces : 2 * pieces]
-    outs = refs[2 * pieces : 2 * pieces + lefts]
-    a_full, s_full, sems = refs[2 * pieces + lefts :]
+    outs = refs[2 * pieces :]
     e, blocks, rows, _ = outs[0].shape
-    copies = []
+    spans = [pl.ds(pl.multiple_of(place_ref[j] * rows, rows), rows) for j in range(pieces)]
     for n in range(e):
-        batch = []
-        for k, (ins, full) in enumerate(((a_in, a_full), (s_in, s_full))):
-            for i in range(pieces):
-                at = pl.ds(pl.multiple_of(place_ref[i] * rows, rows), rows)
-                batch.append(
-                    pltpu.make_async_copy(
-                        ins[i].at[n], full.at[n, :, at, :], sems.at[n, k, i]
-                    )
-                )
-        for copy in batch:
-            copy.start()
-        copies.append(batch)
-    for n in range(e):
-        for copy in copies[n]:
-            copy.wait()
         for b in range(blocks):
             left = jnp.concatenate(
                 [
-                    a_full[n, b, pl.ds(pl.multiple_of(place_ref[i] * rows, rows), rows), :]
+                    jnp.concatenate([a_in[i][n, b, :, at] for at in spans], axis=1)
                     for i in range(lefts)
                 ],
                 axis=0,
             )
             first = jnp.dot(
-                left, s_full[n, b], preferred_element_type=jnp.float32
+                left,
+                jnp.concatenate([s[n, b] for s in s_in], axis=0),
+                preferred_element_type=jnp.float32,
             ).astype(BF16)
             both = lax.dot_general(
                 first,
-                a_full[n, b],
+                jnp.concatenate([a[n, b] for a in a_in], axis=0),
                 (((1,), (1,)), ((), ())),
                 preferred_element_type=jnp.float32,
             ).astype(BF16)
             for i in range(lefts):
-                outs[i][n, b] = both[i * rows : (i + 1) * rows]
+                for j, at in enumerate(spans):
+                    outs[i][n, b, :, at] = both[i * rows : (i + 1) * rows, j * rows : (j + 1) * rows]
 
 
 def product(a_pieces, s_pieces, places, lefts):
     pieces = len(a_pieces)
     e, blocks, rows, o = a_pieces[0].shape
-    anywhere = pl.BlockSpec(memory_space=pl.ANY)
-    full = pltpu.VMEM((e, blocks, pieces * rows, o), BF16)
+    whole = pl.BlockSpec(memory_space=pltpu.VMEM)
     return pl.pallas_call(
         functools.partial(product_kernel, pieces, lefts),
-        in_specs=[pl.BlockSpec(memory_space=pltpu.SMEM)] + [anywhere] * (2 * pieces),
-        out_specs=[pl.BlockSpec(memory_space=pltpu.VMEM)] * lefts,
+        in_specs=[pl.BlockSpec(memory_space=pltpu.SMEM)] + [whole] * (2 * pieces),
+        out_specs=[whole] * lefts,
         out_shape=[jax.ShapeDtypeStruct((e, blocks, rows, o), BF16)] * lefts,
-        scratch_shapes=[full, full, pltpu.SemaphoreType.DMA((e, 2, pieces))],
         compiler_params=pltpu.CompilerParams(vmem_limit_bytes=32 * 1024 * 1024),
         cost_estimate=pl.CostEstimate(
             flops=4 * e * blocks * lefts * rows * o * o,
@@ -130,7 +110,7 @@
         lanes = ph // owners
         owned = nb // owners
         en_at, ph_at = lax.axis_index("en"), lax.axis_index("ph")
-        owner, lane = ph_at // lanes, ph_at % lanes
+        owner, lane = lax.div(ph_at, lanes), lax.rem(ph_at, lanes)
 
         def to_owner(x, d):
             pairs = [
@@ -154,21 +134,13 @@
         shifts = [t for t in range(1, en) if t <= reach or en - t <= reach]
         sources = len(shifts) + 1
 
-        lesser_from = [lesser_in] + [to_energy(lesser_in, t) for t in shifts]
-        greater_own = blocks_of(greater_in, owner)
-        greater_rows = [greater_own] + [
-            to_owner(blocks_of(greater_in, (owner + d) % owners), d) for d in range(1, owners)
-        ]
-        inverse_rows = [blocks_of(inverse, owner)] + [
-            to_owner(blocks_of(inverse, (owner + d) % owners), d) for d in range(1, owners)
-        ]
-
-        small = lax.all_gather(
-            jnp.stack([offsets.astype(jnp.float32), couplings]), "ph", axis=2, tiled=True
+        own = jnp.stack([offsets.astype(jnp.float32), couplings])
+        small = jnp.concatenate(
+            [own]
+            + [lax.ppermute(own, "ph", [((p + q) % ph, p) for p in range(ph)]) for q in range(1, ph)],
+            axis=2,
         )
-        away = jnp.stack(
-            [((en_at + t) % en - en_at) * e for t in [0] + shifts]
-        )
+        away = jnp.stack([((en_at + t) % en - en_at) * e for t in [0] + shifts])
         apart = (away[:, None] + jnp.arange(e)[None, :]).reshape(1, -1) - jnp.arange(e)[:, None]
         weights = jnp.sum(
             jnp.where(
@@ -179,6 +151,15 @@
             axis=2,
         )
 
+        lesser_from = [lesser_in] + [to_energy(lesser_in, t) for t in shifts]
+        inverse_rows = [blocks_of(inverse, owner)] + [
+            to_owner(blocks_of(inverse, (owner + d) % owners), d) for d in range(1, owners)
+        ]
+        greater_in, small = lax.optimization_barrier((greater_in, small))
+        greater_rows = [blocks_of(greater_in, owner)] + [
+            to_owner(blocks_of(greater_in, (owner + d) % owners), d) for d in range(1, owners)
+        ]
+
         zero = jnp.zeros((), jnp.int32)
         lesser_rows = [None] * owners
         for d in range(1, owners):

time: 80.6 us -> 72.1 us (0.89)
  waiting for transfers between devices: 20.3 us -> 39.9 us
  Pallas kernels: 26.4 us -> 8.95 us
  blocking collectives: 13.9 us -> 0 us
  starting transfers between devices: 10.2 us -> 14.4 us
  local copies, waits for them, and re-layouts: 7.46 us -> 6.54 us
    all_gather x1 -> x0, blocking collectives: 13.9 us -> none  [on_device(): lax.all_gather(jnp.stack([offsets.astype(jnp.float32), couplings]), 'ph',...]
    ppermute x5, waiting for transfers between devices: 12.5 us -> 26.2 us  [to_owner(): return lax.ppermute(x, 'ph', pairs)]
    pallas_call x4, Pallas kernels: 13.8 us -> 3.9 us  [mix(): pl.pallas_call(functools.partial(mix_kernel, len(ins)), in_specs=[scalars...]
    pallas_call x2, Pallas kernels: 12.6 us -> 5.05 us  [product(): pl.pallas_call(functools.partial(product_kernel, pieces, lefts), in_specs...]
    ppermute x3, waiting for transfers between devices: 7.71 us -> 13.6 us  [to_energy(): return lax.ppermute(x, 'en', [((i + t) % en, i) for i in range(en)])]
    unnamed x26 -> x13, local copies, waits for them, and re-layouts: 4.88 us -> 1.57 us
    ppermute x0 -> x3, starting transfers between devices: none -> 3.2 us  [on_device(): lax.ppermute(own, 'ph', [((p + q) % ph, p) for p in range(ph)])]
    ppermute x0 -> x3, local copies, waits for them, and re-layouts: none -> 1.61 us  [on_device(): lax.ppermute(own, 'ph', [((p + q) % ph, p) for p in range(ph)])]
  transfers between devices with their start and end apart: 14 -> 17, of which waited for: 3 -> 7; matrix products, arithmetic and copies ran while one was open for 3% -> 8% of each run, Pallas kernels for 33% -> 12%
where the time goes in v2:
time: 72.1 us; the launch traced here: 71.8 us
  waiting for transfers between devices  39.9 us (55%)
  starting transfers between devices  14.4 us (20%)
  Pallas kernels  8.95 us (12%)
  local copies, waits for them, and re-layouts  6.54 us (9%)
  other arithmetic  1.15 us (2%)
  between operations  0.82 us (1%)
    ppermute x5, waiting for transfers between devices, to_owner(): return lax.ppermute(x, 'ph', pairs)  26.2 us
    ppermute x3, waiting for transfers between devices, to_energy(): return lax.ppermute(x, 'en', [((i + t) % en, i) for i in range(en)])  13.6 us
    ppermute x5, starting transfers between devices, to_owner(): return lax.ppermute(x, 'ph', pairs)  6.41 us
    pallas_call x2, Pallas kernels, product(): pl.pallas_call(functools.partial(product_kernel, pieces, lefts), in_specs...  5.05 us
    pallas_call x4, Pallas kernels, mix(): pl.pallas_call(functools.partial(mix_kernel, len(ins)), in_specs=[scalars...  3.9 us
    ppermute x3, starting transfers between devices, to_energy(): return lax.ppermute(x, 'en', [((i + t) % en, i) for i in range(en)])  3.52 us
    ppermute x3, starting transfers between devices, on_device(): lax.ppermute(own, 'ph', [((p + q) % ph, p) for p in range(ph)])  3.2 us
    ppermute x3, local copies, waits for them, and re-layouts, on_device(): lax.ppermute(own, 'ph', [((p + q) % ph, p) for p in range(ph)])  1.61 us
  transfers between devices with their start and end apart: 17, of which 7 were waited for; matrix products, arithmetic and copies ran while one was open for 8% of the time, Pallas kernels for 12%

profile of v2, /device:TPU:0, one launch (start us, length us, event | category | flops | bytes accessed | tf_op | source)
XLA Modules:
  0.0 71.8 jit_solution(2990352300758937677)
XLA Ops:
  0.6 0.7 convert_bitcast_fusion
  1.3 0.7 copy-done.4
  2.0 2.4 %collective-permute-start.3 = (f32[2,3,2]{1,2,0:T(2,128)S(1)}, f32[2,3,2]{1,2,0:T(2,128)S(1)}, u32[]{:S(2)}, u32[]{:S(2)}) collective-permute-start(f32[2,3,2]{1,2,0:T(2,128)S(1)} %pad_maximum_fusion.1), channel_id=1, source_target_pairs={{4,0},{8,4},{12,8},{0,12},{5,1},{9,5},{13,9},{1,13},{6,2},{10,6},{... | collective-permute-start | bytes 152 | tf_op jit(solution)/shard_map/ppermute | solution.py:140
  4.4 0.6 collective-permute-start.4
  5.0 0.2 collective-permute-start.5
  5.2 1.3 %constant_dynamic-slice_fusion.2 = (bf16[3,1,128,512]{3,2,1,0:T(8,128)(2,1)S(1)}, bf16[3,1,128,512]{3,2,1,0:T(8,128)(2,1)S(1)}) fusion(bf16[3,2,128,512]{3,2,1,0:T(8,128)(2,1)} %param.7, s32[]{:T(128)S(6)} %select_n.75, s32[]{:T(128)S(6)} %select_n.73), kind=kLoop, calls=%fused_computation.12 | loop fusion | bytes 1572872 | tf_op jit(solution)/shard_map/dynamic_slice | solution.py:131
  6.5 1.3 %collective-permute-start = (bf16[3,1,128,512]{3,2,1,0:T(8,128)(2,1)S(1)}, bf16[3,1,128,512]{3,2,1,0:T(8,128)(2,1)S(1)}, u32[]{:S(2)}, u32[]{:S(2)}) collective-permute-start(bf16[3,1,128,512]{3,2,1,0:T(8,128)(2,1)S(1)} %get-tuple-element.14), channel_id=1, source_target_pairs={{0,8},{4,12},{8,0},{12,4},{1,9},{5,13},{9,1},{13,5},{2,10},{6,14},... | collective-permute-start | bytes 1179656 | tf_op jit(solution)/shard_map/ppermute | solution.py:119
  7.8 0.5 collective-permute-start.1
  8.2 0.1 copy.13
  8.3 0.1 pad_add_fusion.1
  8.4 0.1 iota_add_fusion
  8.5 0.6 add.108
  9.1 0.0 collective-permute-done.3
  9.1 0.0 copy-done
  9.1 1.5 %collective-permute-start.6 = (bf16[3,2,128,512]{3,2,1,0:T(8,128)(2,1)S(1)}, bf16[3,2,128,512]{3,2,1,0:T(8,128)(2,1)S(1)}, u32[]{:S(2)}, u32[]{:S(2)}) collective-permute-start(bf16[3,2,128,512]{3,2,1,0:T(8,128)(2,1)S(1)} %copy-done), channel_id=1, source_target_pairs={{16,0},{0,16},{17,1},{1,17},{18,2},{2,18},{19,3},{3,19},{20,4},{4,... | collective-permute-start | bytes 2359304 | tf_op jit(solution)/shard_map/ppermute | solution.py:128
  10.6 0.1 copy.14
  10.7 0.0 collective-permute-done.4
  10.7 0.8 %copy.15 = f32[2,3,2]{2,0,1:T(2,128)S(1)} copy(f32[2,3,2]{1,2,0:T(2,128)} %collective-permute-done.4) | data formatting | bytes 96 | tf_op jit(solution)/shard_map/ppermute | solution.py:140
  11.5 0.0 collective-permute-done.5
  11.5 0.8 %copy.16 = f32[2,3,2]{2,0,1:T(2,128)S(1)} copy(f32[2,3,2]{1,2,0:T(2,128)} %collective-permute-done.5) | data formatting | bytes 96 | tf_op jit(solution)/shard_map/ppermute | solution.py:140
  12.3 0.1 pad_maximum_fusion
  12.3 0.0 copy-done.3
  12.3 0.1 constant_dynamic-slice_fusion
  12.4 0.0 copy-start.5
  12.4 1.5 %collective-permute-start.12 = (bf16[3,1,128,512]{3,2,1,0:T(8,128)(2,1)S(1)}, bf16[3,1,128,512]{3,2,1,0:T(8,128)(2,1)S(1)}, u32[]{:S(2)}, u32[]{:S(2)}) collective-permute-start(bf16[3,1,128,512]{3,2,1,0:T(8,128)(2,1)S(1)} %get-tuple-element.12), channel_id=1, source_target_pairs={{0,8},{4,12},{8,0},{12,4},{1,9},{5,13},{9,1},{13,5},{2,10},{6,14},... | collective-permute-start | bytes 1179656 | tf_op jit(solution)/shard_map/ppermute | solution.py:119
  13.9 0.0 copy-done.5
  13.9 0.5 collective-permute-start.11
  14.5 12.2 %collective-permute-done.12.refs_0_ = bf16[3,1,128,512]{3,2,1,0:T(8,128)(2,1)S(1)} collective-permute-done((bf16[3,1,128,512]{3,2,1,0:T(8,128)(2,1)S(1)}, bf16[3,1,128,512]{3,2,1,0:T(8,128)(2,1)S(1)}, u32[]{:S(2)}, u32[]{:S(2)}) %collective-permute-start.12) | collective-permute-done | bytes 393248 | tf_op jit(solution)/shard_map/ppermute | solution.py:119
  26.7 1.5 %collective-permute-start.13 = (bf16[3,1,128,512]{3,2,1,0:T(8,128)(2,1)S(1)}, bf16[3,1,128,512]{3,2,1,0:T(8,128)(2,1)S(1)}, u32[]{:S(2)}, u32[]{:S(2)}) collective-permute-start(bf16[3,1,128,512]{3,2,1,0:T(8,128)(2,1)S(1)} %collective-permute-done.12.refs_0_), channel_id=1, source_target_pairs={{16,0},{0,16},{17,1},{1,17},{18,2},{2,18},{19,3},{3,19},{20,4},{4,... | collective-permute-start | bytes 1179656 | tf_op jit(solution)/shard_map/ppermute | solution.py:128
  28.2 0.2 select_reduce_fusion.weight_ref
  28.3 1.2 %collective-permute-done.6.refs_1_ = bf16[3,2,128,512]{3,2,1,0:T(8,128)(2,1)S(1)} collective-permute-done((bf16[3,2,128,512]{3,2,1,0:T(8,128)(2,1)S(1)}, bf16[3,2,128,512]{3,2,1,0:T(8,128)(2,1)S(1)}, u32[]{:S(2)}, u32[]{:S(2)}) %collective-permute-start.6) | collective-permute-done | bytes 786464 | tf_op jit(solution)/shard_map/ppermute | solution.py:128
  29.5 1.0 %mix.5 = bf16[3,1,128,512]{3,2,1,0:T(8,128)(2,1)S(1)} custom-call(s32[1]{0:T(128)} %bitcast.9.index_ref, f32[3,6]{1,0:T(4,128)S(1)} %select_reduce_fusion.weight_ref, bf16[3,2,128,512]{3,2,1,0:T(8,128)(2,1)S(1)} %copy-done, bf16[3,2,128,512]{3,2,1,0:T(8,128)(2,1)S(1)} %collective-permute-done.6.refs_1_), custom_call_target="tpu_custom_call" | custom-call | flops 2359296 | bytes 1179648 | tf_op jit(solution)/shard_map/mix/pallas_call | solution.py:40
  30.5 1.5 %collective-permute-start.7 = (bf16[3,1,128,512]{3,2,1,0:T(8,128)(2,1)S(1)}, bf16[3,1,128,512]{3,2,1,0:T(8,128)(2,1)}, u32[]{:S(2)}, u32[]{:S(2)}) collective-permute-start(bf16[3,1,128,512]{3,2,1,0:T(8,128)(2,1)S(1)} %mix.5), channel_id=1, source_target_pairs={{0,8},{4,12},{8,0},{12,4},{1,9},{5,13},{9,1},{13,5},{2,10},{6,14},... | collective-permute-start | bytes 1179656 | tf_op jit(solution)/shard_map/ppermute | solution.py:119
  32.0 0.0 collective-permute-done.refs_1_
  32.0 0.0 collective-permute-start.2
  32.0 6.0 %collective-permute-done.11.refs_1_ = bf16[3,1,128,512]{3,2,1,0:T(8,128)(2,1)S(1)} collective-permute-done((bf16[3,1,128,512]{3,2,1,0:T(8,128)(2,1)S(1)}, bf16[3,1,128,512]{3,2,1,0:T(8,128)(2,1)S(1)}, u32[]{:S(2)}, u32[]{:S(2)}) %collective-permute-start.11) | collective-permute-done | bytes 393248 | tf_op jit(solution)/shard_map/ppermute | solution.py:128
  38.0 1.0 %mix.6.refs_4_ = bf16[3,1,128,512]{3,2,1,0:T(8,128)(2,1)S(1)} custom-call(s32[1]{0:T(128)} %constant.84.clone.1.index_ref, f32[3,6]{1,0:T(4,128)S(1)} %select_reduce_fusion.weight_ref, bf16[3,1,128,512]{3,2,1,0:T(8,128)(2,1)S(1)} %get-tuple-element.13.refs_0_, bf16[3,1,128,512]{3,2,1,0:T(8,128)(2,1)S(1)} %collective-permute-done.11.refs_1_), custom_call_target="tpu_custom_call" | custom-call | flops 2359296 | bytes 1179648 | tf_op jit(solution)/shard_map/mix/pallas_call | solution.py:40
  39.0 0.1 collective-permute-start.14
  39.0 6.5 %collective-permute-done.13.refs_1_ = bf16[3,1,128,512]{3,2,1,0:T(8,128)(2,1)S(1)} collective-permute-done((bf16[3,1,128,512]{3,2,1,0:T(8,128)(2,1)S(1)}, bf16[3,1,128,512]{3,2,1,0:T(8,128)(2,1)S(1)}, u32[]{:S(2)}, u32[]{:S(2)}) %collective-permute-start.13) | collective-permute-done | bytes 393248 | tf_op jit(solution)/shard_map/ppermute | solution.py:128
  45.5 1.0 %mix.7.refs_5_ = bf16[3,1,128,512]{3,2,1,0:T(8,128)(2,1)S(1)} custom-call(s32[1]{0:T(128)} %constant.84.clone.1.index_ref, f32[3,6]{1,0:T(4,128)S(1)} %select_reduce_fusion.weight_ref, bf16[3,1,128,512]{3,2,1,0:T(8,128)(2,1)S(1)} %collective-permute-done.12.refs_0_, bf16[3,1,128,512]{3,2,1,0:T(8,128)(2,1)S(1)} %collective-permute-done.13.refs_1_), custom_call_target="tpu_custom_call" | custom-call | flops 2359296 | bytes 1179648 | tf_op jit(solution)/shard_map/mix/pallas_call | solution.py:40
  46.5 0.1 collective-permute-start.15
  46.6 1.0 %mix.4.refs_4_ = bf16[3,1,128,512]{3,2,1,0:T(8,128)(2,1)S(1)} custom-call(s32[1]{0:T(128)} %bitcast.4.index_ref, f32[3,6]{1,0:T(4,128)S(1)} %select_reduce_fusion.weight_ref, bf16[3,2,128,512]{3,2,1,0:T(8,128)(2,1)S(1)} %copy-done, bf16[3,2,128,512]{3,2,1,0:T(8,128)(2,1)S(1)} %collective-permute-done.6.refs_1_), custom_call_target="tpu_custom_call" | custom-call | flops 2359296 | bytes 1179648 | tf_op jit(solution)/shard_map/mix/pallas_call | solution.py:40
  47.6 0.0 collective-permute-done.1.refs_2_
  47.6 0.6 collective-permute-start.8
  48.1 0.0 collective-permute-done.7.refs_5_
  48.1 0.1 collective-permute-start.9
  48.2 0.1 pad_add_fusion.place_ref
  48.3 0.0 collective-permute-done.2.refs_3_
  48.3 0.0 collective-permute-done.14.refs_6_
  48.3 0.1 collective-permute-done.15.refs_7_
  48.4 2.6 %product.3 = (bf16[3,1,128,512]{3,2,1,0:T(8,128)(2,1)S(1)}, bf16[3,1,128,512]{3,2,1,0:T(8,128)(2,1)S(1)}) custom-call(s32[4]{0:T(128)S(1)} %pad_add_fusion.place_ref, bf16[3,1,128,512]{3,2,1,0:T(8,128)(2,1)S(1)} %get-tuple-element.15.refs_0_, bf16[3,1,128,512]{3,2,1,0:T(8,128)(2,1)S(1)} %collective-permute-done.refs_1_, ...), custom_call_target="tpu_custom_call" | custom-call | flops 805306368 | bytes 3932160 | tf_op jit(solution)/shard_map/product/pallas_call | solution.py:89
  51.0 1.4 %collective-permute-start.16 = (bf16[3,1,128,512]{3,2,1,0:T(8,128)(2,1)S(1)}, bf16[3,1,128,512]{3,2,1,0:T(8,128)(2,1)}, u32[]{:S(2)}, u32[]{:S(2)}) collective-permute-start(bf16[3,1,128,512]{3,2,1,0:T(8,128)(2,1)S(1)} %get-tuple-element.11), channel_id=1, source_target_pairs={{0,8},{4,12},{8,0},{12,4},{1,9},{5,13},{9,1},{13,5},{2,10},{6,14},... | collective-permute-start | bytes 1179656 | tf_op jit(solution)/shard_map/ppermute | solution.py:119
  52.4 0.0 collective-permute-done.8.refs_6_
  52.4 0.0 collective-permute-done.9.refs_7_
  52.4 2.5 %product.2 = (bf16[3,1,128,512]{3,2,1,0:T(8,128)(2,1)S(1)}, bf16[3,1,128,512]{3,2,1,0:T(8,128)(2,1)S(1)}) custom-call(s32[4]{0:T(128)S(1)} %pad_add_fusion.place_ref, bf16[3,1,128,512]{3,2,1,0:T(8,128)(2,1)S(1)} %get-tuple-element.15.refs_0_, bf16[3,1,128,512]{3,2,1,0:T(8,128)(2,1)S(1)} %collective-permute-done.refs_1_, ...), custom_call_target="tpu_custom_call" | custom-call | flops 805306368 | bytes 3932160 | tf_op jit(solution)/shard_map/product/pallas_call | solution.py:89
  54.9 0.7 %collective-permute-start.10 = (bf16[3,1,128,512]{3,2,1,0:T(8,128)(2,1)S(1)}, bf16[3,1,128,512]{3,2,1,0:T(8,128)(2,1)S(1)}, u32[]{:S(2)}, u32[]{:S(2)}) collective-permute-start(bf16[3,1,128,512]{3,2,1,0:T(8,128)(2,1)S(1)} %get-tuple-element.8), channel_id=1, source_target_pairs={{0,8},{4,12},{8,0},{12,4},{1,9},{5,13},{9,1},{13,5},{2,10},{6,14},... | collective-permute-start | bytes 1179656 | tf_op jit(solution)/shard_map/ppermute | solution.py:119
  55.6 0.1 broadcast.26.clone.1
  55.7 0.1 broadcast.26.clone
  55.9 7.2 %collective-permute-done.16 = bf16[3,1,128,512]{3,2,1,0:T(8,128)(2,1)} collective-permute-done((bf16[3,1,128,512]{3,2,1,0:T(8,128)(2,1)S(1)}, bf16[3,1,128,512]{3,2,1,0:T(8,128)(2,1)}, u32[]{:S(2)}, u32[]{:S(2)}) %collective-permute-start.16) | collective-permute-done | bytes 393248 | tf_op jit(solution)/shard_map/ppermute | solution.py:119
  63.1 1.0 %constant_dynamic-update-slice_fusion = bf16[3,2,128,512]{3,2,1,0:T(8,128)(2,1)S(1)} fusion(bf16[3,2,128,512]{3,2,1,0:T(8,128)(2,1)S(1)} %constant_dynamic-update-slice_fusion.1, bf16[3,1,128,512]{3,2,1,0:T(8,128)(2,1)} %collective-permute-done.16, s32[]{:T(128)S(6)} %select_n.75), kind=kLoop, calls=%fused_computation.6 | loop fusion | bytes 786436 | tf_op jit(solution)/shard_map/dynamic_update_slice | solution.py:191
  64.1 0.0 copy-start.2
  64.1 6.7 %collective-permute-done.10 = bf16[3,1,128,512]{3,2,1,0:T(8,128)(2,1)S(1)} collective-permute-done((bf16[3,1,128,512]{3,2,1,0:T(8,128)(2,1)S(1)}, bf16[3,1,128,512]{3,2,1,0:T(8,128)(2,1)S(1)}, u32[]{:S(2)}, u32[]{:S(2)}) %collective-permute-start.10) | collective-permute-done | bytes 393248 | tf_op jit(solution)/shard_map/ppermute | solution.py:119
  70.9 0.0 copy-start.1
  70.9 0.9 %copy-done.1 = bf16[3,2,128,512]{3,2,1,0:T(8,128)(2,1)} copy-done((bf16[3,2,128,512]{3,2,1,0:T(8,128)(2,1)}, bf16[3,2,128,512]{3,2,1,0:T(8,128)(2,1)S(1)}, u32[]{:S(2)}) %copy-start.1) | copy-done | bytes 786456
  (11 shorter events, 0.1 us)
Async XLA Ops:
  1.3 0.7 copy-start.4
  2.0 7.1 %collective-permute-start.3 = (f32[2,3,2]{1,2,0:T(2,128)S(1)}, f32[2,3,2]{1,2,0:T(2,128)S(1)}, u32[]{:S(2)}, u32[]{:S(2)}) collective-permute-start(f32[2,3,2]{1,2,0:T(2,128)S(1)} %pad_maximum_fusion.1), channel_id=1, source_target_pairs={{4,0},{8,4},{12,8},{0,12},{5,1},{9,5},{13,9},{1,13},{6,2},{10,6},{... | collective-permute-start | bytes 152 | tf_op jit(solution)/shard_map/ppermute | solution.py:140
  4.4 6.3 %collective-permute-start.4 = (f32[2,3,2]{1,2,0:T(2,128)S(1)}, f32[2,3,2]{1,2,0:T(2,128)}, u32[]{:S(2)}, u32[]{:S(2)}) collective-permute-start(f32[2,3,2]{1,2,0:T(2,128)S(1)} %pad_maximum_fusion.1), channel_id=1, source_target_pairs={{8,0},{12,4},{0,8},{4,12},{9,1},{13,5},{1,9},{5,13},{10,2},{14,6},... | collective-permute-start | bytes 152 | tf_op jit(solution)/shard_map/ppermute | solution.py:140
  5.0 6.5 %collective-permute-start.5 = (f32[2,3,2]{1,2,0:T(2,128)S(1)}, f32[2,3,2]{1,2,0:T(2,128)}, u32[]{:S(2)}, u32[]{:S(2)}) collective-permute-start(f32[2,3,2]{1,2,0:T(2,128)S(1)} %pad_maximum_fusion.1), channel_id=1, source_target_pairs={{12,0},{0,4},{4,8},{8,12},{13,1},{1,5},{5,9},{9,13},{14,2},{2,6},{... | collective-permute-start | bytes 152 | tf_op jit(solution)/shard_map/ppermute | solution.py:140
  5.2 4.0 %copy-start = (bf16[3,2,128,512]{3,2,1,0:T(8,128)(2,1)S(1)}, bf16[3,2,128,512]{3,2,1,0:T(8,128)(2,1)}, u32[]{:S(2)}) copy-start(bf16[3,2,128,512]{3,2,1,0:T(8,128)(2,1)} %refs_0_.3) | copy-start | bytes 2359300
  5.2 7.1 %copy-start.3 = (bf16[3,2,128,512]{3,2,1,0:T(8,128)(2,1)S(1)}, bf16[3,2,128,512]{3,2,1,0:T(8,128)(2,1)}, u32[]{:S(2)}) copy-start(bf16[3,2,128,512]{3,2,1,0:T(8,128)(2,1)} %param.6) | copy-start | bytes 2359300
  6.5 25.5 %collective-permute-start = (bf16[3,1,128,512]{3,2,1,0:T(8,128)(2,1)S(1)}, bf16[3,1,128,512]{3,2,1,0:T(8,128)(2,1)S(1)}, u32[]{:S(2)}, u32[]{:S(2)}) collective-permute-start(bf16[3,1,128,512]{3,2,1,0:T(8,128)(2,1)S(1)} %get-tuple-element.14), channel_id=1, source_target_pairs={{0,8},{4,12},{8,0},{12,4},{1,9},{5,13},{9,1},{13,5},{2,10},{6,14},... | collective-permute-start | bytes 1179656 | tf_op jit(solution)/shard_map/ppermute | solution.py:119
  7.8 39.8 %collective-permute-start.1 = (bf16[3,1,128,512]{3,2,1,0:T(8,128)(2,1)S(1)}, bf16[3,1,128,512]{3,2,1,0:T(8,128)(2,1)}, u32[]{:S(2)}, u32[]{:S(2)}) collective-permute-start(bf16[3,1,128,512]{3,2,1,0:T(8,128)(2,1)S(1)} %get-tuple-element.15.refs_0_), channel_id=1, source_target_pairs={{0,4},{4,0},{8,12},{12,8},{1,5},{5,1},{9,13},{13,9},{2,6},{6,2},{1... | collective-permute-start | bytes 1179656 | tf_op jit(solution)/shard_map/ppermute | solution.py:125
  9.1 20.4 %collective-permute-start.6 = (bf16[3,2,128,512]{3,2,1,0:T(8,128)(2,1)S(1)}, bf16[3,2,128,512]{3,2,1,0:T(8,128)(2,1)S(1)}, u32[]{:S(2)}, u32[]{:S(2)}) collective-permute-start(bf16[3,2,128,512]{3,2,1,0:T(8,128)(2,1)S(1)} %copy-done), channel_id=1, source_target_pairs={{16,0},{0,16},{17,1},{1,17},{18,2},{2,18},{19,3},{3,19},{20,4},{4,... | collective-permute-start | bytes 2359304 | tf_op jit(solution)/shard_map/ppermute | solution.py:128
  12.4 1.5 %copy-start.5 = (s32[6]{0:T(128)S(1)}, s32[6]{0:T(128)}, u32[]{:S(2)}) copy-start(s32[6]{0:T(128)} %add.108) | copy-start | bytes 76
  12.4 14.2 %collective-permute-start.12 = (bf16[3,1,128,512]{3,2,1,0:T(8,128)(2,1)S(1)}, bf16[3,1,128,512]{3,2,1,0:T(8,128)(2,1)S(1)}, u32[]{:S(2)}, u32[]{:S(2)}) collective-permute-start(bf16[3,1,128,512]{3,2,1,0:T(8,128)(2,1)S(1)} %get-tuple-element.12), channel_id=1, source_target_pairs={{0,8},{4,12},{8,0},{12,4},{1,9},{5,13},{9,1},{13,5},{2,10},{6,14},... | collective-permute-start | bytes 1179656 | tf_op jit(solution)/shard_map/ppermute | solution.py:119
  13.9 24.1 %collective-permute-start.11 = (bf16[3,1,128,512]{3,2,1,0:T(8,128)(2,1)S(1)}, bf16[3,1,128,512]{3,2,1,0:T(8,128)(2,1)S(1)}, u32[]{:S(2)}, u32[]{:S(2)}) collective-permute-start(bf16[3,1,128,512]{3,2,1,0:T(8,128)(2,1)S(1)} %get-tuple-element.13.refs_0_), channel_id=1, source_target_pairs={{16,0},{0,16},{17,1},{1,17},{18,2},{2,18},{19,3},{3,19},{20,4},{4,... | collective-permute-start | bytes 1179656 | tf_op jit(solution)/shard_map/ppermute | solution.py:128
  26.7 18.8 %collective-permute-start.13 = (bf16[3,1,128,512]{3,2,1,0:T(8,128)(2,1)S(1)}, bf16[3,1,128,512]{3,2,1,0:T(8,128)(2,1)S(1)}, u32[]{:S(2)}, u32[]{:S(2)}) collective-permute-start(bf16[3,1,128,512]{3,2,1,0:T(8,128)(2,1)S(1)} %collective-permute-done.12.refs_0_), channel_id=1, source_target_pairs={{16,0},{0,16},{17,1},{1,17},{18,2},{2,18},{19,3},{3,19},{20,4},{4,... | collective-permute-start | bytes 1179656 | tf_op jit(solution)/shard_map/ppermute | solution.py:128
  30.5 17.6 %collective-permute-start.7 = (bf16[3,1,128,512]{3,2,1,0:T(8,128)(2,1)S(1)}, bf16[3,1,128,512]{3,2,1,0:T(8,128)(2,1)}, u32[]{:S(2)}, u32[]{:S(2)}) collective-permute-start(bf16[3,1,128,512]{3,2,1,0:T(8,128)(2,1)S(1)} %mix.5), channel_id=1, source_target_pairs={{0,8},{4,12},{8,0},{12,4},{1,9},{5,13},{9,1},{13,5},{2,10},{6,14},... | collective-permute-start | bytes 1179656 | tf_op jit(solution)/shard_map/ppermute | solution.py:119
  32.0 16.3 %collective-permute-start.2 = (bf16[3,1,128,512]{3,2,1,0:T(8,128)(2,1)S(1)}, bf16[3,1,128,512]{3,2,1,0:T(8,128)(2,1)}, u32[]{:S(2)}, u32[]{:S(2)}) collective-permute-start(bf16[3,1,128,512]{3,2,1,0:T(8,128)(2,1)S(1)} %collective-permute-done.refs_1_), channel_id=1, source_target_pairs={{0,4},{4,0},{8,12},{12,8},{1,5},{5,1},{9,13},{13,9},{2,6},{6,2},{1... | collective-permute-start | bytes 1179656 | tf_op jit(solution)/shard_map/ppermute | solution.py:125
  39.0 9.3 %collective-permute-start.14 = (bf16[3,1,128,512]{3,2,1,0:T(8,128)(2,1)S(1)}, bf16[3,1,128,512]{3,2,1,0:T(8,128)(2,1)}, u32[]{:S(2)}, u32[]{:S(2)}) collective-permute-start(bf16[3,1,128,512]{3,2,1,0:T(8,128)(2,1)S(1)} %mix.6.refs_4_), channel_id=1, source_target_pairs={{0,4},{4,0},{8,12},{12,8},{1,5},{5,1},{9,13},{13,9},{2,6},{6,2},{1... | collective-permute-start | bytes 1179656 | tf_op jit(solution)/shard_map/ppermute | solution.py:125
  46.5 1.9 %collective-permute-start.15 = (bf16[3,1,128,512]{3,2,1,0:T(8,128)(2,1)S(1)}, bf16[3,1,128,512]{3,2,1,0:T(8,128)(2,1)}, u32[]{:S(2)}, u32[]{:S(2)}) collective-permute-start(bf16[3,1,128,512]{3,2,1,0:T(8,128)(2,1)S(1)} %mix.7.refs_5_), channel_id=1, source_target_pairs={{0,4},{4,0},{8,12},{12,8},{1,5},{5,1},{9,13},{13,9},{2,6},{6,2},{1... | collective-permute-start | bytes 1179656 | tf_op jit(solution)/shard_map/ppermute | solution.py:125
  47.6 4.9 %collective-permute-start.8 = (bf16[3,1,128,512]{3,2,1,0:T(8,128)(2,1)S(1)}, bf16[3,1,128,512]{3,2,1,0:T(8,128)(2,1)S(1)}, u32[]{:S(2)}, u32[]{:S(2)}) collective-permute-start(bf16[3,1,128,512]{3,2,1,0:T(8,128)(2,1)S(1)} %mix.4.refs_4_), channel_id=1, source_target_pairs={{0,4},{4,0},{8,12},{12,8},{1,5},{5,1},{9,13},{13,9},{2,6},{6,2},{1... | collective-permute-start | bytes 1179656 | tf_op jit(solution)/shard_map/ppermute | solution.py:125
  48.1 4.3 %collective-permute-start.9 = (bf16[3,1,128,512]{3,2,1,0:T(8,128)(2,1)}, bf16[3,1,128,512]{3,2,1,0:T(8,128)(2,1)S(1)}, u32[]{:S(2)}, u32[]{:S(2)}) collective-permute-start(bf16[3,1,128,512]{3,2,1,0:T(8,128)(2,1)} %collective-permute-done.7.refs_5_), channel_id=1, source_target_pairs={{0,4},{4,0},{8,12},{12,8},{1,5},{5,1},{9,13},{13,9},{2,6},{6,2},{1... | collective-permute-start | bytes 1179656 | tf_op jit(solution)/shard_map/ppermute | solution.py:125
  51.0 12.1 %collective-permute-start.16 = (bf16[3,1,128,512]{3,2,1,0:T(8,128)(2,1)S(1)}, bf16[3,1,128,512]{3,2,1,0:T(8,128)(2,1)}, u32[]{:S(2)}, u32[]{:S(2)}) collective-permute-start(bf16[3,1,128,512]{3,2,1,0:T(8,128)(2,1)S(1)} %get-tuple-element.11), channel_id=1, source_target_pairs={{0,8},{4,12},{8,0},{12,4},{1,9},{5,13},{9,1},{13,5},{2,10},{6,14},... | collective-permute-start | bytes 1179656 | tf_op jit(solution)/shard_map/ppermute | solution.py:119
  54.9 15.9 %collective-permute-start.10 = (bf16[3,1,128,512]{3,2,1,0:T(8,128)(2,1)S(1)}, bf16[3,1,128,512]{3,2,1,0:T(8,128)(2,1)S(1)}, u32[]{:S(2)}, u32[]{:S(2)}) collective-permute-start(bf16[3,1,128,512]{3,2,1,0:T(8,128)(2,1)S(1)} %get-tuple-element.8), channel_id=1, source_target_pairs={{0,8},{4,12},{8,0},{12,4},{1,9},{5,13},{9,1},{13,5},{2,10},{6,14},... | collective-permute-start | bytes 1179656 | tf_op jit(solution)/shard_map/ppermute | solution.py:119
  64.1 6.8 %copy-start.2 = (bf16[3,2,128,512]{3,2,1,0:T(8,128)(2,1)}, bf16[3,2,128,512]{3,2,1,0:T(8,128)(2,1)S(1)}, u32[]{:S(2)}) copy-start(bf16[3,2,128,512]{3,2,1,0:T(8,128)(2,1)S(1)} %constant_dynamic-update-slice_fusion) | copy-start | bytes 2359300
  70.9 0.9 %copy-start.1 = (bf16[3,2,128,512]{3,2,1,0:T(8,128)(2,1)}, bf16[3,2,128,512]{3,2,1,0:T(8,128)(2,1)S(1)}, u32[]{:S(2)}) copy-start(bf16[3,2,128,512]{3,2,1,0:T(8,128)(2,1)S(1)} %constant_dynamic-update-slice_fusion.2) | copy-start | bytes 2359300

commit v3 on v0

v3 whole, which is shorter than its diff:
```python
import functools
import math

import jax
import jax.numpy as jnp
from jax import lax
from jax.experimental import pallas as pl
from jax.experimental.pallas import tpu as pltpu
from jax.sharding import PartitionSpec as P

MAXOFF = 9
BF16 = jnp.bfloat16
STEP = 16
WHOLE = pl.BlockSpec(memory_space=pltpu.VMEM)
SCALARS = pl.BlockSpec(memory_space=pltpu.SMEM)


def call(kernel, outs, flops, name, *args, scalars=0):
    moved = sum(x.size for x in args) + sum(math.prod(x) for x in outs)
    return pl.pallas_call(
        kernel,
        in_specs=[SCALARS] * scalars + [WHOLE] * (len(args) - scalars),
        out_specs=[WHOLE] * len(outs),
        out_shape=[jax.ShapeDtypeStruct(x, BF16) for x in outs],
        compiler_params=pltpu.CompilerParams(vmem_limit_bytes=32 * 1024 * 1024),
        cost_estimate=pl.CostEstimate(
            flops=flops, bytes_accessed=2 * moved, transcendentals=0
        ),
        name=name,
    )(*args)


def weighted(weight_ref, rows, columns, load):
    totals = [None] * len(rows)
    for m in columns:
        g = load(m).astype(jnp.float32)
        for i, n in enumerate(rows):
            term = weight_ref[n, m] * g
            totals[i] = term if totals[i] is None else totals[i] + term
    return totals


def chunks(rows, body):
    @pl.loop(0, rows // STEP)
    def _(i):
        body(pl.ds(pl.multiple_of(i * STEP, STEP), STEP))


def mix(whole, others, index, weights, owned):
    e, _, rows, o = whole.shape
    sources = 1 + len(others)

    def kernel(index_ref, weight_ref, *refs):
        out_ref = refs[-1]
        blocks = out_ref.shape[1]
        for b in range(blocks):
            block = index_ref[0] * blocks + b

            def body(at):
                def load(m):
                    if m < e:
                        return refs[0][m, block, at, :]
                    return refs[m // e][m % e, b, at, :]

                totals = weighted(weight_ref, range(e), range(sources * e), load)
                for n in range(e):
                    out_ref[n, b, at, :] = totals[n].astype(BF16)

            chunks(rows, body)

    shape = (e, owned, rows, o)
    flops = 2 * sources * e * math.prod(shape)
    return call(kernel, [shape], flops, "mix", index.reshape(1), weights, whole, *others, scalars=2)[0]


def partial_sums(row_pieces, weights):
    e, owned, rows, o = row_pieces[0].shape
    pieces = len(row_pieces)

    def kernel(weight_ref, *refs):
        for d in range(pieces):
            for b in range(owned):

                def body(at):
                    totals = weighted(
                        weight_ref, range(e), range(e), lambda m: refs[d][m, b, at, :]
                    )
                    for n in range(e):
                        refs[pieces + n][d, b, at, :] = totals[n].astype(BF16)

                chunks(rows, body)

    shape = (pieces, owned, rows, o)
    return call(
        kernel, [shape] * e, 2 * e * e * math.prod(shape), "partial_sums", weights, *row_pieces, scalars=1
    )


def add_partial(n, row_pieces, received, weights):
    e, owned, rows, o = row_pieces[0].shape
    pieces = len(row_pieces)

    def kernel(weight_ref, *refs):
        for d in range(pieces):
            for b in range(owned):

                def body(at):
                    (total,) = weighted(
                        weight_ref, [n], range(e), lambda m: refs[d][m, b, at, :]
                    )
                    for other in refs[pieces:-1]:
                        total = total + other[d, b, at, :].astype(jnp.float32)
                    refs[-1][d, b, at, :] = total.astype(BF16)

                chunks(rows, body)

    shape = (pieces, owned, rows, o)
    return call(
        kernel, [shape], 2 * e * math.prod(shape), "add_partial", weights, *row_pieces, *received, scalars=1
    )[0]


def product(energies, a_pieces, s_arrays, s_at, places, lefts):
    pieces = len(a_pieces)
    _, owned, rows, o = a_pieces[0].shape

    def kernel(place_ref, *refs):
        a_in, s_in = refs[:pieces], refs[pieces : pieces + len(s_arrays)]
        outs = refs[pieces + len(s_arrays) :]
        spans = [pl.ds(pl.multiple_of(place_ref[j] * rows, rows), rows) for j in range(pieces)]
        for k, n in enumerate(energies):
            for b in range(owned):
                left = jnp.concatenate(
                    [
                        jnp.concatenate([a_in[i][n, b, :, at] for at in spans], axis=1)
                        for i in range(lefts)
                    ],
                    axis=0,
                )
                at_piece = [s_at(n, j) for j in range(pieces)]
                sigma = jnp.concatenate([s_in[which][lead, b] for which, lead in at_piece], axis=0)
                first = jnp.dot(left, sigma, preferred_element_type=jnp.float32).astype(BF16)
                both = lax.dot_general(
                    first,
                    jnp.concatenate([a[n, b] for a in a_in], axis=0),
                    (((1,), (1,)), ((), ())),
                    preferred_element_type=jnp.float32,
                ).astype(BF16)
                for i in range(lefts):
                    for j, at in enumerate(spans):
                        outs[i][k, b, :, at] = both[i * rows : (i + 1) * rows, j * rows : (j + 1) * rows]

    shape = (len(energies), owned, rows, o)
    return call(
        kernel,
        [shape] * lefts,
        4 * lefts * o * math.prod(shape),
        "product",
        places,
        *a_pieces,
        *s_arrays,
        scalars=1,
    )


def after(x, *earlier):
    return lax.optimization_barrier((x,) + earlier)[0]


def solution(mesh):
    en, ph = mesh.shape["en"], mesh.shape["ph"]

    def on_device(lesser_in, greater_in, inverse, offsets, couplings):
        e, nb, r, o = lesser_in.shape
        owners = math.gcd(nb, ph)
        lanes = ph // owners
        owned = nb // owners
        en_at, ph_at = lax.axis_index("en"), lax.axis_index("ph")
        owner, lane = lax.div(ph_at, lanes), lax.rem(ph_at, lanes)

        def place_of(d, q):
            back = lax.rem(owner + owners - d, owners) if d else owner
            beside = lax.rem(lane + lanes - q, lanes) if q else lane
            return back * lanes + beside

        def owner_at(d):
            return lax.rem(owner + d, owners) if d else owner

        def to_owner(x, d):
            pairs = [(p, (p // lanes + d) % owners * lanes + p % lanes) for p in range(ph)]
            return lax.ppermute(x, "ph", pairs)

        def to_lane(x, q):
            pairs = [(p, p // lanes * lanes + (p % lanes + q) % lanes) for p in range(ph)]
            return lax.ppermute(x, "ph", pairs)

        def from_energy(x, t):
            return lax.ppermute(x, "en", [((i + t) % en, i) for i in range(en)])

        def blocks_of(x, d):
            return lax.dynamic_slice_in_dim(x, owner_at(d) * owned, owned, axis=1)

        reach = (MAXOFF + e - 1) // e
        shifts = [t for t in range(1, en) if t <= reach or en - t <= reach]

        lesser_part = [blocks_of(lesser_in, d) for d in range(1, owners)]
        lesser_from = [[from_energy(x, t) for t in shifts] for x in lesser_part]

        mine = after(jnp.stack([offsets.astype(jnp.float32), couplings]), *lesser_part)
        column = jnp.concatenate([mine] + [to_owner(mine, d) for d in range(1, owners)], axis=2)

        greater_part = [after(blocks_of(greater_in, d), mine) for d in range(1, owners)]
        greater_rows = [to_owner(x, d + 1) for d, x in enumerate(greater_part)]
        inverse_part = [after(blocks_of(inverse, d), *greater_part) for d in range(1, owners)]
        inverse_rows = [to_owner(x, d + 1) for d, x in enumerate(inverse_part)]
        lesser_own = after(blocks_of(lesser_in, 0), *inverse_part)
        lesser_from.insert(0, [from_energy(lesser_own, t) for t in shifts])
        inverse_rows.insert(0, after(blocks_of(inverse, 0), lesser_own))
        greater_rows.insert(0, after(blocks_of(greater_in, 0), lesser_own))

        small = jnp.concatenate([column] + [to_lane(column, q) for q in range(1, lanes)], axis=2)
        away = jnp.stack([(lax.rem(en_at + t, en) - en_at) * e for t in [0] + shifts])
        apart = (away[:, None] + jnp.arange(e)[None, :]).reshape(1, -1) - jnp.arange(e)[:, None]
        weights = jnp.sum(
            jnp.where(
                small[0][:, None, :] == apart[:, :, None].astype(jnp.float32),
                small[1][:, None, :],
                jnp.float32(0.0),
            ),
            axis=2,
        )
        weights_for = [
            lax.ppermute(
                weights[:, (i + 1) * e : (i + 2) * e], "en", [(j, (j + t) % en) for j in range(en)]
            )
            for i, t in enumerate(shifts)
        ]

        lesser_rows = [None] * owners
        last = weights
        for d in range(1, owners):
            mixed = mix(after(lesser_in, last), lesser_from[d], owner_at(d), weights, owned)
            lesser_rows[d] = to_owner(mixed, d)
            last = mixed
        received = [[] for _ in range(e)]
        for t, weight in zip(shifts, weights_for):
            for n, part in enumerate(partial_sums(greater_rows, after(weight, last))):
                received[n].append(from_energy(part, t))
                last = part
        lesser_rows[0] = mix(after(lesser_in, last), lesser_from[0], owner, weights, owned)
        last = lesser_rows[0]

        def all_lanes(pieces):
            return pieces + [to_lane(x, q) for q in range(1, lanes) for x in pieces]

        places = jnp.stack([place_of(d, q) for q in range(lanes) for d in range(owners)])
        inverse_full = all_lanes(inverse_rows)

        def put(result, outs, n):
            for d, out in enumerate(outs):
                back = to_owner(out, owners - d) if d else out
                result = lax.dynamic_update_slice(result, back, (n, owner_at(d) * owned, 0, 0))
            return result

        lesser_out = jnp.zeros((e, nb, r, o), BF16)
        greater_out = jnp.zeros((e, nb, r, o), BF16)
        for n in range(e):
            sigma = add_partial(n, greater_rows, received[n], after(weights, last))
            outs = product(
                [n],
                inverse_full,
                all_lanes([sigma]),
                lambda n, j: (j // owners, j % owners),
                places,
                owners,
            )
            greater_out = put(greater_out, outs, n)
            last = outs[-1]
            if n == 0:
                outs = product(
                    range(e),
                    inverse_full,
                    all_lanes(lesser_rows),
                    lambda n, j: (j, n),
                    after(places, last),
                    owners,
                )
                lesser_out = put(lesser_out, outs, 0)
                last = outs[-1]

        return lesser_out, greater_out

    block, coupled = P("en", "blk", "ph", None), P("en", "ph")
    return jax.shard_map(
        on_device,
        mesh=mesh,
        in_specs=(block, block, block, coupled, coupled),
        out_specs=(block, block),
        check_vma=False,
    )
```

time: 144 us -> 72.7 us (0.50)
  waiting for transfers between devices: 63.1 us -> 29.8 us
  blocking collectives: 28.9 us -> 0 us
  between operations: 14.2 us -> 0.94 us
  Pallas kernels: 0 us -> 11.6 us
  matrix products: 8.25 us -> 0 us
  local copies, waits for them, and re-layouts: 12.2 us -> 9.64 us
  starting transfers between devices: 15.7 us -> 17.7 us
    all_gather x2 -> x0, waiting for transfers between devices: 47.8 us -> none  [the longest x1 47.8 us: on_device(): lax.all_gather(self_energy, 'ph', axis=3, tiled=True)]
    ppermute x0 -> x22, waiting for transfers between devices: none -> 29.8 us  [the longest x8 17.9 us: to_owner(): return lax.ppermute(x, 'ph', pairs)]
    all_gather x4 -> x0, blocking collectives: 28.9 us -> none  [the longest x1 13.8 us: on_device(): weight_every = lax.all_gather(weights_all, 'en', axis=0, tiled=True)]
    ppermute x0 -> x22, starting transfers between devices: none -> 17.7 us  [the longest x8 7.59 us: to_owner(): return lax.ppermute(x, 'ph', pairs)]
    all_to_all x4 -> x0, starting transfers between devices: 15.6 us -> none  [the longest x2 7.86 us: on_device(): lax.all_to_all(shortened(mixed), 'en', split_axis=0, concat_axis=3, tiled...]
    all_to_all x4 -> x0, waiting for transfers between devices: 14.6 us -> none  [the longest x2 14.6 us: on_device(): lax.all_to_all(shortened(mixed), 'en', split_axis=0, concat_axis=3, tiled...]
    pallas_call x0 -> x9, Pallas kernels: none -> 11.6 us  [call(): pl.pallas_call(kernel, in_specs=[SCALARS] * scalars + [WHOLE] * (len(args...]
    dot_general x3 -> x0, matrix products: 8.25 us -> none  [the longest x1 6.32 us: on_device(): jnp.einsum('sebrk,ebck->sebrc', left_product, inverse_full, preferred_ele...]
  transfers between devices with their start and end apart: 6 -> 22, of which waited for: 3 -> 9; matrix products, arithmetic and copies ran while one was open for 10% -> 9% of each run, Pallas kernels for 0% -> 14%
where the time goes in v3:
time: 72.7 us; the launch traced here: 72.4 us
  waiting for transfers between devices  29.8 us (41%)
  starting transfers between devices  17.7 us (24%)
  Pallas kernels  11.6 us (16%)
  local copies, waits for them, and re-layouts  9.64 us (13%)
  other arithmetic  2.8 us (4%)
  between operations  0.94 us (1%)
    ppermute x8, waiting for transfers between devices, to_owner(): return lax.ppermute(x, 'ph', pairs)  17.9 us
    pallas_call x9, Pallas kernels, call(): pl.pallas_call(kernel, in_specs=[SCALARS] * scalars + [WHOLE] * (len(args...  11.6 us
    ppermute x8, starting transfers between devices, to_owner(): return lax.ppermute(x, 'ph', pairs)  7.59 us
    ppermute x5, starting transfers between devices, from_energy(): return lax.ppermute(x, 'en', [((i + t) % en, i) for i in range(en)])  7.33 us
    ppermute x5, waiting for transfers between devices, from_energy(): return lax.ppermute(x, 'en', [((i + t) % en, i) for i in range(en)])  7.31 us
    unnamed x23, local copies, waits for them, and re-layouts  4.03 us
    dynamic_slice x3, local copies, waits for them, and re-layouts, blocks_of(): return lax.dynamic_slice_in_dim(x, owner_at(d) * owned, owned, axis=1)  3.67 us
    ppermute x1, waiting for transfers between devices, on_device(): lax.ppermute(weights[:, (i + 1) * e:(i + 2) * e], 'en', [(j, (j + t) % en...  2.92 us
  transfers between devices with their start and end apart: 22, of which 9 were waited for; matrix products, arithmetic and copies ran while one was open for 9% of the time, Pallas kernels for 14%

profile of v3, /device:TPU:0, one launch (start us, length us, event | category | flops | bytes accessed | tf_op | source)
XLA Modules:
  0.0 72.4 jit_solution(2700248841791021520)
XLA Ops:
  0.7 2.0 %constant_dynamic-slice_fusion.1 = (bf16[3,1,128,512]{3,2,1,0:T(8,128)(2,1)S(1)}, bf16[3,1,128,512]{3,2,1,0:T(8,128)(2,1)}) fusion(bf16[3,2,128,512]{3,2,1,0:T(8,128)(2,1)} %refs_0_.1, s32[]{:T(128)S(6)} %select_n.9, s32[]{:T(128)S(6)} %select_n.8), kind=kLoop, calls=%fused_computation.11 | loop fusion | bytes 1572872 | tf_op jit(solution)/shard_map/dynamic_slice | solution.py:201
  2.7 2.9 %collective-permute-start.6 = (bf16[3,1,128,512]{3,2,1,0:T(8,128)(2,1)S(1)}, bf16[3,1,128,512]{3,2,1,0:T(8,128)(2,1)S(1)}, u32[]{:S(2)}, u32[]{:S(2)}) collective-permute-start(bf16[3,1,128,512]{3,2,1,0:T(8,128)(2,1)S(1)} %get-tuple-element.56), channel_id=1, source_target_pairs={{16,0},{0,16},{17,1},{1,17},{18,2},{2,18},{19,3},{3,19},{20,4},{4,... | collective-permute-start | bytes 1179656 | tf_op jit(solution)/shard_map/ppermute | solution.py:198
  5.6 0.7 copy-done.10
  6.3 1.5 %collective-permute-start.3 = (f32[2,3,2]{1,2,0:T(2,128)S(1)}, f32[2,3,2]{1,2,0:T(2,128)S(1)}, u32[]{:S(2)}, u32[]{:S(2)}) collective-permute-start(f32[2,3,2]{1,2,0:T(2,128)S(1)} %pad_maximum_fusion.2), channel_id=1, source_target_pairs={{0,8},{4,12},{8,0},{12,4},{1,9},{5,13},{9,1},{13,5},{2,10},{6,14},... | collective-permute-start | bytes 152 | tf_op jit(solution)/shard_map/ppermute | solution.py:191
  7.8 0.8 %constant_dynamic-slice_fusion = (bf16[3,1,128,512]{3,2,1,0:T(8,128)(2,1)S(1)}, bf16[3,1,128,512]{3,2,1,0:T(8,128)(2,1)}) fusion(bf16[3,2,128,512]{3,2,1,0:T(8,128)(2,1)S(1)} %copy-done.7, s32[]{:T(128)S(6)} %select_n.8, s32[]{:T(128)S(6)} %select_n.9), kind=kLoop, calls=%fused_computation.10 | loop fusion | bytes 1572872 | tf_op jit(solution)/shard_map/dynamic_slice | solution.py:201
  8.7 0.5 collective-permute-start.7
  9.2 0.8 %constant_dynamic-slice_fusion.3 = (bf16[3,1,128,512]{3,2,1,0:T(8,128)(2,1)}, bf16[3,1,128,512]{3,2,1,0:T(8,128)(2,1)S(1)}) fusion(bf16[3,2,128,512]{3,2,1,0:T(8,128)(2,1)S(1)} %copy-done.8, s32[]{:T(128)S(6)} %select_n.9, s32[]{:T(128)S(6)} %select_n.8), kind=kLoop, calls=%fused_computation.13 | loop fusion | bytes 1572872 | tf_op jit(solution)/shard_map/dynamic_slice | solution.py:201
  10.0 1.5 %collective-permute-start = (bf16[3,1,128,512]{3,2,1,0:T(8,128)(2,1)}, bf16[3,1,128,512]{3,2,1,0:T(8,128)(2,1)S(1)}, u32[]{:S(2)}, u32[]{:S(2)}) collective-permute-start(bf16[3,1,128,512]{3,2,1,0:T(8,128)(2,1)} %get-tuple-element.28), channel_id=1, source_target_pairs={{0,8},{4,12},{8,0},{12,4},{1,9},{5,13},{9,1},{13,5},{2,10},{6,14},... | collective-permute-start | bytes 1179656 | tf_op jit(solution)/shard_map/ppermute | solution.py:191
  11.5 0.7 collective-permute-start.8
  12.2 0.1 copy.12
  12.3 0.1 pad_add_fusion.1
  12.4 0.1 iota_add_fusion
  12.4 0.6 add.81
  13.1 0.7 subtract_convert_fusion
  13.8 0.0 collective-permute-done.3
  13.8 0.6 pad_maximum_fusion
  14.4 0.1 copy.13
  14.5 1.4 %collective-permute-done.4 = f32[2,3,4]{1,2,0:T(4,128)} collective-permute-done((f32[2,3,4]{1,2,0:T(4,128)}, f32[2,3,4]{1,2,0:T(4,128)}, u32[]{:S(2)}, u32[]{:S(2)}) %collective-permute-start.4) | collective-permute-done | bytes 128 | tf_op jit(solution)/shard_map/ppermute | solution.py:195
  15.9 0.8 %copy.14 = f32[2,3,4]{2,0,1:T(2,128)S(1)} copy(f32[2,3,4]{1,2,0:T(4,128)} %collective-permute-done.4) | data formatting | bytes 192 | tf_op jit(solution)/shard_map/ppermute | solution.py:195
  16.6 0.1 pad_maximum_fusion.1
  16.7 0.2 select_reduce_fusion.weight_ref
  16.9 1.0 %mix.2 = bf16[3,1,128,512]{3,2,1,0:T(8,128)(2,1)S(1)} custom-call(s32[1]{0:T(128)} %bitcast.9.index_ref, f32[3,6]{1,0:T(4,128)S(1)} %select_reduce_fusion.weight_ref, bf16[3,2,128,512]{3,2,1,0:T(8,128)(2,1)S(1)} %copy-done, bf16[3,1,128,512]{3,2,1,0:T(8,128)(2,1)S(1)} %collective-permute-done.6.refs_1_), custom_call_target="tpu_custom_call" | custom-call | flops 2359296 | bytes 1572902 | tf_op jit(solution)/shard_map/mix/pallas_call | solution.py:20
  17.9 0.8 %collective-permute-start.11 = (bf16[3,1,128,512]{3,2,1,0:T(8,128)(2,1)S(1)}, bf16[3,1,128,512]{3,2,1,0:T(8,128)(2,1)}, u32[]{:S(2)}, u32[]{:S(2)}) collective-permute-start(bf16[3,1,128,512]{3,2,1,0:T(8,128)(2,1)S(1)} %mix.2), channel_id=1, source_target_pairs={{0,8},{4,12},{8,0},{12,4},{1,9},{5,13},{9,1},{13,5},{2,10},{6,14},... | collective-permute-start | bytes 1179656 | tf_op jit(solution)/shard_map/ppermute | solution.py:191
  18.7 0.1 slice.11
  18.8 1.5 %collective-permute-start.5 = (f32[3,3]{1,0:T(4,128)S(1)}, f32[3,3]{1,0:T(4,128)S(1)}, u32[]{:S(2)}, u32[]{:S(2)}) collective-permute-start(f32[3,3]{1,0:T(4,128)S(1)} %slice.11), channel_id=1, source_target_pairs={{0,16},{16,0},{1,17},{17,1},{2,18},{18,2},{3,19},{19,3},{4,20},{20... | collective-permute-start | bytes 116 | tf_op jit(solution)/shard_map/ppermute | solution.py:233
  20.3 2.9 %collective-permute-done.5.weight_ref = f32[3,3]{1,0:T(4,128)S(1)} collective-permute-done((f32[3,3]{1,0:T(4,128)S(1)}, f32[3,3]{1,0:T(4,128)S(1)}, u32[]{:S(2)}, u32[]{:S(2)}) %collective-permute-start.5) | collective-permute-done | bytes 68 | tf_op jit(solution)/shard_map/ppermute | solution.py:233
  23.2 0.0 collective-permute-start.1
  23.2 0.0 collective-permute-done.7.refs_1_
  23.2 1.7 %partial_sums.1 = (bf16[2,1,128,512]{3,2,1,0:T(8,128)(2,1)S(1)}, bf16[2,1,128,512]{3,2,1,0:T(8,128)(2,1)}, bf16[2,1,128,512]{3,2,1,0:T(8,128)(2,1)S(1)}) custom-call(f32[3,3]{1,0:T(4,128)S(1)} %collective-permute-done.5.weight_ref, bf16[3,1,128,512]{3,2,1,0:T(8,128)(2,1)S(1)} %get-tuple-element.33.refs_0_, ...), custom_call_target="tpu_custom_call" | custom-call | flops 2359296 | bytes 1572882 | tf_op jit(solution)/shard_map/partial_sums/pallas_call | solution.py:20
  24.9 0.7 copy-done.3
  25.6 1.7 %collective-permute-start.9 = (bf16[2,1,128,512]{3,2,1,0:T(8,128)(2,1)S(1)}, bf16[2,1,128,512]{3,2,1,0:T(8,128)(2,1)S(1)}, u32[]{:S(2)}, u32[]{:S(2)}) collective-permute-start(bf16[2,1,128,512]{3,2,1,0:T(8,128)(2,1)S(1)} %get-tuple-element.37), channel_id=1, source_target_pairs={{16,0},{0,16},{17,1},{1,17},{18,2},{2,18},{19,3},{3,19},{20,4},{4,... | collective-permute-start | bytes 786440 | tf_op jit(solution)/shard_map/ppermute | solution.py:198
  27.3 2.0 %collective-permute-done.refs_1_ = bf16[3,1,128,512]{3,2,1,0:T(8,128)(2,1)S(1)} collective-permute-done((bf16[3,1,128,512]{3,2,1,0:T(8,128)(2,1)}, bf16[3,1,128,512]{3,2,1,0:T(8,128)(2,1)S(1)}, u32[]{:S(2)}, u32[]{:S(2)}) %collective-permute-start) | collective-permute-done | bytes 393248 | tf_op jit(solution)/shard_map/ppermute | solution.py:191
  29.4 0.7 %copy-done.1 = bf16[3,1,128,512]{3,2,1,0:T(8,128)(2,1)} copy-done((bf16[3,1,128,512]{3,2,1,0:T(8,128)(2,1)}, bf16[3,1,128,512]{3,2,1,0:T(8,128)(2,1)S(1)}, u32[]{:S(2)}) %copy-start.1) | copy-done | bytes 393240
  30.1 1.0 %copy-done.2 = bf16[3,1,128,512]{3,2,1,0:T(8,128)(2,1)S(1)} copy-done((bf16[3,1,128,512]{3,2,1,0:T(8,128)(2,1)S(1)}, bf16[3,1,128,512]{3,2,1,0:T(8,128)(2,1)}, u32[]{:S(2)}) %copy-start.2) | copy-done | bytes 393240
  31.1 1.0 %mix.3.refs_4_ = bf16[3,1,128,512]{3,2,1,0:T(8,128)(2,1)S(1)} custom-call(s32[1]{0:T(128)} %bitcast.8.index_ref, f32[3,6]{1,0:T(4,128)S(1)} %select_reduce_fusion.weight_ref, bf16[3,2,128,512]{3,2,1,0:T(8,128)(2,1)S(1)} %copy-done, bf16[3,1,128,512]{3,2,1,0:T(8,128)(2,1)S(1)} %copy-done.2), custom_call_target="tpu_custom_call" | custom-call | flops 2359296 | bytes 1572902 | tf_op jit(solution)/shard_map/mix/pallas_call | solution.py:20
  32.1 0.6 collective-permute-start.12
  32.7 3.5 %collective-permute-done.11.refs_5_ = bf16[3,1,128,512]{3,2,1,0:T(8,128)(2,1)} collective-permute-done((bf16[3,1,128,512]{3,2,1,0:T(8,128)(2,1)S(1)}, bf16[3,1,128,512]{3,2,1,0:T(8,128)(2,1)}, u32[]{:S(2)}, u32[]{:S(2)}) %collective-permute-start.11) | collective-permute-done | bytes 393248 | tf_op jit(solution)/shard_map/ppermute | solution.py:191
  36.1 0.9 %add_partial.3.refs_4_ = bf16[2,1,128,512]{3,2,1,0:T(8,128)(2,1)S(1)} custom-call(f32[3,6]{1,0:T(4,128)S(1)} %select_reduce_fusion.weight_ref, bf16[3,1,128,512]{3,2,1,0:T(8,128)(2,1)S(1)} %get-tuple-element.33.refs_0_, bf16[3,1,128,512]{3,2,1,0:T(8,128)(2,1)S(1)} %collective-permute-done.7.refs_1_, bf16[2,1,128,512]{3,2,1,0:T(8,128)(2,1)S(1)} %collective-permute-done.9.refs_2_), custom_call_target="tpu_custom_call" | custom-call | flops 786432 | bytes 1310756 | tf_op jit(solution)/shard_map/add_partial/pallas_call | solution.py:20
  37.0 0.6 collective-permute-start.10
  37.6 1.0 %collective-permute-start.16 = (bf16[2,1,128,512]{3,2,1,0:T(8,128)(2,1)}, bf16[2,1,128,512]{3,2,1,0:T(8,128)(2,1)}, u32[]{:S(2)}, u32[]{:S(2)}) collective-permute-start(bf16[2,1,128,512]{3,2,1,0:T(8,128)(2,1)} %get-tuple-element.44), channel_id=1, source_target_pairs={{16,0},{0,16},{17,1},{1,17},{18,2},{2,18},{19,3},{3,19},{20,4},{4,... | collective-permute-start | bytes 786440 | tf_op jit(solution)/shard_map/ppermute | solution.py:198
  38.5 0.1 pad_add_fusion.place_ref
  38.6 0.3 collective-permute-done.10.refs_5_
  38.9 1.5 %product.4 = (bf16[1,1,128,512]{3,2,1,0:T(8,128)(2,1)S(1)}, bf16[1,1,128,512]{3,2,1,0:T(8,128)(2,1)S(1)}) custom-call(s32[4]{0:T(128)S(1)} %pad_add_fusion.place_ref, bf16[3,1,128,512]{3,2,1,0:T(8,128)(2,1)S(1)} %get-tuple-element.30.refs_0_, bf16[3,1,128,512]{3,2,1,0:T(8,128)(2,1)S(1)} %collective-permute-done.refs_1_, ...), custom_call_target="tpu_custom_call" | custom-call | flops 268435456 | bytes 2359304 | tf_op jit(solution)/shard_map/product/pallas_call | solution.py:20
  40.4 2.4 %product.5 = (bf16[3,1,128,512]{3,2,1,0:T(8,128)(2,1)S(1)}, bf16[3,1,128,512]{3,2,1,0:T(8,128)(2,1)S(1)}) custom-call(s32[4]{0:T(128)S(1)} %pad_add_fusion.place_ref, bf16[3,1,128,512]{3,2,1,0:T(8,128)(2,1)S(1)} %get-tuple-element.30.refs_0_, bf16[3,1,128,512]{3,2,1,0:T(8,128)(2,1)S(1)} %collective-permute-done.refs_1_, ...), custom_call_target="tpu_custom_call" | custom-call | flops 805306368 | bytes 3932168 | tf_op jit(solution)/shard_map/product/pallas_call | solution.py:20
  42.8 3.4 %collective-permute-done.16.refs_2_ = bf16[2,1,128,512]{3,2,1,0:T(8,128)(2,1)} collective-permute-done((bf16[2,1,128,512]{3,2,1,0:T(8,128)(2,1)}, bf16[2,1,128,512]{3,2,1,0:T(8,128)(2,1)}, u32[]{:S(2)}, u32[]{:S(2)}) %collective-permute-start.16) | collective-permute-done | bytes 262176 | tf_op jit(solution)/shard_map/ppermute | solution.py:198
  46.2 1.3 %add_partial.4.refs_4_ = bf16[2,1,128,512]{3,2,1,0:T(8,128)(2,1)S(1)} custom-call(f32[3,6]{1,0:T(4,128)S(1)} %select_reduce_fusion.weight_ref, bf16[3,1,128,512]{3,2,1,0:T(8,128)(2,1)S(1)} %get-tuple-element.33.refs_0_, bf16[3,1,128,512]{3,2,1,0:T(8,128)(2,1)S(1)} %collective-permute-done.7.refs_1_, bf16[2,1,128,512]{3,2,1,0:T(8,128)(2,1)} %collective-permute-done.16.refs_2_), custom_call_target="tpu_custom_call" | custom-call | flops 786432 | bytes 1310756 | tf_op jit(solution)/shard_map/add_partial/pallas_call | solution.py:20
  47.5 0.1 collective-permute-start.17
  47.5 1.0 %collective-permute-start.19 = (bf16[2,1,128,512]{3,2,1,0:T(8,128)(2,1)S(1)}, bf16[2,1,128,512]{3,2,1,0:T(8,128)(2,1)S(1)}, u32[]{:S(2)}, u32[]{:S(2)}) collective-permute-start(bf16[2,1,128,512]{3,2,1,0:T(8,128)(2,1)S(1)} %copy-done.4), channel_id=1, source_target_pairs={{16,0},{0,16},{17,1},{1,17},{18,2},{2,18},{19,3},{3,19},{20,4},{4,... | collective-permute-start | bytes 786440 | tf_op jit(solution)/shard_map/ppermute | solution.py:198
  48.6 0.5 collective-permute-start.15
  49.1 0.1 broadcast.24.clone.1
  49.2 1.6 %collective-permute-start.14 = (bf16[3,1,128,512]{3,2,1,0:T(8,128)(2,1)S(1)}, bf16[3,1,128,512]{3,2,1,0:T(8,128)(2,1)S(1)}, u32[]{:S(2)}, u32[]{:S(2)}) collective-permute-start(bf16[3,1,128,512]{3,2,1,0:T(8,128)(2,1)S(1)} %get-tuple-element.41), channel_id=1, source_target_pairs={{0,8},{4,12},{8,0},{12,4},{1,9},{5,13},{9,1},{13,5},{2,10},{6,14},... | collective-permute-start | bytes 1179656 | tf_op jit(solution)/shard_map/ppermute | solution.py:191
  50.8 1.1 %product.6 = (bf16[1,1,128,512]{3,2,1,0:T(8,128)(2,1)S(1)}, bf16[1,1,128,512]{3,2,1,0:T(8,128)(2,1)S(1)}) custom-call(s32[4]{0:T(128)S(1)} %pad_add_fusion.place_ref, bf16[3,1,128,512]{3,2,1,0:T(8,128)(2,1)S(1)} %get-tuple-element.30.refs_0_, bf16[3,1,128,512]{3,2,1,0:T(8,128)(2,1)S(1)} %collective-permute-done.refs_1_, ...), custom_call_target="tpu_custom_call" | custom-call | flops 268435456 | bytes 2359304 | tf_op jit(solution)/shard_map/product/pallas_call | solution.py:20
  51.8 0.6 collective-permute-start.18
  52.4 3.9 %collective-permute-done.19.refs_2_ = bf16[2,1,128,512]{3,2,1,0:T(8,128)(2,1)S(1)} collective-permute-done((bf16[2,1,128,512]{3,2,1,0:T(8,128)(2,1)S(1)}, bf16[2,1,128,512]{3,2,1,0:T(8,128)(2,1)S(1)}, u32[]{:S(2)}, u32[]{:S(2)}) %collective-permute-start.19) | collective-permute-done | bytes 262176 | tf_op jit(solution)/shard_map/ppermute | solution.py:198
  56.3 0.9 %add_partial.5 = bf16[2,1,128,512]{3,2,1,0:T(8,128)(2,1)S(1)} custom-call(f32[3,6]{1,0:T(4,128)S(1)} %select_reduce_fusion.weight_ref, bf16[3,1,128,512]{3,2,1,0:T(8,128)(2,1)S(1)} %get-tuple-element.33.refs_0_, bf16[3,1,128,512]{3,2,1,0:T(8,128)(2,1)S(1)} %collective-permute-done.7.refs_1_, bf16[2,1,128,512]{3,2,1,0:T(8,128)(2,1)S(1)} %collective-permute-done.19.refs_2_), custom_call_target="tpu_custom_call" | custom-call | flops 786432 | bytes 1310756 | tf_op jit(solution)/shard_map/add_partial/pallas_call | solution.py:20
  57.1 0.1 collective-permute-start.20
  57.3 8.1 %collective-permute-done.18 = bf16[1,1,128,512]{3,2,1,0:T(8,128)(2,1)S(1)} collective-permute-done((bf16[1,1,128,512]{3,2,1,0:T(8,128)(2,1)S(1)}, bf16[1,1,128,512]{3,2,1,0:T(8,128)(2,1)S(1)}, u32[]{:S(2)}, u32[]{:S(2)}) %collective-permute-start.18) | collective-permute-done | bytes 131104 | tf_op jit(solution)/shard_map/ppermute | solution.py:191
  65.4 1.1 %product.7 = (bf16[3,2,128,512]{3,2,1,0:T(8,128)(2,1)S(1)}, bf16[1,1,128,512]{3,2,1,0:T(8,128)(2,1)S(1)}) fusion(bf16[3,2,128,512]{3,2,1,0:T(8,128)(2,1)S(1)} %constant_dynamic-update-slice_fusion.2, s32[]{:T(128)S(6)} %select_n.8, s32[4]{0:T(128)S(1)} %pad_add_fusion.place_ref, bf16[3,1,128,512]{3,2,1,0:T(8,128)(2,1)S(1)} %get-tuple-element.30.refs_0_, ...), kind=kCustom, calls=%fused_computation.3 | custom fusion | flops 268435456 | bytes 2359812 | tf_op jit(solution)/shard_map/product/pallas_call | solution.py:20
  66.5 0.6 collective-permute-start.21
  67.0 0.1 broadcast.24.clone
  67.2 0.0 copy-start.5
  67.2 4.3 %collective-permute-done.21 = bf16[1,1,128,512]{3,2,1,0:T(8,128)(2,1)S(1)} collective-permute-done((bf16[1,1,128,512]{3,2,1,0:T(8,128)(2,1)S(1)}, bf16[1,1,128,512]{3,2,1,0:T(8,128)(2,1)S(1)}, u32[]{:S(2)}, u32[]{:S(2)}) %collective-permute-start.21) | collective-permute-done | bytes 131104 | tf_op jit(solution)/shard_map/ppermute | solution.py:191
  71.5 0.0 copy-start.6
  71.5 0.9 %copy-done.6 = bf16[3,2,128,512]{3,2,1,0:T(8,128)(2,1)} copy-done((bf16[3,2,128,512]{3,2,1,0:T(8,128)(2,1)}, bf16[3,2,128,512]{3,2,1,0:T(8,128)(2,1)S(1)}, u32[]{:S(2)}) %copy-start.6) | copy-done | bytes 786456
  (40 shorter events, 0.2 us)
Async XLA Ops:
  0.7 7.2 %copy-start.7 = (bf16[3,2,128,512]{3,2,1,0:T(8,128)(2,1)S(1)}, bf16[3,2,128,512]{3,2,1,0:T(8,128)(2,1)}, u32[]{:S(2)}) copy-start(bf16[3,2,128,512]{3,2,1,0:T(8,128)(2,1)} %param.6) | copy-start | bytes 2359300
  2.7 2.9 %copy-start.9 = (s32[3,2]{0,1:T(2,128)S(1)}, s32[3,2]{0,1:T(2,128)}, u32[]{:S(2)}) copy-start(s32[3,2]{0,1:T(2,128)} %param.8) | copy-start | bytes 76
  2.7 14.2 %collective-permute-start.6 = (bf16[3,1,128,512]{3,2,1,0:T(8,128)(2,1)S(1)}, bf16[3,1,128,512]{3,2,1,0:T(8,128)(2,1)S(1)}, u32[]{:S(2)}, u32[]{:S(2)}) collective-permute-start(bf16[3,1,128,512]{3,2,1,0:T(8,128)(2,1)S(1)} %get-tuple-element.56), channel_id=1, source_target_pairs={{16,0},{0,16},{17,1},{1,17},{18,2},{2,18},{19,3},{3,19},{20,4},{4,... | collective-permute-start | bytes 1179656 | tf_op jit(solution)/shard_map/ppermute | solution.py:198
  5.6 0.7 copy-start.10
  6.3 2.9 %copy-start.8 = (bf16[3,2,128,512]{3,2,1,0:T(8,128)(2,1)S(1)}, bf16[3,2,128,512]{3,2,1,0:T(8,128)(2,1)}, u32[]{:S(2)}) copy-start(bf16[3,2,128,512]{3,2,1,0:T(8,128)(2,1)} %param.7) | copy-start | bytes 2359300
  6.3 7.5 %collective-permute-start.3 = (f32[2,3,2]{1,2,0:T(2,128)S(1)}, f32[2,3,2]{1,2,0:T(2,128)S(1)}, u32[]{:S(2)}, u32[]{:S(2)}) collective-permute-start(f32[2,3,2]{1,2,0:T(2,128)S(1)} %pad_maximum_fusion.2), channel_id=1, source_target_pairs={{0,8},{4,12},{8,0},{12,4},{1,9},{5,13},{9,1},{13,5},{2,10},{6,14},... | collective-permute-start | bytes 152 | tf_op jit(solution)/shard_map/ppermute | solution.py:191
  8.7 8.2 %copy-start = (bf16[3,2,128,512]{3,2,1,0:T(8,128)(2,1)S(1)}, bf16[3,2,128,512]{3,2,1,0:T(8,128)(2,1)}, u32[]{:S(2)}) copy-start(bf16[3,2,128,512]{3,2,1,0:T(8,128)(2,1)} %refs_0_.1) | copy-start | bytes 2359300
  8.7 14.5 %collective-permute-start.7 = (bf16[3,1,128,512]{3,2,1,0:T(8,128)(2,1)}, bf16[3,1,128,512]{3,2,1,0:T(8,128)(2,1)S(1)}, u32[]{:S(2)}, u32[]{:S(2)}) collective-permute-start(bf16[3,1,128,512]{3,2,1,0:T(8,128)(2,1)} %get-tuple-element.27), channel_id=1, source_target_pairs={{0,8},{4,12},{8,0},{12,4},{1,9},{5,13},{9,1},{13,5},{2,10},{6,14},... | collective-permute-start | bytes 1179656 | tf_op jit(solution)/shard_map/ppermute | solution.py:191
  10.0 19.4 %collective-permute-start = (bf16[3,1,128,512]{3,2,1,0:T(8,128)(2,1)}, bf16[3,1,128,512]{3,2,1,0:T(8,128)(2,1)S(1)}, u32[]{:S(2)}, u32[]{:S(2)}) collective-permute-start(bf16[3,1,128,512]{3,2,1,0:T(8,128)(2,1)} %get-tuple-element.28), channel_id=1, source_target_pairs={{0,8},{4,12},{8,0},{12,4},{1,9},{5,13},{9,1},{13,5},{2,10},{6,14},... | collective-permute-start | bytes 1179656 | tf_op jit(solution)/shard_map/ppermute | solution.py:191
  11.5 17.8 %collective-permute-start.8 = (bf16[3,1,128,512]{3,2,1,0:T(8,128)(2,1)}, bf16[3,1,128,512]{3,2,1,0:T(8,128)(2,1)S(1)}, u32[]{:S(2)}, u32[]{:S(2)}) collective-permute-start(bf16[3,1,128,512]{3,2,1,0:T(8,128)(2,1)} %get-tuple-element.29), channel_id=1, source_target_pairs={{16,0},{0,16},{17,1},{1,17},{18,2},{2,18},{19,3},{3,19},{20,4},{4,... | collective-permute-start | bytes 1179656 | tf_op jit(solution)/shard_map/ppermute | solution.py:198
  14.4 1.5 %collective-permute-start.4 = (f32[2,3,4]{1,2,0:T(4,128)}, f32[2,3,4]{1,2,0:T(4,128)}, u32[]{:S(2)}, u32[]{:S(2)}) collective-permute-start(f32[2,3,4]{1,2,0:T(4,128)} %pad_maximum_fusion), channel_id=1, source_target_pairs={{0,4},{4,0},{8,12},{12,8},{1,5},{5,1},{9,13},{13,9},{2,6},{6,2},{1... | collective-permute-start | bytes 296 | tf_op jit(solution)/shard_map/ppermute | solution.py:195
  17.9 18.2 %collective-permute-start.11 = (bf16[3,1,128,512]{3,2,1,0:T(8,128)(2,1)S(1)}, bf16[3,1,128,512]{3,2,1,0:T(8,128)(2,1)}, u32[]{:S(2)}, u32[]{:S(2)}) collective-permute-start(bf16[3,1,128,512]{3,2,1,0:T(8,128)(2,1)S(1)} %mix.2), channel_id=1, source_target_pairs={{0,8},{4,12},{8,0},{12,4},{1,9},{5,13},{9,1},{13,5},{2,10},{6,14},... | collective-permute-start | bytes 1179656 | tf_op jit(solution)/shard_map/ppermute | solution.py:191
  18.8 4.4 %collective-permute-start.5 = (f32[3,3]{1,0:T(4,128)S(1)}, f32[3,3]{1,0:T(4,128)S(1)}, u32[]{:S(2)}, u32[]{:S(2)}) collective-permute-start(f32[3,3]{1,0:T(4,128)S(1)} %slice.11), channel_id=1, source_target_pairs={{0,16},{16,0},{1,17},{17,1},{2,18},{18,2},{3,19},{19,3},{4,20},{20... | collective-permute-start | bytes 116 | tf_op jit(solution)/shard_map/ppermute | solution.py:233
  23.2 14.4 %collective-permute-start.1 = (bf16[3,1,128,512]{3,2,1,0:T(8,128)(2,1)S(1)}, bf16[3,1,128,512]{3,2,1,0:T(8,128)(2,1)S(1)}, u32[]{:S(2)}, u32[]{:S(2)}) collective-permute-start(bf16[3,1,128,512]{3,2,1,0:T(8,128)(2,1)S(1)} %get-tuple-element.30.refs_0_), channel_id=1, source_target_pairs={{0,4},{4,0},{8,12},{12,8},{1,5},{5,1},{9,13},{13,9},{2,6},{6,2},{1... | collective-permute-start | bytes 1179656 | tf_op jit(solution)/shard_map/ppermute | solution.py:195
  24.9 0.7 copy-start.3
  25.6 10.5 %collective-permute-start.9 = (bf16[2,1,128,512]{3,2,1,0:T(8,128)(2,1)S(1)}, bf16[2,1,128,512]{3,2,1,0:T(8,128)(2,1)S(1)}, u32[]{:S(2)}, u32[]{:S(2)}) collective-permute-start(bf16[2,1,128,512]{3,2,1,0:T(8,128)(2,1)S(1)} %get-tuple-element.37), channel_id=1, source_target_pairs={{16,0},{0,16},{17,1},{1,17},{18,2},{2,18},{19,3},{3,19},{20,4},{4,... | collective-permute-start | bytes 786440 | tf_op jit(solution)/shard_map/ppermute | solution.py:198
  29.4 9.3 %collective-permute-start.2 = (bf16[3,1,128,512]{3,2,1,0:T(8,128)(2,1)S(1)}, bf16[3,1,128,512]{3,2,1,0:T(8,128)(2,1)S(1)}, u32[]{:S(2)}, u32[]{:S(2)}) collective-permute-start(bf16[3,1,128,512]{3,2,1,0:T(8,128)(2,1)S(1)} %collective-permute-done.refs_1_), channel_id=1, source_target_pairs={{0,4},{4,0},{8,12},{12,8},{1,5},{5,1},{9,13},{13,9},{2,6},{6,2},{1... | collective-permute-start | bytes 1179656 | tf_op jit(solution)/shard_map/ppermute | solution.py:195
  29.4 0.7 %copy-start.1 = (bf16[3,1,128,512]{3,2,1,0:T(8,128)(2,1)}, bf16[3,1,128,512]{3,2,1,0:T(8,128)(2,1)S(1)}, u32[]{:S(2)}) copy-start(bf16[3,1,128,512]{3,2,1,0:T(8,128)(2,1)S(1)} %collective-permute-done.8.refs_1_) | copy-start | bytes 1179652
  30.1 1.0 %copy-start.2 = (bf16[3,1,128,512]{3,2,1,0:T(8,128)(2,1)S(1)}, bf16[3,1,128,512]{3,2,1,0:T(8,128)(2,1)}, u32[]{:S(2)}) copy-start(bf16[3,1,128,512]{3,2,1,0:T(8,128)(2,1)} %copy-done.1) | copy-start | bytes 1179652
  32.1 8.3 %collective-permute-start.12 = (bf16[3,1,128,512]{3,2,1,0:T(8,128)(2,1)S(1)}, bf16[3,1,128,512]{3,2,1,0:T(8,128)(2,1)S(1)}, u32[]{:S(2)}, u32[]{:S(2)}) collective-permute-start(bf16[3,1,128,512]{3,2,1,0:T(8,128)(2,1)S(1)} %mix.3.refs_4_), channel_id=1, source_target_pairs={{0,4},{4,0},{8,12},{12,8},{1,5},{5,1},{9,13},{13,9},{2,6},{6,2},{1... | collective-permute-start | bytes 1179656 | tf_op jit(solution)/shard_map/ppermute | solution.py:195
  36.1 4.2 %collective-permute-start.13 = (bf16[3,1,128,512]{3,2,1,0:T(8,128)(2,1)}, bf16[3,1,128,512]{3,2,1,0:T(8,128)(2,1)}, u32[]{:S(2)}, u32[]{:S(2)}) collective-permute-start(bf16[3,1,128,512]{3,2,1,0:T(8,128)(2,1)} %collective-permute-done.11.refs_5_), channel_id=1, source_target_pairs={{0,4},{4,0},{8,12},{12,8},{1,5},{5,1},{9,13},{13,9},{2,6},{6,2},{1... | collective-permute-start | bytes 1179656 | tf_op jit(solution)/shard_map/ppermute | solution.py:195
  37.0 1.9 %collective-permute-start.10 = (bf16[2,1,128,512]{3,2,1,0:T(8,128)(2,1)S(1)}, bf16[2,1,128,512]{3,2,1,0:T(8,128)(2,1)}, u32[]{:S(2)}, u32[]{:S(2)}) collective-permute-start(bf16[2,1,128,512]{3,2,1,0:T(8,128)(2,1)S(1)} %add_partial.3.refs_4_), channel_id=1, source_target_pairs={{0,4},{4,0},{8,12},{12,8},{1,5},{5,1},{9,13},{13,9},{2,6},{6,2},{1... | collective-permute-start | bytes 786440 | tf_op jit(solution)/shard_map/ppermute | solution.py:195
  37.6 8.6 %collective-permute-start.16 = (bf16[2,1,128,512]{3,2,1,0:T(8,128)(2,1)}, bf16[2,1,128,512]{3,2,1,0:T(8,128)(2,1)}, u32[]{:S(2)}, u32[]{:S(2)}) collective-permute-start(bf16[2,1,128,512]{3,2,1,0:T(8,128)(2,1)} %get-tuple-element.44), channel_id=1, source_target_pairs={{16,0},{0,16},{17,1},{1,17},{18,2},{2,18},{19,3},{3,19},{20,4},{4,... | collective-permute-start | bytes 786440 | tf_op jit(solution)/shard_map/ppermute | solution.py:198
  42.7 4.8 %copy-start.4 = (bf16[2,1,128,512]{3,2,1,0:T(8,128)(2,1)S(1)}, bf16[2,1,128,512]{3,2,1,0:T(8,128)(2,1)}, u32[]{:S(2)}) copy-start(bf16[2,1,128,512]{3,2,1,0:T(8,128)(2,1)} %copy-done.3) | copy-start | bytes 786436
  47.5 3.3 %collective-permute-start.17 = (bf16[2,1,128,512]{3,2,1,0:T(8,128)(2,1)S(1)}, bf16[2,1,128,512]{3,2,1,0:T(8,128)(2,1)S(1)}, u32[]{:S(2)}, u32[]{:S(2)}) collective-permute-start(bf16[2,1,128,512]{3,2,1,0:T(8,128)(2,1)S(1)} %add_partial.4.refs_4_), channel_id=1, source_target_pairs={{0,4},{4,0},{8,12},{12,8},{1,5},{5,1},{9,13},{13,9},{2,6},{6,2},{1... | collective-permute-start | bytes 786440 | tf_op jit(solution)/shard_map/ppermute | solution.py:195
  47.5 8.7 %collective-permute-start.19 = (bf16[2,1,128,512]{3,2,1,0:T(8,128)(2,1)S(1)}, bf16[2,1,128,512]{3,2,1,0:T(8,128)(2,1)S(1)}, u32[]{:S(2)}, u32[]{:S(2)}) collective-permute-start(bf16[2,1,128,512]{3,2,1,0:T(8,128)(2,1)S(1)} %copy-done.4), channel_id=1, source_target_pairs={{16,0},{0,16},{17,1},{1,17},{18,2},{2,18},{19,3},{3,19},{20,4},{4,... | collective-permute-start | bytes 786440 | tf_op jit(solution)/shard_map/ppermute | solution.py:198
  48.6 8.6 %collective-permute-start.15 = (bf16[1,1,128,512]{3,2,1,0:T(8,128)(2,1)S(1)}, bf16[1,1,128,512]{3,2,1,0:T(8,128)(2,1)S(1)}, u32[]{:S(2)}, u32[]{:S(2)}) collective-permute-start(bf16[1,1,128,512]{3,2,1,0:T(8,128)(2,1)S(1)} %get-tuple-element.38), channel_id=1, source_target_pairs={{0,8},{4,12},{8,0},{12,4},{1,9},{5,13},{9,1},{13,5},{2,10},{6,14},... | collective-permute-start | bytes 393224 | tf_op jit(solution)/shard_map/ppermute | solution.py:191
  49.2 18.0 %collective-permute-start.14 = (bf16[3,1,128,512]{3,2,1,0:T(8,128)(2,1)S(1)}, bf16[3,1,128,512]{3,2,1,0:T(8,128)(2,1)S(1)}, u32[]{:S(2)}, u32[]{:S(2)}) collective-permute-start(bf16[3,1,128,512]{3,2,1,0:T(8,128)(2,1)S(1)} %get-tuple-element.41), channel_id=1, source_target_pairs={{0,8},{4,12},{8,0},{12,4},{1,9},{5,13},{9,1},{13,5},{2,10},{6,14},... | collective-permute-start | bytes 1179656 | tf_op jit(solution)/shard_map/ppermute | solution.py:191
  51.8 13.5 %collective-permute-start.18 = (bf16[1,1,128,512]{3,2,1,0:T(8,128)(2,1)S(1)}, bf16[1,1,128,512]{3,2,1,0:T(8,128)(2,1)S(1)}, u32[]{:S(2)}, u32[]{:S(2)}) collective-permute-start(bf16[1,1,128,512]{3,2,1,0:T(8,128)(2,1)S(1)} %get-tuple-element.46), channel_id=1, source_target_pairs={{0,8},{4,12},{8,0},{12,4},{1,9},{5,13},{9,1},{13,5},{2,10},{6,14},... | collective-permute-start | bytes 393224 | tf_op jit(solution)/shard_map/ppermute | solution.py:191
  57.1 8.3 %collective-permute-start.20 = (bf16[2,1,128,512]{3,2,1,0:T(8,128)(2,1)S(1)}, bf16[2,1,128,512]{3,2,1,0:T(8,128)(2,1)S(1)}, u32[]{:S(2)}, u32[]{:S(2)}) collective-permute-start(bf16[2,1,128,512]{3,2,1,0:T(8,128)(2,1)S(1)} %add_partial.5), channel_id=1, source_target_pairs={{0,4},{4,0},{8,12},{12,8},{1,5},{5,1},{9,13},{13,9},{2,6},{6,2},{1... | collective-permute-start | bytes 786440 | tf_op jit(solution)/shard_map/ppermute | solution.py:195
  66.5 5.0 %collective-permute-start.21 = (bf16[1,1,128,512]{3,2,1,0:T(8,128)(2,1)S(1)}, bf16[1,1,128,512]{3,2,1,0:T(8,128)(2,1)S(1)}, u32[]{:S(2)}, u32[]{:S(2)}) collective-permute-start(bf16[1,1,128,512]{3,2,1,0:T(8,128)(2,1)S(1)} %get-tuple-element.53), channel_id=1, source_target_pairs={{0,8},{4,12},{8,0},{12,4},{1,9},{5,13},{9,1},{13,5},{2,10},{6,14},... | collective-permute-start | bytes 393224 | tf_op jit(solution)/shard_map/ppermute | solution.py:191
  67.2 4.3 %copy-start.5 = (bf16[3,2,128,512]{3,2,1,0:T(8,128)(2,1)}, bf16[3,2,128,512]{3,2,1,0:T(8,128)(2,1)S(1)}, u32[]{:S(2)}) copy-start(bf16[3,2,128,512]{3,2,1,0:T(8,128)(2,1)S(1)} %constant_dynamic-update-slice_fusion.6) | copy-start | bytes 2359300
  71.5 0.9 %copy-start.6 = (bf16[3,2,128,512]{3,2,1,0:T(8,128)(2,1)}, bf16[3,2,128,512]{3,2,1,0:T(8,128)(2,1)S(1)}, u32[]{:S(2)}) copy-start(bf16[3,2,128,512]{3,2,1,0:T(8,128)(2,1)S(1)} %constant_dynamic-update-slice_fusion) | copy-start | bytes 2359300

commit v4 on v3

--- a/solution.py
+++ b/solution.py
@@ -15,17 +15,14 @@
 SCALARS = pl.BlockSpec(memory_space=pltpu.SMEM)
 
 
-def call(kernel, outs, flops, name, *args, scalars=0):
-    moved = sum(x.size for x in args) + sum(math.prod(x) for x in outs)
+def call(kernel, outs, name, *args, scalars=0):
     return pl.pallas_call(
         kernel,
         in_specs=[SCALARS] * scalars + [WHOLE] * (len(args) - scalars),
         out_specs=[WHOLE] * len(outs),
         out_shape=[jax.ShapeDtypeStruct(x, BF16) for x in outs],
         compiler_params=pltpu.CompilerParams(vmem_limit_bytes=32 * 1024 * 1024),
-        cost_estimate=pl.CostEstimate(
-            flops=flops, bytes_accessed=2 * moved, transcendentals=0
-        ),
+        cost_estimate=pl.CostEstimate(flops=1, bytes_accessed=1, transcendentals=0),
         name=name,
     )(*args)
 
@@ -69,8 +66,7 @@
             chunks(rows, body)
 
     shape = (e, owned, rows, o)
-    flops = 2 * sources * e * math.prod(shape)
-    return call(kernel, [shape], flops, "mix", index.reshape(1), weights, whole, *others, scalars=2)[0]
+    return call(kernel, [shape], "mix", index.reshape(1), weights, whole, *others, scalars=2)[0]
 
 
 def partial_sums(row_pieces, weights):
@@ -92,7 +88,7 @@
 
     shape = (pieces, owned, rows, o)
     return call(
-        kernel, [shape] * e, 2 * e * e * math.prod(shape), "partial_sums", weights, *row_pieces, scalars=1
+        kernel, [shape] * e, "partial_sums", weights, *row_pieces, scalars=1
     )
 
 
@@ -116,7 +112,7 @@
 
     shape = (pieces, owned, rows, o)
     return call(
-        kernel, [shape], 2 * e * math.prod(shape), "add_partial", weights, *row_pieces, *received, scalars=1
+        kernel, [shape], "add_partial", weights, *row_pieces, *received, scalars=1
     )[0]
 
 
@@ -154,7 +150,6 @@
     return call(
         kernel,
         [shape] * lefts,
-        4 * lefts * o * math.prod(shape),
         "product",
         places,
         *a_pieces,

time: 72.7 us -> 72.7 us (level)
  no operation moved by 1% of the time
where the time goes in v4:
time: 72.7 us; the launch traced here: 72.4 us
  waiting for transfers between devices  29.8 us (41%)
  starting transfers between devices  17.7 us (24%)
  Pallas kernels  11.6 us (16%)
  local copies, waits for them, and re-layouts  9.64 us (13%)
  other arithmetic  2.8 us (4%)
  between operations  0.94 us (1%)
    ppermute x8, waiting for transfers between devices, to_owner(): return lax.ppermute(x, 'ph', pairs)  17.9 us
    pallas_call x9, Pallas kernels, call(): pl.pallas_call(kernel, in_specs=[SCALARS] * scalars + [WHOLE] * (len(args...  11.6 us
    ppermute x8, starting transfers between devices, to_owner(): return lax.ppermute(x, 'ph', pairs)  7.59 us
    ppermute x5, starting transfers between devices, from_energy(): return lax.ppermute(x, 'en', [((i + t) % en, i) for i in range(en)])  7.33 us
    ppermute x5, waiting for transfers between devices, from_energy(): return lax.ppermute(x, 'en', [((i + t) % en, i) for i in range(en)])  7.31 us
    unnamed x23, local copies, waits for them, and re-layouts  4.03 us
    dynamic_slice x3, local copies, waits for them, and re-layouts, blocks_of(): return lax.dynamic_slice_in_dim(x, owner_at(d) * owned, owned, axis=1)  3.67 us
    ppermute x1, waiting for transfers between devices, on_device(): lax.ppermute(weights[:, (i + 1) * e:(i + 2) * e], 'en', [(j, (j + t) % en...  2.92 us
  transfers between devices with their start and end apart: 22, of which 9 were waited for; matrix products, arithmetic and copies ran while one was open for 9% of the time, Pallas kernels for 14%

profile of v4, /device:TPU:0, one launch (start us, length us, event | category | flops | bytes accessed | tf_op | source)
XLA Modules:
  0.0 72.4 jit_solution(2700248841791021520)
XLA Ops:
  0.7 2.0 %constant_dynamic-slice_fusion.1 = (bf16[3,1,128,512]{3,2,1,0:T(8,128)(2,1)S(1)}, bf16[3,1,128,512]{3,2,1,0:T(8,128)(2,1)}) fusion(bf16[3,2,128,512]{3,2,1,0:T(8,128)(2,1)} %refs_0_.1, s32[]{:T(128)S(6)} %select_n.9, s32[]{:T(128)S(6)} %select_n.8), kind=kLoop, calls=%fused_computation.11 | loop fusion | bytes 1572872 | tf_op jit(solution)/shard_map/dynamic_slice | solution.py:196
  2.7 2.9 %collective-permute-start.6 = (bf16[3,1,128,512]{3,2,1,0:T(8,128)(2,1)S(1)}, bf16[3,1,128,512]{3,2,1,0:T(8,128)(2,1)S(1)}, u32[]{:S(2)}, u32[]{:S(2)}) collective-permute-start(bf16[3,1,128,512]{3,2,1,0:T(8,128)(2,1)S(1)} %get-tuple-element.56), channel_id=1, source_target_pairs={{16,0},{0,16},{17,1},{1,17},{18,2},{2,18},{19,3},{3,19},{20,4},{4,... | collective-permute-start | bytes 1179656 | tf_op jit(solution)/shard_map/ppermute | solution.py:193
  5.6 0.7 copy-done.10
  6.3 1.5 %collective-permute-start.3 = (f32[2,3,2]{1,2,0:T(2,128)S(1)}, f32[2,3,2]{1,2,0:T(2,128)S(1)}, u32[]{:S(2)}, u32[]{:S(2)}) collective-permute-start(f32[2,3,2]{1,2,0:T(2,128)S(1)} %pad_maximum_fusion.2), channel_id=1, source_target_pairs={{0,8},{4,12},{8,0},{12,4},{1,9},{5,13},{9,1},{13,5},{2,10},{6,14},... | collective-permute-start | bytes 152 | tf_op jit(solution)/shard_map/ppermute | solution.py:186
  7.8 0.8 %constant_dynamic-slice_fusion = (bf16[3,1,128,512]{3,2,1,0:T(8,128)(2,1)S(1)}, bf16[3,1,128,512]{3,2,1,0:T(8,128)(2,1)}) fusion(bf16[3,2,128,512]{3,2,1,0:T(8,128)(2,1)S(1)} %copy-done.7, s32[]{:T(128)S(6)} %select_n.8, s32[]{:T(128)S(6)} %select_n.9), kind=kLoop, calls=%fused_computation.10 | loop fusion | bytes 1572872 | tf_op jit(solution)/shard_map/dynamic_slice | solution.py:196
  8.7 0.5 collective-permute-start.7
  9.2 0.8 %constant_dynamic-slice_fusion.3 = (bf16[3,1,128,512]{3,2,1,0:T(8,128)(2,1)}, bf16[3,1,128,512]{3,2,1,0:T(8,128)(2,1)S(1)}) fusion(bf16[3,2,128,512]{3,2,1,0:T(8,128)(2,1)S(1)} %copy-done.8, s32[]{:T(128)S(6)} %select_n.9, s32[]{:T(128)S(6)} %select_n.8), kind=kLoop, calls=%fused_computation.13 | loop fusion | bytes 1572872 | tf_op jit(solution)/shard_map/dynamic_slice | solution.py:196
  10.0 1.5 %collective-permute-start = (bf16[3,1,128,512]{3,2,1,0:T(8,128)(2,1)}, bf16[3,1,128,512]{3,2,1,0:T(8,128)(2,1)S(1)}, u32[]{:S(2)}, u32[]{:S(2)}) collective-permute-start(bf16[3,1,128,512]{3,2,1,0:T(8,128)(2,1)} %get-tuple-element.28), channel_id=1, source_target_pairs={{0,8},{4,12},{8,0},{12,4},{1,9},{5,13},{9,1},{13,5},{2,10},{6,14},... | collective-permute-start | bytes 1179656 | tf_op jit(solution)/shard_map/ppermute | solution.py:186
  11.5 0.7 collective-permute-start.8
  12.2 0.1 copy.12
  12.3 0.1 pad_add_fusion.1
  12.4 0.1 iota_add_fusion
  12.4 0.6 add.81
  13.1 0.7 subtract_convert_fusion
  13.8 0.0 collective-permute-done.3
  13.8 0.6 pad_maximum_fusion
  14.4 0.1 copy.13
  14.5 1.4 %collective-permute-done.4 = f32[2,3,4]{1,2,0:T(4,128)} collective-permute-done((f32[2,3,4]{1,2,0:T(4,128)}, f32[2,3,4]{1,2,0:T(4,128)}, u32[]{:S(2)}, u32[]{:S(2)}) %collective-permute-start.4) | collective-permute-done | bytes 128 | tf_op jit(solution)/shard_map/ppermute | solution.py:190
  15.9 0.8 %copy.14 = f32[2,3,4]{2,0,1:T(2,128)S(1)} copy(f32[2,3,4]{1,2,0:T(4,128)} %collective-permute-done.4) | data formatting | bytes 192 | tf_op jit(solution)/shard_map/ppermute | solution.py:190
  16.6 0.1 pad_maximum_fusion.1
  16.7 0.2 select_reduce_fusion.weight_ref
  16.9 1.0 %mix.2 = bf16[3,1,128,512]{3,2,1,0:T(8,128)(2,1)S(1)} custom-call(s32[1]{0:T(128)} %bitcast.9.index_ref, f32[3,6]{1,0:T(4,128)S(1)} %select_reduce_fusion.weight_ref, bf16[3,2,128,512]{3,2,1,0:T(8,128)(2,1)S(1)} %copy-done, bf16[3,1,128,512]{3,2,1,0:T(8,128)(2,1)S(1)} %collective-permute-done.6.refs_1_), custom_call_target="tpu_custom_call" | custom-call | flops 1 | bytes 1 | tf_op jit(solution)/shard_map/mix/pallas_call | solution.py:19
  17.9 0.8 %collective-permute-start.11 = (bf16[3,1,128,512]{3,2,1,0:T(8,128)(2,1)S(1)}, bf16[3,1,128,512]{3,2,1,0:T(8,128)(2,1)}, u32[]{:S(2)}, u32[]{:S(2)}) collective-permute-start(bf16[3,1,128,512]{3,2,1,0:T(8,128)(2,1)S(1)} %mix.2), channel_id=1, source_target_pairs={{0,8},{4,12},{8,0},{12,4},{1,9},{5,13},{9,1},{13,5},{2,10},{6,14},... | collective-permute-start | bytes 1179656 | tf_op jit(solution)/shard_map/ppermute | solution.py:186
  18.7 0.1 slice.11
  18.8 1.5 %collective-permute-start.5 = (f32[3,3]{1,0:T(4,128)S(1)}, f32[3,3]{1,0:T(4,128)S(1)}, u32[]{:S(2)}, u32[]{:S(2)}) collective-permute-start(f32[3,3]{1,0:T(4,128)S(1)} %slice.11), channel_id=1, source_target_pairs={{0,16},{16,0},{1,17},{17,1},{2,18},{18,2},{3,19},{19,3},{4,20},{20... | collective-permute-start | bytes 116 | tf_op jit(solution)/shard_map/ppermute | solution.py:228
  20.3 2.9 %collective-permute-done.5.weight_ref = f32[3,3]{1,0:T(4,128)S(1)} collective-permute-done((f32[3,3]{1,0:T(4,128)S(1)}, f32[3,3]{1,0:T(4,128)S(1)}, u32[]{:S(2)}, u32[]{:S(2)}) %collective-permute-start.5) | collective-permute-done | bytes 68 | tf_op jit(solution)/shard_map/ppermute | solution.py:228
  23.2 0.0 collective-permute-start.1
  23.2 0.0 collective-permute-done.7.refs_1_
  23.2 1.7 %partial_sums.1 = (bf16[2,1,128,512]{3,2,1,0:T(8,128)(2,1)S(1)}, bf16[2,1,128,512]{3,2,1,0:T(8,128)(2,1)}, bf16[2,1,128,512]{3,2,1,0:T(8,128)(2,1)S(1)}) custom-call(f32[3,3]{1,0:T(4,128)S(1)} %collective-permute-done.5.weight_ref, bf16[3,1,128,512]{3,2,1,0:T(8,128)(2,1)S(1)} %get-tuple-element.33.refs_0_, ...), custom_call_target="tpu_custom_call" | custom-call | flops 1 | bytes 1 | tf_op jit(solution)/shard_map/partial_sums/pallas_call | solution.py:19
  24.9 0.7 copy-done.3
  25.6 1.7 %collective-permute-start.9 = (bf16[2,1,128,512]{3,2,1,0:T(8,128)(2,1)S(1)}, bf16[2,1,128,512]{3,2,1,0:T(8,128)(2,1)S(1)}, u32[]{:S(2)}, u32[]{:S(2)}) collective-permute-start(bf16[2,1,128,512]{3,2,1,0:T(8,128)(2,1)S(1)} %get-tuple-element.37), channel_id=1, source_target_pairs={{16,0},{0,16},{17,1},{1,17},{18,2},{2,18},{19,3},{3,19},{20,4},{4,... | collective-permute-start | bytes 786440 | tf_op jit(solution)/shard_map/ppermute | solution.py:193
  27.3 2.0 %collective-permute-done.refs_1_ = bf16[3,1,128,512]{3,2,1,0:T(8,128)(2,1)S(1)} collective-permute-done((bf16[3,1,128,512]{3,2,1,0:T(8,128)(2,1)}, bf16[3,1,128,512]{3,2,1,0:T(8,128)(2,1)S(1)}, u32[]{:S(2)}, u32[]{:S(2)}) %collective-permute-start) | collective-permute-done | bytes 393248 | tf_op jit(solution)/shard_map/ppermute | solution.py:186
  29.4 0.7 %copy-done.1 = bf16[3,1,128,512]{3,2,1,0:T(8,128)(2,1)} copy-done((bf16[3,1,128,512]{3,2,1,0:T(8,128)(2,1)}, bf16[3,1,128,512]{3,2,1,0:T(8,128)(2,1)S(1)}, u32[]{:S(2)}) %copy-start.1) | copy-done | bytes 393240
  30.1 1.0 %copy-done.2 = bf16[3,1,128,512]{3,2,1,0:T(8,128)(2,1)S(1)} copy-done((bf16[3,1,128,512]{3,2,1,0:T(8,128)(2,1)S(1)}, bf16[3,1,128,512]{3,2,1,0:T(8,128)(2,1)}, u32[]{:S(2)}) %copy-start.2) | copy-done | bytes 393240
  31.1 1.0 %mix.3.refs_4_ = bf16[3,1,128,512]{3,2,1,0:T(8,128)(2,1)S(1)} custom-call(s32[1]{0:T(128)} %bitcast.8.index_ref, f32[3,6]{1,0:T(4,128)S(1)} %select_reduce_fusion.weight_ref, bf16[3,2,128,512]{3,2,1,0:T(8,128)(2,1)S(1)} %copy-done, bf16[3,1,128,512]{3,2,1,0:T(8,128)(2,1)S(1)} %copy-done.2), custom_call_target="tpu_custom_call" | custom-call | flops 1 | bytes 1 | tf_op jit(solution)/shard_map/mix/pallas_call | solution.py:19
  32.1 0.6 collective-permute-start.12
  32.7 3.5 %collective-permute-done.11.refs_5_ = bf16[3,1,128,512]{3,2,1,0:T(8,128)(2,1)} collective-permute-done((bf16[3,1,128,512]{3,2,1,0:T(8,128)(2,1)S(1)}, bf16[3,1,128,512]{3,2,1,0:T(8,128)(2,1)}, u32[]{:S(2)}, u32[]{:S(2)}) %collective-permute-start.11) | collective-permute-done | bytes 393248 | tf_op jit(solution)/shard_map/ppermute | solution.py:186
  36.1 0.9 %add_partial.3.refs_4_ = bf16[2,1,128,512]{3,2,1,0:T(8,128)(2,1)S(1)} custom-call(f32[3,6]{1,0:T(4,128)S(1)} %select_reduce_fusion.weight_ref, bf16[3,1,128,512]{3,2,1,0:T(8,128)(2,1)S(1)} %get-tuple-element.33.refs_0_, bf16[3,1,128,512]{3,2,1,0:T(8,128)(2,1)S(1)} %collective-permute-done.7.refs_1_, bf16[2,1,128,512]{3,2,1,0:T(8,128)(2,1)S(1)} %collective-permute-done.9.refs_2_), custom_call_target="tpu_custom_call" | custom-call | flops 1 | bytes 1 | tf_op jit(solution)/shard_map/add_partial/pallas_call | solution.py:19
  37.0 0.6 collective-permute-start.10
  37.6 1.0 %collective-permute-start.16 = (bf16[2,1,128,512]{3,2,1,0:T(8,128)(2,1)}, bf16[2,1,128,512]{3,2,1,0:T(8,128)(2,1)}, u32[]{:S(2)}, u32[]{:S(2)}) collective-permute-start(bf16[2,1,128,512]{3,2,1,0:T(8,128)(2,1)} %get-tuple-element.44), channel_id=1, source_target_pairs={{16,0},{0,16},{17,1},{1,17},{18,2},{2,18},{19,3},{3,19},{20,4},{4,... | collective-permute-start | bytes 786440 | tf_op jit(solution)/shard_map/ppermute | solution.py:193
  38.5 0.1 pad_add_fusion.place_ref
  38.6 0.3 collective-permute-done.10.refs_5_
  38.9 1.5 %product.4 = (bf16[1,1,128,512]{3,2,1,0:T(8,128)(2,1)S(1)}, bf16[1,1,128,512]{3,2,1,0:T(8,128)(2,1)S(1)}) custom-call(s32[4]{0:T(128)S(1)} %pad_add_fusion.place_ref, bf16[3,1,128,512]{3,2,1,0:T(8,128)(2,1)S(1)} %get-tuple-element.30.refs_0_, bf16[3,1,128,512]{3,2,1,0:T(8,128)(2,1)S(1)} %collective-permute-done.refs_1_, ...), custom_call_target="tpu_custom_call" | custom-call | flops 1 | bytes 1 | tf_op jit(solution)/shard_map/product/pallas_call | solution.py:19
  40.4 2.4 %product.5 = (bf16[3,1,128,512]{3,2,1,0:T(8,128)(2,1)S(1)}, bf16[3,1,128,512]{3,2,1,0:T(8,128)(2,1)S(1)}) custom-call(s32[4]{0:T(128)S(1)} %pad_add_fusion.place_ref, bf16[3,1,128,512]{3,2,1,0:T(8,128)(2,1)S(1)} %get-tuple-element.30.refs_0_, bf16[3,1,128,512]{3,2,1,0:T(8,128)(2,1)S(1)} %collective-permute-done.refs_1_, ...), custom_call_target="tpu_custom_call" | custom-call | flops 1 | bytes 1 | tf_op jit(solution)/shard_map/product/pallas_call | solution.py:19
  42.8 3.4 %collective-permute-done.16.refs_2_ = bf16[2,1,128,512]{3,2,1,0:T(8,128)(2,1)} collective-permute-done((bf16[2,1,128,512]{3,2,1,0:T(8,128)(2,1)}, bf16[2,1,128,512]{3,2,1,0:T(8,128)(2,1)}, u32[]{:S(2)}, u32[]{:S(2)}) %collective-permute-start.16) | collective-permute-done | bytes 262176 | tf_op jit(solution)/shard_map/ppermute | solution.py:193
  46.2 1.3 %add_partial.4.refs_4_ = bf16[2,1,128,512]{3,2,1,0:T(8,128)(2,1)S(1)} custom-call(f32[3,6]{1,0:T(4,128)S(1)} %select_reduce_fusion.weight_ref, bf16[3,1,128,512]{3,2,1,0:T(8,128)(2,1)S(1)} %get-tuple-element.33.refs_0_, bf16[3,1,128,512]{3,2,1,0:T(8,128)(2,1)S(1)} %collective-permute-done.7.refs_1_, bf16[2,1,128,512]{3,2,1,0:T(8,128)(2,1)} %collective-permute-done.16.refs_2_), custom_call_target="tpu_custom_call" | custom-call | flops 1 | bytes 1 | tf_op jit(solution)/shard_map/add_partial/pallas_call | solution.py:19
  47.5 0.1 collective-permute-start.17
  47.5 1.0 %collective-permute-start.19 = (bf16[2,1,128,512]{3,2,1,0:T(8,128)(2,1)S(1)}, bf16[2,1,128,512]{3,2,1,0:T(8,128)(2,1)S(1)}, u32[]{:S(2)}, u32[]{:S(2)}) collective-permute-start(bf16[2,1,128,512]{3,2,1,0:T(8,128)(2,1)S(1)} %copy-done.4), channel_id=1, source_target_pairs={{16,0},{0,16},{17,1},{1,17},{18,2},{2,18},{19,3},{3,19},{20,4},{4,... | collective-permute-start | bytes 786440 | tf_op jit(solution)/shard_map/ppermute | solution.py:193
  48.6 0.5 collective-permute-start.15
  49.1 0.1 broadcast.24.clone.1
  49.2 1.6 %collective-permute-start.14 = (bf16[3,1,128,512]{3,2,1,0:T(8,128)(2,1)S(1)}, bf16[3,1,128,512]{3,2,1,0:T(8,128)(2,1)S(1)}, u32[]{:S(2)}, u32[]{:S(2)}) collective-permute-start(bf16[3,1,128,512]{3,2,1,0:T(8,128)(2,1)S(1)} %get-tuple-element.41), channel_id=1, source_target_pairs={{0,8},{4,12},{8,0},{12,4},{1,9},{5,13},{9,1},{13,5},{2,10},{6,14},... | collective-permute-start | bytes 1179656 | tf_op jit(solution)/shard_map/ppermute | solution.py:186
  50.8 1.1 %product.6 = (bf16[1,1,128,512]{3,2,1,0:T(8,128)(2,1)S(1)}, bf16[1,1,128,512]{3,2,1,0:T(8,128)(2,1)S(1)}) custom-call(s32[4]{0:T(128)S(1)} %pad_add_fusion.place_ref, bf16[3,1,128,512]{3,2,1,0:T(8,128)(2,1)S(1)} %get-tuple-element.30.refs_0_, bf16[3,1,128,512]{3,2,1,0:T(8,128)(2,1)S(1)} %collective-permute-done.refs_1_, ...), custom_call_target="tpu_custom_call" | custom-call | flops 1 | bytes 1 | tf_op jit(solution)/shard_map/product/pallas_call | solution.py:19
  51.8 0.6 collective-permute-start.18
  52.4 3.9 %collective-permute-done.19.refs_2_ = bf16[2,1,128,512]{3,2,1,0:T(8,128)(2,1)S(1)} collective-permute-done((bf16[2,1,128,512]{3,2,1,0:T(8,128)(2,1)S(1)}, bf16[2,1,128,512]{3,2,1,0:T(8,128)(2,1)S(1)}, u32[]{:S(2)}, u32[]{:S(2)}) %collective-permute-start.19) | collective-permute-done | bytes 262176 | tf_op jit(solution)/shard_map/ppermute | solution.py:193
  56.3 0.9 %add_partial.5 = bf16[2,1,128,512]{3,2,1,0:T(8,128)(2,1)S(1)} custom-call(f32[3,6]{1,0:T(4,128)S(1)} %select_reduce_fusion.weight_ref, bf16[3,1,128,512]{3,2,1,0:T(8,128)(2,1)S(1)} %get-tuple-element.33.refs_0_, bf16[3,1,128,512]{3,2,1,0:T(8,128)(2,1)S(1)} %collective-permute-done.7.refs_1_, bf16[2,1,128,512]{3,2,1,0:T(8,128)(2,1)S(1)} %collective-permute-done.19.refs_2_), custom_call_target="tpu_custom_call" | custom-call | flops 1 | bytes 1 | tf_op jit(solution)/shard_map/add_partial/pallas_call | solution.py:19
  57.1 0.1 collective-permute-start.20
  57.3 8.1 %collective-permute-done.18 = bf16[1,1,128,512]{3,2,1,0:T(8,128)(2,1)S(1)} collective-permute-done((bf16[1,1,128,512]{3,2,1,0:T(8,128)(2,1)S(1)}, bf16[1,1,128,512]{3,2,1,0:T(8,128)(2,1)S(1)}, u32[]{:S(2)}, u32[]{:S(2)}) %collective-permute-start.18) | collective-permute-done | bytes 131104 | tf_op jit(solution)/shard_map/ppermute | solution.py:186
  65.4 1.1 %product.7 = (bf16[3,2,128,512]{3,2,1,0:T(8,128)(2,1)S(1)}, bf16[1,1,128,512]{3,2,1,0:T(8,128)(2,1)S(1)}) fusion(bf16[3,2,128,512]{3,2,1,0:T(8,128)(2,1)S(1)} %constant_dynamic-update-slice_fusion.2, s32[]{:T(128)S(6)} %select_n.8, s32[4]{0:T(128)S(1)} %pad_add_fusion.place_ref, bf16[3,1,128,512]{3,2,1,0:T(8,128)(2,1)S(1)} %get-tuple-element.30.refs_0_, ...), kind=kCustom, calls=%fused_computation.3 | custom fusion | flops 1 | bytes 2359812 | tf_op jit(solution)/shard_map/product/pallas_call | solution.py:19
  66.5 0.6 collective-permute-start.21
  67.0 0.1 broadcast.24.clone
  67.2 0.0 copy-start.5
  67.2 4.3 %collective-permute-done.21 = bf16[1,1,128,512]{3,2,1,0:T(8,128)(2,1)S(1)} collective-permute-done((bf16[1,1,128,512]{3,2,1,0:T(8,128)(2,1)S(1)}, bf16[1,1,128,512]{3,2,1,0:T(8,128)(2,1)S(1)}, u32[]{:S(2)}, u32[]{:S(2)}) %collective-permute-start.21) | collective-permute-done | bytes 131104 | tf_op jit(solution)/shard_map/ppermute | solution.py:186
  71.5 0.0 copy-start.6
  71.5 0.9 %copy-done.6 = bf16[3,2,128,512]{3,2,1,0:T(8,128)(2,1)} copy-done((bf16[3,2,128,512]{3,2,1,0:T(8,128)(2,1)}, bf16[3,2,128,512]{3,2,1,0:T(8,128)(2,1)S(1)}, u32[]{:S(2)}) %copy-start.6) | copy-done | bytes 786456
  (40 shorter events, 0.2 us)
Async XLA Ops:
  0.7 7.2 %copy-start.7 = (bf16[3,2,128,512]{3,2,1,0:T(8,128)(2,1)S(1)}, bf16[3,2,128,512]{3,2,1,0:T(8,128)(2,1)}, u32[]{:S(2)}) copy-start(bf16[3,2,128,512]{3,2,1,0:T(8,128)(2,1)} %param.6) | copy-start | bytes 2359300
  2.7 2.9 %copy-start.9 = (s32[3,2]{0,1:T(2,128)S(1)}, s32[3,2]{0,1:T(2,128)}, u32[]{:S(2)}) copy-start(s32[3,2]{0,1:T(2,128)} %param.8) | copy-start | bytes 76
  2.7 14.2 %collective-permute-start.6 = (bf16[3,1,128,512]{3,2,1,0:T(8,128)(2,1)S(1)}, bf16[3,1,128,512]{3,2,1,0:T(8,128)(2,1)S(1)}, u32[]{:S(2)}, u32[]{:S(2)}) collective-permute-start(bf16[3,1,128,512]{3,2,1,0:T(8,128)(2,1)S(1)} %get-tuple-element.56), channel_id=1, source_target_pairs={{16,0},{0,16},{17,1},{1,17},{18,2},{2,18},{19,3},{3,19},{20,4},{4,... | collective-permute-start | bytes 1179656 | tf_op jit(solution)/shard_map/ppermute | solution.py:193
  5.6 0.7 copy-start.10
  6.3 2.9 %copy-start.8 = (bf16[3,2,128,512]{3,2,1,0:T(8,128)(2,1)S(1)}, bf16[3,2,128,512]{3,2,1,0:T(8,128)(2,1)}, u32[]{:S(2)}) copy-start(bf16[3,2,128,512]{3,2,1,0:T(8,128)(2,1)} %param.7) | copy-start | bytes 2359300
  6.3 7.5 %collective-permute-start.3 = (f32[2,3,2]{1,2,0:T(2,128)S(1)}, f32[2,3,2]{1,2,0:T(2,128)S(1)}, u32[]{:S(2)}, u32[]{:S(2)}) collective-permute-start(f32[2,3,2]{1,2,0:T(2,128)S(1)} %pad_maximum_fusion.2), channel_id=1, source_target_pairs={{0,8},{4,12},{8,0},{12,4},{1,9},{5,13},{9,1},{13,5},{2,10},{6,14},... | collective-permute-start | bytes 152 | tf_op jit(solution)/shard_map/ppermute | solution.py:186
  8.7 8.2 %copy-start = (bf16[3,2,128,512]{3,2,1,0:T(8,128)(2,1)S(1)}, bf16[3,2,128,512]{3,2,1,0:T(8,128)(2,1)}, u32[]{:S(2)}) copy-start(bf16[3,2,128,512]{3,2,1,0:T(8,128)(2,1)} %refs_0_.1) | copy-start | bytes 2359300
  8.7 14.5 %collective-permute-start.7 = (bf16[3,1,128,512]{3,2,1,0:T(8,128)(2,1)}, bf16[3,1,128,512]{3,2,1,0:T(8,128)(2,1)S(1)}, u32[]{:S(2)}, u32[]{:S(2)}) collective-permute-start(bf16[3,1,128,512]{3,2,1,0:T(8,128)(2,1)} %get-tuple-element.27), channel_id=1, source_target_pairs={{0,8},{4,12},{8,0},{12,4},{1,9},{5,13},{9,1},{13,5},{2,10},{6,14},... | collective-permute-start | bytes 1179656 | tf_op jit(solution)/shard_map/ppermute | solution.py:186
  10.0 19.4 %collective-permute-start = (bf16[3,1,128,512]{3,2,1,0:T(8,128)(2,1)}, bf16[3,1,128,512]{3,2,1,0:T(8,128)(2,1)S(1)}, u32[]{:S(2)}, u32[]{:S(2)}) collective-permute-start(bf16[3,1,128,512]{3,2,1,0:T(8,128)(2,1)} %get-tuple-element.28), channel_id=1, source_target_pairs={{0,8},{4,12},{8,0},{12,4},{1,9},{5,13},{9,1},{13,5},{2,10},{6,14},... | collective-permute-start | bytes 1179656 | tf_op jit(solution)/shard_map/ppermute | solution.py:186
  11.5 17.8 %collective-permute-start.8 = (bf16[3,1,128,512]{3,2,1,0:T(8,128)(2,1)}, bf16[3,1,128,512]{3,2,1,0:T(8,128)(2,1)S(1)}, u32[]{:S(2)}, u32[]{:S(2)}) collective-permute-start(bf16[3,1,128,512]{3,2,1,0:T(8,128)(2,1)} %get-tuple-element.29), channel_id=1, source_target_pairs={{16,0},{0,16},{17,1},{1,17},{18,2},{2,18},{19,3},{3,19},{20,4},{4,... | collective-permute-start | bytes 1179656 | tf_op jit(solution)/shard_map/ppermute | solution.py:193
  14.4 1.5 %collective-permute-start.4 = (f32[2,3,4]{1,2,0:T(4,128)}, f32[2,3,4]{1,2,0:T(4,128)}, u32[]{:S(2)}, u32[]{:S(2)}) collective-permute-start(f32[2,3,4]{1,2,0:T(4,128)} %pad_maximum_fusion), channel_id=1, source_target_pairs={{0,4},{4,0},{8,12},{12,8},{1,5},{5,1},{9,13},{13,9},{2,6},{6,2},{1... | collective-permute-start | bytes 296 | tf_op jit(solution)/shard_map/ppermute | solution.py:190
  17.9 18.2 %collective-permute-start.11 = (bf16[3,1,128,512]{3,2,1,0:T(8,128)(2,1)S(1)}, bf16[3,1,128,512]{3,2,1,0:T(8,128)(2,1)}, u32[]{:S(2)}, u32[]{:S(2)}) collective-permute-start(bf16[3,1,128,512]{3,2,1,0:T(8,128)(2,1)S(1)} %mix.2), channel_id=1, source_target_pairs={{0,8},{4,12},{8,0},{12,4},{1,9},{5,13},{9,1},{13,5},{2,10},{6,14},... | collective-permute-start | bytes 1179656 | tf_op jit(solution)/shard_map/ppermute | solution.py:186
  18.8 4.4 %collective-permute-start.5 = (f32[3,3]{1,0:T(4,128)S(1)}, f32[3,3]{1,0:T(4,128)S(1)}, u32[]{:S(2)}, u32[]{:S(2)}) collective-permute-start(f32[3,3]{1,0:T(4,128)S(1)} %slice.11), channel_id=1, source_target_pairs={{0,16},{16,0},{1,17},{17,1},{2,18},{18,2},{3,19},{19,3},{4,20},{20... | collective-permute-start | bytes 116 | tf_op jit(solution)/shard_map/ppermute | solution.py:228
  23.2 14.4 %collective-permute-start.1 = (bf16[3,1,128,512]{3,2,1,0:T(8,128)(2,1)S(1)}, bf16[3,1,128,512]{3,2,1,0:T(8,128)(2,1)S(1)}, u32[]{:S(2)}, u32[]{:S(2)}) collective-permute-start(bf16[3,1,128,512]{3,2,1,0:T(8,128)(2,1)S(1)} %get-tuple-element.30.refs_0_), channel_id=1, source_target_pairs={{0,4},{4,0},{8,12},{12,8},{1,5},{5,1},{9,13},{13,9},{2,6},{6,2},{1... | collective-permute-start | bytes 1179656 | tf_op jit(solution)/shard_map/ppermute | solution.py:190
  24.9 0.7 copy-start.3
  25.6 10.5 %collective-permute-start.9 = (bf16[2,1,128,512]{3,2,1,0:T(8,128)(2,1)S(1)}, bf16[2,1,128,512]{3,2,1,0:T(8,128)(2,1)S(1)}, u32[]{:S(2)}, u32[]{:S(2)}) collective-permute-start(bf16[2,1,128,512]{3,2,1,0:T(8,128)(2,1)S(1)} %get-tuple-element.37), channel_id=1, source_target_pairs={{16,0},{0,16},{17,1},{1,17},{18,2},{2,18},{19,3},{3,19},{20,4},{4,... | collective-permute-start | bytes 786440 | tf_op jit(solution)/shard_map/ppermute | solution.py:193
  29.4 9.3 %collective-permute-start.2 = (bf16[3,1,128,512]{3,2,1,0:T(8,128)(2,1)S(1)}, bf16[3,1,128,512]{3,2,1,0:T(8,128)(2,1)S(1)}, u32[]{:S(2)}, u32[]{:S(2)}) collective-permute-start(bf16[3,1,128,512]{3,2,1,0:T(8,128)(2,1)S(1)} %collective-permute-done.refs_1_), channel_id=1, source_target_pairs={{0,4},{4,0},{8,12},{12,8},{1,5},{5,1},{9,13},{13,9},{2,6},{6,2},{1... | collective-permute-start | bytes 1179656 | tf_op jit(solution)/shard_map/ppermute | solution.py:190
  29.4 0.7 %copy-start.1 = (bf16[3,1,128,512]{3,2,1,0:T(8,128)(2,1)}, bf16[3,1,128,512]{3,2,1,0:T(8,128)(2,1)S(1)}, u32[]{:S(2)}) copy-start(bf16[3,1,128,512]{3,2,1,0:T(8,128)(2,1)S(1)} %collective-permute-done.8.refs_1_) | copy-start | bytes 1179652
  30.1 1.0 %copy-start.2 = (bf16[3,1,128,512]{3,2,1,0:T(8,128)(2,1)S(1)}, bf16[3,1,128,512]{3,2,1,0:T(8,128)(2,1)}, u32[]{:S(2)}) copy-start(bf16[3,1,128,512]{3,2,1,0:T(8,128)(2,1)} %copy-done.1) | copy-start | bytes 1179652
  32.1 8.3 %collective-permute-start.12 = (bf16[3,1,128,512]{3,2,1,0:T(8,128)(2,1)S(1)}, bf16[3,1,128,512]{3,2,1,0:T(8,128)(2,1)S(1)}, u32[]{:S(2)}, u32[]{:S(2)}) collective-permute-start(bf16[3,1,128,512]{3,2,1,0:T(8,128)(2,1)S(1)} %mix.3.refs_4_), channel_id=1, source_target_pairs={{0,4},{4,0},{8,12},{12,8},{1,5},{5,1},{9,13},{13,9},{2,6},{6,2},{1... | collective-permute-start | bytes 1179656 | tf_op jit(solution)/shard_map/ppermute | solution.py:190
  36.1 4.2 %collective-permute-start.13 = (bf16[3,1,128,512]{3,2,1,0:T(8,128)(2,1)}, bf16[3,1,128,512]{3,2,1,0:T(8,128)(2,1)}, u32[]{:S(2)}, u32[]{:S(2)}) collective-permute-start(bf16[3,1,128,512]{3,2,1,0:T(8,128)(2,1)} %collective-permute-done.11.refs_5_), channel_id=1, source_target_pairs={{0,4},{4,0},{8,12},{12,8},{1,5},{5,1},{9,13},{13,9},{2,6},{6,2},{1... | collective-permute-start | bytes 1179656 | tf_op jit(solution)/shard_map/ppermute | solution.py:190
  37.0 1.9 %collective-permute-start.10 = (bf16[2,1,128,512]{3,2,1,0:T(8,128)(2,1)S(1)}, bf16[2,1,128,512]{3,2,1,0:T(8,128)(2,1)}, u32[]{:S(2)}, u32[]{:S(2)}) collective-permute-start(bf16[2,1,128,512]{3,2,1,0:T(8,128)(2,1)S(1)} %add_partial.3.refs_4_), channel_id=1, source_target_pairs={{0,4},{4,0},{8,12},{12,8},{1,5},{5,1},{9,13},{13,9},{2,6},{6,2},{1... | collective-permute-start | bytes 786440 | tf_op jit(solution)/shard_map/ppermute | solution.py:190
  37.6 8.6 %collective-permute-start.16 = (bf16[2,1,128,512]{3,2,1,0:T(8,128)(2,1)}, bf16[2,1,128,512]{3,2,1,0:T(8,128)(2,1)}, u32[]{:S(2)}, u32[]{:S(2)}) collective-permute-start(bf16[2,1,128,512]{3,2,1,0:T(8,128)(2,1)} %get-tuple-element.44), channel_id=1, source_target_pairs={{16,0},{0,16},{17,1},{1,17},{18,2},{2,18},{19,3},{3,19},{20,4},{4,... | collective-permute-start | bytes 786440 | tf_op jit(solution)/shard_map/ppermute | solution.py:193
  42.7 4.8 %copy-start.4 = (bf16[2,1,128,512]{3,2,1,0:T(8,128)(2,1)S(1)}, bf16[2,1,128,512]{3,2,1,0:T(8,128)(2,1)}, u32[]{:S(2)}) copy-start(bf16[2,1,128,512]{3,2,1,0:T(8,128)(2,1)} %copy-done.3) | copy-start | bytes 786436
  47.5 3.3 %collective-permute-start.17 = (bf16[2,1,128,512]{3,2,1,0:T(8,128)(2,1)S(1)}, bf16[2,1,128,512]{3,2,1,0:T(8,128)(2,1)S(1)}, u32[]{:S(2)}, u32[]{:S(2)}) collective-permute-start(bf16[2,1,128,512]{3,2,1,0:T(8,128)(2,1)S(1)} %add_partial.4.refs_4_), channel_id=1, source_target_pairs={{0,4},{4,0},{8,12},{12,8},{1,5},{5,1},{9,13},{13,9},{2,6},{6,2},{1... | collective-permute-start | bytes 786440 | tf_op jit(solution)/shard_map/ppermute | solution.py:190
  47.5 8.7 %collective-permute-start.19 = (bf16[2,1,128,512]{3,2,1,0:T(8,128)(2,1)S(1)}, bf16[2,1,128,512]{3,2,1,0:T(8,128)(2,1)S(1)}, u32[]{:S(2)}, u32[]{:S(2)}) collective-permute-start(bf16[2,1,128,512]{3,2,1,0:T(8,128)(2,1)S(1)} %copy-done.4), channel_id=1, source_target_pairs={{16,0},{0,16},{17,1},{1,17},{18,2},{2,18},{19,3},{3,19},{20,4},{4,... | collective-permute-start | bytes 786440 | tf_op jit(solution)/shard_map/ppermute | solution.py:193
  48.6 8.6 %collective-permute-start.15 = (bf16[1,1,128,512]{3,2,1,0:T(8,128)(2,1)S(1)}, bf16[1,1,128,512]{3,2,1,0:T(8,128)(2,1)S(1)}, u32[]{:S(2)}, u32[]{:S(2)}) collective-permute-start(bf16[1,1,128,512]{3,2,1,0:T(8,128)(2,1)S(1)} %get-tuple-element.38), channel_id=1, source_target_pairs={{0,8},{4,12},{8,0},{12,4},{1,9},{5,13},{9,1},{13,5},{2,10},{6,14},... | collective-permute-start | bytes 393224 | tf_op jit(solution)/shard_map/ppermute | solution.py:186
  49.2 18.0 %collective-permute-start.14 = (bf16[3,1,128,512]{3,2,1,0:T(8,128)(2,1)S(1)}, bf16[3,1,128,512]{3,2,1,0:T(8,128)(2,1)S(1)}, u32[]{:S(2)}, u32[]{:S(2)}) collective-permute-start(bf16[3,1,128,512]{3,2,1,0:T(8,128)(2,1)S(1)} %get-tuple-element.41), channel_id=1, source_target_pairs={{0,8},{4,12},{8,0},{12,4},{1,9},{5,13},{9,1},{13,5},{2,10},{6,14},... | collective-permute-start | bytes 1179656 | tf_op jit(solution)/shard_map/ppermute | solution.py:186
  51.8 13.5 %collective-permute-start.18 = (bf16[1,1,128,512]{3,2,1,0:T(8,128)(2,1)S(1)}, bf16[1,1,128,512]{3,2,1,0:T(8,128)(2,1)S(1)}, u32[]{:S(2)}, u32[]{:S(2)}) collective-permute-start(bf16[1,1,128,512]{3,2,1,0:T(8,128)(2,1)S(1)} %get-tuple-element.46), channel_id=1, source_target_pairs={{0,8},{4,12},{8,0},{12,4},{1,9},{5,13},{9,1},{13,5},{2,10},{6,14},... | collective-permute-start | bytes 393224 | tf_op jit(solution)/shard_map/ppermute | solution.py:186
  57.1 8.3 %collective-permute-start.20 = (bf16[2,1,128,512]{3,2,1,0:T(8,128)(2,1)S(1)}, bf16[2,1,128,512]{3,2,1,0:T(8,128)(2,1)S(1)}, u32[]{:S(2)}, u32[]{:S(2)}) collective-permute-start(bf16[2,1,128,512]{3,2,1,0:T(8,128)(2,1)S(1)} %add_partial.5), channel_id=1, source_target_pairs={{0,4},{4,0},{8,12},{12,8},{1,5},{5,1},{9,13},{13,9},{2,6},{6,2},{1... | collective-permute-start | bytes 786440 | tf_op jit(solution)/shard_map/ppermute | solution.py:190
  66.5 5.0 %collective-permute-start.21 = (bf16[1,1,128,512]{3,2,1,0:T(8,128)(2,1)S(1)}, bf16[1,1,128,512]{3,2,1,0:T(8,128)(2,1)S(1)}, u32[]{:S(2)}, u32[]{:S(2)}) collective-permute-start(bf16[1,1,128,512]{3,2,1,0:T(8,128)(2,1)S(1)} %get-tuple-element.53), channel_id=1, source_target_pairs={{0,8},{4,12},{8,0},{12,4},{1,9},{5,13},{9,1},{13,5},{2,10},{6,14},... | collective-permute-start | bytes 393224 | tf_op jit(solution)/shard_map/ppermute | solution.py:186
  67.2 4.3 %copy-start.5 = (bf16[3,2,128,512]{3,2,1,0:T(8,128)(2,1)}, bf16[3,2,128,512]{3,2,1,0:T(8,128)(2,1)S(1)}, u32[]{:S(2)}) copy-start(bf16[3,2,128,512]{3,2,1,0:T(8,128)(2,1)S(1)} %constant_dynamic-update-slice_fusion.6) | copy-start | bytes 2359300
  71.5 0.9 %copy-start.6 = (bf16[3,2,128,512]{3,2,1,0:T(8,128)(2,1)}, bf16[3,2,128,512]{3,2,1,0:T(8,128)(2,1)S(1)}, u32[]{:S(2)}) copy-start(bf16[3,2,128,512]{3,2,1,0:T(8,128)(2,1)S(1)} %constant_dynamic-update-slice_fusion) | copy-start | bytes 2359300

commit v5 on v4

v5 whole, which is shorter than its diff:
```python
import functools
import math

import jax
import jax.numpy as jnp
from jax import lax
from jax.experimental import pallas as pl
from jax.experimental.pallas import tpu as pltpu
from jax.sharding import PartitionSpec as P

MAXOFF = 9
BF16 = jnp.bfloat16
STEP = 16
WHOLE = pl.BlockSpec(memory_space=pltpu.VMEM)
SCALARS = pl.BlockSpec(memory_space=pltpu.SMEM)


def call(kernel, outs, name, *args, scalars=0):
    return pl.pallas_call(
        kernel,
        in_specs=[SCALARS] * scalars + [WHOLE] * (len(args) - scalars),
        out_specs=[WHOLE] * len(outs),
        out_shape=[jax.ShapeDtypeStruct(x, BF16) for x in outs],
        compiler_params=pltpu.CompilerParams(vmem_limit_bytes=12 * 1024 * 1024),
        cost_estimate=pl.CostEstimate(flops=1, bytes_accessed=1, transcendentals=0),
        name=name,
    )(*args)


def slices(arrays, index, owned):
    def kernel(index_ref, *refs):
        for i in range(len(arrays)):
            for b in range(owned):
                refs[len(arrays) + i][:, b] = refs[i][:, index_ref[i] * owned + b]

    shapes = [x.shape[:1] + (owned,) + x.shape[2:] for x in arrays]
    return call(kernel, shapes, "slices", jnp.stack(index), *arrays, scalars=1)


def weight_tables(en, en_at, shifts, pieces):
    _, e, _ = pieces[0].shape
    sources = len(shifts) + 1

    def kernel(at_ref, *refs):
        at, outs = at_ref[0], refs[len(pieces) :]
        for i, t in enumerate([0] + list(shifts)):
            away = (lax.rem(at + t, en) - at) * e
            for n in range(e):
                totals = [jnp.float32(0.0)] * e
                for ref in refs[: len(pieces)]:
                    for k in range(ref.shape[2]):
                        shift = ref[0, n, k].astype(jnp.int32) - away + n
                        for m in range(e):
                            totals[m] += jnp.where(shift == m, ref[1, n, k], jnp.float32(0.0))
                for m in range(e):
                    outs[i][n, m] = totals[m]

    return pl.pallas_call(
        kernel,
        in_specs=[SCALARS] * (1 + len(pieces)),
        out_specs=[SCALARS] * sources,
        out_shape=[jax.ShapeDtypeStruct((e, e), jnp.float32)] * sources,
        cost_estimate=pl.CostEstimate(flops=1, bytes_accessed=1, transcendentals=0),
        name="weight_tables",
    )(en_at.reshape(1), *pieces)


def weighted(tables, rows, sources, load):
    totals = [None] * len(rows)
    for t in range(sources):
        for m in range(tables[t].shape[1]):
            g = load(t, m).astype(jnp.float32)
            for i, n in enumerate(rows):
                term = tables[t][n, m] * g
                totals[i] = term if totals[i] is None else totals[i] + term
    return totals


def chunks(rows, body):
    @pl.loop(0, rows // STEP, unroll=math.gcd(rows // STEP, 4))
    def _(i):
        body(pl.ds(pl.multiple_of(i * STEP, STEP), STEP))


def mix(whole, others, index, tables, owned):
    e, _, rows, o = whole.shape
    sources = 1 + len(others)

    def kernel(index_ref, *refs):
        weight_refs, ins, out_ref = refs[:sources], refs[sources:-1], refs[-1]
        for b in range(owned):
            block = index_ref[0] * owned + b

            def body(at):
                def load(t, m):
                    return ins[t][m, b if t else block, at, :]

                totals = weighted(weight_refs, range(e), sources, load)
                for n in range(e):
                    out_ref[n, b, at, :] = totals[n].astype(BF16)

            chunks(rows, body)

    shape = (e, owned, rows, o)
    return call(kernel, [shape], "mix", index.reshape(1), *tables, whole, *others, scalars=1 + sources)[0]


def partial_sums(whole, others, index, table, owned):
    e, _, rows, o = whole.shape
    pieces = 1 + len(others)

    def kernel(index_ref, table_ref, *refs):
        for d in range(pieces):
            for b in range(owned):
                block = b if d else index_ref[0] * owned + b

                def body(at):
                    totals = weighted(
                        [table_ref], range(e), 1, lambda t, m: refs[d][m, block, at, :]
                    )
                    for n in range(e):
                        refs[pieces + n][d, b, at, :] = totals[n].astype(BF16)

                chunks(rows, body)

    shape = (pieces, owned, rows, o)
    return call(kernel, [shape] * e, "partial_sums", index.reshape(1), table, whole, *others, scalars=2)


def add_partial(n, whole, others, index, received, table, owned):
    e, _, rows, o = whole.shape
    pieces = 1 + len(others)

    def kernel(index_ref, table_ref, *refs):
        for d in range(pieces):
            for b in range(owned):
                block = b if d else index_ref[0] * owned + b

                def body(at):
                    (total,) = weighted(
                        [table_ref], [n], 1, lambda t, m: refs[d][m, block, at, :]
                    )
                    for other in refs[pieces:-1]:
                        total = total + other[d, b, at, :].astype(jnp.float32)
                    refs[-1][d, b, at, :] = total.astype(BF16)

                chunks(rows, body)

    shape = (pieces, owned, rows, o)
    return call(
        kernel, [shape], "add_partial", index.reshape(1), table, whole, *others, *received, scalars=2
    )[0]


def product(energies, a_pieces, s_arrays, s_at, places, lefts):
    pieces = len(a_pieces)
    _, owned, rows, o = a_pieces[0].shape

    def kernel(place_ref, *refs):
        a_in, s_in = refs[:pieces], refs[pieces : pieces + len(s_arrays)]
        outs = refs[pieces + len(s_arrays) :]
        spans = [pl.ds(pl.multiple_of(place_ref[j] * rows, rows), rows) for j in range(pieces)]
        for k, n in enumerate(energies):
            for b in range(owned):
                left = jnp.concatenate(
                    [
                        jnp.concatenate([a_in[i][n, b, :, at] for at in spans], axis=1)
                        for i in range(lefts)
                    ],
                    axis=0,
                )
                at_piece = [s_at(n, j) for j in range(pieces)]
                sigma = jnp.concatenate([s_in[which][lead, b] for which, lead in at_piece], axis=0)
                first = jnp.dot(left, sigma, preferred_element_type=jnp.float32).astype(BF16)
                both = lax.dot_general(
                    first,
                    jnp.concatenate([a[n, b] for a in a_in], axis=0),
                    (((1,), (1,)), ((), ())),
                    preferred_element_type=jnp.float32,
                ).astype(BF16)
                for i in range(lefts):
                    for j, at in enumerate(spans):
                        outs[i][k, b, :, at] = both[i * rows : (i + 1) * rows, j * rows : (j + 1) * rows]

    shape = (len(energies), owned, rows, o)
    return call(
        kernel,
        [shape] * lefts,
        "product",
        places,
        *a_pieces,
        *s_arrays,
        scalars=1,
    )


def after(x, *earlier):
    return lax.optimization_barrier((x,) + earlier)[0]


def ordered(xs, *earlier):
    return [after(x, *earlier) for x in xs]


def solution(mesh):
    en, ph = mesh.shape["en"], mesh.shape["ph"]

    def on_device(lesser_in, greater_in, inverse, offsets, couplings):
        e, nb, r, o = lesser_in.shape
        owners = math.gcd(nb, ph)
        lanes = ph // owners
        owned = nb // owners
        en_at, ph_at = lax.axis_index("en"), lax.axis_index("ph")
        owner, lane = lax.div(ph_at, lanes), lax.rem(ph_at, lanes)

        def place_of(d, q):
            back = lax.rem(owner + owners - d, owners) if d else owner
            beside = lax.rem(lane + lanes - q, lanes) if q else lane
            return back * lanes + beside

        def owner_at(d):
            return lax.rem(owner + d, owners) if d else owner

        def to_owner(x, d):
            pairs = [(p, (p // lanes + d) % owners * lanes + p % lanes) for p in range(ph)]
            return lax.ppermute(x, "ph", pairs)

        def to_lane(x, q):
            pairs = [(p, p // lanes * lanes + (p % lanes + q) % lanes) for p in range(ph)]
            return lax.ppermute(x, "ph", pairs)

        def from_energy(x, t):
            return lax.ppermute(x, "en", [((i + t) % en, i) for i in range(en)])

        reach = (MAXOFF + e - 1) // e
        shifts = [t for t in range(1, en) if t <= reach or en - t <= reach]

        mine = jnp.stack([offsets.astype(jnp.float32), couplings])
        column = jnp.concatenate([mine] + [to_owner(mine, d) for d in range(1, owners)], axis=2)

        away = [owner_at(d) for d in range(1, owners)]
        greater_part = slices([greater_in] * len(away), ordered(away, mine), owned)
        greater_rows = [to_owner(x, d + 1) for d, x in enumerate(greater_part)]
        lesser_part = slices([lesser_in] * len(away), ordered(away, *greater_part), owned)
        lesser_from = [[from_energy(x, t) for t in shifts] for x in lesser_part]

        def all_lanes(pieces):
            return pieces + [to_lane(x, q) for q in range(1, lanes) for x in pieces]

        inverse_part = slices([inverse] * len(away), ordered(away, *lesser_part), owned)
        inverse_rows = [to_owner(x, d + 1) for d, x in enumerate(inverse_part)]

        tables = weight_tables(en, after(en_at, *inverse_part), shifts, all_lanes([column]))
        tables_for = [
            lax.ppermute(table, "en", [(i, (i + t) % en) for i in range(en)])
            for t, table in zip(shifts, tables[1:])
        ]
        (lesser_own,) = slices([lesser_in], [after(owner, *tables)], owned)
        lesser_from.insert(0, [from_energy(lesser_own, t) for t in shifts])

        lesser_rows = [None] * owners
        last = (lesser_own,)
        for d in range(1, owners):
            mixed = mix(lesser_in, lesser_from[d], after(owner_at(d), *last), tables, owned)
            lesser_rows[d] = to_owner(mixed, d)
            last = (mixed,)
        (inverse_own,) = slices([inverse], [after(owner, *last)], owned)
        inverse_lanes = [[to_lane(inverse_own, q) for q in range(1, lanes)]]
        last = (inverse_own, *inverse_lanes[0])
        received = [[] for _ in range(e)]
        for t, table in zip(shifts, tables_for):
            parts = partial_sums(greater_in, greater_rows, after(owner, *last), table, owned)
            for n, part in enumerate(parts):
                received[n].append(from_energy(part, t))
            last = tuple(parts)
        inverse_lanes += [[to_lane(x, q) for q in range(1, lanes)] for x in inverse_rows]
        last += sum(map(tuple, inverse_lanes[1:]), ())
        lesser_rows[0] = mix(lesser_in, lesser_from[0], after(owner, *last), tables, owned)
        lesser_lanes = [[to_lane(lesser_rows[0], q) for q in range(1, lanes)]]
        last = (lesser_rows[0], *lesser_lanes[0])

        places = jnp.stack([place_of(d, q) for q in range(lanes) for d in range(owners)])

        def lane_order(rows, beside):
            return rows + [x[q] for q in range(lanes - 1) for x in beside]

        inverse_full = lane_order([inverse_own] + inverse_rows, inverse_lanes)

        def put(result, outs, n):
            for d, out in enumerate(outs):
                back = to_owner(out, owners - d) if d else out
                result = lax.dynamic_update_slice(result, back, (n, owner_at(d) * owned, 0, 0))
            return result

        lesser_out = jnp.zeros((e, nb, r, o), BF16)
        greater_out = jnp.zeros((e, nb, r, o), BF16)
        for n in range(e):
            sigma = add_partial(
                n, greater_in, greater_rows, after(owner, *last), received[n], tables[0], owned
            )
            outs = product(
                [n],
                inverse_full,
                all_lanes([sigma]),
                lambda n, j: (j // owners, j % owners),
                places,
                owners,
            )
            greater_out = put(greater_out, outs, n)
            last = tuple(outs)
            if n == 0:
                lesser_lanes += [[to_lane(x, q) for q in range(1, lanes)] for x in lesser_rows[1:]]
                outs = product(
                    range(e),
                    inverse_full,
                    lane_order(lesser_rows, lesser_lanes),
                    lambda n, j: (j, n),
                    after(places, *last),
                    owners,
                )
                lesser_out = put(lesser_out, outs, 0)
                last = tuple(outs)

        return lesser_out, greater_out

    block, coupled = P("en", "blk", "ph", None), P("en", "ph")
    return jax.shard_map(
        on_device,
        mesh=mesh,
        in_specs=(block, block, block, coupled, coupled),
        out_specs=(block, block),
        check_vma=False,
    )
```

time: 72.7 us -> 87 us (1.20)
  waiting for transfers between devices: 29.8 us -> 41.8 us
  Pallas kernels: 11.6 us -> 15.1 us
  starting transfers between devices: 17.7 us -> 16 us
  local copies, waits for them, and re-layouts: 9.64 us -> 11.3 us
  other arithmetic: 2.8 us -> 1.23 us
    ppermute x1, waiting for transfers between devices: 2.92 us -> 9.03 us  [on_device(): lax.ppermute(table, 'en', [(i, (i + t) % en) for i in range(en)])]
    unnamed x23 -> x46, local copies, waits for them, and re-layouts: 4.03 us -> 9.94 us
    ppermute x8, waiting for transfers between devices: 17.9 us -> 22.7 us  [to_owner(): return lax.ppermute(x, 'ph', pairs)]
    dynamic_slice x3 -> x0, local copies, waits for them, and re-layouts: 3.67 us -> none  [blocks_of(): return lax.dynamic_slice_in_dim(x, owner_at(d) * owned, owned, axis=1)]
    pallas_call x9 -> x14, Pallas kernels: 11.6 us -> 13.5 us  [call(): pl.pallas_call(kernel, in_specs=[SCALARS] * scalars + [WHOLE] * (len(args...]
    pallas_call x0 -> x1, Pallas kernels: none -> 1.62 us  [weight_tables(): pl.pallas_call(kernel, in_specs=[SCALARS] * (1 + len(pieces)), out_specs=...]
    ppermute x5, waiting for transfers between devices: 7.31 us -> 8.22 us  [from_energy(): return lax.ppermute(x, 'en', [((i + t) % en, i) for i in range(en)])]
    dynamic_update_slice x7, local copies, waits for them, and re-layouts: 0.14 us -> 1.04 us  [put(): lax.dynamic_update_slice(result, back, (n, owner_at(d) * owned, 0, 0))]
  transfers between devices with their start and end apart: 22 -> 22, of which waited for: 9 -> 10; matrix products, arithmetic and copies ran while one was open for 9% -> 3% of each run, Pallas kernels for 14% -> 16%
where the time goes in v5:
time: 87 us; the launch traced here: 86.5 us
  waiting for transfers between devices  41.8 us (48%)
  starting transfers between devices  16 us (18%)
  Pallas kernels  15.1 us (17%)
  local copies, waits for them, and re-layouts  11.3 us (13%)
  other arithmetic  1.23 us (1%)
  between operations  1.01 us (1%)
    ppermute x8, waiting for transfers between devices, to_owner(): return lax.ppermute(x, 'ph', pairs)  22.7 us
    pallas_call x14, Pallas kernels, call(): pl.pallas_call(kernel, in_specs=[SCALARS] * scalars + [WHOLE] * (len(args...  13.5 us
    unnamed x46, local copies, waits for them, and re-layouts  9.94 us
    ppermute x1, waiting for transfers between devices, on_device(): lax.ppermute(table, 'en', [(i, (i + t) % en) for i in range(en)])  9.03 us
    ppermute x5, waiting for transfers between devices, from_energy(): return lax.ppermute(x, 'en', [((i + t) % en, i) for i in range(en)])  8.22 us
    ppermute x8, starting transfers between devices, to_owner(): return lax.ppermute(x, 'ph', pairs)  7.54 us
    ppermute x5, starting transfers between devices, from_energy(): return lax.ppermute(x, 'en', [((i + t) % en, i) for i in range(en)])  6.67 us
    ppermute x8, waiting for transfers between devices, to_lane(): return lax.ppermute(x, 'ph', pairs)  1.79 us
  transfers between devices with their start and end apart: 22, of which 10 were waited for; matrix products, arithmetic and copies ran while one was open for 3% of the time, Pallas kernels for 16%

profile of v5, /device:TPU:0, one launch (start us, length us, event | category | flops | bytes accessed | tf_op | source)
XLA Modules:
  0.0 86.5 jit_solution(13884558377410133188)
XLA Ops:
  0.7 0.7 copy-done.22
  1.3 0.1 copy.7
  1.4 0.7 copy-done.21
  2.1 0.1 copy.8
  2.2 1.1 %copy-done = bf16[3,2,128,512]{3,2,1,0:T(8,128)(2,1)S(1)} copy-done((bf16[3,2,128,512]{3,2,1,0:T(8,128)(2,1)S(1)}, bf16[3,2,128,512]{3,2,1,0:T(8,128)(2,1)}, u32[]{:S(2)}) %copy-start) | copy-done | bytes 786456
  3.4 0.7 copy-done.6
  4.1 0.5 copy-done.2
  4.6 3.0 %collective-permute-start.2 = (bf16[3,1,128,512]{3,2,1,0:T(8,128)(2,1)S(1)}, bf16[3,1,128,512]{3,2,1,0:T(8,128)(2,1)S(1)}, u32[]{:S(2)}, u32[]{:S(2)}) collective-permute-start(bf16[3,1,128,512]{3,2,1,0:T(8,128)(2,1)S(1)} %slices.6), channel_id=1, source_target_pairs={{16,0},{0,16},{17,1},{1,17},{18,2},{2,18},{19,3},{3,19},{20,4},{4,... | collective-permute-start | bytes 1179656 | tf_op jit(solution)/shard_map/ppermute | solution.py:233
  7.6 0.8 slices.7
  8.4 1.5 %collective-permute-start.3 = (bf16[3,1,128,512]{3,2,1,0:T(8,128)(2,1)}, bf16[3,1,128,512]{3,2,1,0:T(8,128)(2,1)S(1)}, u32[]{:S(2)}, u32[]{:S(2)}) collective-permute-start(bf16[3,1,128,512]{3,2,1,0:T(8,128)(2,1)} %slices.7), channel_id=1, source_target_pairs={{0,8},{4,12},{8,0},{12,4},{1,9},{5,13},{9,1},{13,5},{2,10},{6,14},... | collective-permute-start | bytes 1179656 | tf_op jit(solution)/shard_map/ppermute | solution.py:226
  9.9 0.5 collective-permute-start
  10.4 8.8 %collective-permute-done = f32[2,3,2]{2,1,0:T(4,128)S(1)} collective-permute-done((f32[2,3,2]{2,1,0:T(4,128)S(1)}, f32[2,3,2]{2,1,0:T(4,128)S(1)}, u32[]{:S(2)}, u32[]{:S(2)}) %collective-permute-start) | collective-permute-done | bytes 80 | tf_op jit(solution)/shard_map/ppermute | solution.py:226
  19.3 0.1 pad_maximum_fusion.1.refs_0_
  19.4 0.0 collective-permute-start.1
  19.4 1.2 %collective-permute-done.1.refs_1_ = f32[2,3,4]{2,1,0:T(4,128)S(1)} collective-permute-done((f32[2,3,4]{2,1,0:T(4,128)S(1)}, f32[2,3,4]{2,1,0:T(4,128)S(1)}, u32[]{:S(2)}, u32[]{:S(2)}) %collective-permute-start.1) | collective-permute-done | bytes 128 | tf_op jit(solution)/shard_map/ppermute | solution.py:230
  20.6 0.6 copy-done.20
  21.1 1.6 %weight_tables.1 = (f32[3,3]{1,0:T(4,128)}, f32[3,3]{1,0:T(4,128)}) custom-call(s32[1]{0:T(128)} %bitcast.9.at_ref, f32[2,3,4]{2,1,0:T(4,128)} %copy-done.19, f32[2,3,4]{2,1,0:T(4,128)} %copy-done.20), custom_call_target="tpu_custom_call" | custom-call | flops 1 | bytes 1 | tf_op jit(solution)/shard_map/weight_tables/pallas_call | solution.py:58
  22.8 0.6 copy-done.14
  23.4 0.0 copy-done.15
  23.5 1.0 %mix.2 = bf16[3,1,128,512]{3,2,1,0:T(8,128)(2,1)S(1)} custom-call(s32[1]{0:T(128)} %bitcast.11.index_ref, f32[3,3]{1,0:T(4,128)S(1)} %copy-done.14, f32[3,3]{1,0:T(4,128)S(1)} %copy-done.15, bf16[3,2,128,512]{3,2,1,0:T(8,128)(2,1)S(1)} %copy-done.2, bf16[3,1,128,512]{3,2,1,0:T(8,128)(2,1)S(1)} %collective-permute-done.2.refs_3_), custom_call_target="tpu_custom_call" | custom-call | flops 1 | bytes 1 | tf_op jit(solution)/shard_map/mix/pallas_call | solution.py:19
  24.5 0.2 collective-permute-start.4
  24.7 0.8 copy-done.7
  25.5 1.5 %collective-permute-start.7 = (bf16[3,1,128,512]{3,2,1,0:T(8,128)(2,1)S(1)}, bf16[3,1,128,512]{3,2,1,0:T(8,128)(2,1)S(1)}, u32[]{:S(2)}, u32[]{:S(2)}) collective-permute-start(bf16[3,1,128,512]{3,2,1,0:T(8,128)(2,1)S(1)} %copy-done.7), channel_id=1, source_target_pairs={{0,8},{4,12},{8,0},{12,4},{1,9},{5,13},{9,1},{13,5},{2,10},{6,14},... | collective-permute-start | bytes 1179656 | tf_op jit(solution)/shard_map/ppermute | solution.py:226
  27.0 0.9 %collective-permute-start.8 = (bf16[3,1,128,512]{3,2,1,0:T(8,128)(2,1)S(1)}, bf16[3,1,128,512]{3,2,1,0:T(8,128)(2,1)S(1)}, u32[]{:S(2)}, u32[]{:S(2)}) collective-permute-start(bf16[3,1,128,512]{3,2,1,0:T(8,128)(2,1)S(1)} %slices.8), channel_id=1, source_target_pairs={{16,0},{0,16},{17,1},{1,17},{18,2},{2,18},{19,3},{3,19},{20,4},{4,... | collective-permute-start | bytes 1179656 | tf_op jit(solution)/shard_map/ppermute | solution.py:233
  27.9 0.5 collective-permute-start.12
  28.4 1.1 %collective-permute-start.6 = (f32[3,3]{1,0:T(4,128)S(1)}, f32[3,3]{1,0:T(4,128)S(1)}, u32[]{:S(2)}, u32[]{:S(2)}) collective-permute-start(f32[3,3]{1,0:T(4,128)S(1)} %copy-done.15), channel_id=1, source_target_pairs={{0,16},{16,0},{1,17},{17,1},{2,18},{18,2},{3,19},{19,3},{4,20},{20... | collective-permute-start | bytes 116 | tf_op jit(solution)/shard_map/ppermute | solution.py:255
  29.6 9.0 %collective-permute-done.6.table_ref = f32[3,3]{1,0:T(4,128)S(1)} collective-permute-done((f32[3,3]{1,0:T(4,128)S(1)}, f32[3,3]{1,0:T(4,128)S(1)}, u32[]{:S(2)}, u32[]{:S(2)}) %collective-permute-start.6) | collective-permute-done | bytes 68 | tf_op jit(solution)/shard_map/ppermute | solution.py:255
  38.6 1.7 %partial_sums.1 = (bf16[2,1,128,512]{3,2,1,0:T(8,128)(2,1)S(1)}, bf16[2,1,128,512]{3,2,1,0:T(8,128)(2,1)}, bf16[2,1,128,512]{3,2,1,0:T(8,128)(2,1)}) custom-call(s32[1]{0:T(128)} %bitcast.13.index_ref, f32[3,3]{1,0:T(4,128)S(1)} %collective-permute-done.6.table_ref, bf16[3,2,128,512]{3,2,1,0:T(8,128)(2,1)S(1)} %copy-done.1, ...), custom_call_target="tpu_custom_call" | custom-call | flops 1 | bytes 1 | tf_op jit(solution)/shard_map/partial_sums/pallas_call | solution.py:19
  40.4 1.0 %mix.3.refs_4_ = bf16[3,1,128,512]{3,2,1,0:T(8,128)(2,1)S(1)} custom-call(s32[1]{0:T(128)} %bitcast.14.index_ref, f32[3,3]{1,0:T(4,128)S(1)} %copy-done.14, f32[3,3]{1,0:T(4,128)S(1)} %copy-done.15, bf16[3,2,128,512]{3,2,1,0:T(8,128)(2,1)S(1)} %copy-done.2, bf16[3,1,128,512]{3,2,1,0:T(8,128)(2,1)S(1)} %collective-permute-done.8.refs_3_), custom_call_target="tpu_custom_call" | custom-call | flops 1 | bytes 1 | tf_op jit(solution)/shard_map/mix/pallas_call | solution.py:19
  41.4 0.1 collective-permute-start.9
  41.4 0.9 %collective-permute-start.10 = (bf16[2,1,128,512]{3,2,1,0:T(8,128)(2,1)S(1)}, bf16[2,1,128,512]{3,2,1,0:T(8,128)(2,1)S(1)}, u32[]{:S(2)}, u32[]{:S(2)}) collective-permute-start(bf16[2,1,128,512]{3,2,1,0:T(8,128)(2,1)S(1)} %get-tuple-element.38), channel_id=1, source_target_pairs={{16,0},{0,16},{17,1},{1,17},{18,2},{2,18},{19,3},{3,19},{20,4},{4,... | collective-permute-start | bytes 786440 | tf_op jit(solution)/shard_map/ppermute | solution.py:233
  42.4 2.9 %collective-permute-done.12.refs_5_ = bf16[3,1,128,512]{3,2,1,0:T(8,128)(2,1)} collective-permute-done((bf16[3,1,128,512]{3,2,1,0:T(8,128)(2,1)S(1)}, bf16[3,1,128,512]{3,2,1,0:T(8,128)(2,1)}, u32[]{:S(2)}, u32[]{:S(2)}) %collective-permute-start.12) | collective-permute-done | bytes 393248 | tf_op jit(solution)/shard_map/ppermute | solution.py:226
  45.2 0.7 copy-done.8
  46.0 4.2 %collective-permute-done.10.refs_2_ = bf16[2,1,128,512]{3,2,1,0:T(8,128)(2,1)S(1)} collective-permute-done((bf16[2,1,128,512]{3,2,1,0:T(8,128)(2,1)S(1)}, bf16[2,1,128,512]{3,2,1,0:T(8,128)(2,1)S(1)}, u32[]{:S(2)}, u32[]{:S(2)}) %collective-permute-start.10) | collective-permute-done | bytes 262176 | tf_op jit(solution)/shard_map/ppermute | solution.py:233
  50.2 0.8 add_partial.3.refs_4_
  50.9 0.1 collective-permute-start.11
  51.0 0.9 %collective-permute-start.16 = (bf16[2,1,128,512]{3,2,1,0:T(8,128)(2,1)}, bf16[2,1,128,512]{3,2,1,0:T(8,128)(2,1)}, u32[]{:S(2)}, u32[]{:S(2)}) collective-permute-start(bf16[2,1,128,512]{3,2,1,0:T(8,128)(2,1)} %get-tuple-element.39), channel_id=1, source_target_pairs={{16,0},{0,16},{17,1},{1,17},{18,2},{2,18},{19,3},{3,19},{20,4},{4,... | collective-permute-start | bytes 786440 | tf_op jit(solution)/shard_map/ppermute | solution.py:233
  52.0 0.1 pad_add_fusion.place_ref
  52.1 0.6 collective-permute-done.11.refs_5_
  52.7 2.1 %product.4 = (bf16[1,1,128,512]{3,2,1,0:T(8,128)(2,1)S(1)}, bf16[1,1,128,512]{3,2,1,0:T(8,128)(2,1)}) custom-call(s32[4]{0:T(128)S(1)} %pad_add_fusion.place_ref, bf16[3,1,128,512]{3,2,1,0:T(8,128)(2,1)S(1)} %slices.9.refs_0_, bf16[3,1,128,512]{3,2,1,0:T(8,128)(2,1)S(1)} %collective-permute-done.3.refs_1_, ...), custom_call_target="tpu_custom_call" | custom-call | flops 1 | bytes 1 | tf_op jit(solution)/shard_map/product/pallas_call | solution.py:19
  54.8 0.6 copy-done.12
  55.5 0.8 copy-done.10
  56.2 1.0 %copy-done.11 = bf16[3,1,128,512]{3,2,1,0:T(8,128)(2,1)S(1)} copy-done((bf16[3,1,128,512]{3,2,1,0:T(8,128)(2,1)S(1)}, bf16[3,1,128,512]{3,2,1,0:T(8,128)(2,1)}, u32[]{:S(2)}) %copy-start.11) | copy-done | bytes 393240
  57.2 2.2 %product.5 = (bf16[3,1,128,512]{3,2,1,0:T(8,128)(2,1)S(1)}, bf16[3,1,128,512]{3,2,1,0:T(8,128)(2,1)S(1)}) custom-call(s32[4]{0:T(128)S(1)} %pad_add_fusion.place_ref, bf16[3,1,128,512]{3,2,1,0:T(8,128)(2,1)S(1)} %slices.9.refs_0_, bf16[3,1,128,512]{3,2,1,0:T(8,128)(2,1)S(1)} %collective-permute-done.3.refs_1_, ...), custom_call_target="tpu_custom_call" | custom-call | flops 1 | bytes 1 | tf_op jit(solution)/shard_map/product/pallas_call | solution.py:19
  59.5 0.6 collective-permute-done.16.refs_2_
  60.1 0.2 copy-done.16
  60.2 1.2 %add_partial.4.refs_4_ = bf16[2,1,128,512]{3,2,1,0:T(8,128)(2,1)S(1)} custom-call(s32[1]{0:T(128)} %bitcast.16.index_ref, f32[3,3]{1,0:T(4,128)S(1)} %copy-done.14, bf16[3,2,128,512]{3,2,1,0:T(8,128)(2,1)S(1)} %copy-done.1, bf16[3,1,128,512]{3,2,1,0:T(8,128)(2,1)S(1)} %collective-permute-done.7.refs_1_, bf16[2,1,128,512]{3,2,1,0:T(8,128)(2,1)} %collective-permute-done.16.refs_2_), custom_call_target="tpu_custom_call" | custom-call | flops 1 | bytes 1 | tf_op jit(solution)/shard_map/add_partial/pallas_call | solution.py:19
  61.4 0.2 collective-permute-start.17
  61.6 0.9 %collective-permute-start.19 = (bf16[2,1,128,512]{3,2,1,0:T(8,128)(2,1)}, bf16[2,1,128,512]{3,2,1,0:T(8,128)(2,1)}, u32[]{:S(2)}, u32[]{:S(2)}) collective-permute-start(bf16[2,1,128,512]{3,2,1,0:T(8,128)(2,1)} %get-tuple-element.40), channel_id=1, source_target_pairs={{16,0},{0,16},{17,1},{1,17},{18,2},{2,18},{19,3},{3,19},{20,4},{4,... | collective-permute-start | bytes 786440 | tf_op jit(solution)/shard_map/ppermute | solution.py:233
  62.5 0.5 collective-permute-start.15
  63.0 1.5 %collective-permute-start.14 = (bf16[3,1,128,512]{3,2,1,0:T(8,128)(2,1)}, bf16[3,1,128,512]{3,2,1,0:T(8,128)(2,1)S(1)}, u32[]{:S(2)}, u32[]{:S(2)}) collective-permute-start(bf16[3,1,128,512]{3,2,1,0:T(8,128)(2,1)} %copy-done.16), channel_id=1, source_target_pairs={{0,8},{4,12},{8,0},{12,4},{1,9},{5,13},{9,1},{13,5},{2,10},{6,14},... | collective-permute-start | bytes 1179656 | tf_op jit(solution)/shard_map/ppermute | solution.py:226
  64.5 0.1 broadcast.7.clone.1
  64.7 1.5 %product.6 = (bf16[1,1,128,512]{3,2,1,0:T(8,128)(2,1)S(1)}, bf16[1,1,128,512]{3,2,1,0:T(8,128)(2,1)S(1)}) custom-call(s32[4]{0:T(128)S(1)} %pad_add_fusion.place_ref, bf16[3,1,128,512]{3,2,1,0:T(8,128)(2,1)S(1)} %slices.9.refs_0_, bf16[3,1,128,512]{3,2,1,0:T(8,128)(2,1)S(1)} %collective-permute-done.3.refs_1_, ...), custom_call_target="tpu_custom_call" | custom-call | flops 1 | bytes 1 | tf_op jit(solution)/shard_map/product/pallas_call | solution.py:19
  66.1 0.9 %collective-permute-start.18 = (bf16[1,1,128,512]{3,2,1,0:T(8,128)(2,1)S(1)}, bf16[1,1,128,512]{3,2,1,0:T(8,128)(2,1)S(1)}, u32[]{:S(2)}, u32[]{:S(2)}) collective-permute-start(bf16[1,1,128,512]{3,2,1,0:T(8,128)(2,1)S(1)} %get-tuple-element.50), channel_id=1, source_target_pairs={{0,8},{4,12},{8,0},{12,4},{1,9},{5,13},{9,1},{13,5},{2,10},{6,14},... | collective-permute-start | bytes 393224 | tf_op jit(solution)/shard_map/ppermute | solution.py:226
  67.0 3.5 %collective-permute-done.19.refs_2_ = bf16[2,1,128,512]{3,2,1,0:T(8,128)(2,1)} collective-permute-done((bf16[2,1,128,512]{3,2,1,0:T(8,128)(2,1)}, bf16[2,1,128,512]{3,2,1,0:T(8,128)(2,1)}, u32[]{:S(2)}, u32[]{:S(2)}) %collective-permute-start.19) | collective-permute-done | bytes 262176 | tf_op jit(solution)/shard_map/ppermute | solution.py:233
  70.5 1.2 %add_partial.5 = bf16[2,1,128,512]{3,2,1,0:T(8,128)(2,1)S(1)} custom-call(s32[1]{0:T(128)} %bitcast.17.index_ref, f32[3,3]{1,0:T(4,128)S(1)} %copy-done.14, bf16[3,2,128,512]{3,2,1,0:T(8,128)(2,1)S(1)} %copy-done.1, bf16[3,1,128,512]{3,2,1,0:T(8,128)(2,1)S(1)} %collective-permute-done.7.refs_1_, bf16[2,1,128,512]{3,2,1,0:T(8,128)(2,1)} %collective-permute-done.19.refs_2_), custom_call_target="tpu_custom_call" | custom-call | flops 1 | bytes 1 | tf_op jit(solution)/shard_map/add_partial/pallas_call | solution.py:19
  71.7 0.1 collective-permute-start.20
  71.8 0.9 %constant_dynamic-update-slice_fusion.4 = bf16[3,2,128,512]{3,2,1,0:T(8,128)(2,1)S(1)} fusion(bf16[3,2,128,512]{3,2,1,0:T(8,128)(2,1)S(1)} %constant_dynamic-update-slice_fusion.5, bf16[1,1,128,512]{3,2,1,0:T(8,128)(2,1)} %collective-permute-done.15, s32[]{:T(128)S(6)} %select_n.5), kind=kLoop, calls=%fused_computation.6 | loop fusion | bytes 262148 | tf_op jit(solution)/shard_map/dynamic_update_slice | solution.py:292
  72.7 6.7 %collective-permute-done.18 = bf16[1,1,128,512]{3,2,1,0:T(8,128)(2,1)S(1)} collective-permute-done((bf16[1,1,128,512]{3,2,1,0:T(8,128)(2,1)S(1)}, bf16[1,1,128,512]{3,2,1,0:T(8,128)(2,1)S(1)}, u32[]{:S(2)}, u32[]{:S(2)}) %collective-permute-start.18) | collective-permute-done | bytes 131104 | tf_op jit(solution)/shard_map/ppermute | solution.py:226
  79.5 1.1 %product.7 = (bf16[3,2,128,512]{3,2,1,0:T(8,128)(2,1)S(1)}, bf16[1,1,128,512]{3,2,1,0:T(8,128)(2,1)S(1)}) fusion(bf16[3,2,128,512]{3,2,1,0:T(8,128)(2,1)S(1)} %constant_dynamic-update-slice_fusion.2, s32[]{:T(128)S(6)} %select_n.4, s32[4]{0:T(128)S(1)} %pad_add_fusion.place_ref, bf16[3,1,128,512]{3,2,1,0:T(8,128)(2,1)S(1)} %slices.9.refs_0_, ...), kind=kCustom, calls=%fused_computation.3 | custom fusion | flops 1 | bytes 2359812 | tf_op jit(solution)/shard_map/product/pallas_call | solution.py:19
  80.5 0.6 collective-permute-start.21
  81.1 0.1 broadcast.7.clone
  81.3 4.3 %collective-permute-done.21 = bf16[1,1,128,512]{3,2,1,0:T(8,128)(2,1)S(1)} collective-permute-done((bf16[1,1,128,512]{3,2,1,0:T(8,128)(2,1)S(1)}, bf16[1,1,128,512]{3,2,1,0:T(8,128)(2,1)S(1)}, u32[]{:S(2)}, u32[]{:S(2)}) %collective-permute-start.21) | collective-permute-done | bytes 131104 | tf_op jit(solution)/shard_map/ppermute | solution.py:226
  85.6 0.9 %copy-done.18 = bf16[3,2,128,512]{3,2,1,0:T(8,128)(2,1)} copy-done((bf16[3,2,128,512]{3,2,1,0:T(8,128)(2,1)}, bf16[3,2,128,512]{3,2,1,0:T(8,128)(2,1)S(1)}, u32[]{:S(2)}) %copy-start.18) | copy-done | bytes 786456
  (57 shorter events, 0.4 us)
Async XLA Ops:
  0.6 0.7 copy-start.22
  1.4 0.7 copy-start.21
  2.2 1.1 %copy-start = (bf16[3,2,128,512]{3,2,1,0:T(8,128)(2,1)S(1)}, bf16[3,2,128,512]{3,2,1,0:T(8,128)(2,1)}, u32[]{:S(2)}) copy-start(bf16[3,2,128,512]{3,2,1,0:T(8,128)(2,1)} %refs_0_.17) | copy-start | bytes 2359300
  3.3 1.3 %copy-start.2 = (bf16[3,2,128,512]{3,2,1,0:T(8,128)(2,1)S(1)}, bf16[3,2,128,512]{3,2,1,0:T(8,128)(2,1)}, u32[]{:S(2)}) copy-start(bf16[3,2,128,512]{3,2,1,0:T(8,128)(2,1)} %refs_2_.3) | copy-start | bytes 2359300
  3.4 0.7 copy-start.6
  4.1 3.5 %copy-start.3 = (bf16[3,2,128,512]{3,2,1,0:T(8,128)(2,1)S(1)}, bf16[3,2,128,512]{3,2,1,0:T(8,128)(2,1)}, u32[]{:S(2)}) copy-start(bf16[3,2,128,512]{3,2,1,0:T(8,128)(2,1)} %refs_0_.13) | copy-start | bytes 2359300
  4.6 18.2 %collective-permute-start.2 = (bf16[3,1,128,512]{3,2,1,0:T(8,128)(2,1)S(1)}, bf16[3,1,128,512]{3,2,1,0:T(8,128)(2,1)S(1)}, u32[]{:S(2)}, u32[]{:S(2)}) collective-permute-start(bf16[3,1,128,512]{3,2,1,0:T(8,128)(2,1)S(1)} %slices.6), channel_id=1, source_target_pairs={{16,0},{0,16},{17,1},{1,17},{18,2},{2,18},{19,3},{3,19},{20,4},{4,... | collective-permute-start | bytes 1179656 | tf_op jit(solution)/shard_map/ppermute | solution.py:233
  8.4 18.6 %collective-permute-start.3 = (bf16[3,1,128,512]{3,2,1,0:T(8,128)(2,1)}, bf16[3,1,128,512]{3,2,1,0:T(8,128)(2,1)S(1)}, u32[]{:S(2)}, u32[]{:S(2)}) collective-permute-start(bf16[3,1,128,512]{3,2,1,0:T(8,128)(2,1)} %slices.7), channel_id=1, source_target_pairs={{0,8},{4,12},{8,0},{12,4},{1,9},{5,13},{9,1},{13,5},{2,10},{6,14},... | collective-permute-start | bytes 1179656 | tf_op jit(solution)/shard_map/ppermute | solution.py:226
  9.9 9.4 %collective-permute-start = (f32[2,3,2]{2,1,0:T(4,128)S(1)}, f32[2,3,2]{2,1,0:T(4,128)S(1)}, u32[]{:S(2)}, u32[]{:S(2)}) collective-permute-start(f32[2,3,2]{2,1,0:T(4,128)S(1)} %pad_maximum_fusion), channel_id=1, source_target_pairs={{0,8},{4,12},{8,0},{12,4},{1,9},{5,13},{9,1},{13,5},{2,10},{6,14},... | collective-permute-start | bytes 152 | tf_op jit(solution)/shard_map/ppermute | solution.py:226
  19.4 1.2 %copy-start.19 = (f32[2,3,4]{2,1,0:T(4,128)}, f32[2,3,4]{2,1,0:T(4,128)S(1)}, u32[]{:S(2)}) copy-start(f32[2,3,4]{2,1,0:T(4,128)S(1)} %pad_maximum_fusion.1.refs_0_) | copy-start | bytes 292
  19.4 1.2 %collective-permute-start.1 = (f32[2,3,4]{2,1,0:T(4,128)S(1)}, f32[2,3,4]{2,1,0:T(4,128)S(1)}, u32[]{:S(2)}, u32[]{:S(2)}) collective-permute-start(f32[2,3,4]{2,1,0:T(4,128)S(1)} %pad_maximum_fusion.1.refs_0_), channel_id=1, source_target_pairs={{0,4},{4,0},{8,12},{12,8},{1,5},{5,1},{9,13},{13,9},{2,6},{6,2},{1... | collective-permute-start | bytes 296 | tf_op jit(solution)/shard_map/ppermute | solution.py:230
  20.5 0.6 copy-start.20
  22.8 0.7 copy-start.14
  22.8 0.7 copy-start.15
  24.4 14.2 %copy-start.1 = (bf16[3,2,128,512]{3,2,1,0:T(8,128)(2,1)S(1)}, bf16[3,2,128,512]{3,2,1,0:T(8,128)(2,1)}, u32[]{:S(2)}) copy-start(bf16[3,2,128,512]{3,2,1,0:T(8,128)(2,1)} %refs_0_.17) | copy-start | bytes 2359300
  24.4 1.1 %copy-start.7 = (bf16[3,1,128,512]{3,2,1,0:T(8,128)(2,1)S(1)}, bf16[3,1,128,512]{3,2,1,0:T(8,128)(2,1)}, u32[]{:S(2)}) copy-start(bf16[3,1,128,512]{3,2,1,0:T(8,128)(2,1)} %copy-done.6) | copy-start | bytes 1179652
  24.5 3.9 %collective-permute-start.4 = (bf16[3,1,128,512]{3,2,1,0:T(8,128)(2,1)S(1)}, bf16[3,1,128,512]{3,2,1,0:T(8,128)(2,1)S(1)}, u32[]{:S(2)}, u32[]{:S(2)}) collective-permute-start(bf16[3,1,128,512]{3,2,1,0:T(8,128)(2,1)S(1)} %slices.9.refs_0_), channel_id=1, source_target_pairs={{0,4},{4,0},{8,12},{12,8},{1,5},{5,1},{9,13},{13,9},{2,6},{6,2},{1... | collective-permute-start | bytes 1179656 | tf_op jit(solution)/shard_map/ppermute | solution.py:230
  25.5 13.1 %collective-permute-start.7 = (bf16[3,1,128,512]{3,2,1,0:T(8,128)(2,1)S(1)}, bf16[3,1,128,512]{3,2,1,0:T(8,128)(2,1)S(1)}, u32[]{:S(2)}, u32[]{:S(2)}) collective-permute-start(bf16[3,1,128,512]{3,2,1,0:T(8,128)(2,1)S(1)} %copy-done.7), channel_id=1, source_target_pairs={{0,8},{4,12},{8,0},{12,4},{1,9},{5,13},{9,1},{13,5},{2,10},{6,14},... | collective-permute-start | bytes 1179656 | tf_op jit(solution)/shard_map/ppermute | solution.py:226
  27.0 13.3 %collective-permute-start.5 = (bf16[3,1,128,512]{3,2,1,0:T(8,128)(2,1)S(1)}, bf16[3,1,128,512]{3,2,1,0:T(8,128)(2,1)S(1)}, u32[]{:S(2)}, u32[]{:S(2)}) collective-permute-start(bf16[3,1,128,512]{3,2,1,0:T(8,128)(2,1)S(1)} %collective-permute-done.3.refs_1_), channel_id=1, source_target_pairs={{0,4},{4,0},{8,12},{12,8},{1,5},{5,1},{9,13},{13,9},{2,6},{6,2},{1... | collective-permute-start | bytes 1179656 | tf_op jit(solution)/shard_map/ppermute | solution.py:230
  27.0 13.3 %collective-permute-start.8 = (bf16[3,1,128,512]{3,2,1,0:T(8,128)(2,1)S(1)}, bf16[3,1,128,512]{3,2,1,0:T(8,128)(2,1)S(1)}, u32[]{:S(2)}, u32[]{:S(2)}) collective-permute-start(bf16[3,1,128,512]{3,2,1,0:T(8,128)(2,1)S(1)} %slices.8), channel_id=1, source_target_pairs={{16,0},{0,16},{17,1},{1,17},{18,2},{2,18},{19,3},{3,19},{20,4},{4,... | collective-permute-start | bytes 1179656 | tf_op jit(solution)/shard_map/ppermute | solution.py:233
  27.9 17.3 %collective-permute-start.12 = (bf16[3,1,128,512]{3,2,1,0:T(8,128)(2,1)S(1)}, bf16[3,1,128,512]{3,2,1,0:T(8,128)(2,1)}, u32[]{:S(2)}, u32[]{:S(2)}) collective-permute-start(bf16[3,1,128,512]{3,2,1,0:T(8,128)(2,1)S(1)} %mix.2), channel_id=1, source_target_pairs={{0,8},{4,12},{8,0},{12,4},{1,9},{5,13},{9,1},{13,5},{2,10},{6,14},... | collective-permute-start | bytes 1179656 | tf_op jit(solution)/shard_map/ppermute | solution.py:226
  28.4 10.2 %collective-permute-start.6 = (f32[3,3]{1,0:T(4,128)S(1)}, f32[3,3]{1,0:T(4,128)S(1)}, u32[]{:S(2)}, u32[]{:S(2)}) collective-permute-start(f32[3,3]{1,0:T(4,128)S(1)} %copy-done.15), channel_id=1, source_target_pairs={{0,16},{16,0},{1,17},{17,1},{2,18},{18,2},{3,19},{19,3},{4,20},{20... | collective-permute-start | bytes 116 | tf_op jit(solution)/shard_map/ppermute | solution.py:255
  41.3 9.6 %copy-start.4 = (bf16[3,1,128,512]{3,2,1,0:T(8,128)(2,1)}, bf16[3,1,128,512]{3,2,1,0:T(8,128)(2,1)S(1)}, u32[]{:S(2)}) copy-start(bf16[3,1,128,512]{3,2,1,0:T(8,128)(2,1)S(1)} %mix.3.refs_4_) | copy-start | bytes 1179652
  41.4 3.9 %collective-permute-start.9 = (bf16[3,1,128,512]{3,2,1,0:T(8,128)(2,1)S(1)}, bf16[3,1,128,512]{3,2,1,0:T(8,128)(2,1)S(1)}, u32[]{:S(2)}, u32[]{:S(2)}) collective-permute-start(bf16[3,1,128,512]{3,2,1,0:T(8,128)(2,1)S(1)} %mix.3.refs_4_), channel_id=1, source_target_pairs={{0,4},{4,0},{8,12},{12,8},{1,5},{5,1},{9,13},{13,9},{2,6},{6,2},{1... | collective-permute-start | bytes 1179656 | tf_op jit(solution)/shard_map/ppermute | solution.py:230
  41.4 8.7 %collective-permute-start.10 = (bf16[2,1,128,512]{3,2,1,0:T(8,128)(2,1)S(1)}, bf16[2,1,128,512]{3,2,1,0:T(8,128)(2,1)S(1)}, u32[]{:S(2)}, u32[]{:S(2)}) collective-permute-start(bf16[2,1,128,512]{3,2,1,0:T(8,128)(2,1)S(1)} %get-tuple-element.38), channel_id=1, source_target_pairs={{16,0},{0,16},{17,1},{1,17},{18,2},{2,18},{19,3},{3,19},{20,4},{4,... | collective-permute-start | bytes 786440 | tf_op jit(solution)/shard_map/ppermute | solution.py:233
  45.2 10.2 %collective-permute-start.13 = (bf16[3,1,128,512]{3,2,1,0:T(8,128)(2,1)}, bf16[3,1,128,512]{3,2,1,0:T(8,128)(2,1)S(1)}, u32[]{:S(2)}, u32[]{:S(2)}) collective-permute-start(bf16[3,1,128,512]{3,2,1,0:T(8,128)(2,1)} %collective-permute-done.12.refs_5_), channel_id=1, source_target_pairs={{0,4},{4,0},{8,12},{12,8},{1,5},{5,1},{9,13},{13,9},{2,6},{6,2},{1... | collective-permute-start | bytes 1179656 | tf_op jit(solution)/shard_map/ppermute | solution.py:230
  45.2 0.7 copy-start.8
  50.9 1.7 %collective-permute-start.11 = (bf16[2,1,128,512]{3,2,1,0:T(8,128)(2,1)S(1)}, bf16[2,1,128,512]{3,2,1,0:T(8,128)(2,1)}, u32[]{:S(2)}, u32[]{:S(2)}) collective-permute-start(bf16[2,1,128,512]{3,2,1,0:T(8,128)(2,1)S(1)} %add_partial.3.refs_4_), channel_id=1, source_target_pairs={{0,4},{4,0},{8,12},{12,8},{1,5},{5,1},{9,13},{13,9},{2,6},{6,2},{1... | collective-permute-start | bytes 786440 | tf_op jit(solution)/shard_map/ppermute | solution.py:230
  51.0 9.0 %collective-permute-start.16 = (bf16[2,1,128,512]{3,2,1,0:T(8,128)(2,1)}, bf16[2,1,128,512]{3,2,1,0:T(8,128)(2,1)}, u32[]{:S(2)}, u32[]{:S(2)}) collective-permute-start(bf16[2,1,128,512]{3,2,1,0:T(8,128)(2,1)} %get-tuple-element.39), channel_id=1, source_target_pairs={{16,0},{0,16},{17,1},{1,17},{18,2},{2,18},{19,3},{3,19},{20,4},{4,... | collective-permute-start | bytes 786440 | tf_op jit(solution)/shard_map/ppermute | solution.py:233
  52.1 4.2 %copy-start.5 = (bf16[3,1,128,512]{3,2,1,0:T(8,128)(2,1)S(1)}, bf16[3,1,128,512]{3,2,1,0:T(8,128)(2,1)}, u32[]{:S(2)}) copy-start(bf16[3,1,128,512]{3,2,1,0:T(8,128)(2,1)} %copy-done.4) | copy-start | bytes 1179652
  52.1 4.2 %copy-start.9 = (bf16[3,1,128,512]{3,2,1,0:T(8,128)(2,1)S(1)}, bf16[3,1,128,512]{3,2,1,0:T(8,128)(2,1)}, u32[]{:S(2)}) copy-start(bf16[3,1,128,512]{3,2,1,0:T(8,128)(2,1)} %copy-done.8) | copy-start | bytes 1179652
  54.8 0.7 copy-start.12
  55.5 0.8 copy-start.10
  56.2 1.0 %copy-start.11 = (bf16[3,1,128,512]{3,2,1,0:T(8,128)(2,1)S(1)}, bf16[3,1,128,512]{3,2,1,0:T(8,128)(2,1)}, u32[]{:S(2)}) copy-start(bf16[3,1,128,512]{3,2,1,0:T(8,128)(2,1)} %copy-done.10) | copy-start | bytes 1179652
  59.5 0.7 copy-start.16
  61.4 3.2 %collective-permute-start.17 = (bf16[2,1,128,512]{3,2,1,0:T(8,128)(2,1)S(1)}, bf16[2,1,128,512]{3,2,1,0:T(8,128)(2,1)}, u32[]{:S(2)}, u32[]{:S(2)}) collective-permute-start(bf16[2,1,128,512]{3,2,1,0:T(8,128)(2,1)S(1)} %add_partial.4.refs_4_), channel_id=1, source_target_pairs={{0,4},{4,0},{8,12},{12,8},{1,5},{5,1},{9,13},{13,9},{2,6},{6,2},{1... | collective-permute-start | bytes 786440 | tf_op jit(solution)/shard_map/ppermute | solution.py:230
  61.6 8.9 %collective-permute-start.19 = (bf16[2,1,128,512]{3,2,1,0:T(8,128)(2,1)}, bf16[2,1,128,512]{3,2,1,0:T(8,128)(2,1)}, u32[]{:S(2)}, u32[]{:S(2)}) collective-permute-start(bf16[2,1,128,512]{3,2,1,0:T(8,128)(2,1)} %get-tuple-element.40), channel_id=1, source_target_pairs={{16,0},{0,16},{17,1},{1,17},{18,2},{2,18},{19,3},{3,19},{20,4},{4,... | collective-permute-start | bytes 786440 | tf_op jit(solution)/shard_map/ppermute | solution.py:233
  62.5 9.3 %collective-permute-start.15 = (bf16[1,1,128,512]{3,2,1,0:T(8,128)(2,1)}, bf16[1,1,128,512]{3,2,1,0:T(8,128)(2,1)}, u32[]{:S(2)}, u32[]{:S(2)}) collective-permute-start(bf16[1,1,128,512]{3,2,1,0:T(8,128)(2,1)} %get-tuple-element.44), channel_id=1, source_target_pairs={{0,8},{4,12},{8,0},{12,4},{1,9},{5,13},{9,1},{13,5},{2,10},{6,14},... | collective-permute-start | bytes 393224 | tf_op jit(solution)/shard_map/ppermute | solution.py:226
  63.0 1.6 %copy-start.13 = (bf16[1,1,128,512]{3,2,1,0:T(8,128)(2,1)S(1)}, bf16[1,1,128,512]{3,2,1,0:T(8,128)(2,1)}, u32[]{:S(2)}) copy-start(bf16[1,1,128,512]{3,2,1,0:T(8,128)(2,1)} %copy-done.12) | copy-start | bytes 393220
  63.0 18.2 %collective-permute-start.14 = (bf16[3,1,128,512]{3,2,1,0:T(8,128)(2,1)}, bf16[3,1,128,512]{3,2,1,0:T(8,128)(2,1)S(1)}, u32[]{:S(2)}, u32[]{:S(2)}) collective-permute-start(bf16[3,1,128,512]{3,2,1,0:T(8,128)(2,1)} %copy-done.16), channel_id=1, source_target_pairs={{0,8},{4,12},{8,0},{12,4},{1,9},{5,13},{9,1},{13,5},{2,10},{6,14},... | collective-permute-start | bytes 1179656 | tf_op jit(solution)/shard_map/ppermute | solution.py:226
  66.1 13.3 %collective-permute-start.18 = (bf16[1,1,128,512]{3,2,1,0:T(8,128)(2,1)S(1)}, bf16[1,1,128,512]{3,2,1,0:T(8,128)(2,1)S(1)}, u32[]{:S(2)}, u32[]{:S(2)}) collective-permute-start(bf16[1,1,128,512]{3,2,1,0:T(8,128)(2,1)S(1)} %get-tuple-element.50), channel_id=1, source_target_pairs={{0,8},{4,12},{8,0},{12,4},{1,9},{5,13},{9,1},{13,5},{2,10},{6,14},... | collective-permute-start | bytes 393224 | tf_op jit(solution)/shard_map/ppermute | solution.py:226
  71.7 7.8 %collective-permute-start.20 = (bf16[2,1,128,512]{3,2,1,0:T(8,128)(2,1)S(1)}, bf16[2,1,128,512]{3,2,1,0:T(8,128)(2,1)S(1)}, u32[]{:S(2)}, u32[]{:S(2)}) collective-permute-start(bf16[2,1,128,512]{3,2,1,0:T(8,128)(2,1)S(1)} %add_partial.5), channel_id=1, source_target_pairs={{0,4},{4,0},{8,12},{12,8},{1,5},{5,1},{9,13},{13,9},{2,6},{6,2},{1... | collective-permute-start | bytes 786440 | tf_op jit(solution)/shard_map/ppermute | solution.py:230
  80.5 5.0 %collective-permute-start.21 = (bf16[1,1,128,512]{3,2,1,0:T(8,128)(2,1)S(1)}, bf16[1,1,128,512]{3,2,1,0:T(8,128)(2,1)S(1)}, u32[]{:S(2)}, u32[]{:S(2)}) collective-permute-start(bf16[1,1,128,512]{3,2,1,0:T(8,128)(2,1)S(1)} %get-tuple-element.57), channel_id=1, source_target_pairs={{0,8},{4,12},{8,0},{12,4},{1,9},{5,13},{9,1},{13,5},{2,10},{6,14},... | collective-permute-start | bytes 393224 | tf_op jit(solution)/shard_map/ppermute | solution.py:226
  81.3 4.3 %copy-start.17 = (bf16[3,2,128,512]{3,2,1,0:T(8,128)(2,1)}, bf16[3,2,128,512]{3,2,1,0:T(8,128)(2,1)S(1)}, u32[]{:S(2)}) copy-start(bf16[3,2,128,512]{3,2,1,0:T(8,128)(2,1)S(1)} %constant_dynamic-update-slice_fusion.6) | copy-start | bytes 2359300
  85.6 0.9 %copy-start.18 = (bf16[3,2,128,512]{3,2,1,0:T(8,128)(2,1)}, bf16[3,2,128,512]{3,2,1,0:T(8,128)(2,1)S(1)}, u32[]{:S(2)}) copy-start(bf16[3,2,128,512]{3,2,1,0:T(8,128)(2,1)S(1)} %constant_dynamic-update-slice_fusion) | copy-start | bytes 2359300

commit v6 on v0

v6 whole, which is shorter than its diff:
```python
import math

import jax
import jax.numpy as jnp
from jax import lax
from jax.experimental import pallas as pl
from jax.experimental.pallas import tpu as pltpu
from jax.sharding import PartitionSpec as P

MAXOFF = 9
BF16 = jnp.bfloat16
STEP = 16
LANES = 128
WHOLE = pl.BlockSpec(memory_space=pltpu.VMEM)
PARAMS = pltpu.CompilerParams(vmem_limit_bytes=12 * 1024 * 1024)
COST = pl.CostEstimate(flops=1, bytes_accessed=1, transcendentals=0)


def call(kernel, outs, name, *args):
    outs = [x if isinstance(x, jax.ShapeDtypeStruct) else jax.ShapeDtypeStruct(x, BF16) for x in outs]
    return pl.pallas_call(
        kernel,
        in_specs=[WHOLE] * len(args),
        out_specs=[WHOLE] * len(outs),
        out_shape=outs,
        compiler_params=PARAMS,
        cost_estimate=COST,
        name=name,
    )(*args)


def after(xs, *earlier):
    return lax.optimization_barrier((tuple(xs), earlier))[0]


def chunks(rows, body):
    @pl.loop(0, rows // STEP, unroll=math.gcd(rows // STEP, 4))
    def _(i):
        body(pl.ds(pl.multiple_of(i * STEP, STEP), STEP))


def weighted(tables, energies, load):
    totals = [None] * len(energies)
    for t, table in enumerate(tables):
        for m in range(table.shape[0]):
            g = load(t, m).astype(jnp.float32)
            for i, n in enumerate(energies):
                row = table[m, n : n + 1, :]
                term = jnp.concatenate([row] * (g.shape[1] // LANES), axis=1) * g
                totals[i] = term if totals[i] is None else totals[i] + term
    return totals


def solution(mesh):
    en, ph = mesh.shape["en"], mesh.shape["ph"]

    def on_device(lesser_in, greater_in, inverse, offsets, couplings):
        e, nb, r, o = lesser_in.shape
        held = offsets.shape[1]
        owners = math.gcd(nb, ph)
        lanes = ph // owners
        owned = nb // owners
        pieces = ph
        others = range(1, owners)
        reach = (MAXOFF + e - 1) // e
        shifts = [t for t in range(1, en) if t <= reach or en - t <= reach]
        block = (e, owned, r, o)
        tile = -(-e // 8) * 8

        def owner_at(d):
            return lax.rem(lax.div(lax.axis_index("ph"), lanes) + d, owners)

        def place_of(j):
            at = lax.axis_index("ph")
            back = lax.rem(lax.div(at, lanes) + owners - j % owners, owners)
            return back * lanes + lax.rem(lax.rem(at, lanes) + lanes - j // owners, lanes)

        def to_owner(x, d):
            pairs = [(p, (p // lanes + d) % owners * lanes + p % lanes) for p in range(ph)]
            return lax.ppermute(x, "ph", pairs)

        def to_lanes(x):
            return [
                lax.ppermute(
                    x, "ph", [(p, p // lanes * lanes + (p % lanes + q) % lanes) for p in range(ph)]
                )
                for q in range(1, lanes)
            ]

        def from_energy(x, t):
            return lax.ppermute(x, "en", [((i + t) % en, i) for i in range(en)])

        def slices(wanted, earlier=()):
            def kernel(*refs):
                for i, (_, d) in enumerate(wanted):
                    for b in range(owned):
                        refs[len(wanted) + i][:, b] = refs[i][:, owner_at(d) * owned + b]

            arrays = after([x for x, _ in wanted], *earlier)
            return call(kernel, [block] * len(wanted), "slices", *arrays)

        def first(offsets_ref, couplings_ref, lesser_ref, greater_ref, packed_ref, *refs):
            packed_ref[...] = jnp.zeros_like(packed_ref)
            packed_ref[0, :e, :held] = offsets_ref[...].astype(jnp.float32)
            packed_ref[1, :e, :held] = couplings_ref[...]
            for i, d in enumerate(others):
                for b in range(owned):
                    refs[i][:, b] = greater_ref[:, owner_at(d) * owned + b]
                    refs[owners - 1 + i][:, b] = lesser_ref[:, owner_at(d) * owned + b]

        def join(*refs):
            for i, ref in enumerate(refs[:-1]):
                refs[-1][i] = ref[...]

        def weights(*refs):
            ins, outs = refs[:lanes], refs[lanes:]
            at = lax.axis_index("en")
            row = lax.broadcasted_iota(jnp.int32, (tile, LANES), 0)
            for i, t in enumerate([0] + shifts):
                away = (lax.rem(at + t, en) - at) * e
                for m in range(e):
                    apart = (away + m - row).astype(jnp.float32)
                    total = jnp.zeros((tile, LANES), jnp.float32)
                    for ref in ins:
                        for d in range(owners):
                            total += jnp.where(ref[d, 0] == apart, ref[d, 1], 0.0)
                    outs[i][m] = jnp.broadcast_to(
                        jnp.sum(total, axis=1, keepdims=True), (tile, LANES)
                    )

        def mix(tables, received, d, earlier):
            def kernel(*refs):
                table_refs, ins = refs[: len(tables)], refs[len(tables) : -1]
                for b in range(owned):
                    at_block = owner_at(d) * owned + b

                    def body(at):
                        totals = weighted(
                            table_refs, range(e), lambda t, m: ins[t][m, b if t else at_block, at, :]
                        )
                        for n in range(e):
                            refs[-1][n, b, at, :] = totals[n].astype(BF16)

                    chunks(r, body)

            return call(kernel, [block], "mix", *after(tables, *earlier), lesser_in, *received)[0]

        def greater_at(refs, m, d, b, at):
            return refs[d][m, b if d else owner_at(0) * owned + b, at, :]

        def partial_sums(table, rows, earlier):
            def kernel(table_ref, *refs):
                for d in range(owners):
                    for b in range(owned):

                        def body(at):
                            totals = weighted(
                                [table_ref], range(e), lambda t, m: greater_at(refs, m, d, b, at)
                            )
                            for n in range(e):
                                refs[owners + n][d, b, at, :] = totals[n].astype(BF16)

                        chunks(r, body)

            (table,) = after([table], *earlier)
            return call(kernel, [(owners,) + block[1:]] * e, "partial_sums", table, greater_in, *rows)

        def add_partial(n, table, rows, received, earlier):
            def kernel(table_ref, *refs):
                for d in range(owners):
                    for b in range(owned):

                        def body(at):
                            (total,) = weighted(
                                [table_ref], [n], lambda t, m: greater_at(refs, m, d, b, at)
                            )
                            for ref in refs[owners:-1]:
                                total = total + ref[d, b, at, :].astype(jnp.float32)
                            refs[-1][d, b, at, :] = total.astype(BF16)

                        chunks(r, body)

            (table,) = after([table], *earlier)
            return call(
                kernel, [(owners,) + block[1:]], "add_partial", table, greater_in, *rows, *received
            )[0]

        def product(energies, inverse_pieces, sigma, sigma_at, earlier):
            def kernel(*refs):
                a_in, s_in, outs = refs[:pieces], refs[pieces:-owners], refs[-owners:]
                spans = [pl.ds(pl.multiple_of(place_of(j) * r, r), r) for j in range(pieces)]
                for k, n in enumerate(energies):
                    for b in range(owned):
                        left = jnp.concatenate(
                            [
                                jnp.concatenate([a_in[i][n, b, :, at] for at in spans], axis=1)
                                for i in range(owners)
                            ],
                            axis=0,
                        )
                        stands = [sigma_at(n, j) for j in range(pieces)]
                        right = jnp.concatenate([s_in[i][lead, b] for i, lead in stands], axis=0)
                        half = jnp.dot(left, right, preferred_element_type=jnp.float32).astype(BF16)
                        full = lax.dot_general(
                            half,
                            jnp.concatenate([a[n, b] for a in a_in], axis=0),
                            (((1,), (1,)), ((), ())),
                            preferred_element_type=jnp.float32,
                        ).astype(BF16)
                        for i in range(owners):
                            for j, at in enumerate(spans):
                                outs[i][k, b, :, at] = full[i * r : (i + 1) * r, j * r : (j + 1) * r]

            shape = (len(energies),) + block[1:]
            return call(kernel, [shape] * owners, "product", *after(inverse_pieces, *earlier), *sigma)

        def back_to_rows(outs):
            return [outs[0]] + [to_owner(outs[d], owners - d) for d in others]

        def place(result, parts, earlier):
            def kernel(*refs):
                sems, ins, out = refs[-1], refs[: len(parts)], refs[-2]
                copies = [
                    pltpu.make_async_copy(
                        ins[i],
                        out.at[pl.ds(n, x.shape[0]), pl.ds(owner_at(d) * owned, owned)],
                        sems.at[i],
                    )
                    for i, (n, d, x) in enumerate(parts)
                ]
                for copy in copies:
                    copy.start()
                for copy in copies:
                    copy.wait()

            arrays = after([x for _, _, x in parts], *earlier)
            far = pl.BlockSpec(memory_space=pltpu.HBM)
            return pl.pallas_call(
                kernel,
                in_specs=[WHOLE] * len(parts) + [far] * (result is not None),
                out_specs=far,
                out_shape=jax.ShapeDtypeStruct((e, nb, r, o), BF16),
                scratch_shapes=[pltpu.SemaphoreType.DMA((len(parts),))],
                input_output_aliases={} if result is None else {len(parts): 0},
                compiler_params=PARAMS,
                cost_estimate=COST,
                name="place",
            )(*arrays, *([] if result is None else [result]))

        packed, *parts = call(
            first,
            [jax.ShapeDtypeStruct((2, tile, LANES), jnp.float32)] + [block] * (2 * len(others)),
            "first",
            offsets,
            couplings,
            lesser_in,
            greater_in,
        )
        greater_part, lesser_part = parts[: owners - 1], parts[owners - 1 :]
        packed_from = [packed] + [to_owner(packed, d) for d in others]
        lesser_from = [[from_energy(x, t) for t in shifts] for x in lesser_part]
        greater_part = after(greater_part, *packed_from)
        greater_rows = [to_owner(x, d) for d, x in zip(others, greater_part)]

        (column,) = call(
            join,
            [jax.ShapeDtypeStruct((owners, 2, tile, LANES), jnp.float32)],
            "join",
            *after(packed_from, *greater_part),
        )
        tables = call(
            weights,
            [jax.ShapeDtypeStruct((e, tile, LANES), jnp.float32)] * (1 + len(shifts)),
            "weights",
            column,
            *to_lanes(column),
        )
        tables_for = [
            lax.ppermute(table, "en", [(i, (i + t) % en) for i in range(en)])
            for t, table in zip(shifts, tables[1:])
        ]

        inverse_part = slices([(inverse, d) for d in others], tables)
        inverse_rows = [to_owner(x, d) for d, x in zip(others, inverse_part)]
        (lesser_own,) = slices([(lesser_in, 0)], inverse_part)
        lesser_from.insert(0, [from_energy(lesser_own, t) for t in shifts])

        last = [lesser_own]
        lesser_rows = [None]
        for d in others:
            last = [mix(tables, lesser_from[d], d, last)]
            lesser_rows.append(to_owner(last[0], d))
        (inverse_own,) = slices([(inverse, 0)], last)
        inverse_lanes = [to_lanes(inverse_own)]
        last = [inverse_own, *inverse_lanes[0]]
        received = [[] for _ in range(e)]
        for t, table in zip(shifts, tables_for):
            last = partial_sums(table, greater_rows, last)
            for n, part in enumerate(last):
                received[n].append(from_energy(part, t))
        inverse_lanes += [to_lanes(x) for x in inverse_rows]
        lesser_rows[0] = mix(tables, lesser_from[0], 0, [*last, *sum(inverse_lanes[1:], [])])
        lesser_lanes = [to_lanes(lesser_rows[0])]
        last = [lesser_rows[0], *lesser_lanes[0]]

        def in_order(rows, beside):
            return rows + [x[q] for q in range(lanes - 1) for x in beside]

        inverse_full = in_order([inverse_own] + inverse_rows, inverse_lanes)

        lesser_out = greater_out = None
        for n in range(e):
            sigma = add_partial(n, tables[0], greater_rows, received[n], last)
            outs = product(
                [n],
                inverse_full,
                [sigma] + to_lanes(sigma),
                lambda n, j: (j // owners, j % owners),
                [],
            )
            greater_back = back_to_rows(outs)
            last = outs
            if n == 0:
                lesser_lanes += [to_lanes(x) for x in lesser_rows[1:]]
                outs = product(
                    range(e), inverse_full, in_order(lesser_rows, lesser_lanes), lambda n, j: (j, n), last
                )
                lesser_back = back_to_rows(outs)
                last = outs
            if n < e - 1:
                greater_out = place(greater_out, [(n, d, x) for d, x in enumerate(greater_back)], [])
            else:
                lesser_out = place(None, [(0, d, x) for d, x in enumerate(lesser_back)], last)
                greater_out = place(greater_out, [(n, 0, outs[0])], [lesser_out])
                greater_out = place(greater_out, [(n, d, greater_back[d]) for d in others], [])

        return lesser_out, greater_out

    block, coupled = P("en", "blk", "ph", None), P("en", "ph")
    return jax.shard_map(
        on_device,
        mesh=mesh,
        in_specs=(block, block, block, coupled, coupled),
        out_specs=(block, block),
        check_vma=False,
    )
```

time: 144 us -> 76.6 us (0.53)
  blocking collectives: 28.9 us -> 0 us
  waiting for transfers between devices: 63.1 us -> 43 us
  between operations: 14.2 us -> 0.87 us
  local copies, waits for them, and re-layouts: 12.2 us -> 3.15 us
  Pallas kernels: 0 us -> 8.55 us
  matrix products: 8.25 us -> 0 us
  starting transfers between devices: 15.7 us -> 20.8 us
    all_gather x2 -> x0, waiting for transfers between devices: 47.8 us -> none  [the longest x1 47.8 us: on_device(): lax.all_gather(self_energy, 'ph', axis=3, tiled=True)]
    ppermute x0 -> x22, waiting for transfers between devices: none -> 43 us  [the longest x5 18.7 us: from_energy(): return lax.ppermute(x, 'en', [((i + t) % en, i) for i in range(en)])]
    all_gather x4 -> x0, blocking collectives: 28.9 us -> none  [the longest x1 13.8 us: on_device(): weight_every = lax.all_gather(weights_all, 'en', axis=0, tiled=True)]
    ppermute x0 -> x22, starting transfers between devices: none -> 20.8 us  [the longest x8 11.5 us: to_owner(): return lax.ppermute(x, 'ph', pairs)]
    all_to_all x4 -> x0, starting transfers between devices: 15.6 us -> none  [the longest x2 7.86 us: on_device(): lax.all_to_all(shortened(mixed), 'en', split_axis=0, concat_axis=3, tiled...]
    all_to_all x4 -> x0, waiting for transfers between devices: 14.6 us -> none  [the longest x2 14.6 us: on_device(): lax.all_to_all(shortened(mixed), 'en', split_axis=0, concat_axis=3, tiled...]
    pallas_call x0 -> x21, Pallas kernels: none -> 8.55 us  [the longest x16 4.85 us: call(): pl.pallas_call(kernel, in_specs=[WHOLE] * len(args), out_specs=[WHOLE] *...]
    dot_general x3 -> x0, matrix products: 8.25 us -> none  [the longest x1 6.32 us: on_device(): jnp.einsum('sebrk,ebck->sebrc', left_product, inverse_full, preferred_ele...]
  transfers between devices with their start and end apart: 6 -> 22, of which waited for: 3 -> 8; matrix products, arithmetic and copies ran while one was open for 10% -> 0% of each run, Pallas kernels for 0% -> 10%
where the time goes in v6:
time: 76.6 us; the launch traced here: 76.4 us
  waiting for transfers between devices  43 us (56%)
  starting transfers between devices  20.8 us (27%)
  Pallas kernels  8.55 us (11%)
  local copies, waits for them, and re-layouts  3.15 us (4%)
  between operations  0.87 us (1%)
    ppermute x5, waiting for transfers between devices, from_energy(): return lax.ppermute(x, 'en', [((i + t) % en, i) for i in range(en)])  18.7 us
    ppermute x8, waiting for transfers between devices, to_owner(): return lax.ppermute(x, 'ph', pairs)  14.7 us
    ppermute x8, starting transfers between devices, to_owner(): return lax.ppermute(x, 'ph', pairs)  11.5 us
    ppermute x1, waiting for transfers between devices, on_device(): lax.ppermute(table, 'en', [(i, (i + t) % en) for i in range(en)])  9.6 us
    ppermute x5, starting transfers between devices, from_energy(): return lax.ppermute(x, 'en', [((i + t) % en, i) for i in range(en)])  7.78 us
    pallas_call x16, Pallas kernels, call(): pl.pallas_call(kernel, in_specs=[WHOLE] * len(args), out_specs=[WHOLE] *...  4.85 us
    pallas_call x5, Pallas kernels, place(): pl.pallas_call(kernel, in_specs=[WHOLE] * len(parts) + [far] * (result is...  3.7 us
    unnamed x14, local copies, waits for them, and re-layouts  3.15 us
  transfers between devices with their start and end apart: 22, of which 8 were waited for; matrix products, arithmetic and copies ran while one was open for 0% of the time, Pallas kernels for 10%

profile of v6, /device:TPU:0, one launch (start us, length us, event | category | flops | bytes accessed | tf_op | source)
XLA Modules:
  0.0 76.4 jit_solution(16561355095433138195)
XLA Ops:
  0.6 0.8 %copy.10.offsets_ref = s32[3,2]{1,0:T(4,128)S(1)} copy(s32[3,2]{0,1:T(2,128)} %param.8) | data formatting | bytes 48 | tf_op args[3]
  1.4 0.1 copy.11.couplings_ref
  1.5 1.1 %copy-done = bf16[3,2,128,512]{3,2,1,0:T(8,128)(2,1)S(1)} copy-done((bf16[3,2,128,512]{3,2,1,0:T(8,128)(2,1)S(1)}, bf16[3,2,128,512]{3,2,1,0:T(8,128)(2,1)}, u32[]{:S(2)}) %copy-start) | copy-done | bytes 786456
  2.6 1.1 %copy-done.2 = bf16[3,2,128,512]{3,2,1,0:T(8,128)(2,1)S(1)} copy-done((bf16[3,2,128,512]{3,2,1,0:T(8,128)(2,1)S(1)}, bf16[3,2,128,512]{3,2,1,0:T(8,128)(2,1)}, u32[]{:S(2)}) %copy-start.2) | copy-done | bytes 786456
  3.8 0.1 first.1
  3.8 0.0 copy-start.3
  3.8 3.0 %collective-permute-start = (f32[2,8,128]{2,1,0:T(8,128)S(1)}, f32[2,8,128]{2,1,0:T(8,128)S(1)}, u32[]{:S(2)}, u32[]{:S(2)}) collective-permute-start(f32[2,8,128]{2,1,0:T(8,128)S(1)} %get-tuple-element.50.refs_0_), channel_id=1, source_target_pairs={{0,8},{4,12},{8,0},{12,4},{1,9},{5,13},{9,1},{13,5},{2,10},{6,14},... | collective-permute-start | bytes 24584 | tf_op jit(solution)/shard_map/ppermute | solution.py:80
  6.9 1.6 %collective-permute-done.refs_1_ = f32[2,8,128]{2,1,0:T(8,128)S(1)} collective-permute-done((f32[2,8,128]{2,1,0:T(8,128)S(1)}, f32[2,8,128]{2,1,0:T(8,128)S(1)}, u32[]{:S(2)}, u32[]{:S(2)}) %collective-permute-start) | collective-permute-done | bytes 8224 | tf_op jit(solution)/shard_map/ppermute | solution.py:80
  8.5 0.0 collective-permute-start.1
  8.5 2.0 %collective-permute-start.2 = (bf16[3,1,128,512]{3,2,1,0:T(8,128)(2,1)S(1)}, bf16[3,1,128,512]{3,2,1,0:T(8,128)(2,1)S(1)}, u32[]{:S(2)}, u32[]{:S(2)}) collective-permute-start(bf16[3,1,128,512]{3,2,1,0:T(8,128)(2,1)S(1)} %get-tuple-element.58), channel_id=1, source_target_pairs={{16,0},{0,16},{17,1},{1,17},{18,2},{2,18},{19,3},{3,19},{20,4},{4,... | collective-permute-start | bytes 1179656 | tf_op jit(solution)/shard_map/ppermute | solution.py:91
  10.5 0.0 collective-permute-done.1.refs_1_
  10.5 0.1 weights.1
  10.6 1.6 %collective-permute-start.3 = (bf16[3,1,128,512]{3,2,1,0:T(8,128)(2,1)S(1)}, bf16[3,1,128,512]{3,2,1,0:T(8,128)(2,1)S(1)}, u32[]{:S(2)}, u32[]{:S(2)}) collective-permute-start(bf16[3,1,128,512]{3,2,1,0:T(8,128)(2,1)S(1)} %slices.3), channel_id=1, source_target_pairs={{0,8},{4,12},{8,0},{12,4},{1,9},{5,13},{9,1},{13,5},{2,10},{6,14},... | collective-permute-start | bytes 1179656 | tf_op jit(solution)/shard_map/ppermute | solution.py:80
  12.3 8.0 %collective-permute-done.2.refs_3_ = bf16[3,1,128,512]{3,2,1,0:T(8,128)(2,1)S(1)} collective-permute-done((bf16[3,1,128,512]{3,2,1,0:T(8,128)(2,1)S(1)}, bf16[3,1,128,512]{3,2,1,0:T(8,128)(2,1)S(1)}, u32[]{:S(2)}, u32[]{:S(2)}) %collective-permute-start.2) | collective-permute-done | bytes 393248 | tf_op jit(solution)/shard_map/ppermute | solution.py:91
  20.3 0.4 mix.2
  20.7 0.0 copy-start.1
  20.7 0.1 collective-permute-start.4
  20.8 1.8 %collective-permute-start.7 = (bf16[3,1,128,512]{3,2,1,0:T(8,128)(2,1)S(1)}, bf16[3,1,128,512]{3,2,1,0:T(8,128)(2,1)S(1)}, u32[]{:S(2)}, u32[]{:S(2)}) collective-permute-start(bf16[3,1,128,512]{3,2,1,0:T(8,128)(2,1)S(1)} %get-tuple-element.49), channel_id=1, source_target_pairs={{0,8},{4,12},{8,0},{12,4},{1,9},{5,13},{9,1},{13,5},{2,10},{6,14},... | collective-permute-start | bytes 1179656 | tf_op jit(solution)/shard_map/ppermute | solution.py:80
  22.6 0.0 collective-permute-done.3.refs_1_
  22.7 0.2 collective-permute-start.5
  22.8 1.5 %collective-permute-start.8 = (bf16[3,1,128,512]{3,2,1,0:T(8,128)(2,1)S(1)}, bf16[3,1,128,512]{3,2,1,0:T(8,128)(2,1)S(1)}, u32[]{:S(2)}, u32[]{:S(2)}) collective-permute-start(bf16[3,1,128,512]{3,2,1,0:T(8,128)(2,1)S(1)} %slices.4), channel_id=1, source_target_pairs={{16,0},{0,16},{17,1},{1,17},{18,2},{2,18},{19,3},{3,19},{20,4},{4,... | collective-permute-start | bytes 1179656 | tf_op jit(solution)/shard_map/ppermute | solution.py:91
  24.3 0.5 collective-permute-start.6
  24.8 9.6 %collective-permute-done.6.table_ref = f32[3,8,128]{2,1,0:T(8,128)S(1)} collective-permute-done((f32[3,8,128]{2,1,0:T(8,128)S(1)}, f32[3,8,128]{2,1,0:T(8,128)S(1)}, u32[]{:S(2)}, u32[]{:S(2)}) %collective-permute-start.6) | collective-permute-done | bytes 12320 | tf_op jit(solution)/shard_map/ppermute | solution.py:279
  34.4 0.8 %collective-permute-start.12 = (bf16[3,1,128,512]{3,2,1,0:T(8,128)(2,1)S(1)}, bf16[3,1,128,512]{3,2,1,0:T(8,128)(2,1)S(1)}, u32[]{:S(2)}, u32[]{:S(2)}) collective-permute-start(bf16[3,1,128,512]{3,2,1,0:T(8,128)(2,1)S(1)} %mix.2), channel_id=1, source_target_pairs={{0,8},{4,12},{8,0},{12,4},{1,9},{5,13},{9,1},{13,5},{2,10},{6,14},... | collective-permute-start | bytes 1179656 | tf_op jit(solution)/shard_map/ppermute | solution.py:80
  35.3 0.0 collective-permute-done.4.refs_2_
  35.3 0.0 collective-permute-done.7.refs_1_
  35.3 0.4 partial_sums.1
  35.7 0.0 collective-permute-done.5.refs_3_
  35.7 0.0 collective-permute-done.8.refs_3_
  35.7 0.4 mix.3.refs_4_
  36.1 0.1 collective-permute-start.9
  36.2 1.2 %collective-permute-start.10 = (bf16[2,1,128,512]{3,2,1,0:T(8,128)(2,1)S(1)}, bf16[2,1,128,512]{3,2,1,0:T(8,128)(2,1)S(1)}, u32[]{:S(2)}, u32[]{:S(2)}) collective-permute-start(bf16[2,1,128,512]{3,2,1,0:T(8,128)(2,1)S(1)} %get-tuple-element.65), channel_id=1, source_target_pairs={{16,0},{0,16},{17,1},{1,17},{18,2},{2,18},{19,3},{3,19},{20,4},{4,... | collective-permute-start | bytes 786440 | tf_op jit(solution)/shard_map/ppermute | solution.py:91
  37.4 7.6 %collective-permute-done.12.refs_5_ = bf16[3,1,128,512]{3,2,1,0:T(8,128)(2,1)S(1)} collective-permute-done((bf16[3,1,128,512]{3,2,1,0:T(8,128)(2,1)S(1)}, bf16[3,1,128,512]{3,2,1,0:T(8,128)(2,1)S(1)}, u32[]{:S(2)}, u32[]{:S(2)}) %collective-permute-start.12) | collective-permute-done | bytes 393248 | tf_op jit(solution)/shard_map/ppermute | solution.py:80
  45.0 0.0 collective-permute-start.13
  45.0 0.0 collective-permute-done.9.refs_6_
  45.0 0.0 collective-permute-done.10.refs_2_
  45.0 0.2 add_partial.3.refs_4_
  45.3 0.6 collective-permute-start.11
  45.8 1.5 %collective-permute-start.15 = (bf16[2,1,128,512]{3,2,1,0:T(8,128)(2,1)S(1)}, bf16[2,1,128,512]{3,2,1,0:T(8,128)(2,1)S(1)}, u32[]{:S(2)}, u32[]{:S(2)}) collective-permute-start(bf16[2,1,128,512]{3,2,1,0:T(8,128)(2,1)S(1)} %get-tuple-element.66), channel_id=1, source_target_pairs={{16,0},{0,16},{17,1},{1,17},{18,2},{2,18},{19,3},{3,19},{20,4},{4,... | collective-permute-start | bytes 786440 | tf_op jit(solution)/shard_map/ppermute | solution.py:91
  47.3 0.0 collective-permute-done.11.refs_5_
  47.3 0.5 product.4
  47.8 0.0 collective-permute-done.13.refs_7_
  47.9 1.2 %product.5 = (bf16[3,1,128,512]{3,2,1,0:T(8,128)(2,1)S(1)}, bf16[3,1,128,512]{3,2,1,0:T(8,128)(2,1)S(1)}) custom-call(bf16[3,1,128,512]{3,2,1,0:T(8,128)(2,1)S(1)} %slices.5.refs_0_, bf16[3,1,128,512]{3,2,1,0:T(8,128)(2,1)S(1)} %collective-permute-done.3.refs_1_, bf16[3,1,128,512]{3,2,1,0:T(8,128)(2,1)S(1)} %collective-permute-done.4.refs_2_, ...), custom_call_target="tpu_custom_call" | custom-call | flops 1 | bytes 1 | tf_op jit(solution)/shard_map/product/pallas_call | solution.py:21
  49.1 5.0 %collective-permute-done.15.refs_2_ = bf16[2,1,128,512]{3,2,1,0:T(8,128)(2,1)S(1)} collective-permute-done((bf16[2,1,128,512]{3,2,1,0:T(8,128)(2,1)S(1)}, bf16[2,1,128,512]{3,2,1,0:T(8,128)(2,1)S(1)}, u32[]{:S(2)}, u32[]{:S(2)}) %collective-permute-start.15) | collective-permute-done | bytes 262176 | tf_op jit(solution)/shard_map/ppermute | solution.py:91
  54.1 0.2 add_partial.4.refs_4_
  54.3 0.1 collective-permute-start.16
  54.4 1.6 %collective-permute-start.17 = (bf16[2,1,128,512]{3,2,1,0:T(8,128)(2,1)S(1)}, bf16[2,1,128,512]{3,2,1,0:T(8,128)(2,1)S(1)}, u32[]{:S(2)}, u32[]{:S(2)}) collective-permute-start(bf16[2,1,128,512]{3,2,1,0:T(8,128)(2,1)S(1)} %get-tuple-element.67), channel_id=1, source_target_pairs={{16,0},{0,16},{17,1},{1,17},{18,2},{2,18},{19,3},{3,19},{20,4},{4,... | collective-permute-start | bytes 786440 | tf_op jit(solution)/shard_map/ppermute | solution.py:91
  56.0 1.0 %collective-permute-start.14 = (bf16[3,1,128,512]{3,2,1,0:T(8,128)(2,1)S(1)}, bf16[3,1,128,512]{3,2,1,0:T(8,128)(2,1)S(1)}, u32[]{:S(2)}, u32[]{:S(2)}) collective-permute-start(bf16[3,1,128,512]{3,2,1,0:T(8,128)(2,1)S(1)} %get-tuple-element.78), channel_id=1, source_target_pairs={{0,8},{4,12},{8,0},{12,4},{1,9},{5,13},{9,1},{13,5},{2,10},{6,14},... | collective-permute-start | bytes 1179656 | tf_op jit(solution)/shard_map/ppermute | solution.py:80
  57.0 0.5 product.6
  57.5 5.6 %collective-permute-done.17.refs_2_ = bf16[2,1,128,512]{3,2,1,0:T(8,128)(2,1)S(1)} collective-permute-done((bf16[2,1,128,512]{3,2,1,0:T(8,128)(2,1)S(1)}, bf16[2,1,128,512]{3,2,1,0:T(8,128)(2,1)S(1)}, u32[]{:S(2)}, u32[]{:S(2)}) %collective-permute-start.17) | collective-permute-done | bytes 262176 | tf_op jit(solution)/shard_map/ppermute | solution.py:91
  63.1 0.2 add_partial.5.refs_4_
  63.4 0.1 collective-permute-start.18
  63.4 1.1 %collective-permute-start.21 = (bf16[1,1,128,512]{3,2,1,0:T(8,128)(2,1)S(1)}, bf16[1,1,128,512]{3,2,1,0:T(8,128)(2,1)S(1)}, u32[]{:S(2)}, u32[]{:S(2)}) collective-permute-start(bf16[1,1,128,512]{3,2,1,0:T(8,128)(2,1)S(1)} %get-tuple-element.72), channel_id=1, source_target_pairs={{0,8},{4,12},{8,0},{12,4},{1,9},{5,13},{9,1},{13,5},{2,10},{6,14},... | collective-permute-start | bytes 393224 | tf_op jit(solution)/shard_map/ppermute | solution.py:80
  64.5 1.0 %collective-permute-start.20 = (bf16[1,1,128,512]{3,2,1,0:T(8,128)(2,1)S(1)}, bf16[1,1,128,512]{3,2,1,0:T(8,128)(2,1)S(1)}, u32[]{:S(2)}, u32[]{:S(2)}) collective-permute-start(bf16[1,1,128,512]{3,2,1,0:T(8,128)(2,1)S(1)} %get-tuple-element.81), channel_id=1, source_target_pairs={{0,8},{4,12},{8,0},{12,4},{1,9},{5,13},{9,1},{13,5},{2,10},{6,14},... | collective-permute-start | bytes 393224 | tf_op jit(solution)/shard_map/ppermute | solution.py:80
  65.5 0.5 product.7
  66.1 1.1 %collective-permute-start.19 = (bf16[1,1,128,512]{3,2,1,0:T(8,128)(2,1)S(1)}, bf16[1,1,128,512]{3,2,1,0:T(8,128)(2,1)S(1)}, u32[]{:S(2)}, u32[]{:S(2)}) collective-permute-start(bf16[1,1,128,512]{3,2,1,0:T(8,128)(2,1)S(1)} %get-tuple-element.84), channel_id=1, source_target_pairs={{0,8},{4,12},{8,0},{12,4},{1,9},{5,13},{9,1},{13,5},{2,10},{6,14},... | collective-permute-start | bytes 393224 | tf_op jit(solution)/shard_map/ppermute | solution.py:80
  67.1 3.4 %collective-permute-done.21.refs_1_ = bf16[1,1,128,512]{3,2,1,0:T(8,128)(2,1)S(1)} collective-permute-done((bf16[1,1,128,512]{3,2,1,0:T(8,128)(2,1)S(1)}, bf16[1,1,128,512]{3,2,1,0:T(8,128)(2,1)S(1)}, u32[]{:S(2)}, u32[]{:S(2)}) %collective-permute-start.21) | collective-permute-done | bytes 131104 | tf_op jit(solution)/shard_map/ppermute | solution.py:80
  70.5 0.7 place.6.refs_2_
  71.2 2.1 %collective-permute-done.20.refs_1_ = bf16[1,1,128,512]{3,2,1,0:T(8,128)(2,1)S(1)} collective-permute-done((bf16[1,1,128,512]{3,2,1,0:T(8,128)(2,1)S(1)}, bf16[1,1,128,512]{3,2,1,0:T(8,128)(2,1)S(1)}, u32[]{:S(2)}, u32[]{:S(2)}) %collective-permute-start.20) | collective-permute-done | bytes 131104 | tf_op jit(solution)/shard_map/ppermute | solution.py:80
  73.3 0.7 place.7.refs_1_
  74.1 0.9 %place.5 = bf16[3,2,128,512]{3,2,1,0:T(8,128)(2,1)} custom-call(bf16[3,1,128,512]{3,2,1,0:T(8,128)(2,1)S(1)} %get-tuple-element.85.refs_0_, bf16[3,1,128,512]{3,2,1,0:T(8,128)(2,1)S(1)} %collective-permute-done.14.refs_1_), custom_call_target="tpu_custom_call" | custom-call | flops 1 | bytes 1 | tf_op jit(solution)/shard_map/place/pallas_call | solution.py:238
  75.0 0.7 place.8.refs_1_
  75.7 0.0 collective-permute-done.19.refs_0_
  75.7 0.7 place.9
  (15 shorter events, 0.1 us)
Async XLA Ops:
  0.6 0.8 %copy-start.5 = (f32[3,2]{0,1:T(2,128)S(1)}, f32[3,2]{0,1:T(2,128)}, u32[]{:S(2)}) copy-start(f32[3,2]{0,1:T(2,128)} %param.9) | copy-start | bytes 76
  1.5 1.1 %copy-start = (bf16[3,2,128,512]{3,2,1,0:T(8,128)(2,1)S(1)}, bf16[3,2,128,512]{3,2,1,0:T(8,128)(2,1)}, u32[]{:S(2)}) copy-start(bf16[3,2,128,512]{3,2,1,0:T(8,128)(2,1)} %refs_0_.10) | copy-start | bytes 2359300
  2.6 1.1 %copy-start.2 = (bf16[3,2,128,512]{3,2,1,0:T(8,128)(2,1)S(1)}, bf16[3,2,128,512]{3,2,1,0:T(8,128)(2,1)}, u32[]{:S(2)}) copy-start(bf16[3,2,128,512]{3,2,1,0:T(8,128)(2,1)} %refs_2_.3) | copy-start | bytes 2359300
  3.8 6.8 %copy-start.4 = (bf16[3,2,128,512]{3,2,1,0:T(8,128)(2,1)S(1)}, bf16[3,2,128,512]{3,2,1,0:T(8,128)(2,1)}, u32[]{:S(2)}) copy-start(bf16[3,2,128,512]{3,2,1,0:T(8,128)(2,1)} %refs_0_.6) | copy-start | bytes 2359300
  3.8 8.4 %copy-start.3 = (bf16[3,2,128,512]{3,2,1,0:T(8,128)(2,1)S(1)}, bf16[3,2,128,512]{3,2,1,0:T(8,128)(2,1)}, u32[]{:S(2)}) copy-start(bf16[3,2,128,512]{3,2,1,0:T(8,128)(2,1)} %refs_2_.3) | copy-start | bytes 2359300
  3.8 4.7 %collective-permute-start = (f32[2,8,128]{2,1,0:T(8,128)S(1)}, f32[2,8,128]{2,1,0:T(8,128)S(1)}, u32[]{:S(2)}, u32[]{:S(2)}) collective-permute-start(f32[2,8,128]{2,1,0:T(8,128)S(1)} %get-tuple-element.50.refs_0_), channel_id=1, source_target_pairs={{0,8},{4,12},{8,0},{12,4},{1,9},{5,13},{9,1},{13,5},{2,10},{6,14},... | collective-permute-start | bytes 24584 | tf_op jit(solution)/shard_map/ppermute | solution.py:80
  8.5 2.0 %collective-permute-start.1 = (f32[2,2,8,128]{3,2,1,0:T(8,128)S(1)}, f32[2,2,8,128]{3,2,1,0:T(8,128)S(1)}, u32[]{:S(2)}, u32[]{:S(2)}) collective-permute-start(f32[2,2,8,128]{3,2,1,0:T(8,128)S(1)} %join.1.refs_0_), channel_id=1, source_target_pairs={{0,4},{4,0},{8,12},{12,8},{1,5},{5,1},{9,13},{13,9},{2,6},{6,2},{1... | collective-permute-start | bytes 49160 | tf_op jit(solution)/shard_map/ppermute | solution.py:84
  8.5 11.8 %collective-permute-start.2 = (bf16[3,1,128,512]{3,2,1,0:T(8,128)(2,1)S(1)}, bf16[3,1,128,512]{3,2,1,0:T(8,128)(2,1)S(1)}, u32[]{:S(2)}, u32[]{:S(2)}) collective-permute-start(bf16[3,1,128,512]{3,2,1,0:T(8,128)(2,1)S(1)} %get-tuple-element.58), channel_id=1, source_target_pairs={{16,0},{0,16},{17,1},{1,17},{18,2},{2,18},{19,3},{3,19},{20,4},{4,... | collective-permute-start | bytes 1179656 | tf_op jit(solution)/shard_map/ppermute | solution.py:91
  10.6 12.0 %collective-permute-start.3 = (bf16[3,1,128,512]{3,2,1,0:T(8,128)(2,1)S(1)}, bf16[3,1,128,512]{3,2,1,0:T(8,128)(2,1)S(1)}, u32[]{:S(2)}, u32[]{:S(2)}) collective-permute-start(bf16[3,1,128,512]{3,2,1,0:T(8,128)(2,1)S(1)} %slices.3), channel_id=1, source_target_pairs={{0,8},{4,12},{8,0},{12,4},{1,9},{5,13},{9,1},{13,5},{2,10},{6,14},... | collective-permute-start | bytes 1179656 | tf_op jit(solution)/shard_map/ppermute | solution.py:80
  20.7 14.6 %copy-start.1 = (bf16[3,2,128,512]{3,2,1,0:T(8,128)(2,1)S(1)}, bf16[3,2,128,512]{3,2,1,0:T(8,128)(2,1)}, u32[]{:S(2)}) copy-start(bf16[3,2,128,512]{3,2,1,0:T(8,128)(2,1)} %refs_0_.10) | copy-start | bytes 2359300
  20.7 14.5 %collective-permute-start.4 = (bf16[3,1,128,512]{3,2,1,0:T(8,128)(2,1)S(1)}, bf16[3,1,128,512]{3,2,1,0:T(8,128)(2,1)S(1)}, u32[]{:S(2)}, u32[]{:S(2)}) collective-permute-start(bf16[3,1,128,512]{3,2,1,0:T(8,128)(2,1)S(1)} %slices.5.refs_0_), channel_id=1, source_target_pairs={{0,4},{4,0},{8,12},{12,8},{1,5},{5,1},{9,13},{13,9},{2,6},{6,2},{1... | collective-permute-start | bytes 1179656 | tf_op jit(solution)/shard_map/ppermute | solution.py:84
  20.8 14.5 %collective-permute-start.7 = (bf16[3,1,128,512]{3,2,1,0:T(8,128)(2,1)S(1)}, bf16[3,1,128,512]{3,2,1,0:T(8,128)(2,1)S(1)}, u32[]{:S(2)}, u32[]{:S(2)}) collective-permute-start(bf16[3,1,128,512]{3,2,1,0:T(8,128)(2,1)S(1)} %get-tuple-element.49), channel_id=1, source_target_pairs={{0,8},{4,12},{8,0},{12,4},{1,9},{5,13},{9,1},{13,5},{2,10},{6,14},... | collective-permute-start | bytes 1179656 | tf_op jit(solution)/shard_map/ppermute | solution.py:80
  22.7 13.0 %collective-permute-start.5 = (bf16[3,1,128,512]{3,2,1,0:T(8,128)(2,1)S(1)}, bf16[3,1,128,512]{3,2,1,0:T(8,128)(2,1)S(1)}, u32[]{:S(2)}, u32[]{:S(2)}) collective-permute-start(bf16[3,1,128,512]{3,2,1,0:T(8,128)(2,1)S(1)} %collective-permute-done.3.refs_1_), channel_id=1, source_target_pairs={{0,4},{4,0},{8,12},{12,8},{1,5},{5,1},{9,13},{13,9},{2,6},{6,2},{1... | collective-permute-start | bytes 1179656 | tf_op jit(solution)/shard_map/ppermute | solution.py:84
  22.8 12.9 %collective-permute-start.8 = (bf16[3,1,128,512]{3,2,1,0:T(8,128)(2,1)S(1)}, bf16[3,1,128,512]{3,2,1,0:T(8,128)(2,1)S(1)}, u32[]{:S(2)}, u32[]{:S(2)}) collective-permute-start(bf16[3,1,128,512]{3,2,1,0:T(8,128)(2,1)S(1)} %slices.4), channel_id=1, source_target_pairs={{16,0},{0,16},{17,1},{1,17},{18,2},{2,18},{19,3},{3,19},{20,4},{4,... | collective-permute-start | bytes 1179656 | tf_op jit(solution)/shard_map/ppermute | solution.py:91
  24.3 10.1 %collective-permute-start.6 = (f32[3,8,128]{2,1,0:T(8,128)S(1)}, f32[3,8,128]{2,1,0:T(8,128)S(1)}, u32[]{:S(2)}, u32[]{:S(2)}) collective-permute-start(f32[3,8,128]{2,1,0:T(8,128)S(1)} %get-tuple-element.69.refs_1_), channel_id=1, source_target_pairs={{0,16},{16,0},{1,17},{17,1},{2,18},{18,2},{3,19},{19,3},{4,20},{20... | collective-permute-start | bytes 36872 | tf_op jit(solution)/shard_map/ppermute | solution.py:279
  34.4 10.6 %collective-permute-start.12 = (bf16[3,1,128,512]{3,2,1,0:T(8,128)(2,1)S(1)}, bf16[3,1,128,512]{3,2,1,0:T(8,128)(2,1)S(1)}, u32[]{:S(2)}, u32[]{:S(2)}) collective-permute-start(bf16[3,1,128,512]{3,2,1,0:T(8,128)(2,1)S(1)} %mix.2), channel_id=1, source_target_pairs={{0,8},{4,12},{8,0},{12,4},{1,9},{5,13},{9,1},{13,5},{2,10},{6,14},... | collective-permute-start | bytes 1179656 | tf_op jit(solution)/shard_map/ppermute | solution.py:80
  36.1 8.9 %collective-permute-start.9 = (bf16[3,1,128,512]{3,2,1,0:T(8,128)(2,1)S(1)}, bf16[3,1,128,512]{3,2,1,0:T(8,128)(2,1)S(1)}, u32[]{:S(2)}, u32[]{:S(2)}) collective-permute-start(bf16[3,1,128,512]{3,2,1,0:T(8,128)(2,1)S(1)} %mix.3.refs_4_), channel_id=1, source_target_pairs={{0,4},{4,0},{8,12},{12,8},{1,5},{5,1},{9,13},{13,9},{2,6},{6,2},{1... | collective-permute-start | bytes 1179656 | tf_op jit(solution)/shard_map/ppermute | solution.py:84
  36.2 8.8 %collective-permute-start.10 = (bf16[2,1,128,512]{3,2,1,0:T(8,128)(2,1)S(1)}, bf16[2,1,128,512]{3,2,1,0:T(8,128)(2,1)S(1)}, u32[]{:S(2)}, u32[]{:S(2)}) collective-permute-start(bf16[2,1,128,512]{3,2,1,0:T(8,128)(2,1)S(1)} %get-tuple-element.65), channel_id=1, source_target_pairs={{16,0},{0,16},{17,1},{1,17},{18,2},{2,18},{19,3},{3,19},{20,4},{4,... | collective-permute-start | bytes 786440 | tf_op jit(solution)/shard_map/ppermute | solution.py:91
  45.0 2.8 %collective-permute-start.13 = (bf16[3,1,128,512]{3,2,1,0:T(8,128)(2,1)S(1)}, bf16[3,1,128,512]{3,2,1,0:T(8,128)(2,1)S(1)}, u32[]{:S(2)}, u32[]{:S(2)}) collective-permute-start(bf16[3,1,128,512]{3,2,1,0:T(8,128)(2,1)S(1)} %collective-permute-done.12.refs_5_), channel_id=1, source_target_pairs={{0,4},{4,0},{8,12},{12,8},{1,5},{5,1},{9,13},{13,9},{2,6},{6,2},{1... | collective-permute-start | bytes 1179656 | tf_op jit(solution)/shard_map/ppermute | solution.py:84
  45.3 2.1 %collective-permute-start.11 = (bf16[2,1,128,512]{3,2,1,0:T(8,128)(2,1)S(1)}, bf16[2,1,128,512]{3,2,1,0:T(8,128)(2,1)S(1)}, u32[]{:S(2)}, u32[]{:S(2)}) collective-permute-start(bf16[2,1,128,512]{3,2,1,0:T(8,128)(2,1)S(1)} %add_partial.3.refs_4_), channel_id=1, source_target_pairs={{0,4},{4,0},{8,12},{12,8},{1,5},{5,1},{9,13},{13,9},{2,6},{6,2},{1... | collective-permute-start | bytes 786440 | tf_op jit(solution)/shard_map/ppermute | solution.py:84
  45.8 8.3 %collective-permute-start.15 = (bf16[2,1,128,512]{3,2,1,0:T(8,128)(2,1)S(1)}, bf16[2,1,128,512]{3,2,1,0:T(8,128)(2,1)S(1)}, u32[]{:S(2)}, u32[]{:S(2)}) collective-permute-start(bf16[2,1,128,512]{3,2,1,0:T(8,128)(2,1)S(1)} %get-tuple-element.66), channel_id=1, source_target_pairs={{16,0},{0,16},{17,1},{1,17},{18,2},{2,18},{19,3},{3,19},{20,4},{4,... | collective-permute-start | bytes 786440 | tf_op jit(solution)/shard_map/ppermute | solution.py:91
  54.3 2.7 %collective-permute-start.16 = (bf16[2,1,128,512]{3,2,1,0:T(8,128)(2,1)S(1)}, bf16[2,1,128,512]{3,2,1,0:T(8,128)(2,1)S(1)}, u32[]{:S(2)}, u32[]{:S(2)}) collective-permute-start(bf16[2,1,128,512]{3,2,1,0:T(8,128)(2,1)S(1)} %add_partial.4.refs_4_), channel_id=1, source_target_pairs={{0,4},{4,0},{8,12},{12,8},{1,5},{5,1},{9,13},{13,9},{2,6},{6,2},{1... | collective-permute-start | bytes 786440 | tf_op jit(solution)/shard_map/ppermute | solution.py:84
  54.4 8.7 %collective-permute-start.17 = (bf16[2,1,128,512]{3,2,1,0:T(8,128)(2,1)S(1)}, bf16[2,1,128,512]{3,2,1,0:T(8,128)(2,1)S(1)}, u32[]{:S(2)}, u32[]{:S(2)}) collective-permute-start(bf16[2,1,128,512]{3,2,1,0:T(8,128)(2,1)S(1)} %get-tuple-element.67), channel_id=1, source_target_pairs={{16,0},{0,16},{17,1},{1,17},{18,2},{2,18},{19,3},{3,19},{20,4},{4,... | collective-permute-start | bytes 786440 | tf_op jit(solution)/shard_map/ppermute | solution.py:91
  56.0 18.1 %collective-permute-start.14 = (bf16[3,1,128,512]{3,2,1,0:T(8,128)(2,1)S(1)}, bf16[3,1,128,512]{3,2,1,0:T(8,128)(2,1)S(1)}, u32[]{:S(2)}, u32[]{:S(2)}) collective-permute-start(bf16[3,1,128,512]{3,2,1,0:T(8,128)(2,1)S(1)} %get-tuple-element.78), channel_id=1, source_target_pairs={{0,8},{4,12},{8,0},{12,4},{1,9},{5,13},{9,1},{13,5},{2,10},{6,14},... | collective-permute-start | bytes 1179656 | tf_op jit(solution)/shard_map/ppermute | solution.py:80
  63.4 2.2 %collective-permute-start.18 = (bf16[2,1,128,512]{3,2,1,0:T(8,128)(2,1)S(1)}, bf16[2,1,128,512]{3,2,1,0:T(8,128)(2,1)S(1)}, u32[]{:S(2)}, u32[]{:S(2)}) collective-permute-start(bf16[2,1,128,512]{3,2,1,0:T(8,128)(2,1)S(1)} %add_partial.5.refs_4_), channel_id=1, source_target_pairs={{0,4},{4,0},{8,12},{12,8},{1,5},{5,1},{9,13},{13,9},{2,6},{6,2},{1... | collective-permute-start | bytes 786440 | tf_op jit(solution)/shard_map/ppermute | solution.py:84
  63.4 7.1 %collective-permute-start.21 = (bf16[1,1,128,512]{3,2,1,0:T(8,128)(2,1)S(1)}, bf16[1,1,128,512]{3,2,1,0:T(8,128)(2,1)S(1)}, u32[]{:S(2)}, u32[]{:S(2)}) collective-permute-start(bf16[1,1,128,512]{3,2,1,0:T(8,128)(2,1)S(1)} %get-tuple-element.72), channel_id=1, source_target_pairs={{0,8},{4,12},{8,0},{12,4},{1,9},{5,13},{9,1},{13,5},{2,10},{6,14},... | collective-permute-start | bytes 393224 | tf_op jit(solution)/shard_map/ppermute | solution.py:80
  64.5 8.8 %collective-permute-start.20 = (bf16[1,1,128,512]{3,2,1,0:T(8,128)(2,1)S(1)}, bf16[1,1,128,512]{3,2,1,0:T(8,128)(2,1)S(1)}, u32[]{:S(2)}, u32[]{:S(2)}) collective-permute-start(bf16[1,1,128,512]{3,2,1,0:T(8,128)(2,1)S(1)} %get-tuple-element.81), channel_id=1, source_target_pairs={{0,8},{4,12},{8,0},{12,4},{1,9},{5,13},{9,1},{13,5},{2,10},{6,14},... | collective-permute-start | bytes 393224 | tf_op jit(solution)/shard_map/ppermute | solution.py:80
  66.1 9.6 %collective-permute-start.19 = (bf16[1,1,128,512]{3,2,1,0:T(8,128)(2,1)S(1)}, bf16[1,1,128,512]{3,2,1,0:T(8,128)(2,1)S(1)}, u32[]{:S(2)}, u32[]{:S(2)}) collective-permute-start(bf16[1,1,128,512]{3,2,1,0:T(8,128)(2,1)S(1)} %get-tuple-element.84), channel_id=1, source_target_pairs={{0,8},{4,12},{8,0},{12,4},{1,9},{5,13},{9,1},{13,5},{2,10},{6,14},... | collective-permute-start | bytes 393224 | tf_op jit(solution)/shard_map/ppermute | solution.py:80

commit v7 on v6

v7 whole, which is shorter than its diff:
```python
import math

import jax
import jax.numpy as jnp
from jax import lax
from jax.experimental import pallas as pl
from jax.experimental.pallas import tpu as pltpu
from jax.sharding import PartitionSpec as P

MAXOFF = 9
BF16 = jnp.bfloat16
STEP = 16
LANES = 128
WHOLE = pl.BlockSpec(memory_space=pltpu.VMEM)
PARAMS = pltpu.CompilerParams(vmem_limit_bytes=12 * 1024 * 1024)
COST = pl.CostEstimate(flops=1, bytes_accessed=1, transcendentals=0)


def call(kernel, outs, name, *args):
    outs = [x if isinstance(x, jax.ShapeDtypeStruct) else jax.ShapeDtypeStruct(x, BF16) for x in outs]
    return pl.pallas_call(
        kernel,
        in_specs=[WHOLE] * len(args),
        out_specs=[WHOLE] * len(outs),
        out_shape=outs,
        compiler_params=PARAMS,
        cost_estimate=COST,
        name=name,
    )(*args)


def after(xs, *earlier):
    return lax.optimization_barrier((tuple(xs), earlier))[0]


def chunks(rows, body):
    @pl.loop(0, rows // STEP, unroll=math.gcd(rows // STEP, 4))
    def _(i):
        body(pl.ds(pl.multiple_of(i * STEP, STEP), STEP))


def weighted(tables, energies, load):
    totals = [None] * len(energies)
    for t, table in enumerate(tables):
        for m in range(table.shape[0]):
            g = load(t, m).astype(jnp.float32)
            for i, n in enumerate(energies):
                row = table[m, n : n + 1, :]
                term = jnp.concatenate([row] * (g.shape[1] // LANES), axis=1) * g
                totals[i] = term if totals[i] is None else totals[i] + term
    return totals


def solution(mesh):
    en, ph = mesh.shape["en"], mesh.shape["ph"]

    def on_device(lesser_in, greater_in, inverse, offsets, couplings):
        e, nb, r, o = lesser_in.shape
        held = offsets.shape[1]
        owners = math.gcd(nb, ph)
        lanes = ph // owners
        owned = nb // owners
        pieces = ph
        others = range(1, owners)
        reach = (MAXOFF + e - 1) // e
        shifts = [t for t in range(1, en) if t <= reach or en - t <= reach]
        block = (e, owned, r, o)
        tile = -(-e // 8) * 8
        tail = -(-4 * held // 16) * 16

        def owner_at(d):
            return lax.rem(lax.div(lax.axis_index("ph"), lanes) + d, owners)

        def place_of(j):
            at = lax.axis_index("ph")
            back = lax.rem(lax.div(at, lanes) + owners - j % owners, owners)
            return back * lanes + lax.rem(lax.rem(at, lanes) + lanes - j // owners, lanes)

        def to_owner(x, d):
            pairs = [(p, (p // lanes + d) % owners * lanes + p % lanes) for p in range(ph)]
            return lax.ppermute(x, "ph", pairs)

        def to_lanes(x):
            return [
                lax.ppermute(
                    x, "ph", [(p, p // lanes * lanes + (p % lanes + q) % lanes) for p in range(ph)]
                )
                for q in range(1, lanes)
            ]

        def from_energy(x, t):
            return lax.ppermute(x, "en", [((i + t) % en, i) for i in range(en)])

        def first(offsets_ref, couplings_ref, lesser_ref, greater_ref, inverse_ref, *refs):
            outs, (offsets_at, couplings_at, sems) = refs[:-3], refs[-3:]
            leads, inverses, lessers = (outs[i :: 3][: owners - 1] for i in range(3))
            copies = [(offsets_ref, offsets_at), (couplings_ref, couplings_at)]
            for i, d in enumerate(others):
                blocks = pl.ds(owner_at(d) * owned, owned)
                for n in range(e):
                    for b in range(owned):
                        to = leads[i].at[pl.ds((n * owned + b) * r, r)]
                        copies.append((greater_ref.at[n, owner_at(d) * owned + b], to))
                copies.append((lesser_ref.at[:, blocks], lessers[i]))
                copies.append((inverse_ref.at[:, blocks], inverses[i]))
            own = pl.ds(owner_at(0) * owned, owned)
            copies += [(inverse_ref.at[:, own], outs[-2]), (lesser_ref.at[:, own], outs[-1])]
            copies = [pltpu.make_async_copy(x, y, sems.at[i]) for i, (x, y) in enumerate(copies)]
            for copy in copies:
                copy.start()
            for copy in copies[:2]:
                copy.wait()
            rest = couplings_at[...]
            parts = [offsets_at[...].astype(jnp.float32)]
            for _ in range(3):
                parts.append(rest.astype(BF16).astype(jnp.float32))
                rest = rest - parts[-1]
            row = lax.broadcasted_iota(jnp.int32, (tail, e), 0)
            packed = jnp.zeros((tail, e), jnp.float32)
            for i, x in enumerate(parts):
                for k in range(held):
                    packed = jnp.where(row == i * held + k, x[k : k + 1, :], packed)
            packed = jnp.concatenate([packed, jnp.zeros((tail, LANES - e), jnp.float32)], axis=1)
            for out in leads:
                out[e * owned * r :, :LANES] = packed.astype(BF16)
                out[e * owned * r :, LANES:] = jnp.zeros((tail, o - LANES), BF16)
            for copy in copies[2:]:
                copy.wait()

        def join(*refs):
            for d in range(owners):
                refs[-1][d] = refs[d][e * owned * r :, :LANES]

        def from_hbm(kernel, outs, name, scratch, *args):
            far = pl.BlockSpec(memory_space=pltpu.HBM)
            return pl.pallas_call(
                kernel,
                in_specs=[far] * len(args),
                out_specs=[WHOLE] * len(outs),
                out_shape=[jax.ShapeDtypeStruct(x, BF16) for x in outs],
                scratch_shapes=scratch,
                compiler_params=PARAMS,
                cost_estimate=COST,
                name=name,
            )(*args)

        def weights(*refs):
            ins, outs = refs[:lanes], refs[lanes:]
            at = lax.axis_index("en")
            row = lax.broadcasted_iota(jnp.int32, (tile, LANES), 0)
            lane = lax.broadcasted_iota(jnp.int32, (tile, LANES), 1)
            pairs = []
            for ref in ins:
                for d in range(owners):
                    x = ref[d].astype(jnp.float32)
                    for k in range(held):
                        shift, *terms = [x[i * held + k : i * held + k + 1, :] for i in range(4)]
                        pairs.append((shift, terms[0] + terms[1] + terms[2]))
            for i, t in enumerate([0] + shifts):
                away = (lax.rem(at + t, en) - at) * e
                for m in range(e):
                    apart = (away + m - lane[:1]).astype(jnp.float32)
                    total = jnp.zeros((1, LANES), jnp.float32)
                    for shift, coupling in pairs:
                        total += jnp.where(shift == apart, coupling, 0.0)
                    spread = jnp.where(row == lane, jnp.broadcast_to(total, (tile, LANES)), 0.0)
                    outs[i][m] = jnp.broadcast_to(
                        jnp.sum(spread, axis=1, keepdims=True), (tile, LANES)
                    )

        def mix(tables, received, d, groups, earlier):
            def kernel(*refs):
                table_refs, refs = refs[: len(tables)], refs[len(tables) :]
                ins, outs = refs[: 1 + len(received)], refs[1 + len(received) :]
                for b in range(owned):
                    at_block = owner_at(d) * owned + b

                    def body(at):
                        totals = weighted(
                            table_refs, range(e), lambda t, m: ins[t][m, b if t else at_block, at, :]
                        )
                        for out, group in zip(outs, groups):
                            for i, n in enumerate(group):
                                out[i, b, at, :] = totals[n].astype(BF16)

                    chunks(r, body)

            shapes = [(len(group),) + block[1:] for group in groups]
            return call(kernel, shapes, "mix", *after(tables, *earlier), lesser_in, *received)

        def greater_at(refs, m, d, b, at):
            if not d:
                return refs[0][m, owner_at(0) * owned + b, at, :]
            return refs[d][pl.ds(pl.multiple_of((m * owned + b) * r + at.start, STEP), STEP), :]

        def partial_sums(table, rows, groups, earlier):
            def kernel(table_ref, *refs):
                for d in range(owners):
                    for b in range(owned):

                        def body(at):
                            totals = weighted(
                                [table_ref], range(e), lambda t, m: greater_at(refs, m, d, b, at)
                            )
                            for out, group in zip(refs[owners:], groups):
                                for i, n in enumerate(group):
                                    out[i, d, b, at, :] = totals[n].astype(BF16)

                        chunks(r, body)

            (table,) = after([table], *earlier)
            shapes = [(len(group), owners) + block[1:] for group in groups]
            return call(kernel, shapes, "partial_sums", table, greater_in, *rows)

        def add_partial(group, table, rows, received, earlier):
            def kernel(table_ref, *refs):
                for d in range(owners):
                    for b in range(owned):

                        def body(at):
                            totals = weighted(
                                [table_ref], group, lambda t, m: greater_at(refs, m, d, b, at)
                            )
                            for i in range(len(group)):
                                for ref in refs[owners:-owners]:
                                    totals[i] += ref[i, d, b, at, :].astype(jnp.float32)
                                refs[d - owners][i, b, at, :] = totals[i].astype(BF16)

                        chunks(r, body)

            (table,) = after([table], *earlier)
            shape = (len(group),) + block[1:]
            return call(kernel, [shape] * owners, "add_partial", table, greater_in, *rows, *received)

        def product(jobs, earlier):
            arrays = []
            for job in jobs:
                for x, _ in [*job[0], *job[1]]:
                    if not any(x is y for y in arrays):
                        arrays.append(x)
            where = {id(x): i for i, x in enumerate(arrays)}

            def kernel(*refs):
                outs = refs[-owners:]
                spans = [pl.ds(pl.multiple_of(place_of(j) * r, r), r) for j in range(pieces)]
                for k, job in enumerate(jobs):
                    a_in, s_in = ([(refs[where[id(x)]], index) for x, index in part] for part in job)
                    for b in range(owned):
                        left = jnp.concatenate(
                            [
                                jnp.concatenate([a[(*index, b, slice(None), at)] for at in spans], axis=1)
                                for a, index in a_in[:owners]
                            ],
                            axis=0,
                        )
                        right = jnp.concatenate([x[(*index, b)] for x, index in s_in], axis=0)
                        half = jnp.dot(left, right, preferred_element_type=jnp.float32).astype(BF16)
                        full = lax.dot_general(
                            half,
                            jnp.concatenate([a[(*index, b)] for a, index in a_in], axis=0),
                            (((1,), (1,)), ((), ())),
                            preferred_element_type=jnp.float32,
                        ).astype(BF16)
                        for i in range(owners):
                            for j, at in enumerate(spans):
                                outs[i][k, b, :, at] = full[i * r : (i + 1) * r, j * r : (j + 1) * r]

            shape = (len(jobs),) + block[1:]
            return call(kernel, [shape] * owners, "product", *after(arrays, *earlier))

        def back_to_rows(outs):
            return [outs[0]] + [to_owner(outs[d], owners - d) for d in others]

        def place(result, parts, earlier):
            arrays = []
            for _, _, x, _, _ in parts:
                if not any(x is y for y in arrays):
                    arrays.append(x)
            where = {id(x): i for i, x in enumerate(arrays)}

            def kernel(*refs):
                sems, out = refs[-1], refs[-2]
                copies = [
                    pltpu.make_async_copy(
                        refs[where[id(x)]].at[k],
                        out.at[n, pl.ds(owner_at(d) * owned, owned)],
                        sems.at[i],
                    )
                    for i, (n, d, x, k, _) in enumerate(parts)
                ]
                for copy in copies:
                    copy.start()
                for copy in copies:
                    copy.wait()

            far = pl.BlockSpec(memory_space=pltpu.HBM)
            return pl.pallas_call(
                kernel,
                in_specs=[WHOLE] * len(arrays) + [far] * (result is not None),
                out_specs=far,
                out_shape=jax.ShapeDtypeStruct((e, nb, r, o), BF16),
                scratch_shapes=[pltpu.SemaphoreType.DMA((len(parts),))],
                input_output_aliases={} if result is None else {len(arrays): 0},
                compiler_params=PARAMS,
                cost_estimate=COST,
                name="place",
            )(*after(arrays, *earlier), *([] if result is None else [result]))

        def in_order(own, rows, beside):
            return [own, *rows, *(x for q in range(lanes - 1) for x in [y[q] for y in beside])]

        def at(arrays, index):
            return [(x, index) for x in arrays]

        shapes = [(e * owned * r + tail, o), block, block]
        *parts, inverse_own, lesser_own = from_hbm(
            first,
            shapes * len(others) + [block] * 2,
            "first",
            [
                pltpu.VMEM((held, e), jnp.int32),
                pltpu.VMEM((held, e), jnp.float32),
                pltpu.SemaphoreType.DMA((4 + (e * owned + 2) * len(others),)),
            ],
            offsets.T,
            couplings.T,
            lesser_in,
            greater_in,
            inverse,
        )
        leads, inverses, lessers = (parts[i::3] for i in range(3))
        greater_rows = [to_owner(x, d) for d, x in zip(others, leads)]
        lesser_from = [[from_energy(x, t) for t in shifts] for x in lessers]
        inverse_rows = [to_owner(x, d) for d, x in zip(others, inverses)]

        (joined,) = call(join, [(owners, tail, LANES)], "join", leads[0], *greater_rows)
        tables = call(
            weights,
            [jax.ShapeDtypeStruct((e, tile, LANES), jnp.float32)] * (1 + len(shifts)),
            "weights",
            joined,
            *to_lanes(joined),
        )
        tables_for = [
            lax.ppermute(table, "en", [(i, (i + t) % en) for i in range(en)])
            for t, table in zip(shifts, tables[1:])
        ]
        lesser_own_from = [from_energy(lesser_own, t) for t in shifts]

        groups = [tuple(range(e - 1)), (e - 1,)] if e > 1 else [(0,)]
        singles = [(n,) for n in range(e)]
        lesser_rows = []
        last = []
        for d, came in zip(others, lesser_from):
            last = mix(tables, came, d, groups, last)
            lesser_rows.append([to_owner(x, d) for x in last])
        inverse_own_beside = to_lanes(inverse_own)
        last = [*last, *inverse_own_beside]
        received = [[] for _ in singles]
        for t, table in zip(shifts, tables_for):
            last = partial_sums(table, greater_rows, singles, last)
            for g, part in enumerate(last):
                received[g].append(from_energy(part, t))
        inverse_rows = list(after(inverse_rows, *last))
        inverse_rows_beside = [to_lanes(x) for x in inverse_rows]
        lesser_mixed = mix(tables, lesser_own_from, 0, groups, last)
        lesser_mixed_beside = [to_lanes(x) for x in lesser_mixed]
        last = lesser_mixed

        def find(groups, n):
            return next((g, group.index(n)) for g, group in enumerate(groups) if n in group)

        def inverse_at(n):
            beside = [at(inverse_own_beside, (n,)), *(at(x, (n,)) for x in inverse_rows_beside)]
            return in_order((inverse_own, (n,)), at(inverse_rows, (n,)), beside)

        def lesser_job(n):
            g, i = find(groups, n)
            h, k = find(groups, n)
            rows = [x[g] for x in lesser_rows]
            beside = [at(lesser_mixed_beside[h], (k,))] + [at(x[g], (i,)) for x in lesser_rows_beside]
            return inverse_at(n), in_order((lesser_mixed[h], (k,)), at(rows, (i,)), beside)

        lesser_rows_beside = [[to_lanes(x) for x in rows] for rows in lesser_rows]

        results = {"L": None, "G": None}
        waiting = {"L": [], "G": []}

        def put(kind, some, earlier):
            parts = [part for part in waiting[kind] if some(part)]
            waiting[kind] = [part for part in waiting[kind] if not some(part)]
            if parts:
                results[kind] = place(results[kind], parts, earlier)
                return [results[kind]]
            return earlier

        last = [*last, *[x[-1] for x in lesser_rows]]
        sigmas = {}
        steps = ["a0", "L0"]
        for n in range(1, e):
            steps.append(f"a{n}")
            if n == 2:
                steps.append("pL0")
            steps.append("L1+G0" if n == 1 else f"G{n - 1}")
        steps.append(f"G{e - 1}")
        for step in steps:
            if step[0] == "p":
                last = put(step[1], lambda part: len(step) < 3 or part[4] == int(step[2]), last)
                continue
            if step[0] == "a":
                g = int(step[1])
                group = singles[g]
                sigma = add_partial(group, tables[0], greater_rows, received[g], last)
                last = sigma
                sigmas[g] = (sigma, [to_lanes(x) for x in sigma])
                continue
            jobs, made = [], []
            for kind, g in step.split("+"):
                g = int(g)
                for i, n in enumerate(groups[g] if kind == "L" else singles[g]):
                    made.append((kind, n, g))
                    if kind == "L":
                        jobs.append(lesser_job(n))
                    else:
                        sigma, beside = sigmas[g]
                        beside = [at(x, (i,)) for x in beside]
                        jobs.append((inverse_at(n), in_order((sigma[0], (i,)), at(sigma[1:], (i,)), beside)))
            last = product(jobs, last)
            back = back_to_rows(last)
            for k, (kind, n, g) in enumerate(made):
                waiting[kind] += [(n, d, x, k, g) for d, x in enumerate(back)]
        last = put("L", lambda part: part[1] == 0, last)
        last = put("G", lambda part: part[1] == 0, last)
        for kind, g in [*(("L", g) for g in range(len(groups))), *(("G", n) for n in range(e))]:
            last = put(kind, lambda part: part[4] == g, last)
        lesser_out, greater_out = results["L"], results["G"]
        return lesser_out, greater_out

    block, coupled = P("en", "blk", "ph", None), P("en", "ph")
    return jax.shard_map(
        on_device,
        mesh=mesh,
        in_specs=(block, block, block, coupled, coupled),
        out_specs=(block, block),
        check_vma=False,
    )
```

time: 76.6 us -> 61.9 us (0.81)
  waiting for transfers between devices: 43 us -> 26.3 us
  Pallas kernels: 8.55 us -> 10.4 us
  local copies, waits for them, and re-layouts: 3.15 us -> 4.09 us
  starting transfers between devices: 20.8 us -> 20 us
    ppermute x5, waiting for transfers between devices: 18.7 us -> 4.66 us  [from_energy(): return lax.ppermute(x, 'en', [((i + t) % en, i) for i in range(en)])]
    ppermute x1, waiting for transfers between devices: 9.6 us -> 3.67 us  [on_device(): lax.ppermute(table, 'en', [(i, (i + t) % en) for i in range(en)])]
    pallas_call x5 -> x8, Pallas kernels: 3.7 us -> 5.78 us  [the longest x7 4.93 us: place(): pl.pallas_call(kernel, in_specs=[WHOLE] * len(arrays) + [far] * (result i...]
    ppermute x5, starting transfers between devices: 7.78 us -> 5.88 us  [from_energy(): return lax.ppermute(x, 'en', [((i + t) % en, i) for i in range(en)])]
    ppermute x8 -> x13, waiting for transfers between devices: 0.02 us -> 1.64 us  [to_lanes(): lax.ppermute(x, 'ph', [(p, p // lanes * lanes + (p % lanes + q) % lanes)...]
    ppermute x8, waiting for transfers between devices: 14.7 us -> 16.3 us  [to_owner(): return lax.ppermute(x, 'ph', pairs)]
    ppermute x1, starting transfers between devices: 0.53 us -> 1.49 us  [on_device(): lax.ppermute(table, 'en', [(i, (i + t) % en) for i in range(en)])]
    unnamed x14, local copies, waits for them, and re-layouts: 3.15 us -> 4.09 us
  transfers between devices with their start and end apart: 22 -> 27, of which waited for: 8 -> 13; matrix products, arithmetic and copies ran while one was open for 0% -> 0% of each run, Pallas kernels for 10% -> 14%
where the time goes in v7:
time: 61.9 us; the launch traced here: 61.7 us
  waiting for transfers between devices  26.3 us (42%)
  starting transfers between devices  20 us (32%)
  Pallas kernels  10.4 us (17%)
  local copies, waits for them, and re-layouts  4.09 us (7%)
  between operations  0.89 us (1%)
    ppermute x8, waiting for transfers between devices, to_owner(): return lax.ppermute(x, 'ph', pairs)  16.3 us
    ppermute x8, starting transfers between devices, to_owner(): return lax.ppermute(x, 'ph', pairs)  10.7 us
    ppermute x5, starting transfers between devices, from_energy(): return lax.ppermute(x, 'en', [((i + t) % en, i) for i in range(en)])  5.88 us
    pallas_call x7, Pallas kernels, place(): pl.pallas_call(kernel, in_specs=[WHOLE] * len(arrays) + [far] * (result i...  4.93 us
    pallas_call x12, Pallas kernels, call(): pl.pallas_call(kernel, in_specs=[WHOLE] * len(args), out_specs=[WHOLE] *...  4.66 us
    ppermute x5, waiting for transfers between devices, from_energy(): return lax.ppermute(x, 'en', [((i + t) % en, i) for i in range(en)])  4.66 us
    unnamed x14, local copies, waits for them, and re-layouts  4.09 us
    ppermute x1, waiting for transfers between devices, on_device(): lax.ppermute(table, 'en', [(i, (i + t) % en) for i in range(en)])  3.67 us
  transfers between devices with their start and end apart: 27, of which 13 were waited for; matrix products, arithmetic and copies ran while one was open for 0% of the time, Pallas kernels for 14%

profile of v7, /device:TPU:0, one launch (start us, length us, event | category | flops | bytes accessed | tf_op | source)
XLA Modules:
  0.0 61.7 jit_solution(2347400854138358717)
XLA Ops:
  0.7 0.7 %copy-done.6 = f32[3,2]{0,1:T(2,128)S(1)} copy-done((f32[3,2]{0,1:T(2,128)S(1)}, f32[3,2]{0,1:T(2,128)}, u32[]{:S(2)}) %copy-start.6) | copy-done | bytes 48
  1.3 0.0 copy-done.5
  1.3 1.1 %copy-done = bf16[3,2,128,512]{3,2,1,0:T(8,128)(2,1)S(1)} copy-done((bf16[3,2,128,512]{3,2,1,0:T(8,128)(2,1)S(1)}, bf16[3,2,128,512]{3,2,1,0:T(8,128)(2,1)}, u32[]{:S(2)}) %copy-start) | copy-done | bytes 786456
  2.5 1.1 %copy-done.2 = bf16[3,2,128,512]{3,2,1,0:T(8,128)(2,1)S(1)} copy-done((bf16[3,2,128,512]{3,2,1,0:T(8,128)(2,1)S(1)}, bf16[3,2,128,512]{3,2,1,0:T(8,128)(2,1)}, u32[]{:S(2)}) %copy-start.2) | copy-done | bytes 786456
  3.6 1.1 %copy-done.4 = bf16[3,2,128,512]{3,2,1,0:T(8,128)(2,1)S(1)} copy-done((bf16[3,2,128,512]{3,2,1,0:T(8,128)(2,1)S(1)}, bf16[3,2,128,512]{3,2,1,0:T(8,128)(2,1)}, u32[]{:S(2)}) %copy-start.4) | copy-done | bytes 786456
  4.7 0.8 %first.1 = (bf16[400,512]{1,0:T(8,128)(2,1)S(1)}, bf16[3,1,128,512]{3,2,1,0:T(8,128)(2,1)S(1)}, bf16[3,1,128,512]{3,2,1,0:T(8,128)(2,1)S(1)}, bf16[3,1,128,512]{...) custom-call(s32[2,3]{1,0:T(2,128)S(1)} %bitcast.2, f32[2,3]{1,0:T(2,128)S(1)} %bitcast.3, ...), custom_call_target="tpu_custom_call" | custom-call | flops 1 | bytes 1 | tf_op jit(solution)/shard_map/first/pallas_call | solution.py:136
  5.6 0.0 copy-start.3
  5.6 3.0 %collective-permute-start.1 = (bf16[400,512]{1,0:T(8,128)(2,1)S(1)}, bf16[400,512]{1,0:T(8,128)(2,1)S(1)}, u32[]{:S(2)}, u32[]{:S(2)}) collective-permute-start(bf16[400,512]{1,0:T(8,128)(2,1)S(1)} %get-tuple-element.87.refs_0_), channel_id=1, source_target_pairs={{0,8},{4,12},{8,0},{12,4},{1,9},{5,13},{9,1},{13,5},{2,10},{6,14},... | collective-permute-start | bytes 1228808 | tf_op jit(solution)/shard_map/ppermute | solution.py:81
  8.6 1.5 %collective-permute-start.4 = (bf16[3,1,128,512]{3,2,1,0:T(8,128)(2,1)S(1)}, bf16[3,1,128,512]{3,2,1,0:T(8,128)(2,1)S(1)}, u32[]{:S(2)}, u32[]{:S(2)}) collective-permute-start(bf16[3,1,128,512]{3,2,1,0:T(8,128)(2,1)S(1)} %get-tuple-element.91), channel_id=1, source_target_pairs={{16,0},{0,16},{17,1},{1,17},{18,2},{2,18},{19,3},{3,19},{20,4},{4,... | collective-permute-start | bytes 1179656 | tf_op jit(solution)/shard_map/ppermute | solution.py:92
  10.1 0.0 collective-permute-start.5
  10.1 0.5 collective-permute-start
  10.6 0.1 collective-permute-start.7
  10.7 8.2 %collective-permute-done.1.refs_1_ = bf16[400,512]{1,0:T(8,128)(2,1)S(1)} collective-permute-done((bf16[400,512]{1,0:T(8,128)(2,1)S(1)}, bf16[400,512]{1,0:T(8,128)(2,1)S(1)}, u32[]{:S(2)}, u32[]{:S(2)}) %collective-permute-start.1) | collective-permute-done | bytes 409632 | tf_op jit(solution)/shard_map/ppermute | solution.py:81
  18.9 1.2 %collective-permute-done.2.refs_1_ = bf16[2,16,128]{2,1,0:T(8,128)(2,1)S(1)} collective-permute-done((bf16[2,16,128]{2,1,0:T(8,128)(2,1)S(1)}, bf16[2,16,128]{2,1,0:T(8,128)(2,1)S(1)}, u32[]{:S(2)}, u32[]{:S(2)}) %collective-permute-start.2) | collective-permute-done | bytes 8224 | tf_op jit(solution)/shard_map/ppermute | solution.py:85
  20.1 0.1 weights.1
  20.2 0.5 collective-permute-done.4.refs_3_
  20.7 0.4 mix.2
  21.0 1.7 %collective-permute-start.14 = (bf16[2,1,128,512]{3,2,1,0:T(8,128)(2,1)S(1)}, bf16[2,1,128,512]{3,2,1,0:T(8,128)(2,1)S(1)}, u32[]{:S(2)}, u32[]{:S(2)}) collective-permute-start(bf16[2,1,128,512]{3,2,1,0:T(8,128)(2,1)S(1)} %get-tuple-element.92), channel_id=1, source_target_pairs={{0,8},{4,12},{8,0},{12,4},{1,9},{5,13},{9,1},{13,5},{2,10},{6,14},... | collective-permute-start | bytes 786440 | tf_op jit(solution)/shard_map/ppermute | solution.py:81
  22.7 1.5 %collective-permute-start.3 = (f32[3,8,128]{2,1,0:T(8,128)S(1)}, f32[3,8,128]{2,1,0:T(8,128)S(1)}, u32[]{:S(2)}, u32[]{:S(2)}) collective-permute-start(f32[3,8,128]{2,1,0:T(8,128)S(1)} %get-tuple-element.101.refs_1_), channel_id=1, source_target_pairs={{0,16},{16,0},{1,17},{17,1},{2,18},{18,2},{3,19},{19,3},{4,20},{20... | collective-permute-start | bytes 36872 | tf_op jit(solution)/shard_map/ppermute | solution.py:345
  24.2 0.0 collective-permute-done.5.refs_2_
  24.2 3.7 %collective-permute-done.3.table_ref = f32[3,8,128]{2,1,0:T(8,128)S(1)} collective-permute-done((f32[3,8,128]{2,1,0:T(8,128)S(1)}, f32[3,8,128]{2,1,0:T(8,128)S(1)}, u32[]{:S(2)}, u32[]{:S(2)}) %collective-permute-start.3) | collective-permute-done | bytes 12320 | tf_op jit(solution)/shard_map/ppermute | solution.py:345
  27.9 0.4 partial_sums.1
  28.3 0.1 collective-permute-start.6
  28.4 1.6 %collective-permute-start.11 = (bf16[1,2,1,128,512]{4,3,2,1,0:T(8,128)(2,1)S(1)}, bf16[1,2,1,128,512]{4,3,2,1,0:T(8,128)(2,1)S(1)}, u32[]{:S(2)}, u32[]{:S(2)}) collective-permute-start(bf16[1,2,1,128,512]{4,3,2,1,0:T(8,128)(2,1)S(1)} %get-tuple-element.95), channel_id=1, source_target_pairs={{16,0},{0,16},{17,1},{1,17},{18,2},{2,18},{19,3},{3,19},{20,4},{4,... | collective-permute-start | bytes 786440 | tf_op jit(solution)/shard_map/ppermute | solution.py:92
  29.9 1.0 %collective-permute-start.8 = (bf16[1,1,128,512]{3,2,1,0:T(8,128)(2,1)S(1)}, bf16[1,1,128,512]{3,2,1,0:T(8,128)(2,1)S(1)}, u32[]{:S(2)}, u32[]{:S(2)}) collective-permute-start(bf16[1,1,128,512]{3,2,1,0:T(8,128)(2,1)S(1)} %get-tuple-element.93), channel_id=1, source_target_pairs={{0,8},{4,12},{8,0},{12,4},{1,9},{5,13},{9,1},{13,5},{2,10},{6,14},... | collective-permute-start | bytes 393224 | tf_op jit(solution)/shard_map/ppermute | solution.py:81
  30.9 0.4 mix.3
  31.3 0.1 collective-permute-start.15
  31.4 0.8 %collective-permute-done.14.refs_5_ = bf16[2,1,128,512]{3,2,1,0:T(8,128)(2,1)S(1)} collective-permute-done((bf16[2,1,128,512]{3,2,1,0:T(8,128)(2,1)S(1)}, bf16[2,1,128,512]{3,2,1,0:T(8,128)(2,1)S(1)}, u32[]{:S(2)}, u32[]{:S(2)}) %collective-permute-start.14) | collective-permute-done | bytes 262176 | tf_op jit(solution)/shard_map/ppermute | solution.py:81
  32.1 0.0 collective-permute-start.16
  32.1 3.3 %collective-permute-done.8.refs_5_ = bf16[1,1,128,512]{3,2,1,0:T(8,128)(2,1)S(1)} collective-permute-done((bf16[1,1,128,512]{3,2,1,0:T(8,128)(2,1)S(1)}, bf16[1,1,128,512]{3,2,1,0:T(8,128)(2,1)S(1)}, u32[]{:S(2)}, u32[]{:S(2)}) %collective-permute-start.8) | collective-permute-done | bytes 131104 | tf_op jit(solution)/shard_map/ppermute | solution.py:81
  35.5 1.2 %collective-permute-start.17 = (bf16[1,2,1,128,512]{4,3,2,1,0:T(8,128)(2,1)S(1)}, bf16[1,2,1,128,512]{4,3,2,1,0:T(8,128)(2,1)S(1)}, u32[]{:S(2)}, u32[]{:S(2)}) collective-permute-start(bf16[1,2,1,128,512]{4,3,2,1,0:T(8,128)(2,1)S(1)} %get-tuple-element.96), channel_id=1, source_target_pairs={{16,0},{0,16},{17,1},{1,17},{18,2},{2,18},{19,3},{3,19},{20,4},{4,... | collective-permute-start | bytes 786440 | tf_op jit(solution)/shard_map/ppermute | solution.py:92
  36.7 0.4 collective-permute-done.11.refs_2_
  37.1 0.0 collective-permute-start.9
  37.1 0.2 add_partial.3
  37.3 0.0 collective-permute-done.15.refs_6_
  37.3 1.6 %collective-permute-start.22 = (bf16[1,2,1,128,512]{4,3,2,1,0:T(8,128)(2,1)S(1)}, bf16[1,2,1,128,512]{4,3,2,1,0:T(8,128)(2,1)S(1)}, u32[]{:S(2)}, u32[]{:S(2)}) collective-permute-start(bf16[1,2,1,128,512]{4,3,2,1,0:T(8,128)(2,1)S(1)} %get-tuple-element.97), channel_id=1, source_target_pairs={{16,0},{0,16},{17,1},{1,17},{18,2},{2,18},{19,3},{3,19},{20,4},{4,... | collective-permute-start | bytes 786440 | tf_op jit(solution)/shard_map/ppermute | solution.py:92
  38.9 0.9 %product.4 = (bf16[2,1,128,512]{3,2,1,0:T(8,128)(2,1)S(1)}, bf16[2,1,128,512]{3,2,1,0:T(8,128)(2,1)S(1)}) custom-call(bf16[3,1,128,512]{3,2,1,0:T(8,128)(2,1)S(1)} %get-tuple-element.150.refs_0_, bf16[3,1,128,512]{3,2,1,0:T(8,128)(2,1)S(1)} %collective-permute-done.refs_1_, bf16[3,1,128,512]{3,2,1,0:T(8,128)(2,1)S(1)} %collective-permute-done.5.refs_2_, ...), custom_call_target="tpu_custom_call" | custom-call | flops 1 | bytes 1 | tf_op jit(solution)/shard_map/product/pallas_call | solution.py:21
  39.8 1.1 %collective-permute-start.21 = (bf16[2,1,128,512]{3,2,1,0:T(8,128)(2,1)S(1)}, bf16[2,1,128,512]{3,2,1,0:T(8,128)(2,1)S(1)}, u32[]{:S(2)}, u32[]{:S(2)}) collective-permute-start(bf16[2,1,128,512]{3,2,1,0:T(8,128)(2,1)S(1)} %get-tuple-element.117), channel_id=1, source_target_pairs={{0,8},{4,12},{8,0},{12,4},{1,9},{5,13},{9,1},{13,5},{2,10},{6,14},... | collective-permute-start | bytes 786440 | tf_op jit(solution)/shard_map/ppermute | solution.py:81
  40.9 0.5 collective-permute-start.12
  41.4 3.3 %collective-permute-done.17.refs_2_ = bf16[1,2,1,128,512]{4,3,2,1,0:T(8,128)(2,1)S(1)} collective-permute-done((bf16[1,2,1,128,512]{4,3,2,1,0:T(8,128)(2,1)S(1)}, bf16[1,2,1,128,512]{4,3,2,1,0:T(8,128)(2,1)S(1)}, u32[]{:S(2)}, u32[]{:S(2)}) %collective-permute-start.17) | collective-permute-done | bytes 262176 | tf_op jit(solution)/shard_map/ppermute | solution.py:92
  44.7 0.2 add_partial.4
  45.0 0.6 collective-permute-start.19
  45.5 0.1 collective-permute-start.20
  45.6 0.4 collective-permute-done.13.refs_11_
  46.1 0.9 %product.5 = (bf16[2,1,128,512]{3,2,1,0:T(8,128)(2,1)S(1)}, bf16[2,1,128,512]{3,2,1,0:T(8,128)(2,1)S(1)}) custom-call(bf16[3,1,128,512]{3,2,1,0:T(8,128)(2,1)S(1)} %get-tuple-element.150.refs_0_, bf16[3,1,128,512]{3,2,1,0:T(8,128)(2,1)S(1)} %collective-permute-done.refs_1_, bf16[3,1,128,512]{3,2,1,0:T(8,128)(2,1)S(1)} %collective-permute-done.5.refs_2_, ...), custom_call_target="tpu_custom_call" | custom-call | flops 1 | bytes 1 | tf_op jit(solution)/shard_map/product/pallas_call | solution.py:21
  46.9 1.3 %collective-permute-start.18 = (bf16[2,1,128,512]{3,2,1,0:T(8,128)(2,1)S(1)}, bf16[2,1,128,512]{3,2,1,0:T(8,128)(2,1)S(1)}, u32[]{:S(2)}, u32[]{:S(2)}) collective-permute-start(bf16[2,1,128,512]{3,2,1,0:T(8,128)(2,1)S(1)} %get-tuple-element.133), channel_id=1, source_target_pairs={{0,8},{4,12},{8,0},{12,4},{1,9},{5,13},{9,1},{13,5},{2,10},{6,14},... | collective-permute-start | bytes 786440 | tf_op jit(solution)/shard_map/ppermute | solution.py:81
  48.2 0.4 collective-permute-done.22.refs_2_
  48.6 0.2 add_partial.5
  48.9 0.1 collective-permute-start.23
  49.0 0.5 collective-permute-start.24
  49.5 0.8 %place.7.refs_1_ = bf16[3,2,128,512]{3,2,1,0:T(8,128)(2,1)} custom-call(bf16[2,1,128,512]{3,2,1,0:T(8,128)(2,1)S(1)} %get-tuple-element.138.refs_0_, bf16[2,1,128,512]{3,2,1,0:T(8,128)(2,1)S(1)} %collective-permute-done.21.refs_1_), custom_call_target="tpu_custom_call" | custom-call | flops 1 | bytes 1 | tf_op jit(solution)/shard_map/place/pallas_call | solution.py:297
  50.3 0.5 product.6
  50.8 1.5 %collective-permute-start.26 = (bf16[1,1,128,512]{3,2,1,0:T(8,128)(2,1)S(1)}, bf16[1,1,128,512]{3,2,1,0:T(8,128)(2,1)S(1)}, u32[]{:S(2)}, u32[]{:S(2)}) collective-permute-start(bf16[1,1,128,512]{3,2,1,0:T(8,128)(2,1)S(1)} %get-tuple-element.149), channel_id=1, source_target_pairs={{0,8},{4,12},{8,0},{12,4},{1,9},{5,13},{9,1},{13,5},{2,10},{6,14},... | collective-permute-start | bytes 393224 | tf_op jit(solution)/shard_map/ppermute | solution.py:81
  52.3 0.5 product.7
  52.9 0.7 %collective-permute-start.25 = (bf16[1,1,128,512]{3,2,1,0:T(8,128)(2,1)S(1)}, bf16[1,1,128,512]{3,2,1,0:T(8,128)(2,1)S(1)}, u32[]{:S(2)}, u32[]{:S(2)}) collective-permute-start(bf16[1,1,128,512]{3,2,1,0:T(8,128)(2,1)S(1)} %get-tuple-element.159), channel_id=1, source_target_pairs={{0,8},{4,12},{8,0},{12,4},{1,9},{5,13},{9,1},{13,5},{2,10},{6,14},... | collective-permute-start | bytes 393224 | tf_op jit(solution)/shard_map/ppermute | solution.py:81
  53.5 0.7 %place.8.refs_1_ = bf16[3,2,128,512]{3,2,1,0:T(8,128)(2,1)} custom-call(bf16[2,1,128,512]{3,2,1,0:T(8,128)(2,1)S(1)} %get-tuple-element.161.refs_0_, bf16[3,2,128,512]{3,2,1,0:T(8,128)(2,1)} %place.7.refs_1_), custom_call_target="tpu_custom_call", output_to_operand_aliasing={{}: (1, {})} | custom-call | flops 1 | bytes 1 | tf_op jit(solution)/shard_map/place/pallas_call | solution.py:297
  54.2 0.8 %place.9.refs_1_ = bf16[3,2,128,512]{3,2,1,0:T(8,128)(2,1)} custom-call(bf16[2,1,128,512]{3,2,1,0:T(8,128)(2,1)S(1)} %get-tuple-element.161.refs_0_, bf16[1,1,128,512]{3,2,1,0:T(8,128)(2,1)S(1)} %get-tuple-element.162.refs_1_, bf16[1,1,128,512]{3,2,1,0:T(8,128)(2,1)S(1)} %get-tuple-element.163.refs_2_), custom_call_target="tpu_custom_call" | custom-call | flops 1 | bytes 1 | tf_op jit(solution)/shard_map/place/pallas_call | solution.py:297
  55.0 1.2 %collective-permute-done.18.refs_0_ = bf16[2,1,128,512]{3,2,1,0:T(8,128)(2,1)S(1)} collective-permute-done((bf16[2,1,128,512]{3,2,1,0:T(8,128)(2,1)S(1)}, bf16[2,1,128,512]{3,2,1,0:T(8,128)(2,1)S(1)}, u32[]{:S(2)}, u32[]{:S(2)}) %collective-permute-start.18) | collective-permute-done | bytes 262176 | tf_op jit(solution)/shard_map/ppermute | solution.py:81
  56.2 0.7 %place.10 = bf16[3,2,128,512]{3,2,1,0:T(8,128)(2,1)} custom-call(bf16[2,1,128,512]{3,2,1,0:T(8,128)(2,1)S(1)} %collective-permute-done.18.refs_0_, bf16[3,2,128,512]{3,2,1,0:T(8,128)(2,1)} %place.8.refs_1_), custom_call_target="tpu_custom_call", output_to_operand_aliasing={{}: (1, {})} | custom-call | flops 1 | bytes 1 | tf_op jit(solution)/shard_map/place/pallas_call | solution.py:297
  56.8 0.7 %place.11.refs_1_ = bf16[3,2,128,512]{3,2,1,0:T(8,128)(2,1)} custom-call(bf16[2,1,128,512]{3,2,1,0:T(8,128)(2,1)S(1)} %collective-permute-done.18.refs_0_, bf16[3,2,128,512]{3,2,1,0:T(8,128)(2,1)} %place.9.refs_1_), custom_call_target="tpu_custom_call", output_to_operand_aliasing={{}: (1, {})} | custom-call | flops 1 | bytes 1 | tf_op jit(solution)/shard_map/place/pallas_call | solution.py:297
  57.5 1.4 %collective-permute-done.26.refs_0_ = bf16[1,1,128,512]{3,2,1,0:T(8,128)(2,1)S(1)} collective-permute-done((bf16[1,1,128,512]{3,2,1,0:T(8,128)(2,1)S(1)}, bf16[1,1,128,512]{3,2,1,0:T(8,128)(2,1)S(1)}, u32[]{:S(2)}, u32[]{:S(2)}) %collective-permute-start.26) | collective-permute-done | bytes 131104 | tf_op jit(solution)/shard_map/ppermute | solution.py:81
  59.0 0.7 %place.12.refs_1_ = bf16[3,2,128,512]{3,2,1,0:T(8,128)(2,1)} custom-call(bf16[1,1,128,512]{3,2,1,0:T(8,128)(2,1)S(1)} %collective-permute-done.26.refs_0_, bf16[3,2,128,512]{3,2,1,0:T(8,128)(2,1)} %place.11.refs_1_), custom_call_target="tpu_custom_call", output_to_operand_aliasing={{}: (1, {})} | custom-call | flops 1 | bytes 1 | tf_op jit(solution)/shard_map/place/pallas_call | solution.py:297
  59.6 1.4 %collective-permute-done.25.refs_0_ = bf16[1,1,128,512]{3,2,1,0:T(8,128)(2,1)S(1)} collective-permute-done((bf16[1,1,128,512]{3,2,1,0:T(8,128)(2,1)S(1)}, bf16[1,1,128,512]{3,2,1,0:T(8,128)(2,1)S(1)}, u32[]{:S(2)}, u32[]{:S(2)}) %collective-permute-start.25) | collective-permute-done | bytes 131104 | tf_op jit(solution)/shard_map/ppermute | solution.py:81
  61.0 0.7 %place.13 = bf16[3,2,128,512]{3,2,1,0:T(8,128)(2,1)} custom-call(bf16[1,1,128,512]{3,2,1,0:T(8,128)(2,1)S(1)} %collective-permute-done.25.refs_0_, bf16[3,2,128,512]{3,2,1,0:T(8,128)(2,1)} %place.12.refs_1_), custom_call_target="tpu_custom_call", output_to_operand_aliasing={{}: (1, {})} | custom-call | flops 1 | bytes 1 | tf_op jit(solution)/shard_map/place/pallas_call | solution.py:297
  (24 shorter events, 0.1 us)
Async XLA Ops:
  0.6 0.7 %copy-start.6 = (f32[3,2]{0,1:T(2,128)S(1)}, f32[3,2]{0,1:T(2,128)}, u32[]{:S(2)}) copy-start(f32[3,2]{0,1:T(2,128)} %param.9) | copy-start | bytes 76
  0.6 0.7 %copy-start.5 = (s32[3,2]{0,1:T(2,128)S(1)}, s32[3,2]{0,1:T(2,128)}, u32[]{:S(2)}) copy-start(s32[3,2]{0,1:T(2,128)} %param.8) | copy-start | bytes 76
  1.3 1.1 %copy-start = (bf16[3,2,128,512]{3,2,1,0:T(8,128)(2,1)S(1)}, bf16[3,2,128,512]{3,2,1,0:T(8,128)(2,1)}, u32[]{:S(2)}) copy-start(bf16[3,2,128,512]{3,2,1,0:T(8,128)(2,1)} %refs_0_.7) | copy-start | bytes 2359300
  2.5 1.1 %copy-start.2 = (bf16[3,2,128,512]{3,2,1,0:T(8,128)(2,1)S(1)}, bf16[3,2,128,512]{3,2,1,0:T(8,128)(2,1)}, u32[]{:S(2)}) copy-start(bf16[3,2,128,512]{3,2,1,0:T(8,128)(2,1)} %refs_2_.3) | copy-start | bytes 2359300
  3.6 1.1 %copy-start.4 = (bf16[3,2,128,512]{3,2,1,0:T(8,128)(2,1)S(1)}, bf16[3,2,128,512]{3,2,1,0:T(8,128)(2,1)}, u32[]{:S(2)}) copy-start(bf16[3,2,128,512]{3,2,1,0:T(8,128)(2,1)} %inverse_ref.1) | copy-start | bytes 2359300
  5.6 15.1 %copy-start.3 = (bf16[3,2,128,512]{3,2,1,0:T(8,128)(2,1)S(1)}, bf16[3,2,128,512]{3,2,1,0:T(8,128)(2,1)}, u32[]{:S(2)}) copy-start(bf16[3,2,128,512]{3,2,1,0:T(8,128)(2,1)} %refs_2_.3) | copy-start | bytes 2359300
  5.6 13.3 %collective-permute-start.1 = (bf16[400,512]{1,0:T(8,128)(2,1)S(1)}, bf16[400,512]{1,0:T(8,128)(2,1)S(1)}, u32[]{:S(2)}, u32[]{:S(2)}) collective-permute-start(bf16[400,512]{1,0:T(8,128)(2,1)S(1)} %get-tuple-element.87.refs_0_), channel_id=1, source_target_pairs={{0,8},{4,12},{8,0},{12,4},{1,9},{5,13},{9,1},{13,5},{2,10},{6,14},... | collective-permute-start | bytes 1228808 | tf_op jit(solution)/shard_map/ppermute | solution.py:81
  8.6 12.0 %collective-permute-start.4 = (bf16[3,1,128,512]{3,2,1,0:T(8,128)(2,1)S(1)}, bf16[3,1,128,512]{3,2,1,0:T(8,128)(2,1)S(1)}, u32[]{:S(2)}, u32[]{:S(2)}) collective-permute-start(bf16[3,1,128,512]{3,2,1,0:T(8,128)(2,1)S(1)} %get-tuple-element.91), channel_id=1, source_target_pairs={{16,0},{0,16},{17,1},{1,17},{18,2},{2,18},{19,3},{3,19},{20,4},{4,... | collective-permute-start | bytes 1179656 | tf_op jit(solution)/shard_map/ppermute | solution.py:92
  10.1 14.1 %collective-permute-start.5 = (bf16[3,1,128,512]{3,2,1,0:T(8,128)(2,1)S(1)}, bf16[3,1,128,512]{3,2,1,0:T(8,128)(2,1)S(1)}, u32[]{:S(2)}, u32[]{:S(2)}) collective-permute-start(bf16[3,1,128,512]{3,2,1,0:T(8,128)(2,1)S(1)} %get-tuple-element.150.refs_0_), channel_id=1, source_target_pairs={{0,4},{4,0},{8,12},{12,8},{1,5},{5,1},{9,13},{13,9},{2,6},{6,2},{1... | collective-permute-start | bytes 1179656 | tf_op jit(solution)/shard_map/ppermute | solution.py:85
  10.1 18.2 %collective-permute-start = (bf16[3,1,128,512]{3,2,1,0:T(8,128)(2,1)S(1)}, bf16[3,1,128,512]{3,2,1,0:T(8,128)(2,1)S(1)}, u32[]{:S(2)}, u32[]{:S(2)}) collective-permute-start(bf16[3,1,128,512]{3,2,1,0:T(8,128)(2,1)S(1)} %get-tuple-element.86), channel_id=1, source_target_pairs={{0,8},{4,12},{8,0},{12,4},{1,9},{5,13},{9,1},{13,5},{2,10},{6,14},... | collective-permute-start | bytes 1179656 | tf_op jit(solution)/shard_map/ppermute | solution.py:81
  10.6 20.3 %collective-permute-start.7 = (bf16[3,1,128,512]{3,2,1,0:T(8,128)(2,1)S(1)}, bf16[3,1,128,512]{3,2,1,0:T(8,128)(2,1)S(1)}, u32[]{:S(2)}, u32[]{:S(2)}) collective-permute-start(bf16[3,1,128,512]{3,2,1,0:T(8,128)(2,1)S(1)} %get-tuple-element.102), channel_id=1, source_target_pairs={{16,0},{0,16},{17,1},{1,17},{18,2},{2,18},{19,3},{3,19},{20,4},{4,... | collective-permute-start | bytes 1179656 | tf_op jit(solution)/shard_map/ppermute | solution.py:92
  18.9 9.0 %copy-start.1 = (bf16[3,2,128,512]{3,2,1,0:T(8,128)(2,1)S(1)}, bf16[3,2,128,512]{3,2,1,0:T(8,128)(2,1)}, u32[]{:S(2)}) copy-start(bf16[3,2,128,512]{3,2,1,0:T(8,128)(2,1)} %refs_0_.7) | copy-start | bytes 2359300
  18.9 1.2 %collective-permute-start.2 = (bf16[2,16,128]{2,1,0:T(8,128)(2,1)S(1)}, bf16[2,16,128]{2,1,0:T(8,128)(2,1)S(1)}, u32[]{:S(2)}, u32[]{:S(2)}) collective-permute-start(bf16[2,16,128]{2,1,0:T(8,128)(2,1)S(1)} %join.1.refs_0_), channel_id=1, source_target_pairs={{0,4},{4,0},{8,12},{12,8},{1,5},{5,1},{9,13},{13,9},{2,6},{6,2},{1... | collective-permute-start | bytes 24584 | tf_op jit(solution)/shard_map/ppermute | solution.py:85
  21.0 11.1 %collective-permute-start.14 = (bf16[2,1,128,512]{3,2,1,0:T(8,128)(2,1)S(1)}, bf16[2,1,128,512]{3,2,1,0:T(8,128)(2,1)S(1)}, u32[]{:S(2)}, u32[]{:S(2)}) collective-permute-start(bf16[2,1,128,512]{3,2,1,0:T(8,128)(2,1)S(1)} %get-tuple-element.92), channel_id=1, source_target_pairs={{0,8},{4,12},{8,0},{12,4},{1,9},{5,13},{9,1},{13,5},{2,10},{6,14},... | collective-permute-start | bytes 786440 | tf_op jit(solution)/shard_map/ppermute | solution.py:81
  22.7 5.2 %collective-permute-start.3 = (f32[3,8,128]{2,1,0:T(8,128)S(1)}, f32[3,8,128]{2,1,0:T(8,128)S(1)}, u32[]{:S(2)}, u32[]{:S(2)}) collective-permute-start(f32[3,8,128]{2,1,0:T(8,128)S(1)} %get-tuple-element.101.refs_1_), channel_id=1, source_target_pairs={{0,16},{16,0},{1,17},{17,1},{2,18},{18,2},{3,19},{19,3},{4,20},{20... | collective-permute-start | bytes 36872 | tf_op jit(solution)/shard_map/ppermute | solution.py:345
  28.3 10.6 %collective-permute-start.6 = (bf16[3,1,128,512]{3,2,1,0:T(8,128)(2,1)S(1)}, bf16[3,1,128,512]{3,2,1,0:T(8,128)(2,1)S(1)}, u32[]{:S(2)}, u32[]{:S(2)}) collective-permute-start(bf16[3,1,128,512]{3,2,1,0:T(8,128)(2,1)S(1)} %collective-permute-done.refs_1_), channel_id=1, source_target_pairs={{0,4},{4,0},{8,12},{12,8},{1,5},{5,1},{9,13},{13,9},{2,6},{6,2},{1... | collective-permute-start | bytes 1179656 | tf_op jit(solution)/shard_map/ppermute | solution.py:85
  28.4 8.7 %collective-permute-start.11 = (bf16[1,2,1,128,512]{4,3,2,1,0:T(8,128)(2,1)S(1)}, bf16[1,2,1,128,512]{4,3,2,1,0:T(8,128)(2,1)S(1)}, u32[]{:S(2)}, u32[]{:S(2)}) collective-permute-start(bf16[1,2,1,128,512]{4,3,2,1,0:T(8,128)(2,1)S(1)} %get-tuple-element.95), channel_id=1, source_target_pairs={{16,0},{0,16},{17,1},{1,17},{18,2},{2,18},{19,3},{3,19},{20,4},{4,... | collective-permute-start | bytes 786440 | tf_op jit(solution)/shard_map/ppermute | solution.py:92
  29.9 5.6 %collective-permute-start.8 = (bf16[1,1,128,512]{3,2,1,0:T(8,128)(2,1)S(1)}, bf16[1,1,128,512]{3,2,1,0:T(8,128)(2,1)S(1)}, u32[]{:S(2)}, u32[]{:S(2)}) collective-permute-start(bf16[1,1,128,512]{3,2,1,0:T(8,128)(2,1)S(1)} %get-tuple-element.93), channel_id=1, source_target_pairs={{0,8},{4,12},{8,0},{12,4},{1,9},{5,13},{9,1},{13,5},{2,10},{6,14},... | collective-permute-start | bytes 393224 | tf_op jit(solution)/shard_map/ppermute | solution.py:81
  31.3 6.0 %collective-permute-start.15 = (bf16[2,1,128,512]{3,2,1,0:T(8,128)(2,1)S(1)}, bf16[2,1,128,512]{3,2,1,0:T(8,128)(2,1)S(1)}, u32[]{:S(2)}, u32[]{:S(2)}) collective-permute-start(bf16[2,1,128,512]{3,2,1,0:T(8,128)(2,1)S(1)} %get-tuple-element.112.refs_4_), channel_id=1, source_target_pairs={{0,4},{4,0},{8,12},{12,8},{1,5},{5,1},{9,13},{13,9},{2,6},{6,2},{1... | collective-permute-start | bytes 786440 | tf_op jit(solution)/shard_map/ppermute | solution.py:85
  32.1 6.8 %collective-permute-start.16 = (bf16[2,1,128,512]{3,2,1,0:T(8,128)(2,1)S(1)}, bf16[2,1,128,512]{3,2,1,0:T(8,128)(2,1)S(1)}, u32[]{:S(2)}, u32[]{:S(2)}) collective-permute-start(bf16[2,1,128,512]{3,2,1,0:T(8,128)(2,1)S(1)} %collective-permute-done.14.refs_5_), channel_id=1, source_target_pairs={{0,4},{4,0},{8,12},{12,8},{1,5},{5,1},{9,13},{13,9},{2,6},{6,2},{1... | collective-permute-start | bytes 786440 | tf_op jit(solution)/shard_map/ppermute | solution.py:85
  35.5 9.2 %collective-permute-start.17 = (bf16[1,2,1,128,512]{4,3,2,1,0:T(8,128)(2,1)S(1)}, bf16[1,2,1,128,512]{4,3,2,1,0:T(8,128)(2,1)S(1)}, u32[]{:S(2)}, u32[]{:S(2)}) collective-permute-start(bf16[1,2,1,128,512]{4,3,2,1,0:T(8,128)(2,1)S(1)} %get-tuple-element.96), channel_id=1, source_target_pairs={{16,0},{0,16},{17,1},{1,17},{18,2},{2,18},{19,3},{3,19},{20,4},{4,... | collective-permute-start | bytes 786440 | tf_op jit(solution)/shard_map/ppermute | solution.py:92
  37.1 3.8 %collective-permute-start.9 = (bf16[1,1,128,512]{3,2,1,0:T(8,128)(2,1)S(1)}, bf16[1,1,128,512]{3,2,1,0:T(8,128)(2,1)S(1)}, u32[]{:S(2)}, u32[]{:S(2)}) collective-permute-start(bf16[1,1,128,512]{3,2,1,0:T(8,128)(2,1)S(1)} %get-tuple-element.125.refs_4_), channel_id=1, source_target_pairs={{0,4},{4,0},{8,12},{12,8},{1,5},{5,1},{9,13},{13,9},{2,6},{6,2},{1... | collective-permute-start | bytes 393224 | tf_op jit(solution)/shard_map/ppermute | solution.py:85
  37.3 11.3 %collective-permute-start.22 = (bf16[1,2,1,128,512]{4,3,2,1,0:T(8,128)(2,1)S(1)}, bf16[1,2,1,128,512]{4,3,2,1,0:T(8,128)(2,1)S(1)}, u32[]{:S(2)}, u32[]{:S(2)}) collective-permute-start(bf16[1,2,1,128,512]{4,3,2,1,0:T(8,128)(2,1)S(1)} %get-tuple-element.97), channel_id=1, source_target_pairs={{16,0},{0,16},{17,1},{1,17},{18,2},{2,18},{19,3},{3,19},{20,4},{4,... | collective-permute-start | bytes 786440 | tf_op jit(solution)/shard_map/ppermute | solution.py:92
  39.8 9.2 %collective-permute-start.21 = (bf16[2,1,128,512]{3,2,1,0:T(8,128)(2,1)S(1)}, bf16[2,1,128,512]{3,2,1,0:T(8,128)(2,1)S(1)}, u32[]{:S(2)}, u32[]{:S(2)}) collective-permute-start(bf16[2,1,128,512]{3,2,1,0:T(8,128)(2,1)S(1)} %get-tuple-element.117), channel_id=1, source_target_pairs={{0,8},{4,12},{8,0},{12,4},{1,9},{5,13},{9,1},{13,5},{2,10},{6,14},... | collective-permute-start | bytes 786440 | tf_op jit(solution)/shard_map/ppermute | solution.py:81
  40.9 4.1 %collective-permute-start.10 = (bf16[1,1,128,512]{3,2,1,0:T(8,128)(2,1)S(1)}, bf16[1,1,128,512]{3,2,1,0:T(8,128)(2,1)S(1)}, u32[]{:S(2)}, u32[]{:S(2)}) collective-permute-start(bf16[1,1,128,512]{3,2,1,0:T(8,128)(2,1)S(1)} %collective-permute-done.8.refs_5_), channel_id=1, source_target_pairs={{0,4},{4,0},{8,12},{12,8},{1,5},{5,1},{9,13},{13,9},{2,6},{6,2},{1... | collective-permute-start | bytes 393224 | tf_op jit(solution)/shard_map/ppermute | solution.py:85
  40.9 4.7 %collective-permute-start.12 = (bf16[1,1,128,512]{3,2,1,0:T(8,128)(2,1)S(1)}, bf16[1,1,128,512]{3,2,1,0:T(8,128)(2,1)S(1)}, u32[]{:S(2)}, u32[]{:S(2)}) collective-permute-start(bf16[1,1,128,512]{3,2,1,0:T(8,128)(2,1)S(1)} %get-tuple-element.129.refs_8_), channel_id=1, source_target_pairs={{0,4},{4,0},{8,12},{12,8},{1,5},{5,1},{9,13},{13,9},{2,6},{6,2},{1... | collective-permute-start | bytes 393224 | tf_op jit(solution)/shard_map/ppermute | solution.py:85
  44.7 1.3 %collective-permute-start.13 = (bf16[1,1,128,512]{3,2,1,0:T(8,128)(2,1)S(1)}, bf16[1,1,128,512]{3,2,1,0:T(8,128)(2,1)S(1)}, u32[]{:S(2)}, u32[]{:S(2)}) collective-permute-start(bf16[1,1,128,512]{3,2,1,0:T(8,128)(2,1)S(1)} %get-tuple-element.130.refs_9_), channel_id=1, source_target_pairs={{0,4},{4,0},{8,12},{12,8},{1,5},{5,1},{9,13},{13,9},{2,6},{6,2},{1... | collective-permute-start | bytes 393224 | tf_op jit(solution)/shard_map/ppermute | solution.py:85
  45.0 5.3 %collective-permute-start.19 = (bf16[1,1,128,512]{3,2,1,0:T(8,128)(2,1)S(1)}, bf16[1,1,128,512]{3,2,1,0:T(8,128)(2,1)S(1)}, u32[]{:S(2)}, u32[]{:S(2)}) collective-permute-start(bf16[1,1,128,512]{3,2,1,0:T(8,128)(2,1)S(1)} %get-tuple-element.144.refs_4_), channel_id=1, source_target_pairs={{0,4},{4,0},{8,12},{12,8},{1,5},{5,1},{9,13},{13,9},{2,6},{6,2},{1... | collective-permute-start | bytes 393224 | tf_op jit(solution)/shard_map/ppermute | solution.py:85
  45.5 4.8 %collective-permute-start.20 = (bf16[1,1,128,512]{3,2,1,0:T(8,128)(2,1)S(1)}, bf16[1,1,128,512]{3,2,1,0:T(8,128)(2,1)S(1)}, u32[]{:S(2)}, u32[]{:S(2)}) collective-permute-start(bf16[1,1,128,512]{3,2,1,0:T(8,128)(2,1)S(1)} %get-tuple-element.145.refs_5_), channel_id=1, source_target_pairs={{0,4},{4,0},{8,12},{12,8},{1,5},{5,1},{9,13},{13,9},{2,6},{6,2},{1... | collective-permute-start | bytes 393224 | tf_op jit(solution)/shard_map/ppermute | solution.py:85
  46.9 9.2 %collective-permute-start.18 = (bf16[2,1,128,512]{3,2,1,0:T(8,128)(2,1)S(1)}, bf16[2,1,128,512]{3,2,1,0:T(8,128)(2,1)S(1)}, u32[]{:S(2)}, u32[]{:S(2)}) collective-permute-start(bf16[2,1,128,512]{3,2,1,0:T(8,128)(2,1)S(1)} %get-tuple-element.133), channel_id=1, source_target_pairs={{0,8},{4,12},{8,0},{12,4},{1,9},{5,13},{9,1},{13,5},{2,10},{6,14},... | collective-permute-start | bytes 786440 | tf_op jit(solution)/shard_map/ppermute | solution.py:81
  48.9 3.4 %collective-permute-start.23 = (bf16[1,1,128,512]{3,2,1,0:T(8,128)(2,1)S(1)}, bf16[1,1,128,512]{3,2,1,0:T(8,128)(2,1)S(1)}, u32[]{:S(2)}, u32[]{:S(2)}) collective-permute-start(bf16[1,1,128,512]{3,2,1,0:T(8,128)(2,1)S(1)} %get-tuple-element.154.refs_4_), channel_id=1, source_target_pairs={{0,4},{4,0},{8,12},{12,8},{1,5},{5,1},{9,13},{13,9},{2,6},{6,2},{1... | collective-permute-start | bytes 393224 | tf_op jit(solution)/shard_map/ppermute | solution.py:85
  49.0 3.4 %collective-permute-start.24 = (bf16[1,1,128,512]{3,2,1,0:T(8,128)(2,1)S(1)}, bf16[1,1,128,512]{3,2,1,0:T(8,128)(2,1)S(1)}, u32[]{:S(2)}, u32[]{:S(2)}) collective-permute-start(bf16[1,1,128,512]{3,2,1,0:T(8,128)(2,1)S(1)} %get-tuple-element.155.refs_5_), channel_id=1, source_target_pairs={{0,4},{4,0},{8,12},{12,8},{1,5},{5,1},{9,13},{13,9},{2,6},{6,2},{1... | collective-permute-start | bytes 393224 | tf_op jit(solution)/shard_map/ppermute | solution.py:85
  50.8 8.2 %collective-permute-start.26 = (bf16[1,1,128,512]{3,2,1,0:T(8,128)(2,1)S(1)}, bf16[1,1,128,512]{3,2,1,0:T(8,128)(2,1)S(1)}, u32[]{:S(2)}, u32[]{:S(2)}) collective-permute-start(bf16[1,1,128,512]{3,2,1,0:T(8,128)(2,1)S(1)} %get-tuple-element.149), channel_id=1, source_target_pairs={{0,8},{4,12},{8,0},{12,4},{1,9},{5,13},{9,1},{13,5},{2,10},{6,14},... | collective-permute-start | bytes 393224 | tf_op jit(solution)/shard_map/ppermute | solution.py:81
  52.9 8.1 %collective-permute-start.25 = (bf16[1,1,128,512]{3,2,1,0:T(8,128)(2,1)S(1)}, bf16[1,1,128,512]{3,2,1,0:T(8,128)(2,1)S(1)}, u32[]{:S(2)}, u32[]{:S(2)}) collective-permute-start(bf16[1,1,128,512]{3,2,1,0:T(8,128)(2,1)S(1)} %get-tuple-element.159), channel_id=1, source_target_pairs={{0,8},{4,12},{8,0},{12,4},{1,9},{5,13},{9,1},{13,5},{2,10},{6,14},... | collective-permute-start | bytes 393224 | tf_op jit(solution)/shard_map/ppermute | solution.py:81

commit v8 on v7

--- a/solution.py
+++ b/solution.py
@@ -91,20 +91,23 @@
         def from_energy(x, t):
             return lax.ppermute(x, "en", [((i + t) % en, i) for i in range(en)])
 
+        cuts = [(0, e - 1), (e - 1, 1)]
+
         def first(offsets_ref, couplings_ref, lesser_ref, greater_ref, inverse_ref, *refs):
             outs, (offsets_at, couplings_at, sems) = refs[:-3], refs[-3:]
-            leads, inverses, lessers = (outs[i :: 3][: owners - 1] for i in range(3))
+            leads, inverses, greaters, lessers = (outs[i :: 4][: owners - 1] for i in range(4))
             copies = [(offsets_ref, offsets_at), (couplings_ref, couplings_at)]
             for i, d in enumerate(others):
                 blocks = pl.ds(owner_at(d) * owned, owned)
-                for n in range(e):
+                for n in range(e - 1):
                     for b in range(owned):
                         to = leads[i].at[pl.ds((n * owned + b) * r, r)]
-                        copies.append((greater_ref.at[n, owner_at(d) * owned + b], to))
+                        copies.append((inverse_ref.at[n, owner_at(d) * owned + b], to))
                 copies.append((lesser_ref.at[:, blocks], lessers[i]))
-                copies.append((inverse_ref.at[:, blocks], inverses[i]))
+                copies.append((greater_ref.at[:, blocks], greaters[i]))
+                copies.append((inverse_ref.at[pl.ds(e - 1, 1), blocks], inverses[i]))
             own = pl.ds(owner_at(0) * owned, owned)
-            copies += [(inverse_ref.at[:, own], outs[-2]), (lesser_ref.at[:, own], outs[-1])]
+            copies += [(inverse_ref.at[:, own], outs[-1 - len(cuts)]), *((lesser_ref.at[pl.ds(n, k), own], outs[-len(cuts) + i]) for i, (n, k) in enumerate(cuts))]
             copies = [pltpu.make_async_copy(x, y, sems.at[i]) for i, (x, y) in enumerate(copies)]
             for copy in copies:
                 copy.start()
@@ -122,14 +125,19 @@
                     packed = jnp.where(row == i * held + k, x[k : k + 1, :], packed)
             packed = jnp.concatenate([packed, jnp.zeros((tail, LANES - e), jnp.float32)], axis=1)
             for out in leads:
-                out[e * owned * r :, :LANES] = packed.astype(BF16)
-                out[e * owned * r :, LANES:] = jnp.zeros((tail, o - LANES), BF16)
+                out[(e - 1) * owned * r :, :LANES] = packed.astype(BF16)
+                out[(e - 1) * owned * r :, LANES:] = jnp.zeros((tail, o - LANES), BF16)
             for copy in copies[2:]:
                 copy.wait()
 
         def join(*refs):
             for d in range(owners):
-                refs[-1][d] = refs[d][e * owned * r :, :LANES]
+                refs[owners][d] = refs[d][(e - 1) * owned * r :, :LANES]
+            for d in others:
+                for n in range(e - 1):
+                    for b in range(owned):
+                        at_row = (n * owned + b) * r
+                        refs[owners + d][n, b] = refs[d][at_row : at_row + r]
 
         def from_hbm(kernel, outs, name, scratch, *args):
             far = pl.BlockSpec(memory_space=pltpu.HBM)
@@ -139,7 +147,7 @@
                 out_specs=[WHOLE] * len(outs),
                 out_shape=[jax.ShapeDtypeStruct(x, BF16) for x in outs],
                 scratch_shapes=scratch,
-                compiler_params=PARAMS,
+                compiler_params=pltpu.CompilerParams(vmem_limit_bytes=61 * 1024 * 1024),
                 cost_estimate=COST,
                 name=name,
             )(*args)
@@ -168,16 +176,31 @@
                         jnp.sum(spread, axis=1, keepdims=True), (tile, LANES)
                     )
 
-        def mix(tables, received, d, groups, earlier):
+        def mix(tables, received, d, groups, passengers, earlier):
+            flat = [x for came in received for x in came]
+            stands = [
+                [(1 + i, k) for i, x in enumerate(flat) if any(x is y for y in came) for k in range(x.shape[0])]
+                for came in received
+            ]
+
+            def load(ins, t, m, at_block, b, at):
+                if not t:
+                    return ins[0][m, at_block, at, :]
+                i, k = stands[t - 1][m]
+                return ins[i][k, b, at, :]
+
             def kernel(*refs):
                 table_refs, refs = refs[: len(tables)], refs[len(tables) :]
-                ins, outs = refs[: 1 + len(received)], refs[1 + len(received) :]
+                ins, refs = refs[: 1 + len(flat)], refs[1 + len(flat) :]
+                outs = refs[len(passengers) :]
+                for i in range(len(passengers)):
+                    outs[-1][len(groups[-1]) + i] = refs[i][0]
                 for b in range(owned):
                     at_block = owner_at(d) * owned + b
 
                     def body(at):
                         totals = weighted(
-                            table_refs, range(e), lambda t, m: ins[t][m, b if t else at_block, at, :]
+                            table_refs, range(e), lambda t, m: load(ins, t, m, at_block, b, at)
                         )
                         for out, group in zip(outs, groups):
                             for i, n in enumerate(group):
@@ -186,12 +209,11 @@
                     chunks(r, body)
 
             shapes = [(len(group),) + block[1:] for group in groups]
-            return call(kernel, shapes, "mix", *after(tables, *earlier), lesser_in, *received)
+            shapes[-1] = (len(groups[-1]) + len(passengers),) + block[1:]
+            return call(kernel, shapes, "mix", *after(tables, *earlier), lesser_in, *flat, *passengers)
 
         def greater_at(refs, m, d, b, at):
-            if not d:
-                return refs[0][m, owner_at(0) * owned + b, at, :]
-            return refs[d][pl.ds(pl.multiple_of((m * owned + b) * r + at.start, STEP), STEP), :]
+            return refs[d][m, b if d else owner_at(0) * owned + b, at, :]
 
         def partial_sums(table, rows, groups, earlier):
             def kernel(table_ref, *refs):
@@ -209,7 +231,8 @@
                         chunks(r, body)
 
             (table,) = after([table], *earlier)
-            shapes = [(len(group), owners) + block[1:] for group in groups]
+            spare = [STEP] * (len(groups) - 1) + [0]
+            shapes = [(len(group), owners, owned, r + x, o) for group, x in zip(groups, spare)]
             return call(kernel, shapes, "partial_sums", table, greater_in, *rows)
 
         def add_partial(group, table, rows, received, earlier):
@@ -232,7 +255,7 @@
             shape = (len(group),) + block[1:]
             return call(kernel, [shape] * owners, "add_partial", table, greater_in, *rows, *received)
 
-        def product(jobs, earlier):
+        def product(jobs, earlier, pad=0):
             arrays = []
             for job in jobs:
                 for x, _ in [*job[0], *job[1]]:
@@ -263,10 +286,10 @@
                         ).astype(BF16)
                         for i in range(owners):
                             for j, at in enumerate(spans):
-                                outs[i][k, b, :, at] = full[i * r : (i + 1) * r, j * r : (j + 1) * r]
-
-            shape = (len(jobs),) + block[1:]
-            return call(kernel, [shape] * owners, "product", *after(arrays, *earlier))
+                                outs[i][k, b, :r, at] = full[i * r : (i + 1) * r, j * r : (j + 1) * r]
+
+            shapes = [(len(jobs), owned, r + pad if d else r, o) for d in range(owners)]
+            return call(kernel, shapes, "product", *after(arrays, *earlier))
 
         def back_to_rows(outs):
             return [outs[0]] + [to_owner(outs[d], owners - d) for d in others]
@@ -282,7 +305,7 @@
                 sems, out = refs[-1], refs[-2]
                 copies = [
                     pltpu.make_async_copy(
-                        refs[where[id(x)]].at[k],
+                        refs[where[id(x)]].at[k, :, pl.ds(0, r)],
                         out.at[n, pl.ds(owner_at(d) * owned, owned)],
                         sems.at[i],
                     )
@@ -312,15 +335,15 @@
         def at(arrays, index):
             return [(x, index) for x in arrays]
 
-        shapes = [(e * owned * r + tail, o), block, block]
-        *parts, inverse_own, lesser_own = from_hbm(
+        shapes = [((e - 1) * owned * r + tail, o), (1,) + block[1:], block, block]
+        parts = from_hbm(
             first,
-            shapes * len(others) + [block] * 2,
+            shapes * len(others) + [block] + [(k,) + block[1:] for _, k in cuts],
             "first",
             [
                 pltpu.VMEM((held, e), jnp.int32),
                 pltpu.VMEM((held, e), jnp.float32),
-                pltpu.SemaphoreType.DMA((4 + (e * owned + 2) * len(others),)),
+                pltpu.SemaphoreType.DMA((3 + len(cuts) + ((e - 1) * owned + 3) * len(others),)),
             ],
             offsets.T,
             couplings.T,
@@ -328,12 +351,15 @@
             greater_in,
             inverse,
         )
-        leads, inverses, lessers = (parts[i::3] for i in range(3))
-        greater_rows = [to_owner(x, d) for d, x in zip(others, leads)]
-        lesser_from = [[from_energy(x, t) for t in shifts] for x in lessers]
-        inverse_rows = [to_owner(x, d) for d, x in zip(others, inverses)]
-
-        (joined,) = call(join, [(owners, tail, LANES)], "join", leads[0], *greater_rows)
+        parts, (inverse_own, *lesser_own) = parts[: 4 * len(others)], parts[4 * len(others) :]
+        leads, inverses, greaters, lessers = (parts[i::4] for i in range(4))
+        leads_from = [to_owner(x, d) for d, x in zip(others, leads)]
+        lesser_from = [[[from_energy(x, t)] for t in shifts] for x in lessers]
+        greater_rows = [to_owner(x, d) for d, x in zip(others, greaters)]
+
+        joined, *inverse_rows = call(
+            join, [(owners, tail, LANES)] + [(e - 1,) + block[1:]] * len(others), "join", leads[0], *leads_from
+        )
         tables = call(
             weights,
             [jax.ShapeDtypeStruct((e, tile, LANES), jnp.float32)] * (1 + len(shifts)),
@@ -345,14 +371,15 @@
             lax.ppermute(table, "en", [(i, (i + t) % en) for i in range(en)])
             for t, table in zip(shifts, tables[1:])
         ]
-        lesser_own_from = [from_energy(lesser_own, t) for t in shifts]
-
-        groups = [tuple(range(e - 1)), (e - 1,)] if e > 1 else [(0,)]
+        lesser_own = after(lesser_own, *tables)
+        lesser_own_from = [[from_energy(x, t) for x in lesser_own] for t in shifts]
+
+        groups = [tuple(range(e - 1)), (e - 1,)]
         singles = [(n,) for n in range(e)]
         lesser_rows = []
-        last = []
-        for d, came in zip(others, lesser_from):
-            last = mix(tables, came, d, groups, last)
+        last = tables_for
+        for i, (d, came) in enumerate(zip(others, lesser_from)):
+            last = mix(tables, came, d, groups, [inverses[i]], last)
             lesser_rows.append([to_owner(x, d) for x in last])
         inverse_own_beside = to_lanes(inverse_own)
         last = [*last, *inverse_own_beside]
@@ -361,9 +388,8 @@
             last = partial_sums(table, greater_rows, singles, last)
             for g, part in enumerate(last):
                 received[g].append(from_energy(part, t))
-        inverse_rows = list(after(inverse_rows, *last))
         inverse_rows_beside = [to_lanes(x) for x in inverse_rows]
-        lesser_mixed = mix(tables, lesser_own_from, 0, groups, last)
+        lesser_mixed = mix(tables, lesser_own_from, 0, groups, [], last)
         lesser_mixed_beside = [to_lanes(x) for x in lesser_mixed]
         last = lesser_mixed
 
@@ -371,17 +397,24 @@
             return next((g, group.index(n)) for g, group in enumerate(groups) if n in group)
 
         def inverse_at(n):
-            beside = [at(inverse_own_beside, (n,)), *(at(x, (n,)) for x in inverse_rows_beside)]
-            return in_order((inverse_own, (n,)), at(inverse_rows, (n,)), beside)
+            own = [at(inverse_own_beside, (n,))]
+            if n < e - 1:
+                beside = [at(x, (n,)) for x in inverse_rows_beside]
+                return in_order((inverse_own, (n,)), at(inverse_rows, (n,)), own + beside)
+            at_n = len(groups[-1])
+            beside = [at(x[-1], (at_n,)) for x in lesser_rows_beside]
+            return in_order((inverse_own, (n,)), at([x[-1] for x in lesser_rows], (at_n,)), own + beside)
 
         def lesser_job(n):
             g, i = find(groups, n)
             h, k = find(groups, n)
             rows = [x[g] for x in lesser_rows]
-            beside = [at(lesser_mixed_beside[h], (k,))] + [at(x[g], (i,)) for x in lesser_rows_beside]
+            beside = [at(lesser_mixed_beside[h], (k,))]
+            for x in lesser_rows_beside:
+                beside.append(at(x[g], (i,)))
             return inverse_at(n), in_order((lesser_mixed[h], (k,)), at(rows, (i,)), beside)
 
-        lesser_rows_beside = [[to_lanes(x) for x in rows] for rows in lesser_rows]
+        lesser_rows_beside = [[*(to_lanes(x) for x in rows[:-1]), None] for rows in lesser_rows]
 
         results = {"L": None, "G": None}
         waiting = {"L": [], "G": []}
@@ -394,14 +427,11 @@
                 return [results[kind]]
             return earlier
 
-        last = [*last, *[x[-1] for x in lesser_rows]]
         sigmas = {}
-        steps = ["a0", "L0"]
+        steps = ["L0", "a0", "L1+G0"]
         for n in range(1, e):
             steps.append(f"a{n}")
-            if n == 2:
-                steps.append("pL0")
-            steps.append("L1+G0" if n == 1 else f"G{n - 1}")
+            steps.append("pL0" if n == 1 else f"G{n - 1}")
         steps.append(f"G{e - 1}")
         for step in steps:
             if step[0] == "p":
@@ -425,8 +455,12 @@
                         sigma, beside = sigmas[g]
                         beside = [at(x, (i,)) for x in beside]
                         jobs.append((inverse_at(n), in_order((sigma[0], (i,)), at(sigma[1:], (i,)), beside)))
-            last = product(jobs, last)
+            last = product(jobs, last, STEP if step == "L0" else 0)
             back = back_to_rows(last)
+            if step == "L0":
+                for rows, beside in zip(lesser_rows, lesser_rows_beside):
+                    rows[-1] = after([rows[-1]], *last)[0]
+                    beside[-1] = to_lanes(rows[-1])
             for k, (kind, n, g) in enumerate(made):
                 waiting[kind] += [(n, d, x, k, g) for d, x in enumerate(back)]
         last = put("L", lambda part: part[1] == 0, last)

time: 61.9 us -> 60.4 us (0.976)
  waiting for transfers between devices: 26.3 us -> 22.9 us
  local copies, waits for them, and re-layouts: 4.09 us -> 0.98 us
  starting transfers between devices: 20 us -> 22.9 us
  Pallas kernels: 10.4 us -> 12.6 us
    ppermute x5 -> x6, starting transfers between devices: 5.88 us -> 10.5 us  [from_energy(): return lax.ppermute(x, 'en', [((i + t) % en, i) for i in range(en)])]
    unnamed x14, local copies, waits for them, and re-layouts: 4.09 us -> 0.98 us
    ppermute x8, waiting for transfers between devices: 16.3 us -> 13.3 us  [to_owner(): return lax.ppermute(x, 'ph', pairs)]
    pallas_call x1, Pallas kernels: 0.84 us -> 2.95 us  [from_hbm(): pl.pallas_call(kernel, in_specs=[far] * len(args), out_specs=[WHOLE] * le...]
    ppermute x1, waiting for transfers between devices: 3.67 us -> 1.77 us  [on_device(): lax.ppermute(table, 'en', [(i, (i + t) % en) for i in range(en)])]
    ppermute x1, starting transfers between devices: 1.49 us -> 0.04 us  [on_device(): lax.ppermute(table, 'en', [(i, (i + t) % en) for i in range(en)])]
    ppermute x5 -> x6, waiting for transfers between devices: 4.66 us -> 5.47 us  [from_energy(): return lax.ppermute(x, 'en', [((i + t) % en, i) for i in range(en)])]
    ppermute x13, waiting for transfers between devices: 1.64 us -> 2.31 us  [to_lanes(): lax.ppermute(x, 'ph', [(p, p // lanes * lanes + (p % lanes + q) % lanes)...]
  transfers between devices with their start and end apart: 27 -> 28, of which waited for: 13 -> 9; matrix products, arithmetic and copies ran while one was open for 0% -> 0% of each run, Pallas kernels for 14% -> 15%
where the time goes in v8:
time: 60.4 us; the launch traced here: 60.2 us
  starting transfers between devices  22.9 us (38%)
  waiting for transfers between devices  22.9 us (38%)
  Pallas kernels  12.6 us (21%)
  local copies, waits for them, and re-layouts  0.98 us (2%)
  between operations  0.89 us (1%)
    ppermute x8, waiting for transfers between devices, to_owner(): return lax.ppermute(x, 'ph', pairs)  13.3 us
    ppermute x6, starting transfers between devices, from_energy(): return lax.ppermute(x, 'en', [((i + t) % en, i) for i in range(en)])  10.5 us
    ppermute x8, starting transfers between devices, to_owner(): return lax.ppermute(x, 'ph', pairs)  10.3 us
    ppermute x6, waiting for transfers between devices, from_energy(): return lax.ppermute(x, 'en', [((i + t) % en, i) for i in range(en)])  5.47 us
    pallas_call x7, Pallas kernels, place(): pl.pallas_call(kernel, in_specs=[WHOLE] * len(arrays) + [far] * (result i...  4.95 us
    pallas_call x12, Pallas kernels, call(): pl.pallas_call(kernel, in_specs=[WHOLE] * len(args), out_specs=[WHOLE] *...  4.7 us
    pallas_call x1, Pallas kernels, from_hbm(): pl.pallas_call(kernel, in_specs=[far] * len(args), out_specs=[WHOLE] * le...  2.95 us
    ppermute x13, waiting for transfers between devices, to_lanes(): lax.ppermute(x, 'ph', [(p, p // lanes * lanes + (p % lanes + q) % lanes)...  2.31 us
  transfers between devices with their start and end apart: 28, of which 9 were waited for; matrix products, arithmetic and copies ran while one was open for 0% of the time, Pallas kernels for 15%

profile of v8, /device:TPU:0, one launch (start us, length us, event | category | flops | bytes accessed | tf_op | source)
XLA Modules:
  0.0 60.2 jit_solution(13323966690523638197)
XLA Ops:
  0.6 3.0 %first.1 = (bf16[272,512]{1,0:T(8,128)(2,1)}, bf16[1,1,128,512]{3,2,1,0:T(8,128)(2,1)}, bf16[3,1,128,512]{3,2,1,0:T(8,128)(2,1)}, bf16[3,1,128,512]{3,2,1,0:T(8,...) custom-call(s32[2,3]{1,0:T(2,128)} %bitcast.2, ...), custom_call_target="tpu_custom_call" | custom-call | flops 1 | bytes 1 | tf_op jit(solution)/shard_map/first/pallas_call | solution.py:144
  3.6 3.0 %collective-permute-start.3 = (bf16[3,1,128,512]{3,2,1,0:T(8,128)(2,1)}, bf16[3,1,128,512]{3,2,1,0:T(8,128)(2,1)S(1)}, u32[]{:S(2)}, u32[]{:S(2)}) collective-permute-start(bf16[3,1,128,512]{3,2,1,0:T(8,128)(2,1)} %get-tuple-element.98), channel_id=1, source_target_pairs={{16,0},{0,16},{17,1},{1,17},{18,2},{2,18},{19,3},{3,19},{20,4},{4,... | collective-permute-start | bytes 1179656 | tf_op jit(solution)/shard_map/ppermute | solution.py:92
  6.6 1.5 %collective-permute-start = (bf16[272,512]{1,0:T(8,128)(2,1)}, bf16[272,512]{1,0:T(8,128)(2,1)S(1)}, u32[]{:S(2)}, u32[]{:S(2)}) collective-permute-start(bf16[272,512]{1,0:T(8,128)(2,1)} %get-tuple-element.92.refs_0_), channel_id=1, source_target_pairs={{0,8},{4,12},{8,0},{12,4},{1,9},{5,13},{9,1},{13,5},{2,10},{6,14},... | collective-permute-start | bytes 835592 | tf_op jit(solution)/shard_map/ppermute | solution.py:81
  8.1 0.5 collective-permute-start.7
  8.6 7.8 %collective-permute-done.refs_1_ = bf16[272,512]{1,0:T(8,128)(2,1)S(1)} collective-permute-done((bf16[272,512]{1,0:T(8,128)(2,1)}, bf16[272,512]{1,0:T(8,128)(2,1)S(1)}, u32[]{:S(2)}, u32[]{:S(2)}) %collective-permute-start) | collective-permute-done | bytes 278560 | tf_op jit(solution)/shard_map/ppermute | solution.py:81
  16.4 1.0 %copy-done.3 = bf16[272,512]{1,0:T(8,128)(2,1)S(1)} copy-done((bf16[272,512]{1,0:T(8,128)(2,1)S(1)}, bf16[272,512]{1,0:T(8,128)(2,1)}, u32[]{:S(2)}) %copy-start.3) | copy-done | bytes 278552
  17.4 0.0 copy-start
  17.4 0.1 collective-permute-start.1
  17.5 1.2 %collective-permute-done.1.refs_1_ = bf16[2,16,128]{2,1,0:T(8,128)(2,1)S(1)} collective-permute-done((bf16[2,16,128]{2,1,0:T(8,128)(2,1)S(1)}, bf16[2,16,128]{2,1,0:T(8,128)(2,1)S(1)}, u32[]{:S(2)}, u32[]{:S(2)}) %collective-permute-start.1) | collective-permute-done | bytes 8224 | tf_op jit(solution)/shard_map/ppermute | solution.py:85
  18.6 0.1 weights.1
  18.7 0.0 collective-permute-start.2
  18.8 2.0 %collective-permute-start.8 = (bf16[2,1,128,512]{3,2,1,0:T(8,128)(2,1)S(1)}, bf16[2,1,128,512]{3,2,1,0:T(8,128)(2,1)S(1)}, u32[]{:S(2)}, u32[]{:S(2)}) collective-permute-start(bf16[2,1,128,512]{3,2,1,0:T(8,128)(2,1)S(1)} %copy-done.5), channel_id=1, source_target_pairs={{16,0},{0,16},{17,1},{1,17},{18,2},{2,18},{19,3},{3,19},{20,4},{4,... | collective-permute-start | bytes 786440 | tf_op jit(solution)/shard_map/ppermute | solution.py:92
  20.8 1.8 %collective-permute-done.2.table_ref = f32[3,8,128]{2,1,0:T(8,128)S(1)} collective-permute-done((f32[3,8,128]{2,1,0:T(8,128)S(1)}, f32[3,8,128]{2,1,0:T(8,128)S(1)}, u32[]{:S(2)}, u32[]{:S(2)}) %collective-permute-start.2) | collective-permute-done | bytes 12320 | tf_op jit(solution)/shard_map/ppermute | solution.py:371
  22.5 0.0 collective-permute-done.3.refs_3_
  22.6 0.4 mix.2
  22.9 1.5 %collective-permute-start.10 = (bf16[2,1,128,512]{3,2,1,0:T(8,128)(2,1)S(1)}, bf16[2,1,128,512]{3,2,1,0:T(8,128)(2,1)S(1)}, u32[]{:S(2)}, u32[]{:S(2)}) collective-permute-start(bf16[2,1,128,512]{3,2,1,0:T(8,128)(2,1)S(1)} %get-tuple-element.102), channel_id=1, source_target_pairs={{0,8},{4,12},{8,0},{12,4},{1,9},{5,13},{9,1},{13,5},{2,10},{6,14},... | collective-permute-start | bytes 786440 | tf_op jit(solution)/shard_map/ppermute | solution.py:81
  24.5 0.5 collective-permute-start.9
  25.0 0.0 collective-permute-done.5.refs_2_
  25.0 0.0 collective-permute-start.6
  25.0 0.0 collective-permute-done.7.refs_1_
  25.0 0.4 partial_sums.1
  25.4 1.6 %collective-permute-start.15 = (bf16[1,2,1,144,512]{4,3,2,1,0:T(8,128)(2,1)S(1)}, bf16[1,2,1,144,512]{4,3,2,1,0:T(8,128)(2,1)S(1)}, u32[]{:S(2)}, u32[]{:S(2)}) collective-permute-start(bf16[1,2,1,144,512]{4,3,2,1,0:T(8,128)(2,1)S(1)} %get-tuple-element.105), channel_id=1, source_target_pairs={{16,0},{0,16},{17,1},{1,17},{18,2},{2,18},{19,3},{3,19},{20,4},{4,... | collective-permute-start | bytes 884744 | tf_op jit(solution)/shard_map/ppermute | solution.py:92
  27.0 4.0 %collective-permute-done.9.refs_4_ = bf16[1,1,128,512]{3,2,1,0:T(8,128)(2,1)S(1)} collective-permute-done((bf16[1,1,128,512]{3,2,1,0:T(8,128)(2,1)S(1)}, bf16[1,1,128,512]{3,2,1,0:T(8,128)(2,1)S(1)}, u32[]{:S(2)}, u32[]{:S(2)}) %collective-permute-start.9) | collective-permute-done | bytes 131104 | tf_op jit(solution)/shard_map/ppermute | solution.py:92
  31.0 0.0 collective-permute-done.8.refs_3_
  31.0 0.4 mix.3
  31.3 0.1 collective-permute-start.11
  31.4 0.0 collective-permute-done.10.refs_5_
  31.4 0.5 collective-permute-start.12
  31.9 1.8 %collective-permute-start.4 = (bf16[2,1,128,512]{3,2,1,0:T(8,128)(2,1)S(1)}, bf16[2,1,128,512]{3,2,1,0:T(8,128)(2,1)S(1)}, u32[]{:S(2)}, u32[]{:S(2)}) collective-permute-start(bf16[2,1,128,512]{3,2,1,0:T(8,128)(2,1)S(1)} %get-tuple-element.100), channel_id=1, source_target_pairs={{0,8},{4,12},{8,0},{12,4},{1,9},{5,13},{9,1},{13,5},{2,10},{6,14},... | collective-permute-start | bytes 786440 | tf_op jit(solution)/shard_map/ppermute | solution.py:81
  33.8 1.6 %collective-permute-start.19 = (bf16[1,2,1,144,512]{4,3,2,1,0:T(8,128)(2,1)S(1)}, bf16[1,2,1,144,512]{4,3,2,1,0:T(8,128)(2,1)S(1)}, u32[]{:S(2)}, u32[]{:S(2)}) collective-permute-start(bf16[1,2,1,144,512]{4,3,2,1,0:T(8,128)(2,1)S(1)} %get-tuple-element.106), channel_id=1, source_target_pairs={{16,0},{0,16},{17,1},{1,17},{18,2},{2,18},{19,3},{3,19},{20,4},{4,... | collective-permute-start | bytes 884744 | tf_op jit(solution)/shard_map/ppermute | solution.py:92
  35.3 0.0 collective-permute-done.12.refs_7_
  35.3 0.9 %product.4 = (bf16[2,1,128,512]{3,2,1,0:T(8,128)(2,1)S(1)}, bf16[2,1,144,512]{3,2,1,0:T(8,128)(2,1)S(1)}) custom-call(bf16[3,1,128,512]{3,2,1,0:T(8,128)(2,1)S(1)} %copy-done.2, bf16[2,1,128,512]{3,2,1,0:T(8,128)(2,1)S(1)} %get-tuple-element.153.refs_1_.refs_6_, bf16[3,1,128,512]{3,2,1,0:T(8,128)(2,1)S(1)} %collective-permute-done.5.refs_2_, ...), custom_call_target="tpu_custom_call" | custom-call | flops 1 | bytes 1 | tf_op jit(solution)/shard_map/product/pallas_call | solution.py:21
  36.2 1.0 %collective-permute-start.22 = (bf16[2,1,144,512]{3,2,1,0:T(8,128)(2,1)S(1)}, bf16[2,1,144,512]{3,2,1,0:T(8,128)(2,1)S(1)}, u32[]{:S(2)}, u32[]{:S(2)}) collective-permute-start(bf16[2,1,144,512]{3,2,1,0:T(8,128)(2,1)S(1)} %get-tuple-element.125), channel_id=1, source_target_pairs={{0,8},{4,12},{8,0},{12,4},{1,9},{5,13},{9,1},{13,5},{2,10},{6,14},... | collective-permute-start | bytes 884744 | tf_op jit(solution)/shard_map/ppermute | solution.py:81
  37.2 0.2 add_partial.3
  37.5 0.1 collective-permute-start.16
  37.5 3.5 %collective-permute-done.4.refs_1_ = bf16[2,1,128,512]{3,2,1,0:T(8,128)(2,1)S(1)} collective-permute-done((bf16[2,1,128,512]{3,2,1,0:T(8,128)(2,1)S(1)}, bf16[2,1,128,512]{3,2,1,0:T(8,128)(2,1)S(1)}, u32[]{:S(2)}, u32[]{:S(2)}) %collective-permute-start.4) | collective-permute-done | bytes 262176 | tf_op jit(solution)/shard_map/ppermute | solution.py:81
  41.1 0.0 collective-permute-start.13
  41.1 1.8 %collective-permute-start.23 = (bf16[1,2,1,128,512]{4,3,2,1,0:T(8,128)(2,1)S(1)}, bf16[1,2,1,128,512]{4,3,2,1,0:T(8,128)(2,1)S(1)}, u32[]{:S(2)}, u32[]{:S(2)}) collective-permute-start(bf16[1,2,1,128,512]{4,3,2,1,0:T(8,128)(2,1)S(1)} %get-tuple-element.107), channel_id=1, source_target_pairs={{16,0},{0,16},{17,1},{1,17},{18,2},{2,18},{19,3},{3,19},{20,4},{4,... | collective-permute-start | bytes 786440 | tf_op jit(solution)/shard_map/ppermute | solution.py:92
  42.9 0.2 collective-permute-start.17
  43.1 1.1 %collective-permute-done.17.refs_11_ = bf16[1,1,128,512]{3,2,1,0:T(8,128)(2,1)S(1)} collective-permute-done((bf16[1,1,128,512]{3,2,1,0:T(8,128)(2,1)S(1)}, bf16[1,1,128,512]{3,2,1,0:T(8,128)(2,1)S(1)}, u32[]{:S(2)}, u32[]{:S(2)}) %collective-permute-start.17) | collective-permute-done | bytes 131104 | tf_op jit(solution)/shard_map/ppermute | solution.py:85
  44.2 0.0 collective-permute-done.13.refs_3_
  44.3 0.9 %product.5 = (bf16[2,1,128,512]{3,2,1,0:T(8,128)(2,1)S(1)}, bf16[2,1,128,512]{3,2,1,0:T(8,128)(2,1)S(1)}) custom-call(bf16[3,1,128,512]{3,2,1,0:T(8,128)(2,1)S(1)} %copy-done.2, bf16[2,1,128,512]{3,2,1,0:T(8,128)(2,1)S(1)} %collective-permute-done.4.refs_1_, bf16[3,1,128,512]{3,2,1,0:T(8,128)(2,1)S(1)} %collective-permute-done.5.refs_2_, ...), custom_call_target="tpu_custom_call" | custom-call | flops 1 | bytes 1 | tf_op jit(solution)/shard_map/product/pallas_call | solution.py:21
  45.1 1.6 %collective-permute-start.18 = (bf16[2,1,128,512]{3,2,1,0:T(8,128)(2,1)S(1)}, bf16[2,1,128,512]{3,2,1,0:T(8,128)(2,1)S(1)}, u32[]{:S(2)}, u32[]{:S(2)}) collective-permute-start(bf16[2,1,128,512]{3,2,1,0:T(8,128)(2,1)S(1)} %get-tuple-element.142), channel_id=1, source_target_pairs={{0,8},{4,12},{8,0},{12,4},{1,9},{5,13},{9,1},{13,5},{2,10},{6,14},... | collective-permute-start | bytes 786440 | tf_op jit(solution)/shard_map/ppermute | solution.py:81
  46.7 0.0 collective-permute-done.19.refs_2_
  46.7 0.2 add_partial.4
  47.0 0.1 collective-permute-start.20
  47.0 0.5 collective-permute-start.21
  47.5 0.8 %place.7.refs_1_ = bf16[3,2,128,512]{3,2,1,0:T(8,128)(2,1)} custom-call(bf16[2,1,128,512]{3,2,1,0:T(8,128)(2,1)S(1)} %get-tuple-element.147.refs_0_, bf16[2,1,144,512]{3,2,1,0:T(8,128)(2,1)S(1)} %collective-permute-done.22.refs_1_), custom_call_target="tpu_custom_call" | custom-call | flops 1 | bytes 1 | tf_op jit(solution)/shard_map/place/pallas_call | solution.py:320
  48.4 1.5 %collective-permute-done.23.refs_2_ = bf16[1,2,1,128,512]{4,3,2,1,0:T(8,128)(2,1)S(1)} collective-permute-done((bf16[1,2,1,128,512]{4,3,2,1,0:T(8,128)(2,1)S(1)}, bf16[1,2,1,128,512]{4,3,2,1,0:T(8,128)(2,1)S(1)}, u32[]{:S(2)}, u32[]{:S(2)}) %collective-permute-start.23) | collective-permute-done | bytes 262176 | tf_op jit(solution)/shard_map/ppermute | solution.py:92
  49.9 0.2 add_partial.5
  50.1 0.1 collective-permute-start.24
  50.2 0.5 collective-permute-start.25
  50.7 0.5 product.6
  51.2 1.8 %collective-permute-start.27 = (bf16[1,1,128,512]{3,2,1,0:T(8,128)(2,1)S(1)}, bf16[1,1,128,512]{3,2,1,0:T(8,128)(2,1)S(1)}, u32[]{:S(2)}, u32[]{:S(2)}) collective-permute-start(bf16[1,1,128,512]{3,2,1,0:T(8,128)(2,1)S(1)} %get-tuple-element.161), channel_id=1, source_target_pairs={{0,8},{4,12},{8,0},{12,4},{1,9},{5,13},{9,1},{13,5},{2,10},{6,14},... | collective-permute-start | bytes 393224 | tf_op jit(solution)/shard_map/ppermute | solution.py:81
  53.0 0.5 product.7
  53.6 0.5 collective-permute-start.26
  54.1 0.7 %place.8.refs_1_ = bf16[3,2,128,512]{3,2,1,0:T(8,128)(2,1)} custom-call(bf16[2,1,128,512]{3,2,1,0:T(8,128)(2,1)S(1)} %get-tuple-element.173.refs_0_, bf16[3,2,128,512]{3,2,1,0:T(8,128)(2,1)} %place.7.refs_1_), custom_call_target="tpu_custom_call", output_to_operand_aliasing={{}: (1, {})} | custom-call | flops 1 | bytes 1 | tf_op jit(solution)/shard_map/place/pallas_call | solution.py:320
  54.7 0.8 %place.9.refs_1_ = bf16[3,2,128,512]{3,2,1,0:T(8,128)(2,1)} custom-call(bf16[2,1,128,512]{3,2,1,0:T(8,128)(2,1)S(1)} %get-tuple-element.173.refs_0_, bf16[1,1,128,512]{3,2,1,0:T(8,128)(2,1)S(1)} %get-tuple-element.174.refs_1_, bf16[1,1,128,512]{3,2,1,0:T(8,128)(2,1)S(1)} %get-tuple-element.175.refs_2_), custom_call_target="tpu_custom_call" | custom-call | flops 1 | bytes 1 | tf_op jit(solution)/shard_map/place/pallas_call | solution.py:320
  55.5 0.7 %place.10 = bf16[3,2,128,512]{3,2,1,0:T(8,128)(2,1)} custom-call(bf16[2,1,128,512]{3,2,1,0:T(8,128)(2,1)S(1)} %collective-permute-done.18.refs_0_, bf16[3,2,128,512]{3,2,1,0:T(8,128)(2,1)} %place.8.refs_1_), custom_call_target="tpu_custom_call", output_to_operand_aliasing={{}: (1, {})} | custom-call | flops 1 | bytes 1 | tf_op jit(solution)/shard_map/place/pallas_call | solution.py:320
  56.2 0.7 %place.11.refs_1_ = bf16[3,2,128,512]{3,2,1,0:T(8,128)(2,1)} custom-call(bf16[2,1,128,512]{3,2,1,0:T(8,128)(2,1)S(1)} %collective-permute-done.18.refs_0_, bf16[3,2,128,512]{3,2,1,0:T(8,128)(2,1)} %place.9.refs_1_), custom_call_target="tpu_custom_call", output_to_operand_aliasing={{}: (1, {})} | custom-call | flops 1 | bytes 1 | tf_op jit(solution)/shard_map/place/pallas_call | solution.py:320
  56.9 0.6 collective-permute-done.27.refs_0_
  57.5 0.7 %place.12.refs_1_ = bf16[3,2,128,512]{3,2,1,0:T(8,128)(2,1)} custom-call(bf16[1,1,128,512]{3,2,1,0:T(8,128)(2,1)S(1)} %collective-permute-done.27.refs_0_, bf16[3,2,128,512]{3,2,1,0:T(8,128)(2,1)} %place.11.refs_1_), custom_call_target="tpu_custom_call", output_to_operand_aliasing={{}: (1, {})} | custom-call | flops 1 | bytes 1 | tf_op jit(solution)/shard_map/place/pallas_call | solution.py:320
  58.2 1.4 %collective-permute-done.26.refs_0_ = bf16[1,1,128,512]{3,2,1,0:T(8,128)(2,1)S(1)} collective-permute-done((bf16[1,1,128,512]{3,2,1,0:T(8,128)(2,1)S(1)}, bf16[1,1,128,512]{3,2,1,0:T(8,128)(2,1)S(1)}, u32[]{:S(2)}, u32[]{:S(2)}) %collective-permute-start.26) | collective-permute-done | bytes 131104 | tf_op jit(solution)/shard_map/ppermute | solution.py:81
  59.6 0.7 %place.13 = bf16[3,2,128,512]{3,2,1,0:T(8,128)(2,1)} custom-call(bf16[1,1,128,512]{3,2,1,0:T(8,128)(2,1)S(1)} %collective-permute-done.26.refs_0_, bf16[3,2,128,512]{3,2,1,0:T(8,128)(2,1)} %place.12.refs_1_), custom_call_target="tpu_custom_call", output_to_operand_aliasing={{}: (1, {})} | custom-call | flops 1 | bytes 1 | tf_op jit(solution)/shard_map/place/pallas_call | solution.py:320
  (26 shorter events, 0.1 us)
Async XLA Ops:
  0.6 21.9 %copy-start.1 = (bf16[3,2,128,512]{3,2,1,0:T(8,128)(2,1)S(1)}, bf16[3,2,128,512]{3,2,1,0:T(8,128)(2,1)}, u32[]{:S(2)}) copy-start(bf16[3,2,128,512]{3,2,1,0:T(8,128)(2,1)} %refs_2_.3) | copy-start | bytes 2359300
  3.6 18.9 %collective-permute-start.3 = (bf16[3,1,128,512]{3,2,1,0:T(8,128)(2,1)}, bf16[3,1,128,512]{3,2,1,0:T(8,128)(2,1)S(1)}, u32[]{:S(2)}, u32[]{:S(2)}) collective-permute-start(bf16[3,1,128,512]{3,2,1,0:T(8,128)(2,1)} %get-tuple-element.98), channel_id=1, source_target_pairs={{16,0},{0,16},{17,1},{1,17},{18,2},{2,18},{19,3},{3,19},{20,4},{4,... | collective-permute-start | bytes 1179656 | tf_op jit(solution)/shard_map/ppermute | solution.py:92
  6.6 9.8 %collective-permute-start = (bf16[272,512]{1,0:T(8,128)(2,1)}, bf16[272,512]{1,0:T(8,128)(2,1)S(1)}, u32[]{:S(2)}, u32[]{:S(2)}) collective-permute-start(bf16[272,512]{1,0:T(8,128)(2,1)} %get-tuple-element.92.refs_0_), channel_id=1, source_target_pairs={{0,8},{4,12},{8,0},{12,4},{1,9},{5,13},{9,1},{13,5},{2,10},{6,14},... | collective-permute-start | bytes 835592 | tf_op jit(solution)/shard_map/ppermute | solution.py:81
  8.1 16.8 %collective-permute-start.5 = (bf16[3,1,128,512]{3,2,1,0:T(8,128)(2,1)}, bf16[3,1,128,512]{3,2,1,0:T(8,128)(2,1)S(1)}, u32[]{:S(2)}, u32[]{:S(2)}) collective-permute-start(bf16[3,1,128,512]{3,2,1,0:T(8,128)(2,1)} %get-tuple-element.162.refs_0_), channel_id=1, source_target_pairs={{0,4},{4,0},{8,12},{12,8},{1,5},{5,1},{9,13},{13,9},{2,6},{6,2},{1... | collective-permute-start | bytes 1179656 | tf_op jit(solution)/shard_map/ppermute | solution.py:85
  8.1 16.9 %collective-permute-start.7 = (bf16[3,1,128,512]{3,2,1,0:T(8,128)(2,1)}, bf16[3,1,128,512]{3,2,1,0:T(8,128)(2,1)S(1)}, u32[]{:S(2)}, u32[]{:S(2)}) collective-permute-start(bf16[3,1,128,512]{3,2,1,0:T(8,128)(2,1)} %get-tuple-element.104), channel_id=1, source_target_pairs={{0,8},{4,12},{8,0},{12,4},{1,9},{5,13},{9,1},{13,5},{2,10},{6,14},... | collective-permute-start | bytes 1179656 | tf_op jit(solution)/shard_map/ppermute | solution.py:81
  16.4 1.0 %copy-start.3 = (bf16[272,512]{1,0:T(8,128)(2,1)S(1)}, bf16[272,512]{1,0:T(8,128)(2,1)}, u32[]{:S(2)}) copy-start(bf16[272,512]{1,0:T(8,128)(2,1)} %get-tuple-element.92.refs_0_) | copy-start | bytes 835588
  17.4 1.4 %copy-start.5 = (bf16[2,1,128,512]{3,2,1,0:T(8,128)(2,1)S(1)}, bf16[2,1,128,512]{3,2,1,0:T(8,128)(2,1)}, u32[]{:S(2)}) copy-start(bf16[2,1,128,512]{3,2,1,0:T(8,128)(2,1)} %get-tuple-element.112) | copy-start | bytes 786436
  17.4 5.2 %copy-start.4 = (bf16[1,1,128,512]{3,2,1,0:T(8,128)(2,1)S(1)}, bf16[1,1,128,512]{3,2,1,0:T(8,128)(2,1)}, u32[]{:S(2)}) copy-start(bf16[1,1,128,512]{3,2,1,0:T(8,128)(2,1)} %get-tuple-element.99.refs_4_) | copy-start | bytes 393220
  17.4 7.6 %copy-start = (bf16[3,2,128,512]{3,2,1,0:T(8,128)(2,1)S(1)}, bf16[3,2,128,512]{3,2,1,0:T(8,128)(2,1)}, u32[]{:S(2)}) copy-start(bf16[3,2,128,512]{3,2,1,0:T(8,128)(2,1)} %refs_0_.7) | copy-start | bytes 2359300
  17.4 1.2 %collective-permute-start.1 = (bf16[2,16,128]{2,1,0:T(8,128)(2,1)S(1)}, bf16[2,16,128]{2,1,0:T(8,128)(2,1)S(1)}, u32[]{:S(2)}, u32[]{:S(2)}) collective-permute-start(bf16[2,16,128]{2,1,0:T(8,128)(2,1)S(1)} %get-tuple-element.93.refs_0_), channel_id=1, source_target_pairs={{0,4},{4,0},{8,12},{12,8},{1,5},{5,1},{9,13},{13,9},{2,6},{6,2},{1... | collective-permute-start | bytes 24584 | tf_op jit(solution)/shard_map/ppermute | solution.py:85
  18.7 3.8 %collective-permute-start.2 = (f32[3,8,128]{2,1,0:T(8,128)S(1)}, f32[3,8,128]{2,1,0:T(8,128)S(1)}, u32[]{:S(2)}, u32[]{:S(2)}) collective-permute-start(f32[3,8,128]{2,1,0:T(8,128)S(1)} %get-tuple-element.109.refs_1_), channel_id=1, source_target_pairs={{0,16},{16,0},{1,17},{17,1},{2,18},{18,2},{3,19},{19,3},{4,20},{20... | collective-permute-start | bytes 36872 | tf_op jit(solution)/shard_map/ppermute | solution.py:371
  18.8 12.2 %collective-permute-start.8 = (bf16[2,1,128,512]{3,2,1,0:T(8,128)(2,1)S(1)}, bf16[2,1,128,512]{3,2,1,0:T(8,128)(2,1)S(1)}, u32[]{:S(2)}, u32[]{:S(2)}) collective-permute-start(bf16[2,1,128,512]{3,2,1,0:T(8,128)(2,1)S(1)} %copy-done.5), channel_id=1, source_target_pairs={{16,0},{0,16},{17,1},{1,17},{18,2},{2,18},{19,3},{3,19},{20,4},{4,... | collective-permute-start | bytes 786440 | tf_op jit(solution)/shard_map/ppermute | solution.py:92
  22.5 1.9 %copy-start.6 = (bf16[1,1,128,512]{3,2,1,0:T(8,128)(2,1)S(1)}, bf16[1,1,128,512]{3,2,1,0:T(8,128)(2,1)}, u32[]{:S(2)}) copy-start(bf16[1,1,128,512]{3,2,1,0:T(8,128)(2,1)} %get-tuple-element.113) | copy-start | bytes 393220
  22.9 8.5 %collective-permute-start.10 = (bf16[2,1,128,512]{3,2,1,0:T(8,128)(2,1)S(1)}, bf16[2,1,128,512]{3,2,1,0:T(8,128)(2,1)S(1)}, u32[]{:S(2)}, u32[]{:S(2)}) collective-permute-start(bf16[2,1,128,512]{3,2,1,0:T(8,128)(2,1)S(1)} %get-tuple-element.102), channel_id=1, source_target_pairs={{0,8},{4,12},{8,0},{12,4},{1,9},{5,13},{9,1},{13,5},{2,10},{6,14},... | collective-permute-start | bytes 786440 | tf_op jit(solution)/shard_map/ppermute | solution.py:81
  24.5 6.5 %collective-permute-start.9 = (bf16[1,1,128,512]{3,2,1,0:T(8,128)(2,1)S(1)}, bf16[1,1,128,512]{3,2,1,0:T(8,128)(2,1)S(1)}, u32[]{:S(2)}, u32[]{:S(2)}) collective-permute-start(bf16[1,1,128,512]{3,2,1,0:T(8,128)(2,1)S(1)} %copy-done.6), channel_id=1, source_target_pairs={{16,0},{0,16},{17,1},{1,17},{18,2},{2,18},{19,3},{3,19},{20,4},{4,... | collective-permute-start | bytes 393224 | tf_op jit(solution)/shard_map/ppermute | solution.py:92
  25.0 8.8 %collective-permute-start.6 = (bf16[2,1,128,512]{3,2,1,0:T(8,128)(2,1)S(1)}, bf16[2,1,128,512]{3,2,1,0:T(8,128)(2,1)S(1)}, u32[]{:S(2)}, u32[]{:S(2)}) collective-permute-start(bf16[2,1,128,512]{3,2,1,0:T(8,128)(2,1)S(1)} %get-tuple-element.153.refs_1_.refs_6_), channel_id=1, source_target_pairs={{0,4},{4,0},{8,12},{12,8},{1,5},{5,1},{9,13},{13,9},{2,6},{6,2},{1... | collective-permute-start | bytes 786440 | tf_op jit(solution)/shard_map/ppermute | solution.py:85
  25.4 11.8 %collective-permute-start.15 = (bf16[1,2,1,144,512]{4,3,2,1,0:T(8,128)(2,1)S(1)}, bf16[1,2,1,144,512]{4,3,2,1,0:T(8,128)(2,1)S(1)}, u32[]{:S(2)}, u32[]{:S(2)}) collective-permute-start(bf16[1,2,1,144,512]{4,3,2,1,0:T(8,128)(2,1)S(1)} %get-tuple-element.105), channel_id=1, source_target_pairs={{16,0},{0,16},{17,1},{1,17},{18,2},{2,18},{19,3},{3,19},{20,4},{4,... | collective-permute-start | bytes 884744 | tf_op jit(solution)/shard_map/ppermute | solution.py:92
  27.0 8.3 %copy-start.2 = (bf16[3,1,128,512]{3,2,1,0:T(8,128)(2,1)S(1)}, bf16[3,1,128,512]{3,2,1,0:T(8,128)(2,1)}, u32[]{:S(2)}) copy-start(bf16[3,1,128,512]{3,2,1,0:T(8,128)(2,1)} %get-tuple-element.162.refs_0_) | copy-start | bytes 1179652
  31.3 2.4 %collective-permute-start.11 = (bf16[2,1,128,512]{3,2,1,0:T(8,128)(2,1)S(1)}, bf16[2,1,128,512]{3,2,1,0:T(8,128)(2,1)S(1)}, u32[]{:S(2)}, u32[]{:S(2)}) collective-permute-start(bf16[2,1,128,512]{3,2,1,0:T(8,128)(2,1)S(1)} %get-tuple-element.120.refs_4_), channel_id=1, source_target_pairs={{0,4},{4,0},{8,12},{12,8},{1,5},{5,1},{9,13},{13,9},{2,6},{6,2},{1... | collective-permute-start | bytes 786440 | tf_op jit(solution)/shard_map/ppermute | solution.py:85
  31.4 3.9 %collective-permute-start.12 = (bf16[2,1,128,512]{3,2,1,0:T(8,128)(2,1)S(1)}, bf16[2,1,128,512]{3,2,1,0:T(8,128)(2,1)S(1)}, u32[]{:S(2)}, u32[]{:S(2)}) collective-permute-start(bf16[2,1,128,512]{3,2,1,0:T(8,128)(2,1)S(1)} %collective-permute-done.10.refs_5_), channel_id=1, source_target_pairs={{0,4},{4,0},{8,12},{12,8},{1,5},{5,1},{9,13},{13,9},{2,6},{6,2},{1... | collective-permute-start | bytes 786440 | tf_op jit(solution)/shard_map/ppermute | solution.py:85
  31.9 9.2 %collective-permute-start.4 = (bf16[2,1,128,512]{3,2,1,0:T(8,128)(2,1)S(1)}, bf16[2,1,128,512]{3,2,1,0:T(8,128)(2,1)S(1)}, u32[]{:S(2)}, u32[]{:S(2)}) collective-permute-start(bf16[2,1,128,512]{3,2,1,0:T(8,128)(2,1)S(1)} %get-tuple-element.100), channel_id=1, source_target_pairs={{0,8},{4,12},{8,0},{12,4},{1,9},{5,13},{9,1},{13,5},{2,10},{6,14},... | collective-permute-start | bytes 786440 | tf_op jit(solution)/shard_map/ppermute | solution.py:81
  33.7 7.3 %collective-permute-start.14 = (bf16[1,1,128,512]{3,2,1,0:T(8,128)(2,1)S(1)}, bf16[1,1,128,512]{3,2,1,0:T(8,128)(2,1)S(1)}, u32[]{:S(2)}, u32[]{:S(2)}) collective-permute-start(bf16[1,1,128,512]{3,2,1,0:T(8,128)(2,1)S(1)} %get-tuple-element.134.refs_4_), channel_id=1, source_target_pairs={{0,4},{4,0},{8,12},{12,8},{1,5},{5,1},{9,13},{13,9},{2,6},{6,2},{1... | collective-permute-start | bytes 393224 | tf_op jit(solution)/shard_map/ppermute | solution.py:85
  33.8 13.0 %collective-permute-start.19 = (bf16[1,2,1,144,512]{4,3,2,1,0:T(8,128)(2,1)S(1)}, bf16[1,2,1,144,512]{4,3,2,1,0:T(8,128)(2,1)S(1)}, u32[]{:S(2)}, u32[]{:S(2)}) collective-permute-start(bf16[1,2,1,144,512]{4,3,2,1,0:T(8,128)(2,1)S(1)} %get-tuple-element.106), channel_id=1, source_target_pairs={{16,0},{0,16},{17,1},{1,17},{18,2},{2,18},{19,3},{3,19},{20,4},{4,... | collective-permute-start | bytes 884744 | tf_op jit(solution)/shard_map/ppermute | solution.py:92
  36.2 11.3 %collective-permute-start.22 = (bf16[2,1,144,512]{3,2,1,0:T(8,128)(2,1)S(1)}, bf16[2,1,144,512]{3,2,1,0:T(8,128)(2,1)S(1)}, u32[]{:S(2)}, u32[]{:S(2)}) collective-permute-start(bf16[2,1,144,512]{3,2,1,0:T(8,128)(2,1)S(1)} %get-tuple-element.125), channel_id=1, source_target_pairs={{0,8},{4,12},{8,0},{12,4},{1,9},{5,13},{9,1},{13,5},{2,10},{6,14},... | collective-permute-start | bytes 884744 | tf_op jit(solution)/shard_map/ppermute | solution.py:81
  37.5 5.4 %collective-permute-start.16 = (bf16[1,1,128,512]{3,2,1,0:T(8,128)(2,1)S(1)}, bf16[1,1,128,512]{3,2,1,0:T(8,128)(2,1)S(1)}, u32[]{:S(2)}, u32[]{:S(2)}) collective-permute-start(bf16[1,1,128,512]{3,2,1,0:T(8,128)(2,1)S(1)} %get-tuple-element.138.refs_8_), channel_id=1, source_target_pairs={{0,4},{4,0},{8,12},{12,8},{1,5},{5,1},{9,13},{13,9},{2,6},{6,2},{1... | collective-permute-start | bytes 393224 | tf_op jit(solution)/shard_map/ppermute | solution.py:85
  41.1 3.2 %collective-permute-start.13 = (bf16[2,1,128,512]{3,2,1,0:T(8,128)(2,1)S(1)}, bf16[2,1,128,512]{3,2,1,0:T(8,128)(2,1)S(1)}, u32[]{:S(2)}, u32[]{:S(2)}) collective-permute-start(bf16[2,1,128,512]{3,2,1,0:T(8,128)(2,1)S(1)} %collective-permute-done.4.refs_1_), channel_id=1, source_target_pairs={{0,4},{4,0},{8,12},{12,8},{1,5},{5,1},{9,13},{13,9},{2,6},{6,2},{1... | collective-permute-start | bytes 786440 | tf_op jit(solution)/shard_map/ppermute | solution.py:85
  41.1 8.8 %collective-permute-start.23 = (bf16[1,2,1,128,512]{4,3,2,1,0:T(8,128)(2,1)S(1)}, bf16[1,2,1,128,512]{4,3,2,1,0:T(8,128)(2,1)S(1)}, u32[]{:S(2)}, u32[]{:S(2)}) collective-permute-start(bf16[1,2,1,128,512]{4,3,2,1,0:T(8,128)(2,1)S(1)} %get-tuple-element.107), channel_id=1, source_target_pairs={{16,0},{0,16},{17,1},{1,17},{18,2},{2,18},{19,3},{3,19},{20,4},{4,... | collective-permute-start | bytes 786440 | tf_op jit(solution)/shard_map/ppermute | solution.py:92
  42.9 1.3 %collective-permute-start.17 = (bf16[1,1,128,512]{3,2,1,0:T(8,128)(2,1)S(1)}, bf16[1,1,128,512]{3,2,1,0:T(8,128)(2,1)S(1)}, u32[]{:S(2)}, u32[]{:S(2)}) collective-permute-start(bf16[1,1,128,512]{3,2,1,0:T(8,128)(2,1)S(1)} %get-tuple-element.139.refs_9_), channel_id=1, source_target_pairs={{0,4},{4,0},{8,12},{12,8},{1,5},{5,1},{9,13},{13,9},{2,6},{6,2},{1... | collective-permute-start | bytes 393224 | tf_op jit(solution)/shard_map/ppermute | solution.py:85
  45.1 10.4 %collective-permute-start.18 = (bf16[2,1,128,512]{3,2,1,0:T(8,128)(2,1)S(1)}, bf16[2,1,128,512]{3,2,1,0:T(8,128)(2,1)S(1)}, u32[]{:S(2)}, u32[]{:S(2)}) collective-permute-start(bf16[2,1,128,512]{3,2,1,0:T(8,128)(2,1)S(1)} %get-tuple-element.142), channel_id=1, source_target_pairs={{0,8},{4,12},{8,0},{12,4},{1,9},{5,13},{9,1},{13,5},{2,10},{6,14},... | collective-permute-start | bytes 786440 | tf_op jit(solution)/shard_map/ppermute | solution.py:81
  47.0 3.7 %collective-permute-start.20 = (bf16[1,1,128,512]{3,2,1,0:T(8,128)(2,1)S(1)}, bf16[1,1,128,512]{3,2,1,0:T(8,128)(2,1)S(1)}, u32[]{:S(2)}, u32[]{:S(2)}) collective-permute-start(bf16[1,1,128,512]{3,2,1,0:T(8,128)(2,1)S(1)} %get-tuple-element.156.refs_4_), channel_id=1, source_target_pairs={{0,4},{4,0},{8,12},{12,8},{1,5},{5,1},{9,13},{13,9},{2,6},{6,2},{1... | collective-permute-start | bytes 393224 | tf_op jit(solution)/shard_map/ppermute | solution.py:85
  47.0 3.6 %collective-permute-start.21 = (bf16[1,1,128,512]{3,2,1,0:T(8,128)(2,1)S(1)}, bf16[1,1,128,512]{3,2,1,0:T(8,128)(2,1)S(1)}, u32[]{:S(2)}, u32[]{:S(2)}) collective-permute-start(bf16[1,1,128,512]{3,2,1,0:T(8,128)(2,1)S(1)} %get-tuple-element.157.refs_5_), channel_id=1, source_target_pairs={{0,4},{4,0},{8,12},{12,8},{1,5},{5,1},{9,13},{13,9},{2,6},{6,2},{1... | collective-permute-start | bytes 393224 | tf_op jit(solution)/shard_map/ppermute | solution.py:85
  50.1 2.9 %collective-permute-start.24 = (bf16[1,1,128,512]{3,2,1,0:T(8,128)(2,1)S(1)}, bf16[1,1,128,512]{3,2,1,0:T(8,128)(2,1)S(1)}, u32[]{:S(2)}, u32[]{:S(2)}) collective-permute-start(bf16[1,1,128,512]{3,2,1,0:T(8,128)(2,1)S(1)} %get-tuple-element.166.refs_4_), channel_id=1, source_target_pairs={{0,4},{4,0},{8,12},{12,8},{1,5},{5,1},{9,13},{13,9},{2,6},{6,2},{1... | collective-permute-start | bytes 393224 | tf_op jit(solution)/shard_map/ppermute | solution.py:85
  50.2 2.9 %collective-permute-start.25 = (bf16[1,1,128,512]{3,2,1,0:T(8,128)(2,1)S(1)}, bf16[1,1,128,512]{3,2,1,0:T(8,128)(2,1)S(1)}, u32[]{:S(2)}, u32[]{:S(2)}) collective-permute-start(bf16[1,1,128,512]{3,2,1,0:T(8,128)(2,1)S(1)} %get-tuple-element.167.refs_5_), channel_id=1, source_target_pairs={{0,4},{4,0},{8,12},{12,8},{1,5},{5,1},{9,13},{13,9},{2,6},{6,2},{1... | collective-permute-start | bytes 393224 | tf_op jit(solution)/shard_map/ppermute | solution.py:85
  51.2 6.3 %collective-permute-start.27 = (bf16[1,1,128,512]{3,2,1,0:T(8,128)(2,1)S(1)}, bf16[1,1,128,512]{3,2,1,0:T(8,128)(2,1)S(1)}, u32[]{:S(2)}, u32[]{:S(2)}) collective-permute-start(bf16[1,1,128,512]{3,2,1,0:T(8,128)(2,1)S(1)} %get-tuple-element.161), channel_id=1, source_target_pairs={{0,8},{4,12},{8,0},{12,4},{1,9},{5,13},{9,1},{13,5},{2,10},{6,14},... | collective-permute-start | bytes 393224 | tf_op jit(solution)/shard_map/ppermute | solution.py:81
  53.6 6.0 %collective-permute-start.26 = (bf16[1,1,128,512]{3,2,1,0:T(8,128)(2,1)S(1)}, bf16[1,1,128,512]{3,2,1,0:T(8,128)(2,1)S(1)}, u32[]{:S(2)}, u32[]{:S(2)}) collective-permute-start(bf16[1,1,128,512]{3,2,1,0:T(8,128)(2,1)S(1)} %get-tuple-element.171), channel_id=1, source_target_pairs={{0,8},{4,12},{8,0},{12,4},{1,9},{5,13},{9,1},{13,5},{2,10},{6,14},... | collective-permute-start | bytes 393224 | tf_op jit(solution)/shard_map/ppermute | solution.py:81

commit v9 on v8

--- a/solution.py
+++ b/solution.py
@@ -91,23 +91,15 @@
         def from_energy(x, t):
             return lax.ppermute(x, "en", [((i + t) % en, i) for i in range(en)])
 
-        cuts = [(0, e - 1), (e - 1, 1)]
-
-        def first(offsets_ref, couplings_ref, lesser_ref, greater_ref, inverse_ref, *refs):
-            outs, (offsets_at, couplings_at, sems) = refs[:-3], refs[-3:]
-            leads, inverses, greaters, lessers = (outs[i :: 4][: owners - 1] for i in range(4))
+
+        def lead(offsets_ref, couplings_ref, inverse_ref, *refs):
+            leads, (offsets_at, couplings_at, sems) = refs[:-3], refs[-3:]
             copies = [(offsets_ref, offsets_at), (couplings_ref, couplings_at)]
             for i, d in enumerate(others):
-                blocks = pl.ds(owner_at(d) * owned, owned)
-                for n in range(e - 1):
+                for n in range(e):
                     for b in range(owned):
                         to = leads[i].at[pl.ds((n * owned + b) * r, r)]
                         copies.append((inverse_ref.at[n, owner_at(d) * owned + b], to))
-                copies.append((lesser_ref.at[:, blocks], lessers[i]))
-                copies.append((greater_ref.at[:, blocks], greaters[i]))
-                copies.append((inverse_ref.at[pl.ds(e - 1, 1), blocks], inverses[i]))
-            own = pl.ds(owner_at(0) * owned, owned)
-            copies += [(inverse_ref.at[:, own], outs[-1 - len(cuts)]), *((lesser_ref.at[pl.ds(n, k), own], outs[-len(cuts) + i]) for i, (n, k) in enumerate(cuts))]
             copies = [pltpu.make_async_copy(x, y, sems.at[i]) for i, (x, y) in enumerate(copies)]
             for copy in copies:
                 copy.start()
@@ -125,16 +117,33 @@
                     packed = jnp.where(row == i * held + k, x[k : k + 1, :], packed)
             packed = jnp.concatenate([packed, jnp.zeros((tail, LANES - e), jnp.float32)], axis=1)
             for out in leads:
-                out[(e - 1) * owned * r :, :LANES] = packed.astype(BF16)
-                out[(e - 1) * owned * r :, LANES:] = jnp.zeros((tail, o - LANES), BF16)
+                out[e * owned * r :, :LANES] = packed.astype(BF16)
+                out[e * owned * r :, LANES:] = jnp.zeros((tail, o - LANES), BF16)
             for copy in copies[2:]:
                 copy.wait()
 
+        def cut(wanted, earlier):
+            arrays = after([x for x, *_ in wanted], *earlier)
+
+            def kernel(*refs):
+                ins, outs, sems = refs[: len(wanted)], refs[len(wanted) : -1], refs[-1]
+                copies = []
+                for i, (_, d, n, k) in enumerate(wanted):
+                    at_d = pl.ds(owner_at(d) * owned, owned)
+                    copies.append(pltpu.make_async_copy(ins[i].at[pl.ds(n, k), at_d], outs[i], sems.at[i]))
+                for copy in copies:
+                    copy.start()
+                for copy in copies:
+                    copy.wait()
+
+            shapes = [(k,) + block[1:] for *_, k in wanted]
+            return from_hbm(kernel, shapes, "cut", [pltpu.SemaphoreType.DMA((len(wanted),))], *arrays)
+
         def join(*refs):
             for d in range(owners):
-                refs[owners][d] = refs[d][(e - 1) * owned * r :, :LANES]
+                refs[owners][d] = refs[d][e * owned * r :, :LANES]
             for d in others:
-                for n in range(e - 1):
+                for n in range(e):
                     for b in range(owned):
                         at_row = (n * owned + b) * r
                         refs[owners + d][n, b] = refs[d][at_row : at_row + r]
@@ -176,7 +185,7 @@
                         jnp.sum(spread, axis=1, keepdims=True), (tile, LANES)
                     )
 
-        def mix(tables, received, d, groups, passengers, earlier):
+        def mix(tables, received, d, groups, earlier):
             flat = [x for came in received for x in came]
             stands = [
                 [(1 + i, k) for i, x in enumerate(flat) if any(x is y for y in came) for k in range(x.shape[0])]
@@ -191,10 +200,7 @@
 
             def kernel(*refs):
                 table_refs, refs = refs[: len(tables)], refs[len(tables) :]
-                ins, refs = refs[: 1 + len(flat)], refs[1 + len(flat) :]
-                outs = refs[len(passengers) :]
-                for i in range(len(passengers)):
-                    outs[-1][len(groups[-1]) + i] = refs[i][0]
+                ins, outs = refs[: 1 + len(flat)], refs[1 + len(flat) :]
                 for b in range(owned):
                     at_block = owner_at(d) * owned + b
 
@@ -209,8 +215,7 @@
                     chunks(r, body)
 
             shapes = [(len(group),) + block[1:] for group in groups]
-            shapes[-1] = (len(groups[-1]) + len(passengers),) + block[1:]
-            return call(kernel, shapes, "mix", *after(tables, *earlier), lesser_in, *flat, *passengers)
+            return call(kernel, shapes, "mix", *after(tables, *earlier), lesser_in, *flat)
 
         def greater_at(refs, m, d, b, at):
             return refs[d][m, b if d else owner_at(0) * owned + b, at, :]
@@ -271,16 +276,16 @@
                     for b in range(owned):
                         left = jnp.concatenate(
                             [
-                                jnp.concatenate([a[(*index, b, slice(None), at)] for at in spans], axis=1)
+                                jnp.concatenate([a[(*index, b, slice(0, r), at)] for at in spans], axis=1)
                                 for a, index in a_in[:owners]
                             ],
                             axis=0,
                         )
-                        right = jnp.concatenate([x[(*index, b)] for x, index in s_in], axis=0)
+                        right = jnp.concatenate([x[(*index, b, slice(0, r))] for x, index in s_in], axis=0)
                         half = jnp.dot(left, right, preferred_element_type=jnp.float32).astype(BF16)
                         full = lax.dot_general(
                             half,
-                            jnp.concatenate([a[(*index, b)] for a, index in a_in], axis=0),
+                            jnp.concatenate([a[(*index, b, slice(0, r))] for a, index in a_in], axis=0),
                             (((1,), (1,)), ((), ())),
                             preferred_element_type=jnp.float32,
                         ).astype(BF16)
@@ -335,30 +340,29 @@
         def at(arrays, index):
             return [(x, index) for x in arrays]
 
-        shapes = [((e - 1) * owned * r + tail, o), (1,) + block[1:], block, block]
-        parts = from_hbm(
-            first,
-            shapes * len(others) + [block] + [(k,) + block[1:] for _, k in cuts],
-            "first",
+        leads = from_hbm(
+            lead,
+            [(e * owned * r + tail, o)] * len(others),
+            "lead",
             [
                 pltpu.VMEM((held, e), jnp.int32),
                 pltpu.VMEM((held, e), jnp.float32),
-                pltpu.SemaphoreType.DMA((3 + len(cuts) + ((e - 1) * owned + 3) * len(others),)),
+                pltpu.SemaphoreType.DMA((2 + e * owned * len(others),)),
             ],
             offsets.T,
             couplings.T,
-            lesser_in,
-            greater_in,
             inverse,
         )
-        parts, (inverse_own, *lesser_own) = parts[: 4 * len(others)], parts[4 * len(others) :]
-        leads, inverses, greaters, lessers = (parts[i::4] for i in range(4))
         leads_from = [to_owner(x, d) for d, x in zip(others, leads)]
+        lessers = cut([(lesser_in, d, 0, e) for d in others], leads)
         lesser_from = [[[from_energy(x, t)] for t in shifts] for x in lessers]
+        greaters = cut([(greater_in, d, 0, e) for d in others], lessers)
         greater_rows = [to_owner(x, d) for d, x in zip(others, greaters)]
+        (inverse_own,) = cut([(inverse, 0, 0, e)], greaters)
+        lesser_own = cut([(lesser_in, 0, n, k) for n, k in ((0, e - 1), (e - 1, 1))], [inverse_own])
 
         joined, *inverse_rows = call(
-            join, [(owners, tail, LANES)] + [(e - 1,) + block[1:]] * len(others), "join", leads[0], *leads_from
+            join, [(owners, tail, LANES)] + [block] * len(others), "join", leads[0], *leads_from
         )
         tables = call(
             weights,
@@ -377,9 +381,9 @@
         groups = [tuple(range(e - 1)), (e - 1,)]
         singles = [(n,) for n in range(e)]
         lesser_rows = []
-        last = tables_for
-        for i, (d, came) in enumerate(zip(others, lesser_from)):
-            last = mix(tables, came, d, groups, [inverses[i]], last)
+        last = []
+        for d, came in zip(others, lesser_from):
+            last = mix(tables, came, d, groups, last)
             lesser_rows.append([to_owner(x, d) for x in last])
         inverse_own_beside = to_lanes(inverse_own)
         last = [*last, *inverse_own_beside]
@@ -389,7 +393,7 @@
             for g, part in enumerate(last):
                 received[g].append(from_energy(part, t))
         inverse_rows_beside = [to_lanes(x) for x in inverse_rows]
-        lesser_mixed = mix(tables, lesser_own_from, 0, groups, [], last)
+        lesser_mixed = mix(tables, lesser_own_from, 0, groups, last)
         lesser_mixed_beside = [to_lanes(x) for x in lesser_mixed]
         last = lesser_mixed
 
@@ -397,13 +401,8 @@
             return next((g, group.index(n)) for g, group in enumerate(groups) if n in group)
 
         def inverse_at(n):
-            own = [at(inverse_own_beside, (n,))]
-            if n < e - 1:
-                beside = [at(x, (n,)) for x in inverse_rows_beside]
-                return in_order((inverse_own, (n,)), at(inverse_rows, (n,)), own + beside)
-            at_n = len(groups[-1])
-            beside = [at(x[-1], (at_n,)) for x in lesser_rows_beside]
-            return in_order((inverse_own, (n,)), at([x[-1] for x in lesser_rows], (at_n,)), own + beside)
+            beside = [at(inverse_own_beside, (n,)), *(at(x, (n,)) for x in inverse_rows_beside)]
+            return in_order((inverse_own, (n,)), at(inverse_rows, (n,)), beside)
 
         def lesser_job(n):
             g, i = find(groups, n)

time: 60.4 us -> 60.2 us (level)
  waiting for transfers between devices: 22.9 us -> 12.2 us
  Pallas kernels: 12.6 us -> 19.7 us
  starting transfers between devices: 22.9 us -> 27.1 us
  local copies, waits for them, and re-layouts: 0.98 us -> 0.03 us
    ppermute x8, waiting for transfers between devices: 13.3 us -> 4.13 us  [to_owner(): return lax.ppermute(x, 'ph', pairs)]
    pallas_call x1 -> x5, Pallas kernels: 2.95 us -> 8.99 us  [from_hbm(): pl.pallas_call(kernel, in_specs=[far] * len(args), out_specs=[WHOLE] * le...]
    ppermute x8, starting transfers between devices: 10.3 us -> 13.2 us  [to_owner(): return lax.ppermute(x, 'ph', pairs)]
    ppermute x13, waiting for transfers between devices: 2.31 us -> 1.05 us  [to_lanes(): lax.ppermute(x, 'ph', [(p, p // lanes * lanes + (p % lanes + q) % lanes)...]
    pallas_call x12, Pallas kernels: 4.7 us -> 5.75 us  [call(): pl.pallas_call(kernel, in_specs=[WHOLE] * len(args), out_specs=[WHOLE] *...]
    unnamed x14 -> x10, local copies, waits for them, and re-layouts: 0.98 us -> 0.03 us
    ppermute x6, starting transfers between devices: 10.5 us -> 11.4 us  [from_energy(): return lax.ppermute(x, 'en', [((i + t) % en, i) for i in range(en)])]
  transfers between devices with their start and end apart: 28 -> 28, of which waited for: 9 -> 9; matrix products, arithmetic and copies ran while one was open for 0% -> 0% of each run, Pallas kernels for 15% -> 29%
where the time goes in v9:
time: 60.2 us; the launch traced here: 59.9 us
  starting transfers between devices  27.1 us (45%)
  Pallas kernels  19.7 us (33%)
  waiting for transfers between devices  12.2 us (20%)
  between operations  0.91 us (2%)
    ppermute x8, starting transfers between devices, to_owner(): return lax.ppermute(x, 'ph', pairs)  13.2 us
    ppermute x6, starting transfers between devices, from_energy(): return lax.ppermute(x, 'en', [((i + t) % en, i) for i in range(en)])  11.4 us
    pallas_call x5, Pallas kernels, from_hbm(): pl.pallas_call(kernel, in_specs=[far] * len(args), out_specs=[WHOLE] * le...  8.99 us
    pallas_call x12, Pallas kernels, call(): pl.pallas_call(kernel, in_specs=[WHOLE] * len(args), out_specs=[WHOLE] *...  5.75 us
    ppermute x6, waiting for transfers between devices, from_energy(): return lax.ppermute(x, 'en', [((i + t) % en, i) for i in range(en)])  5.06 us
    pallas_call x7, Pallas kernels, place(): pl.pallas_call(kernel, in_specs=[WHOLE] * len(arrays) + [far] * (result i...  4.95 us
    ppermute x8, waiting for transfers between devices, to_owner(): return lax.ppermute(x, 'ph', pairs)  4.13 us
    ppermute x13, starting transfers between devices, to_lanes(): lax.ppermute(x, 'ph', [(p, p // lanes * lanes + (p % lanes + q) % lanes)...  2.51 us
  transfers between devices with their start and end apart: 28, of which 9 were waited for; matrix products, arithmetic and copies ran while one was open for 0% of the time, Pallas kernels for 29%

profile of v9, /device:TPU:0, one launch (start us, length us, event | category | flops | bytes accessed | tf_op | source)
XLA Modules:
  0.0 59.9 jit_solution(11734014917856611513)
XLA Ops:
  0.6 1.9 %lead.1.refs_0_ = bf16[400,512]{1,0:T(8,128)(2,1)} custom-call(s32[2,3]{1,0:T(2,128)} %bitcast.2, f32[2,3]{1,0:T(2,128)} %bitcast.3, bf16[3,2,128,512]{3,2,1,0:T(8,128)(2,1)} %refs_0_.6), custom_call_target="tpu_custom_call" | custom-call | flops 1 | bytes 1 | tf_op jit(solution)/shard_map/lead/pallas_call | solution.py:153
  2.5 3.0 %collective-permute-start = (bf16[400,512]{1,0:T(8,128)(2,1)}, bf16[400,512]{1,0:T(8,128)(2,1)S(1)}, u32[]{:S(2)}, u32[]{:S(2)}) collective-permute-start(bf16[400,512]{1,0:T(8,128)(2,1)} %lead.1.refs_0_), channel_id=1, source_target_pairs={{0,8},{4,12},{8,0},{12,4},{1,9},{5,13},{9,1},{13,5},{2,10},{6,14},... | collective-permute-start | bytes 1228808 | tf_op jit(solution)/shard_map/ppermute | solution.py:81
  5.5 1.8 %cut.4 = bf16[3,1,128,512]{3,2,1,0:T(8,128)(2,1)} custom-call(bf16[3,2,128,512]{3,2,1,0:T(8,128)(2,1)} %refs_2_.3), custom_call_target="tpu_custom_call" | custom-call | flops 1 | bytes 1 | tf_op jit(solution)/shard_map/cut/pallas_call | solution.py:153
  7.3 1.6 %collective-permute-start.5 = (bf16[3,1,128,512]{3,2,1,0:T(8,128)(2,1)}, bf16[3,1,128,512]{3,2,1,0:T(8,128)(2,1)}, u32[]{:S(2)}, u32[]{:S(2)}) collective-permute-start(bf16[3,1,128,512]{3,2,1,0:T(8,128)(2,1)} %cut.4), channel_id=1, source_target_pairs={{16,0},{0,16},{17,1},{1,17},{18,2},{2,18},{19,3},{3,19},{20,4},{4,... | collective-permute-start | bytes 1179656 | tf_op jit(solution)/shard_map/ppermute | solution.py:92
  8.9 1.7 %cut.5 = bf16[3,1,128,512]{3,2,1,0:T(8,128)(2,1)} custom-call(bf16[3,2,128,512]{3,2,1,0:T(8,128)(2,1)} %refs_0_.11), custom_call_target="tpu_custom_call" | custom-call | flops 1 | bytes 1 | tf_op jit(solution)/shard_map/cut/pallas_call | solution.py:153
  10.6 0.0 copy-start.3
  10.6 1.8 %cut.6.refs_0_ = bf16[3,1,128,512]{3,2,1,0:T(8,128)(2,1)} custom-call(bf16[3,2,128,512]{3,2,1,0:T(8,128)(2,1)} %refs_0_.6), custom_call_target="tpu_custom_call" | custom-call | flops 1 | bytes 1 | tf_op jit(solution)/shard_map/cut/pallas_call | solution.py:153
  12.4 0.1 collective-permute-start.1
  12.5 0.6 collective-permute-start.6
  13.1 2.1 %collective-permute-done.refs_1_ = bf16[400,512]{1,0:T(8,128)(2,1)S(1)} collective-permute-done((bf16[400,512]{1,0:T(8,128)(2,1)}, bf16[400,512]{1,0:T(8,128)(2,1)S(1)}, u32[]{:S(2)}, u32[]{:S(2)}) %collective-permute-start) | collective-permute-done | bytes 409632 | tf_op jit(solution)/shard_map/ppermute | solution.py:81
  15.2 0.0 copy-start
  15.2 0.1 collective-permute-start.3
  15.3 1.8 %cut.7 = (bf16[2,1,128,512]{3,2,1,0:T(8,128)(2,1)}, bf16[1,1,128,512]{3,2,1,0:T(8,128)(2,1)}) custom-call(bf16[3,2,128,512]{3,2,1,0:T(8,128)(2,1)} %refs_2_.3, bf16[3,2,128,512]{3,2,1,0:T(8,128)(2,1)} %refs_2_.3), custom_call_target="tpu_custom_call" | custom-call | flops 1 | bytes 1 | tf_op jit(solution)/shard_map/cut/pallas_call | solution.py:153
  17.1 0.0 copy-start.1
  17.2 0.0 collective-permute-done.3.refs_1_
  17.2 0.1 weights.1
  17.3 2.2 %collective-permute-start.7 = (bf16[2,1,128,512]{3,2,1,0:T(8,128)(2,1)}, bf16[2,1,128,512]{3,2,1,0:T(8,128)(2,1)S(1)}, u32[]{:S(2)}, u32[]{:S(2)}) collective-permute-start(bf16[2,1,128,512]{3,2,1,0:T(8,128)(2,1)} %get-tuple-element.112), channel_id=1, source_target_pairs={{16,0},{0,16},{17,1},{1,17},{18,2},{2,18},{19,3},{3,19},{20,4},{4,... | collective-permute-start | bytes 786440 | tf_op jit(solution)/shard_map/ppermute | solution.py:92
  19.5 0.0 collective-permute-done.5.refs_3_
  19.5 1.4 %mix.2 = (bf16[2,1,128,512]{3,2,1,0:T(8,128)(2,1)S(1)}, bf16[1,1,128,512]{3,2,1,0:T(8,128)(2,1)S(1)}) custom-call(f32[3,8,128]{2,1,0:T(8,128)S(1)} %get-tuple-element.149.refs_0_.table_ref, f32[3,8,128]{2,1,0:T(8,128)S(1)} %get-tuple-element.107.refs_1_, bf16[3,2,128,512]{3,2,1,0:T(8,128)(2,1)S(1)} %copy-done, ...), custom_call_target="tpu_custom_call" | custom-call | flops 1 | bytes 1 | tf_op jit(solution)/shard_map/mix/pallas_call | solution.py:21
  20.9 2.3 %collective-permute-start.10 = (bf16[2,1,128,512]{3,2,1,0:T(8,128)(2,1)S(1)}, bf16[2,1,128,512]{3,2,1,0:T(8,128)(2,1)S(1)}, u32[]{:S(2)}, u32[]{:S(2)}) collective-permute-start(bf16[2,1,128,512]{3,2,1,0:T(8,128)(2,1)S(1)} %get-tuple-element.100), channel_id=1, source_target_pairs={{0,8},{4,12},{8,0},{12,4},{1,9},{5,13},{9,1},{13,5},{2,10},{6,14},... | collective-permute-start | bytes 786440 | tf_op jit(solution)/shard_map/ppermute | solution.py:81
  23.1 0.1 collective-permute-start.4
  23.2 1.9 %collective-permute-start.8 = (bf16[1,1,128,512]{3,2,1,0:T(8,128)(2,1)S(1)}, bf16[1,1,128,512]{3,2,1,0:T(8,128)(2,1)S(1)}, u32[]{:S(2)}, u32[]{:S(2)}) collective-permute-start(bf16[1,1,128,512]{3,2,1,0:T(8,128)(2,1)S(1)} %copy-done.4), channel_id=1, source_target_pairs={{16,0},{0,16},{17,1},{1,17},{18,2},{2,18},{19,3},{3,19},{20,4},{4,... | collective-permute-start | bytes 393224 | tf_op jit(solution)/shard_map/ppermute | solution.py:92
  25.2 1.9 %collective-permute-done.4.table_ref = f32[3,8,128]{2,1,0:T(8,128)S(1)} collective-permute-done((f32[3,8,128]{2,1,0:T(8,128)S(1)}, f32[3,8,128]{2,1,0:T(8,128)S(1)}, u32[]{:S(2)}, u32[]{:S(2)}) %collective-permute-start.4) | collective-permute-done | bytes 12320 | tf_op jit(solution)/shard_map/ppermute | solution.py:375
  27.1 0.4 partial_sums.1
  27.5 2.0 %collective-permute-start.15 = (bf16[1,2,1,144,512]{4,3,2,1,0:T(8,128)(2,1)S(1)}, bf16[1,2,1,144,512]{4,3,2,1,0:T(8,128)(2,1)S(1)}, u32[]{:S(2)}, u32[]{:S(2)}) collective-permute-start(bf16[1,2,1,144,512]{4,3,2,1,0:T(8,128)(2,1)S(1)} %get-tuple-element.103), channel_id=1, source_target_pairs={{16,0},{0,16},{17,1},{1,17},{18,2},{2,18},{19,3},{3,19},{20,4},{4,... | collective-permute-start | bytes 884744 | tf_op jit(solution)/shard_map/ppermute | solution.py:92
  29.5 0.1 collective-permute-done.8.refs_4_
  29.6 0.4 mix.3
  30.0 0.2 collective-permute-start.11
  30.2 0.4 collective-permute-start.12
  30.6 2.2 %collective-permute-start.9 = (bf16[1,1,128,512]{3,2,1,0:T(8,128)(2,1)S(1)}, bf16[1,1,128,512]{3,2,1,0:T(8,128)(2,1)S(1)}, u32[]{:S(2)}, u32[]{:S(2)}) collective-permute-start(bf16[1,1,128,512]{3,2,1,0:T(8,128)(2,1)S(1)} %get-tuple-element.101), channel_id=1, source_target_pairs={{0,8},{4,12},{8,0},{12,4},{1,9},{5,13},{9,1},{13,5},{2,10},{6,14},... | collective-permute-start | bytes 393224 | tf_op jit(solution)/shard_map/ppermute | solution.py:81
  32.8 1.8 %collective-permute-start.19 = (bf16[1,2,1,144,512]{4,3,2,1,0:T(8,128)(2,1)S(1)}, bf16[1,2,1,144,512]{4,3,2,1,0:T(8,128)(2,1)S(1)}, u32[]{:S(2)}, u32[]{:S(2)}) collective-permute-start(bf16[1,2,1,144,512]{4,3,2,1,0:T(8,128)(2,1)S(1)} %get-tuple-element.104), channel_id=1, source_target_pairs={{16,0},{0,16},{17,1},{1,17},{18,2},{2,18},{19,3},{3,19},{20,4},{4,... | collective-permute-start | bytes 884744 | tf_op jit(solution)/shard_map/ppermute | solution.py:92
  34.6 0.9 %product.4 = (bf16[2,1,128,512]{3,2,1,0:T(8,128)(2,1)S(1)}, bf16[2,1,144,512]{3,2,1,0:T(8,128)(2,1)S(1)}) custom-call(bf16[3,1,128,512]{3,2,1,0:T(8,128)(2,1)S(1)} %copy-done.2, bf16[3,1,128,512]{3,2,1,0:T(8,128)(2,1)S(1)} %get-tuple-element.163.refs_1_, bf16[3,1,128,512]{3,2,1,0:T(8,128)(2,1)S(1)} %collective-permute-done.1.refs_2_, ...), custom_call_target="tpu_custom_call" | custom-call | flops 1 | bytes 1 | tf_op jit(solution)/shard_map/product/pallas_call | solution.py:21
  35.5 0.1 collective-permute-start.22
  35.5 0.1 collective-permute-start.13
  35.6 1.8 %collective-permute-done.15.refs_2_ = bf16[1,2,1,144,512]{4,3,2,1,0:T(8,128)(2,1)S(1)} collective-permute-done((bf16[1,2,1,144,512]{4,3,2,1,0:T(8,128)(2,1)S(1)}, bf16[1,2,1,144,512]{4,3,2,1,0:T(8,128)(2,1)S(1)}, u32[]{:S(2)}, u32[]{:S(2)}) %collective-permute-start.15) | collective-permute-done | bytes 294944 | tf_op jit(solution)/shard_map/ppermute | solution.py:92
  37.5 0.2 add_partial.3
  37.7 0.1 collective-permute-start.16
  37.8 1.9 %collective-permute-start.23 = (bf16[1,2,1,128,512]{4,3,2,1,0:T(8,128)(2,1)S(1)}, bf16[1,2,1,128,512]{4,3,2,1,0:T(8,128)(2,1)S(1)}, u32[]{:S(2)}, u32[]{:S(2)}) collective-permute-start(bf16[1,2,1,128,512]{4,3,2,1,0:T(8,128)(2,1)S(1)} %get-tuple-element.105), channel_id=1, source_target_pairs={{16,0},{0,16},{17,1},{1,17},{18,2},{2,18},{19,3},{3,19},{20,4},{4,... | collective-permute-start | bytes 786440 | tf_op jit(solution)/shard_map/ppermute | solution.py:92
  39.7 0.2 collective-permute-start.17
  39.9 0.4 collective-permute-start.14
  40.2 0.8 %collective-permute-done.17.refs_11_ = bf16[1,1,128,512]{3,2,1,0:T(8,128)(2,1)S(1)} collective-permute-done((bf16[1,1,128,512]{3,2,1,0:T(8,128)(2,1)S(1)}, bf16[1,1,128,512]{3,2,1,0:T(8,128)(2,1)S(1)}, u32[]{:S(2)}, u32[]{:S(2)}) %collective-permute-start.17) | collective-permute-done | bytes 131104 | tf_op jit(solution)/shard_map/ppermute | solution.py:85
  41.1 0.2 collective-permute-done.14.refs_7_
  41.2 0.9 %product.5 = (bf16[2,1,128,512]{3,2,1,0:T(8,128)(2,1)S(1)}, bf16[2,1,128,512]{3,2,1,0:T(8,128)(2,1)S(1)}) custom-call(bf16[3,1,128,512]{3,2,1,0:T(8,128)(2,1)S(1)} %copy-done.2, bf16[3,1,128,512]{3,2,1,0:T(8,128)(2,1)S(1)} %get-tuple-element.163.refs_1_, bf16[3,1,128,512]{3,2,1,0:T(8,128)(2,1)S(1)} %collective-permute-done.1.refs_2_, ...), custom_call_target="tpu_custom_call" | custom-call | flops 1 | bytes 1 | tf_op jit(solution)/shard_map/product/pallas_call | solution.py:21
  42.1 2.3 %collective-permute-start.18 = (bf16[2,1,128,512]{3,2,1,0:T(8,128)(2,1)S(1)}, bf16[2,1,128,512]{3,2,1,0:T(8,128)(2,1)S(1)}, u32[]{:S(2)}, u32[]{:S(2)}) collective-permute-start(bf16[2,1,128,512]{3,2,1,0:T(8,128)(2,1)S(1)} %get-tuple-element.142), channel_id=1, source_target_pairs={{0,8},{4,12},{8,0},{12,4},{1,9},{5,13},{9,1},{13,5},{2,10},{6,14},... | collective-permute-start | bytes 786440 | tf_op jit(solution)/shard_map/ppermute | solution.py:81
  44.4 0.2 add_partial.4
  44.6 0.1 collective-permute-start.20
  44.7 0.5 collective-permute-start.21
  45.2 0.8 %place.7.refs_1_ = bf16[3,2,128,512]{3,2,1,0:T(8,128)(2,1)} custom-call(bf16[2,1,128,512]{3,2,1,0:T(8,128)(2,1)S(1)} %get-tuple-element.147.refs_0_, bf16[2,1,144,512]{3,2,1,0:T(8,128)(2,1)S(1)} %collective-permute-done.22.refs_1_), custom_call_target="tpu_custom_call" | custom-call | flops 1 | bytes 1 | tf_op jit(solution)/shard_map/place/pallas_call | solution.py:325
  46.0 3.1 %collective-permute-done.23.refs_2_ = bf16[1,2,1,128,512]{4,3,2,1,0:T(8,128)(2,1)S(1)} collective-permute-done((bf16[1,2,1,128,512]{4,3,2,1,0:T(8,128)(2,1)S(1)}, bf16[1,2,1,128,512]{4,3,2,1,0:T(8,128)(2,1)S(1)}, u32[]{:S(2)}, u32[]{:S(2)}) %collective-permute-start.23) | collective-permute-done | bytes 262176 | tf_op jit(solution)/shard_map/ppermute | solution.py:92
  49.1 0.2 add_partial.5
  49.3 0.1 collective-permute-start.24
  49.4 0.5 collective-permute-start.25
  49.9 0.5 product.6
  50.5 2.3 %collective-permute-start.27 = (bf16[1,1,128,512]{3,2,1,0:T(8,128)(2,1)S(1)}, bf16[1,1,128,512]{3,2,1,0:T(8,128)(2,1)S(1)}, u32[]{:S(2)}, u32[]{:S(2)}) collective-permute-start(bf16[1,1,128,512]{3,2,1,0:T(8,128)(2,1)S(1)} %get-tuple-element.161), channel_id=1, source_target_pairs={{0,8},{4,12},{8,0},{12,4},{1,9},{5,13},{9,1},{13,5},{2,10},{6,14},... | collective-permute-start | bytes 393224 | tf_op jit(solution)/shard_map/ppermute | solution.py:81
  52.7 0.5 product.7
  53.2 0.5 collective-permute-start.26
  53.7 0.7 %place.8.refs_1_ = bf16[3,2,128,512]{3,2,1,0:T(8,128)(2,1)} custom-call(bf16[2,1,128,512]{3,2,1,0:T(8,128)(2,1)S(1)} %get-tuple-element.173.refs_0_, bf16[3,2,128,512]{3,2,1,0:T(8,128)(2,1)} %place.7.refs_1_), custom_call_target="tpu_custom_call", output_to_operand_aliasing={{}: (1, {})} | custom-call | flops 1 | bytes 1 | tf_op jit(solution)/shard_map/place/pallas_call | solution.py:325
  54.4 0.8 %place.9.refs_1_ = bf16[3,2,128,512]{3,2,1,0:T(8,128)(2,1)} custom-call(bf16[2,1,128,512]{3,2,1,0:T(8,128)(2,1)S(1)} %get-tuple-element.173.refs_0_, bf16[1,1,128,512]{3,2,1,0:T(8,128)(2,1)S(1)} %get-tuple-element.174.refs_1_, bf16[1,1,128,512]{3,2,1,0:T(8,128)(2,1)S(1)} %get-tuple-element.175.refs_2_), custom_call_target="tpu_custom_call" | custom-call | flops 1 | bytes 1 | tf_op jit(solution)/shard_map/place/pallas_call | solution.py:325
  55.2 0.7 %place.10 = bf16[3,2,128,512]{3,2,1,0:T(8,128)(2,1)} custom-call(bf16[2,1,128,512]{3,2,1,0:T(8,128)(2,1)S(1)} %collective-permute-done.18.refs_0_, bf16[3,2,128,512]{3,2,1,0:T(8,128)(2,1)} %place.8.refs_1_), custom_call_target="tpu_custom_call", output_to_operand_aliasing={{}: (1, {})} | custom-call | flops 1 | bytes 1 | tf_op jit(solution)/shard_map/place/pallas_call | solution.py:325
  55.9 0.7 %place.11.refs_1_ = bf16[3,2,128,512]{3,2,1,0:T(8,128)(2,1)} custom-call(bf16[2,1,128,512]{3,2,1,0:T(8,128)(2,1)S(1)} %collective-permute-done.18.refs_0_, bf16[3,2,128,512]{3,2,1,0:T(8,128)(2,1)} %place.9.refs_1_), custom_call_target="tpu_custom_call", output_to_operand_aliasing={{}: (1, {})} | custom-call | flops 1 | bytes 1 | tf_op jit(solution)/shard_map/place/pallas_call | solution.py:325
  56.6 0.4 collective-permute-done.27.refs_0_
  57.0 0.7 %place.12.refs_1_ = bf16[3,2,128,512]{3,2,1,0:T(8,128)(2,1)} custom-call(bf16[1,1,128,512]{3,2,1,0:T(8,128)(2,1)S(1)} %collective-permute-done.27.refs_0_, bf16[3,2,128,512]{3,2,1,0:T(8,128)(2,1)} %place.11.refs_1_), custom_call_target="tpu_custom_call", output_to_operand_aliasing={{}: (1, {})} | custom-call | flops 1 | bytes 1 | tf_op jit(solution)/shard_map/place/pallas_call | solution.py:325
  57.7 1.6 %collective-permute-done.26.refs_0_ = bf16[1,1,128,512]{3,2,1,0:T(8,128)(2,1)S(1)} collective-permute-done((bf16[1,1,128,512]{3,2,1,0:T(8,128)(2,1)S(1)}, bf16[1,1,128,512]{3,2,1,0:T(8,128)(2,1)S(1)}, u32[]{:S(2)}, u32[]{:S(2)}) %collective-permute-start.26) | collective-permute-done | bytes 131104 | tf_op jit(solution)/shard_map/ppermute | solution.py:81
  59.3 0.7 %place.13 = bf16[3,2,128,512]{3,2,1,0:T(8,128)(2,1)} custom-call(bf16[1,1,128,512]{3,2,1,0:T(8,128)(2,1)S(1)} %collective-permute-done.26.refs_0_, bf16[3,2,128,512]{3,2,1,0:T(8,128)(2,1)} %place.12.refs_1_), custom_call_target="tpu_custom_call", output_to_operand_aliasing={{}: (1, {})} | custom-call | flops 1 | bytes 1 | tf_op jit(solution)/shard_map/place/pallas_call | solution.py:325
  (26 shorter events, 0.1 us)
Async XLA Ops:
  2.5 12.7 %collective-permute-start = (bf16[400,512]{1,0:T(8,128)(2,1)}, bf16[400,512]{1,0:T(8,128)(2,1)S(1)}, u32[]{:S(2)}, u32[]{:S(2)}) collective-permute-start(bf16[400,512]{1,0:T(8,128)(2,1)} %lead.1.refs_0_), channel_id=1, source_target_pairs={{0,8},{4,12},{8,0},{12,4},{1,9},{5,13},{9,1},{13,5},{2,10},{6,14},... | collective-permute-start | bytes 1228808 | tf_op jit(solution)/shard_map/ppermute | solution.py:81
  7.3 12.2 %collective-permute-start.5 = (bf16[3,1,128,512]{3,2,1,0:T(8,128)(2,1)}, bf16[3,1,128,512]{3,2,1,0:T(8,128)(2,1)}, u32[]{:S(2)}, u32[]{:S(2)}) collective-permute-start(bf16[3,1,128,512]{3,2,1,0:T(8,128)(2,1)} %cut.4), channel_id=1, source_target_pairs={{16,0},{0,16},{17,1},{1,17},{18,2},{2,18},{19,3},{3,19},{20,4},{4,... | collective-permute-start | bytes 1179656 | tf_op jit(solution)/shard_map/ppermute | solution.py:92
  10.6 4.6 %copy-start.3 = (bf16[400,512]{1,0:T(8,128)(2,1)S(1)}, bf16[400,512]{1,0:T(8,128)(2,1)}, u32[]{:S(2)}) copy-start(bf16[400,512]{1,0:T(8,128)(2,1)} %lead.1.refs_0_) | copy-start | bytes 1228804
  12.4 10.8 %collective-permute-start.1 = (bf16[3,1,128,512]{3,2,1,0:T(8,128)(2,1)}, bf16[3,1,128,512]{3,2,1,0:T(8,128)(2,1)S(1)}, u32[]{:S(2)}, u32[]{:S(2)}) collective-permute-start(bf16[3,1,128,512]{3,2,1,0:T(8,128)(2,1)} %cut.6.refs_0_), channel_id=1, source_target_pairs={{0,4},{4,0},{8,12},{12,8},{1,5},{5,1},{9,13},{13,9},{2,6},{6,2},{1... | collective-permute-start | bytes 1179656 | tf_op jit(solution)/shard_map/ppermute | solution.py:85
  12.5 14.6 %collective-permute-start.6 = (bf16[3,1,128,512]{3,2,1,0:T(8,128)(2,1)}, bf16[3,1,128,512]{3,2,1,0:T(8,128)(2,1)S(1)}, u32[]{:S(2)}, u32[]{:S(2)}) collective-permute-start(bf16[3,1,128,512]{3,2,1,0:T(8,128)(2,1)} %cut.5), channel_id=1, source_target_pairs={{0,8},{4,12},{8,0},{12,4},{1,9},{5,13},{9,1},{13,5},{2,10},{6,14},... | collective-permute-start | bytes 1179656 | tf_op jit(solution)/shard_map/ppermute | solution.py:81
  15.2 4.2 %copy-start = (bf16[3,2,128,512]{3,2,1,0:T(8,128)(2,1)S(1)}, bf16[3,2,128,512]{3,2,1,0:T(8,128)(2,1)}, u32[]{:S(2)}) copy-start(bf16[3,2,128,512]{3,2,1,0:T(8,128)(2,1)} %refs_2_.3) | copy-start | bytes 2359300
  15.2 1.9 %collective-permute-start.3 = (bf16[2,16,128]{2,1,0:T(8,128)(2,1)S(1)}, bf16[2,16,128]{2,1,0:T(8,128)(2,1)S(1)}, u32[]{:S(2)}, u32[]{:S(2)}) collective-permute-start(bf16[2,16,128]{2,1,0:T(8,128)(2,1)S(1)} %get-tuple-element.95.refs_0_), channel_id=1, source_target_pairs={{0,4},{4,0},{8,12},{12,8},{1,5},{5,1},{9,13},{13,9},{2,6},{6,2},{1... | collective-permute-start | bytes 24584 | tf_op jit(solution)/shard_map/ppermute | solution.py:85
  17.1 10.0 %copy-start.1 = (bf16[3,2,128,512]{3,2,1,0:T(8,128)(2,1)S(1)}, bf16[3,2,128,512]{3,2,1,0:T(8,128)(2,1)}, u32[]{:S(2)}) copy-start(bf16[3,2,128,512]{3,2,1,0:T(8,128)(2,1)} %refs_0_.11) | copy-start | bytes 2359300
  17.3 12.4 %collective-permute-start.7 = (bf16[2,1,128,512]{3,2,1,0:T(8,128)(2,1)}, bf16[2,1,128,512]{3,2,1,0:T(8,128)(2,1)S(1)}, u32[]{:S(2)}, u32[]{:S(2)}) collective-permute-start(bf16[2,1,128,512]{3,2,1,0:T(8,128)(2,1)} %get-tuple-element.112), channel_id=1, source_target_pairs={{16,0},{0,16},{17,1},{1,17},{18,2},{2,18},{19,3},{3,19},{20,4},{4,... | collective-permute-start | bytes 786440 | tf_op jit(solution)/shard_map/ppermute | solution.py:92
  19.5 3.8 %copy-start.4 = (bf16[1,1,128,512]{3,2,1,0:T(8,128)(2,1)S(1)}, bf16[1,1,128,512]{3,2,1,0:T(8,128)(2,1)}, u32[]{:S(2)}) copy-start(bf16[1,1,128,512]{3,2,1,0:T(8,128)(2,1)} %get-tuple-element.113) | copy-start | bytes 393220
  20.9 9.3 %collective-permute-start.10 = (bf16[2,1,128,512]{3,2,1,0:T(8,128)(2,1)S(1)}, bf16[2,1,128,512]{3,2,1,0:T(8,128)(2,1)S(1)}, u32[]{:S(2)}, u32[]{:S(2)}) collective-permute-start(bf16[2,1,128,512]{3,2,1,0:T(8,128)(2,1)S(1)} %get-tuple-element.100), channel_id=1, source_target_pairs={{0,8},{4,12},{8,0},{12,4},{1,9},{5,13},{9,1},{13,5},{2,10},{6,14},... | collective-permute-start | bytes 786440 | tf_op jit(solution)/shard_map/ppermute | solution.py:81
  23.1 4.0 %collective-permute-start.4 = (f32[3,8,128]{2,1,0:T(8,128)S(1)}, f32[3,8,128]{2,1,0:T(8,128)S(1)}, u32[]{:S(2)}, u32[]{:S(2)}) collective-permute-start(f32[3,8,128]{2,1,0:T(8,128)S(1)} %get-tuple-element.107.refs_1_), channel_id=1, source_target_pairs={{0,16},{16,0},{1,17},{17,1},{2,18},{18,2},{3,19},{19,3},{4,20},{20... | collective-permute-start | bytes 36872 | tf_op jit(solution)/shard_map/ppermute | solution.py:375
  23.2 6.4 %collective-permute-start.8 = (bf16[1,1,128,512]{3,2,1,0:T(8,128)(2,1)S(1)}, bf16[1,1,128,512]{3,2,1,0:T(8,128)(2,1)S(1)}, u32[]{:S(2)}, u32[]{:S(2)}) collective-permute-start(bf16[1,1,128,512]{3,2,1,0:T(8,128)(2,1)S(1)} %copy-done.4), channel_id=1, source_target_pairs={{16,0},{0,16},{17,1},{1,17},{18,2},{2,18},{19,3},{3,19},{20,4},{4,... | collective-permute-start | bytes 393224 | tf_op jit(solution)/shard_map/ppermute | solution.py:92
  27.1 5.7 %collective-permute-start.2 = (bf16[3,1,128,512]{3,2,1,0:T(8,128)(2,1)S(1)}, bf16[3,1,128,512]{3,2,1,0:T(8,128)(2,1)S(1)}, u32[]{:S(2)}, u32[]{:S(2)}) collective-permute-start(bf16[3,1,128,512]{3,2,1,0:T(8,128)(2,1)S(1)} %get-tuple-element.163.refs_1_), channel_id=1, source_target_pairs={{0,4},{4,0},{8,12},{12,8},{1,5},{5,1},{9,13},{13,9},{2,6},{6,2},{1... | collective-permute-start | bytes 1179656 | tf_op jit(solution)/shard_map/ppermute | solution.py:85
  27.5 9.9 %collective-permute-start.15 = (bf16[1,2,1,144,512]{4,3,2,1,0:T(8,128)(2,1)S(1)}, bf16[1,2,1,144,512]{4,3,2,1,0:T(8,128)(2,1)S(1)}, u32[]{:S(2)}, u32[]{:S(2)}) collective-permute-start(bf16[1,2,1,144,512]{4,3,2,1,0:T(8,128)(2,1)S(1)} %get-tuple-element.103), channel_id=1, source_target_pairs={{16,0},{0,16},{17,1},{1,17},{18,2},{2,18},{19,3},{3,19},{20,4},{4,... | collective-permute-start | bytes 884744 | tf_op jit(solution)/shard_map/ppermute | solution.py:92
  29.5 5.0 %copy-start.2 = (bf16[3,1,128,512]{3,2,1,0:T(8,128)(2,1)S(1)}, bf16[3,1,128,512]{3,2,1,0:T(8,128)(2,1)}, u32[]{:S(2)}) copy-start(bf16[3,1,128,512]{3,2,1,0:T(8,128)(2,1)} %cut.6.refs_0_) | copy-start | bytes 1179652
  30.0 4.5 %collective-permute-start.11 = (bf16[2,1,128,512]{3,2,1,0:T(8,128)(2,1)S(1)}, bf16[2,1,128,512]{3,2,1,0:T(8,128)(2,1)S(1)}, u32[]{:S(2)}, u32[]{:S(2)}) collective-permute-start(bf16[2,1,128,512]{3,2,1,0:T(8,128)(2,1)S(1)} %get-tuple-element.120.refs_4_), channel_id=1, source_target_pairs={{0,4},{4,0},{8,12},{12,8},{1,5},{5,1},{9,13},{13,9},{2,6},{6,2},{1... | collective-permute-start | bytes 786440 | tf_op jit(solution)/shard_map/ppermute | solution.py:85
  30.2 4.4 %collective-permute-start.12 = (bf16[2,1,128,512]{3,2,1,0:T(8,128)(2,1)S(1)}, bf16[2,1,128,512]{3,2,1,0:T(8,128)(2,1)S(1)}, u32[]{:S(2)}, u32[]{:S(2)}) collective-permute-start(bf16[2,1,128,512]{3,2,1,0:T(8,128)(2,1)S(1)} %collective-permute-done.10.refs_5_), channel_id=1, source_target_pairs={{0,4},{4,0},{8,12},{12,8},{1,5},{5,1},{9,13},{13,9},{2,6},{6,2},{1... | collective-permute-start | bytes 786440 | tf_op jit(solution)/shard_map/ppermute | solution.py:85
  30.6 7.2 %collective-permute-start.9 = (bf16[1,1,128,512]{3,2,1,0:T(8,128)(2,1)S(1)}, bf16[1,1,128,512]{3,2,1,0:T(8,128)(2,1)S(1)}, u32[]{:S(2)}, u32[]{:S(2)}) collective-permute-start(bf16[1,1,128,512]{3,2,1,0:T(8,128)(2,1)S(1)} %get-tuple-element.101), channel_id=1, source_target_pairs={{0,8},{4,12},{8,0},{12,4},{1,9},{5,13},{9,1},{13,5},{2,10},{6,14},... | collective-permute-start | bytes 393224 | tf_op jit(solution)/shard_map/ppermute | solution.py:81
  32.8 11.6 %collective-permute-start.19 = (bf16[1,2,1,144,512]{4,3,2,1,0:T(8,128)(2,1)S(1)}, bf16[1,2,1,144,512]{4,3,2,1,0:T(8,128)(2,1)S(1)}, u32[]{:S(2)}, u32[]{:S(2)}) collective-permute-start(bf16[1,2,1,144,512]{4,3,2,1,0:T(8,128)(2,1)S(1)} %get-tuple-element.104), channel_id=1, source_target_pairs={{16,0},{0,16},{17,1},{1,17},{18,2},{2,18},{19,3},{3,19},{20,4},{4,... | collective-permute-start | bytes 884744 | tf_op jit(solution)/shard_map/ppermute | solution.py:92
  35.5 9.7 %collective-permute-start.22 = (bf16[2,1,144,512]{3,2,1,0:T(8,128)(2,1)S(1)}, bf16[2,1,144,512]{3,2,1,0:T(8,128)(2,1)S(1)}, u32[]{:S(2)}, u32[]{:S(2)}) collective-permute-start(bf16[2,1,144,512]{3,2,1,0:T(8,128)(2,1)S(1)} %get-tuple-element.125), channel_id=1, source_target_pairs={{0,8},{4,12},{8,0},{12,4},{1,9},{5,13},{9,1},{13,5},{2,10},{6,14},... | collective-permute-start | bytes 884744 | tf_op jit(solution)/shard_map/ppermute | solution.py:81
  35.5 4.2 %collective-permute-start.13 = (bf16[1,1,128,512]{3,2,1,0:T(8,128)(2,1)S(1)}, bf16[1,1,128,512]{3,2,1,0:T(8,128)(2,1)S(1)}, u32[]{:S(2)}, u32[]{:S(2)}) collective-permute-start(bf16[1,1,128,512]{3,2,1,0:T(8,128)(2,1)S(1)} %get-tuple-element.134.refs_4_), channel_id=1, source_target_pairs={{0,4},{4,0},{8,12},{12,8},{1,5},{5,1},{9,13},{13,9},{2,6},{6,2},{1... | collective-permute-start | bytes 393224 | tf_op jit(solution)/shard_map/ppermute | solution.py:85
  37.7 2.2 %collective-permute-start.16 = (bf16[1,1,128,512]{3,2,1,0:T(8,128)(2,1)S(1)}, bf16[1,1,128,512]{3,2,1,0:T(8,128)(2,1)S(1)}, u32[]{:S(2)}, u32[]{:S(2)}) collective-permute-start(bf16[1,1,128,512]{3,2,1,0:T(8,128)(2,1)S(1)} %get-tuple-element.138.refs_8_), channel_id=1, source_target_pairs={{0,4},{4,0},{8,12},{12,8},{1,5},{5,1},{9,13},{13,9},{2,6},{6,2},{1... | collective-permute-start | bytes 393224 | tf_op jit(solution)/shard_map/ppermute | solution.py:85
  37.8 11.3 %collective-permute-start.23 = (bf16[1,2,1,128,512]{4,3,2,1,0:T(8,128)(2,1)S(1)}, bf16[1,2,1,128,512]{4,3,2,1,0:T(8,128)(2,1)S(1)}, u32[]{:S(2)}, u32[]{:S(2)}) collective-permute-start(bf16[1,2,1,128,512]{4,3,2,1,0:T(8,128)(2,1)S(1)} %get-tuple-element.105), channel_id=1, source_target_pairs={{16,0},{0,16},{17,1},{1,17},{18,2},{2,18},{19,3},{3,19},{20,4},{4,... | collective-permute-start | bytes 786440 | tf_op jit(solution)/shard_map/ppermute | solution.py:92
  39.7 1.3 %collective-permute-start.17 = (bf16[1,1,128,512]{3,2,1,0:T(8,128)(2,1)S(1)}, bf16[1,1,128,512]{3,2,1,0:T(8,128)(2,1)S(1)}, u32[]{:S(2)}, u32[]{:S(2)}) collective-permute-start(bf16[1,1,128,512]{3,2,1,0:T(8,128)(2,1)S(1)} %get-tuple-element.139.refs_9_), channel_id=1, source_target_pairs={{0,4},{4,0},{8,12},{12,8},{1,5},{5,1},{9,13},{13,9},{2,6},{6,2},{1... | collective-permute-start | bytes 393224 | tf_op jit(solution)/shard_map/ppermute | solution.py:85
  39.9 1.4 %collective-permute-start.14 = (bf16[1,1,128,512]{3,2,1,0:T(8,128)(2,1)S(1)}, bf16[1,1,128,512]{3,2,1,0:T(8,128)(2,1)S(1)}, u32[]{:S(2)}, u32[]{:S(2)}) collective-permute-start(bf16[1,1,128,512]{3,2,1,0:T(8,128)(2,1)S(1)} %collective-permute-done.9.refs_5_), channel_id=1, source_target_pairs={{0,4},{4,0},{8,12},{12,8},{1,5},{5,1},{9,13},{13,9},{2,6},{6,2},{1... | collective-permute-start | bytes 393224 | tf_op jit(solution)/shard_map/ppermute | solution.py:85
  42.1 13.1 %collective-permute-start.18 = (bf16[2,1,128,512]{3,2,1,0:T(8,128)(2,1)S(1)}, bf16[2,1,128,512]{3,2,1,0:T(8,128)(2,1)S(1)}, u32[]{:S(2)}, u32[]{:S(2)}) collective-permute-start(bf16[2,1,128,512]{3,2,1,0:T(8,128)(2,1)S(1)} %get-tuple-element.142), channel_id=1, source_target_pairs={{0,8},{4,12},{8,0},{12,4},{1,9},{5,13},{9,1},{13,5},{2,10},{6,14},... | collective-permute-start | bytes 786440 | tf_op jit(solution)/shard_map/ppermute | solution.py:81
  44.6 5.3 %collective-permute-start.20 = (bf16[1,1,128,512]{3,2,1,0:T(8,128)(2,1)S(1)}, bf16[1,1,128,512]{3,2,1,0:T(8,128)(2,1)S(1)}, u32[]{:S(2)}, u32[]{:S(2)}) collective-permute-start(bf16[1,1,128,512]{3,2,1,0:T(8,128)(2,1)S(1)} %get-tuple-element.156.refs_4_), channel_id=1, source_target_pairs={{0,4},{4,0},{8,12},{12,8},{1,5},{5,1},{9,13},{13,9},{2,6},{6,2},{1... | collective-permute-start | bytes 393224 | tf_op jit(solution)/shard_map/ppermute | solution.py:85
  44.7 5.2 %collective-permute-start.21 = (bf16[1,1,128,512]{3,2,1,0:T(8,128)(2,1)S(1)}, bf16[1,1,128,512]{3,2,1,0:T(8,128)(2,1)S(1)}, u32[]{:S(2)}, u32[]{:S(2)}) collective-permute-start(bf16[1,1,128,512]{3,2,1,0:T(8,128)(2,1)S(1)} %get-tuple-element.157.refs_5_), channel_id=1, source_target_pairs={{0,4},{4,0},{8,12},{12,8},{1,5},{5,1},{9,13},{13,9},{2,6},{6,2},{1... | collective-permute-start | bytes 393224 | tf_op jit(solution)/shard_map/ppermute | solution.py:85
  49.3 3.4 %collective-permute-start.24 = (bf16[1,1,128,512]{3,2,1,0:T(8,128)(2,1)S(1)}, bf16[1,1,128,512]{3,2,1,0:T(8,128)(2,1)S(1)}, u32[]{:S(2)}, u32[]{:S(2)}) collective-permute-start(bf16[1,1,128,512]{3,2,1,0:T(8,128)(2,1)S(1)} %get-tuple-element.166.refs_4_), channel_id=1, source_target_pairs={{0,4},{4,0},{8,12},{12,8},{1,5},{5,1},{9,13},{13,9},{2,6},{6,2},{1... | collective-permute-start | bytes 393224 | tf_op jit(solution)/shard_map/ppermute | solution.py:85
  49.4 3.3 %collective-permute-start.25 = (bf16[1,1,128,512]{3,2,1,0:T(8,128)(2,1)S(1)}, bf16[1,1,128,512]{3,2,1,0:T(8,128)(2,1)S(1)}, u32[]{:S(2)}, u32[]{:S(2)}) collective-permute-start(bf16[1,1,128,512]{3,2,1,0:T(8,128)(2,1)S(1)} %get-tuple-element.167.refs_5_), channel_id=1, source_target_pairs={{0,4},{4,0},{8,12},{12,8},{1,5},{5,1},{9,13},{13,9},{2,6},{6,2},{1... | collective-permute-start | bytes 393224 | tf_op jit(solution)/shard_map/ppermute | solution.py:85
  50.5 6.6 %collective-permute-start.27 = (bf16[1,1,128,512]{3,2,1,0:T(8,128)(2,1)S(1)}, bf16[1,1,128,512]{3,2,1,0:T(8,128)(2,1)S(1)}, u32[]{:S(2)}, u32[]{:S(2)}) collective-permute-start(bf16[1,1,128,512]{3,2,1,0:T(8,128)(2,1)S(1)} %get-tuple-element.161), channel_id=1, source_target_pairs={{0,8},{4,12},{8,0},{12,4},{1,9},{5,13},{9,1},{13,5},{2,10},{6,14},... | collective-permute-start | bytes 393224 | tf_op jit(solution)/shard_map/ppermute | solution.py:81
  53.2 6.0 %collective-permute-start.26 = (bf16[1,1,128,512]{3,2,1,0:T(8,128)(2,1)S(1)}, bf16[1,1,128,512]{3,2,1,0:T(8,128)(2,1)S(1)}, u32[]{:S(2)}, u32[]{:S(2)}) collective-permute-start(bf16[1,1,128,512]{3,2,1,0:T(8,128)(2,1)S(1)} %get-tuple-element.171), channel_id=1, source_target_pairs={{0,8},{4,12},{8,0},{12,4},{1,9},{5,13},{9,1},{13,5},{2,10},{6,14},... | collective-permute-start | bytes 393224 | tf_op jit(solution)/shard_map/ppermute | solution.py:81

commit v10 on v9

--- a/solution.py
+++ b/solution.py
@@ -236,7 +236,7 @@
                         chunks(r, body)
 
             (table,) = after([table], *earlier)
-            spare = [STEP] * (len(groups) - 1) + [0]
+            spare = [STEP] + [0] * (len(groups) - 1)
             shapes = [(len(group), owners, owned, r + x, o) for group, x in zip(groups, spare)]
             return call(kernel, shapes, "partial_sums", table, greater_in, *rows)
 
@@ -260,7 +260,7 @@
             shape = (len(group),) + block[1:]
             return call(kernel, [shape] * owners, "add_partial", table, greater_in, *rows, *received)
 
-        def product(jobs, earlier, pad=0):
+        def product(jobs, earlier):
             arrays = []
             for job in jobs:
                 for x, _ in [*job[0], *job[1]]:
@@ -276,25 +276,25 @@
                     for b in range(owned):
                         left = jnp.concatenate(
                             [
-                                jnp.concatenate([a[(*index, b, slice(0, r), at)] for at in spans], axis=1)
+                                jnp.concatenate([a[(*index, b, slice(None), at)] for at in spans], axis=1)
                                 for a, index in a_in[:owners]
                             ],
                             axis=0,
                         )
-                        right = jnp.concatenate([x[(*index, b, slice(0, r))] for x, index in s_in], axis=0)
+                        right = jnp.concatenate([x[(*index, b)] for x, index in s_in], axis=0)
                         half = jnp.dot(left, right, preferred_element_type=jnp.float32).astype(BF16)
                         full = lax.dot_general(
                             half,
-                            jnp.concatenate([a[(*index, b, slice(0, r))] for a, index in a_in], axis=0),
+                            jnp.concatenate([a[(*index, b)] for a, index in a_in], axis=0),
                             (((1,), (1,)), ((), ())),
                             preferred_element_type=jnp.float32,
                         ).astype(BF16)
                         for i in range(owners):
                             for j, at in enumerate(spans):
-                                outs[i][k, b, :r, at] = full[i * r : (i + 1) * r, j * r : (j + 1) * r]
-
-            shapes = [(len(jobs), owned, r + pad if d else r, o) for d in range(owners)]
-            return call(kernel, shapes, "product", *after(arrays, *earlier))
+                                outs[i][k, b, :, at] = full[i * r : (i + 1) * r, j * r : (j + 1) * r]
+
+            shape = (len(jobs),) + block[1:]
+            return call(kernel, [shape] * owners, "product", *after(arrays, *earlier))
 
         def back_to_rows(outs):
             return [outs[0]] + [to_owner(outs[d], owners - d) for d in others]
@@ -310,7 +310,7 @@
                 sems, out = refs[-1], refs[-2]
                 copies = [
                     pltpu.make_async_copy(
-                        refs[where[id(x)]].at[k, :, pl.ds(0, r)],
+                        refs[where[id(x)]].at[k],
                         out.at[n, pl.ds(owner_at(d) * owned, owned)],
                         sems.at[i],
                     )
@@ -356,10 +356,12 @@
         leads_from = [to_owner(x, d) for d, x in zip(others, leads)]
         lessers = cut([(lesser_in, d, 0, e) for d in others], leads)
         lesser_from = [[[from_energy(x, t)] for t in shifts] for x in lessers]
-        greaters = cut([(greater_in, d, 0, e) for d in others], lessers)
+        rest = cut(
+            [*((greater_in, d, 0, e) for d in others), (inverse, 0, 0, e), (lesser_in, 0, 0, e - 1), (lesser_in, 0, e - 1, 1)],
+            lessers,
+        )
+        greaters, inverse_own, lesser_own = rest[: owners - 1], rest[owners - 1], rest[owners:]
         greater_rows = [to_owner(x, d) for d, x in zip(others, greaters)]
-        (inverse_own,) = cut([(inverse, 0, 0, e)], greaters)
-        lesser_own = cut([(lesser_in, 0, n, k) for n, k in ((0, e - 1), (e - 1, 1))], [inverse_own])
 
         joined, *inverse_rows = call(
             join, [(owners, tail, LANES)] + [block] * len(others), "join", leads[0], *leads_from
@@ -429,9 +431,7 @@
         sigmas = {}
         steps = ["L0", "a0", "L1+G0"]
         for n in range(1, e):
-            steps.append(f"a{n}")
-            steps.append("pL0" if n == 1 else f"G{n - 1}")
-        steps.append(f"G{e - 1}")
+            steps += [f"a{n}", "pL0", f"G{n}"] if n == 1 else [f"a{n}", f"G{n}"]
         for step in steps:
             if step[0] == "p":
                 last = put(step[1], lambda part: len(step) < 3 or part[4] == int(step[2]), last)
@@ -454,7 +454,7 @@
                         sigma, beside = sigmas[g]
                         beside = [at(x, (i,)) for x in beside]
                         jobs.append((inverse_at(n), in_order((sigma[0], (i,)), at(sigma[1:], (i,)), beside)))
-            last = product(jobs, last, STEP if step == "L0" else 0)
+            last = product(jobs, last)
             back = back_to_rows(last)
             if step == "L0":
                 for rows, beside in zip(lesser_rows, lesser_rows_beside):

time: 60.2 us -> 59.3 us (0.985)
  Pallas kernels: 19.7 us -> 16.6 us
  waiting for transfers between devices: 12.2 us -> 14.2 us
    ppermute x8, waiting for transfers between devices: 4.13 us -> 7.45 us  [to_owner(): return lax.ppermute(x, 'ph', pairs)]
    pallas_call x5 -> x3, Pallas kernels: 8.99 us -> 5.87 us  [from_hbm(): pl.pallas_call(kernel, in_specs=[far] * len(args), out_specs=[WHOLE] * le...]
    ppermute x6, waiting for transfers between devices: 5.06 us -> 3.02 us  [from_energy(): return lax.ppermute(x, 'en', [((i + t) % en, i) for i in range(en)])]
    ppermute x6, starting transfers between devices: 11.4 us -> 10.5 us  [from_energy(): return lax.ppermute(x, 'en', [((i + t) % en, i) for i in range(en)])]
    ppermute x8, starting transfers between devices: 13.2 us -> 13.8 us  [to_owner(): return lax.ppermute(x, 'ph', pairs)]
  transfers between devices with their start and end apart: 28 -> 28, of which waited for: 9 -> 8; matrix products, arithmetic and copies ran while one was open for 0% -> 0% of each run, Pallas kernels for 29% -> 24%
where the time goes in v10:
time: 59.3 us; the launch traced here: 59.1 us
  starting transfers between devices  27.3 us (46%)
  Pallas kernels  16.6 us (28%)
  waiting for transfers between devices  14.2 us (24%)
  between operations  0.9 us (2%)
    ppermute x8, starting transfers between devices, to_owner(): return lax.ppermute(x, 'ph', pairs)  13.8 us
    ppermute x6, starting transfers between devices, from_energy(): return lax.ppermute(x, 'en', [((i + t) % en, i) for i in range(en)])  10.5 us
    ppermute x8, waiting for transfers between devices, to_owner(): return lax.ppermute(x, 'ph', pairs)  7.45 us
    pallas_call x3, Pallas kernels, from_hbm(): pl.pallas_call(kernel, in_specs=[far] * len(args), out_specs=[WHOLE] * le...  5.87 us
    pallas_call x12, Pallas kernels, call(): pl.pallas_call(kernel, in_specs=[WHOLE] * len(args), out_specs=[WHOLE] *...  5.8 us
    pallas_call x7, Pallas kernels, place(): pl.pallas_call(kernel, in_specs=[WHOLE] * len(arrays) + [far] * (result i...  4.95 us
    ppermute x6, waiting for transfers between devices, from_energy(): return lax.ppermute(x, 'en', [((i + t) % en, i) for i in range(en)])  3.02 us
    ppermute x1, waiting for transfers between devices, on_device(): lax.ppermute(table, 'en', [(i, (i + t) % en) for i in range(en)])  2.53 us
  transfers between devices with their start and end apart: 28, of which 8 were waited for; matrix products, arithmetic and copies ran while one was open for 0% of the time, Pallas kernels for 24%

profile of v10, /device:TPU:0, one launch (start us, length us, event | category | flops | bytes accessed | tf_op | source)
XLA Modules:
  0.0 59.1 jit_solution(13582897588204647077)
XLA Ops:
  0.6 1.9 %lead.1.refs_0_ = bf16[400,512]{1,0:T(8,128)(2,1)} custom-call(s32[2,3]{1,0:T(2,128)} %bitcast.2, f32[2,3]{1,0:T(2,128)} %bitcast.3, bf16[3,2,128,512]{3,2,1,0:T(8,128)(2,1)} %refs_1_), custom_call_target="tpu_custom_call" | custom-call | flops 1 | bytes 1 | tf_op jit(solution)/shard_map/lead/pallas_call | solution.py:153
  2.5 3.0 %collective-permute-start = (bf16[400,512]{1,0:T(8,128)(2,1)}, bf16[400,512]{1,0:T(8,128)(2,1)S(1)}, u32[]{:S(2)}, u32[]{:S(2)}) collective-permute-start(bf16[400,512]{1,0:T(8,128)(2,1)} %lead.1.refs_0_), channel_id=1, source_target_pairs={{0,8},{4,12},{8,0},{12,4},{1,9},{5,13},{9,1},{13,5},{2,10},{6,14},... | collective-permute-start | bytes 1228808 | tf_op jit(solution)/shard_map/ppermute | solution.py:81
  5.5 1.8 %cut.2 = bf16[3,1,128,512]{3,2,1,0:T(8,128)(2,1)} custom-call(bf16[3,2,128,512]{3,2,1,0:T(8,128)(2,1)} %refs_2_.4), custom_call_target="tpu_custom_call" | custom-call | flops 1 | bytes 1 | tf_op jit(solution)/shard_map/cut/pallas_call | solution.py:153
  7.3 0.0 copy-start.3
  7.3 1.6 %collective-permute-start.5 = (bf16[3,1,128,512]{3,2,1,0:T(8,128)(2,1)}, bf16[3,1,128,512]{3,2,1,0:T(8,128)(2,1)}, u32[]{:S(2)}, u32[]{:S(2)}) collective-permute-start(bf16[3,1,128,512]{3,2,1,0:T(8,128)(2,1)} %cut.2), channel_id=1, source_target_pairs={{16,0},{0,16},{17,1},{1,17},{18,2},{2,18},{19,3},{3,19},{20,4},{4,... | collective-permute-start | bytes 1179656 | tf_op jit(solution)/shard_map/ppermute | solution.py:92
  8.9 2.2 %cut.3 = (bf16[3,1,128,512]{3,2,1,0:T(8,128)(2,1)}, bf16[3,1,128,512]{3,2,1,0:T(8,128)(2,1)}, bf16[2,1,128,512]{3,2,1,0:T(8,128)(2,1)}, bf16[1,1,128,512]{3,2,1,0:T(8,128)(2,1)}) custom-call(bf16[3,2,128,512]{3,2,1,0:T(8,128)(2,1)} %refs_0_.9, bf16[3,2,128,512]{3,2,1,0:T(8,128)(2,1)} %refs_1_, bf16[3,2,128,512]{3,2,1,0:T(8,128)(2,1)} %refs_2_.4, ...), custom_call_target="tpu_custom_call" | custom-call | flops 1 | bytes 1 | tf_op jit(solution)/shard_map/cut/pallas_call | solution.py:153
  11.1 0.0 copy-start.1
  11.1 0.1 collective-permute-start.1
  11.2 0.6 collective-permute-start.6
  11.8 4.0 %collective-permute-done.refs_1_ = bf16[400,512]{1,0:T(8,128)(2,1)S(1)} collective-permute-done((bf16[400,512]{1,0:T(8,128)(2,1)}, bf16[400,512]{1,0:T(8,128)(2,1)S(1)}, u32[]{:S(2)}, u32[]{:S(2)}) %collective-permute-start) | collective-permute-done | bytes 409632 | tf_op jit(solution)/shard_map/ppermute | solution.py:81
  15.8 0.0 copy-start
  15.8 0.1 collective-permute-start.3
  15.9 1.2 %collective-permute-done.3.refs_1_ = bf16[2,16,128]{2,1,0:T(8,128)(2,1)S(1)} collective-permute-done((bf16[2,16,128]{2,1,0:T(8,128)(2,1)S(1)}, bf16[2,16,128]{2,1,0:T(8,128)(2,1)S(1)}, u32[]{:S(2)}, u32[]{:S(2)}) %collective-permute-start.3) | collective-permute-done | bytes 8224 | tf_op jit(solution)/shard_map/ppermute | solution.py:85
  17.1 0.1 weights.1
  17.2 2.3 %collective-permute-start.7 = (bf16[2,1,128,512]{3,2,1,0:T(8,128)(2,1)}, bf16[2,1,128,512]{3,2,1,0:T(8,128)(2,1)S(1)}, u32[]{:S(2)}, u32[]{:S(2)}) collective-permute-start(bf16[2,1,128,512]{3,2,1,0:T(8,128)(2,1)} %get-tuple-element.116), channel_id=1, source_target_pairs={{16,0},{0,16},{17,1},{1,17},{18,2},{2,18},{19,3},{3,19},{20,4},{4,... | collective-permute-start | bytes 786440 | tf_op jit(solution)/shard_map/ppermute | solution.py:92
  19.5 1.4 %mix.2 = (bf16[2,1,128,512]{3,2,1,0:T(8,128)(2,1)S(1)}, bf16[1,1,128,512]{3,2,1,0:T(8,128)(2,1)S(1)}) custom-call(f32[3,8,128]{2,1,0:T(8,128)S(1)} %get-tuple-element.163.refs_0_.table_ref, f32[3,8,128]{2,1,0:T(8,128)S(1)} %get-tuple-element.113.refs_1_, bf16[3,2,128,512]{3,2,1,0:T(8,128)(2,1)S(1)} %copy-done.1, ...), custom_call_target="tpu_custom_call" | custom-call | flops 1 | bytes 1 | tf_op jit(solution)/shard_map/mix/pallas_call | solution.py:21
  20.9 1.6 %collective-permute-start.10 = (bf16[2,1,128,512]{3,2,1,0:T(8,128)(2,1)S(1)}, bf16[2,1,128,512]{3,2,1,0:T(8,128)(2,1)S(1)}, u32[]{:S(2)}, u32[]{:S(2)}) collective-permute-start(bf16[2,1,128,512]{3,2,1,0:T(8,128)(2,1)S(1)} %get-tuple-element.105), channel_id=1, source_target_pairs={{0,8},{4,12},{8,0},{12,4},{1,9},{5,13},{9,1},{13,5},{2,10},{6,14},... | collective-permute-start | bytes 786440 | tf_op jit(solution)/shard_map/ppermute | solution.py:81
  22.5 0.5 collective-permute-start.4
  23.0 1.5 %collective-permute-start.8 = (bf16[1,1,128,512]{3,2,1,0:T(8,128)(2,1)S(1)}, bf16[1,1,128,512]{3,2,1,0:T(8,128)(2,1)S(1)}, u32[]{:S(2)}, u32[]{:S(2)}) collective-permute-start(bf16[1,1,128,512]{3,2,1,0:T(8,128)(2,1)S(1)} %copy-done.4), channel_id=1, source_target_pairs={{16,0},{0,16},{17,1},{1,17},{18,2},{2,18},{19,3},{3,19},{20,4},{4,... | collective-permute-start | bytes 393224 | tf_op jit(solution)/shard_map/ppermute | solution.py:92
  24.5 2.5 %collective-permute-done.4.table_ref = f32[3,8,128]{2,1,0:T(8,128)S(1)} collective-permute-done((f32[3,8,128]{2,1,0:T(8,128)S(1)}, f32[3,8,128]{2,1,0:T(8,128)S(1)}, u32[]{:S(2)}, u32[]{:S(2)}) %collective-permute-start.4) | collective-permute-done | bytes 12320 | tf_op jit(solution)/shard_map/ppermute | solution.py:377
  27.0 0.0 collective-permute-start.2
  27.0 0.0 collective-permute-done.6.refs_1_
  27.0 0.4 partial_sums.1
  27.4 2.1 %collective-permute-start.15 = (bf16[1,2,1,144,512]{4,3,2,1,0:T(8,128)(2,1)S(1)}, bf16[1,2,1,144,512]{4,3,2,1,0:T(8,128)(2,1)S(1)}, u32[]{:S(2)}, u32[]{:S(2)}) collective-permute-start(bf16[1,2,1,144,512]{4,3,2,1,0:T(8,128)(2,1)S(1)} %get-tuple-element.109), channel_id=1, source_target_pairs={{16,0},{0,16},{17,1},{1,17},{18,2},{2,18},{19,3},{3,19},{20,4},{4,... | collective-permute-start | bytes 884744 | tf_op jit(solution)/shard_map/ppermute | solution.py:92
  29.6 0.0 collective-permute-done.8.refs_4_
  29.6 0.0 collective-permute-done.7.refs_3_
  29.6 0.4 mix.3
  30.0 0.3 collective-permute-start.11
  30.2 0.0 collective-permute-done.10.refs_5_
  30.2 0.3 collective-permute-start.12
  30.5 1.6 %collective-permute-start.9 = (bf16[1,1,128,512]{3,2,1,0:T(8,128)(2,1)S(1)}, bf16[1,1,128,512]{3,2,1,0:T(8,128)(2,1)S(1)}, u32[]{:S(2)}, u32[]{:S(2)}) collective-permute-start(bf16[1,1,128,512]{3,2,1,0:T(8,128)(2,1)S(1)} %get-tuple-element.106), channel_id=1, source_target_pairs={{0,8},{4,12},{8,0},{12,4},{1,9},{5,13},{9,1},{13,5},{2,10},{6,14},... | collective-permute-start | bytes 393224 | tf_op jit(solution)/shard_map/ppermute | solution.py:81
  32.1 0.0 collective-permute-done.2.refs_3_
  32.1 1.6 %collective-permute-start.19 = (bf16[1,2,1,128,512]{4,3,2,1,0:T(8,128)(2,1)S(1)}, bf16[1,2,1,128,512]{4,3,2,1,0:T(8,128)(2,1)S(1)}, u32[]{:S(2)}, u32[]{:S(2)}) collective-permute-start(bf16[1,2,1,128,512]{4,3,2,1,0:T(8,128)(2,1)S(1)} %get-tuple-element.110), channel_id=1, source_target_pairs={{16,0},{0,16},{17,1},{1,17},{18,2},{2,18},{19,3},{3,19},{20,4},{4,... | collective-permute-start | bytes 786440 | tf_op jit(solution)/shard_map/ppermute | solution.py:92
  33.7 0.9 %product.4 = (bf16[2,1,128,512]{3,2,1,0:T(8,128)(2,1)S(1)}, bf16[2,1,128,512]{3,2,1,0:T(8,128)(2,1)S(1)}) custom-call(bf16[3,1,128,512]{3,2,1,0:T(8,128)(2,1)S(1)} %copy-done.2, bf16[3,1,128,512]{3,2,1,0:T(8,128)(2,1)S(1)} %get-tuple-element.167.refs_1_, bf16[3,1,128,512]{3,2,1,0:T(8,128)(2,1)S(1)} %collective-permute-done.1.refs_2_, ...), custom_call_target="tpu_custom_call" | custom-call | flops 1 | bytes 1 | tf_op jit(solution)/shard_map/product/pallas_call | solution.py:21
  34.6 2.9 %collective-permute-done.15.refs_2_ = bf16[1,2,1,144,512]{4,3,2,1,0:T(8,128)(2,1)S(1)} collective-permute-done((bf16[1,2,1,144,512]{4,3,2,1,0:T(8,128)(2,1)S(1)}, bf16[1,2,1,144,512]{4,3,2,1,0:T(8,128)(2,1)S(1)}, u32[]{:S(2)}, u32[]{:S(2)}) %collective-permute-start.15) | collective-permute-done | bytes 294944 | tf_op jit(solution)/shard_map/ppermute | solution.py:92
  37.4 0.2 add_partial.3
  37.6 0.1 collective-permute-start.16
  37.7 0.5 collective-permute-start.17
  38.2 0.1 collective-permute-start.14
  38.3 2.0 %collective-permute-start.22 = (bf16[2,1,128,512]{3,2,1,0:T(8,128)(2,1)S(1)}, bf16[2,1,128,512]{3,2,1,0:T(8,128)(2,1)S(1)}, u32[]{:S(2)}, u32[]{:S(2)}) collective-permute-start(bf16[2,1,128,512]{3,2,1,0:T(8,128)(2,1)S(1)} %get-tuple-element.129), channel_id=1, source_target_pairs={{0,8},{4,12},{8,0},{12,4},{1,9},{5,13},{9,1},{13,5},{2,10},{6,14},... | collective-permute-start | bytes 786440 | tf_op jit(solution)/shard_map/ppermute | solution.py:81
  40.3 1.5 %collective-permute-start.23 = (bf16[1,2,1,128,512]{4,3,2,1,0:T(8,128)(2,1)S(1)}, bf16[1,2,1,128,512]{4,3,2,1,0:T(8,128)(2,1)S(1)}, u32[]{:S(2)}, u32[]{:S(2)}) collective-permute-start(bf16[1,2,1,128,512]{4,3,2,1,0:T(8,128)(2,1)S(1)} %get-tuple-element.111), channel_id=1, source_target_pairs={{16,0},{0,16},{17,1},{1,17},{18,2},{2,18},{19,3},{3,19},{20,4},{4,... | collective-permute-start | bytes 786440 | tf_op jit(solution)/shard_map/ppermute | solution.py:92
  41.8 0.9 %product.5 = (bf16[2,1,128,512]{3,2,1,0:T(8,128)(2,1)S(1)}, bf16[2,1,128,512]{3,2,1,0:T(8,128)(2,1)S(1)}) custom-call(bf16[3,1,128,512]{3,2,1,0:T(8,128)(2,1)S(1)} %copy-done.2, bf16[3,1,128,512]{3,2,1,0:T(8,128)(2,1)S(1)} %get-tuple-element.167.refs_1_, bf16[3,1,128,512]{3,2,1,0:T(8,128)(2,1)S(1)} %collective-permute-done.1.refs_2_, ...), custom_call_target="tpu_custom_call" | custom-call | flops 1 | bytes 1 | tf_op jit(solution)/shard_map/product/pallas_call | solution.py:21
  42.7 0.2 collective-permute-done.19.refs_2_
  42.8 0.2 add_partial.4
  43.1 0.1 collective-permute-start.20
  43.1 0.5 collective-permute-start.21
  43.6 2.2 %collective-permute-start.18 = (bf16[2,1,128,512]{3,2,1,0:T(8,128)(2,1)S(1)}, bf16[2,1,128,512]{3,2,1,0:T(8,128)(2,1)S(1)}, u32[]{:S(2)}, u32[]{:S(2)}) collective-permute-start(bf16[2,1,128,512]{3,2,1,0:T(8,128)(2,1)S(1)} %get-tuple-element.146), channel_id=1, source_target_pairs={{0,8},{4,12},{8,0},{12,4},{1,9},{5,13},{9,1},{13,5},{2,10},{6,14},... | collective-permute-start | bytes 786440 | tf_op jit(solution)/shard_map/ppermute | solution.py:81
  45.8 1.7 %collective-permute-done.22.refs_1_ = bf16[2,1,128,512]{3,2,1,0:T(8,128)(2,1)S(1)} collective-permute-done((bf16[2,1,128,512]{3,2,1,0:T(8,128)(2,1)S(1)}, bf16[2,1,128,512]{3,2,1,0:T(8,128)(2,1)S(1)}, u32[]{:S(2)}, u32[]{:S(2)}) %collective-permute-start.22) | collective-permute-done | bytes 262176 | tf_op jit(solution)/shard_map/ppermute | solution.py:81
  47.5 0.8 %place.7.refs_1_ = bf16[3,2,128,512]{3,2,1,0:T(8,128)(2,1)} custom-call(bf16[2,1,128,512]{3,2,1,0:T(8,128)(2,1)S(1)} %get-tuple-element.151.refs_0_, bf16[2,1,128,512]{3,2,1,0:T(8,128)(2,1)S(1)} %collective-permute-done.22.refs_1_), custom_call_target="tpu_custom_call" | custom-call | flops 1 | bytes 1 | tf_op jit(solution)/shard_map/place/pallas_call | solution.py:325
  48.3 0.5 product.6
  48.9 0.2 add_partial.5
  49.1 0.1 collective-permute-start.24
  49.2 0.5 collective-permute-start.25
  49.7 1.8 %collective-permute-start.27 = (bf16[1,1,128,512]{3,2,1,0:T(8,128)(2,1)S(1)}, bf16[1,1,128,512]{3,2,1,0:T(8,128)(2,1)S(1)}, u32[]{:S(2)}, u32[]{:S(2)}) collective-permute-start(bf16[1,1,128,512]{3,2,1,0:T(8,128)(2,1)S(1)} %get-tuple-element.162), channel_id=1, source_target_pairs={{0,8},{4,12},{8,0},{12,4},{1,9},{5,13},{9,1},{13,5},{2,10},{6,14},... | collective-permute-start | bytes 393224 | tf_op jit(solution)/shard_map/ppermute | solution.py:81
  51.5 0.5 product.7
  52.0 1.1 %collective-permute-start.26 = (bf16[1,1,128,512]{3,2,1,0:T(8,128)(2,1)S(1)}, bf16[1,1,128,512]{3,2,1,0:T(8,128)(2,1)S(1)}, u32[]{:S(2)}, u32[]{:S(2)}) collective-permute-start(bf16[1,1,128,512]{3,2,1,0:T(8,128)(2,1)S(1)} %get-tuple-element.175), channel_id=1, source_target_pairs={{0,8},{4,12},{8,0},{12,4},{1,9},{5,13},{9,1},{13,5},{2,10},{6,14},... | collective-permute-start | bytes 393224 | tf_op jit(solution)/shard_map/ppermute | solution.py:81
  53.1 0.7 %place.8.refs_1_ = bf16[3,2,128,512]{3,2,1,0:T(8,128)(2,1)} custom-call(bf16[2,1,128,512]{3,2,1,0:T(8,128)(2,1)S(1)} %get-tuple-element.177.refs_0_, bf16[3,2,128,512]{3,2,1,0:T(8,128)(2,1)} %place.7.refs_1_), custom_call_target="tpu_custom_call", output_to_operand_aliasing={{}: (1, {})} | custom-call | flops 1 | bytes 1 | tf_op jit(solution)/shard_map/place/pallas_call | solution.py:325
  53.8 0.8 %place.9.refs_1_ = bf16[3,2,128,512]{3,2,1,0:T(8,128)(2,1)} custom-call(bf16[2,1,128,512]{3,2,1,0:T(8,128)(2,1)S(1)} %get-tuple-element.177.refs_0_, bf16[1,1,128,512]{3,2,1,0:T(8,128)(2,1)S(1)} %get-tuple-element.178.refs_1_, bf16[1,1,128,512]{3,2,1,0:T(8,128)(2,1)S(1)} %get-tuple-element.179.refs_2_), custom_call_target="tpu_custom_call" | custom-call | flops 1 | bytes 1 | tf_op jit(solution)/shard_map/place/pallas_call | solution.py:325
  54.6 0.7 %place.10 = bf16[3,2,128,512]{3,2,1,0:T(8,128)(2,1)} custom-call(bf16[2,1,128,512]{3,2,1,0:T(8,128)(2,1)S(1)} %collective-permute-done.18.refs_0_, bf16[3,2,128,512]{3,2,1,0:T(8,128)(2,1)} %place.8.refs_1_), custom_call_target="tpu_custom_call", output_to_operand_aliasing={{}: (1, {})} | custom-call | flops 1 | bytes 1 | tf_op jit(solution)/shard_map/place/pallas_call | solution.py:325
  55.3 0.7 %place.11.refs_1_ = bf16[3,2,128,512]{3,2,1,0:T(8,128)(2,1)} custom-call(bf16[2,1,128,512]{3,2,1,0:T(8,128)(2,1)S(1)} %collective-permute-done.18.refs_0_, bf16[3,2,128,512]{3,2,1,0:T(8,128)(2,1)} %place.9.refs_1_), custom_call_target="tpu_custom_call", output_to_operand_aliasing={{}: (1, {})} | custom-call | flops 1 | bytes 1 | tf_op jit(solution)/shard_map/place/pallas_call | solution.py:325
  56.0 0.1 collective-permute-done.27.refs_0_
  56.1 0.7 %place.12.refs_1_ = bf16[3,2,128,512]{3,2,1,0:T(8,128)(2,1)} custom-call(bf16[1,1,128,512]{3,2,1,0:T(8,128)(2,1)S(1)} %collective-permute-done.27.refs_0_, bf16[3,2,128,512]{3,2,1,0:T(8,128)(2,1)} %place.11.refs_1_), custom_call_target="tpu_custom_call", output_to_operand_aliasing={{}: (1, {})} | custom-call | flops 1 | bytes 1 | tf_op jit(solution)/shard_map/place/pallas_call | solution.py:325
  56.8 1.6 %collective-permute-done.26.refs_0_ = bf16[1,1,128,512]{3,2,1,0:T(8,128)(2,1)S(1)} collective-permute-done((bf16[1,1,128,512]{3,2,1,0:T(8,128)(2,1)S(1)}, bf16[1,1,128,512]{3,2,1,0:T(8,128)(2,1)S(1)}, u32[]{:S(2)}, u32[]{:S(2)}) %collective-permute-start.26) | collective-permute-done | bytes 131104 | tf_op jit(solution)/shard_map/ppermute | solution.py:81
  58.4 0.7 %place.13 = bf16[3,2,128,512]{3,2,1,0:T(8,128)(2,1)} custom-call(bf16[1,1,128,512]{3,2,1,0:T(8,128)(2,1)S(1)} %collective-permute-done.26.refs_0_, bf16[3,2,128,512]{3,2,1,0:T(8,128)(2,1)} %place.12.refs_1_), custom_call_target="tpu_custom_call", output_to_operand_aliasing={{}: (1, {})} | custom-call | flops 1 | bytes 1 | tf_op jit(solution)/shard_map/place/pallas_call | solution.py:325
  (24 shorter events, 0.1 us)
Async XLA Ops:
  2.5 13.3 %collective-permute-start = (bf16[400,512]{1,0:T(8,128)(2,1)}, bf16[400,512]{1,0:T(8,128)(2,1)S(1)}, u32[]{:S(2)}, u32[]{:S(2)}) collective-permute-start(bf16[400,512]{1,0:T(8,128)(2,1)} %lead.1.refs_0_), channel_id=1, source_target_pairs={{0,8},{4,12},{8,0},{12,4},{1,9},{5,13},{9,1},{13,5},{2,10},{6,14},... | collective-permute-start | bytes 1228808 | tf_op jit(solution)/shard_map/ppermute | solution.py:81
  7.3 8.5 %copy-start.3 = (bf16[400,512]{1,0:T(8,128)(2,1)S(1)}, bf16[400,512]{1,0:T(8,128)(2,1)}, u32[]{:S(2)}) copy-start(bf16[400,512]{1,0:T(8,128)(2,1)} %lead.1.refs_0_) | copy-start | bytes 1228804
  7.3 12.1 %collective-permute-start.5 = (bf16[3,1,128,512]{3,2,1,0:T(8,128)(2,1)}, bf16[3,1,128,512]{3,2,1,0:T(8,128)(2,1)}, u32[]{:S(2)}, u32[]{:S(2)}) collective-permute-start(bf16[3,1,128,512]{3,2,1,0:T(8,128)(2,1)} %cut.2), channel_id=1, source_target_pairs={{16,0},{0,16},{17,1},{1,17},{18,2},{2,18},{19,3},{3,19},{20,4},{4,... | collective-permute-start | bytes 1179656 | tf_op jit(solution)/shard_map/ppermute | solution.py:92
  11.1 8.3 %copy-start.1 = (bf16[3,2,128,512]{3,2,1,0:T(8,128)(2,1)S(1)}, bf16[3,2,128,512]{3,2,1,0:T(8,128)(2,1)}, u32[]{:S(2)}) copy-start(bf16[3,2,128,512]{3,2,1,0:T(8,128)(2,1)} %refs_2_.4) | copy-start | bytes 2359300
  11.1 11.8 %collective-permute-start.1 = (bf16[3,1,128,512]{3,2,1,0:T(8,128)(2,1)}, bf16[3,1,128,512]{3,2,1,0:T(8,128)(2,1)S(1)}, u32[]{:S(2)}, u32[]{:S(2)}) collective-permute-start(bf16[3,1,128,512]{3,2,1,0:T(8,128)(2,1)} %get-tuple-element.166.refs_0_), channel_id=1, source_target_pairs={{0,4},{4,0},{8,12},{12,8},{1,5},{5,1},{9,13},{13,9},{2,6},{6,2},{1... | collective-permute-start | bytes 1179656 | tf_op jit(solution)/shard_map/ppermute | solution.py:85
  11.2 15.8 %collective-permute-start.6 = (bf16[3,1,128,512]{3,2,1,0:T(8,128)(2,1)}, bf16[3,1,128,512]{3,2,1,0:T(8,128)(2,1)S(1)}, u32[]{:S(2)}, u32[]{:S(2)}) collective-permute-start(bf16[3,1,128,512]{3,2,1,0:T(8,128)(2,1)} %get-tuple-element.108), channel_id=1, source_target_pairs={{0,8},{4,12},{8,0},{12,4},{1,9},{5,13},{9,1},{13,5},{2,10},{6,14},... | collective-permute-start | bytes 1179656 | tf_op jit(solution)/shard_map/ppermute | solution.py:81
  15.8 11.2 %copy-start = (bf16[3,2,128,512]{3,2,1,0:T(8,128)(2,1)S(1)}, bf16[3,2,128,512]{3,2,1,0:T(8,128)(2,1)}, u32[]{:S(2)}) copy-start(bf16[3,2,128,512]{3,2,1,0:T(8,128)(2,1)} %refs_0_.9) | copy-start | bytes 2359300
  15.8 1.2 %collective-permute-start.3 = (bf16[2,16,128]{2,1,0:T(8,128)(2,1)S(1)}, bf16[2,16,128]{2,1,0:T(8,128)(2,1)S(1)}, u32[]{:S(2)}, u32[]{:S(2)}) collective-permute-start(bf16[2,16,128]{2,1,0:T(8,128)(2,1)S(1)} %get-tuple-element.100.refs_0_), channel_id=1, source_target_pairs={{0,4},{4,0},{8,12},{12,8},{1,5},{5,1},{9,13},{13,9},{2,6},{6,2},{1... | collective-permute-start | bytes 24584 | tf_op jit(solution)/shard_map/ppermute | solution.py:85
  17.2 12.4 %collective-permute-start.7 = (bf16[2,1,128,512]{3,2,1,0:T(8,128)(2,1)}, bf16[2,1,128,512]{3,2,1,0:T(8,128)(2,1)S(1)}, u32[]{:S(2)}, u32[]{:S(2)}) collective-permute-start(bf16[2,1,128,512]{3,2,1,0:T(8,128)(2,1)} %get-tuple-element.116), channel_id=1, source_target_pairs={{16,0},{0,16},{17,1},{1,17},{18,2},{2,18},{19,3},{3,19},{20,4},{4,... | collective-permute-start | bytes 786440 | tf_op jit(solution)/shard_map/ppermute | solution.py:92
  19.5 3.5 %copy-start.4 = (bf16[1,1,128,512]{3,2,1,0:T(8,128)(2,1)S(1)}, bf16[1,1,128,512]{3,2,1,0:T(8,128)(2,1)}, u32[]{:S(2)}) copy-start(bf16[1,1,128,512]{3,2,1,0:T(8,128)(2,1)} %get-tuple-element.117) | copy-start | bytes 393220
  20.9 9.4 %collective-permute-start.10 = (bf16[2,1,128,512]{3,2,1,0:T(8,128)(2,1)S(1)}, bf16[2,1,128,512]{3,2,1,0:T(8,128)(2,1)S(1)}, u32[]{:S(2)}, u32[]{:S(2)}) collective-permute-start(bf16[2,1,128,512]{3,2,1,0:T(8,128)(2,1)S(1)} %get-tuple-element.105), channel_id=1, source_target_pairs={{0,8},{4,12},{8,0},{12,4},{1,9},{5,13},{9,1},{13,5},{2,10},{6,14},... | collective-permute-start | bytes 786440 | tf_op jit(solution)/shard_map/ppermute | solution.py:81
  22.5 4.6 %collective-permute-start.4 = (f32[3,8,128]{2,1,0:T(8,128)S(1)}, f32[3,8,128]{2,1,0:T(8,128)S(1)}, u32[]{:S(2)}, u32[]{:S(2)}) collective-permute-start(f32[3,8,128]{2,1,0:T(8,128)S(1)} %get-tuple-element.113.refs_1_), channel_id=1, source_target_pairs={{0,16},{16,0},{1,17},{17,1},{2,18},{18,2},{3,19},{19,3},{4,20},{20... | collective-permute-start | bytes 36872 | tf_op jit(solution)/shard_map/ppermute | solution.py:377
  23.0 6.6 %collective-permute-start.8 = (bf16[1,1,128,512]{3,2,1,0:T(8,128)(2,1)S(1)}, bf16[1,1,128,512]{3,2,1,0:T(8,128)(2,1)S(1)}, u32[]{:S(2)}, u32[]{:S(2)}) collective-permute-start(bf16[1,1,128,512]{3,2,1,0:T(8,128)(2,1)S(1)} %copy-done.4), channel_id=1, source_target_pairs={{16,0},{0,16},{17,1},{1,17},{18,2},{2,18},{19,3},{3,19},{20,4},{4,... | collective-permute-start | bytes 393224 | tf_op jit(solution)/shard_map/ppermute | solution.py:92
  27.0 5.1 %collective-permute-start.2 = (bf16[3,1,128,512]{3,2,1,0:T(8,128)(2,1)S(1)}, bf16[3,1,128,512]{3,2,1,0:T(8,128)(2,1)S(1)}, u32[]{:S(2)}, u32[]{:S(2)}) collective-permute-start(bf16[3,1,128,512]{3,2,1,0:T(8,128)(2,1)S(1)} %get-tuple-element.167.refs_1_), channel_id=1, source_target_pairs={{0,4},{4,0},{8,12},{12,8},{1,5},{5,1},{9,13},{13,9},{2,6},{6,2},{1... | collective-permute-start | bytes 1179656 | tf_op jit(solution)/shard_map/ppermute | solution.py:85
  27.4 10.0 %collective-permute-start.15 = (bf16[1,2,1,144,512]{4,3,2,1,0:T(8,128)(2,1)S(1)}, bf16[1,2,1,144,512]{4,3,2,1,0:T(8,128)(2,1)S(1)}, u32[]{:S(2)}, u32[]{:S(2)}) collective-permute-start(bf16[1,2,1,144,512]{4,3,2,1,0:T(8,128)(2,1)S(1)} %get-tuple-element.109), channel_id=1, source_target_pairs={{16,0},{0,16},{17,1},{1,17},{18,2},{2,18},{19,3},{3,19},{20,4},{4,... | collective-permute-start | bytes 884744 | tf_op jit(solution)/shard_map/ppermute | solution.py:92
  29.6 4.1 %copy-start.2 = (bf16[3,1,128,512]{3,2,1,0:T(8,128)(2,1)S(1)}, bf16[3,1,128,512]{3,2,1,0:T(8,128)(2,1)}, u32[]{:S(2)}) copy-start(bf16[3,1,128,512]{3,2,1,0:T(8,128)(2,1)} %get-tuple-element.166.refs_0_) | copy-start | bytes 1179652
  30.0 2.2 %collective-permute-start.11 = (bf16[2,1,128,512]{3,2,1,0:T(8,128)(2,1)S(1)}, bf16[2,1,128,512]{3,2,1,0:T(8,128)(2,1)S(1)}, u32[]{:S(2)}, u32[]{:S(2)}) collective-permute-start(bf16[2,1,128,512]{3,2,1,0:T(8,128)(2,1)S(1)} %get-tuple-element.124.refs_4_), channel_id=1, source_target_pairs={{0,4},{4,0},{8,12},{12,8},{1,5},{5,1},{9,13},{13,9},{2,6},{6,2},{1... | collective-permute-start | bytes 786440 | tf_op jit(solution)/shard_map/ppermute | solution.py:85
  30.2 3.4 %collective-permute-start.12 = (bf16[2,1,128,512]{3,2,1,0:T(8,128)(2,1)S(1)}, bf16[2,1,128,512]{3,2,1,0:T(8,128)(2,1)S(1)}, u32[]{:S(2)}, u32[]{:S(2)}) collective-permute-start(bf16[2,1,128,512]{3,2,1,0:T(8,128)(2,1)S(1)} %collective-permute-done.10.refs_5_), channel_id=1, source_target_pairs={{0,4},{4,0},{8,12},{12,8},{1,5},{5,1},{9,13},{13,9},{2,6},{6,2},{1... | collective-permute-start | bytes 786440 | tf_op jit(solution)/shard_map/ppermute | solution.py:85
  30.5 7.7 %collective-permute-start.9 = (bf16[1,1,128,512]{3,2,1,0:T(8,128)(2,1)S(1)}, bf16[1,1,128,512]{3,2,1,0:T(8,128)(2,1)S(1)}, u32[]{:S(2)}, u32[]{:S(2)}) collective-permute-start(bf16[1,1,128,512]{3,2,1,0:T(8,128)(2,1)S(1)} %get-tuple-element.106), channel_id=1, source_target_pairs={{0,8},{4,12},{8,0},{12,4},{1,9},{5,13},{9,1},{13,5},{2,10},{6,14},... | collective-permute-start | bytes 393224 | tf_op jit(solution)/shard_map/ppermute | solution.py:81
  32.1 6.2 %collective-permute-start.13 = (bf16[1,1,128,512]{3,2,1,0:T(8,128)(2,1)S(1)}, bf16[1,1,128,512]{3,2,1,0:T(8,128)(2,1)S(1)}, u32[]{:S(2)}, u32[]{:S(2)}) collective-permute-start(bf16[1,1,128,512]{3,2,1,0:T(8,128)(2,1)S(1)} %get-tuple-element.138.refs_4_), channel_id=1, source_target_pairs={{0,4},{4,0},{8,12},{12,8},{1,5},{5,1},{9,13},{13,9},{2,6},{6,2},{1... | collective-permute-start | bytes 393224 | tf_op jit(solution)/shard_map/ppermute | solution.py:85
  32.1 10.7 %collective-permute-start.19 = (bf16[1,2,1,128,512]{4,3,2,1,0:T(8,128)(2,1)S(1)}, bf16[1,2,1,128,512]{4,3,2,1,0:T(8,128)(2,1)S(1)}, u32[]{:S(2)}, u32[]{:S(2)}) collective-permute-start(bf16[1,2,1,128,512]{4,3,2,1,0:T(8,128)(2,1)S(1)} %get-tuple-element.110), channel_id=1, source_target_pairs={{16,0},{0,16},{17,1},{1,17},{18,2},{2,18},{19,3},{3,19},{20,4},{4,... | collective-permute-start | bytes 786440 | tf_op jit(solution)/shard_map/ppermute | solution.py:92
  37.6 2.6 %collective-permute-start.16 = (bf16[1,1,128,512]{3,2,1,0:T(8,128)(2,1)S(1)}, bf16[1,1,128,512]{3,2,1,0:T(8,128)(2,1)S(1)}, u32[]{:S(2)}, u32[]{:S(2)}) collective-permute-start(bf16[1,1,128,512]{3,2,1,0:T(8,128)(2,1)S(1)} %get-tuple-element.142.refs_8_), channel_id=1, source_target_pairs={{0,4},{4,0},{8,12},{12,8},{1,5},{5,1},{9,13},{13,9},{2,6},{6,2},{1... | collective-permute-start | bytes 393224 | tf_op jit(solution)/shard_map/ppermute | solution.py:85
  37.7 4.1 %collective-permute-start.17 = (bf16[1,1,128,512]{3,2,1,0:T(8,128)(2,1)S(1)}, bf16[1,1,128,512]{3,2,1,0:T(8,128)(2,1)S(1)}, u32[]{:S(2)}, u32[]{:S(2)}) collective-permute-start(bf16[1,1,128,512]{3,2,1,0:T(8,128)(2,1)S(1)} %get-tuple-element.143.refs_9_), channel_id=1, source_target_pairs={{0,4},{4,0},{8,12},{12,8},{1,5},{5,1},{9,13},{13,9},{2,6},{6,2},{1... | collective-permute-start | bytes 393224 | tf_op jit(solution)/shard_map/ppermute | solution.py:85
  38.2 3.6 %collective-permute-start.14 = (bf16[1,1,128,512]{3,2,1,0:T(8,128)(2,1)S(1)}, bf16[1,1,128,512]{3,2,1,0:T(8,128)(2,1)S(1)}, u32[]{:S(2)}, u32[]{:S(2)}) collective-permute-start(bf16[1,1,128,512]{3,2,1,0:T(8,128)(2,1)S(1)} %collective-permute-done.9.refs_5_), channel_id=1, source_target_pairs={{0,4},{4,0},{8,12},{12,8},{1,5},{5,1},{9,13},{13,9},{2,6},{6,2},{1... | collective-permute-start | bytes 393224 | tf_op jit(solution)/shard_map/ppermute | solution.py:85
  38.3 9.2 %collective-permute-start.22 = (bf16[2,1,128,512]{3,2,1,0:T(8,128)(2,1)S(1)}, bf16[2,1,128,512]{3,2,1,0:T(8,128)(2,1)S(1)}, u32[]{:S(2)}, u32[]{:S(2)}) collective-permute-start(bf16[2,1,128,512]{3,2,1,0:T(8,128)(2,1)S(1)} %get-tuple-element.129), channel_id=1, source_target_pairs={{0,8},{4,12},{8,0},{12,4},{1,9},{5,13},{9,1},{13,5},{2,10},{6,14},... | collective-permute-start | bytes 786440 | tf_op jit(solution)/shard_map/ppermute | solution.py:81
  40.3 8.6 %collective-permute-start.23 = (bf16[1,2,1,128,512]{4,3,2,1,0:T(8,128)(2,1)S(1)}, bf16[1,2,1,128,512]{4,3,2,1,0:T(8,128)(2,1)S(1)}, u32[]{:S(2)}, u32[]{:S(2)}) collective-permute-start(bf16[1,2,1,128,512]{4,3,2,1,0:T(8,128)(2,1)S(1)} %get-tuple-element.111), channel_id=1, source_target_pairs={{16,0},{0,16},{17,1},{1,17},{18,2},{2,18},{19,3},{3,19},{20,4},{4,... | collective-permute-start | bytes 786440 | tf_op jit(solution)/shard_map/ppermute | solution.py:92
  43.1 5.3 %collective-permute-start.20 = (bf16[1,1,128,512]{3,2,1,0:T(8,128)(2,1)S(1)}, bf16[1,1,128,512]{3,2,1,0:T(8,128)(2,1)S(1)}, u32[]{:S(2)}, u32[]{:S(2)}) collective-permute-start(bf16[1,1,128,512]{3,2,1,0:T(8,128)(2,1)S(1)} %get-tuple-element.157.refs_4_), channel_id=1, source_target_pairs={{0,4},{4,0},{8,12},{12,8},{1,5},{5,1},{9,13},{13,9},{2,6},{6,2},{1... | collective-permute-start | bytes 393224 | tf_op jit(solution)/shard_map/ppermute | solution.py:85
  43.1 5.2 %collective-permute-start.21 = (bf16[1,1,128,512]{3,2,1,0:T(8,128)(2,1)S(1)}, bf16[1,1,128,512]{3,2,1,0:T(8,128)(2,1)S(1)}, u32[]{:S(2)}, u32[]{:S(2)}) collective-permute-start(bf16[1,1,128,512]{3,2,1,0:T(8,128)(2,1)S(1)} %get-tuple-element.158.refs_5_), channel_id=1, source_target_pairs={{0,4},{4,0},{8,12},{12,8},{1,5},{5,1},{9,13},{13,9},{2,6},{6,2},{1... | collective-permute-start | bytes 393224 | tf_op jit(solution)/shard_map/ppermute | solution.py:85
  43.6 11.0 %collective-permute-start.18 = (bf16[2,1,128,512]{3,2,1,0:T(8,128)(2,1)S(1)}, bf16[2,1,128,512]{3,2,1,0:T(8,128)(2,1)S(1)}, u32[]{:S(2)}, u32[]{:S(2)}) collective-permute-start(bf16[2,1,128,512]{3,2,1,0:T(8,128)(2,1)S(1)} %get-tuple-element.146), channel_id=1, source_target_pairs={{0,8},{4,12},{8,0},{12,4},{1,9},{5,13},{9,1},{13,5},{2,10},{6,14},... | collective-permute-start | bytes 786440 | tf_op jit(solution)/shard_map/ppermute | solution.py:81
  49.1 2.4 %collective-permute-start.24 = (bf16[1,1,128,512]{3,2,1,0:T(8,128)(2,1)S(1)}, bf16[1,1,128,512]{3,2,1,0:T(8,128)(2,1)S(1)}, u32[]{:S(2)}, u32[]{:S(2)}) collective-permute-start(bf16[1,1,128,512]{3,2,1,0:T(8,128)(2,1)S(1)} %get-tuple-element.170.refs_4_), channel_id=1, source_target_pairs={{0,4},{4,0},{8,12},{12,8},{1,5},{5,1},{9,13},{13,9},{2,6},{6,2},{1... | collective-permute-start | bytes 393224 | tf_op jit(solution)/shard_map/ppermute | solution.py:85
  49.2 2.3 %collective-permute-start.25 = (bf16[1,1,128,512]{3,2,1,0:T(8,128)(2,1)S(1)}, bf16[1,1,128,512]{3,2,1,0:T(8,128)(2,1)S(1)}, u32[]{:S(2)}, u32[]{:S(2)}) collective-permute-start(bf16[1,1,128,512]{3,2,1,0:T(8,128)(2,1)S(1)} %get-tuple-element.171.refs_5_), channel_id=1, source_target_pairs={{0,4},{4,0},{8,12},{12,8},{1,5},{5,1},{9,13},{13,9},{2,6},{6,2},{1... | collective-permute-start | bytes 393224 | tf_op jit(solution)/shard_map/ppermute | solution.py:85
  49.7 6.4 %collective-permute-start.27 = (bf16[1,1,128,512]{3,2,1,0:T(8,128)(2,1)S(1)}, bf16[1,1,128,512]{3,2,1,0:T(8,128)(2,1)S(1)}, u32[]{:S(2)}, u32[]{:S(2)}) collective-permute-start(bf16[1,1,128,512]{3,2,1,0:T(8,128)(2,1)S(1)} %get-tuple-element.162), channel_id=1, source_target_pairs={{0,8},{4,12},{8,0},{12,4},{1,9},{5,13},{9,1},{13,5},{2,10},{6,14},... | collective-permute-start | bytes 393224 | tf_op jit(solution)/shard_map/ppermute | solution.py:81
  52.0 6.4 %collective-permute-start.26 = (bf16[1,1,128,512]{3,2,1,0:T(8,128)(2,1)S(1)}, bf16[1,1,128,512]{3,2,1,0:T(8,128)(2,1)S(1)}, u32[]{:S(2)}, u32[]{:S(2)}) collective-permute-start(bf16[1,1,128,512]{3,2,1,0:T(8,128)(2,1)S(1)} %get-tuple-element.175), channel_id=1, source_target_pairs={{0,8},{4,12},{8,0},{12,4},{1,9},{5,13},{9,1},{13,5},{2,10},{6,14},... | collective-permute-start | bytes 393224 | tf_op jit(solution)/shard_map/ppermute | solution.py:81

commit v11 on v10

--- a/solution.py
+++ b/solution.py
@@ -126,18 +126,11 @@
             arrays = after([x for x, *_ in wanted], *earlier)
 
             def kernel(*refs):
-                ins, outs, sems = refs[: len(wanted)], refs[len(wanted) : -1], refs[-1]
-                copies = []
                 for i, (_, d, n, k) in enumerate(wanted):
-                    at_d = pl.ds(owner_at(d) * owned, owned)
-                    copies.append(pltpu.make_async_copy(ins[i].at[pl.ds(n, k), at_d], outs[i], sems.at[i]))
-                for copy in copies:
-                    copy.start()
-                for copy in copies:
-                    copy.wait()
-
-            shapes = [(k,) + block[1:] for *_, k in wanted]
-            return from_hbm(kernel, shapes, "cut", [pltpu.SemaphoreType.DMA((len(wanted),))], *arrays)
+                    for b in range(owned):
+                        refs[len(wanted) + i][:, b] = refs[i][n : n + k, owner_at(d) * owned + b]
+
+            return call(kernel, [(k,) + block[1:] for *_, k in wanted], "cut", *arrays)
 
         def join(*refs):
             for d in range(owners):
@@ -236,7 +229,7 @@
                         chunks(r, body)
 
             (table,) = after([table], *earlier)
-            spare = [STEP] + [0] * (len(groups) - 1)
+            spare = [STEP] * (len(groups) - 1) + [0]
             shapes = [(len(group), owners, owned, r + x, o) for group, x in zip(groups, spare)]
             return call(kernel, shapes, "partial_sums", table, greater_in, *rows)
 
@@ -260,7 +253,7 @@
             shape = (len(group),) + block[1:]
             return call(kernel, [shape] * owners, "add_partial", table, greater_in, *rows, *received)
 
-        def product(jobs, earlier):
+        def product(jobs, earlier, pad=0):
             arrays = []
             for job in jobs:
                 for x, _ in [*job[0], *job[1]]:
@@ -291,10 +284,10 @@
                         ).astype(BF16)
                         for i in range(owners):
                             for j, at in enumerate(spans):
-                                outs[i][k, b, :, at] = full[i * r : (i + 1) * r, j * r : (j + 1) * r]
-
-            shape = (len(jobs),) + block[1:]
-            return call(kernel, [shape] * owners, "product", *after(arrays, *earlier))
+                                outs[i][k, b, :r, at] = full[i * r : (i + 1) * r, j * r : (j + 1) * r]
+
+            shapes = [(len(jobs), owned, r + pad if d else r, o) for d in range(owners)]
+            return call(kernel, shapes, "product", *after(arrays, *earlier))
 
         def back_to_rows(outs):
             return [outs[0]] + [to_owner(outs[d], owners - d) for d in others]
@@ -310,7 +303,7 @@
                 sems, out = refs[-1], refs[-2]
                 copies = [
                     pltpu.make_async_copy(
-                        refs[where[id(x)]].at[k],
+                        refs[where[id(x)]].at[k, :, pl.ds(0, r)],
                         out.at[n, pl.ds(owner_at(d) * owned, owned)],
                         sems.at[i],
                     )
@@ -377,7 +370,6 @@
             lax.ppermute(table, "en", [(i, (i + t) % en) for i in range(en)])
             for t, table in zip(shifts, tables[1:])
         ]
-        lesser_own = after(lesser_own, *tables)
         lesser_own_from = [[from_energy(x, t) for x in lesser_own] for t in shifts]
 
         groups = [tuple(range(e - 1)), (e - 1,)]
@@ -454,7 +446,7 @@
                         sigma, beside = sigmas[g]
                         beside = [at(x, (i,)) for x in beside]
                         jobs.append((inverse_at(n), in_order((sigma[0], (i,)), at(sigma[1:], (i,)), beside)))
-            last = product(jobs, last)
+            last = product(jobs, last, STEP if step == "L0" else 0)
             back = back_to_rows(last)
             if step == "L0":
                 for rows, beside in zip(lesser_rows, lesser_rows_beside):

time: 59.3 us -> 58.1 us (0.980)
  Pallas kernels: 16.6 us -> 11.7 us
  waiting for transfers between devices: 14.2 us -> 19 us
  starting transfers between devices: 27.3 us -> 26.3 us
    pallas_call x3 -> x1, Pallas kernels: 5.87 us -> 1.97 us  [from_hbm(): pl.pallas_call(kernel, in_specs=[far] * len(args), out_specs=[WHOLE] * le...]
    ppermute x8, waiting for transfers between devices: 7.45 us -> 11.3 us  [to_owner(): return lax.ppermute(x, 'ph', pairs)]
    ppermute x6, waiting for transfers between devices: 3.02 us -> 4.34 us  [from_energy(): return lax.ppermute(x, 'en', [((i + t) % en, i) for i in range(en)])]
    ppermute x13, waiting for transfers between devices: 1.19 us -> 0.03 us  [to_lanes(): lax.ppermute(x, 'ph', [(p, p // lanes * lanes + (p % lanes + q) % lanes)...]
    pallas_call x12 -> x14, Pallas kernels: 5.8 us -> 4.8 us  [call(): pl.pallas_call(kernel, in_specs=[WHOLE] * len(args), out_specs=[WHOLE] *...]
    ppermute x1, waiting for transfers between devices: 2.53 us -> 3.31 us  [on_device(): lax.ppermute(table, 'en', [(i, (i + t) % en) for i in range(en)])]
    ppermute x6, starting transfers between devices: 10.5 us -> 9.81 us  [from_energy(): return lax.ppermute(x, 'en', [((i + t) % en, i) for i in range(en)])]
  transfers between devices with their start and end apart: 28 -> 28, of which waited for: 8 -> 10; matrix products, arithmetic and copies ran while one was open for 0% -> 0% of each run, Pallas kernels for 24% -> 16%
where the time goes in v11:
time: 58.1 us; the launch traced here: 58 us
  starting transfers between devices  26.3 us (45%)
  waiting for transfers between devices  19 us (33%)
  Pallas kernels  11.7 us (20%)
  between operations  0.9 us (2%)
    ppermute x8, starting transfers between devices, to_owner(): return lax.ppermute(x, 'ph', pairs)  13.4 us
    ppermute x8, waiting for transfers between devices, to_owner(): return lax.ppermute(x, 'ph', pairs)  11.3 us
    ppermute x6, starting transfers between devices, from_energy(): return lax.ppermute(x, 'en', [((i + t) % en, i) for i in range(en)])  9.81 us
    pallas_call x7, Pallas kernels, place(): pl.pallas_call(kernel, in_specs=[WHOLE] * len(arrays) + [far] * (result i...  4.95 us
    pallas_call x14, Pallas kernels, call(): pl.pallas_call(kernel, in_specs=[WHOLE] * len(args), out_specs=[WHOLE] *...  4.8 us
    ppermute x6, waiting for transfers between devices, from_energy(): return lax.ppermute(x, 'en', [((i + t) % en, i) for i in range(en)])  4.34 us
    ppermute x1, waiting for transfers between devices, on_device(): lax.ppermute(table, 'en', [(i, (i + t) % en) for i in range(en)])  3.31 us
    ppermute x13, starting transfers between devices, to_lanes(): lax.ppermute(x, 'ph', [(p, p // lanes * lanes + (p % lanes + q) % lanes)...  2.01 us
  transfers between devices with their start and end apart: 28, of which 10 were waited for; matrix products, arithmetic and copies ran while one was open for 0% of the time, Pallas kernels for 16%

profile of v11, /device:TPU:0, one launch (start us, length us, event | category | flops | bytes accessed | tf_op | source)
XLA Modules:
  0.0 58.0 jit_solution(7365287027942729249)
XLA Ops:
  0.7 2.0 %lead.1.refs_0_ = bf16[400,512]{1,0:T(8,128)(2,1)} custom-call(s32[2,3]{1,0:T(2,128)} %bitcast.2, f32[2,3]{1,0:T(2,128)} %bitcast.3, bf16[3,2,128,512]{3,2,1,0:T(8,128)(2,1)} %refs_1_), custom_call_target="tpu_custom_call" | custom-call | flops 1 | bytes 1 | tf_op jit(solution)/shard_map/lead/pallas_call | solution.py:146
  2.6 0.0 copy-start
  2.6 3.0 %collective-permute-start = (bf16[400,512]{1,0:T(8,128)(2,1)}, bf16[400,512]{1,0:T(8,128)(2,1)S(1)}, u32[]{:S(2)}, u32[]{:S(2)}) collective-permute-start(bf16[400,512]{1,0:T(8,128)(2,1)} %lead.1.refs_0_), channel_id=1, source_target_pairs={{0,8},{4,12},{8,0},{12,4},{1,9},{5,13},{9,1},{13,5},{2,10},{6,14},... | collective-permute-start | bytes 1228808 | tf_op jit(solution)/shard_map/ppermute | solution.py:81
  5.7 0.0 copy-start.3
  5.7 1.6 %collective-permute-start.5 = (bf16[3,1,128,512]{3,2,1,0:T(8,128)(2,1)S(1)}, bf16[3,1,128,512]{3,2,1,0:T(8,128)(2,1)S(1)}, u32[]{:S(2)}, u32[]{:S(2)}) collective-permute-start(bf16[3,1,128,512]{3,2,1,0:T(8,128)(2,1)S(1)} %cut.2), channel_id=1, source_target_pairs={{16,0},{0,16},{17,1},{1,17},{18,2},{2,18},{19,3},{3,19},{20,4},{4,... | collective-permute-start | bytes 1179656 | tf_op jit(solution)/shard_map/ppermute | solution.py:92
  7.3 0.1 cut.3
  7.4 0.1 collective-permute-start.1
  7.4 0.6 collective-permute-start.6
  8.0 8.2 %collective-permute-done.refs_1_ = bf16[400,512]{1,0:T(8,128)(2,1)S(1)} collective-permute-done((bf16[400,512]{1,0:T(8,128)(2,1)}, bf16[400,512]{1,0:T(8,128)(2,1)S(1)}, u32[]{:S(2)}, u32[]{:S(2)}) %collective-permute-start) | collective-permute-done | bytes 409632 | tf_op jit(solution)/shard_map/ppermute | solution.py:81
  16.2 0.1 collective-permute-start.3
  16.3 2.1 %collective-permute-start.7 = (bf16[2,1,128,512]{3,2,1,0:T(8,128)(2,1)S(1)}, bf16[2,1,128,512]{3,2,1,0:T(8,128)(2,1)S(1)}, u32[]{:S(2)}, u32[]{:S(2)}) collective-permute-start(bf16[2,1,128,512]{3,2,1,0:T(8,128)(2,1)S(1)} %get-tuple-element.112), channel_id=1, source_target_pairs={{16,0},{0,16},{17,1},{1,17},{18,2},{2,18},{19,3},{3,19},{20,4},{4,... | collective-permute-start | bytes 786440 | tf_op jit(solution)/shard_map/ppermute | solution.py:92
  18.4 0.0 collective-permute-done.3.refs_1_
  18.4 0.1 weights.1
  18.5 0.4 mix.2
  18.9 1.6 %collective-permute-start.10 = (bf16[2,1,128,512]{3,2,1,0:T(8,128)(2,1)S(1)}, bf16[2,1,128,512]{3,2,1,0:T(8,128)(2,1)S(1)}, u32[]{:S(2)}, u32[]{:S(2)}) collective-permute-start(bf16[2,1,128,512]{3,2,1,0:T(8,128)(2,1)S(1)} %get-tuple-element.103), channel_id=1, source_target_pairs={{0,8},{4,12},{8,0},{12,4},{1,9},{5,13},{9,1},{13,5},{2,10},{6,14},... | collective-permute-start | bytes 786440 | tf_op jit(solution)/shard_map/ppermute | solution.py:81
  20.5 1.1 %collective-permute-start.4 = (f32[3,8,128]{2,1,0:T(8,128)S(1)}, f32[3,8,128]{2,1,0:T(8,128)S(1)}, u32[]{:S(2)}, u32[]{:S(2)}) collective-permute-start(f32[3,8,128]{2,1,0:T(8,128)S(1)} %get-tuple-element.111.refs_1_), channel_id=1, source_target_pairs={{0,16},{16,0},{1,17},{17,1},{2,18},{18,2},{3,19},{19,3},{4,20},{20... | collective-permute-start | bytes 36872 | tf_op jit(solution)/shard_map/ppermute | solution.py:370
  21.6 0.0 collective-permute-done.1.refs_2_
  21.6 0.9 %collective-permute-start.8 = (bf16[1,1,128,512]{3,2,1,0:T(8,128)(2,1)S(1)}, bf16[1,1,128,512]{3,2,1,0:T(8,128)(2,1)S(1)}, u32[]{:S(2)}, u32[]{:S(2)}) collective-permute-start(bf16[1,1,128,512]{3,2,1,0:T(8,128)(2,1)S(1)} %get-tuple-element.113), channel_id=1, source_target_pairs={{16,0},{0,16},{17,1},{1,17},{18,2},{2,18},{19,3},{3,19},{20,4},{4,... | collective-permute-start | bytes 393224 | tf_op jit(solution)/shard_map/ppermute | solution.py:92
  22.5 3.3 %collective-permute-done.4.table_ref = f32[3,8,128]{2,1,0:T(8,128)S(1)} collective-permute-done((f32[3,8,128]{2,1,0:T(8,128)S(1)}, f32[3,8,128]{2,1,0:T(8,128)S(1)}, u32[]{:S(2)}, u32[]{:S(2)}) %collective-permute-start.4) | collective-permute-done | bytes 12320 | tf_op jit(solution)/shard_map/ppermute | solution.py:370
  25.8 0.4 partial_sums.1
  26.2 2.0 %collective-permute-start.15 = (bf16[1,2,1,144,512]{4,3,2,1,0:T(8,128)(2,1)S(1)}, bf16[1,2,1,144,512]{4,3,2,1,0:T(8,128)(2,1)S(1)}, u32[]{:S(2)}, u32[]{:S(2)}) collective-permute-start(bf16[1,2,1,144,512]{4,3,2,1,0:T(8,128)(2,1)S(1)} %get-tuple-element.107), channel_id=1, source_target_pairs={{16,0},{0,16},{17,1},{1,17},{18,2},{2,18},{19,3},{3,19},{20,4},{4,... | collective-permute-start | bytes 884744 | tf_op jit(solution)/shard_map/ppermute | solution.py:92
  28.2 0.1 collective-permute-done.8.refs_4_
  28.4 0.0 collective-permute-done.7.refs_3_
  28.4 0.4 mix.3
  28.7 0.1 collective-permute-start.11
  28.9 0.5 collective-permute-done.10.refs_5_
  29.4 0.0 collective-permute-start.12
  29.4 1.7 %collective-permute-start.19 = (bf16[1,2,1,144,512]{4,3,2,1,0:T(8,128)(2,1)S(1)}, bf16[1,2,1,144,512]{4,3,2,1,0:T(8,128)(2,1)S(1)}, u32[]{:S(2)}, u32[]{:S(2)}) collective-permute-start(bf16[1,2,1,144,512]{4,3,2,1,0:T(8,128)(2,1)S(1)} %get-tuple-element.108), channel_id=1, source_target_pairs={{16,0},{0,16},{17,1},{1,17},{18,2},{2,18},{19,3},{3,19},{20,4},{4,... | collective-permute-start | bytes 884744 | tf_op jit(solution)/shard_map/ppermute | solution.py:92
  31.1 1.5 %collective-permute-start.9 = (bf16[1,1,128,512]{3,2,1,0:T(8,128)(2,1)S(1)}, bf16[1,1,128,512]{3,2,1,0:T(8,128)(2,1)S(1)}, u32[]{:S(2)}, u32[]{:S(2)}) collective-permute-start(bf16[1,1,128,512]{3,2,1,0:T(8,128)(2,1)S(1)} %get-tuple-element.104), channel_id=1, source_target_pairs={{0,8},{4,12},{8,0},{12,4},{1,9},{5,13},{9,1},{13,5},{2,10},{6,14},... | collective-permute-start | bytes 393224 | tf_op jit(solution)/shard_map/ppermute | solution.py:81
  32.6 0.0 collective-permute-done.2.refs_3_
  32.6 0.0 collective-permute-start.13
  32.6 0.9 %product.4 = (bf16[2,1,128,512]{3,2,1,0:T(8,128)(2,1)S(1)}, bf16[2,1,144,512]{3,2,1,0:T(8,128)(2,1)S(1)}) custom-call(bf16[3,1,128,512]{3,2,1,0:T(8,128)(2,1)S(1)} %get-tuple-element.162.refs_0_, bf16[3,1,128,512]{3,2,1,0:T(8,128)(2,1)S(1)} %get-tuple-element.163.refs_1_, bf16[3,1,128,512]{3,2,1,0:T(8,128)(2,1)S(1)} %collective-permute-done.1.refs_2_, ...), custom_call_target="tpu_custom_call" | custom-call | flops 1 | bytes 1 | tf_op jit(solution)/shard_map/product/pallas_call | solution.py:21
  33.5 2.6 %collective-permute-done.15.refs_2_ = bf16[1,2,1,144,512]{4,3,2,1,0:T(8,128)(2,1)S(1)} collective-permute-done((bf16[1,2,1,144,512]{4,3,2,1,0:T(8,128)(2,1)S(1)}, bf16[1,2,1,144,512]{4,3,2,1,0:T(8,128)(2,1)S(1)}, u32[]{:S(2)}, u32[]{:S(2)}) %collective-permute-start.15) | collective-permute-done | bytes 294944 | tf_op jit(solution)/shard_map/ppermute | solution.py:92
  36.1 0.2 add_partial.3
  36.4 0.1 collective-permute-start.16
  36.5 2.0 %collective-permute-start.22 = (bf16[2,1,144,512]{3,2,1,0:T(8,128)(2,1)S(1)}, bf16[2,1,144,512]{3,2,1,0:T(8,128)(2,1)S(1)}, u32[]{:S(2)}, u32[]{:S(2)}) collective-permute-start(bf16[2,1,144,512]{3,2,1,0:T(8,128)(2,1)S(1)} %get-tuple-element.125), channel_id=1, source_target_pairs={{0,8},{4,12},{8,0},{12,4},{1,9},{5,13},{9,1},{13,5},{2,10},{6,14},... | collective-permute-start | bytes 884744 | tf_op jit(solution)/shard_map/ppermute | solution.py:81
  38.4 0.0 collective-permute-done.9.refs_5_
  38.4 0.2 collective-permute-start.17
  38.6 0.3 collective-permute-start.14
  38.9 1.5 %collective-permute-start.23 = (bf16[1,2,1,128,512]{4,3,2,1,0:T(8,128)(2,1)S(1)}, bf16[1,2,1,128,512]{4,3,2,1,0:T(8,128)(2,1)S(1)}, u32[]{:S(2)}, u32[]{:S(2)}) collective-permute-start(bf16[1,2,1,128,512]{4,3,2,1,0:T(8,128)(2,1)S(1)} %get-tuple-element.109), channel_id=1, source_target_pairs={{16,0},{0,16},{17,1},{1,17},{18,2},{2,18},{19,3},{3,19},{20,4},{4,... | collective-permute-start | bytes 786440 | tf_op jit(solution)/shard_map/ppermute | solution.py:92
  40.4 0.9 %product.5 = (bf16[2,1,128,512]{3,2,1,0:T(8,128)(2,1)S(1)}, bf16[2,1,128,512]{3,2,1,0:T(8,128)(2,1)S(1)}) custom-call(bf16[3,1,128,512]{3,2,1,0:T(8,128)(2,1)S(1)} %get-tuple-element.162.refs_0_, bf16[3,1,128,512]{3,2,1,0:T(8,128)(2,1)S(1)} %get-tuple-element.163.refs_1_, bf16[3,1,128,512]{3,2,1,0:T(8,128)(2,1)S(1)} %collective-permute-done.1.refs_2_, ...), custom_call_target="tpu_custom_call" | custom-call | flops 1 | bytes 1 | tf_op jit(solution)/shard_map/product/pallas_call | solution.py:21
  41.3 1.1 %collective-permute-done.19.refs_2_ = bf16[1,2,1,144,512]{4,3,2,1,0:T(8,128)(2,1)S(1)} collective-permute-done((bf16[1,2,1,144,512]{4,3,2,1,0:T(8,128)(2,1)S(1)}, bf16[1,2,1,144,512]{4,3,2,1,0:T(8,128)(2,1)S(1)}, u32[]{:S(2)}, u32[]{:S(2)}) %collective-permute-start.19) | collective-permute-done | bytes 294944 | tf_op jit(solution)/shard_map/ppermute | solution.py:92
  42.5 0.2 add_partial.4
  42.7 0.1 collective-permute-start.20
  42.8 0.5 collective-permute-start.21
  43.3 1.9 %collective-permute-start.18 = (bf16[2,1,128,512]{3,2,1,0:T(8,128)(2,1)S(1)}, bf16[2,1,128,512]{3,2,1,0:T(8,128)(2,1)S(1)}, u32[]{:S(2)}, u32[]{:S(2)}) collective-permute-start(bf16[2,1,128,512]{3,2,1,0:T(8,128)(2,1)S(1)} %get-tuple-element.142), channel_id=1, source_target_pairs={{0,8},{4,12},{8,0},{12,4},{1,9},{5,13},{9,1},{13,5},{2,10},{6,14},... | collective-permute-start | bytes 786440 | tf_op jit(solution)/shard_map/ppermute | solution.py:81
  45.2 0.8 %collective-permute-done.22.refs_1_ = bf16[2,1,144,512]{3,2,1,0:T(8,128)(2,1)S(1)} collective-permute-done((bf16[2,1,144,512]{3,2,1,0:T(8,128)(2,1)S(1)}, bf16[2,1,144,512]{3,2,1,0:T(8,128)(2,1)S(1)}, u32[]{:S(2)}, u32[]{:S(2)}) %collective-permute-start.22) | collective-permute-done | bytes 294944 | tf_op jit(solution)/shard_map/ppermute | solution.py:81
  46.0 0.8 %place.7.refs_1_ = bf16[3,2,128,512]{3,2,1,0:T(8,128)(2,1)} custom-call(bf16[2,1,128,512]{3,2,1,0:T(8,128)(2,1)S(1)} %get-tuple-element.147.refs_0_, bf16[2,1,144,512]{3,2,1,0:T(8,128)(2,1)S(1)} %collective-permute-done.22.refs_1_), custom_call_target="tpu_custom_call" | custom-call | flops 1 | bytes 1 | tf_op jit(solution)/shard_map/place/pallas_call | solution.py:318
  46.9 0.5 product.6
  47.4 0.4 collective-permute-done.23.refs_2_
  47.8 0.2 add_partial.5
  48.0 0.1 collective-permute-start.24
  48.1 0.5 collective-permute-start.25
  48.6 1.8 %collective-permute-start.27 = (bf16[1,1,128,512]{3,2,1,0:T(8,128)(2,1)S(1)}, bf16[1,1,128,512]{3,2,1,0:T(8,128)(2,1)S(1)}, u32[]{:S(2)}, u32[]{:S(2)}) collective-permute-start(bf16[1,1,128,512]{3,2,1,0:T(8,128)(2,1)S(1)} %get-tuple-element.158), channel_id=1, source_target_pairs={{0,8},{4,12},{8,0},{12,4},{1,9},{5,13},{9,1},{13,5},{2,10},{6,14},... | collective-permute-start | bytes 393224 | tf_op jit(solution)/shard_map/ppermute | solution.py:81
  50.4 0.5 product.7
  50.9 1.1 %collective-permute-start.26 = (bf16[1,1,128,512]{3,2,1,0:T(8,128)(2,1)S(1)}, bf16[1,1,128,512]{3,2,1,0:T(8,128)(2,1)S(1)}, u32[]{:S(2)}, u32[]{:S(2)}) collective-permute-start(bf16[1,1,128,512]{3,2,1,0:T(8,128)(2,1)S(1)} %get-tuple-element.171), channel_id=1, source_target_pairs={{0,8},{4,12},{8,0},{12,4},{1,9},{5,13},{9,1},{13,5},{2,10},{6,14},... | collective-permute-start | bytes 393224 | tf_op jit(solution)/shard_map/ppermute | solution.py:81
  52.0 0.7 %place.8.refs_1_ = bf16[3,2,128,512]{3,2,1,0:T(8,128)(2,1)} custom-call(bf16[2,1,128,512]{3,2,1,0:T(8,128)(2,1)S(1)} %get-tuple-element.173.refs_0_, bf16[3,2,128,512]{3,2,1,0:T(8,128)(2,1)} %place.7.refs_1_), custom_call_target="tpu_custom_call", output_to_operand_aliasing={{}: (1, {})} | custom-call | flops 1 | bytes 1 | tf_op jit(solution)/shard_map/place/pallas_call | solution.py:318
  52.7 0.8 %place.9.refs_1_ = bf16[3,2,128,512]{3,2,1,0:T(8,128)(2,1)} custom-call(bf16[2,1,128,512]{3,2,1,0:T(8,128)(2,1)S(1)} %get-tuple-element.173.refs_0_, bf16[1,1,128,512]{3,2,1,0:T(8,128)(2,1)S(1)} %get-tuple-element.174.refs_1_, bf16[1,1,128,512]{3,2,1,0:T(8,128)(2,1)S(1)} %get-tuple-element.175.refs_2_), custom_call_target="tpu_custom_call" | custom-call | flops 1 | bytes 1 | tf_op jit(solution)/shard_map/place/pallas_call | solution.py:318
  53.5 0.7 %place.10 = bf16[3,2,128,512]{3,2,1,0:T(8,128)(2,1)} custom-call(bf16[2,1,128,512]{3,2,1,0:T(8,128)(2,1)S(1)} %collective-permute-done.18.refs_0_, bf16[3,2,128,512]{3,2,1,0:T(8,128)(2,1)} %place.8.refs_1_), custom_call_target="tpu_custom_call", output_to_operand_aliasing={{}: (1, {})} | custom-call | flops 1 | bytes 1 | tf_op jit(solution)/shard_map/place/pallas_call | solution.py:318
  54.2 0.7 %place.11.refs_1_ = bf16[3,2,128,512]{3,2,1,0:T(8,128)(2,1)} custom-call(bf16[2,1,128,512]{3,2,1,0:T(8,128)(2,1)S(1)} %collective-permute-done.18.refs_0_, bf16[3,2,128,512]{3,2,1,0:T(8,128)(2,1)} %place.9.refs_1_), custom_call_target="tpu_custom_call", output_to_operand_aliasing={{}: (1, {})} | custom-call | flops 1 | bytes 1 | tf_op jit(solution)/shard_map/place/pallas_call | solution.py:318
  54.9 0.1 collective-permute-done.27.refs_0_
  55.0 0.7 %place.12.refs_1_ = bf16[3,2,128,512]{3,2,1,0:T(8,128)(2,1)} custom-call(bf16[1,1,128,512]{3,2,1,0:T(8,128)(2,1)S(1)} %collective-permute-done.27.refs_0_, bf16[3,2,128,512]{3,2,1,0:T(8,128)(2,1)} %place.11.refs_1_), custom_call_target="tpu_custom_call", output_to_operand_aliasing={{}: (1, {})} | custom-call | flops 1 | bytes 1 | tf_op jit(solution)/shard_map/place/pallas_call | solution.py:318
  55.6 1.7 %collective-permute-done.26.refs_0_ = bf16[1,1,128,512]{3,2,1,0:T(8,128)(2,1)S(1)} collective-permute-done((bf16[1,1,128,512]{3,2,1,0:T(8,128)(2,1)S(1)}, bf16[1,1,128,512]{3,2,1,0:T(8,128)(2,1)S(1)}, u32[]{:S(2)}, u32[]{:S(2)}) %collective-permute-start.26) | collective-permute-done | bytes 131104 | tf_op jit(solution)/shard_map/ppermute | solution.py:81
  57.3 0.7 %place.13 = bf16[3,2,128,512]{3,2,1,0:T(8,128)(2,1)} custom-call(bf16[1,1,128,512]{3,2,1,0:T(8,128)(2,1)S(1)} %collective-permute-done.26.refs_0_, bf16[3,2,128,512]{3,2,1,0:T(8,128)(2,1)} %place.12.refs_1_), custom_call_target="tpu_custom_call", output_to_operand_aliasing={{}: (1, {})} | custom-call | flops 1 | bytes 1 | tf_op jit(solution)/shard_map/place/pallas_call | solution.py:318
  (22 shorter events, 0.1 us)
Async XLA Ops:
  0.6 5.0 %copy-start.1 = (bf16[3,2,128,512]{3,2,1,0:T(8,128)(2,1)S(1)}, bf16[3,2,128,512]{3,2,1,0:T(8,128)(2,1)}, u32[]{:S(2)}) copy-start(bf16[3,2,128,512]{3,2,1,0:T(8,128)(2,1)} %refs_2_.4) | copy-start | bytes 2359300
  0.6 6.6 %copy-start.2 = (bf16[3,2,128,512]{3,2,1,0:T(8,128)(2,1)S(1)}, bf16[3,2,128,512]{3,2,1,0:T(8,128)(2,1)}, u32[]{:S(2)}) copy-start(bf16[3,2,128,512]{3,2,1,0:T(8,128)(2,1)} %refs_1_) | copy-start | bytes 2359300
  2.6 4.7 %copy-start = (bf16[3,2,128,512]{3,2,1,0:T(8,128)(2,1)S(1)}, bf16[3,2,128,512]{3,2,1,0:T(8,128)(2,1)}, u32[]{:S(2)}) copy-start(bf16[3,2,128,512]{3,2,1,0:T(8,128)(2,1)} %refs_0_.9) | copy-start | bytes 2359300
  2.6 13.5 %collective-permute-start = (bf16[400,512]{1,0:T(8,128)(2,1)}, bf16[400,512]{1,0:T(8,128)(2,1)S(1)}, u32[]{:S(2)}, u32[]{:S(2)}) collective-permute-start(bf16[400,512]{1,0:T(8,128)(2,1)} %lead.1.refs_0_), channel_id=1, source_target_pairs={{0,8},{4,12},{8,0},{12,4},{1,9},{5,13},{9,1},{13,5},{2,10},{6,14},... | collective-permute-start | bytes 1228808 | tf_op jit(solution)/shard_map/ppermute | solution.py:81
  5.7 10.5 %copy-start.3 = (bf16[400,512]{1,0:T(8,128)(2,1)S(1)}, bf16[400,512]{1,0:T(8,128)(2,1)}, u32[]{:S(2)}) copy-start(bf16[400,512]{1,0:T(8,128)(2,1)} %lead.1.refs_0_) | copy-start | bytes 1228804
  5.7 12.8 %collective-permute-start.5 = (bf16[3,1,128,512]{3,2,1,0:T(8,128)(2,1)S(1)}, bf16[3,1,128,512]{3,2,1,0:T(8,128)(2,1)S(1)}, u32[]{:S(2)}, u32[]{:S(2)}) collective-permute-start(bf16[3,1,128,512]{3,2,1,0:T(8,128)(2,1)S(1)} %cut.2), channel_id=1, source_target_pairs={{16,0},{0,16},{17,1},{1,17},{18,2},{2,18},{19,3},{3,19},{20,4},{4,... | collective-permute-start | bytes 1179656 | tf_op jit(solution)/shard_map/ppermute | solution.py:92
  7.4 14.2 %collective-permute-start.1 = (bf16[3,1,128,512]{3,2,1,0:T(8,128)(2,1)S(1)}, bf16[3,1,128,512]{3,2,1,0:T(8,128)(2,1)S(1)}, u32[]{:S(2)}, u32[]{:S(2)}) collective-permute-start(bf16[3,1,128,512]{3,2,1,0:T(8,128)(2,1)S(1)} %get-tuple-element.162.refs_0_), channel_id=1, source_target_pairs={{0,4},{4,0},{8,12},{12,8},{1,5},{5,1},{9,13},{13,9},{2,6},{6,2},{1... | collective-permute-start | bytes 1179656 | tf_op jit(solution)/shard_map/ppermute | solution.py:85
  7.4 18.4 %collective-permute-start.6 = (bf16[3,1,128,512]{3,2,1,0:T(8,128)(2,1)S(1)}, bf16[3,1,128,512]{3,2,1,0:T(8,128)(2,1)S(1)}, u32[]{:S(2)}, u32[]{:S(2)}) collective-permute-start(bf16[3,1,128,512]{3,2,1,0:T(8,128)(2,1)S(1)} %get-tuple-element.106), channel_id=1, source_target_pairs={{0,8},{4,12},{8,0},{12,4},{1,9},{5,13},{9,1},{13,5},{2,10},{6,14},... | collective-permute-start | bytes 1179656 | tf_op jit(solution)/shard_map/ppermute | solution.py:81
  16.2 2.2 %collective-permute-start.3 = (bf16[2,16,128]{2,1,0:T(8,128)(2,1)S(1)}, bf16[2,16,128]{2,1,0:T(8,128)(2,1)S(1)}, u32[]{:S(2)}, u32[]{:S(2)}) collective-permute-start(bf16[2,16,128]{2,1,0:T(8,128)(2,1)S(1)} %get-tuple-element.98.refs_0_), channel_id=1, source_target_pairs={{0,4},{4,0},{8,12},{12,8},{1,5},{5,1},{9,13},{13,9},{2,6},{6,2},{1... | collective-permute-start | bytes 24584 | tf_op jit(solution)/shard_map/ppermute | solution.py:85
  16.3 12.1 %collective-permute-start.7 = (bf16[2,1,128,512]{3,2,1,0:T(8,128)(2,1)S(1)}, bf16[2,1,128,512]{3,2,1,0:T(8,128)(2,1)S(1)}, u32[]{:S(2)}, u32[]{:S(2)}) collective-permute-start(bf16[2,1,128,512]{3,2,1,0:T(8,128)(2,1)S(1)} %get-tuple-element.112), channel_id=1, source_target_pairs={{16,0},{0,16},{17,1},{1,17},{18,2},{2,18},{19,3},{3,19},{20,4},{4,... | collective-permute-start | bytes 786440 | tf_op jit(solution)/shard_map/ppermute | solution.py:92
  18.9 10.5 %collective-permute-start.10 = (bf16[2,1,128,512]{3,2,1,0:T(8,128)(2,1)S(1)}, bf16[2,1,128,512]{3,2,1,0:T(8,128)(2,1)S(1)}, u32[]{:S(2)}, u32[]{:S(2)}) collective-permute-start(bf16[2,1,128,512]{3,2,1,0:T(8,128)(2,1)S(1)} %get-tuple-element.103), channel_id=1, source_target_pairs={{0,8},{4,12},{8,0},{12,4},{1,9},{5,13},{9,1},{13,5},{2,10},{6,14},... | collective-permute-start | bytes 786440 | tf_op jit(solution)/shard_map/ppermute | solution.py:81
  20.5 5.3 %collective-permute-start.4 = (f32[3,8,128]{2,1,0:T(8,128)S(1)}, f32[3,8,128]{2,1,0:T(8,128)S(1)}, u32[]{:S(2)}, u32[]{:S(2)}) collective-permute-start(f32[3,8,128]{2,1,0:T(8,128)S(1)} %get-tuple-element.111.refs_1_), channel_id=1, source_target_pairs={{0,16},{16,0},{1,17},{17,1},{2,18},{18,2},{3,19},{19,3},{4,20},{20... | collective-permute-start | bytes 36872 | tf_op jit(solution)/shard_map/ppermute | solution.py:370
  21.6 6.8 %collective-permute-start.8 = (bf16[1,1,128,512]{3,2,1,0:T(8,128)(2,1)S(1)}, bf16[1,1,128,512]{3,2,1,0:T(8,128)(2,1)S(1)}, u32[]{:S(2)}, u32[]{:S(2)}) collective-permute-start(bf16[1,1,128,512]{3,2,1,0:T(8,128)(2,1)S(1)} %get-tuple-element.113), channel_id=1, source_target_pairs={{16,0},{0,16},{17,1},{1,17},{18,2},{2,18},{19,3},{3,19},{20,4},{4,... | collective-permute-start | bytes 393224 | tf_op jit(solution)/shard_map/ppermute | solution.py:92
  25.8 6.8 %collective-permute-start.2 = (bf16[3,1,128,512]{3,2,1,0:T(8,128)(2,1)S(1)}, bf16[3,1,128,512]{3,2,1,0:T(8,128)(2,1)S(1)}, u32[]{:S(2)}, u32[]{:S(2)}) collective-permute-start(bf16[3,1,128,512]{3,2,1,0:T(8,128)(2,1)S(1)} %get-tuple-element.163.refs_1_), channel_id=1, source_target_pairs={{0,4},{4,0},{8,12},{12,8},{1,5},{5,1},{9,13},{13,9},{2,6},{6,2},{1... | collective-permute-start | bytes 1179656 | tf_op jit(solution)/shard_map/ppermute | solution.py:85
  26.2 9.9 %collective-permute-start.15 = (bf16[1,2,1,144,512]{4,3,2,1,0:T(8,128)(2,1)S(1)}, bf16[1,2,1,144,512]{4,3,2,1,0:T(8,128)(2,1)S(1)}, u32[]{:S(2)}, u32[]{:S(2)}) collective-permute-start(bf16[1,2,1,144,512]{4,3,2,1,0:T(8,128)(2,1)S(1)} %get-tuple-element.107), channel_id=1, source_target_pairs={{16,0},{0,16},{17,1},{1,17},{18,2},{2,18},{19,3},{3,19},{20,4},{4,... | collective-permute-start | bytes 884744 | tf_op jit(solution)/shard_map/ppermute | solution.py:92
  28.7 2.4 %collective-permute-start.11 = (bf16[2,1,128,512]{3,2,1,0:T(8,128)(2,1)S(1)}, bf16[2,1,128,512]{3,2,1,0:T(8,128)(2,1)S(1)}, u32[]{:S(2)}, u32[]{:S(2)}) collective-permute-start(bf16[2,1,128,512]{3,2,1,0:T(8,128)(2,1)S(1)} %get-tuple-element.120.refs_4_), channel_id=1, source_target_pairs={{0,4},{4,0},{8,12},{12,8},{1,5},{5,1},{9,13},{13,9},{2,6},{6,2},{1... | collective-permute-start | bytes 786440 | tf_op jit(solution)/shard_map/ppermute | solution.py:85
  29.4 3.2 %collective-permute-start.12 = (bf16[2,1,128,512]{3,2,1,0:T(8,128)(2,1)S(1)}, bf16[2,1,128,512]{3,2,1,0:T(8,128)(2,1)S(1)}, u32[]{:S(2)}, u32[]{:S(2)}) collective-permute-start(bf16[2,1,128,512]{3,2,1,0:T(8,128)(2,1)S(1)} %collective-permute-done.10.refs_5_), channel_id=1, source_target_pairs={{0,4},{4,0},{8,12},{12,8},{1,5},{5,1},{9,13},{13,9},{2,6},{6,2},{1... | collective-permute-start | bytes 786440 | tf_op jit(solution)/shard_map/ppermute | solution.py:85
  29.4 13.1 %collective-permute-start.19 = (bf16[1,2,1,144,512]{4,3,2,1,0:T(8,128)(2,1)S(1)}, bf16[1,2,1,144,512]{4,3,2,1,0:T(8,128)(2,1)S(1)}, u32[]{:S(2)}, u32[]{:S(2)}) collective-permute-start(bf16[1,2,1,144,512]{4,3,2,1,0:T(8,128)(2,1)S(1)} %get-tuple-element.108), channel_id=1, source_target_pairs={{16,0},{0,16},{17,1},{1,17},{18,2},{2,18},{19,3},{3,19},{20,4},{4,... | collective-permute-start | bytes 884744 | tf_op jit(solution)/shard_map/ppermute | solution.py:92
  31.1 7.3 %collective-permute-start.9 = (bf16[1,1,128,512]{3,2,1,0:T(8,128)(2,1)S(1)}, bf16[1,1,128,512]{3,2,1,0:T(8,128)(2,1)S(1)}, u32[]{:S(2)}, u32[]{:S(2)}) collective-permute-start(bf16[1,1,128,512]{3,2,1,0:T(8,128)(2,1)S(1)} %get-tuple-element.104), channel_id=1, source_target_pairs={{0,8},{4,12},{8,0},{12,4},{1,9},{5,13},{9,1},{13,5},{2,10},{6,14},... | collective-permute-start | bytes 393224 | tf_op jit(solution)/shard_map/ppermute | solution.py:81
  32.6 6.0 %collective-permute-start.13 = (bf16[1,1,128,512]{3,2,1,0:T(8,128)(2,1)S(1)}, bf16[1,1,128,512]{3,2,1,0:T(8,128)(2,1)S(1)}, u32[]{:S(2)}, u32[]{:S(2)}) collective-permute-start(bf16[1,1,128,512]{3,2,1,0:T(8,128)(2,1)S(1)} %get-tuple-element.134.refs_4_), channel_id=1, source_target_pairs={{0,4},{4,0},{8,12},{12,8},{1,5},{5,1},{9,13},{13,9},{2,6},{6,2},{1... | collective-permute-start | bytes 393224 | tf_op jit(solution)/shard_map/ppermute | solution.py:85
  36.4 2.6 %collective-permute-start.16 = (bf16[1,1,128,512]{3,2,1,0:T(8,128)(2,1)S(1)}, bf16[1,1,128,512]{3,2,1,0:T(8,128)(2,1)S(1)}, u32[]{:S(2)}, u32[]{:S(2)}) collective-permute-start(bf16[1,1,128,512]{3,2,1,0:T(8,128)(2,1)S(1)} %get-tuple-element.138.refs_8_), channel_id=1, source_target_pairs={{0,4},{4,0},{8,12},{12,8},{1,5},{5,1},{9,13},{13,9},{2,6},{6,2},{1... | collective-permute-start | bytes 393224 | tf_op jit(solution)/shard_map/ppermute | solution.py:85
  36.5 9.6 %collective-permute-start.22 = (bf16[2,1,144,512]{3,2,1,0:T(8,128)(2,1)S(1)}, bf16[2,1,144,512]{3,2,1,0:T(8,128)(2,1)S(1)}, u32[]{:S(2)}, u32[]{:S(2)}) collective-permute-start(bf16[2,1,144,512]{3,2,1,0:T(8,128)(2,1)S(1)} %get-tuple-element.125), channel_id=1, source_target_pairs={{0,8},{4,12},{8,0},{12,4},{1,9},{5,13},{9,1},{13,5},{2,10},{6,14},... | collective-permute-start | bytes 884744 | tf_op jit(solution)/shard_map/ppermute | solution.py:81
  38.4 2.0 %collective-permute-start.17 = (bf16[1,1,128,512]{3,2,1,0:T(8,128)(2,1)S(1)}, bf16[1,1,128,512]{3,2,1,0:T(8,128)(2,1)S(1)}, u32[]{:S(2)}, u32[]{:S(2)}) collective-permute-start(bf16[1,1,128,512]{3,2,1,0:T(8,128)(2,1)S(1)} %get-tuple-element.139.refs_9_), channel_id=1, source_target_pairs={{0,4},{4,0},{8,12},{12,8},{1,5},{5,1},{9,13},{13,9},{2,6},{6,2},{1... | collective-permute-start | bytes 393224 | tf_op jit(solution)/shard_map/ppermute | solution.py:85
  38.6 1.8 %collective-permute-start.14 = (bf16[1,1,128,512]{3,2,1,0:T(8,128)(2,1)S(1)}, bf16[1,1,128,512]{3,2,1,0:T(8,128)(2,1)S(1)}, u32[]{:S(2)}, u32[]{:S(2)}) collective-permute-start(bf16[1,1,128,512]{3,2,1,0:T(8,128)(2,1)S(1)} %collective-permute-done.9.refs_5_), channel_id=1, source_target_pairs={{0,4},{4,0},{8,12},{12,8},{1,5},{5,1},{9,13},{13,9},{2,6},{6,2},{1... | collective-permute-start | bytes 393224 | tf_op jit(solution)/shard_map/ppermute | solution.py:85
  38.9 8.9 %collective-permute-start.23 = (bf16[1,2,1,128,512]{4,3,2,1,0:T(8,128)(2,1)S(1)}, bf16[1,2,1,128,512]{4,3,2,1,0:T(8,128)(2,1)S(1)}, u32[]{:S(2)}, u32[]{:S(2)}) collective-permute-start(bf16[1,2,1,128,512]{4,3,2,1,0:T(8,128)(2,1)S(1)} %get-tuple-element.109), channel_id=1, source_target_pairs={{16,0},{0,16},{17,1},{1,17},{18,2},{2,18},{19,3},{3,19},{20,4},{4,... | collective-permute-start | bytes 786440 | tf_op jit(solution)/shard_map/ppermute | solution.py:92
  42.7 4.2 %collective-permute-start.20 = (bf16[1,1,128,512]{3,2,1,0:T(8,128)(2,1)S(1)}, bf16[1,1,128,512]{3,2,1,0:T(8,128)(2,1)S(1)}, u32[]{:S(2)}, u32[]{:S(2)}) collective-permute-start(bf16[1,1,128,512]{3,2,1,0:T(8,128)(2,1)S(1)} %get-tuple-element.153.refs_4_), channel_id=1, source_target_pairs={{0,4},{4,0},{8,12},{12,8},{1,5},{5,1},{9,13},{13,9},{2,6},{6,2},{1... | collective-permute-start | bytes 393224 | tf_op jit(solution)/shard_map/ppermute | solution.py:85
  42.8 4.1 %collective-permute-start.21 = (bf16[1,1,128,512]{3,2,1,0:T(8,128)(2,1)S(1)}, bf16[1,1,128,512]{3,2,1,0:T(8,128)(2,1)S(1)}, u32[]{:S(2)}, u32[]{:S(2)}) collective-permute-start(bf16[1,1,128,512]{3,2,1,0:T(8,128)(2,1)S(1)} %get-tuple-element.154.refs_5_), channel_id=1, source_target_pairs={{0,4},{4,0},{8,12},{12,8},{1,5},{5,1},{9,13},{13,9},{2,6},{6,2},{1... | collective-permute-start | bytes 393224 | tf_op jit(solution)/shard_map/ppermute | solution.py:85
  43.3 10.2 %collective-permute-start.18 = (bf16[2,1,128,512]{3,2,1,0:T(8,128)(2,1)S(1)}, bf16[2,1,128,512]{3,2,1,0:T(8,128)(2,1)S(1)}, u32[]{:S(2)}, u32[]{:S(2)}) collective-permute-start(bf16[2,1,128,512]{3,2,1,0:T(8,128)(2,1)S(1)} %get-tuple-element.142), channel_id=1, source_target_pairs={{0,8},{4,12},{8,0},{12,4},{1,9},{5,13},{9,1},{13,5},{2,10},{6,14},... | collective-permute-start | bytes 786440 | tf_op jit(solution)/shard_map/ppermute | solution.py:81
  48.0 2.3 %collective-permute-start.24 = (bf16[1,1,128,512]{3,2,1,0:T(8,128)(2,1)S(1)}, bf16[1,1,128,512]{3,2,1,0:T(8,128)(2,1)S(1)}, u32[]{:S(2)}, u32[]{:S(2)}) collective-permute-start(bf16[1,1,128,512]{3,2,1,0:T(8,128)(2,1)S(1)} %get-tuple-element.166.refs_4_), channel_id=1, source_target_pairs={{0,4},{4,0},{8,12},{12,8},{1,5},{5,1},{9,13},{13,9},{2,6},{6,2},{1... | collective-permute-start | bytes 393224 | tf_op jit(solution)/shard_map/ppermute | solution.py:85
  48.1 2.3 %collective-permute-start.25 = (bf16[1,1,128,512]{3,2,1,0:T(8,128)(2,1)S(1)}, bf16[1,1,128,512]{3,2,1,0:T(8,128)(2,1)S(1)}, u32[]{:S(2)}, u32[]{:S(2)}) collective-permute-start(bf16[1,1,128,512]{3,2,1,0:T(8,128)(2,1)S(1)} %get-tuple-element.167.refs_5_), channel_id=1, source_target_pairs={{0,4},{4,0},{8,12},{12,8},{1,5},{5,1},{9,13},{13,9},{2,6},{6,2},{1... | collective-permute-start | bytes 393224 | tf_op jit(solution)/shard_map/ppermute | solution.py:85
  48.6 6.3 %collective-permute-start.27 = (bf16[1,1,128,512]{3,2,1,0:T(8,128)(2,1)S(1)}, bf16[1,1,128,512]{3,2,1,0:T(8,128)(2,1)S(1)}, u32[]{:S(2)}, u32[]{:S(2)}) collective-permute-start(bf16[1,1,128,512]{3,2,1,0:T(8,128)(2,1)S(1)} %get-tuple-element.158), channel_id=1, source_target_pairs={{0,8},{4,12},{8,0},{12,4},{1,9},{5,13},{9,1},{13,5},{2,10},{6,14},... | collective-permute-start | bytes 393224 | tf_op jit(solution)/shard_map/ppermute | solution.py:81
  50.9 6.4 %collective-permute-start.26 = (bf16[1,1,128,512]{3,2,1,0:T(8,128)(2,1)S(1)}, bf16[1,1,128,512]{3,2,1,0:T(8,128)(2,1)S(1)}, u32[]{:S(2)}, u32[]{:S(2)}) collective-permute-start(bf16[1,1,128,512]{3,2,1,0:T(8,128)(2,1)S(1)} %get-tuple-element.171), channel_id=1, source_target_pairs={{0,8},{4,12},{8,0},{12,4},{1,9},{5,13},{9,1},{13,5},{2,10},{6,14},... | collective-permute-start | bytes 393224 | tf_op jit(solution)/shard_map/ppermute | solution.py:81

commit v12 on v11

--- a/solution.py
+++ b/solution.py
@@ -126,11 +126,11 @@
             arrays = after([x for x, *_ in wanted], *earlier)
 
             def kernel(*refs):
-                for i, (_, d, n, k) in enumerate(wanted):
-                    for b in range(owned):
-                        refs[len(wanted) + i][:, b] = refs[i][n : n + k, owner_at(d) * owned + b]
-
-            return call(kernel, [(k,) + block[1:] for *_, k in wanted], "cut", *arrays)
+                for i, (_, d, n, k, _) in enumerate(wanted):
+                    for b in range(owned):
+                        refs[len(wanted) + i][:, b, :r] = refs[i][n : n + k, owner_at(d) * owned + b]
+
+            return call(kernel, [(k, owned, r + spare, o) for *_, k, spare in wanted], "cut", *arrays)
 
         def join(*refs):
             for d in range(owners):
@@ -347,10 +347,10 @@
             inverse,
         )
         leads_from = [to_owner(x, d) for d, x in zip(others, leads)]
-        lessers = cut([(lesser_in, d, 0, e) for d in others], leads)
+        lessers = cut([(lesser_in, d, 0, e, 0) for d in others], leads)
         lesser_from = [[[from_energy(x, t)] for t in shifts] for x in lessers]
         rest = cut(
-            [*((greater_in, d, 0, e) for d in others), (inverse, 0, 0, e), (lesser_in, 0, 0, e - 1), (lesser_in, 0, e - 1, 1)],
+            [*((greater_in, d, 0, e, 0) for d in others), (inverse, 0, 0, e, 0), (lesser_in, 0, 0, e - 1, STEP), (lesser_in, 0, e - 1, 1, 0)],
             lessers,
         )
         greaters, inverse_own, lesser_own = rest[: owners - 1], rest[owners - 1], rest[owners:]

time: 58.1 us -> 56.5 us (0.972)
  starting transfers between devices: 26.3 us -> 20.1 us
  waiting for transfers between devices: 19 us -> 23.6 us
    ppermute x8, waiting for transfers between devices: 11.3 us -> 17.9 us  [to_owner(): return lax.ppermute(x, 'ph', pairs)]
    ppermute x8, starting transfers between devices: 13.4 us -> 9.68 us  [to_owner(): return lax.ppermute(x, 'ph', pairs)]
    ppermute x6, starting transfers between devices: 9.81 us -> 6.94 us  [from_energy(): return lax.ppermute(x, 'en', [((i + t) % en, i) for i in range(en)])]
    ppermute x6, waiting for transfers between devices: 4.34 us -> 2.26 us  [from_energy(): return lax.ppermute(x, 'en', [((i + t) % en, i) for i in range(en)])]
    ppermute x13, waiting for transfers between devices: 0.03 us -> 1.81 us  [to_lanes(): lax.ppermute(x, 'ph', [(p, p // lanes * lanes + (p % lanes + q) % lanes)...]
    ppermute x1, waiting for transfers between devices: 3.31 us -> 1.66 us  [on_device(): lax.ppermute(table, 'en', [(i, (i + t) % en) for i in range(en)])]
  transfers between devices with their start and end apart: 28 -> 28, of which waited for: 10 -> 15; matrix products, arithmetic and copies ran while one was open for 0% -> 0% of each run, Pallas kernels for 16% -> 16%
where the time goes in v12:
time: 56.5 us; the launch traced here: 56.3 us
  waiting for transfers between devices  23.6 us (42%)
  starting transfers between devices  20.1 us (36%)
  Pallas kernels  11.7 us (21%)
  between operations  0.91 us (2%)
    ppermute x8, waiting for transfers between devices, to_owner(): return lax.ppermute(x, 'ph', pairs)  17.9 us
    ppermute x8, starting transfers between devices, to_owner(): return lax.ppermute(x, 'ph', pairs)  9.68 us
    ppermute x6, starting transfers between devices, from_energy(): return lax.ppermute(x, 'en', [((i + t) % en, i) for i in range(en)])  6.94 us
    pallas_call x7, Pallas kernels, place(): pl.pallas_call(kernel, in_specs=[WHOLE] * len(arrays) + [far] * (result i...  4.95 us
    pallas_call x14, Pallas kernels, call(): pl.pallas_call(kernel, in_specs=[WHOLE] * len(args), out_specs=[WHOLE] *...  4.79 us
    ppermute x6, waiting for transfers between devices, from_energy(): return lax.ppermute(x, 'en', [((i + t) % en, i) for i in range(en)])  2.26 us
    pallas_call x1, Pallas kernels, from_hbm(): pl.pallas_call(kernel, in_specs=[far] * len(args), out_specs=[WHOLE] * le...  1.97 us
    ppermute x13, starting transfers between devices, to_lanes(): lax.ppermute(x, 'ph', [(p, p // lanes * lanes + (p % lanes + q) % lanes)...  1.94 us
  transfers between devices with their start and end apart: 28, of which 15 were waited for; matrix products, arithmetic and copies ran while one was open for 0% of the time, Pallas kernels for 16%

profile of v12, /device:TPU:0, one launch (start us, length us, event | category | flops | bytes accessed | tf_op | source)
XLA Modules:
  0.0 56.3 jit_solution(18413318821796257893)
XLA Ops:
  0.7 2.0 %lead.1.refs_0_ = bf16[400,512]{1,0:T(8,128)(2,1)} custom-call(s32[2,3]{1,0:T(2,128)} %bitcast.2, f32[2,3]{1,0:T(2,128)} %bitcast.3, bf16[3,2,128,512]{3,2,1,0:T(8,128)(2,1)} %refs_1_), custom_call_target="tpu_custom_call" | custom-call | flops 1 | bytes 1 | tf_op jit(solution)/shard_map/lead/pallas_call | solution.py:146
  2.6 0.0 copy-start
  2.6 3.0 %collective-permute-start = (bf16[400,512]{1,0:T(8,128)(2,1)}, bf16[400,512]{1,0:T(8,128)(2,1)S(1)}, u32[]{:S(2)}, u32[]{:S(2)}) collective-permute-start(bf16[400,512]{1,0:T(8,128)(2,1)} %lead.1.refs_0_), channel_id=1, source_target_pairs={{0,8},{4,12},{8,0},{12,4},{1,9},{5,13},{9,1},{13,5},{2,10},{6,14},... | collective-permute-start | bytes 1228808 | tf_op jit(solution)/shard_map/ppermute | solution.py:81
  5.7 0.0 copy-start.3
  5.7 1.6 %collective-permute-start.5 = (bf16[3,1,128,512]{3,2,1,0:T(8,128)(2,1)S(1)}, bf16[3,1,128,512]{3,2,1,0:T(8,128)(2,1)S(1)}, u32[]{:S(2)}, u32[]{:S(2)}) collective-permute-start(bf16[3,1,128,512]{3,2,1,0:T(8,128)(2,1)S(1)} %cut.2), channel_id=1, source_target_pairs={{16,0},{0,16},{17,1},{1,17},{18,2},{2,18},{19,3},{3,19},{20,4},{4,... | collective-permute-start | bytes 1179656 | tf_op jit(solution)/shard_map/ppermute | solution.py:92
  7.3 0.1 cut.3
  7.4 0.1 collective-permute-start.1
  7.4 0.6 %collective-permute-start.6 = (bf16[3,1,128,512]{3,2,1,0:T(8,128)(2,1)S(1)}, bf16[3,1,128,512]{3,2,1,0:T(8,128)(2,1)S(1)}, u32[]{:S(2)}, u32[]{:S(2)}) collective-permute-start(bf16[3,1,128,512]{3,2,1,0:T(8,128)(2,1)S(1)} %get-tuple-element.106), channel_id=1, source_target_pairs={{0,8},{4,12},{8,0},{12,4},{1,9},{5,13},{9,1},{13,5},{2,10},{6,14},... | collective-permute-start | bytes 1179656 | tf_op jit(solution)/shard_map/ppermute | solution.py:81
  8.0 0.4 collective-permute-start.7
  8.4 7.7 %collective-permute-done.refs_1_ = bf16[400,512]{1,0:T(8,128)(2,1)S(1)} collective-permute-done((bf16[400,512]{1,0:T(8,128)(2,1)}, bf16[400,512]{1,0:T(8,128)(2,1)S(1)}, u32[]{:S(2)}, u32[]{:S(2)}) %collective-permute-start) | collective-permute-done | bytes 409632 | tf_op jit(solution)/shard_map/ppermute | solution.py:81
  16.2 0.1 collective-permute-start.3
  16.3 1.2 %collective-permute-done.3.refs_1_ = bf16[2,16,128]{2,1,0:T(8,128)(2,1)S(1)} collective-permute-done((bf16[2,16,128]{2,1,0:T(8,128)(2,1)S(1)}, bf16[2,16,128]{2,1,0:T(8,128)(2,1)S(1)}, u32[]{:S(2)}, u32[]{:S(2)}) %collective-permute-start.3) | collective-permute-done | bytes 8224 | tf_op jit(solution)/shard_map/ppermute | solution.py:85
  17.5 0.1 weights.1
  17.6 0.3 collective-permute-done.5.refs_3_
  17.8 0.4 mix.2
  18.2 1.9 %collective-permute-start.10 = (bf16[2,1,128,512]{3,2,1,0:T(8,128)(2,1)S(1)}, bf16[2,1,128,512]{3,2,1,0:T(8,128)(2,1)S(1)}, u32[]{:S(2)}, u32[]{:S(2)}) collective-permute-start(bf16[2,1,128,512]{3,2,1,0:T(8,128)(2,1)S(1)} %get-tuple-element.103), channel_id=1, source_target_pairs={{0,8},{4,12},{8,0},{12,4},{1,9},{5,13},{9,1},{13,5},{2,10},{6,14},... | collective-permute-start | bytes 786440 | tf_op jit(solution)/shard_map/ppermute | solution.py:81
  20.1 1.5 %collective-permute-start.4 = (f32[3,8,128]{2,1,0:T(8,128)S(1)}, f32[3,8,128]{2,1,0:T(8,128)S(1)}, u32[]{:S(2)}, u32[]{:S(2)}) collective-permute-start(f32[3,8,128]{2,1,0:T(8,128)S(1)} %get-tuple-element.111.refs_1_), channel_id=1, source_target_pairs={{0,16},{16,0},{1,17},{17,1},{2,18},{18,2},{3,19},{19,3},{4,20},{20... | collective-permute-start | bytes 36872 | tf_op jit(solution)/shard_map/ppermute | solution.py:370
  21.6 0.5 collective-permute-start.8
  22.1 1.7 %collective-permute-done.4.table_ref = f32[3,8,128]{2,1,0:T(8,128)S(1)} collective-permute-done((f32[3,8,128]{2,1,0:T(8,128)S(1)}, f32[3,8,128]{2,1,0:T(8,128)S(1)}, u32[]{:S(2)}, u32[]{:S(2)}) %collective-permute-start.4) | collective-permute-done | bytes 12320 | tf_op jit(solution)/shard_map/ppermute | solution.py:370
  23.8 0.0 collective-permute-start.2
  23.8 0.8 %collective-permute-done.6.refs_1_ = bf16[3,1,128,512]{3,2,1,0:T(8,128)(2,1)S(1)} collective-permute-done((bf16[3,1,128,512]{3,2,1,0:T(8,128)(2,1)S(1)}, bf16[3,1,128,512]{3,2,1,0:T(8,128)(2,1)S(1)}, u32[]{:S(2)}, u32[]{:S(2)}) %collective-permute-start.6) | collective-permute-done | bytes 393248 | tf_op jit(solution)/shard_map/ppermute | solution.py:81
  24.6 0.4 partial_sums.1
  25.0 2.1 %collective-permute-start.15 = (bf16[1,2,1,144,512]{4,3,2,1,0:T(8,128)(2,1)S(1)}, bf16[1,2,1,144,512]{4,3,2,1,0:T(8,128)(2,1)S(1)}, u32[]{:S(2)}, u32[]{:S(2)}) collective-permute-start(bf16[1,2,1,144,512]{4,3,2,1,0:T(8,128)(2,1)S(1)} %get-tuple-element.107), channel_id=1, source_target_pairs={{16,0},{0,16},{17,1},{1,17},{18,2},{2,18},{19,3},{3,19},{20,4},{4,... | collective-permute-start | bytes 884744 | tf_op jit(solution)/shard_map/ppermute | solution.py:92
  27.1 0.4 mix.3
  27.5 0.1 collective-permute-start.11
  27.5 1.9 %collective-permute-done.10.refs_5_ = bf16[2,1,128,512]{3,2,1,0:T(8,128)(2,1)S(1)} collective-permute-done((bf16[2,1,128,512]{3,2,1,0:T(8,128)(2,1)S(1)}, bf16[2,1,128,512]{3,2,1,0:T(8,128)(2,1)S(1)}, u32[]{:S(2)}, u32[]{:S(2)}) %collective-permute-start.10) | collective-permute-done | bytes 262176 | tf_op jit(solution)/shard_map/ppermute | solution.py:81
  29.4 0.0 collective-permute-start.12
  29.4 1.7 %collective-permute-start.19 = (bf16[1,2,1,144,512]{4,3,2,1,0:T(8,128)(2,1)S(1)}, bf16[1,2,1,144,512]{4,3,2,1,0:T(8,128)(2,1)S(1)}, u32[]{:S(2)}, u32[]{:S(2)}) collective-permute-start(bf16[1,2,1,144,512]{4,3,2,1,0:T(8,128)(2,1)S(1)} %get-tuple-element.108), channel_id=1, source_target_pairs={{16,0},{0,16},{17,1},{1,17},{18,2},{2,18},{19,3},{3,19},{20,4},{4,... | collective-permute-start | bytes 884744 | tf_op jit(solution)/shard_map/ppermute | solution.py:92
  31.1 1.5 %collective-permute-start.9 = (bf16[1,1,128,512]{3,2,1,0:T(8,128)(2,1)S(1)}, bf16[1,1,128,512]{3,2,1,0:T(8,128)(2,1)S(1)}, u32[]{:S(2)}, u32[]{:S(2)}) collective-permute-start(bf16[1,1,128,512]{3,2,1,0:T(8,128)(2,1)S(1)} %get-tuple-element.104), channel_id=1, source_target_pairs={{0,8},{4,12},{8,0},{12,4},{1,9},{5,13},{9,1},{13,5},{2,10},{6,14},... | collective-permute-start | bytes 393224 | tf_op jit(solution)/shard_map/ppermute | solution.py:81
  32.6 0.9 %product.4 = (bf16[2,1,128,512]{3,2,1,0:T(8,128)(2,1)S(1)}, bf16[2,1,144,512]{3,2,1,0:T(8,128)(2,1)S(1)}) custom-call(bf16[3,1,128,512]{3,2,1,0:T(8,128)(2,1)S(1)} %get-tuple-element.162.refs_0_, bf16[3,1,128,512]{3,2,1,0:T(8,128)(2,1)S(1)} %get-tuple-element.163.refs_1_, bf16[3,1,128,512]{3,2,1,0:T(8,128)(2,1)S(1)} %collective-permute-done.1.refs_2_, ...), custom_call_target="tpu_custom_call" | custom-call | flops 1 | bytes 1 | tf_op jit(solution)/shard_map/product/pallas_call | solution.py:21
  33.5 1.2 %collective-permute-done.15.refs_2_ = bf16[1,2,1,144,512]{4,3,2,1,0:T(8,128)(2,1)S(1)} collective-permute-done((bf16[1,2,1,144,512]{4,3,2,1,0:T(8,128)(2,1)S(1)}, bf16[1,2,1,144,512]{4,3,2,1,0:T(8,128)(2,1)S(1)}, u32[]{:S(2)}, u32[]{:S(2)}) %collective-permute-start.15) | collective-permute-done | bytes 294944 | tf_op jit(solution)/shard_map/ppermute | solution.py:92
  34.7 0.2 add_partial.3
  34.9 0.1 collective-permute-start.16
  35.0 0.1 collective-permute-start.22
  35.1 1.7 %collective-permute-done.9.refs_5_ = bf16[1,1,128,512]{3,2,1,0:T(8,128)(2,1)S(1)} collective-permute-done((bf16[1,1,128,512]{3,2,1,0:T(8,128)(2,1)S(1)}, bf16[1,1,128,512]{3,2,1,0:T(8,128)(2,1)S(1)}, u32[]{:S(2)}, u32[]{:S(2)}) %collective-permute-start.9) | collective-permute-done | bytes 131104 | tf_op jit(solution)/shard_map/ppermute | solution.py:81
  36.8 0.5 collective-permute-start.14
  37.3 0.6 %collective-permute-start.23 = (bf16[1,2,1,128,512]{4,3,2,1,0:T(8,128)(2,1)S(1)}, bf16[1,2,1,128,512]{4,3,2,1,0:T(8,128)(2,1)S(1)}, u32[]{:S(2)}, u32[]{:S(2)}) collective-permute-start(bf16[1,2,1,128,512]{4,3,2,1,0:T(8,128)(2,1)S(1)} %get-tuple-element.109), channel_id=1, source_target_pairs={{16,0},{0,16},{17,1},{1,17},{18,2},{2,18},{19,3},{3,19},{20,4},{4,... | collective-permute-start | bytes 786440 | tf_op jit(solution)/shard_map/ppermute | solution.py:92
  37.9 0.2 collective-permute-done.17.refs_11_
  38.1 0.2 collective-permute-done.14.refs_7_
  38.3 0.9 %product.5 = (bf16[2,1,128,512]{3,2,1,0:T(8,128)(2,1)S(1)}, bf16[2,1,128,512]{3,2,1,0:T(8,128)(2,1)S(1)}) custom-call(bf16[3,1,128,512]{3,2,1,0:T(8,128)(2,1)S(1)} %get-tuple-element.162.refs_0_, bf16[3,1,128,512]{3,2,1,0:T(8,128)(2,1)S(1)} %get-tuple-element.163.refs_1_, bf16[3,1,128,512]{3,2,1,0:T(8,128)(2,1)S(1)} %collective-permute-done.1.refs_2_, ...), custom_call_target="tpu_custom_call" | custom-call | flops 1 | bytes 1 | tf_op jit(solution)/shard_map/product/pallas_call | solution.py:21
  39.2 0.8 %collective-permute-done.19.refs_2_ = bf16[1,2,1,144,512]{4,3,2,1,0:T(8,128)(2,1)S(1)} collective-permute-done((bf16[1,2,1,144,512]{4,3,2,1,0:T(8,128)(2,1)S(1)}, bf16[1,2,1,144,512]{4,3,2,1,0:T(8,128)(2,1)S(1)}, u32[]{:S(2)}, u32[]{:S(2)}) %collective-permute-start.19) | collective-permute-done | bytes 294944 | tf_op jit(solution)/shard_map/ppermute | solution.py:92
  40.0 0.2 add_partial.4
  40.2 0.1 collective-permute-start.20
  40.3 0.5 collective-permute-start.21
  40.8 0.7 %collective-permute-start.18 = (bf16[2,1,128,512]{3,2,1,0:T(8,128)(2,1)S(1)}, bf16[2,1,128,512]{3,2,1,0:T(8,128)(2,1)S(1)}, u32[]{:S(2)}, u32[]{:S(2)}) collective-permute-start(bf16[2,1,128,512]{3,2,1,0:T(8,128)(2,1)S(1)} %get-tuple-element.142), channel_id=1, source_target_pairs={{0,8},{4,12},{8,0},{12,4},{1,9},{5,13},{9,1},{13,5},{2,10},{6,14},... | collective-permute-start | bytes 786440 | tf_op jit(solution)/shard_map/ppermute | solution.py:81
  41.5 3.3 %collective-permute-done.22.refs_1_ = bf16[2,1,144,512]{3,2,1,0:T(8,128)(2,1)S(1)} collective-permute-done((bf16[2,1,144,512]{3,2,1,0:T(8,128)(2,1)S(1)}, bf16[2,1,144,512]{3,2,1,0:T(8,128)(2,1)S(1)}, u32[]{:S(2)}, u32[]{:S(2)}) %collective-permute-start.22) | collective-permute-done | bytes 294944 | tf_op jit(solution)/shard_map/ppermute | solution.py:81
  44.9 0.8 %place.7.refs_1_ = bf16[3,2,128,512]{3,2,1,0:T(8,128)(2,1)} custom-call(bf16[2,1,128,512]{3,2,1,0:T(8,128)(2,1)S(1)} %get-tuple-element.147.refs_0_, bf16[2,1,144,512]{3,2,1,0:T(8,128)(2,1)S(1)} %collective-permute-done.22.refs_1_), custom_call_target="tpu_custom_call" | custom-call | flops 1 | bytes 1 | tf_op jit(solution)/shard_map/place/pallas_call | solution.py:318
  45.7 0.5 product.6
  46.2 0.2 add_partial.5
  46.5 0.1 collective-permute-start.24
  46.6 0.5 collective-permute-start.25
  47.1 0.8 %collective-permute-start.27 = (bf16[1,1,128,512]{3,2,1,0:T(8,128)(2,1)S(1)}, bf16[1,1,128,512]{3,2,1,0:T(8,128)(2,1)S(1)}, u32[]{:S(2)}, u32[]{:S(2)}) collective-permute-start(bf16[1,1,128,512]{3,2,1,0:T(8,128)(2,1)S(1)} %get-tuple-element.158), channel_id=1, source_target_pairs={{0,8},{4,12},{8,0},{12,4},{1,9},{5,13},{9,1},{13,5},{2,10},{6,14},... | collective-permute-start | bytes 393224 | tf_op jit(solution)/shard_map/ppermute | solution.py:81
  47.9 0.0 collective-permute-done.24.refs_6_
  47.9 0.2 collective-permute-done.25.refs_7_
  48.1 0.5 product.7
  48.6 1.1 %collective-permute-start.26 = (bf16[1,1,128,512]{3,2,1,0:T(8,128)(2,1)S(1)}, bf16[1,1,128,512]{3,2,1,0:T(8,128)(2,1)S(1)}, u32[]{:S(2)}, u32[]{:S(2)}) collective-permute-start(bf16[1,1,128,512]{3,2,1,0:T(8,128)(2,1)S(1)} %get-tuple-element.171), channel_id=1, source_target_pairs={{0,8},{4,12},{8,0},{12,4},{1,9},{5,13},{9,1},{13,5},{2,10},{6,14},... | collective-permute-start | bytes 393224 | tf_op jit(solution)/shard_map/ppermute | solution.py:81
  49.7 0.7 %place.8.refs_1_ = bf16[3,2,128,512]{3,2,1,0:T(8,128)(2,1)} custom-call(bf16[2,1,128,512]{3,2,1,0:T(8,128)(2,1)S(1)} %get-tuple-element.173.refs_0_, bf16[3,2,128,512]{3,2,1,0:T(8,128)(2,1)} %place.7.refs_1_), custom_call_target="tpu_custom_call", output_to_operand_aliasing={{}: (1, {})} | custom-call | flops 1 | bytes 1 | tf_op jit(solution)/shard_map/place/pallas_call | solution.py:318
  50.4 0.8 %place.9.refs_1_ = bf16[3,2,128,512]{3,2,1,0:T(8,128)(2,1)} custom-call(bf16[2,1,128,512]{3,2,1,0:T(8,128)(2,1)S(1)} %get-tuple-element.173.refs_0_, bf16[1,1,128,512]{3,2,1,0:T(8,128)(2,1)S(1)} %get-tuple-element.174.refs_1_, bf16[1,1,128,512]{3,2,1,0:T(8,128)(2,1)S(1)} %get-tuple-element.175.refs_2_), custom_call_target="tpu_custom_call" | custom-call | flops 1 | bytes 1 | tf_op jit(solution)/shard_map/place/pallas_call | solution.py:318
  51.2 0.7 %place.10 = bf16[3,2,128,512]{3,2,1,0:T(8,128)(2,1)} custom-call(bf16[2,1,128,512]{3,2,1,0:T(8,128)(2,1)S(1)} %collective-permute-done.18.refs_0_, bf16[3,2,128,512]{3,2,1,0:T(8,128)(2,1)} %place.8.refs_1_), custom_call_target="tpu_custom_call", output_to_operand_aliasing={{}: (1, {})} | custom-call | flops 1 | bytes 1 | tf_op jit(solution)/shard_map/place/pallas_call | solution.py:318
  51.9 0.7 %place.11.refs_1_ = bf16[3,2,128,512]{3,2,1,0:T(8,128)(2,1)} custom-call(bf16[2,1,128,512]{3,2,1,0:T(8,128)(2,1)S(1)} %collective-permute-done.18.refs_0_, bf16[3,2,128,512]{3,2,1,0:T(8,128)(2,1)} %place.9.refs_1_), custom_call_target="tpu_custom_call", output_to_operand_aliasing={{}: (1, {})} | custom-call | flops 1 | bytes 1 | tf_op jit(solution)/shard_map/place/pallas_call | solution.py:318
  52.6 0.9 %collective-permute-done.27.refs_0_ = bf16[1,1,128,512]{3,2,1,0:T(8,128)(2,1)S(1)} collective-permute-done((bf16[1,1,128,512]{3,2,1,0:T(8,128)(2,1)S(1)}, bf16[1,1,128,512]{3,2,1,0:T(8,128)(2,1)S(1)}, u32[]{:S(2)}, u32[]{:S(2)}) %collective-permute-start.27) | collective-permute-done | bytes 131104 | tf_op jit(solution)/shard_map/ppermute | solution.py:81
  53.4 0.7 %place.12.refs_1_ = bf16[3,2,128,512]{3,2,1,0:T(8,128)(2,1)} custom-call(bf16[1,1,128,512]{3,2,1,0:T(8,128)(2,1)S(1)} %collective-permute-done.27.refs_0_, bf16[3,2,128,512]{3,2,1,0:T(8,128)(2,1)} %place.11.refs_1_), custom_call_target="tpu_custom_call", output_to_operand_aliasing={{}: (1, {})} | custom-call | flops 1 | bytes 1 | tf_op jit(solution)/shard_map/place/pallas_call | solution.py:318
  54.1 1.6 %collective-permute-done.26.refs_0_ = bf16[1,1,128,512]{3,2,1,0:T(8,128)(2,1)S(1)} collective-permute-done((bf16[1,1,128,512]{3,2,1,0:T(8,128)(2,1)S(1)}, bf16[1,1,128,512]{3,2,1,0:T(8,128)(2,1)S(1)}, u32[]{:S(2)}, u32[]{:S(2)}) %collective-permute-start.26) | collective-permute-done | bytes 131104 | tf_op jit(solution)/shard_map/ppermute | solution.py:81
  55.6 0.7 %place.13 = bf16[3,2,128,512]{3,2,1,0:T(8,128)(2,1)} custom-call(bf16[1,1,128,512]{3,2,1,0:T(8,128)(2,1)S(1)} %collective-permute-done.26.refs_0_, bf16[3,2,128,512]{3,2,1,0:T(8,128)(2,1)} %place.12.refs_1_), custom_call_target="tpu_custom_call", output_to_operand_aliasing={{}: (1, {})} | custom-call | flops 1 | bytes 1 | tf_op jit(solution)/shard_map/place/pallas_call | solution.py:318
  (22 shorter events, 0.1 us)
Async XLA Ops:
  0.6 5.0 %copy-start.1 = (bf16[3,2,128,512]{3,2,1,0:T(8,128)(2,1)S(1)}, bf16[3,2,128,512]{3,2,1,0:T(8,128)(2,1)}, u32[]{:S(2)}) copy-start(bf16[3,2,128,512]{3,2,1,0:T(8,128)(2,1)} %refs_2_.4) | copy-start | bytes 2359300
  0.6 6.6 %copy-start.2 = (bf16[3,2,128,512]{3,2,1,0:T(8,128)(2,1)S(1)}, bf16[3,2,128,512]{3,2,1,0:T(8,128)(2,1)}, u32[]{:S(2)}) copy-start(bf16[3,2,128,512]{3,2,1,0:T(8,128)(2,1)} %refs_1_) | copy-start | bytes 2359300
  2.6 4.7 %copy-start = (bf16[3,2,128,512]{3,2,1,0:T(8,128)(2,1)S(1)}, bf16[3,2,128,512]{3,2,1,0:T(8,128)(2,1)}, u32[]{:S(2)}) copy-start(bf16[3,2,128,512]{3,2,1,0:T(8,128)(2,1)} %refs_0_.9) | copy-start | bytes 2359300
  2.6 13.5 %collective-permute-start = (bf16[400,512]{1,0:T(8,128)(2,1)}, bf16[400,512]{1,0:T(8,128)(2,1)S(1)}, u32[]{:S(2)}, u32[]{:S(2)}) collective-permute-start(bf16[400,512]{1,0:T(8,128)(2,1)} %lead.1.refs_0_), channel_id=1, source_target_pairs={{0,8},{4,12},{8,0},{12,4},{1,9},{5,13},{9,1},{13,5},{2,10},{6,14},... | collective-permute-start | bytes 1228808 | tf_op jit(solution)/shard_map/ppermute | solution.py:81
  5.7 10.5 %copy-start.3 = (bf16[400,512]{1,0:T(8,128)(2,1)S(1)}, bf16[400,512]{1,0:T(8,128)(2,1)}, u32[]{:S(2)}) copy-start(bf16[400,512]{1,0:T(8,128)(2,1)} %lead.1.refs_0_) | copy-start | bytes 1228804
  5.7 12.1 %collective-permute-start.5 = (bf16[3,1,128,512]{3,2,1,0:T(8,128)(2,1)S(1)}, bf16[3,1,128,512]{3,2,1,0:T(8,128)(2,1)S(1)}, u32[]{:S(2)}, u32[]{:S(2)}) collective-permute-start(bf16[3,1,128,512]{3,2,1,0:T(8,128)(2,1)S(1)} %cut.2), channel_id=1, source_target_pairs={{16,0},{0,16},{17,1},{1,17},{18,2},{2,18},{19,3},{3,19},{20,4},{4,... | collective-permute-start | bytes 1179656 | tf_op jit(solution)/shard_map/ppermute | solution.py:92
  7.4 14.2 %collective-permute-start.1 = (bf16[3,1,128,512]{3,2,1,0:T(8,128)(2,1)S(1)}, bf16[3,1,128,512]{3,2,1,0:T(8,128)(2,1)S(1)}, u32[]{:S(2)}, u32[]{:S(2)}) collective-permute-start(bf16[3,1,128,512]{3,2,1,0:T(8,128)(2,1)S(1)} %get-tuple-element.162.refs_0_), channel_id=1, source_target_pairs={{0,4},{4,0},{8,12},{12,8},{1,5},{5,1},{9,13},{13,9},{2,6},{6,2},{1... | collective-permute-start | bytes 1179656 | tf_op jit(solution)/shard_map/ppermute | solution.py:85
  7.4 17.2 %collective-permute-start.6 = (bf16[3,1,128,512]{3,2,1,0:T(8,128)(2,1)S(1)}, bf16[3,1,128,512]{3,2,1,0:T(8,128)(2,1)S(1)}, u32[]{:S(2)}, u32[]{:S(2)}) collective-permute-start(bf16[3,1,128,512]{3,2,1,0:T(8,128)(2,1)S(1)} %get-tuple-element.106), channel_id=1, source_target_pairs={{0,8},{4,12},{8,0},{12,4},{1,9},{5,13},{9,1},{13,5},{2,10},{6,14},... | collective-permute-start | bytes 1179656 | tf_op jit(solution)/shard_map/ppermute | solution.py:81
  8.0 19.1 %collective-permute-start.7 = (bf16[2,1,144,512]{3,2,1,0:T(8,128)(2,1)S(1)}, bf16[2,1,144,512]{3,2,1,0:T(8,128)(2,1)S(1)}, u32[]{:S(2)}, u32[]{:S(2)}) collective-permute-start(bf16[2,1,144,512]{3,2,1,0:T(8,128)(2,1)S(1)} %get-tuple-element.112), channel_id=1, source_target_pairs={{16,0},{0,16},{17,1},{1,17},{18,2},{2,18},{19,3},{3,19},{20,4},{4,... | collective-permute-start | bytes 884744 | tf_op jit(solution)/shard_map/ppermute | solution.py:92
  16.2 1.2 %collective-permute-start.3 = (bf16[2,16,128]{2,1,0:T(8,128)(2,1)S(1)}, bf16[2,16,128]{2,1,0:T(8,128)(2,1)S(1)}, u32[]{:S(2)}, u32[]{:S(2)}) collective-permute-start(bf16[2,16,128]{2,1,0:T(8,128)(2,1)S(1)} %get-tuple-element.98.refs_0_), channel_id=1, source_target_pairs={{0,4},{4,0},{8,12},{12,8},{1,5},{5,1},{9,13},{13,9},{2,6},{6,2},{1... | collective-permute-start | bytes 24584 | tf_op jit(solution)/shard_map/ppermute | solution.py:85
  18.2 11.2 %collective-permute-start.10 = (bf16[2,1,128,512]{3,2,1,0:T(8,128)(2,1)S(1)}, bf16[2,1,128,512]{3,2,1,0:T(8,128)(2,1)S(1)}, u32[]{:S(2)}, u32[]{:S(2)}) collective-permute-start(bf16[2,1,128,512]{3,2,1,0:T(8,128)(2,1)S(1)} %get-tuple-element.103), channel_id=1, source_target_pairs={{0,8},{4,12},{8,0},{12,4},{1,9},{5,13},{9,1},{13,5},{2,10},{6,14},... | collective-permute-start | bytes 786440 | tf_op jit(solution)/shard_map/ppermute | solution.py:81
  20.1 3.7 %collective-permute-start.4 = (f32[3,8,128]{2,1,0:T(8,128)S(1)}, f32[3,8,128]{2,1,0:T(8,128)S(1)}, u32[]{:S(2)}, u32[]{:S(2)}) collective-permute-start(f32[3,8,128]{2,1,0:T(8,128)S(1)} %get-tuple-element.111.refs_1_), channel_id=1, source_target_pairs={{0,16},{16,0},{1,17},{17,1},{2,18},{18,2},{3,19},{19,3},{4,20},{20... | collective-permute-start | bytes 36872 | tf_op jit(solution)/shard_map/ppermute | solution.py:370
  21.6 5.5 %collective-permute-start.8 = (bf16[1,1,128,512]{3,2,1,0:T(8,128)(2,1)S(1)}, bf16[1,1,128,512]{3,2,1,0:T(8,128)(2,1)S(1)}, u32[]{:S(2)}, u32[]{:S(2)}) collective-permute-start(bf16[1,1,128,512]{3,2,1,0:T(8,128)(2,1)S(1)} %get-tuple-element.113), channel_id=1, source_target_pairs={{16,0},{0,16},{17,1},{1,17},{18,2},{2,18},{19,3},{3,19},{20,4},{4,... | collective-permute-start | bytes 393224 | tf_op jit(solution)/shard_map/ppermute | solution.py:92
  23.8 8.9 %collective-permute-start.2 = (bf16[3,1,128,512]{3,2,1,0:T(8,128)(2,1)S(1)}, bf16[3,1,128,512]{3,2,1,0:T(8,128)(2,1)S(1)}, u32[]{:S(2)}, u32[]{:S(2)}) collective-permute-start(bf16[3,1,128,512]{3,2,1,0:T(8,128)(2,1)S(1)} %get-tuple-element.163.refs_1_), channel_id=1, source_target_pairs={{0,4},{4,0},{8,12},{12,8},{1,5},{5,1},{9,13},{13,9},{2,6},{6,2},{1... | collective-permute-start | bytes 1179656 | tf_op jit(solution)/shard_map/ppermute | solution.py:85
  25.0 9.7 %collective-permute-start.15 = (bf16[1,2,1,144,512]{4,3,2,1,0:T(8,128)(2,1)S(1)}, bf16[1,2,1,144,512]{4,3,2,1,0:T(8,128)(2,1)S(1)}, u32[]{:S(2)}, u32[]{:S(2)}) collective-permute-start(bf16[1,2,1,144,512]{4,3,2,1,0:T(8,128)(2,1)S(1)} %get-tuple-element.107), channel_id=1, source_target_pairs={{16,0},{0,16},{17,1},{1,17},{18,2},{2,18},{19,3},{3,19},{20,4},{4,... | collective-permute-start | bytes 884744 | tf_op jit(solution)/shard_map/ppermute | solution.py:92
  27.5 3.7 %collective-permute-start.11 = (bf16[2,1,128,512]{3,2,1,0:T(8,128)(2,1)S(1)}, bf16[2,1,128,512]{3,2,1,0:T(8,128)(2,1)S(1)}, u32[]{:S(2)}, u32[]{:S(2)}) collective-permute-start(bf16[2,1,128,512]{3,2,1,0:T(8,128)(2,1)S(1)} %get-tuple-element.120.refs_4_), channel_id=1, source_target_pairs={{0,4},{4,0},{8,12},{12,8},{1,5},{5,1},{9,13},{13,9},{2,6},{6,2},{1... | collective-permute-start | bytes 786440 | tf_op jit(solution)/shard_map/ppermute | solution.py:85
  29.4 3.2 %collective-permute-start.12 = (bf16[2,1,128,512]{3,2,1,0:T(8,128)(2,1)S(1)}, bf16[2,1,128,512]{3,2,1,0:T(8,128)(2,1)S(1)}, u32[]{:S(2)}, u32[]{:S(2)}) collective-permute-start(bf16[2,1,128,512]{3,2,1,0:T(8,128)(2,1)S(1)} %collective-permute-done.10.refs_5_), channel_id=1, source_target_pairs={{0,4},{4,0},{8,12},{12,8},{1,5},{5,1},{9,13},{13,9},{2,6},{6,2},{1... | collective-permute-start | bytes 786440 | tf_op jit(solution)/shard_map/ppermute | solution.py:85
  29.4 10.6 %collective-permute-start.19 = (bf16[1,2,1,144,512]{4,3,2,1,0:T(8,128)(2,1)S(1)}, bf16[1,2,1,144,512]{4,3,2,1,0:T(8,128)(2,1)S(1)}, u32[]{:S(2)}, u32[]{:S(2)}) collective-permute-start(bf16[1,2,1,144,512]{4,3,2,1,0:T(8,128)(2,1)S(1)} %get-tuple-element.108), channel_id=1, source_target_pairs={{16,0},{0,16},{17,1},{1,17},{18,2},{2,18},{19,3},{3,19},{20,4},{4,... | collective-permute-start | bytes 884744 | tf_op jit(solution)/shard_map/ppermute | solution.py:92
  31.1 5.6 %collective-permute-start.9 = (bf16[1,1,128,512]{3,2,1,0:T(8,128)(2,1)S(1)}, bf16[1,1,128,512]{3,2,1,0:T(8,128)(2,1)S(1)}, u32[]{:S(2)}, u32[]{:S(2)}) collective-permute-start(bf16[1,1,128,512]{3,2,1,0:T(8,128)(2,1)S(1)} %get-tuple-element.104), channel_id=1, source_target_pairs={{0,8},{4,12},{8,0},{12,4},{1,9},{5,13},{9,1},{13,5},{2,10},{6,14},... | collective-permute-start | bytes 393224 | tf_op jit(solution)/shard_map/ppermute | solution.py:81
  32.6 4.1 %collective-permute-start.13 = (bf16[1,1,128,512]{3,2,1,0:T(8,128)(2,1)S(1)}, bf16[1,1,128,512]{3,2,1,0:T(8,128)(2,1)S(1)}, u32[]{:S(2)}, u32[]{:S(2)}) collective-permute-start(bf16[1,1,128,512]{3,2,1,0:T(8,128)(2,1)S(1)} %get-tuple-element.134.refs_4_), channel_id=1, source_target_pairs={{0,4},{4,0},{8,12},{12,8},{1,5},{5,1},{9,13},{13,9},{2,6},{6,2},{1... | collective-permute-start | bytes 393224 | tf_op jit(solution)/shard_map/ppermute | solution.py:85
  34.9 2.4 %collective-permute-start.16 = (bf16[1,1,128,512]{3,2,1,0:T(8,128)(2,1)S(1)}, bf16[1,1,128,512]{3,2,1,0:T(8,128)(2,1)S(1)}, u32[]{:S(2)}, u32[]{:S(2)}) collective-permute-start(bf16[1,1,128,512]{3,2,1,0:T(8,128)(2,1)S(1)} %get-tuple-element.138.refs_8_), channel_id=1, source_target_pairs={{0,4},{4,0},{8,12},{12,8},{1,5},{5,1},{9,13},{13,9},{2,6},{6,2},{1... | collective-permute-start | bytes 393224 | tf_op jit(solution)/shard_map/ppermute | solution.py:85
  35.0 9.9 %collective-permute-start.22 = (bf16[2,1,144,512]{3,2,1,0:T(8,128)(2,1)S(1)}, bf16[2,1,144,512]{3,2,1,0:T(8,128)(2,1)S(1)}, u32[]{:S(2)}, u32[]{:S(2)}) collective-permute-start(bf16[2,1,144,512]{3,2,1,0:T(8,128)(2,1)S(1)} %get-tuple-element.125), channel_id=1, source_target_pairs={{0,8},{4,12},{8,0},{12,4},{1,9},{5,13},{9,1},{13,5},{2,10},{6,14},... | collective-permute-start | bytes 884744 | tf_op jit(solution)/shard_map/ppermute | solution.py:81
  36.7 1.3 %collective-permute-start.17 = (bf16[1,1,128,512]{3,2,1,0:T(8,128)(2,1)S(1)}, bf16[1,1,128,512]{3,2,1,0:T(8,128)(2,1)S(1)}, u32[]{:S(2)}, u32[]{:S(2)}) collective-permute-start(bf16[1,1,128,512]{3,2,1,0:T(8,128)(2,1)S(1)} %get-tuple-element.139.refs_9_), channel_id=1, source_target_pairs={{0,4},{4,0},{8,12},{12,8},{1,5},{5,1},{9,13},{13,9},{2,6},{6,2},{1... | collective-permute-start | bytes 393224 | tf_op jit(solution)/shard_map/ppermute | solution.py:85
  36.8 1.5 %collective-permute-start.14 = (bf16[1,1,128,512]{3,2,1,0:T(8,128)(2,1)S(1)}, bf16[1,1,128,512]{3,2,1,0:T(8,128)(2,1)S(1)}, u32[]{:S(2)}, u32[]{:S(2)}) collective-permute-start(bf16[1,1,128,512]{3,2,1,0:T(8,128)(2,1)S(1)} %collective-permute-done.9.refs_5_), channel_id=1, source_target_pairs={{0,4},{4,0},{8,12},{12,8},{1,5},{5,1},{9,13},{13,9},{2,6},{6,2},{1... | collective-permute-start | bytes 393224 | tf_op jit(solution)/shard_map/ppermute | solution.py:85
  37.3 9.0 %collective-permute-start.23 = (bf16[1,2,1,128,512]{4,3,2,1,0:T(8,128)(2,1)S(1)}, bf16[1,2,1,128,512]{4,3,2,1,0:T(8,128)(2,1)S(1)}, u32[]{:S(2)}, u32[]{:S(2)}) collective-permute-start(bf16[1,2,1,128,512]{4,3,2,1,0:T(8,128)(2,1)S(1)} %get-tuple-element.109), channel_id=1, source_target_pairs={{16,0},{0,16},{17,1},{1,17},{18,2},{2,18},{19,3},{3,19},{20,4},{4,... | collective-permute-start | bytes 786440 | tf_op jit(solution)/shard_map/ppermute | solution.py:92
  40.2 5.5 %collective-permute-start.20 = (bf16[1,1,128,512]{3,2,1,0:T(8,128)(2,1)S(1)}, bf16[1,1,128,512]{3,2,1,0:T(8,128)(2,1)S(1)}, u32[]{:S(2)}, u32[]{:S(2)}) collective-permute-start(bf16[1,1,128,512]{3,2,1,0:T(8,128)(2,1)S(1)} %get-tuple-element.153.refs_4_), channel_id=1, source_target_pairs={{0,4},{4,0},{8,12},{12,8},{1,5},{5,1},{9,13},{13,9},{2,6},{6,2},{1... | collective-permute-start | bytes 393224 | tf_op jit(solution)/shard_map/ppermute | solution.py:85
  40.3 5.4 %collective-permute-start.21 = (bf16[1,1,128,512]{3,2,1,0:T(8,128)(2,1)S(1)}, bf16[1,1,128,512]{3,2,1,0:T(8,128)(2,1)S(1)}, u32[]{:S(2)}, u32[]{:S(2)}) collective-permute-start(bf16[1,1,128,512]{3,2,1,0:T(8,128)(2,1)S(1)} %get-tuple-element.154.refs_5_), channel_id=1, source_target_pairs={{0,4},{4,0},{8,12},{12,8},{1,5},{5,1},{9,13},{13,9},{2,6},{6,2},{1... | collective-permute-start | bytes 393224 | tf_op jit(solution)/shard_map/ppermute | solution.py:85
  40.8 10.4 %collective-permute-start.18 = (bf16[2,1,128,512]{3,2,1,0:T(8,128)(2,1)S(1)}, bf16[2,1,128,512]{3,2,1,0:T(8,128)(2,1)S(1)}, u32[]{:S(2)}, u32[]{:S(2)}) collective-permute-start(bf16[2,1,128,512]{3,2,1,0:T(8,128)(2,1)S(1)} %get-tuple-element.142), channel_id=1, source_target_pairs={{0,8},{4,12},{8,0},{12,4},{1,9},{5,13},{9,1},{13,5},{2,10},{6,14},... | collective-permute-start | bytes 786440 | tf_op jit(solution)/shard_map/ppermute | solution.py:81
  46.5 1.4 %collective-permute-start.24 = (bf16[1,1,128,512]{3,2,1,0:T(8,128)(2,1)S(1)}, bf16[1,1,128,512]{3,2,1,0:T(8,128)(2,1)S(1)}, u32[]{:S(2)}, u32[]{:S(2)}) collective-permute-start(bf16[1,1,128,512]{3,2,1,0:T(8,128)(2,1)S(1)} %get-tuple-element.166.refs_4_), channel_id=1, source_target_pairs={{0,4},{4,0},{8,12},{12,8},{1,5},{5,1},{9,13},{13,9},{2,6},{6,2},{1... | collective-permute-start | bytes 393224 | tf_op jit(solution)/shard_map/ppermute | solution.py:85
  46.6 1.5 %collective-permute-start.25 = (bf16[1,1,128,512]{3,2,1,0:T(8,128)(2,1)S(1)}, bf16[1,1,128,512]{3,2,1,0:T(8,128)(2,1)S(1)}, u32[]{:S(2)}, u32[]{:S(2)}) collective-permute-start(bf16[1,1,128,512]{3,2,1,0:T(8,128)(2,1)S(1)} %get-tuple-element.167.refs_5_), channel_id=1, source_target_pairs={{0,4},{4,0},{8,12},{12,8},{1,5},{5,1},{9,13},{13,9},{2,6},{6,2},{1... | collective-permute-start | bytes 393224 | tf_op jit(solution)/shard_map/ppermute | solution.py:85
  47.1 6.4 %collective-permute-start.27 = (bf16[1,1,128,512]{3,2,1,0:T(8,128)(2,1)S(1)}, bf16[1,1,128,512]{3,2,1,0:T(8,128)(2,1)S(1)}, u32[]{:S(2)}, u32[]{:S(2)}) collective-permute-start(bf16[1,1,128,512]{3,2,1,0:T(8,128)(2,1)S(1)} %get-tuple-element.158), channel_id=1, source_target_pairs={{0,8},{4,12},{8,0},{12,4},{1,9},{5,13},{9,1},{13,5},{2,10},{6,14},... | collective-permute-start | bytes 393224 | tf_op jit(solution)/shard_map/ppermute | solution.py:81
  48.6 7.0 %collective-permute-start.26 = (bf16[1,1,128,512]{3,2,1,0:T(8,128)(2,1)S(1)}, bf16[1,1,128,512]{3,2,1,0:T(8,128)(2,1)S(1)}, u32[]{:S(2)}, u32[]{:S(2)}) collective-permute-start(bf16[1,1,128,512]{3,2,1,0:T(8,128)(2,1)S(1)} %get-tuple-element.171), channel_id=1, source_target_pairs={{0,8},{4,12},{8,0},{12,4},{1,9},{5,13},{9,1},{13,5},{2,10},{6,14},... | collective-permute-start | bytes 393224 | tf_op jit(solution)/shard_map/ppermute | solution.py:81

commit v13 on v12

--- a/solution.py
+++ b/solution.py
@@ -229,7 +229,7 @@
                         chunks(r, body)
 
             (table,) = after([table], *earlier)
-            spare = [STEP] * (len(groups) - 1) + [0]
+            spare = [STEP] + [0] * (len(groups) - 1)
             shapes = [(len(group), owners, owned, r + x, o) for group, x in zip(groups, spare)]
             return call(kernel, shapes, "partial_sums", table, greater_in, *rows)
 
@@ -423,7 +423,7 @@
         sigmas = {}
         steps = ["L0", "a0", "L1+G0"]
         for n in range(1, e):
-            steps += [f"a{n}", "pL0", f"G{n}"] if n == 1 else [f"a{n}", f"G{n}"]
+            steps += [f"a{n}", f"G{n}", "pL0"] if n == 1 else [f"a{n}", f"G{n}"]
         for step in steps:
             if step[0] == "p":
                 last = put(step[1], lambda part: len(step) < 3 or part[4] == int(step[2]), last)

time: 56.5 us -> 56 us (level)
  waiting for transfers between devices: 23.6 us -> 22.5 us
  starting transfers between devices: 20.1 us -> 20.7 us
    ppermute x8, waiting for transfers between devices: 17.9 us -> 14.5 us  [to_owner(): return lax.ppermute(x, 'ph', pairs)]
    ppermute x6, waiting for transfers between devices: 2.26 us -> 3.53 us  [from_energy(): return lax.ppermute(x, 'en', [((i + t) % en, i) for i in range(en)])]
    ppermute x13, waiting for transfers between devices: 1.81 us -> 2.86 us  [to_lanes(): lax.ppermute(x, 'ph', [(p, p // lanes * lanes + (p % lanes + q) % lanes)...]
    ppermute x6, starting transfers between devices: 6.94 us -> 7.83 us  [from_energy(): return lax.ppermute(x, 'en', [((i + t) % en, i) for i in range(en)])]
  transfers between devices with their start and end apart: 28 -> 28, of which waited for: 15 -> 16; matrix products, arithmetic and copies ran while one was open for 0% -> 0% of each run, Pallas kernels for 16% -> 16%
where the time goes in v13:
time: 56 us; the launch traced here: 55.9 us
  waiting for transfers between devices  22.5 us (40%)
  starting transfers between devices  20.7 us (37%)
  Pallas kernels  11.7 us (21%)
  between operations  0.89 us (2%)
    ppermute x8, waiting for transfers between devices, to_owner(): return lax.ppermute(x, 'ph', pairs)  14.5 us
    ppermute x8, starting transfers between devices, to_owner(): return lax.ppermute(x, 'ph', pairs)  9.24 us
    ppermute x6, starting transfers between devices, from_energy(): return lax.ppermute(x, 'en', [((i + t) % en, i) for i in range(en)])  7.83 us
    pallas_call x7, Pallas kernels, place(): pl.pallas_call(kernel, in_specs=[WHOLE] * len(arrays) + [far] * (result i...  4.95 us
    pallas_call x14, Pallas kernels, call(): pl.pallas_call(kernel, in_specs=[WHOLE] * len(args), out_specs=[WHOLE] *...  4.77 us
    ppermute x6, waiting for transfers between devices, from_energy(): return lax.ppermute(x, 'en', [((i + t) % en, i) for i in range(en)])  3.53 us
    ppermute x13, waiting for transfers between devices, to_lanes(): lax.ppermute(x, 'ph', [(p, p // lanes * lanes + (p % lanes + q) % lanes)...  2.86 us
    ppermute x13, starting transfers between devices, to_lanes(): lax.ppermute(x, 'ph', [(p, p // lanes * lanes + (p % lanes + q) % lanes)...  2.16 us
  transfers between devices with their start and end apart: 28, of which 16 were waited for; matrix products, arithmetic and copies ran while one was open for 0% of the time, Pallas kernels for 16%

profile of v13, /device:TPU:0, one launch (start us, length us, event | category | flops | bytes accessed | tf_op | source)
XLA Modules:
  0.0 55.9 jit_solution(555856576757149240)
XLA Ops:
  0.7 2.0 %lead.1.refs_0_ = bf16[400,512]{1,0:T(8,128)(2,1)} custom-call(s32[2,3]{1,0:T(2,128)} %bitcast.2, f32[2,3]{1,0:T(2,128)} %bitcast.3, bf16[3,2,128,512]{3,2,1,0:T(8,128)(2,1)} %refs_1_), custom_call_target="tpu_custom_call" | custom-call | flops 1 | bytes 1 | tf_op jit(solution)/shard_map/lead/pallas_call | solution.py:146
  2.6 0.0 copy-start
  2.6 3.0 %collective-permute-start = (bf16[400,512]{1,0:T(8,128)(2,1)}, bf16[400,512]{1,0:T(8,128)(2,1)S(1)}, u32[]{:S(2)}, u32[]{:S(2)}) collective-permute-start(bf16[400,512]{1,0:T(8,128)(2,1)} %lead.1.refs_0_), channel_id=1, source_target_pairs={{0,8},{4,12},{8,0},{12,4},{1,9},{5,13},{9,1},{13,5},{2,10},{6,14},... | collective-permute-start | bytes 1228808 | tf_op jit(solution)/shard_map/ppermute | solution.py:81
  5.7 0.0 copy-start.3
  5.7 1.6 %collective-permute-start.5 = (bf16[3,1,128,512]{3,2,1,0:T(8,128)(2,1)S(1)}, bf16[3,1,128,512]{3,2,1,0:T(8,128)(2,1)S(1)}, u32[]{:S(2)}, u32[]{:S(2)}) collective-permute-start(bf16[3,1,128,512]{3,2,1,0:T(8,128)(2,1)S(1)} %cut.2), channel_id=1, source_target_pairs={{16,0},{0,16},{17,1},{1,17},{18,2},{2,18},{19,3},{3,19},{20,4},{4,... | collective-permute-start | bytes 1179656 | tf_op jit(solution)/shard_map/ppermute | solution.py:92
  7.3 0.1 cut.3
  7.4 0.1 collective-permute-start.1
  7.4 0.6 %collective-permute-start.6 = (bf16[3,1,128,512]{3,2,1,0:T(8,128)(2,1)S(1)}, bf16[3,1,128,512]{3,2,1,0:T(8,128)(2,1)S(1)}, u32[]{:S(2)}, u32[]{:S(2)}) collective-permute-start(bf16[3,1,128,512]{3,2,1,0:T(8,128)(2,1)S(1)} %get-tuple-element.106), channel_id=1, source_target_pairs={{0,8},{4,12},{8,0},{12,4},{1,9},{5,13},{9,1},{13,5},{2,10},{6,14},... | collective-permute-start | bytes 1179656 | tf_op jit(solution)/shard_map/ppermute | solution.py:81
  8.0 0.4 collective-permute-start.7
  8.4 7.7 %collective-permute-done.refs_1_ = bf16[400,512]{1,0:T(8,128)(2,1)S(1)} collective-permute-done((bf16[400,512]{1,0:T(8,128)(2,1)}, bf16[400,512]{1,0:T(8,128)(2,1)S(1)}, u32[]{:S(2)}, u32[]{:S(2)}) %collective-permute-start) | collective-permute-done | bytes 409632 | tf_op jit(solution)/shard_map/ppermute | solution.py:81
  16.2 0.1 collective-permute-start.3
  16.3 1.2 %collective-permute-done.3.refs_1_ = bf16[2,16,128]{2,1,0:T(8,128)(2,1)S(1)} collective-permute-done((bf16[2,16,128]{2,1,0:T(8,128)(2,1)S(1)}, bf16[2,16,128]{2,1,0:T(8,128)(2,1)S(1)}, u32[]{:S(2)}, u32[]{:S(2)}) %collective-permute-start.3) | collective-permute-done | bytes 8224 | tf_op jit(solution)/shard_map/ppermute | solution.py:85
  17.5 0.1 weights.1
  17.6 0.3 collective-permute-done.5.refs_3_
  17.8 0.4 mix.2
  18.2 1.9 %collective-permute-start.10 = (bf16[2,1,128,512]{3,2,1,0:T(8,128)(2,1)S(1)}, bf16[2,1,128,512]{3,2,1,0:T(8,128)(2,1)S(1)}, u32[]{:S(2)}, u32[]{:S(2)}) collective-permute-start(bf16[2,1,128,512]{3,2,1,0:T(8,128)(2,1)S(1)} %get-tuple-element.103), channel_id=1, source_target_pairs={{0,8},{4,12},{8,0},{12,4},{1,9},{5,13},{9,1},{13,5},{2,10},{6,14},... | collective-permute-start | bytes 786440 | tf_op jit(solution)/shard_map/ppermute | solution.py:81
  20.1 1.5 %collective-permute-start.4 = (f32[3,8,128]{2,1,0:T(8,128)S(1)}, f32[3,8,128]{2,1,0:T(8,128)S(1)}, u32[]{:S(2)}, u32[]{:S(2)}) collective-permute-start(f32[3,8,128]{2,1,0:T(8,128)S(1)} %get-tuple-element.111.refs_1_), channel_id=1, source_target_pairs={{0,16},{16,0},{1,17},{17,1},{2,18},{18,2},{3,19},{19,3},{4,20},{20... | collective-permute-start | bytes 36872 | tf_op jit(solution)/shard_map/ppermute | solution.py:370
  21.6 0.5 collective-permute-start.8
  22.1 1.7 %collective-permute-done.4.table_ref = f32[3,8,128]{2,1,0:T(8,128)S(1)} collective-permute-done((f32[3,8,128]{2,1,0:T(8,128)S(1)}, f32[3,8,128]{2,1,0:T(8,128)S(1)}, u32[]{:S(2)}, u32[]{:S(2)}) %collective-permute-start.4) | collective-permute-done | bytes 12320 | tf_op jit(solution)/shard_map/ppermute | solution.py:370
  23.8 0.0 collective-permute-start.2
  23.8 0.8 %collective-permute-done.6.refs_1_ = bf16[3,1,128,512]{3,2,1,0:T(8,128)(2,1)S(1)} collective-permute-done((bf16[3,1,128,512]{3,2,1,0:T(8,128)(2,1)S(1)}, bf16[3,1,128,512]{3,2,1,0:T(8,128)(2,1)S(1)}, u32[]{:S(2)}, u32[]{:S(2)}) %collective-permute-start.6) | collective-permute-done | bytes 393248 | tf_op jit(solution)/shard_map/ppermute | solution.py:81
  24.6 0.4 partial_sums.1
  25.0 2.1 %collective-permute-start.15 = (bf16[1,2,1,144,512]{4,3,2,1,0:T(8,128)(2,1)S(1)}, bf16[1,2,1,144,512]{4,3,2,1,0:T(8,128)(2,1)S(1)}, u32[]{:S(2)}, u32[]{:S(2)}) collective-permute-start(bf16[1,2,1,144,512]{4,3,2,1,0:T(8,128)(2,1)S(1)} %get-tuple-element.107), channel_id=1, source_target_pairs={{16,0},{0,16},{17,1},{1,17},{18,2},{2,18},{19,3},{3,19},{20,4},{4,... | collective-permute-start | bytes 884744 | tf_op jit(solution)/shard_map/ppermute | solution.py:92
  27.1 0.4 mix.3
  27.5 0.1 collective-permute-start.11
  27.5 1.9 %collective-permute-done.10.refs_5_ = bf16[2,1,128,512]{3,2,1,0:T(8,128)(2,1)S(1)} collective-permute-done((bf16[2,1,128,512]{3,2,1,0:T(8,128)(2,1)S(1)}, bf16[2,1,128,512]{3,2,1,0:T(8,128)(2,1)S(1)}, u32[]{:S(2)}, u32[]{:S(2)}) %collective-permute-start.10) | collective-permute-done | bytes 262176 | tf_op jit(solution)/shard_map/ppermute | solution.py:81
  29.4 0.0 collective-permute-start.12
  29.4 1.7 %collective-permute-start.9 = (bf16[1,1,128,512]{3,2,1,0:T(8,128)(2,1)S(1)}, bf16[1,1,128,512]{3,2,1,0:T(8,128)(2,1)S(1)}, u32[]{:S(2)}, u32[]{:S(2)}) collective-permute-start(bf16[1,1,128,512]{3,2,1,0:T(8,128)(2,1)S(1)} %get-tuple-element.104), channel_id=1, source_target_pairs={{0,8},{4,12},{8,0},{12,4},{1,9},{5,13},{9,1},{13,5},{2,10},{6,14},... | collective-permute-start | bytes 393224 | tf_op jit(solution)/shard_map/ppermute | solution.py:81
  31.1 0.2 collective-permute-start.13
  31.4 1.5 %collective-permute-start.19 = (bf16[1,2,1,128,512]{4,3,2,1,0:T(8,128)(2,1)S(1)}, bf16[1,2,1,128,512]{4,3,2,1,0:T(8,128)(2,1)S(1)}, u32[]{:S(2)}, u32[]{:S(2)}) collective-permute-start(bf16[1,2,1,128,512]{4,3,2,1,0:T(8,128)(2,1)S(1)} %get-tuple-element.108), channel_id=1, source_target_pairs={{16,0},{0,16},{17,1},{1,17},{18,2},{2,18},{19,3},{3,19},{20,4},{4,... | collective-permute-start | bytes 786440 | tf_op jit(solution)/shard_map/ppermute | solution.py:92
  32.9 0.9 %product.4 = (bf16[2,1,128,512]{3,2,1,0:T(8,128)(2,1)S(1)}, bf16[2,1,144,512]{3,2,1,0:T(8,128)(2,1)S(1)}) custom-call(bf16[3,1,128,512]{3,2,1,0:T(8,128)(2,1)S(1)} %get-tuple-element.162.refs_0_, bf16[3,1,128,512]{3,2,1,0:T(8,128)(2,1)S(1)} %get-tuple-element.163.refs_1_, bf16[3,1,128,512]{3,2,1,0:T(8,128)(2,1)S(1)} %collective-permute-done.1.refs_2_, ...), custom_call_target="tpu_custom_call" | custom-call | flops 1 | bytes 1 | tf_op jit(solution)/shard_map/product/pallas_call | solution.py:21
  33.8 0.2 add_partial.3
  34.0 0.1 collective-permute-start.16
  34.1 0.6 %collective-permute-start.22 = (bf16[2,1,144,512]{3,2,1,0:T(8,128)(2,1)S(1)}, bf16[2,1,144,512]{3,2,1,0:T(8,128)(2,1)S(1)}, u32[]{:S(2)}, u32[]{:S(2)}) collective-permute-start(bf16[2,1,144,512]{3,2,1,0:T(8,128)(2,1)S(1)} %get-tuple-element.125), channel_id=1, source_target_pairs={{0,8},{4,12},{8,0},{12,4},{1,9},{5,13},{9,1},{13,5},{2,10},{6,14},... | collective-permute-start | bytes 884744 | tf_op jit(solution)/shard_map/ppermute | solution.py:81
  34.7 0.6 %collective-permute-done.9.refs_5_ = bf16[1,1,128,512]{3,2,1,0:T(8,128)(2,1)S(1)} collective-permute-done((bf16[1,1,128,512]{3,2,1,0:T(8,128)(2,1)S(1)}, bf16[1,1,128,512]{3,2,1,0:T(8,128)(2,1)S(1)}, u32[]{:S(2)}, u32[]{:S(2)}) %collective-permute-start.9) | collective-permute-done | bytes 131104 | tf_op jit(solution)/shard_map/ppermute | solution.py:81
  35.3 0.5 collective-permute-start.14
  35.8 1.7 %collective-permute-start.23 = (bf16[1,2,1,128,512]{4,3,2,1,0:T(8,128)(2,1)S(1)}, bf16[1,2,1,128,512]{4,3,2,1,0:T(8,128)(2,1)S(1)}, u32[]{:S(2)}, u32[]{:S(2)}) collective-permute-start(bf16[1,2,1,128,512]{4,3,2,1,0:T(8,128)(2,1)S(1)} %get-tuple-element.109), channel_id=1, source_target_pairs={{16,0},{0,16},{17,1},{1,17},{18,2},{2,18},{19,3},{3,19},{20,4},{4,... | collective-permute-start | bytes 786440 | tf_op jit(solution)/shard_map/ppermute | solution.py:92
  37.5 0.9 %product.5 = (bf16[2,1,128,512]{3,2,1,0:T(8,128)(2,1)S(1)}, bf16[2,1,128,512]{3,2,1,0:T(8,128)(2,1)S(1)}) custom-call(bf16[3,1,128,512]{3,2,1,0:T(8,128)(2,1)S(1)} %get-tuple-element.162.refs_0_, bf16[3,1,128,512]{3,2,1,0:T(8,128)(2,1)S(1)} %get-tuple-element.163.refs_1_, bf16[3,1,128,512]{3,2,1,0:T(8,128)(2,1)S(1)} %collective-permute-done.1.refs_2_, ...), custom_call_target="tpu_custom_call" | custom-call | flops 1 | bytes 1 | tf_op jit(solution)/shard_map/product/pallas_call | solution.py:21
  38.4 2.1 %collective-permute-done.19.refs_2_ = bf16[1,2,1,128,512]{4,3,2,1,0:T(8,128)(2,1)S(1)} collective-permute-done((bf16[1,2,1,128,512]{4,3,2,1,0:T(8,128)(2,1)S(1)}, bf16[1,2,1,128,512]{4,3,2,1,0:T(8,128)(2,1)S(1)}, u32[]{:S(2)}, u32[]{:S(2)}) %collective-permute-start.19) | collective-permute-done | bytes 262176 | tf_op jit(solution)/shard_map/ppermute | solution.py:92
  40.5 0.2 add_partial.4
  40.7 0.1 collective-permute-start.20
  40.8 0.5 collective-permute-start.21
  41.3 0.8 %collective-permute-done.20.refs_6_ = bf16[1,1,128,512]{3,2,1,0:T(8,128)(2,1)S(1)} collective-permute-done((bf16[1,1,128,512]{3,2,1,0:T(8,128)(2,1)S(1)}, bf16[1,1,128,512]{3,2,1,0:T(8,128)(2,1)S(1)}, u32[]{:S(2)}, u32[]{:S(2)}) %collective-permute-start.20) | collective-permute-done | bytes 131104 | tf_op jit(solution)/shard_map/ppermute | solution.py:85
  42.1 0.2 collective-permute-done.21.refs_7_
  42.3 0.5 product.6
  42.9 0.6 %collective-permute-done.22.refs_1_ = bf16[2,1,144,512]{3,2,1,0:T(8,128)(2,1)S(1)} collective-permute-done((bf16[2,1,144,512]{3,2,1,0:T(8,128)(2,1)S(1)}, bf16[2,1,144,512]{3,2,1,0:T(8,128)(2,1)S(1)}, u32[]{:S(2)}, u32[]{:S(2)}) %collective-permute-start.22) | collective-permute-done | bytes 294944 | tf_op jit(solution)/shard_map/ppermute | solution.py:81
  43.5 0.8 %place.7.refs_1_ = bf16[3,2,128,512]{3,2,1,0:T(8,128)(2,1)} custom-call(bf16[2,1,128,512]{3,2,1,0:T(8,128)(2,1)S(1)} %get-tuple-element.157.refs_0_, bf16[2,1,144,512]{3,2,1,0:T(8,128)(2,1)S(1)} %collective-permute-done.22.refs_1_), custom_call_target="tpu_custom_call" | custom-call | flops 1 | bytes 1 | tf_op jit(solution)/shard_map/place/pallas_call | solution.py:318
  44.3 1.2 %collective-permute-done.23.refs_2_ = bf16[1,2,1,128,512]{4,3,2,1,0:T(8,128)(2,1)S(1)} collective-permute-done((bf16[1,2,1,128,512]{4,3,2,1,0:T(8,128)(2,1)S(1)}, bf16[1,2,1,128,512]{4,3,2,1,0:T(8,128)(2,1)S(1)}, u32[]{:S(2)}, u32[]{:S(2)}) %collective-permute-start.23) | collective-permute-done | bytes 262176 | tf_op jit(solution)/shard_map/ppermute | solution.py:92
  45.5 0.2 add_partial.5
  45.7 0.1 collective-permute-start.24
  45.8 0.5 collective-permute-start.25
  46.3 0.4 collective-permute-start.27
  46.6 0.5 collective-permute-done.24.refs_6_
  47.1 0.2 collective-permute-done.25.refs_7_
  47.3 0.5 product.7
  47.8 1.1 %collective-permute-start.26 = (bf16[1,1,128,512]{3,2,1,0:T(8,128)(2,1)S(1)}, bf16[1,1,128,512]{3,2,1,0:T(8,128)(2,1)S(1)}, u32[]{:S(2)}, u32[]{:S(2)}) collective-permute-start(bf16[1,1,128,512]{3,2,1,0:T(8,128)(2,1)S(1)} %get-tuple-element.171), channel_id=1, source_target_pairs={{0,8},{4,12},{8,0},{12,4},{1,9},{5,13},{9,1},{13,5},{2,10},{6,14},... | collective-permute-start | bytes 393224 | tf_op jit(solution)/shard_map/ppermute | solution.py:81
  48.9 0.7 %place.8.refs_1_ = bf16[3,2,128,512]{3,2,1,0:T(8,128)(2,1)} custom-call(bf16[2,1,128,512]{3,2,1,0:T(8,128)(2,1)S(1)} %get-tuple-element.173.refs_0_, bf16[3,2,128,512]{3,2,1,0:T(8,128)(2,1)} %place.7.refs_1_), custom_call_target="tpu_custom_call", output_to_operand_aliasing={{}: (1, {})} | custom-call | flops 1 | bytes 1 | tf_op jit(solution)/shard_map/place/pallas_call | solution.py:318
  49.6 0.8 %place.9.refs_1_ = bf16[3,2,128,512]{3,2,1,0:T(8,128)(2,1)} custom-call(bf16[2,1,128,512]{3,2,1,0:T(8,128)(2,1)S(1)} %get-tuple-element.173.refs_0_, bf16[1,1,128,512]{3,2,1,0:T(8,128)(2,1)S(1)} %get-tuple-element.174.refs_1_, bf16[1,1,128,512]{3,2,1,0:T(8,128)(2,1)S(1)} %get-tuple-element.175.refs_2_), custom_call_target="tpu_custom_call" | custom-call | flops 1 | bytes 1 | tf_op jit(solution)/shard_map/place/pallas_call | solution.py:318
  50.4 0.7 %place.10 = bf16[3,2,128,512]{3,2,1,0:T(8,128)(2,1)} custom-call(bf16[2,1,128,512]{3,2,1,0:T(8,128)(2,1)S(1)} %collective-permute-done.18.refs_0_, bf16[3,2,128,512]{3,2,1,0:T(8,128)(2,1)} %place.8.refs_1_), custom_call_target="tpu_custom_call", output_to_operand_aliasing={{}: (1, {})} | custom-call | flops 1 | bytes 1 | tf_op jit(solution)/shard_map/place/pallas_call | solution.py:318
  51.1 0.7 %place.11.refs_1_ = bf16[3,2,128,512]{3,2,1,0:T(8,128)(2,1)} custom-call(bf16[2,1,128,512]{3,2,1,0:T(8,128)(2,1)S(1)} %collective-permute-done.18.refs_0_, bf16[3,2,128,512]{3,2,1,0:T(8,128)(2,1)} %place.9.refs_1_), custom_call_target="tpu_custom_call", output_to_operand_aliasing={{}: (1, {})} | custom-call | flops 1 | bytes 1 | tf_op jit(solution)/shard_map/place/pallas_call | solution.py:318
  51.8 1.2 %collective-permute-done.27.refs_0_ = bf16[1,1,128,512]{3,2,1,0:T(8,128)(2,1)S(1)} collective-permute-done((bf16[1,1,128,512]{3,2,1,0:T(8,128)(2,1)S(1)}, bf16[1,1,128,512]{3,2,1,0:T(8,128)(2,1)S(1)}, u32[]{:S(2)}, u32[]{:S(2)}) %collective-permute-start.27) | collective-permute-done | bytes 131104 | tf_op jit(solution)/shard_map/ppermute | solution.py:81
  53.0 0.7 %place.12.refs_1_ = bf16[3,2,128,512]{3,2,1,0:T(8,128)(2,1)} custom-call(bf16[1,1,128,512]{3,2,1,0:T(8,128)(2,1)S(1)} %collective-permute-done.27.refs_0_, bf16[3,2,128,512]{3,2,1,0:T(8,128)(2,1)} %place.11.refs_1_), custom_call_target="tpu_custom_call", output_to_operand_aliasing={{}: (1, {})} | custom-call | flops 1 | bytes 1 | tf_op jit(solution)/shard_map/place/pallas_call | solution.py:318
  53.7 1.6 %collective-permute-done.26.refs_0_ = bf16[1,1,128,512]{3,2,1,0:T(8,128)(2,1)S(1)} collective-permute-done((bf16[1,1,128,512]{3,2,1,0:T(8,128)(2,1)S(1)}, bf16[1,1,128,512]{3,2,1,0:T(8,128)(2,1)S(1)}, u32[]{:S(2)}, u32[]{:S(2)}) %collective-permute-start.26) | collective-permute-done | bytes 131104 | tf_op jit(solution)/shard_map/ppermute | solution.py:81
  55.2 0.7 %place.13 = bf16[3,2,128,512]{3,2,1,0:T(8,128)(2,1)} custom-call(bf16[1,1,128,512]{3,2,1,0:T(8,128)(2,1)S(1)} %collective-permute-done.26.refs_0_, bf16[3,2,128,512]{3,2,1,0:T(8,128)(2,1)} %place.12.refs_1_), custom_call_target="tpu_custom_call", output_to_operand_aliasing={{}: (1, {})} | custom-call | flops 1 | bytes 1 | tf_op jit(solution)/shard_map/place/pallas_call | solution.py:318
  (22 shorter events, 0.1 us)
Async XLA Ops:
  0.6 5.0 %copy-start.1 = (bf16[3,2,128,512]{3,2,1,0:T(8,128)(2,1)S(1)}, bf16[3,2,128,512]{3,2,1,0:T(8,128)(2,1)}, u32[]{:S(2)}) copy-start(bf16[3,2,128,512]{3,2,1,0:T(8,128)(2,1)} %refs_2_.4) | copy-start | bytes 2359300
  0.6 6.6 %copy-start.2 = (bf16[3,2,128,512]{3,2,1,0:T(8,128)(2,1)S(1)}, bf16[3,2,128,512]{3,2,1,0:T(8,128)(2,1)}, u32[]{:S(2)}) copy-start(bf16[3,2,128,512]{3,2,1,0:T(8,128)(2,1)} %refs_1_) | copy-start | bytes 2359300
  2.6 4.7 %copy-start = (bf16[3,2,128,512]{3,2,1,0:T(8,128)(2,1)S(1)}, bf16[3,2,128,512]{3,2,1,0:T(8,128)(2,1)}, u32[]{:S(2)}) copy-start(bf16[3,2,128,512]{3,2,1,0:T(8,128)(2,1)} %refs_0_.9) | copy-start | bytes 2359300
  2.6 13.5 %collective-permute-start = (bf16[400,512]{1,0:T(8,128)(2,1)}, bf16[400,512]{1,0:T(8,128)(2,1)S(1)}, u32[]{:S(2)}, u32[]{:S(2)}) collective-permute-start(bf16[400,512]{1,0:T(8,128)(2,1)} %lead.1.refs_0_), channel_id=1, source_target_pairs={{0,8},{4,12},{8,0},{12,4},{1,9},{5,13},{9,1},{13,5},{2,10},{6,14},... | collective-permute-start | bytes 1228808 | tf_op jit(solution)/shard_map/ppermute | solution.py:81
  5.7 10.5 %copy-start.3 = (bf16[400,512]{1,0:T(8,128)(2,1)S(1)}, bf16[400,512]{1,0:T(8,128)(2,1)}, u32[]{:S(2)}) copy-start(bf16[400,512]{1,0:T(8,128)(2,1)} %lead.1.refs_0_) | copy-start | bytes 1228804
  5.7 12.1 %collective-permute-start.5 = (bf16[3,1,128,512]{3,2,1,0:T(8,128)(2,1)S(1)}, bf16[3,1,128,512]{3,2,1,0:T(8,128)(2,1)S(1)}, u32[]{:S(2)}, u32[]{:S(2)}) collective-permute-start(bf16[3,1,128,512]{3,2,1,0:T(8,128)(2,1)S(1)} %cut.2), channel_id=1, source_target_pairs={{16,0},{0,16},{17,1},{1,17},{18,2},{2,18},{19,3},{3,19},{20,4},{4,... | collective-permute-start | bytes 1179656 | tf_op jit(solution)/shard_map/ppermute | solution.py:92
  7.4 14.2 %collective-permute-start.1 = (bf16[3,1,128,512]{3,2,1,0:T(8,128)(2,1)S(1)}, bf16[3,1,128,512]{3,2,1,0:T(8,128)(2,1)S(1)}, u32[]{:S(2)}, u32[]{:S(2)}) collective-permute-start(bf16[3,1,128,512]{3,2,1,0:T(8,128)(2,1)S(1)} %get-tuple-element.162.refs_0_), channel_id=1, source_target_pairs={{0,4},{4,0},{8,12},{12,8},{1,5},{5,1},{9,13},{13,9},{2,6},{6,2},{1... | collective-permute-start | bytes 1179656 | tf_op jit(solution)/shard_map/ppermute | solution.py:85
  7.4 17.2 %collective-permute-start.6 = (bf16[3,1,128,512]{3,2,1,0:T(8,128)(2,1)S(1)}, bf16[3,1,128,512]{3,2,1,0:T(8,128)(2,1)S(1)}, u32[]{:S(2)}, u32[]{:S(2)}) collective-permute-start(bf16[3,1,128,512]{3,2,1,0:T(8,128)(2,1)S(1)} %get-tuple-element.106), channel_id=1, source_target_pairs={{0,8},{4,12},{8,0},{12,4},{1,9},{5,13},{9,1},{13,5},{2,10},{6,14},... | collective-permute-start | bytes 1179656 | tf_op jit(solution)/shard_map/ppermute | solution.py:81
  8.0 19.1 %collective-permute-start.7 = (bf16[2,1,144,512]{3,2,1,0:T(8,128)(2,1)S(1)}, bf16[2,1,144,512]{3,2,1,0:T(8,128)(2,1)S(1)}, u32[]{:S(2)}, u32[]{:S(2)}) collective-permute-start(bf16[2,1,144,512]{3,2,1,0:T(8,128)(2,1)S(1)} %get-tuple-element.112), channel_id=1, source_target_pairs={{16,0},{0,16},{17,1},{1,17},{18,2},{2,18},{19,3},{3,19},{20,4},{4,... | collective-permute-start | bytes 884744 | tf_op jit(solution)/shard_map/ppermute | solution.py:92
  16.2 1.2 %collective-permute-start.3 = (bf16[2,16,128]{2,1,0:T(8,128)(2,1)S(1)}, bf16[2,16,128]{2,1,0:T(8,128)(2,1)S(1)}, u32[]{:S(2)}, u32[]{:S(2)}) collective-permute-start(bf16[2,16,128]{2,1,0:T(8,128)(2,1)S(1)} %get-tuple-element.98.refs_0_), channel_id=1, source_target_pairs={{0,4},{4,0},{8,12},{12,8},{1,5},{5,1},{9,13},{13,9},{2,6},{6,2},{1... | collective-permute-start | bytes 24584 | tf_op jit(solution)/shard_map/ppermute | solution.py:85
  18.2 11.2 %collective-permute-start.10 = (bf16[2,1,128,512]{3,2,1,0:T(8,128)(2,1)S(1)}, bf16[2,1,128,512]{3,2,1,0:T(8,128)(2,1)S(1)}, u32[]{:S(2)}, u32[]{:S(2)}) collective-permute-start(bf16[2,1,128,512]{3,2,1,0:T(8,128)(2,1)S(1)} %get-tuple-element.103), channel_id=1, source_target_pairs={{0,8},{4,12},{8,0},{12,4},{1,9},{5,13},{9,1},{13,5},{2,10},{6,14},... | collective-permute-start | bytes 786440 | tf_op jit(solution)/shard_map/ppermute | solution.py:81
  20.1 3.7 %collective-permute-start.4 = (f32[3,8,128]{2,1,0:T(8,128)S(1)}, f32[3,8,128]{2,1,0:T(8,128)S(1)}, u32[]{:S(2)}, u32[]{:S(2)}) collective-permute-start(f32[3,8,128]{2,1,0:T(8,128)S(1)} %get-tuple-element.111.refs_1_), channel_id=1, source_target_pairs={{0,16},{16,0},{1,17},{17,1},{2,18},{18,2},{3,19},{19,3},{4,20},{20... | collective-permute-start | bytes 36872 | tf_op jit(solution)/shard_map/ppermute | solution.py:370
  21.6 5.5 %collective-permute-start.8 = (bf16[1,1,128,512]{3,2,1,0:T(8,128)(2,1)S(1)}, bf16[1,1,128,512]{3,2,1,0:T(8,128)(2,1)S(1)}, u32[]{:S(2)}, u32[]{:S(2)}) collective-permute-start(bf16[1,1,128,512]{3,2,1,0:T(8,128)(2,1)S(1)} %get-tuple-element.113), channel_id=1, source_target_pairs={{16,0},{0,16},{17,1},{1,17},{18,2},{2,18},{19,3},{3,19},{20,4},{4,... | collective-permute-start | bytes 393224 | tf_op jit(solution)/shard_map/ppermute | solution.py:92
  23.8 7.6 %collective-permute-start.2 = (bf16[3,1,128,512]{3,2,1,0:T(8,128)(2,1)S(1)}, bf16[3,1,128,512]{3,2,1,0:T(8,128)(2,1)S(1)}, u32[]{:S(2)}, u32[]{:S(2)}) collective-permute-start(bf16[3,1,128,512]{3,2,1,0:T(8,128)(2,1)S(1)} %get-tuple-element.163.refs_1_), channel_id=1, source_target_pairs={{0,4},{4,0},{8,12},{12,8},{1,5},{5,1},{9,13},{13,9},{2,6},{6,2},{1... | collective-permute-start | bytes 1179656 | tf_op jit(solution)/shard_map/ppermute | solution.py:85
  25.0 8.8 %collective-permute-start.15 = (bf16[1,2,1,144,512]{4,3,2,1,0:T(8,128)(2,1)S(1)}, bf16[1,2,1,144,512]{4,3,2,1,0:T(8,128)(2,1)S(1)}, u32[]{:S(2)}, u32[]{:S(2)}) collective-permute-start(bf16[1,2,1,144,512]{4,3,2,1,0:T(8,128)(2,1)S(1)} %get-tuple-element.107), channel_id=1, source_target_pairs={{16,0},{0,16},{17,1},{1,17},{18,2},{2,18},{19,3},{3,19},{20,4},{4,... | collective-permute-start | bytes 884744 | tf_op jit(solution)/shard_map/ppermute | solution.py:92
  27.5 3.7 %collective-permute-start.11 = (bf16[2,1,128,512]{3,2,1,0:T(8,128)(2,1)S(1)}, bf16[2,1,128,512]{3,2,1,0:T(8,128)(2,1)S(1)}, u32[]{:S(2)}, u32[]{:S(2)}) collective-permute-start(bf16[2,1,128,512]{3,2,1,0:T(8,128)(2,1)S(1)} %get-tuple-element.120.refs_4_), channel_id=1, source_target_pairs={{0,4},{4,0},{8,12},{12,8},{1,5},{5,1},{9,13},{13,9},{2,6},{6,2},{1... | collective-permute-start | bytes 786440 | tf_op jit(solution)/shard_map/ppermute | solution.py:85
  29.4 3.5 %collective-permute-start.12 = (bf16[2,1,128,512]{3,2,1,0:T(8,128)(2,1)S(1)}, bf16[2,1,128,512]{3,2,1,0:T(8,128)(2,1)S(1)}, u32[]{:S(2)}, u32[]{:S(2)}) collective-permute-start(bf16[2,1,128,512]{3,2,1,0:T(8,128)(2,1)S(1)} %collective-permute-done.10.refs_5_), channel_id=1, source_target_pairs={{0,4},{4,0},{8,12},{12,8},{1,5},{5,1},{9,13},{13,9},{2,6},{6,2},{1... | collective-permute-start | bytes 786440 | tf_op jit(solution)/shard_map/ppermute | solution.py:85
  29.4 5.9 %collective-permute-start.9 = (bf16[1,1,128,512]{3,2,1,0:T(8,128)(2,1)S(1)}, bf16[1,1,128,512]{3,2,1,0:T(8,128)(2,1)S(1)}, u32[]{:S(2)}, u32[]{:S(2)}) collective-permute-start(bf16[1,1,128,512]{3,2,1,0:T(8,128)(2,1)S(1)} %get-tuple-element.104), channel_id=1, source_target_pairs={{0,8},{4,12},{8,0},{12,4},{1,9},{5,13},{9,1},{13,5},{2,10},{6,14},... | collective-permute-start | bytes 393224 | tf_op jit(solution)/shard_map/ppermute | solution.py:81
  31.1 4.2 %collective-permute-start.13 = (bf16[1,1,128,512]{3,2,1,0:T(8,128)(2,1)S(1)}, bf16[1,1,128,512]{3,2,1,0:T(8,128)(2,1)S(1)}, u32[]{:S(2)}, u32[]{:S(2)}) collective-permute-start(bf16[1,1,128,512]{3,2,1,0:T(8,128)(2,1)S(1)} %get-tuple-element.134.refs_4_), channel_id=1, source_target_pairs={{0,4},{4,0},{8,12},{12,8},{1,5},{5,1},{9,13},{13,9},{2,6},{6,2},{1... | collective-permute-start | bytes 393224 | tf_op jit(solution)/shard_map/ppermute | solution.py:85
  31.4 9.1 %collective-permute-start.19 = (bf16[1,2,1,128,512]{4,3,2,1,0:T(8,128)(2,1)S(1)}, bf16[1,2,1,128,512]{4,3,2,1,0:T(8,128)(2,1)S(1)}, u32[]{:S(2)}, u32[]{:S(2)}) collective-permute-start(bf16[1,2,1,128,512]{4,3,2,1,0:T(8,128)(2,1)S(1)} %get-tuple-element.108), channel_id=1, source_target_pairs={{16,0},{0,16},{17,1},{1,17},{18,2},{2,18},{19,3},{3,19},{20,4},{4,... | collective-permute-start | bytes 786440 | tf_op jit(solution)/shard_map/ppermute | solution.py:92
  34.0 1.8 %collective-permute-start.16 = (bf16[1,1,128,512]{3,2,1,0:T(8,128)(2,1)S(1)}, bf16[1,1,128,512]{3,2,1,0:T(8,128)(2,1)S(1)}, u32[]{:S(2)}, u32[]{:S(2)}) collective-permute-start(bf16[1,1,128,512]{3,2,1,0:T(8,128)(2,1)S(1)} %get-tuple-element.138.refs_8_), channel_id=1, source_target_pairs={{0,4},{4,0},{8,12},{12,8},{1,5},{5,1},{9,13},{13,9},{2,6},{6,2},{1... | collective-permute-start | bytes 393224 | tf_op jit(solution)/shard_map/ppermute | solution.py:85
  34.1 9.4 %collective-permute-start.22 = (bf16[2,1,144,512]{3,2,1,0:T(8,128)(2,1)S(1)}, bf16[2,1,144,512]{3,2,1,0:T(8,128)(2,1)S(1)}, u32[]{:S(2)}, u32[]{:S(2)}) collective-permute-start(bf16[2,1,144,512]{3,2,1,0:T(8,128)(2,1)S(1)} %get-tuple-element.125), channel_id=1, source_target_pairs={{0,8},{4,12},{8,0},{12,4},{1,9},{5,13},{9,1},{13,5},{2,10},{6,14},... | collective-permute-start | bytes 884744 | tf_op jit(solution)/shard_map/ppermute | solution.py:81
  35.3 2.2 %collective-permute-start.17 = (bf16[1,1,128,512]{3,2,1,0:T(8,128)(2,1)S(1)}, bf16[1,1,128,512]{3,2,1,0:T(8,128)(2,1)S(1)}, u32[]{:S(2)}, u32[]{:S(2)}) collective-permute-start(bf16[1,1,128,512]{3,2,1,0:T(8,128)(2,1)S(1)} %get-tuple-element.139.refs_9_), channel_id=1, source_target_pairs={{0,4},{4,0},{8,12},{12,8},{1,5},{5,1},{9,13},{13,9},{2,6},{6,2},{1... | collective-permute-start | bytes 393224 | tf_op jit(solution)/shard_map/ppermute | solution.py:85
  35.3 2.2 %collective-permute-start.14 = (bf16[1,1,128,512]{3,2,1,0:T(8,128)(2,1)S(1)}, bf16[1,1,128,512]{3,2,1,0:T(8,128)(2,1)S(1)}, u32[]{:S(2)}, u32[]{:S(2)}) collective-permute-start(bf16[1,1,128,512]{3,2,1,0:T(8,128)(2,1)S(1)} %collective-permute-done.9.refs_5_), channel_id=1, source_target_pairs={{0,4},{4,0},{8,12},{12,8},{1,5},{5,1},{9,13},{13,9},{2,6},{6,2},{1... | collective-permute-start | bytes 393224 | tf_op jit(solution)/shard_map/ppermute | solution.py:85
  35.8 9.7 %collective-permute-start.23 = (bf16[1,2,1,128,512]{4,3,2,1,0:T(8,128)(2,1)S(1)}, bf16[1,2,1,128,512]{4,3,2,1,0:T(8,128)(2,1)S(1)}, u32[]{:S(2)}, u32[]{:S(2)}) collective-permute-start(bf16[1,2,1,128,512]{4,3,2,1,0:T(8,128)(2,1)S(1)} %get-tuple-element.109), channel_id=1, source_target_pairs={{16,0},{0,16},{17,1},{1,17},{18,2},{2,18},{19,3},{3,19},{20,4},{4,... | collective-permute-start | bytes 786440 | tf_op jit(solution)/shard_map/ppermute | solution.py:92
  40.7 1.4 %collective-permute-start.20 = (bf16[1,1,128,512]{3,2,1,0:T(8,128)(2,1)S(1)}, bf16[1,1,128,512]{3,2,1,0:T(8,128)(2,1)S(1)}, u32[]{:S(2)}, u32[]{:S(2)}) collective-permute-start(bf16[1,1,128,512]{3,2,1,0:T(8,128)(2,1)S(1)} %get-tuple-element.151.refs_4_), channel_id=1, source_target_pairs={{0,4},{4,0},{8,12},{12,8},{1,5},{5,1},{9,13},{13,9},{2,6},{6,2},{1... | collective-permute-start | bytes 393224 | tf_op jit(solution)/shard_map/ppermute | solution.py:85
  40.8 1.5 %collective-permute-start.21 = (bf16[1,1,128,512]{3,2,1,0:T(8,128)(2,1)S(1)}, bf16[1,1,128,512]{3,2,1,0:T(8,128)(2,1)S(1)}, u32[]{:S(2)}, u32[]{:S(2)}) collective-permute-start(bf16[1,1,128,512]{3,2,1,0:T(8,128)(2,1)S(1)} %get-tuple-element.152.refs_5_), channel_id=1, source_target_pairs={{0,4},{4,0},{8,12},{12,8},{1,5},{5,1},{9,13},{13,9},{2,6},{6,2},{1... | collective-permute-start | bytes 393224 | tf_op jit(solution)/shard_map/ppermute | solution.py:85
  41.3 9.1 %collective-permute-start.18 = (bf16[2,1,128,512]{3,2,1,0:T(8,128)(2,1)S(1)}, bf16[2,1,128,512]{3,2,1,0:T(8,128)(2,1)S(1)}, u32[]{:S(2)}, u32[]{:S(2)}) collective-permute-start(bf16[2,1,128,512]{3,2,1,0:T(8,128)(2,1)S(1)} %get-tuple-element.142), channel_id=1, source_target_pairs={{0,8},{4,12},{8,0},{12,4},{1,9},{5,13},{9,1},{13,5},{2,10},{6,14},... | collective-permute-start | bytes 786440 | tf_op jit(solution)/shard_map/ppermute | solution.py:81
  45.7 1.4 %collective-permute-start.24 = (bf16[1,1,128,512]{3,2,1,0:T(8,128)(2,1)S(1)}, bf16[1,1,128,512]{3,2,1,0:T(8,128)(2,1)S(1)}, u32[]{:S(2)}, u32[]{:S(2)}) collective-permute-start(bf16[1,1,128,512]{3,2,1,0:T(8,128)(2,1)S(1)} %get-tuple-element.166.refs_4_), channel_id=1, source_target_pairs={{0,4},{4,0},{8,12},{12,8},{1,5},{5,1},{9,13},{13,9},{2,6},{6,2},{1... | collective-permute-start | bytes 393224 | tf_op jit(solution)/shard_map/ppermute | solution.py:85
  45.8 1.5 %collective-permute-start.25 = (bf16[1,1,128,512]{3,2,1,0:T(8,128)(2,1)S(1)}, bf16[1,1,128,512]{3,2,1,0:T(8,128)(2,1)S(1)}, u32[]{:S(2)}, u32[]{:S(2)}) collective-permute-start(bf16[1,1,128,512]{3,2,1,0:T(8,128)(2,1)S(1)} %get-tuple-element.167.refs_5_), channel_id=1, source_target_pairs={{0,4},{4,0},{8,12},{12,8},{1,5},{5,1},{9,13},{13,9},{2,6},{6,2},{1... | collective-permute-start | bytes 393224 | tf_op jit(solution)/shard_map/ppermute | solution.py:85
  46.3 6.7 %collective-permute-start.27 = (bf16[1,1,128,512]{3,2,1,0:T(8,128)(2,1)S(1)}, bf16[1,1,128,512]{3,2,1,0:T(8,128)(2,1)S(1)}, u32[]{:S(2)}, u32[]{:S(2)}) collective-permute-start(bf16[1,1,128,512]{3,2,1,0:T(8,128)(2,1)S(1)} %get-tuple-element.156), channel_id=1, source_target_pairs={{0,8},{4,12},{8,0},{12,4},{1,9},{5,13},{9,1},{13,5},{2,10},{6,14},... | collective-permute-start | bytes 393224 | tf_op jit(solution)/shard_map/ppermute | solution.py:81
  47.8 7.4 %collective-permute-start.26 = (bf16[1,1,128,512]{3,2,1,0:T(8,128)(2,1)S(1)}, bf16[1,1,128,512]{3,2,1,0:T(8,128)(2,1)S(1)}, u32[]{:S(2)}, u32[]{:S(2)}) collective-permute-start(bf16[1,1,128,512]{3,2,1,0:T(8,128)(2,1)S(1)} %get-tuple-element.171), channel_id=1, source_target_pairs={{0,8},{4,12},{8,0},{12,4},{1,9},{5,13},{9,1},{13,5},{2,10},{6,14},... | collective-permute-start | bytes 393224 | tf_op jit(solution)/shard_map/ppermute | solution.py:81

commit v14 on v13

--- a/solution.py
+++ b/solution.py
@@ -253,7 +253,7 @@
             shape = (len(group),) + block[1:]
             return call(kernel, [shape] * owners, "add_partial", table, greater_in, *rows, *received)
 
-        def product(jobs, earlier, pad=0):
+        def product(jobs, earlier):
             arrays = []
             for job in jobs:
                 for x, _ in [*job[0], *job[1]]:
@@ -284,10 +284,10 @@
                         ).astype(BF16)
                         for i in range(owners):
                             for j, at in enumerate(spans):
-                                outs[i][k, b, :r, at] = full[i * r : (i + 1) * r, j * r : (j + 1) * r]
-
-            shapes = [(len(jobs), owned, r + pad if d else r, o) for d in range(owners)]
-            return call(kernel, shapes, "product", *after(arrays, *earlier))
+                                outs[i][k, b, :, at] = full[i * r : (i + 1) * r, j * r : (j + 1) * r]
+
+            shape = (len(jobs),) + block[1:]
+            return call(kernel, [shape] * owners, "product", *after(arrays, *earlier))
 
         def back_to_rows(outs):
             return [outs[0]] + [to_owner(outs[d], owners - d) for d in others]
@@ -303,7 +303,7 @@
                 sems, out = refs[-1], refs[-2]
                 copies = [
                     pltpu.make_async_copy(
-                        refs[where[id(x)]].at[k, :, pl.ds(0, r)],
+                        refs[where[id(x)]].at[k],
                         out.at[n, pl.ds(owner_at(d) * owned, owned)],
                         sems.at[i],
                     )
@@ -446,7 +446,7 @@
                         sigma, beside = sigmas[g]
                         beside = [at(x, (i,)) for x in beside]
                         jobs.append((inverse_at(n), in_order((sigma[0], (i,)), at(sigma[1:], (i,)), beside)))
-            last = product(jobs, last, STEP if step == "L0" else 0)
+            last = product(jobs, last)
             back = back_to_rows(last)
             if step == "L0":
                 for rows, beside in zip(lesser_rows, lesser_rows_beside):

time: 56 us -> 56.1 us (level)
  starting transfers between devices: 20.7 us -> 23 us
  waiting for transfers between devices: 22.5 us -> 20.3 us
    ppermute x6, waiting for transfers between devices: 3.53 us -> 0.77 us  [from_energy(): return lax.ppermute(x, 'en', [((i + t) % en, i) for i in range(en)])]
    ppermute x8, starting transfers between devices: 9.24 us -> 12 us  [to_owner(): return lax.ppermute(x, 'ph', pairs)]
    ppermute x8, waiting for transfers between devices: 14.5 us -> 16.1 us  [to_owner(): return lax.ppermute(x, 'ph', pairs)]
    ppermute x13, waiting for transfers between devices: 2.86 us -> 1.81 us  [to_lanes(): lax.ppermute(x, 'ph', [(p, p // lanes * lanes + (p % lanes + q) % lanes)...]
  transfers between devices with their start and end apart: 28 -> 28, of which waited for: 16 -> 15; matrix products, arithmetic and copies ran while one was open for 0% -> 0% of each run, Pallas kernels for 16% -> 16%
where the time goes in v14:
time: 56.1 us; the launch traced here: 55.9 us
  starting transfers between devices  23 us (41%)
  waiting for transfers between devices  20.3 us (36%)
  Pallas kernels  11.7 us (21%)
  between operations  0.88 us (2%)
    ppermute x8, waiting for transfers between devices, to_owner(): return lax.ppermute(x, 'ph', pairs)  16.1 us
    ppermute x8, starting transfers between devices, to_owner(): return lax.ppermute(x, 'ph', pairs)  12 us
    ppermute x6, starting transfers between devices, from_energy(): return lax.ppermute(x, 'en', [((i + t) % en, i) for i in range(en)])  7.61 us
    pallas_call x7, Pallas kernels, place(): pl.pallas_call(kernel, in_specs=[WHOLE] * len(arrays) + [far] * (result i...  4.95 us
    pallas_call x14, Pallas kernels, call(): pl.pallas_call(kernel, in_specs=[WHOLE] * len(args), out_specs=[WHOLE] *...  4.77 us
    pallas_call x1, Pallas kernels, from_hbm(): pl.pallas_call(kernel, in_specs=[far] * len(args), out_specs=[WHOLE] * le...  1.97 us
    ppermute x13, starting transfers between devices, to_lanes(): lax.ppermute(x, 'ph', [(p, p // lanes * lanes + (p % lanes + q) % lanes)...  1.94 us
    ppermute x13, waiting for transfers between devices, to_lanes(): lax.ppermute(x, 'ph', [(p, p // lanes * lanes + (p % lanes + q) % lanes)...  1.81 us
  transfers between devices with their start and end apart: 28, of which 15 were waited for; matrix products, arithmetic and copies ran while one was open for 0% of the time, Pallas kernels for 16%

profile of v14, /device:TPU:0, one launch (start us, length us, event | category | flops | bytes accessed | tf_op | source)
XLA Modules:
  0.0 55.9 jit_solution(16650345380107152388)
XLA Ops:
  0.7 2.0 %lead.1.refs_0_ = bf16[400,512]{1,0:T(8,128)(2,1)} custom-call(s32[2,3]{1,0:T(2,128)} %bitcast.2, f32[2,3]{1,0:T(2,128)} %bitcast.3, bf16[3,2,128,512]{3,2,1,0:T(8,128)(2,1)} %refs_1_), custom_call_target="tpu_custom_call" | custom-call | flops 1 | bytes 1 | tf_op jit(solution)/shard_map/lead/pallas_call | solution.py:146
  2.6 0.0 copy-start
  2.6 3.0 %collective-permute-start = (bf16[400,512]{1,0:T(8,128)(2,1)}, bf16[400,512]{1,0:T(8,128)(2,1)S(1)}, u32[]{:S(2)}, u32[]{:S(2)}) collective-permute-start(bf16[400,512]{1,0:T(8,128)(2,1)} %lead.1.refs_0_), channel_id=1, source_target_pairs={{0,8},{4,12},{8,0},{12,4},{1,9},{5,13},{9,1},{13,5},{2,10},{6,14},... | collective-permute-start | bytes 1228808 | tf_op jit(solution)/shard_map/ppermute | solution.py:81
  5.7 0.0 copy-start.3
  5.7 1.6 %collective-permute-start.5 = (bf16[3,1,128,512]{3,2,1,0:T(8,128)(2,1)S(1)}, bf16[3,1,128,512]{3,2,1,0:T(8,128)(2,1)S(1)}, u32[]{:S(2)}, u32[]{:S(2)}) collective-permute-start(bf16[3,1,128,512]{3,2,1,0:T(8,128)(2,1)S(1)} %cut.2), channel_id=1, source_target_pairs={{16,0},{0,16},{17,1},{1,17},{18,2},{2,18},{19,3},{3,19},{20,4},{4,... | collective-permute-start | bytes 1179656 | tf_op jit(solution)/shard_map/ppermute | solution.py:92
  7.3 0.1 cut.3
  7.4 0.1 collective-permute-start.1
  7.4 0.6 %collective-permute-start.6 = (bf16[3,1,128,512]{3,2,1,0:T(8,128)(2,1)S(1)}, bf16[3,1,128,512]{3,2,1,0:T(8,128)(2,1)S(1)}, u32[]{:S(2)}, u32[]{:S(2)}) collective-permute-start(bf16[3,1,128,512]{3,2,1,0:T(8,128)(2,1)S(1)} %get-tuple-element.106), channel_id=1, source_target_pairs={{0,8},{4,12},{8,0},{12,4},{1,9},{5,13},{9,1},{13,5},{2,10},{6,14},... | collective-permute-start | bytes 1179656 | tf_op jit(solution)/shard_map/ppermute | solution.py:81
  8.0 0.4 collective-permute-start.7
  8.4 7.7 %collective-permute-done.refs_1_ = bf16[400,512]{1,0:T(8,128)(2,1)S(1)} collective-permute-done((bf16[400,512]{1,0:T(8,128)(2,1)}, bf16[400,512]{1,0:T(8,128)(2,1)S(1)}, u32[]{:S(2)}, u32[]{:S(2)}) %collective-permute-start) | collective-permute-done | bytes 409632 | tf_op jit(solution)/shard_map/ppermute | solution.py:81
  16.2 0.1 collective-permute-start.3
  16.3 1.2 %collective-permute-done.3.refs_1_ = bf16[2,16,128]{2,1,0:T(8,128)(2,1)S(1)} collective-permute-done((bf16[2,16,128]{2,1,0:T(8,128)(2,1)S(1)}, bf16[2,16,128]{2,1,0:T(8,128)(2,1)S(1)}, u32[]{:S(2)}, u32[]{:S(2)}) %collective-permute-start.3) | collective-permute-done | bytes 8224 | tf_op jit(solution)/shard_map/ppermute | solution.py:85
  17.5 0.1 weights.1
  17.6 0.3 collective-permute-done.5.refs_3_
  17.8 0.4 mix.2
  18.2 1.9 %collective-permute-start.10 = (bf16[2,1,128,512]{3,2,1,0:T(8,128)(2,1)S(1)}, bf16[2,1,128,512]{3,2,1,0:T(8,128)(2,1)S(1)}, u32[]{:S(2)}, u32[]{:S(2)}) collective-permute-start(bf16[2,1,128,512]{3,2,1,0:T(8,128)(2,1)S(1)} %get-tuple-element.103), channel_id=1, source_target_pairs={{0,8},{4,12},{8,0},{12,4},{1,9},{5,13},{9,1},{13,5},{2,10},{6,14},... | collective-permute-start | bytes 786440 | tf_op jit(solution)/shard_map/ppermute | solution.py:81
  20.1 1.5 %collective-permute-start.4 = (f32[3,8,128]{2,1,0:T(8,128)S(1)}, f32[3,8,128]{2,1,0:T(8,128)S(1)}, u32[]{:S(2)}, u32[]{:S(2)}) collective-permute-start(f32[3,8,128]{2,1,0:T(8,128)S(1)} %get-tuple-element.111.refs_1_), channel_id=1, source_target_pairs={{0,16},{16,0},{1,17},{17,1},{2,18},{18,2},{3,19},{19,3},{4,20},{20... | collective-permute-start | bytes 36872 | tf_op jit(solution)/shard_map/ppermute | solution.py:370
  21.6 0.5 collective-permute-start.8
  22.1 1.7 %collective-permute-done.4.table_ref = f32[3,8,128]{2,1,0:T(8,128)S(1)} collective-permute-done((f32[3,8,128]{2,1,0:T(8,128)S(1)}, f32[3,8,128]{2,1,0:T(8,128)S(1)}, u32[]{:S(2)}, u32[]{:S(2)}) %collective-permute-start.4) | collective-permute-done | bytes 12320 | tf_op jit(solution)/shard_map/ppermute | solution.py:370
  23.8 0.0 collective-permute-start.2
  23.8 0.8 %collective-permute-done.6.refs_1_ = bf16[3,1,128,512]{3,2,1,0:T(8,128)(2,1)S(1)} collective-permute-done((bf16[3,1,128,512]{3,2,1,0:T(8,128)(2,1)S(1)}, bf16[3,1,128,512]{3,2,1,0:T(8,128)(2,1)S(1)}, u32[]{:S(2)}, u32[]{:S(2)}) %collective-permute-start.6) | collective-permute-done | bytes 393248 | tf_op jit(solution)/shard_map/ppermute | solution.py:81
  24.6 0.4 partial_sums.1
  25.0 2.1 %collective-permute-start.15 = (bf16[1,2,1,144,512]{4,3,2,1,0:T(8,128)(2,1)S(1)}, bf16[1,2,1,144,512]{4,3,2,1,0:T(8,128)(2,1)S(1)}, u32[]{:S(2)}, u32[]{:S(2)}) collective-permute-start(bf16[1,2,1,144,512]{4,3,2,1,0:T(8,128)(2,1)S(1)} %get-tuple-element.107), channel_id=1, source_target_pairs={{16,0},{0,16},{17,1},{1,17},{18,2},{2,18},{19,3},{3,19},{20,4},{4,... | collective-permute-start | bytes 884744 | tf_op jit(solution)/shard_map/ppermute | solution.py:92
  27.1 0.0 collective-permute-done.8.refs_4_
  27.1 0.0 collective-permute-done.7.refs_3_
  27.1 0.4 mix.3
  27.5 0.1 collective-permute-start.11
  27.5 1.9 %collective-permute-done.10.refs_5_ = bf16[2,1,128,512]{3,2,1,0:T(8,128)(2,1)S(1)} collective-permute-done((bf16[2,1,128,512]{3,2,1,0:T(8,128)(2,1)S(1)}, bf16[2,1,128,512]{3,2,1,0:T(8,128)(2,1)S(1)}, u32[]{:S(2)}, u32[]{:S(2)}) %collective-permute-start.10) | collective-permute-done | bytes 262176 | tf_op jit(solution)/shard_map/ppermute | solution.py:81
  29.4 1.7 %collective-permute-start.9 = (bf16[1,1,128,512]{3,2,1,0:T(8,128)(2,1)S(1)}, bf16[1,1,128,512]{3,2,1,0:T(8,128)(2,1)S(1)}, u32[]{:S(2)}, u32[]{:S(2)}) collective-permute-start(bf16[1,1,128,512]{3,2,1,0:T(8,128)(2,1)S(1)} %get-tuple-element.104), channel_id=1, source_target_pairs={{0,8},{4,12},{8,0},{12,4},{1,9},{5,13},{9,1},{13,5},{2,10},{6,14},... | collective-permute-start | bytes 393224 | tf_op jit(solution)/shard_map/ppermute | solution.py:81
  31.1 1.5 %collective-permute-start.19 = (bf16[1,2,1,128,512]{4,3,2,1,0:T(8,128)(2,1)S(1)}, bf16[1,2,1,128,512]{4,3,2,1,0:T(8,128)(2,1)S(1)}, u32[]{:S(2)}, u32[]{:S(2)}) collective-permute-start(bf16[1,2,1,128,512]{4,3,2,1,0:T(8,128)(2,1)S(1)} %get-tuple-element.108), channel_id=1, source_target_pairs={{16,0},{0,16},{17,1},{1,17},{18,2},{2,18},{19,3},{3,19},{20,4},{4,... | collective-permute-start | bytes 786440 | tf_op jit(solution)/shard_map/ppermute | solution.py:92
  32.6 0.9 %product.4 = (bf16[2,1,128,512]{3,2,1,0:T(8,128)(2,1)S(1)}, bf16[2,1,128,512]{3,2,1,0:T(8,128)(2,1)S(1)}) custom-call(bf16[3,1,128,512]{3,2,1,0:T(8,128)(2,1)S(1)} %get-tuple-element.162.refs_0_, bf16[3,1,128,512]{3,2,1,0:T(8,128)(2,1)S(1)} %get-tuple-element.163.refs_1_, bf16[3,1,128,512]{3,2,1,0:T(8,128)(2,1)S(1)} %collective-permute-done.1.refs_2_, ...), custom_call_target="tpu_custom_call" | custom-call | flops 1 | bytes 1 | tf_op jit(solution)/shard_map/product/pallas_call | solution.py:21
  33.5 0.1 collective-permute-done.15.refs_2_
  33.6 0.2 add_partial.3
  33.8 0.5 collective-permute-start.16
  34.4 0.1 collective-permute-start.17
  34.4 0.9 %collective-permute-done.9.refs_5_ = bf16[1,1,128,512]{3,2,1,0:T(8,128)(2,1)S(1)} collective-permute-done((bf16[1,1,128,512]{3,2,1,0:T(8,128)(2,1)S(1)}, bf16[1,1,128,512]{3,2,1,0:T(8,128)(2,1)S(1)}, u32[]{:S(2)}, u32[]{:S(2)}) %collective-permute-start.9) | collective-permute-done | bytes 131104 | tf_op jit(solution)/shard_map/ppermute | solution.py:81
  35.3 1.7 %collective-permute-start.22 = (bf16[2,1,128,512]{3,2,1,0:T(8,128)(2,1)S(1)}, bf16[2,1,128,512]{3,2,1,0:T(8,128)(2,1)S(1)}, u32[]{:S(2)}, u32[]{:S(2)}) collective-permute-start(bf16[2,1,128,512]{3,2,1,0:T(8,128)(2,1)S(1)} %get-tuple-element.125), channel_id=1, source_target_pairs={{0,8},{4,12},{8,0},{12,4},{1,9},{5,13},{9,1},{13,5},{2,10},{6,14},... | collective-permute-start | bytes 786440 | tf_op jit(solution)/shard_map/ppermute | solution.py:81
  37.1 1.5 %collective-permute-start.23 = (bf16[1,2,1,128,512]{4,3,2,1,0:T(8,128)(2,1)S(1)}, bf16[1,2,1,128,512]{4,3,2,1,0:T(8,128)(2,1)S(1)}, u32[]{:S(2)}, u32[]{:S(2)}) collective-permute-start(bf16[1,2,1,128,512]{4,3,2,1,0:T(8,128)(2,1)S(1)} %get-tuple-element.109), channel_id=1, source_target_pairs={{16,0},{0,16},{17,1},{1,17},{18,2},{2,18},{19,3},{3,19},{20,4},{4,... | collective-permute-start | bytes 786440 | tf_op jit(solution)/shard_map/ppermute | solution.py:92
  38.6 0.9 %product.5 = (bf16[2,1,128,512]{3,2,1,0:T(8,128)(2,1)S(1)}, bf16[2,1,128,512]{3,2,1,0:T(8,128)(2,1)S(1)}) custom-call(bf16[3,1,128,512]{3,2,1,0:T(8,128)(2,1)S(1)} %get-tuple-element.162.refs_0_, bf16[3,1,128,512]{3,2,1,0:T(8,128)(2,1)S(1)} %get-tuple-element.163.refs_1_, bf16[3,1,128,512]{3,2,1,0:T(8,128)(2,1)S(1)} %collective-permute-done.1.refs_2_, ...), custom_call_target="tpu_custom_call" | custom-call | flops 1 | bytes 1 | tf_op jit(solution)/shard_map/product/pallas_call | solution.py:21
  39.4 0.1 collective-permute-done.19.refs_2_
  39.6 0.2 add_partial.4
  39.8 0.1 collective-permute-start.20
  39.9 0.5 collective-permute-start.21
  40.4 0.4 collective-permute-start.18
  40.8 0.4 collective-permute-done.20.refs_6_
  41.2 0.2 collective-permute-done.21.refs_7_
  41.4 0.5 product.6
  41.9 2.5 %collective-permute-done.22.refs_1_ = bf16[2,1,128,512]{3,2,1,0:T(8,128)(2,1)S(1)} collective-permute-done((bf16[2,1,128,512]{3,2,1,0:T(8,128)(2,1)S(1)}, bf16[2,1,128,512]{3,2,1,0:T(8,128)(2,1)S(1)}, u32[]{:S(2)}, u32[]{:S(2)}) %collective-permute-start.22) | collective-permute-done | bytes 262176 | tf_op jit(solution)/shard_map/ppermute | solution.py:81
  44.4 0.8 %place.7.refs_1_ = bf16[3,2,128,512]{3,2,1,0:T(8,128)(2,1)} custom-call(bf16[2,1,128,512]{3,2,1,0:T(8,128)(2,1)S(1)} %get-tuple-element.157.refs_0_, bf16[2,1,128,512]{3,2,1,0:T(8,128)(2,1)S(1)} %collective-permute-done.22.refs_1_), custom_call_target="tpu_custom_call" | custom-call | flops 1 | bytes 1 | tf_op jit(solution)/shard_map/place/pallas_call | solution.py:318
  45.2 0.3 collective-permute-done.23.refs_2_
  45.5 0.2 add_partial.5
  45.7 0.1 collective-permute-start.24
  45.8 0.5 collective-permute-start.25
  46.3 1.5 %collective-permute-start.27 = (bf16[1,1,128,512]{3,2,1,0:T(8,128)(2,1)S(1)}, bf16[1,1,128,512]{3,2,1,0:T(8,128)(2,1)S(1)}, u32[]{:S(2)}, u32[]{:S(2)}) collective-permute-start(bf16[1,1,128,512]{3,2,1,0:T(8,128)(2,1)S(1)} %get-tuple-element.156), channel_id=1, source_target_pairs={{0,8},{4,12},{8,0},{12,4},{1,9},{5,13},{9,1},{13,5},{2,10},{6,14},... | collective-permute-start | bytes 393224 | tf_op jit(solution)/shard_map/ppermute | solution.py:81
  47.8 0.5 product.7
  48.3 1.1 %collective-permute-start.26 = (bf16[1,1,128,512]{3,2,1,0:T(8,128)(2,1)S(1)}, bf16[1,1,128,512]{3,2,1,0:T(8,128)(2,1)S(1)}, u32[]{:S(2)}, u32[]{:S(2)}) collective-permute-start(bf16[1,1,128,512]{3,2,1,0:T(8,128)(2,1)S(1)} %get-tuple-element.171), channel_id=1, source_target_pairs={{0,8},{4,12},{8,0},{12,4},{1,9},{5,13},{9,1},{13,5},{2,10},{6,14},... | collective-permute-start | bytes 393224 | tf_op jit(solution)/shard_map/ppermute | solution.py:81
  49.4 0.7 %place.8.refs_1_ = bf16[3,2,128,512]{3,2,1,0:T(8,128)(2,1)} custom-call(bf16[2,1,128,512]{3,2,1,0:T(8,128)(2,1)S(1)} %get-tuple-element.173.refs_0_, bf16[3,2,128,512]{3,2,1,0:T(8,128)(2,1)} %place.7.refs_1_), custom_call_target="tpu_custom_call", output_to_operand_aliasing={{}: (1, {})} | custom-call | flops 1 | bytes 1 | tf_op jit(solution)/shard_map/place/pallas_call | solution.py:318
  50.1 0.8 %place.9.refs_1_ = bf16[3,2,128,512]{3,2,1,0:T(8,128)(2,1)} custom-call(bf16[2,1,128,512]{3,2,1,0:T(8,128)(2,1)S(1)} %get-tuple-element.173.refs_0_, bf16[1,1,128,512]{3,2,1,0:T(8,128)(2,1)S(1)} %get-tuple-element.174.refs_1_, bf16[1,1,128,512]{3,2,1,0:T(8,128)(2,1)S(1)} %get-tuple-element.175.refs_2_), custom_call_target="tpu_custom_call" | custom-call | flops 1 | bytes 1 | tf_op jit(solution)/shard_map/place/pallas_call | solution.py:318
  50.9 0.7 %place.10 = bf16[3,2,128,512]{3,2,1,0:T(8,128)(2,1)} custom-call(bf16[2,1,128,512]{3,2,1,0:T(8,128)(2,1)S(1)} %collective-permute-done.18.refs_0_, bf16[3,2,128,512]{3,2,1,0:T(8,128)(2,1)} %place.8.refs_1_), custom_call_target="tpu_custom_call", output_to_operand_aliasing={{}: (1, {})} | custom-call | flops 1 | bytes 1 | tf_op jit(solution)/shard_map/place/pallas_call | solution.py:318
  51.6 0.7 %place.11.refs_1_ = bf16[3,2,128,512]{3,2,1,0:T(8,128)(2,1)} custom-call(bf16[2,1,128,512]{3,2,1,0:T(8,128)(2,1)S(1)} %collective-permute-done.18.refs_0_, bf16[3,2,128,512]{3,2,1,0:T(8,128)(2,1)} %place.9.refs_1_), custom_call_target="tpu_custom_call", output_to_operand_aliasing={{}: (1, {})} | custom-call | flops 1 | bytes 1 | tf_op jit(solution)/shard_map/place/pallas_call | solution.py:318
  52.3 0.6 collective-permute-done.27.refs_0_
  52.8 0.7 %place.12.refs_1_ = bf16[3,2,128,512]{3,2,1,0:T(8,128)(2,1)} custom-call(bf16[1,1,128,512]{3,2,1,0:T(8,128)(2,1)S(1)} %collective-permute-done.27.refs_0_, bf16[3,2,128,512]{3,2,1,0:T(8,128)(2,1)} %place.11.refs_1_), custom_call_target="tpu_custom_call", output_to_operand_aliasing={{}: (1, {})} | custom-call | flops 1 | bytes 1 | tf_op jit(solution)/shard_map/place/pallas_call | solution.py:318
  53.5 1.8 %collective-permute-done.26.refs_0_ = bf16[1,1,128,512]{3,2,1,0:T(8,128)(2,1)S(1)} collective-permute-done((bf16[1,1,128,512]{3,2,1,0:T(8,128)(2,1)S(1)}, bf16[1,1,128,512]{3,2,1,0:T(8,128)(2,1)S(1)}, u32[]{:S(2)}, u32[]{:S(2)}) %collective-permute-start.26) | collective-permute-done | bytes 131104 | tf_op jit(solution)/shard_map/ppermute | solution.py:81
  55.3 0.7 %place.13 = bf16[3,2,128,512]{3,2,1,0:T(8,128)(2,1)} custom-call(bf16[1,1,128,512]{3,2,1,0:T(8,128)(2,1)S(1)} %collective-permute-done.26.refs_0_, bf16[3,2,128,512]{3,2,1,0:T(8,128)(2,1)} %place.12.refs_1_), custom_call_target="tpu_custom_call", output_to_operand_aliasing={{}: (1, {})} | custom-call | flops 1 | bytes 1 | tf_op jit(solution)/shard_map/place/pallas_call | solution.py:318
  (22 shorter events, 0.1 us)
Async XLA Ops:
  0.6 5.0 %copy-start.1 = (bf16[3,2,128,512]{3,2,1,0:T(8,128)(2,1)S(1)}, bf16[3,2,128,512]{3,2,1,0:T(8,128)(2,1)}, u32[]{:S(2)}) copy-start(bf16[3,2,128,512]{3,2,1,0:T(8,128)(2,1)} %refs_2_.4) | copy-start | bytes 2359300
  0.6 6.6 %copy-start.2 = (bf16[3,2,128,512]{3,2,1,0:T(8,128)(2,1)S(1)}, bf16[3,2,128,512]{3,2,1,0:T(8,128)(2,1)}, u32[]{:S(2)}) copy-start(bf16[3,2,128,512]{3,2,1,0:T(8,128)(2,1)} %refs_1_) | copy-start | bytes 2359300
  2.6 4.7 %copy-start = (bf16[3,2,128,512]{3,2,1,0:T(8,128)(2,1)S(1)}, bf16[3,2,128,512]{3,2,1,0:T(8,128)(2,1)}, u32[]{:S(2)}) copy-start(bf16[3,2,128,512]{3,2,1,0:T(8,128)(2,1)} %refs_0_.9) | copy-start | bytes 2359300
  2.6 13.5 %collective-permute-start = (bf16[400,512]{1,0:T(8,128)(2,1)}, bf16[400,512]{1,0:T(8,128)(2,1)S(1)}, u32[]{:S(2)}, u32[]{:S(2)}) collective-permute-start(bf16[400,512]{1,0:T(8,128)(2,1)} %lead.1.refs_0_), channel_id=1, source_target_pairs={{0,8},{4,12},{8,0},{12,4},{1,9},{5,13},{9,1},{13,5},{2,10},{6,14},... | collective-permute-start | bytes 1228808 | tf_op jit(solution)/shard_map/ppermute | solution.py:81
  5.7 10.5 %copy-start.3 = (bf16[400,512]{1,0:T(8,128)(2,1)S(1)}, bf16[400,512]{1,0:T(8,128)(2,1)}, u32[]{:S(2)}) copy-start(bf16[400,512]{1,0:T(8,128)(2,1)} %lead.1.refs_0_) | copy-start | bytes 1228804
  5.7 12.1 %collective-permute-start.5 = (bf16[3,1,128,512]{3,2,1,0:T(8,128)(2,1)S(1)}, bf16[3,1,128,512]{3,2,1,0:T(8,128)(2,1)S(1)}, u32[]{:S(2)}, u32[]{:S(2)}) collective-permute-start(bf16[3,1,128,512]{3,2,1,0:T(8,128)(2,1)S(1)} %cut.2), channel_id=1, source_target_pairs={{16,0},{0,16},{17,1},{1,17},{18,2},{2,18},{19,3},{3,19},{20,4},{4,... | collective-permute-start | bytes 1179656 | tf_op jit(solution)/shard_map/ppermute | solution.py:92
  7.4 14.2 %collective-permute-start.1 = (bf16[3,1,128,512]{3,2,1,0:T(8,128)(2,1)S(1)}, bf16[3,1,128,512]{3,2,1,0:T(8,128)(2,1)S(1)}, u32[]{:S(2)}, u32[]{:S(2)}) collective-permute-start(bf16[3,1,128,512]{3,2,1,0:T(8,128)(2,1)S(1)} %get-tuple-element.162.refs_0_), channel_id=1, source_target_pairs={{0,4},{4,0},{8,12},{12,8},{1,5},{5,1},{9,13},{13,9},{2,6},{6,2},{1... | collective-permute-start | bytes 1179656 | tf_op jit(solution)/shard_map/ppermute | solution.py:85
  7.4 17.2 %collective-permute-start.6 = (bf16[3,1,128,512]{3,2,1,0:T(8,128)(2,1)S(1)}, bf16[3,1,128,512]{3,2,1,0:T(8,128)(2,1)S(1)}, u32[]{:S(2)}, u32[]{:S(2)}) collective-permute-start(bf16[3,1,128,512]{3,2,1,0:T(8,128)(2,1)S(1)} %get-tuple-element.106), channel_id=1, source_target_pairs={{0,8},{4,12},{8,0},{12,4},{1,9},{5,13},{9,1},{13,5},{2,10},{6,14},... | collective-permute-start | bytes 1179656 | tf_op jit(solution)/shard_map/ppermute | solution.py:81
  8.0 19.1 %collective-permute-start.7 = (bf16[2,1,144,512]{3,2,1,0:T(8,128)(2,1)S(1)}, bf16[2,1,144,512]{3,2,1,0:T(8,128)(2,1)S(1)}, u32[]{:S(2)}, u32[]{:S(2)}) collective-permute-start(bf16[2,1,144,512]{3,2,1,0:T(8,128)(2,1)S(1)} %get-tuple-element.112), channel_id=1, source_target_pairs={{16,0},{0,16},{17,1},{1,17},{18,2},{2,18},{19,3},{3,19},{20,4},{4,... | collective-permute-start | bytes 884744 | tf_op jit(solution)/shard_map/ppermute | solution.py:92
  16.2 1.2 %collective-permute-start.3 = (bf16[2,16,128]{2,1,0:T(8,128)(2,1)S(1)}, bf16[2,16,128]{2,1,0:T(8,128)(2,1)S(1)}, u32[]{:S(2)}, u32[]{:S(2)}) collective-permute-start(bf16[2,16,128]{2,1,0:T(8,128)(2,1)S(1)} %get-tuple-element.98.refs_0_), channel_id=1, source_target_pairs={{0,4},{4,0},{8,12},{12,8},{1,5},{5,1},{9,13},{13,9},{2,6},{6,2},{1... | collective-permute-start | bytes 24584 | tf_op jit(solution)/shard_map/ppermute | solution.py:85
  18.2 11.2 %collective-permute-start.10 = (bf16[2,1,128,512]{3,2,1,0:T(8,128)(2,1)S(1)}, bf16[2,1,128,512]{3,2,1,0:T(8,128)(2,1)S(1)}, u32[]{:S(2)}, u32[]{:S(2)}) collective-permute-start(bf16[2,1,128,512]{3,2,1,0:T(8,128)(2,1)S(1)} %get-tuple-element.103), channel_id=1, source_target_pairs={{0,8},{4,12},{8,0},{12,4},{1,9},{5,13},{9,1},{13,5},{2,10},{6,14},... | collective-permute-start | bytes 786440 | tf_op jit(solution)/shard_map/ppermute | solution.py:81
  20.1 3.7 %collective-permute-start.4 = (f32[3,8,128]{2,1,0:T(8,128)S(1)}, f32[3,8,128]{2,1,0:T(8,128)S(1)}, u32[]{:S(2)}, u32[]{:S(2)}) collective-permute-start(f32[3,8,128]{2,1,0:T(8,128)S(1)} %get-tuple-element.111.refs_1_), channel_id=1, source_target_pairs={{0,16},{16,0},{1,17},{17,1},{2,18},{18,2},{3,19},{19,3},{4,20},{20... | collective-permute-start | bytes 36872 | tf_op jit(solution)/shard_map/ppermute | solution.py:370
  21.6 5.5 %collective-permute-start.8 = (bf16[1,1,128,512]{3,2,1,0:T(8,128)(2,1)S(1)}, bf16[1,1,128,512]{3,2,1,0:T(8,128)(2,1)S(1)}, u32[]{:S(2)}, u32[]{:S(2)}) collective-permute-start(bf16[1,1,128,512]{3,2,1,0:T(8,128)(2,1)S(1)} %get-tuple-element.113), channel_id=1, source_target_pairs={{16,0},{0,16},{17,1},{1,17},{18,2},{2,18},{19,3},{3,19},{20,4},{4,... | collective-permute-start | bytes 393224 | tf_op jit(solution)/shard_map/ppermute | solution.py:92
  23.8 8.9 %collective-permute-start.2 = (bf16[3,1,128,512]{3,2,1,0:T(8,128)(2,1)S(1)}, bf16[3,1,128,512]{3,2,1,0:T(8,128)(2,1)S(1)}, u32[]{:S(2)}, u32[]{:S(2)}) collective-permute-start(bf16[3,1,128,512]{3,2,1,0:T(8,128)(2,1)S(1)} %get-tuple-element.163.refs_1_), channel_id=1, source_target_pairs={{0,4},{4,0},{8,12},{12,8},{1,5},{5,1},{9,13},{13,9},{2,6},{6,2},{1... | collective-permute-start | bytes 1179656 | tf_op jit(solution)/shard_map/ppermute | solution.py:85
  25.0 8.6 %collective-permute-start.15 = (bf16[1,2,1,144,512]{4,3,2,1,0:T(8,128)(2,1)S(1)}, bf16[1,2,1,144,512]{4,3,2,1,0:T(8,128)(2,1)S(1)}, u32[]{:S(2)}, u32[]{:S(2)}) collective-permute-start(bf16[1,2,1,144,512]{4,3,2,1,0:T(8,128)(2,1)S(1)} %get-tuple-element.107), channel_id=1, source_target_pairs={{16,0},{0,16},{17,1},{1,17},{18,2},{2,18},{19,3},{3,19},{20,4},{4,... | collective-permute-start | bytes 884744 | tf_op jit(solution)/shard_map/ppermute | solution.py:92
  27.5 3.7 %collective-permute-start.11 = (bf16[2,1,128,512]{3,2,1,0:T(8,128)(2,1)S(1)}, bf16[2,1,128,512]{3,2,1,0:T(8,128)(2,1)S(1)}, u32[]{:S(2)}, u32[]{:S(2)}) collective-permute-start(bf16[2,1,128,512]{3,2,1,0:T(8,128)(2,1)S(1)} %get-tuple-element.120.refs_4_), channel_id=1, source_target_pairs={{0,4},{4,0},{8,12},{12,8},{1,5},{5,1},{9,13},{13,9},{2,6},{6,2},{1... | collective-permute-start | bytes 786440 | tf_op jit(solution)/shard_map/ppermute | solution.py:85
  29.4 3.2 %collective-permute-start.12 = (bf16[2,1,128,512]{3,2,1,0:T(8,128)(2,1)S(1)}, bf16[2,1,128,512]{3,2,1,0:T(8,128)(2,1)S(1)}, u32[]{:S(2)}, u32[]{:S(2)}) collective-permute-start(bf16[2,1,128,512]{3,2,1,0:T(8,128)(2,1)S(1)} %collective-permute-done.10.refs_5_), channel_id=1, source_target_pairs={{0,4},{4,0},{8,12},{12,8},{1,5},{5,1},{9,13},{13,9},{2,6},{6,2},{1... | collective-permute-start | bytes 786440 | tf_op jit(solution)/shard_map/ppermute | solution.py:85
  29.4 5.9 %collective-permute-start.9 = (bf16[1,1,128,512]{3,2,1,0:T(8,128)(2,1)S(1)}, bf16[1,1,128,512]{3,2,1,0:T(8,128)(2,1)S(1)}, u32[]{:S(2)}, u32[]{:S(2)}) collective-permute-start(bf16[1,1,128,512]{3,2,1,0:T(8,128)(2,1)S(1)} %get-tuple-element.104), channel_id=1, source_target_pairs={{0,8},{4,12},{8,0},{12,4},{1,9},{5,13},{9,1},{13,5},{2,10},{6,14},... | collective-permute-start | bytes 393224 | tf_op jit(solution)/shard_map/ppermute | solution.py:81
  31.1 8.4 %collective-permute-start.19 = (bf16[1,2,1,128,512]{4,3,2,1,0:T(8,128)(2,1)S(1)}, bf16[1,2,1,128,512]{4,3,2,1,0:T(8,128)(2,1)S(1)}, u32[]{:S(2)}, u32[]{:S(2)}) collective-permute-start(bf16[1,2,1,128,512]{4,3,2,1,0:T(8,128)(2,1)S(1)} %get-tuple-element.108), channel_id=1, source_target_pairs={{16,0},{0,16},{17,1},{1,17},{18,2},{2,18},{19,3},{3,19},{20,4},{4,... | collective-permute-start | bytes 786440 | tf_op jit(solution)/shard_map/ppermute | solution.py:92
  32.6 2.7 %collective-permute-start.13 = (bf16[1,1,128,512]{3,2,1,0:T(8,128)(2,1)S(1)}, bf16[1,1,128,512]{3,2,1,0:T(8,128)(2,1)S(1)}, u32[]{:S(2)}, u32[]{:S(2)}) collective-permute-start(bf16[1,1,128,512]{3,2,1,0:T(8,128)(2,1)S(1)} %get-tuple-element.134.refs_4_), channel_id=1, source_target_pairs={{0,4},{4,0},{8,12},{12,8},{1,5},{5,1},{9,13},{13,9},{2,6},{6,2},{1... | collective-permute-start | bytes 393224 | tf_op jit(solution)/shard_map/ppermute | solution.py:85
  33.8 3.2 %collective-permute-start.16 = (bf16[1,1,128,512]{3,2,1,0:T(8,128)(2,1)S(1)}, bf16[1,1,128,512]{3,2,1,0:T(8,128)(2,1)S(1)}, u32[]{:S(2)}, u32[]{:S(2)}) collective-permute-start(bf16[1,1,128,512]{3,2,1,0:T(8,128)(2,1)S(1)} %get-tuple-element.138.refs_8_), channel_id=1, source_target_pairs={{0,4},{4,0},{8,12},{12,8},{1,5},{5,1},{9,13},{13,9},{2,6},{6,2},{1... | collective-permute-start | bytes 393224 | tf_op jit(solution)/shard_map/ppermute | solution.py:85
  34.4 4.2 %collective-permute-start.17 = (bf16[1,1,128,512]{3,2,1,0:T(8,128)(2,1)S(1)}, bf16[1,1,128,512]{3,2,1,0:T(8,128)(2,1)S(1)}, u32[]{:S(2)}, u32[]{:S(2)}) collective-permute-start(bf16[1,1,128,512]{3,2,1,0:T(8,128)(2,1)S(1)} %get-tuple-element.139.refs_9_), channel_id=1, source_target_pairs={{0,4},{4,0},{8,12},{12,8},{1,5},{5,1},{9,13},{13,9},{2,6},{6,2},{1... | collective-permute-start | bytes 393224 | tf_op jit(solution)/shard_map/ppermute | solution.py:85
  35.3 3.2 %collective-permute-start.14 = (bf16[1,1,128,512]{3,2,1,0:T(8,128)(2,1)S(1)}, bf16[1,1,128,512]{3,2,1,0:T(8,128)(2,1)S(1)}, u32[]{:S(2)}, u32[]{:S(2)}) collective-permute-start(bf16[1,1,128,512]{3,2,1,0:T(8,128)(2,1)S(1)} %collective-permute-done.9.refs_5_), channel_id=1, source_target_pairs={{0,4},{4,0},{8,12},{12,8},{1,5},{5,1},{9,13},{13,9},{2,6},{6,2},{1... | collective-permute-start | bytes 393224 | tf_op jit(solution)/shard_map/ppermute | solution.py:85
  35.3 9.1 %collective-permute-start.22 = (bf16[2,1,128,512]{3,2,1,0:T(8,128)(2,1)S(1)}, bf16[2,1,128,512]{3,2,1,0:T(8,128)(2,1)S(1)}, u32[]{:S(2)}, u32[]{:S(2)}) collective-permute-start(bf16[2,1,128,512]{3,2,1,0:T(8,128)(2,1)S(1)} %get-tuple-element.125), channel_id=1, source_target_pairs={{0,8},{4,12},{8,0},{12,4},{1,9},{5,13},{9,1},{13,5},{2,10},{6,14},... | collective-permute-start | bytes 786440 | tf_op jit(solution)/shard_map/ppermute | solution.py:81
  37.1 8.4 %collective-permute-start.23 = (bf16[1,2,1,128,512]{4,3,2,1,0:T(8,128)(2,1)S(1)}, bf16[1,2,1,128,512]{4,3,2,1,0:T(8,128)(2,1)S(1)}, u32[]{:S(2)}, u32[]{:S(2)}) collective-permute-start(bf16[1,2,1,128,512]{4,3,2,1,0:T(8,128)(2,1)S(1)} %get-tuple-element.109), channel_id=1, source_target_pairs={{16,0},{0,16},{17,1},{1,17},{18,2},{2,18},{19,3},{3,19},{20,4},{4,... | collective-permute-start | bytes 786440 | tf_op jit(solution)/shard_map/ppermute | solution.py:92
  39.8 1.4 %collective-permute-start.20 = (bf16[1,1,128,512]{3,2,1,0:T(8,128)(2,1)S(1)}, bf16[1,1,128,512]{3,2,1,0:T(8,128)(2,1)S(1)}, u32[]{:S(2)}, u32[]{:S(2)}) collective-permute-start(bf16[1,1,128,512]{3,2,1,0:T(8,128)(2,1)S(1)} %get-tuple-element.151.refs_4_), channel_id=1, source_target_pairs={{0,4},{4,0},{8,12},{12,8},{1,5},{5,1},{9,13},{13,9},{2,6},{6,2},{1... | collective-permute-start | bytes 393224 | tf_op jit(solution)/shard_map/ppermute | solution.py:85
  39.9 1.5 %collective-permute-start.21 = (bf16[1,1,128,512]{3,2,1,0:T(8,128)(2,1)S(1)}, bf16[1,1,128,512]{3,2,1,0:T(8,128)(2,1)S(1)}, u32[]{:S(2)}, u32[]{:S(2)}) collective-permute-start(bf16[1,1,128,512]{3,2,1,0:T(8,128)(2,1)S(1)} %get-tuple-element.152.refs_5_), channel_id=1, source_target_pairs={{0,4},{4,0},{8,12},{12,8},{1,5},{5,1},{9,13},{13,9},{2,6},{6,2},{1... | collective-permute-start | bytes 393224 | tf_op jit(solution)/shard_map/ppermute | solution.py:85
  40.4 10.5 %collective-permute-start.18 = (bf16[2,1,128,512]{3,2,1,0:T(8,128)(2,1)S(1)}, bf16[2,1,128,512]{3,2,1,0:T(8,128)(2,1)S(1)}, u32[]{:S(2)}, u32[]{:S(2)}) collective-permute-start(bf16[2,1,128,512]{3,2,1,0:T(8,128)(2,1)S(1)} %get-tuple-element.142), channel_id=1, source_target_pairs={{0,8},{4,12},{8,0},{12,4},{1,9},{5,13},{9,1},{13,5},{2,10},{6,14},... | collective-permute-start | bytes 786440 | tf_op jit(solution)/shard_map/ppermute | solution.py:81
  45.7 2.1 %collective-permute-start.24 = (bf16[1,1,128,512]{3,2,1,0:T(8,128)(2,1)S(1)}, bf16[1,1,128,512]{3,2,1,0:T(8,128)(2,1)S(1)}, u32[]{:S(2)}, u32[]{:S(2)}) collective-permute-start(bf16[1,1,128,512]{3,2,1,0:T(8,128)(2,1)S(1)} %get-tuple-element.166.refs_4_), channel_id=1, source_target_pairs={{0,4},{4,0},{8,12},{12,8},{1,5},{5,1},{9,13},{13,9},{2,6},{6,2},{1... | collective-permute-start | bytes 393224 | tf_op jit(solution)/shard_map/ppermute | solution.py:85
  45.8 2.0 %collective-permute-start.25 = (bf16[1,1,128,512]{3,2,1,0:T(8,128)(2,1)S(1)}, bf16[1,1,128,512]{3,2,1,0:T(8,128)(2,1)S(1)}, u32[]{:S(2)}, u32[]{:S(2)}) collective-permute-start(bf16[1,1,128,512]{3,2,1,0:T(8,128)(2,1)S(1)} %get-tuple-element.167.refs_5_), channel_id=1, source_target_pairs={{0,4},{4,0},{8,12},{12,8},{1,5},{5,1},{9,13},{13,9},{2,6},{6,2},{1... | collective-permute-start | bytes 393224 | tf_op jit(solution)/shard_map/ppermute | solution.py:85
  46.3 6.5 %collective-permute-start.27 = (bf16[1,1,128,512]{3,2,1,0:T(8,128)(2,1)S(1)}, bf16[1,1,128,512]{3,2,1,0:T(8,128)(2,1)S(1)}, u32[]{:S(2)}, u32[]{:S(2)}) collective-permute-start(bf16[1,1,128,512]{3,2,1,0:T(8,128)(2,1)S(1)} %get-tuple-element.156), channel_id=1, source_target_pairs={{0,8},{4,12},{8,0},{12,4},{1,9},{5,13},{9,1},{13,5},{2,10},{6,14},... | collective-permute-start | bytes 393224 | tf_op jit(solution)/shard_map/ppermute | solution.py:81
  48.3 6.9 %collective-permute-start.26 = (bf16[1,1,128,512]{3,2,1,0:T(8,128)(2,1)S(1)}, bf16[1,1,128,512]{3,2,1,0:T(8,128)(2,1)S(1)}, u32[]{:S(2)}, u32[]{:S(2)}) collective-permute-start(bf16[1,1,128,512]{3,2,1,0:T(8,128)(2,1)S(1)} %get-tuple-element.171), channel_id=1, source_target_pairs={{0,8},{4,12},{8,0},{12,4},{1,9},{5,13},{9,1},{13,5},{2,10},{6,14},... | collective-permute-start | bytes 393224 | tf_op jit(solution)/shard_map/ppermute | solution.py:81

commit v15 on v13

--- a/solution.py
+++ b/solution.py
@@ -284,9 +284,14 @@
                         ).astype(BF16)
                         for i in range(owners):
                             for j, at in enumerate(spans):
-                                outs[i][k, b, :r, at] = full[i * r : (i + 1) * r, j * r : (j + 1) * r]
-
-            shapes = [(len(jobs), owned, r + pad if d else r, o) for d in range(owners)]
+                                piece = full[i * r : (i + 1) * r, j * r : (j + 1) * r]
+                                if len(shapes[i]) == 2:
+                                    outs[i][pl.ds((k * owned + b) * r, r), at] = piece
+                                else:
+                                    outs[i][k, b, :, at] = piece
+
+            shape = (len(jobs),) + block[1:]
+            shapes = [(len(jobs) * owned * r + pad, o) if d and pad else shape for d in range(owners)]
             return call(kernel, shapes, "product", *after(arrays, *earlier))
 
         def back_to_rows(outs):
@@ -301,14 +306,13 @@
 
             def kernel(*refs):
                 sems, out = refs[-1], refs[-2]
-                copies = [
-                    pltpu.make_async_copy(
-                        refs[where[id(x)]].at[k, :, pl.ds(0, r)],
-                        out.at[n, pl.ds(owner_at(d) * owned, owned)],
-                        sems.at[i],
-                    )
-                    for i, (n, d, x, k, _) in enumerate(parts)
-                ]
+                copies = []
+                for n, d, x, k, _ in parts:
+                    ref = refs[where[id(x)]]
+                    for b in range(owned):
+                        one = ref.at[pl.ds((k * owned + b) * r, r)] if len(x.shape) == 2 else ref.at[k, b]
+                        to = out.at[n, owner_at(d) * owned + b]
+                        copies.append(pltpu.make_async_copy(one, to, sems.at[len(copies)]))
                 for copy in copies:
                     copy.start()
                 for copy in copies:
@@ -320,7 +324,7 @@
                 in_specs=[WHOLE] * len(arrays) + [far] * (result is not None),
                 out_specs=far,
                 out_shape=jax.ShapeDtypeStruct((e, nb, r, o), BF16),
-                scratch_shapes=[pltpu.SemaphoreType.DMA((len(parts),))],
+                scratch_shapes=[pltpu.SemaphoreType.DMA((len(parts) * owned,))],
                 input_output_aliases={} if result is None else {len(arrays): 0},
                 compiler_params=PARAMS,
                 cost_estimate=COST,

time: 56 us -> 56 us (level)
  no operation moved by 1% of the time
where the time goes in v15:
time: 56 us; the launch traced here: 55.9 us
  waiting for transfers between devices  22.6 us (40%)
  starting transfers between devices  20.7 us (37%)
  Pallas kernels  11.7 us (21%)
  between operations  0.89 us (2%)
    ppermute x8, waiting for transfers between devices, to_owner(): return lax.ppermute(x, 'ph', pairs)  14.1 us
    ppermute x8, starting transfers between devices, to_owner(): return lax.ppermute(x, 'ph', pairs)  9.24 us
    ppermute x6, starting transfers between devices, from_energy(): return lax.ppermute(x, 'en', [((i + t) % en, i) for i in range(en)])  7.83 us
    pallas_call x7, Pallas kernels, place(): pl.pallas_call(kernel, in_specs=[WHOLE] * len(arrays) + [far] * (result i...  4.95 us
    pallas_call x14, Pallas kernels, call(): pl.pallas_call(kernel, in_specs=[WHOLE] * len(args), out_specs=[WHOLE] *...  4.77 us
    ppermute x6, waiting for transfers between devices, from_energy(): return lax.ppermute(x, 'en', [((i + t) % en, i) for i in range(en)])  3.88 us
    ppermute x13, waiting for transfers between devices, to_lanes(): lax.ppermute(x, 'ph', [(p, p // lanes * lanes + (p % lanes + q) % lanes)...  2.86 us
    ppermute x13, starting transfers between devices, to_lanes(): lax.ppermute(x, 'ph', [(p, p // lanes * lanes + (p % lanes + q) % lanes)...  2.16 us
  transfers between devices with their start and end apart: 28, of which 16 were waited for; matrix products, arithmetic and copies ran while one was open for 0% of the time, Pallas kernels for 16%

profile of v15, /device:TPU:0, one launch (start us, length us, event | category | flops | bytes accessed | tf_op | source)
XLA Modules:
  0.0 55.9 jit_solution(9966737351132866059)
XLA Ops:
  0.7 2.0 %lead.1.refs_0_ = bf16[400,512]{1,0:T(8,128)(2,1)} custom-call(s32[2,3]{1,0:T(2,128)} %bitcast.2, f32[2,3]{1,0:T(2,128)} %bitcast.3, bf16[3,2,128,512]{3,2,1,0:T(8,128)(2,1)} %refs_1_), custom_call_target="tpu_custom_call" | custom-call | flops 1 | bytes 1 | tf_op jit(solution)/shard_map/lead/pallas_call | solution.py:146
  2.6 0.0 copy-start
  2.6 3.0 %collective-permute-start = (bf16[400,512]{1,0:T(8,128)(2,1)}, bf16[400,512]{1,0:T(8,128)(2,1)S(1)}, u32[]{:S(2)}, u32[]{:S(2)}) collective-permute-start(bf16[400,512]{1,0:T(8,128)(2,1)} %lead.1.refs_0_), channel_id=1, source_target_pairs={{0,8},{4,12},{8,0},{12,4},{1,9},{5,13},{9,1},{13,5},{2,10},{6,14},... | collective-permute-start | bytes 1228808 | tf_op jit(solution)/shard_map/ppermute | solution.py:81
  5.7 0.0 copy-start.3
  5.7 1.6 %collective-permute-start.5 = (bf16[3,1,128,512]{3,2,1,0:T(8,128)(2,1)S(1)}, bf16[3,1,128,512]{3,2,1,0:T(8,128)(2,1)S(1)}, u32[]{:S(2)}, u32[]{:S(2)}) collective-permute-start(bf16[3,1,128,512]{3,2,1,0:T(8,128)(2,1)S(1)} %cut.2), channel_id=1, source_target_pairs={{16,0},{0,16},{17,1},{1,17},{18,2},{2,18},{19,3},{3,19},{20,4},{4,... | collective-permute-start | bytes 1179656 | tf_op jit(solution)/shard_map/ppermute | solution.py:92
  7.3 0.1 cut.3
  7.4 0.1 collective-permute-start.1
  7.4 0.6 %collective-permute-start.6 = (bf16[3,1,128,512]{3,2,1,0:T(8,128)(2,1)S(1)}, bf16[3,1,128,512]{3,2,1,0:T(8,128)(2,1)S(1)}, u32[]{:S(2)}, u32[]{:S(2)}) collective-permute-start(bf16[3,1,128,512]{3,2,1,0:T(8,128)(2,1)S(1)} %get-tuple-element.106), channel_id=1, source_target_pairs={{0,8},{4,12},{8,0},{12,4},{1,9},{5,13},{9,1},{13,5},{2,10},{6,14},... | collective-permute-start | bytes 1179656 | tf_op jit(solution)/shard_map/ppermute | solution.py:81
  8.0 0.4 collective-permute-start.7
  8.4 7.7 %collective-permute-done.refs_1_ = bf16[400,512]{1,0:T(8,128)(2,1)S(1)} collective-permute-done((bf16[400,512]{1,0:T(8,128)(2,1)}, bf16[400,512]{1,0:T(8,128)(2,1)S(1)}, u32[]{:S(2)}, u32[]{:S(2)}) %collective-permute-start) | collective-permute-done | bytes 409632 | tf_op jit(solution)/shard_map/ppermute | solution.py:81
  16.2 0.1 collective-permute-start.3
  16.3 1.2 %collective-permute-done.3.refs_1_ = bf16[2,16,128]{2,1,0:T(8,128)(2,1)S(1)} collective-permute-done((bf16[2,16,128]{2,1,0:T(8,128)(2,1)S(1)}, bf16[2,16,128]{2,1,0:T(8,128)(2,1)S(1)}, u32[]{:S(2)}, u32[]{:S(2)}) %collective-permute-start.3) | collective-permute-done | bytes 8224 | tf_op jit(solution)/shard_map/ppermute | solution.py:85
  17.5 0.1 weights.1
  17.6 0.3 collective-permute-done.5.refs_3_
  17.8 0.4 mix.2
  18.2 1.9 %collective-permute-start.10 = (bf16[2,1,128,512]{3,2,1,0:T(8,128)(2,1)S(1)}, bf16[2,1,128,512]{3,2,1,0:T(8,128)(2,1)S(1)}, u32[]{:S(2)}, u32[]{:S(2)}) collective-permute-start(bf16[2,1,128,512]{3,2,1,0:T(8,128)(2,1)S(1)} %get-tuple-element.103), channel_id=1, source_target_pairs={{0,8},{4,12},{8,0},{12,4},{1,9},{5,13},{9,1},{13,5},{2,10},{6,14},... | collective-permute-start | bytes 786440 | tf_op jit(solution)/shard_map/ppermute | solution.py:81
  20.1 1.5 %collective-permute-start.4 = (f32[3,8,128]{2,1,0:T(8,128)S(1)}, f32[3,8,128]{2,1,0:T(8,128)S(1)}, u32[]{:S(2)}, u32[]{:S(2)}) collective-permute-start(f32[3,8,128]{2,1,0:T(8,128)S(1)} %get-tuple-element.111.refs_1_), channel_id=1, source_target_pairs={{0,16},{16,0},{1,17},{17,1},{2,18},{18,2},{3,19},{19,3},{4,20},{20... | collective-permute-start | bytes 36872 | tf_op jit(solution)/shard_map/ppermute | solution.py:374
  21.6 0.5 collective-permute-start.8
  22.1 1.7 %collective-permute-done.4.table_ref = f32[3,8,128]{2,1,0:T(8,128)S(1)} collective-permute-done((f32[3,8,128]{2,1,0:T(8,128)S(1)}, f32[3,8,128]{2,1,0:T(8,128)S(1)}, u32[]{:S(2)}, u32[]{:S(2)}) %collective-permute-start.4) | collective-permute-done | bytes 12320 | tf_op jit(solution)/shard_map/ppermute | solution.py:374
  23.8 0.0 collective-permute-start.2
  23.8 0.8 %collective-permute-done.6.refs_1_ = bf16[3,1,128,512]{3,2,1,0:T(8,128)(2,1)S(1)} collective-permute-done((bf16[3,1,128,512]{3,2,1,0:T(8,128)(2,1)S(1)}, bf16[3,1,128,512]{3,2,1,0:T(8,128)(2,1)S(1)}, u32[]{:S(2)}, u32[]{:S(2)}) %collective-permute-start.6) | collective-permute-done | bytes 393248 | tf_op jit(solution)/shard_map/ppermute | solution.py:81
  24.6 0.4 partial_sums.1
  25.0 2.1 %collective-permute-start.15 = (bf16[1,2,1,144,512]{4,3,2,1,0:T(8,128)(2,1)S(1)}, bf16[1,2,1,144,512]{4,3,2,1,0:T(8,128)(2,1)S(1)}, u32[]{:S(2)}, u32[]{:S(2)}) collective-permute-start(bf16[1,2,1,144,512]{4,3,2,1,0:T(8,128)(2,1)S(1)} %get-tuple-element.107), channel_id=1, source_target_pairs={{16,0},{0,16},{17,1},{1,17},{18,2},{2,18},{19,3},{3,19},{20,4},{4,... | collective-permute-start | bytes 884744 | tf_op jit(solution)/shard_map/ppermute | solution.py:92
  27.1 0.4 mix.3
  27.5 0.1 collective-permute-start.11
  27.5 1.9 %collective-permute-done.10.refs_5_ = bf16[2,1,128,512]{3,2,1,0:T(8,128)(2,1)S(1)} collective-permute-done((bf16[2,1,128,512]{3,2,1,0:T(8,128)(2,1)S(1)}, bf16[2,1,128,512]{3,2,1,0:T(8,128)(2,1)S(1)}, u32[]{:S(2)}, u32[]{:S(2)}) %collective-permute-start.10) | collective-permute-done | bytes 262176 | tf_op jit(solution)/shard_map/ppermute | solution.py:81
  29.4 0.0 collective-permute-start.12
  29.4 1.7 %collective-permute-start.9 = (bf16[1,1,128,512]{3,2,1,0:T(8,128)(2,1)S(1)}, bf16[1,1,128,512]{3,2,1,0:T(8,128)(2,1)S(1)}, u32[]{:S(2)}, u32[]{:S(2)}) collective-permute-start(bf16[1,1,128,512]{3,2,1,0:T(8,128)(2,1)S(1)} %get-tuple-element.104), channel_id=1, source_target_pairs={{0,8},{4,12},{8,0},{12,4},{1,9},{5,13},{9,1},{13,5},{2,10},{6,14},... | collective-permute-start | bytes 393224 | tf_op jit(solution)/shard_map/ppermute | solution.py:81
  31.1 0.2 collective-permute-start.13
  31.4 1.5 %collective-permute-start.19 = (bf16[1,2,1,128,512]{4,3,2,1,0:T(8,128)(2,1)S(1)}, bf16[1,2,1,128,512]{4,3,2,1,0:T(8,128)(2,1)S(1)}, u32[]{:S(2)}, u32[]{:S(2)}) collective-permute-start(bf16[1,2,1,128,512]{4,3,2,1,0:T(8,128)(2,1)S(1)} %get-tuple-element.108), channel_id=1, source_target_pairs={{16,0},{0,16},{17,1},{1,17},{18,2},{2,18},{19,3},{3,19},{20,4},{4,... | collective-permute-start | bytes 786440 | tf_op jit(solution)/shard_map/ppermute | solution.py:92
  32.9 0.9 %product.4 = (bf16[2,1,128,512]{3,2,1,0:T(8,128)(2,1)S(1)}, bf16[272,512]{1,0:T(8,128)(2,1)S(1)}) custom-call(bf16[3,1,128,512]{3,2,1,0:T(8,128)(2,1)S(1)} %get-tuple-element.162.refs_0_, bf16[3,1,128,512]{3,2,1,0:T(8,128)(2,1)S(1)} %get-tuple-element.163.refs_1_, bf16[3,1,128,512]{3,2,1,0:T(8,128)(2,1)S(1)} %collective-permute-done.1.refs_2_, ...), custom_call_target="tpu_custom_call" | custom-call | flops 1 | bytes 1 | tf_op jit(solution)/shard_map/product/pallas_call | solution.py:21
  33.8 0.2 add_partial.3
  34.0 0.1 collective-permute-start.16
  34.1 0.6 %collective-permute-start.22 = (bf16[272,512]{1,0:T(8,128)(2,1)S(1)}, bf16[272,512]{1,0:T(8,128)(2,1)S(1)}, u32[]{:S(2)}, u32[]{:S(2)}) collective-permute-start(bf16[272,512]{1,0:T(8,128)(2,1)S(1)} %get-tuple-element.125), channel_id=1, source_target_pairs={{0,8},{4,12},{8,0},{12,4},{1,9},{5,13},{9,1},{13,5},{2,10},{6,14},... | collective-permute-start | bytes 835592 | tf_op jit(solution)/shard_map/ppermute | solution.py:81
  34.7 0.6 %collective-permute-done.9.refs_5_ = bf16[1,1,128,512]{3,2,1,0:T(8,128)(2,1)S(1)} collective-permute-done((bf16[1,1,128,512]{3,2,1,0:T(8,128)(2,1)S(1)}, bf16[1,1,128,512]{3,2,1,0:T(8,128)(2,1)S(1)}, u32[]{:S(2)}, u32[]{:S(2)}) %collective-permute-start.9) | collective-permute-done | bytes 131104 | tf_op jit(solution)/shard_map/ppermute | solution.py:81
  35.3 0.5 collective-permute-start.14
  35.8 1.7 %collective-permute-start.23 = (bf16[1,2,1,128,512]{4,3,2,1,0:T(8,128)(2,1)S(1)}, bf16[1,2,1,128,512]{4,3,2,1,0:T(8,128)(2,1)S(1)}, u32[]{:S(2)}, u32[]{:S(2)}) collective-permute-start(bf16[1,2,1,128,512]{4,3,2,1,0:T(8,128)(2,1)S(1)} %get-tuple-element.109), channel_id=1, source_target_pairs={{16,0},{0,16},{17,1},{1,17},{18,2},{2,18},{19,3},{3,19},{20,4},{4,... | collective-permute-start | bytes 786440 | tf_op jit(solution)/shard_map/ppermute | solution.py:92
  37.5 0.9 %product.5 = (bf16[2,1,128,512]{3,2,1,0:T(8,128)(2,1)S(1)}, bf16[2,1,128,512]{3,2,1,0:T(8,128)(2,1)S(1)}) custom-call(bf16[3,1,128,512]{3,2,1,0:T(8,128)(2,1)S(1)} %get-tuple-element.162.refs_0_, bf16[3,1,128,512]{3,2,1,0:T(8,128)(2,1)S(1)} %get-tuple-element.163.refs_1_, bf16[3,1,128,512]{3,2,1,0:T(8,128)(2,1)S(1)} %collective-permute-done.1.refs_2_, ...), custom_call_target="tpu_custom_call" | custom-call | flops 1 | bytes 1 | tf_op jit(solution)/shard_map/product/pallas_call | solution.py:21
  38.4 2.1 %collective-permute-done.19.refs_2_ = bf16[1,2,1,128,512]{4,3,2,1,0:T(8,128)(2,1)S(1)} collective-permute-done((bf16[1,2,1,128,512]{4,3,2,1,0:T(8,128)(2,1)S(1)}, bf16[1,2,1,128,512]{4,3,2,1,0:T(8,128)(2,1)S(1)}, u32[]{:S(2)}, u32[]{:S(2)}) %collective-permute-start.19) | collective-permute-done | bytes 262176 | tf_op jit(solution)/shard_map/ppermute | solution.py:92
  40.5 0.2 add_partial.4
  40.7 0.1 collective-permute-start.20
  40.8 0.5 collective-permute-start.21
  41.3 0.8 %collective-permute-done.20.refs_6_ = bf16[1,1,128,512]{3,2,1,0:T(8,128)(2,1)S(1)} collective-permute-done((bf16[1,1,128,512]{3,2,1,0:T(8,128)(2,1)S(1)}, bf16[1,1,128,512]{3,2,1,0:T(8,128)(2,1)S(1)}, u32[]{:S(2)}, u32[]{:S(2)}) %collective-permute-start.20) | collective-permute-done | bytes 131104 | tf_op jit(solution)/shard_map/ppermute | solution.py:85
  42.1 0.2 collective-permute-done.21.refs_7_
  42.3 0.5 product.6
  42.9 0.3 collective-permute-done.22.refs_1_
  43.1 0.8 %place.7.refs_1_ = bf16[3,2,128,512]{3,2,1,0:T(8,128)(2,1)} custom-call(bf16[2,1,128,512]{3,2,1,0:T(8,128)(2,1)S(1)} %get-tuple-element.157.refs_0_, bf16[272,512]{1,0:T(8,128)(2,1)S(1)} %collective-permute-done.22.refs_1_), custom_call_target="tpu_custom_call" | custom-call | flops 1 | bytes 1 | tf_op jit(solution)/shard_map/place/pallas_call | solution.py:322
  44.0 1.5 %collective-permute-done.23.refs_2_ = bf16[1,2,1,128,512]{4,3,2,1,0:T(8,128)(2,1)S(1)} collective-permute-done((bf16[1,2,1,128,512]{4,3,2,1,0:T(8,128)(2,1)S(1)}, bf16[1,2,1,128,512]{4,3,2,1,0:T(8,128)(2,1)S(1)}, u32[]{:S(2)}, u32[]{:S(2)}) %collective-permute-start.23) | collective-permute-done | bytes 262176 | tf_op jit(solution)/shard_map/ppermute | solution.py:92
  45.5 0.2 add_partial.5
  45.7 0.1 collective-permute-start.24
  45.8 0.5 collective-permute-start.25
  46.3 0.4 collective-permute-start.27
  46.6 0.5 collective-permute-done.24.refs_6_
  47.1 0.2 collective-permute-done.25.refs_7_
  47.3 0.5 product.7
  47.8 1.1 %collective-permute-start.26 = (bf16[1,1,128,512]{3,2,1,0:T(8,128)(2,1)S(1)}, bf16[1,1,128,512]{3,2,1,0:T(8,128)(2,1)S(1)}, u32[]{:S(2)}, u32[]{:S(2)}) collective-permute-start(bf16[1,1,128,512]{3,2,1,0:T(8,128)(2,1)S(1)} %get-tuple-element.171), channel_id=1, source_target_pairs={{0,8},{4,12},{8,0},{12,4},{1,9},{5,13},{9,1},{13,5},{2,10},{6,14},... | collective-permute-start | bytes 393224 | tf_op jit(solution)/shard_map/ppermute | solution.py:81
  48.9 0.7 %place.8.refs_1_ = bf16[3,2,128,512]{3,2,1,0:T(8,128)(2,1)} custom-call(bf16[2,1,128,512]{3,2,1,0:T(8,128)(2,1)S(1)} %get-tuple-element.173.refs_0_, bf16[3,2,128,512]{3,2,1,0:T(8,128)(2,1)} %place.7.refs_1_), custom_call_target="tpu_custom_call", output_to_operand_aliasing={{}: (1, {})} | custom-call | flops 1 | bytes 1 | tf_op jit(solution)/shard_map/place/pallas_call | solution.py:322
  49.6 0.8 %place.9.refs_1_ = bf16[3,2,128,512]{3,2,1,0:T(8,128)(2,1)} custom-call(bf16[2,1,128,512]{3,2,1,0:T(8,128)(2,1)S(1)} %get-tuple-element.173.refs_0_, bf16[1,1,128,512]{3,2,1,0:T(8,128)(2,1)S(1)} %get-tuple-element.174.refs_1_, bf16[1,1,128,512]{3,2,1,0:T(8,128)(2,1)S(1)} %get-tuple-element.175.refs_2_), custom_call_target="tpu_custom_call" | custom-call | flops 1 | bytes 1 | tf_op jit(solution)/shard_map/place/pallas_call | solution.py:322
  50.4 0.7 %place.10 = bf16[3,2,128,512]{3,2,1,0:T(8,128)(2,1)} custom-call(bf16[2,1,128,512]{3,2,1,0:T(8,128)(2,1)S(1)} %collective-permute-done.18.refs_0_, bf16[3,2,128,512]{3,2,1,0:T(8,128)(2,1)} %place.8.refs_1_), custom_call_target="tpu_custom_call", output_to_operand_aliasing={{}: (1, {})} | custom-call | flops 1 | bytes 1 | tf_op jit(solution)/shard_map/place/pallas_call | solution.py:322
  51.1 0.7 %place.11.refs_1_ = bf16[3,2,128,512]{3,2,1,0:T(8,128)(2,1)} custom-call(bf16[2,1,128,512]{3,2,1,0:T(8,128)(2,1)S(1)} %collective-permute-done.18.refs_0_, bf16[3,2,128,512]{3,2,1,0:T(8,128)(2,1)} %place.9.refs_1_), custom_call_target="tpu_custom_call", output_to_operand_aliasing={{}: (1, {})} | custom-call | flops 1 | bytes 1 | tf_op jit(solution)/shard_map/place/pallas_call | solution.py:322
  51.8 1.2 %collective-permute-done.27.refs_0_ = bf16[1,1,128,512]{3,2,1,0:T(8,128)(2,1)S(1)} collective-permute-done((bf16[1,1,128,512]{3,2,1,0:T(8,128)(2,1)S(1)}, bf16[1,1,128,512]{3,2,1,0:T(8,128)(2,1)S(1)}, u32[]{:S(2)}, u32[]{:S(2)}) %collective-permute-start.27) | collective-permute-done | bytes 131104 | tf_op jit(solution)/shard_map/ppermute | solution.py:81
  53.0 0.7 %place.12.refs_1_ = bf16[3,2,128,512]{3,2,1,0:T(8,128)(2,1)} custom-call(bf16[1,1,128,512]{3,2,1,0:T(8,128)(2,1)S(1)} %collective-permute-done.27.refs_0_, bf16[3,2,128,512]{3,2,1,0:T(8,128)(2,1)} %place.11.refs_1_), custom_call_target="tpu_custom_call", output_to_operand_aliasing={{}: (1, {})} | custom-call | flops 1 | bytes 1 | tf_op jit(solution)/shard_map/place/pallas_call | solution.py:322
  53.7 1.6 %collective-permute-done.26.refs_0_ = bf16[1,1,128,512]{3,2,1,0:T(8,128)(2,1)S(1)} collective-permute-done((bf16[1,1,128,512]{3,2,1,0:T(8,128)(2,1)S(1)}, bf16[1,1,128,512]{3,2,1,0:T(8,128)(2,1)S(1)}, u32[]{:S(2)}, u32[]{:S(2)}) %collective-permute-start.26) | collective-permute-done | bytes 131104 | tf_op jit(solution)/shard_map/ppermute | solution.py:81
  55.2 0.7 %place.13 = bf16[3,2,128,512]{3,2,1,0:T(8,128)(2,1)} custom-call(bf16[1,1,128,512]{3,2,1,0:T(8,128)(2,1)S(1)} %collective-permute-done.26.refs_0_, bf16[3,2,128,512]{3,2,1,0:T(8,128)(2,1)} %place.12.refs_1_), custom_call_target="tpu_custom_call", output_to_operand_aliasing={{}: (1, {})} | custom-call | flops 1 | bytes 1 | tf_op jit(solution)/shard_map/place/pallas_call | solution.py:322
  (22 shorter events, 0.1 us)
Async XLA Ops:
  0.6 5.0 %copy-start.1 = (bf16[3,2,128,512]{3,2,1,0:T(8,128)(2,1)S(1)}, bf16[3,2,128,512]{3,2,1,0:T(8,128)(2,1)}, u32[]{:S(2)}) copy-start(bf16[3,2,128,512]{3,2,1,0:T(8,128)(2,1)} %refs_2_.4) | copy-start | bytes 2359300
  0.6 6.6 %copy-start.2 = (bf16[3,2,128,512]{3,2,1,0:T(8,128)(2,1)S(1)}, bf16[3,2,128,512]{3,2,1,0:T(8,128)(2,1)}, u32[]{:S(2)}) copy-start(bf16[3,2,128,512]{3,2,1,0:T(8,128)(2,1)} %refs_1_) | copy-start | bytes 2359300
  2.6 4.7 %copy-start = (bf16[3,2,128,512]{3,2,1,0:T(8,128)(2,1)S(1)}, bf16[3,2,128,512]{3,2,1,0:T(8,128)(2,1)}, u32[]{:S(2)}) copy-start(bf16[3,2,128,512]{3,2,1,0:T(8,128)(2,1)} %refs_0_.9) | copy-start | bytes 2359300
  2.6 13.5 %collective-permute-start = (bf16[400,512]{1,0:T(8,128)(2,1)}, bf16[400,512]{1,0:T(8,128)(2,1)S(1)}, u32[]{:S(2)}, u32[]{:S(2)}) collective-permute-start(bf16[400,512]{1,0:T(8,128)(2,1)} %lead.1.refs_0_), channel_id=1, source_target_pairs={{0,8},{4,12},{8,0},{12,4},{1,9},{5,13},{9,1},{13,5},{2,10},{6,14},... | collective-permute-start | bytes 1228808 | tf_op jit(solution)/shard_map/ppermute | solution.py:81
  5.7 10.5 %copy-start.3 = (bf16[400,512]{1,0:T(8,128)(2,1)S(1)}, bf16[400,512]{1,0:T(8,128)(2,1)}, u32[]{:S(2)}) copy-start(bf16[400,512]{1,0:T(8,128)(2,1)} %lead.1.refs_0_) | copy-start | bytes 1228804
  5.7 12.1 %collective-permute-start.5 = (bf16[3,1,128,512]{3,2,1,0:T(8,128)(2,1)S(1)}, bf16[3,1,128,512]{3,2,1,0:T(8,128)(2,1)S(1)}, u32[]{:S(2)}, u32[]{:S(2)}) collective-permute-start(bf16[3,1,128,512]{3,2,1,0:T(8,128)(2,1)S(1)} %cut.2), channel_id=1, source_target_pairs={{16,0},{0,16},{17,1},{1,17},{18,2},{2,18},{19,3},{3,19},{20,4},{4,... | collective-permute-start | bytes 1179656 | tf_op jit(solution)/shard_map/ppermute | solution.py:92
  7.4 14.2 %collective-permute-start.1 = (bf16[3,1,128,512]{3,2,1,0:T(8,128)(2,1)S(1)}, bf16[3,1,128,512]{3,2,1,0:T(8,128)(2,1)S(1)}, u32[]{:S(2)}, u32[]{:S(2)}) collective-permute-start(bf16[3,1,128,512]{3,2,1,0:T(8,128)(2,1)S(1)} %get-tuple-element.162.refs_0_), channel_id=1, source_target_pairs={{0,4},{4,0},{8,12},{12,8},{1,5},{5,1},{9,13},{13,9},{2,6},{6,2},{1... | collective-permute-start | bytes 1179656 | tf_op jit(solution)/shard_map/ppermute | solution.py:85
  7.4 17.2 %collective-permute-start.6 = (bf16[3,1,128,512]{3,2,1,0:T(8,128)(2,1)S(1)}, bf16[3,1,128,512]{3,2,1,0:T(8,128)(2,1)S(1)}, u32[]{:S(2)}, u32[]{:S(2)}) collective-permute-start(bf16[3,1,128,512]{3,2,1,0:T(8,128)(2,1)S(1)} %get-tuple-element.106), channel_id=1, source_target_pairs={{0,8},{4,12},{8,0},{12,4},{1,9},{5,13},{9,1},{13,5},{2,10},{6,14},... | collective-permute-start | bytes 1179656 | tf_op jit(solution)/shard_map/ppermute | solution.py:81
  8.0 19.1 %collective-permute-start.7 = (bf16[2,1,144,512]{3,2,1,0:T(8,128)(2,1)S(1)}, bf16[2,1,144,512]{3,2,1,0:T(8,128)(2,1)S(1)}, u32[]{:S(2)}, u32[]{:S(2)}) collective-permute-start(bf16[2,1,144,512]{3,2,1,0:T(8,128)(2,1)S(1)} %get-tuple-element.112), channel_id=1, source_target_pairs={{16,0},{0,16},{17,1},{1,17},{18,2},{2,18},{19,3},{3,19},{20,4},{4,... | collective-permute-start | bytes 884744 | tf_op jit(solution)/shard_map/ppermute | solution.py:92
  16.2 1.2 %collective-permute-start.3 = (bf16[2,16,128]{2,1,0:T(8,128)(2,1)S(1)}, bf16[2,16,128]{2,1,0:T(8,128)(2,1)S(1)}, u32[]{:S(2)}, u32[]{:S(2)}) collective-permute-start(bf16[2,16,128]{2,1,0:T(8,128)(2,1)S(1)} %get-tuple-element.98.refs_0_), channel_id=1, source_target_pairs={{0,4},{4,0},{8,12},{12,8},{1,5},{5,1},{9,13},{13,9},{2,6},{6,2},{1... | collective-permute-start | bytes 24584 | tf_op jit(solution)/shard_map/ppermute | solution.py:85
  18.2 11.2 %collective-permute-start.10 = (bf16[2,1,128,512]{3,2,1,0:T(8,128)(2,1)S(1)}, bf16[2,1,128,512]{3,2,1,0:T(8,128)(2,1)S(1)}, u32[]{:S(2)}, u32[]{:S(2)}) collective-permute-start(bf16[2,1,128,512]{3,2,1,0:T(8,128)(2,1)S(1)} %get-tuple-element.103), channel_id=1, source_target_pairs={{0,8},{4,12},{8,0},{12,4},{1,9},{5,13},{9,1},{13,5},{2,10},{6,14},... | collective-permute-start | bytes 786440 | tf_op jit(solution)/shard_map/ppermute | solution.py:81
  20.1 3.7 %collective-permute-start.4 = (f32[3,8,128]{2,1,0:T(8,128)S(1)}, f32[3,8,128]{2,1,0:T(8,128)S(1)}, u32[]{:S(2)}, u32[]{:S(2)}) collective-permute-start(f32[3,8,128]{2,1,0:T(8,128)S(1)} %get-tuple-element.111.refs_1_), channel_id=1, source_target_pairs={{0,16},{16,0},{1,17},{17,1},{2,18},{18,2},{3,19},{19,3},{4,20},{20... | collective-permute-start | bytes 36872 | tf_op jit(solution)/shard_map/ppermute | solution.py:374
  21.6 5.5 %collective-permute-start.8 = (bf16[1,1,128,512]{3,2,1,0:T(8,128)(2,1)S(1)}, bf16[1,1,128,512]{3,2,1,0:T(8,128)(2,1)S(1)}, u32[]{:S(2)}, u32[]{:S(2)}) collective-permute-start(bf16[1,1,128,512]{3,2,1,0:T(8,128)(2,1)S(1)} %get-tuple-element.113), channel_id=1, source_target_pairs={{16,0},{0,16},{17,1},{1,17},{18,2},{2,18},{19,3},{3,19},{20,4},{4,... | collective-permute-start | bytes 393224 | tf_op jit(solution)/shard_map/ppermute | solution.py:92
  23.8 7.6 %collective-permute-start.2 = (bf16[3,1,128,512]{3,2,1,0:T(8,128)(2,1)S(1)}, bf16[3,1,128,512]{3,2,1,0:T(8,128)(2,1)S(1)}, u32[]{:S(2)}, u32[]{:S(2)}) collective-permute-start(bf16[3,1,128,512]{3,2,1,0:T(8,128)(2,1)S(1)} %get-tuple-element.163.refs_1_), channel_id=1, source_target_pairs={{0,4},{4,0},{8,12},{12,8},{1,5},{5,1},{9,13},{13,9},{2,6},{6,2},{1... | collective-permute-start | bytes 1179656 | tf_op jit(solution)/shard_map/ppermute | solution.py:85
  25.0 8.8 %collective-permute-start.15 = (bf16[1,2,1,144,512]{4,3,2,1,0:T(8,128)(2,1)S(1)}, bf16[1,2,1,144,512]{4,3,2,1,0:T(8,128)(2,1)S(1)}, u32[]{:S(2)}, u32[]{:S(2)}) collective-permute-start(bf16[1,2,1,144,512]{4,3,2,1,0:T(8,128)(2,1)S(1)} %get-tuple-element.107), channel_id=1, source_target_pairs={{16,0},{0,16},{17,1},{1,17},{18,2},{2,18},{19,3},{3,19},{20,4},{4,... | collective-permute-start | bytes 884744 | tf_op jit(solution)/shard_map/ppermute | solution.py:92
  27.5 3.7 %collective-permute-start.11 = (bf16[2,1,128,512]{3,2,1,0:T(8,128)(2,1)S(1)}, bf16[2,1,128,512]{3,2,1,0:T(8,128)(2,1)S(1)}, u32[]{:S(2)}, u32[]{:S(2)}) collective-permute-start(bf16[2,1,128,512]{3,2,1,0:T(8,128)(2,1)S(1)} %get-tuple-element.120.refs_4_), channel_id=1, source_target_pairs={{0,4},{4,0},{8,12},{12,8},{1,5},{5,1},{9,13},{13,9},{2,6},{6,2},{1... | collective-permute-start | bytes 786440 | tf_op jit(solution)/shard_map/ppermute | solution.py:85
  29.4 3.5 %collective-permute-start.12 = (bf16[2,1,128,512]{3,2,1,0:T(8,128)(2,1)S(1)}, bf16[2,1,128,512]{3,2,1,0:T(8,128)(2,1)S(1)}, u32[]{:S(2)}, u32[]{:S(2)}) collective-permute-start(bf16[2,1,128,512]{3,2,1,0:T(8,128)(2,1)S(1)} %collective-permute-done.10.refs_5_), channel_id=1, source_target_pairs={{0,4},{4,0},{8,12},{12,8},{1,5},{5,1},{9,13},{13,9},{2,6},{6,2},{1... | collective-permute-start | bytes 786440 | tf_op jit(solution)/shard_map/ppermute | solution.py:85
  29.4 5.9 %collective-permute-start.9 = (bf16[1,1,128,512]{3,2,1,0:T(8,128)(2,1)S(1)}, bf16[1,1,128,512]{3,2,1,0:T(8,128)(2,1)S(1)}, u32[]{:S(2)}, u32[]{:S(2)}) collective-permute-start(bf16[1,1,128,512]{3,2,1,0:T(8,128)(2,1)S(1)} %get-tuple-element.104), channel_id=1, source_target_pairs={{0,8},{4,12},{8,0},{12,4},{1,9},{5,13},{9,1},{13,5},{2,10},{6,14},... | collective-permute-start | bytes 393224 | tf_op jit(solution)/shard_map/ppermute | solution.py:81
  31.1 4.2 %collective-permute-start.13 = (bf16[1,1,128,512]{3,2,1,0:T(8,128)(2,1)S(1)}, bf16[1,1,128,512]{3,2,1,0:T(8,128)(2,1)S(1)}, u32[]{:S(2)}, u32[]{:S(2)}) collective-permute-start(bf16[1,1,128,512]{3,2,1,0:T(8,128)(2,1)S(1)} %get-tuple-element.134.refs_4_), channel_id=1, source_target_pairs={{0,4},{4,0},{8,12},{12,8},{1,5},{5,1},{9,13},{13,9},{2,6},{6,2},{1... | collective-permute-start | bytes 393224 | tf_op jit(solution)/shard_map/ppermute | solution.py:85
  31.4 9.1 %collective-permute-start.19 = (bf16[1,2,1,128,512]{4,3,2,1,0:T(8,128)(2,1)S(1)}, bf16[1,2,1,128,512]{4,3,2,1,0:T(8,128)(2,1)S(1)}, u32[]{:S(2)}, u32[]{:S(2)}) collective-permute-start(bf16[1,2,1,128,512]{4,3,2,1,0:T(8,128)(2,1)S(1)} %get-tuple-element.108), channel_id=1, source_target_pairs={{16,0},{0,16},{17,1},{1,17},{18,2},{2,18},{19,3},{3,19},{20,4},{4,... | collective-permute-start | bytes 786440 | tf_op jit(solution)/shard_map/ppermute | solution.py:92
  34.0 1.8 %collective-permute-start.16 = (bf16[1,1,128,512]{3,2,1,0:T(8,128)(2,1)S(1)}, bf16[1,1,128,512]{3,2,1,0:T(8,128)(2,1)S(1)}, u32[]{:S(2)}, u32[]{:S(2)}) collective-permute-start(bf16[1,1,128,512]{3,2,1,0:T(8,128)(2,1)S(1)} %get-tuple-element.138.refs_8_), channel_id=1, source_target_pairs={{0,4},{4,0},{8,12},{12,8},{1,5},{5,1},{9,13},{13,9},{2,6},{6,2},{1... | collective-permute-start | bytes 393224 | tf_op jit(solution)/shard_map/ppermute | solution.py:85
  34.1 9.1 %collective-permute-start.22 = (bf16[272,512]{1,0:T(8,128)(2,1)S(1)}, bf16[272,512]{1,0:T(8,128)(2,1)S(1)}, u32[]{:S(2)}, u32[]{:S(2)}) collective-permute-start(bf16[272,512]{1,0:T(8,128)(2,1)S(1)} %get-tuple-element.125), channel_id=1, source_target_pairs={{0,8},{4,12},{8,0},{12,4},{1,9},{5,13},{9,1},{13,5},{2,10},{6,14},... | collective-permute-start | bytes 835592 | tf_op jit(solution)/shard_map/ppermute | solution.py:81
  35.3 2.2 %collective-permute-start.17 = (bf16[1,1,128,512]{3,2,1,0:T(8,128)(2,1)S(1)}, bf16[1,1,128,512]{3,2,1,0:T(8,128)(2,1)S(1)}, u32[]{:S(2)}, u32[]{:S(2)}) collective-permute-start(bf16[1,1,128,512]{3,2,1,0:T(8,128)(2,1)S(1)} %get-tuple-element.139.refs_9_), channel_id=1, source_target_pairs={{0,4},{4,0},{8,12},{12,8},{1,5},{5,1},{9,13},{13,9},{2,6},{6,2},{1... | collective-permute-start | bytes 393224 | tf_op jit(solution)/shard_map/ppermute | solution.py:85
  35.3 2.2 %collective-permute-start.14 = (bf16[1,1,128,512]{3,2,1,0:T(8,128)(2,1)S(1)}, bf16[1,1,128,512]{3,2,1,0:T(8,128)(2,1)S(1)}, u32[]{:S(2)}, u32[]{:S(2)}) collective-permute-start(bf16[1,1,128,512]{3,2,1,0:T(8,128)(2,1)S(1)} %collective-permute-done.9.refs_5_), channel_id=1, source_target_pairs={{0,4},{4,0},{8,12},{12,8},{1,5},{5,1},{9,13},{13,9},{2,6},{6,2},{1... | collective-permute-start | bytes 393224 | tf_op jit(solution)/shard_map/ppermute | solution.py:85
  35.8 9.7 %collective-permute-start.23 = (bf16[1,2,1,128,512]{4,3,2,1,0:T(8,128)(2,1)S(1)}, bf16[1,2,1,128,512]{4,3,2,1,0:T(8,128)(2,1)S(1)}, u32[]{:S(2)}, u32[]{:S(2)}) collective-permute-start(bf16[1,2,1,128,512]{4,3,2,1,0:T(8,128)(2,1)S(1)} %get-tuple-element.109), channel_id=1, source_target_pairs={{16,0},{0,16},{17,1},{1,17},{18,2},{2,18},{19,3},{3,19},{20,4},{4,... | collective-permute-start | bytes 786440 | tf_op jit(solution)/shard_map/ppermute | solution.py:92
  40.7 1.4 %collective-permute-start.20 = (bf16[1,1,128,512]{3,2,1,0:T(8,128)(2,1)S(1)}, bf16[1,1,128,512]{3,2,1,0:T(8,128)(2,1)S(1)}, u32[]{:S(2)}, u32[]{:S(2)}) collective-permute-start(bf16[1,1,128,512]{3,2,1,0:T(8,128)(2,1)S(1)} %get-tuple-element.151.refs_4_), channel_id=1, source_target_pairs={{0,4},{4,0},{8,12},{12,8},{1,5},{5,1},{9,13},{13,9},{2,6},{6,2},{1... | collective-permute-start | bytes 393224 | tf_op jit(solution)/shard_map/ppermute | solution.py:85
  40.8 1.5 %collective-permute-start.21 = (bf16[1,1,128,512]{3,2,1,0:T(8,128)(2,1)S(1)}, bf16[1,1,128,512]{3,2,1,0:T(8,128)(2,1)S(1)}, u32[]{:S(2)}, u32[]{:S(2)}) collective-permute-start(bf16[1,1,128,512]{3,2,1,0:T(8,128)(2,1)S(1)} %get-tuple-element.152.refs_5_), channel_id=1, source_target_pairs={{0,4},{4,0},{8,12},{12,8},{1,5},{5,1},{9,13},{13,9},{2,6},{6,2},{1... | collective-permute-start | bytes 393224 | tf_op jit(solution)/shard_map/ppermute | solution.py:85
  41.3 9.1 %collective-permute-start.18 = (bf16[2,1,128,512]{3,2,1,0:T(8,128)(2,1)S(1)}, bf16[2,1,128,512]{3,2,1,0:T(8,128)(2,1)S(1)}, u32[]{:S(2)}, u32[]{:S(2)}) collective-permute-start(bf16[2,1,128,512]{3,2,1,0:T(8,128)(2,1)S(1)} %get-tuple-element.142), channel_id=1, source_target_pairs={{0,8},{4,12},{8,0},{12,4},{1,9},{5,13},{9,1},{13,5},{2,10},{6,14},... | collective-permute-start | bytes 786440 | tf_op jit(solution)/shard_map/ppermute | solution.py:81
  45.7 1.4 %collective-permute-start.24 = (bf16[1,1,128,512]{3,2,1,0:T(8,128)(2,1)S(1)}, bf16[1,1,128,512]{3,2,1,0:T(8,128)(2,1)S(1)}, u32[]{:S(2)}, u32[]{:S(2)}) collective-permute-start(bf16[1,1,128,512]{3,2,1,0:T(8,128)(2,1)S(1)} %get-tuple-element.166.refs_4_), channel_id=1, source_target_pairs={{0,4},{4,0},{8,12},{12,8},{1,5},{5,1},{9,13},{13,9},{2,6},{6,2},{1... | collective-permute-start | bytes 393224 | tf_op jit(solution)/shard_map/ppermute | solution.py:85
  45.8 1.5 %collective-permute-start.25 = (bf16[1,1,128,512]{3,2,1,0:T(8,128)(2,1)S(1)}, bf16[1,1,128,512]{3,2,1,0:T(8,128)(2,1)S(1)}, u32[]{:S(2)}, u32[]{:S(2)}) collective-permute-start(bf16[1,1,128,512]{3,2,1,0:T(8,128)(2,1)S(1)} %get-tuple-element.167.refs_5_), channel_id=1, source_target_pairs={{0,4},{4,0},{8,12},{12,8},{1,5},{5,1},{9,13},{13,9},{2,6},{6,2},{1... | collective-permute-start | bytes 393224 | tf_op jit(solution)/shard_map/ppermute | solution.py:85
  46.3 6.7 %collective-permute-start.27 = (bf16[1,1,128,512]{3,2,1,0:T(8,128)(2,1)S(1)}, bf16[1,1,128,512]{3,2,1,0:T(8,128)(2,1)S(1)}, u32[]{:S(2)}, u32[]{:S(2)}) collective-permute-start(bf16[1,1,128,512]{3,2,1,0:T(8,128)(2,1)S(1)} %get-tuple-element.156), channel_id=1, source_target_pairs={{0,8},{4,12},{8,0},{12,4},{1,9},{5,13},{9,1},{13,5},{2,10},{6,14},... | collective-permute-start | bytes 393224 | tf_op jit(solution)/shard_map/ppermute | solution.py:81
  47.8 7.4 %collective-permute-start.26 = (bf16[1,1,128,512]{3,2,1,0:T(8,128)(2,1)S(1)}, bf16[1,1,128,512]{3,2,1,0:T(8,128)(2,1)S(1)}, u32[]{:S(2)}, u32[]{:S(2)}) collective-permute-start(bf16[1,1,128,512]{3,2,1,0:T(8,128)(2,1)S(1)} %get-tuple-element.171), channel_id=1, source_target_pairs={{0,8},{4,12},{8,0},{12,4},{1,9},{5,13},{9,1},{13,5},{2,10},{6,14},... | collective-permute-start | bytes 393224 | tf_op jit(solution)/shard_map/ppermute | solution.py:81

commit v16 on v15

--- a/solution.py
+++ b/solution.py
@@ -101,7 +101,7 @@
                         to = leads[i].at[pl.ds((n * owned + b) * r, r)]
                         copies.append((inverse_ref.at[n, owner_at(d) * owned + b], to))
             copies = [pltpu.make_async_copy(x, y, sems.at[i]) for i, (x, y) in enumerate(copies)]
-            for copy in copies:
+            for copy in copies[2:] + copies[:2]:
                 copy.start()
             for copy in copies[:2]:
                 copy.wait()

time: 56 us -> 56 us (level)
  no operation moved by 1% of the time
where the time goes in v16:
time: 56 us; the launch traced here: 55.9 us
  waiting for transfers between devices  22.6 us (40%)
  starting transfers between devices  20.7 us (37%)
  Pallas kernels  11.7 us (21%)
  between operations  0.89 us (2%)
    ppermute x8, waiting for transfers between devices, to_owner(): return lax.ppermute(x, 'ph', pairs)  14.2 us
    ppermute x8, starting transfers between devices, to_owner(): return lax.ppermute(x, 'ph', pairs)  9.22 us
    ppermute x6, starting transfers between devices, from_energy(): return lax.ppermute(x, 'en', [((i + t) % en, i) for i in range(en)])  7.83 us
    pallas_call x7, Pallas kernels, place(): pl.pallas_call(kernel, in_specs=[WHOLE] * len(arrays) + [far] * (result i...  4.95 us
    pallas_call x14, Pallas kernels, call(): pl.pallas_call(kernel, in_specs=[WHOLE] * len(args), out_specs=[WHOLE] *...  4.78 us
    ppermute x6, waiting for transfers between devices, from_energy(): return lax.ppermute(x, 'en', [((i + t) % en, i) for i in range(en)])  3.87 us
    ppermute x13, waiting for transfers between devices, to_lanes(): lax.ppermute(x, 'ph', [(p, p // lanes * lanes + (p % lanes + q) % lanes)...  2.86 us
    ppermute x13, starting transfers between devices, to_lanes(): lax.ppermute(x, 'ph', [(p, p // lanes * lanes + (p % lanes + q) % lanes)...  2.16 us
  transfers between devices with their start and end apart: 28, of which 16 were waited for; matrix products, arithmetic and copies ran while one was open for 0% of the time, Pallas kernels for 16%

profile of v16, /device:TPU:0, one launch (start us, length us, event | category | flops | bytes accessed | tf_op | source)
XLA Modules:
  0.0 55.9 jit_solution(4243236985422215082)
XLA Ops:
  0.7 2.0 %lead.1.refs_0_ = bf16[400,512]{1,0:T(8,128)(2,1)} custom-call(s32[2,3]{1,0:T(2,128)} %bitcast.2, f32[2,3]{1,0:T(2,128)} %bitcast.3, bf16[3,2,128,512]{3,2,1,0:T(8,128)(2,1)} %refs_1_), custom_call_target="tpu_custom_call" | custom-call | flops 1 | bytes 1 | tf_op jit(solution)/shard_map/lead/pallas_call | solution.py:146
  2.6 0.0 copy-start
  2.6 3.0 %collective-permute-start = (bf16[400,512]{1,0:T(8,128)(2,1)}, bf16[400,512]{1,0:T(8,128)(2,1)S(1)}, u32[]{:S(2)}, u32[]{:S(2)}) collective-permute-start(bf16[400,512]{1,0:T(8,128)(2,1)} %lead.1.refs_0_), channel_id=1, source_target_pairs={{0,8},{4,12},{8,0},{12,4},{1,9},{5,13},{9,1},{13,5},{2,10},{6,14},... | collective-permute-start | bytes 1228808 | tf_op jit(solution)/shard_map/ppermute | solution.py:81
  5.7 0.0 copy-start.3
  5.7 1.6 %collective-permute-start.5 = (bf16[3,1,128,512]{3,2,1,0:T(8,128)(2,1)S(1)}, bf16[3,1,128,512]{3,2,1,0:T(8,128)(2,1)S(1)}, u32[]{:S(2)}, u32[]{:S(2)}) collective-permute-start(bf16[3,1,128,512]{3,2,1,0:T(8,128)(2,1)S(1)} %cut.2), channel_id=1, source_target_pairs={{16,0},{0,16},{17,1},{1,17},{18,2},{2,18},{19,3},{3,19},{20,4},{4,... | collective-permute-start | bytes 1179656 | tf_op jit(solution)/shard_map/ppermute | solution.py:92
  7.3 0.1 cut.3
  7.3 0.1 collective-permute-start.1
  7.4 0.6 %collective-permute-start.6 = (bf16[3,1,128,512]{3,2,1,0:T(8,128)(2,1)S(1)}, bf16[3,1,128,512]{3,2,1,0:T(8,128)(2,1)S(1)}, u32[]{:S(2)}, u32[]{:S(2)}) collective-permute-start(bf16[3,1,128,512]{3,2,1,0:T(8,128)(2,1)S(1)} %get-tuple-element.106), channel_id=1, source_target_pairs={{0,8},{4,12},{8,0},{12,4},{1,9},{5,13},{9,1},{13,5},{2,10},{6,14},... | collective-permute-start | bytes 1179656 | tf_op jit(solution)/shard_map/ppermute | solution.py:81
  8.0 0.4 collective-permute-start.7
  8.4 7.7 %collective-permute-done.refs_1_ = bf16[400,512]{1,0:T(8,128)(2,1)S(1)} collective-permute-done((bf16[400,512]{1,0:T(8,128)(2,1)}, bf16[400,512]{1,0:T(8,128)(2,1)S(1)}, u32[]{:S(2)}, u32[]{:S(2)}) %collective-permute-start) | collective-permute-done | bytes 409632 | tf_op jit(solution)/shard_map/ppermute | solution.py:81
  16.2 0.1 collective-permute-start.3
  16.3 1.2 %collective-permute-done.3.refs_1_ = bf16[2,16,128]{2,1,0:T(8,128)(2,1)S(1)} collective-permute-done((bf16[2,16,128]{2,1,0:T(8,128)(2,1)S(1)}, bf16[2,16,128]{2,1,0:T(8,128)(2,1)S(1)}, u32[]{:S(2)}, u32[]{:S(2)}) %collective-permute-start.3) | collective-permute-done | bytes 8224 | tf_op jit(solution)/shard_map/ppermute | solution.py:85
  17.4 0.1 weights.1
  17.5 0.3 collective-permute-done.5.refs_3_
  17.8 0.4 mix.2
  18.2 1.9 %collective-permute-start.10 = (bf16[2,1,128,512]{3,2,1,0:T(8,128)(2,1)S(1)}, bf16[2,1,128,512]{3,2,1,0:T(8,128)(2,1)S(1)}, u32[]{:S(2)}, u32[]{:S(2)}) collective-permute-start(bf16[2,1,128,512]{3,2,1,0:T(8,128)(2,1)S(1)} %get-tuple-element.103), channel_id=1, source_target_pairs={{0,8},{4,12},{8,0},{12,4},{1,9},{5,13},{9,1},{13,5},{2,10},{6,14},... | collective-permute-start | bytes 786440 | tf_op jit(solution)/shard_map/ppermute | solution.py:81
  20.0 1.5 %collective-permute-start.4 = (f32[3,8,128]{2,1,0:T(8,128)S(1)}, f32[3,8,128]{2,1,0:T(8,128)S(1)}, u32[]{:S(2)}, u32[]{:S(2)}) collective-permute-start(f32[3,8,128]{2,1,0:T(8,128)S(1)} %get-tuple-element.111.refs_1_), channel_id=1, source_target_pairs={{0,16},{16,0},{1,17},{17,1},{2,18},{18,2},{3,19},{19,3},{4,20},{20... | collective-permute-start | bytes 36872 | tf_op jit(solution)/shard_map/ppermute | solution.py:374
  21.5 0.5 collective-permute-start.8
  22.1 1.7 %collective-permute-done.4.table_ref = f32[3,8,128]{2,1,0:T(8,128)S(1)} collective-permute-done((f32[3,8,128]{2,1,0:T(8,128)S(1)}, f32[3,8,128]{2,1,0:T(8,128)S(1)}, u32[]{:S(2)}, u32[]{:S(2)}) %collective-permute-start.4) | collective-permute-done | bytes 12320 | tf_op jit(solution)/shard_map/ppermute | solution.py:374
  23.7 0.0 collective-permute-start.2
  23.7 0.8 %collective-permute-done.6.refs_1_ = bf16[3,1,128,512]{3,2,1,0:T(8,128)(2,1)S(1)} collective-permute-done((bf16[3,1,128,512]{3,2,1,0:T(8,128)(2,1)S(1)}, bf16[3,1,128,512]{3,2,1,0:T(8,128)(2,1)S(1)}, u32[]{:S(2)}, u32[]{:S(2)}) %collective-permute-start.6) | collective-permute-done | bytes 393248 | tf_op jit(solution)/shard_map/ppermute | solution.py:81
  24.6 0.4 partial_sums.1
  25.0 2.1 %collective-permute-start.15 = (bf16[1,2,1,144,512]{4,3,2,1,0:T(8,128)(2,1)S(1)}, bf16[1,2,1,144,512]{4,3,2,1,0:T(8,128)(2,1)S(1)}, u32[]{:S(2)}, u32[]{:S(2)}) collective-permute-start(bf16[1,2,1,144,512]{4,3,2,1,0:T(8,128)(2,1)S(1)} %get-tuple-element.107), channel_id=1, source_target_pairs={{16,0},{0,16},{17,1},{1,17},{18,2},{2,18},{19,3},{3,19},{20,4},{4,... | collective-permute-start | bytes 884744 | tf_op jit(solution)/shard_map/ppermute | solution.py:92
  27.1 0.0 collective-permute-done.8.refs_4_
  27.1 0.4 mix.3
  27.4 0.1 collective-permute-start.11
  27.5 1.9 %collective-permute-done.10.refs_5_ = bf16[2,1,128,512]{3,2,1,0:T(8,128)(2,1)S(1)} collective-permute-done((bf16[2,1,128,512]{3,2,1,0:T(8,128)(2,1)S(1)}, bf16[2,1,128,512]{3,2,1,0:T(8,128)(2,1)S(1)}, u32[]{:S(2)}, u32[]{:S(2)}) %collective-permute-start.10) | collective-permute-done | bytes 262176 | tf_op jit(solution)/shard_map/ppermute | solution.py:81
  29.4 1.7 %collective-permute-start.9 = (bf16[1,1,128,512]{3,2,1,0:T(8,128)(2,1)S(1)}, bf16[1,1,128,512]{3,2,1,0:T(8,128)(2,1)S(1)}, u32[]{:S(2)}, u32[]{:S(2)}) collective-permute-start(bf16[1,1,128,512]{3,2,1,0:T(8,128)(2,1)S(1)} %get-tuple-element.104), channel_id=1, source_target_pairs={{0,8},{4,12},{8,0},{12,4},{1,9},{5,13},{9,1},{13,5},{2,10},{6,14},... | collective-permute-start | bytes 393224 | tf_op jit(solution)/shard_map/ppermute | solution.py:81
  31.1 0.2 collective-permute-start.13
  31.4 1.5 %collective-permute-start.19 = (bf16[1,2,1,128,512]{4,3,2,1,0:T(8,128)(2,1)S(1)}, bf16[1,2,1,128,512]{4,3,2,1,0:T(8,128)(2,1)S(1)}, u32[]{:S(2)}, u32[]{:S(2)}) collective-permute-start(bf16[1,2,1,128,512]{4,3,2,1,0:T(8,128)(2,1)S(1)} %get-tuple-element.108), channel_id=1, source_target_pairs={{16,0},{0,16},{17,1},{1,17},{18,2},{2,18},{19,3},{3,19},{20,4},{4,... | collective-permute-start | bytes 786440 | tf_op jit(solution)/shard_map/ppermute | solution.py:92
  32.8 0.9 %product.4 = (bf16[2,1,128,512]{3,2,1,0:T(8,128)(2,1)S(1)}, bf16[272,512]{1,0:T(8,128)(2,1)S(1)}) custom-call(bf16[3,1,128,512]{3,2,1,0:T(8,128)(2,1)S(1)} %get-tuple-element.162.refs_0_, bf16[3,1,128,512]{3,2,1,0:T(8,128)(2,1)S(1)} %get-tuple-element.163.refs_1_, bf16[3,1,128,512]{3,2,1,0:T(8,128)(2,1)S(1)} %collective-permute-done.1.refs_2_, ...), custom_call_target="tpu_custom_call" | custom-call | flops 1 | bytes 1 | tf_op jit(solution)/shard_map/product/pallas_call | solution.py:21
  33.7 0.2 add_partial.3
  34.0 0.1 collective-permute-start.16
  34.1 0.6 %collective-permute-start.22 = (bf16[272,512]{1,0:T(8,128)(2,1)S(1)}, bf16[272,512]{1,0:T(8,128)(2,1)S(1)}, u32[]{:S(2)}, u32[]{:S(2)}) collective-permute-start(bf16[272,512]{1,0:T(8,128)(2,1)S(1)} %get-tuple-element.125), channel_id=1, source_target_pairs={{0,8},{4,12},{8,0},{12,4},{1,9},{5,13},{9,1},{13,5},{2,10},{6,14},... | collective-permute-start | bytes 835592 | tf_op jit(solution)/shard_map/ppermute | solution.py:81
  34.6 0.7 %collective-permute-done.9.refs_5_ = bf16[1,1,128,512]{3,2,1,0:T(8,128)(2,1)S(1)} collective-permute-done((bf16[1,1,128,512]{3,2,1,0:T(8,128)(2,1)S(1)}, bf16[1,1,128,512]{3,2,1,0:T(8,128)(2,1)S(1)}, u32[]{:S(2)}, u32[]{:S(2)}) %collective-permute-start.9) | collective-permute-done | bytes 131104 | tf_op jit(solution)/shard_map/ppermute | solution.py:81
  35.3 0.5 collective-permute-start.14
  35.8 1.7 %collective-permute-start.23 = (bf16[1,2,1,128,512]{4,3,2,1,0:T(8,128)(2,1)S(1)}, bf16[1,2,1,128,512]{4,3,2,1,0:T(8,128)(2,1)S(1)}, u32[]{:S(2)}, u32[]{:S(2)}) collective-permute-start(bf16[1,2,1,128,512]{4,3,2,1,0:T(8,128)(2,1)S(1)} %get-tuple-element.109), channel_id=1, source_target_pairs={{16,0},{0,16},{17,1},{1,17},{18,2},{2,18},{19,3},{3,19},{20,4},{4,... | collective-permute-start | bytes 786440 | tf_op jit(solution)/shard_map/ppermute | solution.py:92
  37.5 0.9 %product.5 = (bf16[2,1,128,512]{3,2,1,0:T(8,128)(2,1)S(1)}, bf16[2,1,128,512]{3,2,1,0:T(8,128)(2,1)S(1)}) custom-call(bf16[3,1,128,512]{3,2,1,0:T(8,128)(2,1)S(1)} %get-tuple-element.162.refs_0_, bf16[3,1,128,512]{3,2,1,0:T(8,128)(2,1)S(1)} %get-tuple-element.163.refs_1_, bf16[3,1,128,512]{3,2,1,0:T(8,128)(2,1)S(1)} %collective-permute-done.1.refs_2_, ...), custom_call_target="tpu_custom_call" | custom-call | flops 1 | bytes 1 | tf_op jit(solution)/shard_map/product/pallas_call | solution.py:21
  38.4 2.1 %collective-permute-done.19.refs_2_ = bf16[1,2,1,128,512]{4,3,2,1,0:T(8,128)(2,1)S(1)} collective-permute-done((bf16[1,2,1,128,512]{4,3,2,1,0:T(8,128)(2,1)S(1)}, bf16[1,2,1,128,512]{4,3,2,1,0:T(8,128)(2,1)S(1)}, u32[]{:S(2)}, u32[]{:S(2)}) %collective-permute-start.19) | collective-permute-done | bytes 262176 | tf_op jit(solution)/shard_map/ppermute | solution.py:92
  40.5 0.2 add_partial.4
  40.7 0.1 collective-permute-start.20
  40.8 0.5 collective-permute-start.21
  41.3 0.8 %collective-permute-done.20.refs_6_ = bf16[1,1,128,512]{3,2,1,0:T(8,128)(2,1)S(1)} collective-permute-done((bf16[1,1,128,512]{3,2,1,0:T(8,128)(2,1)S(1)}, bf16[1,1,128,512]{3,2,1,0:T(8,128)(2,1)S(1)}, u32[]{:S(2)}, u32[]{:S(2)}) %collective-permute-start.20) | collective-permute-done | bytes 131104 | tf_op jit(solution)/shard_map/ppermute | solution.py:85
  42.1 0.2 collective-permute-done.21.refs_7_
  42.3 0.5 product.6
  42.8 0.3 collective-permute-done.22.refs_1_
  43.1 0.8 %place.7.refs_1_ = bf16[3,2,128,512]{3,2,1,0:T(8,128)(2,1)} custom-call(bf16[2,1,128,512]{3,2,1,0:T(8,128)(2,1)S(1)} %get-tuple-element.157.refs_0_, bf16[272,512]{1,0:T(8,128)(2,1)S(1)} %collective-permute-done.22.refs_1_), custom_call_target="tpu_custom_call" | custom-call | flops 1 | bytes 1 | tf_op jit(solution)/shard_map/place/pallas_call | solution.py:322
  44.0 1.5 %collective-permute-done.23.refs_2_ = bf16[1,2,1,128,512]{4,3,2,1,0:T(8,128)(2,1)S(1)} collective-permute-done((bf16[1,2,1,128,512]{4,3,2,1,0:T(8,128)(2,1)S(1)}, bf16[1,2,1,128,512]{4,3,2,1,0:T(8,128)(2,1)S(1)}, u32[]{:S(2)}, u32[]{:S(2)}) %collective-permute-start.23) | collective-permute-done | bytes 262176 | tf_op jit(solution)/shard_map/ppermute | solution.py:92
  45.5 0.2 add_partial.5
  45.7 0.1 collective-permute-start.24
  45.8 0.5 collective-permute-start.25
  46.3 0.4 collective-permute-start.27
  46.6 0.5 collective-permute-done.24.refs_6_
  47.1 0.2 collective-permute-done.25.refs_7_
  47.3 0.5 product.7
  47.8 1.1 %collective-permute-start.26 = (bf16[1,1,128,512]{3,2,1,0:T(8,128)(2,1)S(1)}, bf16[1,1,128,512]{3,2,1,0:T(8,128)(2,1)S(1)}, u32[]{:S(2)}, u32[]{:S(2)}) collective-permute-start(bf16[1,1,128,512]{3,2,1,0:T(8,128)(2,1)S(1)} %get-tuple-element.171), channel_id=1, source_target_pairs={{0,8},{4,12},{8,0},{12,4},{1,9},{5,13},{9,1},{13,5},{2,10},{6,14},... | collective-permute-start | bytes 393224 | tf_op jit(solution)/shard_map/ppermute | solution.py:81
  48.9 0.7 %place.8.refs_1_ = bf16[3,2,128,512]{3,2,1,0:T(8,128)(2,1)} custom-call(bf16[2,1,128,512]{3,2,1,0:T(8,128)(2,1)S(1)} %get-tuple-element.173.refs_0_, bf16[3,2,128,512]{3,2,1,0:T(8,128)(2,1)} %place.7.refs_1_), custom_call_target="tpu_custom_call", output_to_operand_aliasing={{}: (1, {})} | custom-call | flops 1 | bytes 1 | tf_op jit(solution)/shard_map/place/pallas_call | solution.py:322
  49.6 0.8 %place.9.refs_1_ = bf16[3,2,128,512]{3,2,1,0:T(8,128)(2,1)} custom-call(bf16[2,1,128,512]{3,2,1,0:T(8,128)(2,1)S(1)} %get-tuple-element.173.refs_0_, bf16[1,1,128,512]{3,2,1,0:T(8,128)(2,1)S(1)} %get-tuple-element.174.refs_1_, bf16[1,1,128,512]{3,2,1,0:T(8,128)(2,1)S(1)} %get-tuple-element.175.refs_2_), custom_call_target="tpu_custom_call" | custom-call | flops 1 | bytes 1 | tf_op jit(solution)/shard_map/place/pallas_call | solution.py:322
  50.4 0.7 %place.10 = bf16[3,2,128,512]{3,2,1,0:T(8,128)(2,1)} custom-call(bf16[2,1,128,512]{3,2,1,0:T(8,128)(2,1)S(1)} %collective-permute-done.18.refs_0_, bf16[3,2,128,512]{3,2,1,0:T(8,128)(2,1)} %place.8.refs_1_), custom_call_target="tpu_custom_call", output_to_operand_aliasing={{}: (1, {})} | custom-call | flops 1 | bytes 1 | tf_op jit(solution)/shard_map/place/pallas_call | solution.py:322
  51.1 0.7 %place.11.refs_1_ = bf16[3,2,128,512]{3,2,1,0:T(8,128)(2,1)} custom-call(bf16[2,1,128,512]{3,2,1,0:T(8,128)(2,1)S(1)} %collective-permute-done.18.refs_0_, bf16[3,2,128,512]{3,2,1,0:T(8,128)(2,1)} %place.9.refs_1_), custom_call_target="tpu_custom_call", output_to_operand_aliasing={{}: (1, {})} | custom-call | flops 1 | bytes 1 | tf_op jit(solution)/shard_map/place/pallas_call | solution.py:322
  51.7 1.2 %collective-permute-done.27.refs_0_ = bf16[1,1,128,512]{3,2,1,0:T(8,128)(2,1)S(1)} collective-permute-done((bf16[1,1,128,512]{3,2,1,0:T(8,128)(2,1)S(1)}, bf16[1,1,128,512]{3,2,1,0:T(8,128)(2,1)S(1)}, u32[]{:S(2)}, u32[]{:S(2)}) %collective-permute-start.27) | collective-permute-done | bytes 131104 | tf_op jit(solution)/shard_map/ppermute | solution.py:81
  53.0 0.7 %place.12.refs_1_ = bf16[3,2,128,512]{3,2,1,0:T(8,128)(2,1)} custom-call(bf16[1,1,128,512]{3,2,1,0:T(8,128)(2,1)S(1)} %collective-permute-done.27.refs_0_, bf16[3,2,128,512]{3,2,1,0:T(8,128)(2,1)} %place.11.refs_1_), custom_call_target="tpu_custom_call", output_to_operand_aliasing={{}: (1, {})} | custom-call | flops 1 | bytes 1 | tf_op jit(solution)/shard_map/place/pallas_call | solution.py:322
  53.6 1.6 %collective-permute-done.26.refs_0_ = bf16[1,1,128,512]{3,2,1,0:T(8,128)(2,1)S(1)} collective-permute-done((bf16[1,1,128,512]{3,2,1,0:T(8,128)(2,1)S(1)}, bf16[1,1,128,512]{3,2,1,0:T(8,128)(2,1)S(1)}, u32[]{:S(2)}, u32[]{:S(2)}) %collective-permute-start.26) | collective-permute-done | bytes 131104 | tf_op jit(solution)/shard_map/ppermute | solution.py:81
  55.2 0.7 %place.13 = bf16[3,2,128,512]{3,2,1,0:T(8,128)(2,1)} custom-call(bf16[1,1,128,512]{3,2,1,0:T(8,128)(2,1)S(1)} %collective-permute-done.26.refs_0_, bf16[3,2,128,512]{3,2,1,0:T(8,128)(2,1)} %place.12.refs_1_), custom_call_target="tpu_custom_call", output_to_operand_aliasing={{}: (1, {})} | custom-call | flops 1 | bytes 1 | tf_op jit(solution)/shard_map/place/pallas_call | solution.py:322
  (22 shorter events, 0.1 us)
Async XLA Ops:
  0.6 5.0 %copy-start.1 = (bf16[3,2,128,512]{3,2,1,0:T(8,128)(2,1)S(1)}, bf16[3,2,128,512]{3,2,1,0:T(8,128)(2,1)}, u32[]{:S(2)}) copy-start(bf16[3,2,128,512]{3,2,1,0:T(8,128)(2,1)} %refs_2_.4) | copy-start | bytes 2359300
  0.6 6.6 %copy-start.2 = (bf16[3,2,128,512]{3,2,1,0:T(8,128)(2,1)S(1)}, bf16[3,2,128,512]{3,2,1,0:T(8,128)(2,1)}, u32[]{:S(2)}) copy-start(bf16[3,2,128,512]{3,2,1,0:T(8,128)(2,1)} %refs_1_) | copy-start | bytes 2359300
  2.6 4.7 %copy-start = (bf16[3,2,128,512]{3,2,1,0:T(8,128)(2,1)S(1)}, bf16[3,2,128,512]{3,2,1,0:T(8,128)(2,1)}, u32[]{:S(2)}) copy-start(bf16[3,2,128,512]{3,2,1,0:T(8,128)(2,1)} %refs_0_.9) | copy-start | bytes 2359300
  2.6 13.5 %collective-permute-start = (bf16[400,512]{1,0:T(8,128)(2,1)}, bf16[400,512]{1,0:T(8,128)(2,1)S(1)}, u32[]{:S(2)}, u32[]{:S(2)}) collective-permute-start(bf16[400,512]{1,0:T(8,128)(2,1)} %lead.1.refs_0_), channel_id=1, source_target_pairs={{0,8},{4,12},{8,0},{12,4},{1,9},{5,13},{9,1},{13,5},{2,10},{6,14},... | collective-permute-start | bytes 1228808 | tf_op jit(solution)/shard_map/ppermute | solution.py:81
  5.7 10.5 %copy-start.3 = (bf16[400,512]{1,0:T(8,128)(2,1)S(1)}, bf16[400,512]{1,0:T(8,128)(2,1)}, u32[]{:S(2)}) copy-start(bf16[400,512]{1,0:T(8,128)(2,1)} %lead.1.refs_0_) | copy-start | bytes 1228804
  5.7 12.1 %collective-permute-start.5 = (bf16[3,1,128,512]{3,2,1,0:T(8,128)(2,1)S(1)}, bf16[3,1,128,512]{3,2,1,0:T(8,128)(2,1)S(1)}, u32[]{:S(2)}, u32[]{:S(2)}) collective-permute-start(bf16[3,1,128,512]{3,2,1,0:T(8,128)(2,1)S(1)} %cut.2), channel_id=1, source_target_pairs={{16,0},{0,16},{17,1},{1,17},{18,2},{2,18},{19,3},{3,19},{20,4},{4,... | collective-permute-start | bytes 1179656 | tf_op jit(solution)/shard_map/ppermute | solution.py:92
  7.3 14.2 %collective-permute-start.1 = (bf16[3,1,128,512]{3,2,1,0:T(8,128)(2,1)S(1)}, bf16[3,1,128,512]{3,2,1,0:T(8,128)(2,1)S(1)}, u32[]{:S(2)}, u32[]{:S(2)}) collective-permute-start(bf16[3,1,128,512]{3,2,1,0:T(8,128)(2,1)S(1)} %get-tuple-element.162.refs_0_), channel_id=1, source_target_pairs={{0,4},{4,0},{8,12},{12,8},{1,5},{5,1},{9,13},{13,9},{2,6},{6,2},{1... | collective-permute-start | bytes 1179656 | tf_op jit(solution)/shard_map/ppermute | solution.py:85
  7.4 17.2 %collective-permute-start.6 = (bf16[3,1,128,512]{3,2,1,0:T(8,128)(2,1)S(1)}, bf16[3,1,128,512]{3,2,1,0:T(8,128)(2,1)S(1)}, u32[]{:S(2)}, u32[]{:S(2)}) collective-permute-start(bf16[3,1,128,512]{3,2,1,0:T(8,128)(2,1)S(1)} %get-tuple-element.106), channel_id=1, source_target_pairs={{0,8},{4,12},{8,0},{12,4},{1,9},{5,13},{9,1},{13,5},{2,10},{6,14},... | collective-permute-start | bytes 1179656 | tf_op jit(solution)/shard_map/ppermute | solution.py:81
  8.0 19.1 %collective-permute-start.7 = (bf16[2,1,144,512]{3,2,1,0:T(8,128)(2,1)S(1)}, bf16[2,1,144,512]{3,2,1,0:T(8,128)(2,1)S(1)}, u32[]{:S(2)}, u32[]{:S(2)}) collective-permute-start(bf16[2,1,144,512]{3,2,1,0:T(8,128)(2,1)S(1)} %get-tuple-element.112), channel_id=1, source_target_pairs={{16,0},{0,16},{17,1},{1,17},{18,2},{2,18},{19,3},{3,19},{20,4},{4,... | collective-permute-start | bytes 884744 | tf_op jit(solution)/shard_map/ppermute | solution.py:92
  16.2 1.2 %collective-permute-start.3 = (bf16[2,16,128]{2,1,0:T(8,128)(2,1)S(1)}, bf16[2,16,128]{2,1,0:T(8,128)(2,1)S(1)}, u32[]{:S(2)}, u32[]{:S(2)}) collective-permute-start(bf16[2,16,128]{2,1,0:T(8,128)(2,1)S(1)} %get-tuple-element.98.refs_0_), channel_id=1, source_target_pairs={{0,4},{4,0},{8,12},{12,8},{1,5},{5,1},{9,13},{13,9},{2,6},{6,2},{1... | collective-permute-start | bytes 24584 | tf_op jit(solution)/shard_map/ppermute | solution.py:85
  18.2 11.2 %collective-permute-start.10 = (bf16[2,1,128,512]{3,2,1,0:T(8,128)(2,1)S(1)}, bf16[2,1,128,512]{3,2,1,0:T(8,128)(2,1)S(1)}, u32[]{:S(2)}, u32[]{:S(2)}) collective-permute-start(bf16[2,1,128,512]{3,2,1,0:T(8,128)(2,1)S(1)} %get-tuple-element.103), channel_id=1, source_target_pairs={{0,8},{4,12},{8,0},{12,4},{1,9},{5,13},{9,1},{13,5},{2,10},{6,14},... | collective-permute-start | bytes 786440 | tf_op jit(solution)/shard_map/ppermute | solution.py:81
  20.0 3.7 %collective-permute-start.4 = (f32[3,8,128]{2,1,0:T(8,128)S(1)}, f32[3,8,128]{2,1,0:T(8,128)S(1)}, u32[]{:S(2)}, u32[]{:S(2)}) collective-permute-start(f32[3,8,128]{2,1,0:T(8,128)S(1)} %get-tuple-element.111.refs_1_), channel_id=1, source_target_pairs={{0,16},{16,0},{1,17},{17,1},{2,18},{18,2},{3,19},{19,3},{4,20},{20... | collective-permute-start | bytes 36872 | tf_op jit(solution)/shard_map/ppermute | solution.py:374
  21.5 5.5 %collective-permute-start.8 = (bf16[1,1,128,512]{3,2,1,0:T(8,128)(2,1)S(1)}, bf16[1,1,128,512]{3,2,1,0:T(8,128)(2,1)S(1)}, u32[]{:S(2)}, u32[]{:S(2)}) collective-permute-start(bf16[1,1,128,512]{3,2,1,0:T(8,128)(2,1)S(1)} %get-tuple-element.113), channel_id=1, source_target_pairs={{16,0},{0,16},{17,1},{1,17},{18,2},{2,18},{19,3},{3,19},{20,4},{4,... | collective-permute-start | bytes 393224 | tf_op jit(solution)/shard_map/ppermute | solution.py:92
  23.7 7.6 %collective-permute-start.2 = (bf16[3,1,128,512]{3,2,1,0:T(8,128)(2,1)S(1)}, bf16[3,1,128,512]{3,2,1,0:T(8,128)(2,1)S(1)}, u32[]{:S(2)}, u32[]{:S(2)}) collective-permute-start(bf16[3,1,128,512]{3,2,1,0:T(8,128)(2,1)S(1)} %get-tuple-element.163.refs_1_), channel_id=1, source_target_pairs={{0,4},{4,0},{8,12},{12,8},{1,5},{5,1},{9,13},{13,9},{2,6},{6,2},{1... | collective-permute-start | bytes 1179656 | tf_op jit(solution)/shard_map/ppermute | solution.py:85
  25.0 8.8 %collective-permute-start.15 = (bf16[1,2,1,144,512]{4,3,2,1,0:T(8,128)(2,1)S(1)}, bf16[1,2,1,144,512]{4,3,2,1,0:T(8,128)(2,1)S(1)}, u32[]{:S(2)}, u32[]{:S(2)}) collective-permute-start(bf16[1,2,1,144,512]{4,3,2,1,0:T(8,128)(2,1)S(1)} %get-tuple-element.107), channel_id=1, source_target_pairs={{16,0},{0,16},{17,1},{1,17},{18,2},{2,18},{19,3},{3,19},{20,4},{4,... | collective-permute-start | bytes 884744 | tf_op jit(solution)/shard_map/ppermute | solution.py:92
  27.4 3.7 %collective-permute-start.11 = (bf16[2,1,128,512]{3,2,1,0:T(8,128)(2,1)S(1)}, bf16[2,1,128,512]{3,2,1,0:T(8,128)(2,1)S(1)}, u32[]{:S(2)}, u32[]{:S(2)}) collective-permute-start(bf16[2,1,128,512]{3,2,1,0:T(8,128)(2,1)S(1)} %get-tuple-element.120.refs_4_), channel_id=1, source_target_pairs={{0,4},{4,0},{8,12},{12,8},{1,5},{5,1},{9,13},{13,9},{2,6},{6,2},{1... | collective-permute-start | bytes 786440 | tf_op jit(solution)/shard_map/ppermute | solution.py:85
  29.4 3.5 %collective-permute-start.12 = (bf16[2,1,128,512]{3,2,1,0:T(8,128)(2,1)S(1)}, bf16[2,1,128,512]{3,2,1,0:T(8,128)(2,1)S(1)}, u32[]{:S(2)}, u32[]{:S(2)}) collective-permute-start(bf16[2,1,128,512]{3,2,1,0:T(8,128)(2,1)S(1)} %collective-permute-done.10.refs_5_), channel_id=1, source_target_pairs={{0,4},{4,0},{8,12},{12,8},{1,5},{5,1},{9,13},{13,9},{2,6},{6,2},{1... | collective-permute-start | bytes 786440 | tf_op jit(solution)/shard_map/ppermute | solution.py:85
  29.4 5.9 %collective-permute-start.9 = (bf16[1,1,128,512]{3,2,1,0:T(8,128)(2,1)S(1)}, bf16[1,1,128,512]{3,2,1,0:T(8,128)(2,1)S(1)}, u32[]{:S(2)}, u32[]{:S(2)}) collective-permute-start(bf16[1,1,128,512]{3,2,1,0:T(8,128)(2,1)S(1)} %get-tuple-element.104), channel_id=1, source_target_pairs={{0,8},{4,12},{8,0},{12,4},{1,9},{5,13},{9,1},{13,5},{2,10},{6,14},... | collective-permute-start | bytes 393224 | tf_op jit(solution)/shard_map/ppermute | solution.py:81
  31.1 4.2 %collective-permute-start.13 = (bf16[1,1,128,512]{3,2,1,0:T(8,128)(2,1)S(1)}, bf16[1,1,128,512]{3,2,1,0:T(8,128)(2,1)S(1)}, u32[]{:S(2)}, u32[]{:S(2)}) collective-permute-start(bf16[1,1,128,512]{3,2,1,0:T(8,128)(2,1)S(1)} %get-tuple-element.134.refs_4_), channel_id=1, source_target_pairs={{0,4},{4,0},{8,12},{12,8},{1,5},{5,1},{9,13},{13,9},{2,6},{6,2},{1... | collective-permute-start | bytes 393224 | tf_op jit(solution)/shard_map/ppermute | solution.py:85
  31.4 9.1 %collective-permute-start.19 = (bf16[1,2,1,128,512]{4,3,2,1,0:T(8,128)(2,1)S(1)}, bf16[1,2,1,128,512]{4,3,2,1,0:T(8,128)(2,1)S(1)}, u32[]{:S(2)}, u32[]{:S(2)}) collective-permute-start(bf16[1,2,1,128,512]{4,3,2,1,0:T(8,128)(2,1)S(1)} %get-tuple-element.108), channel_id=1, source_target_pairs={{16,0},{0,16},{17,1},{1,17},{18,2},{2,18},{19,3},{3,19},{20,4},{4,... | collective-permute-start | bytes 786440 | tf_op jit(solution)/shard_map/ppermute | solution.py:92
  34.0 1.8 %collective-permute-start.16 = (bf16[1,1,128,512]{3,2,1,0:T(8,128)(2,1)S(1)}, bf16[1,1,128,512]{3,2,1,0:T(8,128)(2,1)S(1)}, u32[]{:S(2)}, u32[]{:S(2)}) collective-permute-start(bf16[1,1,128,512]{3,2,1,0:T(8,128)(2,1)S(1)} %get-tuple-element.138.refs_8_), channel_id=1, source_target_pairs={{0,4},{4,0},{8,12},{12,8},{1,5},{5,1},{9,13},{13,9},{2,6},{6,2},{1... | collective-permute-start | bytes 393224 | tf_op jit(solution)/shard_map/ppermute | solution.py:85
  34.1 9.1 %collective-permute-start.22 = (bf16[272,512]{1,0:T(8,128)(2,1)S(1)}, bf16[272,512]{1,0:T(8,128)(2,1)S(1)}, u32[]{:S(2)}, u32[]{:S(2)}) collective-permute-start(bf16[272,512]{1,0:T(8,128)(2,1)S(1)} %get-tuple-element.125), channel_id=1, source_target_pairs={{0,8},{4,12},{8,0},{12,4},{1,9},{5,13},{9,1},{13,5},{2,10},{6,14},... | collective-permute-start | bytes 835592 | tf_op jit(solution)/shard_map/ppermute | solution.py:81
  35.3 2.2 %collective-permute-start.17 = (bf16[1,1,128,512]{3,2,1,0:T(8,128)(2,1)S(1)}, bf16[1,1,128,512]{3,2,1,0:T(8,128)(2,1)S(1)}, u32[]{:S(2)}, u32[]{:S(2)}) collective-permute-start(bf16[1,1,128,512]{3,2,1,0:T(8,128)(2,1)S(1)} %get-tuple-element.139.refs_9_), channel_id=1, source_target_pairs={{0,4},{4,0},{8,12},{12,8},{1,5},{5,1},{9,13},{13,9},{2,6},{6,2},{1... | collective-permute-start | bytes 393224 | tf_op jit(solution)/shard_map/ppermute | solution.py:85
  35.3 2.2 %collective-permute-start.14 = (bf16[1,1,128,512]{3,2,1,0:T(8,128)(2,1)S(1)}, bf16[1,1,128,512]{3,2,1,0:T(8,128)(2,1)S(1)}, u32[]{:S(2)}, u32[]{:S(2)}) collective-permute-start(bf16[1,1,128,512]{3,2,1,0:T(8,128)(2,1)S(1)} %collective-permute-done.9.refs_5_), channel_id=1, source_target_pairs={{0,4},{4,0},{8,12},{12,8},{1,5},{5,1},{9,13},{13,9},{2,6},{6,2},{1... | collective-permute-start | bytes 393224 | tf_op jit(solution)/shard_map/ppermute | solution.py:85
  35.8 9.7 %collective-permute-start.23 = (bf16[1,2,1,128,512]{4,3,2,1,0:T(8,128)(2,1)S(1)}, bf16[1,2,1,128,512]{4,3,2,1,0:T(8,128)(2,1)S(1)}, u32[]{:S(2)}, u32[]{:S(2)}) collective-permute-start(bf16[1,2,1,128,512]{4,3,2,1,0:T(8,128)(2,1)S(1)} %get-tuple-element.109), channel_id=1, source_target_pairs={{16,0},{0,16},{17,1},{1,17},{18,2},{2,18},{19,3},{3,19},{20,4},{4,... | collective-permute-start | bytes 786440 | tf_op jit(solution)/shard_map/ppermute | solution.py:92
  40.7 1.4 %collective-permute-start.20 = (bf16[1,1,128,512]{3,2,1,0:T(8,128)(2,1)S(1)}, bf16[1,1,128,512]{3,2,1,0:T(8,128)(2,1)S(1)}, u32[]{:S(2)}, u32[]{:S(2)}) collective-permute-start(bf16[1,1,128,512]{3,2,1,0:T(8,128)(2,1)S(1)} %get-tuple-element.151.refs_4_), channel_id=1, source_target_pairs={{0,4},{4,0},{8,12},{12,8},{1,5},{5,1},{9,13},{13,9},{2,6},{6,2},{1... | collective-permute-start | bytes 393224 | tf_op jit(solution)/shard_map/ppermute | solution.py:85
  40.8 1.5 %collective-permute-start.21 = (bf16[1,1,128,512]{3,2,1,0:T(8,128)(2,1)S(1)}, bf16[1,1,128,512]{3,2,1,0:T(8,128)(2,1)S(1)}, u32[]{:S(2)}, u32[]{:S(2)}) collective-permute-start(bf16[1,1,128,512]{3,2,1,0:T(8,128)(2,1)S(1)} %get-tuple-element.152.refs_5_), channel_id=1, source_target_pairs={{0,4},{4,0},{8,12},{12,8},{1,5},{5,1},{9,13},{13,9},{2,6},{6,2},{1... | collective-permute-start | bytes 393224 | tf_op jit(solution)/shard_map/ppermute | solution.py:85
  41.3 9.1 %collective-permute-start.18 = (bf16[2,1,128,512]{3,2,1,0:T(8,128)(2,1)S(1)}, bf16[2,1,128,512]{3,2,1,0:T(8,128)(2,1)S(1)}, u32[]{:S(2)}, u32[]{:S(2)}) collective-permute-start(bf16[2,1,128,512]{3,2,1,0:T(8,128)(2,1)S(1)} %get-tuple-element.142), channel_id=1, source_target_pairs={{0,8},{4,12},{8,0},{12,4},{1,9},{5,13},{9,1},{13,5},{2,10},{6,14},... | collective-permute-start | bytes 786440 | tf_op jit(solution)/shard_map/ppermute | solution.py:81
  45.7 1.4 %collective-permute-start.24 = (bf16[1,1,128,512]{3,2,1,0:T(8,128)(2,1)S(1)}, bf16[1,1,128,512]{3,2,1,0:T(8,128)(2,1)S(1)}, u32[]{:S(2)}, u32[]{:S(2)}) collective-permute-start(bf16[1,1,128,512]{3,2,1,0:T(8,128)(2,1)S(1)} %get-tuple-element.166.refs_4_), channel_id=1, source_target_pairs={{0,4},{4,0},{8,12},{12,8},{1,5},{5,1},{9,13},{13,9},{2,6},{6,2},{1... | collective-permute-start | bytes 393224 | tf_op jit(solution)/shard_map/ppermute | solution.py:85
  45.8 1.5 %collective-permute-start.25 = (bf16[1,1,128,512]{3,2,1,0:T(8,128)(2,1)S(1)}, bf16[1,1,128,512]{3,2,1,0:T(8,128)(2,1)S(1)}, u32[]{:S(2)}, u32[]{:S(2)}) collective-permute-start(bf16[1,1,128,512]{3,2,1,0:T(8,128)(2,1)S(1)} %get-tuple-element.167.refs_5_), channel_id=1, source_target_pairs={{0,4},{4,0},{8,12},{12,8},{1,5},{5,1},{9,13},{13,9},{2,6},{6,2},{1... | collective-permute-start | bytes 393224 | tf_op jit(solution)/shard_map/ppermute | solution.py:85
  46.3 6.7 %collective-permute-start.27 = (bf16[1,1,128,512]{3,2,1,0:T(8,128)(2,1)S(1)}, bf16[1,1,128,512]{3,2,1,0:T(8,128)(2,1)S(1)}, u32[]{:S(2)}, u32[]{:S(2)}) collective-permute-start(bf16[1,1,128,512]{3,2,1,0:T(8,128)(2,1)S(1)} %get-tuple-element.156), channel_id=1, source_target_pairs={{0,8},{4,12},{8,0},{12,4},{1,9},{5,13},{9,1},{13,5},{2,10},{6,14},... | collective-permute-start | bytes 393224 | tf_op jit(solution)/shard_map/ppermute | solution.py:81
  47.8 7.4 %collective-permute-start.26 = (bf16[1,1,128,512]{3,2,1,0:T(8,128)(2,1)S(1)}, bf16[1,1,128,512]{3,2,1,0:T(8,128)(2,1)S(1)}, u32[]{:S(2)}, u32[]{:S(2)}) collective-permute-start(bf16[1,1,128,512]{3,2,1,0:T(8,128)(2,1)S(1)} %get-tuple-element.171), channel_id=1, source_target_pairs={{0,8},{4,12},{8,0},{12,4},{1,9},{5,13},{9,1},{13,5},{2,10},{6,14},... | collective-permute-start | bytes 393224 | tf_op jit(solution)/shard_map/ppermute | solution.py:81
